TPU v7x, 32 devices: a whole 2x2x4 slice. The times are simulated.
32 devices in a mesh: row: 2 (over y), col: 16 (over z, x, core).
Axes of the slice: x: 2, y: 2, z: 4, core: 2. Of those that a mesh axis runs over, the one named last changes fastest.
Arguments:
- own_block: float32 [4, 64, 128, 128], P('row', 'col')
- neighbor_block: float32 [4, 4, 64, 128, 128], P(None, 'row', 'col'), may hold values from -0.1 to 0.1
- pattern: int32 [4, 64, 4], P('row', 'col'), may hold values 0 or 1
- capacity: float32 [4, 64, 128], P('row', 'col'), may hold values from 0.02 to 4
- initial: float32 [4, 64, 128], P('row', 'col'), may hold values from -4 to 4
- currents: float32 [2, 16, 16, 4, 512], P('row', 'col'), may hold values from -6 to 6
- slot_tile: int32 [2, 16, 16, 4], P('row', 'col'), may hold values from 0 to 8, as said below
Outputs:
- drops: float32 [4, 4, 64, 128], P(None, 'row', 'col')
Inputs may be any that keep to these rules, and one draw needn't show every extreme that they name: `slot_tile`: empty slots hold 8. In every mesh row one destination column receives 4 live slots from every source column; other pairs hold 0 to 4 live slots, live ones first.
All inputs are finite; a program needn't handle non-finite values. No bound on the sum of `pattern` on one device may be relied on, other than what follows from the above.
Results may differ from a plain program's by a relative error of at most 0.0001.
Values sent between devices are 32-bit elements; how exact they have to be, the bound alone decides.
No kernel may reach another device: no remote copies, remote signals or barrier semaphores. Data moves between devices by JAX's collectives and lax.ppermute only.
A program may use at most 64 MiB of HBM per device.

v0:
```python
import jax
import jax.numpy as jnp
from jax import lax
from jax.sharding import PartitionSpec as P

STEPS = 4
ITERS = 8


spec_center = 6.4
spec_radius = 5.6


def padded_2(block, sides, width):
    for axis, dim in sides:
        count = lax.axis_size(axis)
        forward = [(i, i + 1) for i in range(count - 1)]
        backward = [(target, source) for source, target in forward]
        low = lax.ppermute(
            lax.slice_in_dim(block, block.shape[dim] - width, None, axis=dim), axis, forward
        )
        high = lax.ppermute(lax.slice_in_dim(block, 0, width, axis=dim), axis, backward)
        block = jnp.concatenate([low, block, high], axis=dim)
    return block


def couple(field, own_block, neighbor_block, pattern, capacity):
    padded = padded_2(field, (("row", 0), ("col", 1)), 1)
    upper_row = padded[:-2, 1:-1]
    lower_row = padded[2:, 1:-1]
    left_col = padded[1:-1, :-2]
    right_col = padded[1:-1, 2:]
    beside_all = jnp.stack([upper_row, lower_row, left_col, right_col])
    coupled = jnp.einsum(
        "nijab,nijb->nija", neighbor_block, beside_all, precision=lax.Precision.HIGHEST
    )
    weights = jnp.moveaxis(pattern, 2, 0).astype(jnp.float32)[..., None]
    outside = jnp.sum(coupled * weights, axis=0)
    inside = jnp.einsum("ijab,ijb->ija", own_block, field, precision=lax.Precision.HIGHEST)
    return inside + outside + capacity * field


def sweeps(estimate, source, blocks):
    residue = source - couple(estimate, *blocks)
    search_dir = residue
    stride = 1.0 / spec_center
    for sweep in range(ITERS):
        if sweep == 0:
            search_dir = residue
            stride = 1.0 / spec_center
        else:
            if sweep == 1:
                momentum = 0.5 * (spec_radius * stride) ** 2
            else:
                momentum = (spec_radius * stride / 2.0) ** 2
            stride = 1.0 / (spec_center - momentum / stride)
            search_dir = residue + momentum * search_dir
        estimate = estimate + stride * search_dir
        if sweep + 1 < ITERS:
            residue = residue - stride * couple(search_dir, *blocks)
    return estimate


def shards(own_block, neighbor_block, pattern, capacity, initial, currents, slot_tile):
    tile_rows, tile_cols, width = initial.shape
    tiles = tile_rows * tile_cols
    tile_ids = jnp.arange(tiles, dtype=jnp.int32)
    targets = lax.all_to_all(slot_tile, "col", split_axis=2, concat_axis=1, tiled=True)
    chooser = (targets[0, :, 0, :, None] == tile_ids[None, None, :]).astype(jnp.float32)
    blocks = (own_block, neighbor_block, pattern, capacity)
    voltage = initial
    frames = []
    arrived_all = lax.all_to_all(currents, "col", split_axis=2, concat_axis=1, tiled=True)
    injected_all = jnp.einsum(
        "skt,skf->tf", chooser, arrived_all[0, :, 0], precision=lax.Precision.HIGHEST
    ).reshape(tile_rows, tile_cols, STEPS, width)
    for instant in range(STEPS):
        source = capacity * voltage + injected_all[:, :, instant]
        voltage = sweeps(voltage, source, blocks)
        frames.append(voltage)
    return jnp.stack(frames)


def solution(mesh):
    return jax.shard_map(
        shards,
        mesh=mesh,
        in_specs=(
            P("row", "col", None, None),
            P(None, "row", "col", None, None),
            P("row", "col", None),
            P("row", "col", None),
            P("row", "col", None),
            P("row", "col", None, None, None),
            P("row", "col", None, None),
        ),
        out_specs=P(None, "row", "col", None),
        check_vma=False,
    )
```

profile of v0, /device:TPU:15, one launch (start us, length us, event | category | flops | bytes accessed | tf_op | source)
XLA Modules:
  0.0 610.2 jit_solution(10686635378361455567)
XLA Ops:
  1.5 6.6 %all-to-all-start = ((s32[1,1,16,4]{3,1,0,2:T(1,128)}), s32[1,1,16,4]{3,1,0,2:T(1,128)S(1)}, u32[]{:S(2)}, u32[]{:S(2)}) async-start(s32[1,1,16,4]{3,1,0,2:T(1,128)} %copy.27), calls=%async_computation | async-start | bytes 16384 | tf_op jit(solution)/shard_map/all_to_all | solution.py:68
  10.1 4.0 collective-permute-start.1
  17.5 3.9 collective-permute-start.2
  23.5 6.3 %all-to-all-start.1 = ((f32[1,1,16,4,512]{4,3,1,0,2:T(4,128)}), f32[1,1,16,4,512]{4,3,1,0,2:T(4,128)S(1)}, u32[]{:S(2)}, u32[]{:S(2)}) async-start(f32[1,1,16,4,512]{4,3,1,0,2:T(4,128)} %bitcast.784), calls=%async_computation.1 | async-start | bytes 262144 | tf_op jit(solution)/shard_map/all_to_all | solution.py:73
  42.3 5.1 collective-permute-start.6
  62.4 3.4 collective-permute-start.10
  71.6 3.4 fusion.180
  80.8 3.4 collective-permute-start.14
  90.0 3.4 fusion.182
  99.2 3.5 collective-permute-start.18
  108.6 3.4 fusion.184
  117.8 3.4 collective-permute-start.22
  136.2 3.4 collective-permute-start.26
  154.6 3.4 collective-permute-start.30
  173.0 3.4 collective-permute-start.34
  191.4 3.4 collective-permute-start.38
  200.6 3.4 fusion.194
  209.8 3.4 collective-permute-start.42
  219.0 3.4 fusion.196
  228.2 3.4 collective-permute-start.46
  237.4 3.4 fusion.198
  246.6 3.4 collective-permute-start.50
  265.0 3.4 collective-permute-start.54
  283.5 3.4 collective-permute-start.58
  301.9 3.4 collective-permute-start.62
  320.3 3.4 collective-permute-start.66
  338.7 3.4 collective-permute-start.70
  357.1 3.4 collective-permute-start.74
  375.5 3.4 collective-permute-start.78
  393.9 3.4 collective-permute-start.82
  412.3 3.4 collective-permute-start.86
  421.5 3.4 fusion.218
  430.7 3.4 collective-permute-start.90
  440.0 3.4 fusion.220
  449.2 3.4 collective-permute-start.94
  458.4 3.4 fusion.222
  467.6 3.4 collective-permute-start.98
  476.8 3.4 fusion.224
  486.0 3.4 collective-permute-start.102
  504.4 3.4 collective-permute-start.106
  522.8 3.4 collective-permute-start.110
  541.2 3.4 collective-permute-start.114
  559.6 3.4 collective-permute-start.118
  568.8 3.4 fusion.234
  578.0 3.4 collective-permute-start.122
  587.2 3.4 fusion.236
  596.4 3.4 collective-permute-start.126
  605.6 3.4 fusion.238
  (487 shorter events, 436.4 us)
Async XLA Ops:
  1.5 21.9 %all-to-all-start = ((s32[1,1,16,4]{3,1,0,2:T(1,128)}), s32[1,1,16,4]{3,1,0,2:T(1,128)S(1)}, u32[]{:S(2)}, u32[]{:S(2)}) async-start(s32[1,1,16,4]{3,1,0,2:T(1,128)} %copy.27), calls=%async_computation | async-start | bytes 16384 | tf_op jit(solution)/shard_map/all_to_all | solution.py:68
  8.8 7.9 %collective-permute-start = (f32[1,4,128]{2,1,0:T(4,128)S(1)}, f32[1,4,128]{2,1,0:T(4,128)S(1)}, u32[]{:S(2)}, u32[]{:S(2)}) collective-permute-start(f32[1,4,128]{2,1,0:T(4,128)S(1)} %get-tuple-element.285), channel_id=1, source_target_pairs={{0,16},{1,17},{2,18},{3,19},{4,20},{5,21},{6,22},{7,23},{8,24},{9,... | collective-permute-start | bytes 6152 | tf_op jit(solution)/shard_map/ppermute | solution.py:19
  10.1 6.7 %collective-permute-start.1 = (f32[1,4,128]{2,1,0:T(4,128)S(1)}, f32[1,4,128]{2,1,0:T(4,128)S(1)}, u32[]{:S(2)}, u32[]{:S(2)}) collective-permute-start(f32[1,4,128]{2,1,0:T(4,128)S(1)} %get-tuple-element.284), channel_id=1, source_target_pairs={{16,0},{17,1},{18,2},{19,3},{20,4},{21,5},{22,6},{23,7},{24,8},{25... | collective-permute-start | bytes 6152 | tf_op jit(solution)/shard_map/ppermute | solution.py:22
  17.5 12.3 %collective-permute-start.2 = (f32[4,1,128]{2,1,0:T(1,128)S(1)}, f32[4,1,128]{2,1,0:T(1,128)S(1)}, u32[]{:S(2)}, u32[]{:S(2)}) collective-permute-start(f32[4,1,128]{2,1,0:T(1,128)S(1)} %get-tuple-element.155), channel_id=1, source_target_pairs={{0,1},{1,2},{2,3},{3,4},{4,5},{5,6},{6,7},{7,8},{8,9},{9,10},{10,1... | collective-permute-start | bytes 6152 | tf_op jit(solution)/shard_map/ppermute | solution.py:19
  21.4 8.5 %collective-permute-start.3 = (f32[4,1,128]{2,1,0:T(1,128)S(1)}, f32[4,1,128]{2,1,0:T(1,128)S(1)}, u32[]{:S(2)}, u32[]{:S(2)}) collective-permute-start(f32[4,1,128]{2,1,0:T(1,128)S(1)} %get-tuple-element.156), channel_id=1, source_target_pairs={{1,0},{2,1},{3,2},{4,3},{5,4},{6,5},{7,6},{8,7},{9,8},{10,9},{11,1... | collective-permute-start | bytes 6152 | tf_op jit(solution)/shard_map/ppermute | solution.py:22
  23.5 11.5 %all-to-all-start.1 = ((f32[1,1,16,4,512]{4,3,1,0,2:T(4,128)}), f32[1,1,16,4,512]{4,3,1,0,2:T(4,128)S(1)}, u32[]{:S(2)}, u32[]{:S(2)}) async-start(f32[1,1,16,4,512]{4,3,1,0,2:T(4,128)} %bitcast.784), calls=%async_computation.1 | async-start | bytes 262144 | tf_op jit(solution)/shard_map/all_to_all | solution.py:73
  42.3 8.0 %collective-permute-start.6 = (f32[4,1,128]{2,1,0:T(1,128)S(1)}, f32[4,1,128]{2,1,0:T(1,128)S(1)}, u32[]{:S(2)}, u32[]{:S(2)}) collective-permute-start(f32[4,1,128]{2,1,0:T(1,128)S(1)} %get-tuple-element.151), channel_id=1, source_target_pairs={{0,1},{1,2},{2,3},{3,4},{4,5},{5,6},{6,7},{7,8},{8,9},{9,10},{10,1... | collective-permute-start | bytes 6152 | tf_op jit(solution)/shard_map/ppermute | solution.py:19
  47.4 5.8 collective-permute-start.7
  62.4 6.2 %collective-permute-start.10 = (f32[4,1,128]{2,1,0:T(1,128)S(1)}, f32[4,1,128]{2,1,0:T(1,128)S(1)}, u32[]{:S(2)}, u32[]{:S(2)}) collective-permute-start(f32[4,1,128]{2,1,0:T(1,128)S(1)} %get-tuple-element.147), channel_id=1, source_target_pairs={{0,1},{1,2},{2,3},{3,4},{4,5},{5,6},{6,7},{7,8},{8,9},{9,10},{10,1... | collective-permute-start | bytes 6152 | tf_op jit(solution)/shard_map/ppermute | solution.py:19
  65.8 5.8 collective-permute-start.11
  80.8 6.7 %collective-permute-start.14 = (f32[4,1,128]{2,1,0:T(1,128)S(1)}, f32[4,1,128]{2,1,0:T(1,128)S(1)}, u32[]{:S(2)}, u32[]{:S(2)}) collective-permute-start(f32[4,1,128]{2,1,0:T(1,128)S(1)} %get-tuple-element.143), channel_id=1, source_target_pairs={{0,1},{1,2},{2,3},{3,4},{4,5},{5,6},{6,7},{7,8},{8,9},{9,10},{10,1... | collective-permute-start | bytes 6152 | tf_op jit(solution)/shard_map/ppermute | solution.py:19
  84.2 5.8 collective-permute-start.15
  99.2 6.4 %collective-permute-start.18 = (f32[4,1,128]{2,1,0:T(1,128)S(1)}, f32[4,1,128]{2,1,0:T(1,128)S(1)}, u32[]{:S(2)}, u32[]{:S(2)}) collective-permute-start(f32[4,1,128]{2,1,0:T(1,128)S(1)} %get-tuple-element.139), channel_id=1, source_target_pairs={{0,1},{1,2},{2,3},{3,4},{4,5},{5,6},{6,7},{7,8},{8,9},{9,10},{10,1... | collective-permute-start | bytes 6152 | tf_op jit(solution)/shard_map/ppermute | solution.py:19
  102.7 5.8 collective-permute-start.19
  117.8 6.2 %collective-permute-start.22 = (f32[4,1,128]{2,1,0:T(1,128)S(1)}, f32[4,1,128]{2,1,0:T(1,128)S(1)}, u32[]{:S(2)}, u32[]{:S(2)}) collective-permute-start(f32[4,1,128]{2,1,0:T(1,128)S(1)} %get-tuple-element.135), channel_id=1, source_target_pairs={{0,1},{1,2},{2,3},{3,4},{4,5},{5,6},{6,7},{7,8},{8,9},{9,10},{10,1... | collective-permute-start | bytes 6152 | tf_op jit(solution)/shard_map/ppermute | solution.py:19
  121.1 5.8 collective-permute-start.23
  136.2 6.4 %collective-permute-start.26 = (f32[4,1,128]{2,1,0:T(1,128)S(1)}, f32[4,1,128]{2,1,0:T(1,128)S(1)}, u32[]{:S(2)}, u32[]{:S(2)}) collective-permute-start(f32[4,1,128]{2,1,0:T(1,128)S(1)} %get-tuple-element.131), channel_id=1, source_target_pairs={{0,1},{1,2},{2,3},{3,4},{4,5},{5,6},{6,7},{7,8},{8,9},{9,10},{10,1... | collective-permute-start | bytes 6152 | tf_op jit(solution)/shard_map/ppermute | solution.py:19
  139.5 5.8 collective-permute-start.27
  154.6 6.2 %collective-permute-start.30 = (f32[4,1,128]{2,1,0:T(1,128)S(1)}, f32[4,1,128]{2,1,0:T(1,128)S(1)}, u32[]{:S(2)}, u32[]{:S(2)}) collective-permute-start(f32[4,1,128]{2,1,0:T(1,128)S(1)} %get-tuple-element.127), channel_id=1, source_target_pairs={{0,1},{1,2},{2,3},{3,4},{4,5},{5,6},{6,7},{7,8},{8,9},{9,10},{10,1... | collective-permute-start | bytes 6152 | tf_op jit(solution)/shard_map/ppermute | solution.py:19
  157.9 5.8 collective-permute-start.31
  173.0 6.2 %collective-permute-start.34 = (f32[4,1,128]{2,1,0:T(1,128)S(1)}, f32[4,1,128]{2,1,0:T(1,128)S(1)}, u32[]{:S(2)}, u32[]{:S(2)}) collective-permute-start(f32[4,1,128]{2,1,0:T(1,128)S(1)} %get-tuple-element.123), channel_id=1, source_target_pairs={{0,1},{1,2},{2,3},{3,4},{4,5},{5,6},{6,7},{7,8},{8,9},{9,10},{10,1... | collective-permute-start | bytes 6152 | tf_op jit(solution)/shard_map/ppermute | solution.py:19
  176.4 5.8 collective-permute-start.35
  191.4 6.5 %collective-permute-start.38 = (f32[4,1,128]{2,1,0:T(1,128)S(1)}, f32[4,1,128]{2,1,0:T(1,128)S(1)}, u32[]{:S(2)}, u32[]{:S(2)}) collective-permute-start(f32[4,1,128]{2,1,0:T(1,128)S(1)} %get-tuple-element.119), channel_id=1, source_target_pairs={{0,1},{1,2},{2,3},{3,4},{4,5},{5,6},{6,7},{7,8},{8,9},{9,10},{10,1... | collective-permute-start | bytes 6152 | tf_op jit(solution)/shard_map/ppermute | solution.py:19
  194.8 5.8 collective-permute-start.39
  209.8 6.2 %collective-permute-start.42 = (f32[4,1,128]{2,1,0:T(1,128)S(1)}, f32[4,1,128]{2,1,0:T(1,128)S(1)}, u32[]{:S(2)}, u32[]{:S(2)}) collective-permute-start(f32[4,1,128]{2,1,0:T(1,128)S(1)} %get-tuple-element.115), channel_id=1, source_target_pairs={{0,1},{1,2},{2,3},{3,4},{4,5},{5,6},{6,7},{7,8},{8,9},{9,10},{10,1... | collective-permute-start | bytes 6152 | tf_op jit(solution)/shard_map/ppermute | solution.py:19
  213.2 5.8 collective-permute-start.43
  228.2 6.2 %collective-permute-start.46 = (f32[4,1,128]{2,1,0:T(1,128)S(1)}, f32[4,1,128]{2,1,0:T(1,128)S(1)}, u32[]{:S(2)}, u32[]{:S(2)}) collective-permute-start(f32[4,1,128]{2,1,0:T(1,128)S(1)} %get-tuple-element.111), channel_id=1, source_target_pairs={{0,1},{1,2},{2,3},{3,4},{4,5},{5,6},{6,7},{7,8},{8,9},{9,10},{10,1... | collective-permute-start | bytes 6152 | tf_op jit(solution)/shard_map/ppermute | solution.py:19
  231.6 5.8 collective-permute-start.47
  246.6 6.6 %collective-permute-start.50 = (f32[4,1,128]{2,1,0:T(1,128)S(1)}, f32[4,1,128]{2,1,0:T(1,128)S(1)}, u32[]{:S(2)}, u32[]{:S(2)}) collective-permute-start(f32[4,1,128]{2,1,0:T(1,128)S(1)} %get-tuple-element.107), channel_id=1, source_target_pairs={{0,1},{1,2},{2,3},{3,4},{4,5},{5,6},{6,7},{7,8},{8,9},{9,10},{10,1... | collective-permute-start | bytes 6152 | tf_op jit(solution)/shard_map/ppermute | solution.py:19
  265.0 6.3 %collective-permute-start.54 = (f32[4,1,128]{2,1,0:T(1,128)S(1)}, f32[4,1,128]{2,1,0:T(1,128)S(1)}, u32[]{:S(2)}, u32[]{:S(2)}) collective-permute-start(f32[4,1,128]{2,1,0:T(1,128)S(1)} %get-tuple-element.103), channel_id=1, source_target_pairs={{0,1},{1,2},{2,3},{3,4},{4,5},{5,6},{6,7},{7,8},{8,9},{9,10},{10,1... | collective-permute-start | bytes 6152 | tf_op jit(solution)/shard_map/ppermute | solution.py:19
  283.5 6.2 %collective-permute-start.58 = (f32[4,1,128]{2,1,0:T(1,128)S(1)}, f32[4,1,128]{2,1,0:T(1,128)S(1)}, u32[]{:S(2)}, u32[]{:S(2)}) collective-permute-start(f32[4,1,128]{2,1,0:T(1,128)S(1)} %get-tuple-element.99), channel_id=1, source_target_pairs={{0,1},{1,2},{2,3},{3,4},{4,5},{5,6},{6,7},{7,8},{8,9},{9,10},{10,1... | collective-permute-start | bytes 6152 | tf_op jit(solution)/shard_map/ppermute | solution.py:19
  301.9 6.4 %collective-permute-start.62 = (f32[4,1,128]{2,1,0:T(1,128)S(1)}, f32[4,1,128]{2,1,0:T(1,128)S(1)}, u32[]{:S(2)}, u32[]{:S(2)}) collective-permute-start(f32[4,1,128]{2,1,0:T(1,128)S(1)} %get-tuple-element.95), channel_id=1, source_target_pairs={{0,1},{1,2},{2,3},{3,4},{4,5},{5,6},{6,7},{7,8},{8,9},{9,10},{10,1... | collective-permute-start | bytes 6152 | tf_op jit(solution)/shard_map/ppermute | solution.py:19
  320.3 6.2 %collective-permute-start.66 = (f32[4,1,128]{2,1,0:T(1,128)S(1)}, f32[4,1,128]{2,1,0:T(1,128)S(1)}, u32[]{:S(2)}, u32[]{:S(2)}) collective-permute-start(f32[4,1,128]{2,1,0:T(1,128)S(1)} %get-tuple-element.91), channel_id=1, source_target_pairs={{0,1},{1,2},{2,3},{3,4},{4,5},{5,6},{6,7},{7,8},{8,9},{9,10},{10,1... | collective-permute-start | bytes 6152 | tf_op jit(solution)/shard_map/ppermute | solution.py:19
  338.7 6.2 %collective-permute-start.70 = (f32[4,1,128]{2,1,0:T(1,128)S(1)}, f32[4,1,128]{2,1,0:T(1,128)S(1)}, u32[]{:S(2)}, u32[]{:S(2)}) collective-permute-start(f32[4,1,128]{2,1,0:T(1,128)S(1)} %get-tuple-element.87), channel_id=1, source_target_pairs={{0,1},{1,2},{2,3},{3,4},{4,5},{5,6},{6,7},{7,8},{8,9},{9,10},{10,1... | collective-permute-start | bytes 6152 | tf_op jit(solution)/shard_map/ppermute | solution.py:19
  357.1 6.5 %collective-permute-start.74 = (f32[4,1,128]{2,1,0:T(1,128)S(1)}, f32[4,1,128]{2,1,0:T(1,128)S(1)}, u32[]{:S(2)}, u32[]{:S(2)}) collective-permute-start(f32[4,1,128]{2,1,0:T(1,128)S(1)} %get-tuple-element.83), channel_id=1, source_target_pairs={{0,1},{1,2},{2,3},{3,4},{4,5},{5,6},{6,7},{7,8},{8,9},{9,10},{10,1... | collective-permute-start | bytes 6152 | tf_op jit(solution)/shard_map/ppermute | solution.py:19
  375.5 6.2 %collective-permute-start.78 = (f32[4,1,128]{2,1,0:T(1,128)S(1)}, f32[4,1,128]{2,1,0:T(1,128)S(1)}, u32[]{:S(2)}, u32[]{:S(2)}) collective-permute-start(f32[4,1,128]{2,1,0:T(1,128)S(1)} %get-tuple-element.79), channel_id=1, source_target_pairs={{0,1},{1,2},{2,3},{3,4},{4,5},{5,6},{6,7},{7,8},{8,9},{9,10},{10,1... | collective-permute-start | bytes 6152 | tf_op jit(solution)/shard_map/ppermute | solution.py:19
  393.9 6.2 %collective-permute-start.82 = (f32[4,1,128]{2,1,0:T(1,128)S(1)}, f32[4,1,128]{2,1,0:T(1,128)S(1)}, u32[]{:S(2)}, u32[]{:S(2)}) collective-permute-start(f32[4,1,128]{2,1,0:T(1,128)S(1)} %get-tuple-element.75), channel_id=1, source_target_pairs={{0,1},{1,2},{2,3},{3,4},{4,5},{5,6},{6,7},{7,8},{8,9},{9,10},{10,1... | collective-permute-start | bytes 6152 | tf_op jit(solution)/shard_map/ppermute | solution.py:19
  412.3 6.6 %collective-permute-start.86 = (f32[4,1,128]{2,1,0:T(1,128)S(1)}, f32[4,1,128]{2,1,0:T(1,128)S(1)}, u32[]{:S(2)}, u32[]{:S(2)}) collective-permute-start(f32[4,1,128]{2,1,0:T(1,128)S(1)} %get-tuple-element.71), channel_id=1, source_target_pairs={{0,1},{1,2},{2,3},{3,4},{4,5},{5,6},{6,7},{7,8},{8,9},{9,10},{10,1... | collective-permute-start | bytes 6152 | tf_op jit(solution)/shard_map/ppermute | solution.py:19
  430.7 6.3 %collective-permute-start.90 = (f32[4,1,128]{2,1,0:T(1,128)S(1)}, f32[4,1,128]{2,1,0:T(1,128)S(1)}, u32[]{:S(2)}, u32[]{:S(2)}) collective-permute-start(f32[4,1,128]{2,1,0:T(1,128)S(1)} %get-tuple-element.67), channel_id=1, source_target_pairs={{0,1},{1,2},{2,3},{3,4},{4,5},{5,6},{6,7},{7,8},{8,9},{9,10},{10,1... | collective-permute-start | bytes 6152 | tf_op jit(solution)/shard_map/ppermute | solution.py:19
  449.2 6.2 %collective-permute-start.94 = (f32[4,1,128]{2,1,0:T(1,128)S(1)}, f32[4,1,128]{2,1,0:T(1,128)S(1)}, u32[]{:S(2)}, u32[]{:S(2)}) collective-permute-start(f32[4,1,128]{2,1,0:T(1,128)S(1)} %get-tuple-element.63), channel_id=1, source_target_pairs={{0,1},{1,2},{2,3},{3,4},{4,5},{5,6},{6,7},{7,8},{8,9},{9,10},{10,1... | collective-permute-start | bytes 6152 | tf_op jit(solution)/shard_map/ppermute | solution.py:19
  467.6 6.4 %collective-permute-start.98 = (f32[4,1,128]{2,1,0:T(1,128)S(1)}, f32[4,1,128]{2,1,0:T(1,128)S(1)}, u32[]{:S(2)}, u32[]{:S(2)}) collective-permute-start(f32[4,1,128]{2,1,0:T(1,128)S(1)} %get-tuple-element.59), channel_id=1, source_target_pairs={{0,1},{1,2},{2,3},{3,4},{4,5},{5,6},{6,7},{7,8},{8,9},{9,10},{10,1... | collective-permute-start | bytes 6152 | tf_op jit(solution)/shard_map/ppermute | solution.py:19
  486.0 6.2 %collective-permute-start.102 = (f32[4,1,128]{2,1,0:T(1,128)S(1)}, f32[4,1,128]{2,1,0:T(1,128)S(1)}, u32[]{:S(2)}, u32[]{:S(2)}) collective-permute-start(f32[4,1,128]{2,1,0:T(1,128)S(1)} %get-tuple-element.55), channel_id=1, source_target_pairs={{0,1},{1,2},{2,3},{3,4},{4,5},{5,6},{6,7},{7,8},{8,9},{9,10},{10,1... | collective-permute-start | bytes 6152 | tf_op jit(solution)/shard_map/ppermute | solution.py:19
  504.4 6.2 %collective-permute-start.106 = (f32[4,1,128]{2,1,0:T(1,128)S(1)}, f32[4,1,128]{2,1,0:T(1,128)S(1)}, u32[]{:S(2)}, u32[]{:S(2)}) collective-permute-start(f32[4,1,128]{2,1,0:T(1,128)S(1)} %get-tuple-element.51), channel_id=1, source_target_pairs={{0,1},{1,2},{2,3},{3,4},{4,5},{5,6},{6,7},{7,8},{8,9},{9,10},{10,1... | collective-permute-start | bytes 6152 | tf_op jit(solution)/shard_map/ppermute | solution.py:19
  522.8 6.5 %collective-permute-start.110 = (f32[4,1,128]{2,1,0:T(1,128)S(1)}, f32[4,1,128]{2,1,0:T(1,128)S(1)}, u32[]{:S(2)}, u32[]{:S(2)}) collective-permute-start(f32[4,1,128]{2,1,0:T(1,128)S(1)} %get-tuple-element.47), channel_id=1, source_target_pairs={{0,1},{1,2},{2,3},{3,4},{4,5},{5,6},{6,7},{7,8},{8,9},{9,10},{10,1... | collective-permute-start | bytes 6152 | tf_op jit(solution)/shard_map/ppermute | solution.py:19
  541.2 6.2 %collective-permute-start.114 = (f32[4,1,128]{2,1,0:T(1,128)S(1)}, f32[4,1,128]{2,1,0:T(1,128)S(1)}, u32[]{:S(2)}, u32[]{:S(2)}) collective-permute-start(f32[4,1,128]{2,1,0:T(1,128)S(1)} %get-tuple-element.43), channel_id=1, source_target_pairs={{0,1},{1,2},{2,3},{3,4},{4,5},{5,6},{6,7},{7,8},{8,9},{9,10},{10,1... | collective-permute-start | bytes 6152 | tf_op jit(solution)/shard_map/ppermute | solution.py:19
  559.6 6.2 %collective-permute-start.118 = (f32[4,1,128]{2,1,0:T(1,128)S(1)}, f32[4,1,128]{2,1,0:T(1,128)S(1)}, u32[]{:S(2)}, u32[]{:S(2)}) collective-permute-start(f32[4,1,128]{2,1,0:T(1,128)S(1)} %get-tuple-element.39), channel_id=1, source_target_pairs={{0,1},{1,2},{2,3},{3,4},{4,5},{5,6},{6,7},{7,8},{8,9},{9,10},{10,1... | collective-permute-start | bytes 6152 | tf_op jit(solution)/shard_map/ppermute | solution.py:19
  578.0 6.5 %collective-permute-start.122 = (f32[4,1,128]{2,1,0:T(1,128)S(1)}, f32[4,1,128]{2,1,0:T(1,128)S(1)}, u32[]{:S(2)}, u32[]{:S(2)}) collective-permute-start(f32[4,1,128]{2,1,0:T(1,128)S(1)} %get-tuple-element.35), channel_id=1, source_target_pairs={{0,1},{1,2},{2,3},{3,4},{4,5},{5,6},{6,7},{7,8},{8,9},{9,10},{10,1... | collective-permute-start | bytes 6152 | tf_op jit(solution)/shard_map/ppermute | solution.py:19
  596.4 6.2 %collective-permute-start.126 = (f32[4,1,128]{2,1,0:T(1,128)S(1)}, f32[4,1,128]{2,1,0:T(1,128)S(1)}, u32[]{:S(2)}, u32[]{:S(2)}) collective-permute-start(f32[4,1,128]{2,1,0:T(1,128)S(1)} %get-tuple-element.31), channel_id=1, source_target_pairs={{0,1},{1,2},{2,3},{3,4},{4,5},{5,6},{6,7},{7,8},{8,9},{9,10},{10,1... | collective-permute-start | bytes 6152 | tf_op jit(solution)/shard_map/ppermute | solution.py:19
  (86 other events, 484.4 us)
where the time goes:
time: 621 us; the launch traced here: 610 us
  starting transfers between devices  276 us (44%)
  waiting for transfers between devices  184 us (30%)
  matrix products  138 us (22%)
  other arithmetic  6.22 us (1%)
    ppermute x64, starting transfers between devices, padded_2(): lax.ppermute(lax.slice_in_dim(block, block.shape[dim] - width, None, axis...  152 us
    ppermute x64, starting transfers between devices, padded_2(): lax.ppermute(lax.slice_in_dim(block, 0, width, axis=dim), axis, backward)  112 us
    dot_general x32, matrix products, couple(): jnp.einsum('nijab,nijb->nija', neighbor_block, beside_all, precision=lax....  107 us
    ppermute x64, waiting for transfers between devices, padded_2(): lax.ppermute(lax.slice_in_dim(block, block.shape[dim] - width, None, axis...  93.7 us
    ppermute x64, waiting for transfers between devices, padded_2(): lax.ppermute(lax.slice_in_dim(block, 0, width, axis=dim), axis, backward)  88.8 us
    dot_general x32, matrix products, couple(): jnp.einsum('ijab,ijb->ija', own_block, field, precision=lax.Precision.HIG...  30.5 us
  transfers between devices with their start and end apart: 130, of which 63 were waited for; matrix products, arithmetic and copies ran while one was open for 6% of the time, Pallas kernels for 0%

commit v1 on v0

v1 whole, which is shorter than its diff:
```python
import functools

import jax
import jax.numpy as jnp
from jax import lax
from jax.experimental import pallas as pl
from jax.experimental.pallas import tpu as pltpu
from jax.sharding import PartitionSpec as P

STEPS = 4
ITERS = 8

spec_center = 6.4
spec_radius = 5.6


def schedule():
    strides, momenta = [], []
    stride = 1.0 / spec_center
    for sweep in range(ITERS):
        if sweep == 0:
            momentum = 0.0
        else:
            if sweep == 1:
                momentum = 0.5 * (spec_radius * stride) ** 2
            else:
                momentum = (spec_radius * stride / 2.0) ** 2
            stride = 1.0 / (spec_center - momentum / stride)
        strides.append(stride)
        momenta.append(momentum)
    return strides, momenta


STRIDES, MOMENTA = schedule()


def swap_pairs(count, first):
    pairs = []
    for i in range(first, count - 1, 2):
        pairs += [(i, i + 1), (i + 1, i)]
    return pairs


def exchange(field):
    arrived = []
    for axis in ("row", "col"):
        count = lax.axis_size(axis)
        for first in (0, 1):
            pairs = swap_pairs(count, first)
            arrived.append(lax.ppermute(field, axis, pairs) if pairs else None)
    return arrived


def beside(field, halos, odd_row, odd_col, cols):
    tiles = field.shape[0]
    row_a, row_b, col_a, col_b = halos
    zero = jnp.zeros_like(field)
    row_a, row_b, col_a, col_b = [zero if h is None else h for h in (row_a, row_b, col_a, col_b)]
    above = jnp.where(odd_row, row_a, row_b)
    below = jnp.where(odd_row, row_b, row_a)
    west = jnp.where(odd_col, col_a, col_b)
    east = jnp.where(odd_col, col_b, col_a)
    up = jnp.concatenate([above[tiles - cols:], field[: tiles - cols]], axis=0)
    down = jnp.concatenate([field[cols:], below[:cols]], axis=0)
    column = lax.broadcasted_iota(jnp.int32, field.shape, 0) % cols
    rolled = jnp.concatenate([field[tiles - 1:], field[: tiles - 1]], axis=0)
    west_edge = jnp.concatenate([west[cols - 1:], west[: cols - 1]], axis=0)
    left = jnp.where(column == 0, west_edge, rolled)
    rolled = jnp.concatenate([field[1:], field[:1]], axis=0)
    east_edge = jnp.concatenate([east[tiles - cols + 1:], east[: tiles - cols + 1]], axis=0)
    right = jnp.where(column == cols - 1, east_edge, rolled)
    return up, down, left, right


def blocks_times(field, around, own_ref, nb_ref):
    tiles, width = field.shape
    chunk = 32
    lane = lax.broadcasted_iota(jnp.int32, (chunk, width), 1)
    sub = lax.broadcasted_iota(jnp.int32, (chunk, width), 0)
    outs = []
    for t in range(tiles):
        vecs = [f[t:t + 1] for f in around]
        mine = field[t:t + 1]
        spread = jnp.zeros((chunk, width), jnp.float32)
        for g in range(0, width, chunk):
            acc = own_ref[t, g:g + chunk, :] * mine
            for n, vec in enumerate(vecs):
                acc = acc + nb_ref[n, t, g:g + chunk, :] * vec
            total = jnp.sum(acc, axis=1, keepdims=True)
            spread = jnp.where(lane == sub + g, total, spread)
        outs.append(jnp.sum(spread, axis=0, keepdims=True))
    return jnp.concatenate(outs, axis=0)


def kernel(sweep, cols, present, flags, own_ref, nb_ref, weights, *refs):
    n_halo = sum(present)
    halo_refs, refs = refs[:n_halo], refs[n_halo:]
    halo_iter = iter(halo_refs)
    halos = [next(halo_iter)[...] if p else None for p in present]
    odd_row, odd_col = flags[0] == 1, flags[1] == 1
    field_ref, refs = refs[0], refs[1:]
    field = field_ref[...]
    around = beside(field, halos, odd_row, odd_col, cols)
    around = [f * weights[n] for n, f in enumerate(around)]
    product = blocks_times(field, around, own_ref, nb_ref)
    if sweep < 0:
        injected, search_out, residue_out, estimate_out = refs
        residue = injected[...] - product
        search_out[...] = residue
        residue_out[...] = residue
        estimate_out[...] = field + STRIDES[0] * residue
    else:
        capacity, residue_in, estimate_in = refs[:3]
        outs = refs[3:]
        residue = residue_in[...] - STRIDES[sweep] * (product + capacity[...] * field)
        search = residue + MOMENTA[sweep + 1] * field
        estimate = estimate_in[...] + STRIDES[sweep + 1] * search
        if sweep + 2 < ITERS:
            outs[0][...] = search
            outs[1][...] = residue
            outs[2][...] = estimate
        else:
            outs[0][...] = estimate


def shards(own_block, neighbor_block, pattern, capacity, initial, currents, slot_tile):
    tile_rows, tile_cols, width = initial.shape
    tiles = tile_rows * tile_cols
    n_col = lax.axis_size("col")
    slots = currents.shape[3]
    frames = currents.shape[4]
    flags = jnp.stack([lax.axis_index("row") % 2, lax.axis_index("col") % 2]).astype(jnp.int32)

    voltage = initial.reshape(tiles, width)
    halos = exchange(voltage)

    names = jnp.pad(slot_tile.astype(jnp.float32)[..., None, :],
                    ((0, 0), (0, 0), (0, 0), (0, 0), (0, frames - slots)))
    packed = jnp.concatenate([currents, names], axis=3)
    arrived = lax.all_to_all(packed, "col", split_axis=2, concat_axis=1, tiled=True)[0, :, 0]
    targets = arrived[:, slots, :slots]
    chooser = (targets[..., None] == jnp.arange(tiles, dtype=jnp.float32)).astype(jnp.float32)
    injected = jnp.einsum("skt,skf->tf", chooser, arrived[:, :slots], precision=lax.Precision.HIGHEST)
    injected = injected.reshape(tiles, STEPS, width)

    own = own_block.reshape(tiles, width, width)
    nb = neighbor_block.reshape(4, tiles, width, width)
    weights = jnp.broadcast_to(
        jnp.moveaxis(pattern.reshape(tiles, 4), 1, 0).astype(jnp.float32)[..., None], (4, tiles, width)
    )
    cap = capacity.reshape(tiles, width)
    shape = jax.ShapeDtypeStruct((tiles, width), jnp.float32)
    vmem = pl.BlockSpec(memory_space=pltpu.VMEM)
    smem = pl.BlockSpec(memory_space=pltpu.SMEM)

    def call(sweep, halos, *state):
        present = tuple(h is not None for h in halos)
        ins = (flags, own, nb, weights) + tuple(h for h in halos if h is not None) + state
        n_out = 1 if sweep + 2 == ITERS else 3
        out = pl.pallas_call(
            functools.partial(kernel, sweep, tile_cols, present),
            out_shape=(shape,) * n_out,
            in_specs=[smem] + [vmem] * (len(ins) - 1),
            out_specs=(vmem,) * n_out,
            compiler_params=pltpu.CompilerParams(vmem_limit_bytes=8 * 2**20),
            cost_estimate=pl.CostEstimate(flops=2 * 5 * tiles * width * width, bytes_accessed=5 * tiles * width * width * 4,
                                          transcendentals=0),
            name="couple",
        )(*ins)
        return out

    frames_out = []
    for instant in range(STEPS):
        if instant:
            halos = exchange(voltage)
        search, residue, estimate = call(-1, halos, voltage, injected[:, instant])
        for sweep in range(ITERS - 1):
            halos = exchange(search)
            out = call(sweep, halos, search, cap, residue, estimate)
            if sweep + 2 < ITERS:
                search, residue, estimate = out
            else:
                (voltage,) = out
        frames_out.append(voltage)
    return jnp.stack(frames_out).reshape(STEPS, tile_rows, tile_cols, width)


def solution(mesh):
    return jax.shard_map(
        shards,
        mesh=mesh,
        in_specs=(
            P("row", "col", None, None),
            P(None, "row", "col", None, None),
            P("row", "col", None),
            P("row", "col", None),
            P("row", "col", None),
            P("row", "col", None, None, None),
            P("row", "col", None, None),
        ),
        out_specs=P(None, "row", "col", None),
        check_vma=False,
    )
```

time: 621 us -> 262 us (0.42)
  the two profiles are of different devices: /device:TPU:15 before, /device:TPU:8 now
where the time goes in v1:
time: 262 us; the launch traced here: 261 us
  waiting for transfers between devices  118 us (45%)
  starting transfers between devices  108 us (41%)
  Pallas kernels  26.6 us (10%)
  local copies, waits for them, and re-layouts  4.72 us (2%)
  other arithmetic  2.88 us (1%)
    ppermute x96, waiting for transfers between devices, exchange(): arrived.append(lax.ppermute(field, axis, pairs) if pairs else None)  118 us
    ppermute x96, starting transfers between devices, exchange(): arrived.append(lax.ppermute(field, axis, pairs) if pairs else None)  102 us
    pallas_call x32, Pallas kernels, call(): pl.pallas_call(functools.partial(kernel, sweep, tile_cols, present), out_...  26.6 us
    all_to_all x1, starting transfers between devices, shards(): lax.all_to_all(packed, 'col', split_axis=2, concat_axis=1, tiled=True)  6.27 us
  transfers between devices with their start and end apart: 97, of which 61 were waited for; matrix products, arithmetic and copies ran while one was open for 0% of the time, Pallas kernels for 0%

profile of v1, /device:TPU:8, one launch (start us, length us, event | category | flops | bytes accessed | tf_op | source)
XLA Modules:
  0.0 260.6 jit_solution(16815081456475571781)
XLA Ops:
  2.6 6.3 %all-to-all-start = ((f32[1,1,16,5,512]{4,1,3,0,2:T(1,128)}), f32[1,1,16,5,512]{4,1,3,0,2:T(1,128)S(1)}, u32[]{:S(2)}, u32[]{:S(2)}) async-start(f32[1,1,16,5,512]{4,1,3,0,2:T(1,128)} %fusion), calls=%async_computation | async-start | bytes 327680 | tf_op jit(solution)/shard_map/all_to_all | solution.py:140
  10.4 3.5 %collective-permute-start.2 = (f32[8,128]{1,0:T(8,128)}, f32[8,128]{1,0:T(8,128)S(1)}, u32[]{:S(2)}, u32[]{:S(2)}) collective-permute-start(f32[8,128]{1,0:T(8,128)} %bitcast.128), channel_id=1, source_target_pairs={{1,2},{2,1},{3,4},{4,3},{5,6},{6,5},{7,8},{8,7},{9,10},{10,9},{11,... | collective-permute-start | bytes 12296 | tf_op jit(solution)/shard_map/ppermute | solution.py:50
  21.5 3.0 %collective-permute-start.5 = (f32[8,128]{1,0:T(8,128)S(1)}, f32[8,128]{1,0:T(8,128)S(1)}, u32[]{:S(2)}, u32[]{:S(2)}) collective-permute-start(f32[8,128]{1,0:T(8,128)S(1)} %get-tuple-element.89.refs_3_), channel_id=1, source_target_pairs={{1,2},{2,1},{3,4},{4,3},{5,6},{6,5},{7,8},{8,7},{9,10},{10,9},{11,... | collective-permute-start | bytes 12296 | tf_op jit(solution)/shard_map/ppermute | solution.py:50
  24.5 2.8 %collective-permute-done.5.refs_2_ = f32[8,128]{1,0:T(8,128)S(1)} collective-permute-done((f32[8,128]{1,0:T(8,128)S(1)}, f32[8,128]{1,0:T(8,128)S(1)}, u32[]{:S(2)}, u32[]{:S(2)}) %collective-permute-start.5) | collective-permute-done | bytes 4128 | tf_op jit(solution)/shard_map/ppermute | solution.py:50
  29.5 2.9 %collective-permute-start.8 = (f32[8,128]{1,0:T(8,128)S(1)}, f32[8,128]{1,0:T(8,128)S(1)}, u32[]{:S(2)}, u32[]{:S(2)}) collective-permute-start(f32[8,128]{1,0:T(8,128)S(1)} %get-tuple-element.92.refs_3_), channel_id=1, source_target_pairs={{1,2},{2,1},{3,4},{4,3},{5,6},{6,5},{7,8},{8,7},{9,10},{10,9},{11,... | collective-permute-start | bytes 12296 | tf_op jit(solution)/shard_map/ppermute | solution.py:50
  32.4 2.9 %collective-permute-done.8.refs_2_ = f32[8,128]{1,0:T(8,128)S(1)} collective-permute-done((f32[8,128]{1,0:T(8,128)S(1)}, f32[8,128]{1,0:T(8,128)S(1)}, u32[]{:S(2)}, u32[]{:S(2)}) %collective-permute-start.8) | collective-permute-done | bytes 4128 | tf_op jit(solution)/shard_map/ppermute | solution.py:50
  36.2 2.9 %collective-permute-start.11 = (f32[8,128]{1,0:T(8,128)S(1)}, f32[8,128]{1,0:T(8,128)S(1)}, u32[]{:S(2)}, u32[]{:S(2)}) collective-permute-start(f32[8,128]{1,0:T(8,128)S(1)} %get-tuple-element.95.refs_3_), channel_id=1, source_target_pairs={{1,2},{2,1},{3,4},{4,3},{5,6},{6,5},{7,8},{8,7},{9,10},{10,9},{11,... | collective-permute-start | bytes 12296 | tf_op jit(solution)/shard_map/ppermute | solution.py:50
  44.7 2.4 collective-permute-start.14
  47.3 3.2 %collective-permute-done.14.refs_2_ = f32[8,128]{1,0:T(8,128)S(1)} collective-permute-done((f32[8,128]{1,0:T(8,128)S(1)}, f32[8,128]{1,0:T(8,128)S(1)}, u32[]{:S(2)}, u32[]{:S(2)}) %collective-permute-start.14) | collective-permute-done | bytes 4128 | tf_op jit(solution)/shard_map/ppermute | solution.py:50
  52.5 2.1 collective-permute-start.17
  55.0 3.3 %collective-permute-done.17.refs_2_ = f32[8,128]{1,0:T(8,128)S(1)} collective-permute-done((f32[8,128]{1,0:T(8,128)S(1)}, f32[8,128]{1,0:T(8,128)S(1)}, u32[]{:S(2)}, u32[]{:S(2)}) %collective-permute-start.17) | collective-permute-done | bytes 4128 | tf_op jit(solution)/shard_map/ppermute | solution.py:50
  62.8 3.2 %collective-permute-done.20.refs_2_ = f32[8,128]{1,0:T(8,128)S(1)} collective-permute-done((f32[8,128]{1,0:T(8,128)S(1)}, f32[8,128]{1,0:T(8,128)S(1)}, u32[]{:S(2)}, u32[]{:S(2)}) %collective-permute-start.20) | collective-permute-done | bytes 4128 | tf_op jit(solution)/shard_map/ppermute | solution.py:50
  67.9 1.9 collective-permute-start.23
  70.5 3.3 %collective-permute-done.23.refs_2_ = f32[8,128]{1,0:T(8,128)S(1)} collective-permute-done((f32[8,128]{1,0:T(8,128)S(1)}, f32[8,128]{1,0:T(8,128)S(1)}, u32[]{:S(2)}, u32[]{:S(2)}) %collective-permute-start.23) | collective-permute-done | bytes 4128 | tf_op jit(solution)/shard_map/ppermute | solution.py:50
  78.2 3.2 %collective-permute-done.26.refs_2_ = f32[8,128]{1,0:T(8,128)S(1)} collective-permute-done((f32[8,128]{1,0:T(8,128)S(1)}, f32[8,128]{1,0:T(8,128)S(1)}, u32[]{:S(2)}, u32[]{:S(2)}) %collective-permute-start.26) | collective-permute-done | bytes 4128 | tf_op jit(solution)/shard_map/ppermute | solution.py:50
  85.9 3.3 %collective-permute-done.29.refs_2_ = f32[8,128]{1,0:T(8,128)S(1)} collective-permute-done((f32[8,128]{1,0:T(8,128)S(1)}, f32[8,128]{1,0:T(8,128)S(1)}, u32[]{:S(2)}, u32[]{:S(2)}) %collective-permute-start.29) | collective-permute-done | bytes 4128 | tf_op jit(solution)/shard_map/ppermute | solution.py:50
  91.0 1.9 collective-permute-start.32
  93.7 3.2 %collective-permute-done.32.refs_2_ = f32[8,128]{1,0:T(8,128)S(1)} collective-permute-done((f32[8,128]{1,0:T(8,128)S(1)}, f32[8,128]{1,0:T(8,128)S(1)}, u32[]{:S(2)}, u32[]{:S(2)}) %collective-permute-start.32) | collective-permute-done | bytes 4128 | tf_op jit(solution)/shard_map/ppermute | solution.py:50
  101.4 3.3 %collective-permute-done.35.refs_2_ = f32[8,128]{1,0:T(8,128)S(1)} collective-permute-done((f32[8,128]{1,0:T(8,128)S(1)}, f32[8,128]{1,0:T(8,128)S(1)}, u32[]{:S(2)}, u32[]{:S(2)}) %collective-permute-start.35) | collective-permute-done | bytes 4128 | tf_op jit(solution)/shard_map/ppermute | solution.py:50
  109.1 3.2 %collective-permute-done.38.refs_2_ = f32[8,128]{1,0:T(8,128)S(1)} collective-permute-done((f32[8,128]{1,0:T(8,128)S(1)}, f32[8,128]{1,0:T(8,128)S(1)}, u32[]{:S(2)}, u32[]{:S(2)}) %collective-permute-start.38) | collective-permute-done | bytes 4128 | tf_op jit(solution)/shard_map/ppermute | solution.py:50
  114.3 1.9 collective-permute-start.41
  116.8 3.3 %collective-permute-done.41.refs_2_ = f32[8,128]{1,0:T(8,128)S(1)} collective-permute-done((f32[8,128]{1,0:T(8,128)S(1)}, f32[8,128]{1,0:T(8,128)S(1)}, u32[]{:S(2)}, u32[]{:S(2)}) %collective-permute-start.41) | collective-permute-done | bytes 4128 | tf_op jit(solution)/shard_map/ppermute | solution.py:50
  124.6 3.2 %collective-permute-done.44.refs_2_ = f32[8,128]{1,0:T(8,128)S(1)} collective-permute-done((f32[8,128]{1,0:T(8,128)S(1)}, f32[8,128]{1,0:T(8,128)S(1)}, u32[]{:S(2)}, u32[]{:S(2)}) %collective-permute-start.44) | collective-permute-done | bytes 4128 | tf_op jit(solution)/shard_map/ppermute | solution.py:50
  129.7 1.9 collective-permute-start.47
  132.3 3.3 %collective-permute-done.47.refs_2_ = f32[8,128]{1,0:T(8,128)S(1)} collective-permute-done((f32[8,128]{1,0:T(8,128)S(1)}, f32[8,128]{1,0:T(8,128)S(1)}, u32[]{:S(2)}, u32[]{:S(2)}) %collective-permute-start.47) | collective-permute-done | bytes 4128 | tf_op jit(solution)/shard_map/ppermute | solution.py:50
  140.0 3.2 %collective-permute-done.50.refs_2_ = f32[8,128]{1,0:T(8,128)S(1)} collective-permute-done((f32[8,128]{1,0:T(8,128)S(1)}, f32[8,128]{1,0:T(8,128)S(1)}, u32[]{:S(2)}, u32[]{:S(2)}) %collective-permute-start.50) | collective-permute-done | bytes 4128 | tf_op jit(solution)/shard_map/ppermute | solution.py:50
  145.2 1.9 collective-permute-start.53
  147.7 3.3 %collective-permute-done.53.refs_2_ = f32[8,128]{1,0:T(8,128)S(1)} collective-permute-done((f32[8,128]{1,0:T(8,128)S(1)}, f32[8,128]{1,0:T(8,128)S(1)}, u32[]{:S(2)}, u32[]{:S(2)}) %collective-permute-start.53) | collective-permute-done | bytes 4128 | tf_op jit(solution)/shard_map/ppermute | solution.py:50
  155.5 3.2 %collective-permute-done.56.refs_2_ = f32[8,128]{1,0:T(8,128)S(1)} collective-permute-done((f32[8,128]{1,0:T(8,128)S(1)}, f32[8,128]{1,0:T(8,128)S(1)}, u32[]{:S(2)}, u32[]{:S(2)}) %collective-permute-start.56) | collective-permute-done | bytes 4128 | tf_op jit(solution)/shard_map/ppermute | solution.py:50
  160.6 1.9 collective-permute-start.59
  163.2 3.3 %collective-permute-done.59.refs_2_ = f32[8,128]{1,0:T(8,128)S(1)} collective-permute-done((f32[8,128]{1,0:T(8,128)S(1)}, f32[8,128]{1,0:T(8,128)S(1)}, u32[]{:S(2)}, u32[]{:S(2)}) %collective-permute-start.59) | collective-permute-done | bytes 4128 | tf_op jit(solution)/shard_map/ppermute | solution.py:50
  170.9 3.2 %collective-permute-done.62.refs_2_ = f32[8,128]{1,0:T(8,128)S(1)} collective-permute-done((f32[8,128]{1,0:T(8,128)S(1)}, f32[8,128]{1,0:T(8,128)S(1)}, u32[]{:S(2)}, u32[]{:S(2)}) %collective-permute-start.62) | collective-permute-done | bytes 4128 | tf_op jit(solution)/shard_map/ppermute | solution.py:50
  176.1 2.1 collective-permute-start.65
  178.6 3.3 %collective-permute-done.65.refs_2_ = f32[8,128]{1,0:T(8,128)S(1)} collective-permute-done((f32[8,128]{1,0:T(8,128)S(1)}, f32[8,128]{1,0:T(8,128)S(1)}, u32[]{:S(2)}, u32[]{:S(2)}) %collective-permute-start.65) | collective-permute-done | bytes 4128 | tf_op jit(solution)/shard_map/ppermute | solution.py:50
  183.8 1.9 collective-permute-start.68
  186.4 3.2 %collective-permute-done.68.refs_2_ = f32[8,128]{1,0:T(8,128)S(1)} collective-permute-done((f32[8,128]{1,0:T(8,128)S(1)}, f32[8,128]{1,0:T(8,128)S(1)}, u32[]{:S(2)}, u32[]{:S(2)}) %collective-permute-start.68) | collective-permute-done | bytes 4128 | tf_op jit(solution)/shard_map/ppermute | solution.py:50
  194.1 3.3 %collective-permute-done.71.refs_2_ = f32[8,128]{1,0:T(8,128)S(1)} collective-permute-done((f32[8,128]{1,0:T(8,128)S(1)}, f32[8,128]{1,0:T(8,128)S(1)}, u32[]{:S(2)}, u32[]{:S(2)}) %collective-permute-start.71) | collective-permute-done | bytes 4128 | tf_op jit(solution)/shard_map/ppermute | solution.py:50
  199.2 1.9 collective-permute-start.74
  201.8 3.2 %collective-permute-done.74.refs_2_ = f32[8,128]{1,0:T(8,128)S(1)} collective-permute-done((f32[8,128]{1,0:T(8,128)S(1)}, f32[8,128]{1,0:T(8,128)S(1)}, u32[]{:S(2)}, u32[]{:S(2)}) %collective-permute-start.74) | collective-permute-done | bytes 4128 | tf_op jit(solution)/shard_map/ppermute | solution.py:50
  209.5 3.3 %collective-permute-done.77.refs_2_ = f32[8,128]{1,0:T(8,128)S(1)} collective-permute-done((f32[8,128]{1,0:T(8,128)S(1)}, f32[8,128]{1,0:T(8,128)S(1)}, u32[]{:S(2)}, u32[]{:S(2)}) %collective-permute-start.77) | collective-permute-done | bytes 4128 | tf_op jit(solution)/shard_map/ppermute | solution.py:50
  217.3 3.2 %collective-permute-done.80.refs_2_ = f32[8,128]{1,0:T(8,128)S(1)} collective-permute-done((f32[8,128]{1,0:T(8,128)S(1)}, f32[8,128]{1,0:T(8,128)S(1)}, u32[]{:S(2)}, u32[]{:S(2)}) %collective-permute-start.80) | collective-permute-done | bytes 4128 | tf_op jit(solution)/shard_map/ppermute | solution.py:50
  222.4 1.9 collective-permute-start.83
  225.0 3.3 %collective-permute-done.83.refs_2_ = f32[8,128]{1,0:T(8,128)S(1)} collective-permute-done((f32[8,128]{1,0:T(8,128)S(1)}, f32[8,128]{1,0:T(8,128)S(1)}, u32[]{:S(2)}, u32[]{:S(2)}) %collective-permute-start.83) | collective-permute-done | bytes 4128 | tf_op jit(solution)/shard_map/ppermute | solution.py:50
  232.7 3.2 %collective-permute-done.86.refs_2_ = f32[8,128]{1,0:T(8,128)S(1)} collective-permute-done((f32[8,128]{1,0:T(8,128)S(1)}, f32[8,128]{1,0:T(8,128)S(1)}, u32[]{:S(2)}, u32[]{:S(2)}) %collective-permute-start.86) | collective-permute-done | bytes 4128 | tf_op jit(solution)/shard_map/ppermute | solution.py:50
  240.4 3.3 %collective-permute-done.89.refs_2_ = f32[8,128]{1,0:T(8,128)S(1)} collective-permute-done((f32[8,128]{1,0:T(8,128)S(1)}, f32[8,128]{1,0:T(8,128)S(1)}, u32[]{:S(2)}, u32[]{:S(2)}) %collective-permute-start.89) | collective-permute-done | bytes 4128 | tf_op jit(solution)/shard_map/ppermute | solution.py:50
  245.6 1.9 collective-permute-start.92
  248.2 3.2 %collective-permute-done.92.refs_2_ = f32[8,128]{1,0:T(8,128)S(1)} collective-permute-done((f32[8,128]{1,0:T(8,128)S(1)}, f32[8,128]{1,0:T(8,128)S(1)}, u32[]{:S(2)}, u32[]{:S(2)}) %collective-permute-start.92) | collective-permute-done | bytes 4128 | tf_op jit(solution)/shard_map/ppermute | solution.py:50
  255.9 3.3 %collective-permute-done.95.refs_2_ = f32[8,128]{1,0:T(8,128)S(1)} collective-permute-done((f32[8,128]{1,0:T(8,128)S(1)}, f32[8,128]{1,0:T(8,128)S(1)}, u32[]{:S(2)}, u32[]{:S(2)}) %collective-permute-start.95) | collective-permute-done | bytes 4128 | tf_op jit(solution)/shard_map/ppermute | solution.py:50
  (200 shorter events, 120.1 us)
Async XLA Ops:
  2.6 12.1 %all-to-all-start = ((f32[1,1,16,5,512]{4,1,3,0,2:T(1,128)}), f32[1,1,16,5,512]{4,1,3,0,2:T(1,128)S(1)}, u32[]{:S(2)}, u32[]{:S(2)}) async-start(f32[1,1,16,5,512]{4,1,3,0,2:T(1,128)} %fusion), calls=%async_computation | async-start | bytes 327680 | tf_op jit(solution)/shard_map/all_to_all | solution.py:140
  8.9 6.2 %collective-permute-start = (f32[8,128]{1,0:T(8,128)}, f32[8,128]{1,0:T(8,128)S(1)}, u32[]{:S(2)}, u32[]{:S(2)}) collective-permute-start(f32[8,128]{1,0:T(8,128)} %bitcast.126), channel_id=1, source_target_pairs={{0,16},{16,0},{1,17},{17,1},{2,18},{18,2},{3,19},{19,3},{4,20},{20... | collective-permute-start | bytes 12296 | tf_op jit(solution)/shard_map/ppermute | solution.py:50
  10.4 4.7 %collective-permute-start.1 = (f32[8,128]{1,0:T(8,128)}, f32[8,128]{1,0:T(8,128)S(1)}, u32[]{:S(2)}, u32[]{:S(2)}) collective-permute-start(f32[8,128]{1,0:T(8,128)} %bitcast.127), channel_id=1, source_target_pairs={{0,1},{1,0},{2,3},{3,2},{4,5},{5,4},{6,7},{7,6},{8,9},{9,8},{10,11... | collective-permute-start | bytes 12296 | tf_op jit(solution)/shard_map/ppermute | solution.py:50
  10.4 6.0 %collective-permute-start.2 = (f32[8,128]{1,0:T(8,128)}, f32[8,128]{1,0:T(8,128)S(1)}, u32[]{:S(2)}, u32[]{:S(2)}) collective-permute-start(f32[8,128]{1,0:T(8,128)} %bitcast.128), channel_id=1, source_target_pairs={{1,2},{2,1},{3,4},{4,3},{5,6},{6,5},{7,8},{8,7},{9,10},{10,9},{11,... | collective-permute-start | bytes 12296 | tf_op jit(solution)/shard_map/ppermute | solution.py:50
  20.7 3.8 %collective-permute-start.3 = (f32[8,128]{1,0:T(8,128)S(1)}, f32[8,128]{1,0:T(8,128)S(1)}, u32[]{:S(2)}, u32[]{:S(2)}) collective-permute-start(f32[8,128]{1,0:T(8,128)S(1)} %get-tuple-element.89.refs_3_), channel_id=1, source_target_pairs={{0,16},{16,0},{1,17},{17,1},{2,18},{18,2},{3,19},{19,3},{4,20},{20... | collective-permute-start | bytes 12296 | tf_op jit(solution)/shard_map/ppermute | solution.py:50
  21.5 5.8 %collective-permute-start.5 = (f32[8,128]{1,0:T(8,128)S(1)}, f32[8,128]{1,0:T(8,128)S(1)}, u32[]{:S(2)}, u32[]{:S(2)}) collective-permute-start(f32[8,128]{1,0:T(8,128)S(1)} %get-tuple-element.89.refs_3_), channel_id=1, source_target_pairs={{1,2},{2,1},{3,4},{4,3},{5,6},{6,5},{7,8},{8,7},{9,10},{10,9},{11,... | collective-permute-start | bytes 12296 | tf_op jit(solution)/shard_map/ppermute | solution.py:50
  28.1 4.3 %collective-permute-start.6 = (f32[8,128]{1,0:T(8,128)S(1)}, f32[8,128]{1,0:T(8,128)S(1)}, u32[]{:S(2)}, u32[]{:S(2)}) collective-permute-start(f32[8,128]{1,0:T(8,128)S(1)} %get-tuple-element.92.refs_3_), channel_id=1, source_target_pairs={{0,16},{16,0},{1,17},{17,1},{2,18},{18,2},{3,19},{19,3},{4,20},{20... | collective-permute-start | bytes 12296 | tf_op jit(solution)/shard_map/ppermute | solution.py:50
  29.5 5.8 %collective-permute-start.8 = (f32[8,128]{1,0:T(8,128)S(1)}, f32[8,128]{1,0:T(8,128)S(1)}, u32[]{:S(2)}, u32[]{:S(2)}) collective-permute-start(f32[8,128]{1,0:T(8,128)S(1)} %get-tuple-element.92.refs_3_), channel_id=1, source_target_pairs={{1,2},{2,1},{3,4},{4,3},{5,6},{6,5},{7,8},{8,7},{9,10},{10,9},{11,... | collective-permute-start | bytes 12296 | tf_op jit(solution)/shard_map/ppermute | solution.py:50
  36.1 4.0 %collective-permute-start.10 = (f32[8,128]{1,0:T(8,128)S(1)}, f32[8,128]{1,0:T(8,128)S(1)}, u32[]{:S(2)}, u32[]{:S(2)}) collective-permute-start(f32[8,128]{1,0:T(8,128)S(1)} %get-tuple-element.95.refs_3_), channel_id=1, source_target_pairs={{0,1},{1,0},{2,3},{3,2},{4,5},{5,4},{6,7},{7,6},{8,9},{9,8},{10,11... | collective-permute-start | bytes 12296 | tf_op jit(solution)/shard_map/ppermute | solution.py:50
  36.2 5.8 %collective-permute-start.11 = (f32[8,128]{1,0:T(8,128)S(1)}, f32[8,128]{1,0:T(8,128)S(1)}, u32[]{:S(2)}, u32[]{:S(2)}) collective-permute-start(f32[8,128]{1,0:T(8,128)S(1)} %get-tuple-element.95.refs_3_), channel_id=1, source_target_pairs={{1,2},{2,1},{3,4},{4,3},{5,6},{6,5},{7,8},{8,7},{9,10},{10,9},{11,... | collective-permute-start | bytes 12296 | tf_op jit(solution)/shard_map/ppermute | solution.py:50
  39.1 3.7 %collective-permute-start.9 = (f32[8,128]{1,0:T(8,128)S(1)}, f32[8,128]{1,0:T(8,128)S(1)}, u32[]{:S(2)}, u32[]{:S(2)}) collective-permute-start(f32[8,128]{1,0:T(8,128)S(1)} %get-tuple-element.95.refs_3_), channel_id=1, source_target_pairs={{0,16},{16,0},{1,17},{17,1},{2,18},{18,2},{3,19},{19,3},{4,20},{20... | collective-permute-start | bytes 12296 | tf_op jit(solution)/shard_map/ppermute | solution.py:50
  43.7 3.7 %collective-permute-start.12 = (f32[8,128]{1,0:T(8,128)S(1)}, f32[8,128]{1,0:T(8,128)S(1)}, u32[]{:S(2)}, u32[]{:S(2)}) collective-permute-start(f32[8,128]{1,0:T(8,128)S(1)} %get-tuple-element.98.refs_3_), channel_id=1, source_target_pairs={{0,16},{16,0},{1,17},{17,1},{2,18},{18,2},{3,19},{19,3},{4,20},{20... | collective-permute-start | bytes 12296 | tf_op jit(solution)/shard_map/ppermute | solution.py:50
  44.7 5.8 %collective-permute-start.14 = (f32[8,128]{1,0:T(8,128)S(1)}, f32[8,128]{1,0:T(8,128)S(1)}, u32[]{:S(2)}, u32[]{:S(2)}) collective-permute-start(f32[8,128]{1,0:T(8,128)S(1)} %get-tuple-element.98.refs_3_), channel_id=1, source_target_pairs={{1,2},{2,1},{3,4},{4,3},{5,6},{6,5},{7,8},{8,7},{9,10},{10,9},{11,... | collective-permute-start | bytes 12296 | tf_op jit(solution)/shard_map/ppermute | solution.py:50
  51.3 3.7 %collective-permute-start.15 = (f32[8,128]{1,0:T(8,128)S(1)}, f32[8,128]{1,0:T(8,128)S(1)}, u32[]{:S(2)}, u32[]{:S(2)}) collective-permute-start(f32[8,128]{1,0:T(8,128)S(1)} %get-tuple-element.101.refs_3_), channel_id=1, source_target_pairs={{0,16},{16,0},{1,17},{17,1},{2,18},{18,2},{3,19},{19,3},{4,20},{20... | collective-permute-start | bytes 12296 | tf_op jit(solution)/shard_map/ppermute | solution.py:50
  52.5 5.8 %collective-permute-start.17 = (f32[8,128]{1,0:T(8,128)S(1)}, f32[8,128]{1,0:T(8,128)S(1)}, u32[]{:S(2)}, u32[]{:S(2)}) collective-permute-start(f32[8,128]{1,0:T(8,128)S(1)} %get-tuple-element.101.refs_3_), channel_id=1, source_target_pairs={{1,2},{2,1},{3,4},{4,3},{5,6},{6,5},{7,8},{8,7},{9,10},{10,9},{11,... | collective-permute-start | bytes 12296 | tf_op jit(solution)/shard_map/ppermute | solution.py:50
  59.1 3.7 %collective-permute-start.18 = (f32[8,128]{1,0:T(8,128)S(1)}, f32[8,128]{1,0:T(8,128)S(1)}, u32[]{:S(2)}, u32[]{:S(2)}) collective-permute-start(f32[8,128]{1,0:T(8,128)S(1)} %get-tuple-element.104.refs_3_), channel_id=1, source_target_pairs={{0,16},{16,0},{1,17},{17,1},{2,18},{18,2},{3,19},{19,3},{4,20},{20... | collective-permute-start | bytes 12296 | tf_op jit(solution)/shard_map/ppermute | solution.py:50
  60.1 5.8 %collective-permute-start.20 = (f32[8,128]{1,0:T(8,128)S(1)}, f32[8,128]{1,0:T(8,128)S(1)}, u32[]{:S(2)}, u32[]{:S(2)}) collective-permute-start(f32[8,128]{1,0:T(8,128)S(1)} %get-tuple-element.104.refs_3_), channel_id=1, source_target_pairs={{1,2},{2,1},{3,4},{4,3},{5,6},{6,5},{7,8},{8,7},{9,10},{10,9},{11,... | collective-permute-start | bytes 12296 | tf_op jit(solution)/shard_map/ppermute | solution.py:50
  66.8 3.7 %collective-permute-start.21 = (f32[8,128]{1,0:T(8,128)S(1)}, f32[8,128]{1,0:T(8,128)S(1)}, u32[]{:S(2)}, u32[]{:S(2)}) collective-permute-start(f32[8,128]{1,0:T(8,128)S(1)} %get-tuple-element.107.refs_3_), channel_id=1, source_target_pairs={{0,16},{16,0},{1,17},{17,1},{2,18},{18,2},{3,19},{19,3},{4,20},{20... | collective-permute-start | bytes 12296 | tf_op jit(solution)/shard_map/ppermute | solution.py:50
  67.9 5.8 %collective-permute-start.23 = (f32[8,128]{1,0:T(8,128)S(1)}, f32[8,128]{1,0:T(8,128)S(1)}, u32[]{:S(2)}, u32[]{:S(2)}) collective-permute-start(f32[8,128]{1,0:T(8,128)S(1)} %get-tuple-element.107.refs_3_), channel_id=1, source_target_pairs={{1,2},{2,1},{3,4},{4,3},{5,6},{6,5},{7,8},{8,7},{9,10},{10,9},{11,... | collective-permute-start | bytes 12296 | tf_op jit(solution)/shard_map/ppermute | solution.py:50
  74.6 3.7 %collective-permute-start.24 = (f32[8,128]{1,0:T(8,128)S(1)}, f32[8,128]{1,0:T(8,128)S(1)}, u32[]{:S(2)}, u32[]{:S(2)}) collective-permute-start(f32[8,128]{1,0:T(8,128)S(1)} %couple.39.refs_3_), channel_id=1, source_target_pairs={{0,16},{16,0},{1,17},{17,1},{2,18},{18,2},{3,19},{19,3},{4,20},{20... | collective-permute-start | bytes 12296 | tf_op jit(solution)/shard_map/ppermute | solution.py:50
  75.6 5.8 %collective-permute-start.26 = (f32[8,128]{1,0:T(8,128)S(1)}, f32[8,128]{1,0:T(8,128)S(1)}, u32[]{:S(2)}, u32[]{:S(2)}) collective-permute-start(f32[8,128]{1,0:T(8,128)S(1)} %couple.39.refs_3_), channel_id=1, source_target_pairs={{1,2},{2,1},{3,4},{4,3},{5,6},{6,5},{7,8},{8,7},{9,10},{10,9},{11,... | collective-permute-start | bytes 12296 | tf_op jit(solution)/shard_map/ppermute | solution.py:50
  82.2 3.7 %collective-permute-start.27 = (f32[8,128]{1,0:T(8,128)S(1)}, f32[8,128]{1,0:T(8,128)S(1)}, u32[]{:S(2)}, u32[]{:S(2)}) collective-permute-start(f32[8,128]{1,0:T(8,128)S(1)} %get-tuple-element.110.refs_3_), channel_id=1, source_target_pairs={{0,16},{16,0},{1,17},{17,1},{2,18},{18,2},{3,19},{19,3},{4,20},{20... | collective-permute-start | bytes 12296 | tf_op jit(solution)/shard_map/ppermute | solution.py:50
  83.4 5.8 %collective-permute-start.29 = (f32[8,128]{1,0:T(8,128)S(1)}, f32[8,128]{1,0:T(8,128)S(1)}, u32[]{:S(2)}, u32[]{:S(2)}) collective-permute-start(f32[8,128]{1,0:T(8,128)S(1)} %get-tuple-element.110.refs_3_), channel_id=1, source_target_pairs={{1,2},{2,1},{3,4},{4,3},{5,6},{6,5},{7,8},{8,7},{9,10},{10,9},{11,... | collective-permute-start | bytes 12296 | tf_op jit(solution)/shard_map/ppermute | solution.py:50
  90.0 3.7 %collective-permute-start.30 = (f32[8,128]{1,0:T(8,128)S(1)}, f32[8,128]{1,0:T(8,128)S(1)}, u32[]{:S(2)}, u32[]{:S(2)}) collective-permute-start(f32[8,128]{1,0:T(8,128)S(1)} %get-tuple-element.113.refs_3_), channel_id=1, source_target_pairs={{0,16},{16,0},{1,17},{17,1},{2,18},{18,2},{3,19},{19,3},{4,20},{20... | collective-permute-start | bytes 12296 | tf_op jit(solution)/shard_map/ppermute | solution.py:50
  91.0 5.8 %collective-permute-start.32 = (f32[8,128]{1,0:T(8,128)S(1)}, f32[8,128]{1,0:T(8,128)S(1)}, u32[]{:S(2)}, u32[]{:S(2)}) collective-permute-start(f32[8,128]{1,0:T(8,128)S(1)} %get-tuple-element.113.refs_3_), channel_id=1, source_target_pairs={{1,2},{2,1},{3,4},{4,3},{5,6},{6,5},{7,8},{8,7},{9,10},{10,9},{11,... | collective-permute-start | bytes 12296 | tf_op jit(solution)/shard_map/ppermute | solution.py:50
  98.8 5.8 %collective-permute-start.35 = (f32[8,128]{1,0:T(8,128)S(1)}, f32[8,128]{1,0:T(8,128)S(1)}, u32[]{:S(2)}, u32[]{:S(2)}) collective-permute-start(f32[8,128]{1,0:T(8,128)S(1)} %get-tuple-element.116.refs_3_), channel_id=1, source_target_pairs={{1,2},{2,1},{3,4},{4,3},{5,6},{6,5},{7,8},{8,7},{9,10},{10,9},{11,... | collective-permute-start | bytes 12296 | tf_op jit(solution)/shard_map/ppermute | solution.py:50
  106.5 5.8 %collective-permute-start.38 = (f32[8,128]{1,0:T(8,128)S(1)}, f32[8,128]{1,0:T(8,128)S(1)}, u32[]{:S(2)}, u32[]{:S(2)}) collective-permute-start(f32[8,128]{1,0:T(8,128)S(1)} %get-tuple-element.119.refs_3_), channel_id=1, source_target_pairs={{1,2},{2,1},{3,4},{4,3},{5,6},{6,5},{7,8},{8,7},{9,10},{10,9},{11,... | collective-permute-start | bytes 12296 | tf_op jit(solution)/shard_map/ppermute | solution.py:50
  114.3 5.8 %collective-permute-start.41 = (f32[8,128]{1,0:T(8,128)S(1)}, f32[8,128]{1,0:T(8,128)S(1)}, u32[]{:S(2)}, u32[]{:S(2)}) collective-permute-start(f32[8,128]{1,0:T(8,128)S(1)} %get-tuple-element.122.refs_3_), channel_id=1, source_target_pairs={{1,2},{2,1},{3,4},{4,3},{5,6},{6,5},{7,8},{8,7},{9,10},{10,9},{11,... | collective-permute-start | bytes 12296 | tf_op jit(solution)/shard_map/ppermute | solution.py:50
  121.9 5.8 %collective-permute-start.44 = (f32[8,128]{1,0:T(8,128)S(1)}, f32[8,128]{1,0:T(8,128)S(1)}, u32[]{:S(2)}, u32[]{:S(2)}) collective-permute-start(f32[8,128]{1,0:T(8,128)S(1)} %get-tuple-element.125.refs_3_), channel_id=1, source_target_pairs={{1,2},{2,1},{3,4},{4,3},{5,6},{6,5},{7,8},{8,7},{9,10},{10,9},{11,... | collective-permute-start | bytes 12296 | tf_op jit(solution)/shard_map/ppermute | solution.py:50
  129.7 5.8 %collective-permute-start.47 = (f32[8,128]{1,0:T(8,128)S(1)}, f32[8,128]{1,0:T(8,128)S(1)}, u32[]{:S(2)}, u32[]{:S(2)}) collective-permute-start(f32[8,128]{1,0:T(8,128)S(1)} %get-tuple-element.128.refs_3_), channel_id=1, source_target_pairs={{1,2},{2,1},{3,4},{4,3},{5,6},{6,5},{7,8},{8,7},{9,10},{10,9},{11,... | collective-permute-start | bytes 12296 | tf_op jit(solution)/shard_map/ppermute | solution.py:50
  137.4 5.8 %collective-permute-start.50 = (f32[8,128]{1,0:T(8,128)S(1)}, f32[8,128]{1,0:T(8,128)S(1)}, u32[]{:S(2)}, u32[]{:S(2)}) collective-permute-start(f32[8,128]{1,0:T(8,128)S(1)} %couple.47.refs_3_), channel_id=1, source_target_pairs={{1,2},{2,1},{3,4},{4,3},{5,6},{6,5},{7,8},{8,7},{9,10},{10,9},{11,... | collective-permute-start | bytes 12296 | tf_op jit(solution)/shard_map/ppermute | solution.py:50
  144.0 3.7 %collective-permute-start.51 = (f32[8,128]{1,0:T(8,128)S(1)}, f32[8,128]{1,0:T(8,128)S(1)}, u32[]{:S(2)}, u32[]{:S(2)}) collective-permute-start(f32[8,128]{1,0:T(8,128)S(1)} %get-tuple-element.131.refs_3_), channel_id=1, source_target_pairs={{0,16},{16,0},{1,17},{17,1},{2,18},{18,2},{3,19},{19,3},{4,20},{20... | collective-permute-start | bytes 12296 | tf_op jit(solution)/shard_map/ppermute | solution.py:50
  145.2 5.8 %collective-permute-start.53 = (f32[8,128]{1,0:T(8,128)S(1)}, f32[8,128]{1,0:T(8,128)S(1)}, u32[]{:S(2)}, u32[]{:S(2)}) collective-permute-start(f32[8,128]{1,0:T(8,128)S(1)} %get-tuple-element.131.refs_3_), channel_id=1, source_target_pairs={{1,2},{2,1},{3,4},{4,3},{5,6},{6,5},{7,8},{8,7},{9,10},{10,9},{11,... | collective-permute-start | bytes 12296 | tf_op jit(solution)/shard_map/ppermute | solution.py:50
  152.8 5.8 %collective-permute-start.56 = (f32[8,128]{1,0:T(8,128)S(1)}, f32[8,128]{1,0:T(8,128)S(1)}, u32[]{:S(2)}, u32[]{:S(2)}) collective-permute-start(f32[8,128]{1,0:T(8,128)S(1)} %get-tuple-element.134.refs_3_), channel_id=1, source_target_pairs={{1,2},{2,1},{3,4},{4,3},{5,6},{6,5},{7,8},{8,7},{9,10},{10,9},{11,... | collective-permute-start | bytes 12296 | tf_op jit(solution)/shard_map/ppermute | solution.py:50
  160.6 5.8 %collective-permute-start.59 = (f32[8,128]{1,0:T(8,128)S(1)}, f32[8,128]{1,0:T(8,128)S(1)}, u32[]{:S(2)}, u32[]{:S(2)}) collective-permute-start(f32[8,128]{1,0:T(8,128)S(1)} %get-tuple-element.137.refs_3_), channel_id=1, source_target_pairs={{1,2},{2,1},{3,4},{4,3},{5,6},{6,5},{7,8},{8,7},{9,10},{10,9},{11,... | collective-permute-start | bytes 12296 | tf_op jit(solution)/shard_map/ppermute | solution.py:50
  168.3 5.8 %collective-permute-start.62 = (f32[8,128]{1,0:T(8,128)S(1)}, f32[8,128]{1,0:T(8,128)S(1)}, u32[]{:S(2)}, u32[]{:S(2)}) collective-permute-start(f32[8,128]{1,0:T(8,128)S(1)} %get-tuple-element.140.refs_3_), channel_id=1, source_target_pairs={{1,2},{2,1},{3,4},{4,3},{5,6},{6,5},{7,8},{8,7},{9,10},{10,9},{11,... | collective-permute-start | bytes 12296 | tf_op jit(solution)/shard_map/ppermute | solution.py:50
  176.1 5.8 %collective-permute-start.65 = (f32[8,128]{1,0:T(8,128)S(1)}, f32[8,128]{1,0:T(8,128)S(1)}, u32[]{:S(2)}, u32[]{:S(2)}) collective-permute-start(f32[8,128]{1,0:T(8,128)S(1)} %get-tuple-element.143.refs_3_), channel_id=1, source_target_pairs={{1,2},{2,1},{3,4},{4,3},{5,6},{6,5},{7,8},{8,7},{9,10},{10,9},{11,... | collective-permute-start | bytes 12296 | tf_op jit(solution)/shard_map/ppermute | solution.py:50
  183.8 5.8 %collective-permute-start.68 = (f32[8,128]{1,0:T(8,128)S(1)}, f32[8,128]{1,0:T(8,128)S(1)}, u32[]{:S(2)}, u32[]{:S(2)}) collective-permute-start(f32[8,128]{1,0:T(8,128)S(1)} %get-tuple-element.146.refs_3_), channel_id=1, source_target_pairs={{1,2},{2,1},{3,4},{4,3},{5,6},{6,5},{7,8},{8,7},{9,10},{10,9},{11,... | collective-permute-start | bytes 12296 | tf_op jit(solution)/shard_map/ppermute | solution.py:50
  191.5 5.8 %collective-permute-start.71 = (f32[8,128]{1,0:T(8,128)S(1)}, f32[8,128]{1,0:T(8,128)S(1)}, u32[]{:S(2)}, u32[]{:S(2)}) collective-permute-start(f32[8,128]{1,0:T(8,128)S(1)} %get-tuple-element.149.refs_3_), channel_id=1, source_target_pairs={{1,2},{2,1},{3,4},{4,3},{5,6},{6,5},{7,8},{8,7},{9,10},{10,9},{11,... | collective-permute-start | bytes 12296 | tf_op jit(solution)/shard_map/ppermute | solution.py:50
  199.2 5.8 %collective-permute-start.74 = (f32[8,128]{1,0:T(8,128)S(1)}, f32[8,128]{1,0:T(8,128)S(1)}, u32[]{:S(2)}, u32[]{:S(2)}) collective-permute-start(f32[8,128]{1,0:T(8,128)S(1)} %couple.55.refs_3_), channel_id=1, source_target_pairs={{1,2},{2,1},{3,4},{4,3},{5,6},{6,5},{7,8},{8,7},{9,10},{10,9},{11,... | collective-permute-start | bytes 12296 | tf_op jit(solution)/shard_map/ppermute | solution.py:50
  205.8 3.7 %collective-permute-start.75 = (f32[8,128]{1,0:T(8,128)S(1)}, f32[8,128]{1,0:T(8,128)S(1)}, u32[]{:S(2)}, u32[]{:S(2)}) collective-permute-start(f32[8,128]{1,0:T(8,128)S(1)} %get-tuple-element.152.refs_3_), channel_id=1, source_target_pairs={{0,16},{16,0},{1,17},{17,1},{2,18},{18,2},{3,19},{19,3},{4,20},{20... | collective-permute-start | bytes 12296 | tf_op jit(solution)/shard_map/ppermute | solution.py:50
  207.0 5.8 %collective-permute-start.77 = (f32[8,128]{1,0:T(8,128)S(1)}, f32[8,128]{1,0:T(8,128)S(1)}, u32[]{:S(2)}, u32[]{:S(2)}) collective-permute-start(f32[8,128]{1,0:T(8,128)S(1)} %get-tuple-element.152.refs_3_), channel_id=1, source_target_pairs={{1,2},{2,1},{3,4},{4,3},{5,6},{6,5},{7,8},{8,7},{9,10},{10,9},{11,... | collective-permute-start | bytes 12296 | tf_op jit(solution)/shard_map/ppermute | solution.py:50
  214.7 5.8 %collective-permute-start.80 = (f32[8,128]{1,0:T(8,128)S(1)}, f32[8,128]{1,0:T(8,128)S(1)}, u32[]{:S(2)}, u32[]{:S(2)}) collective-permute-start(f32[8,128]{1,0:T(8,128)S(1)} %get-tuple-element.155.refs_3_), channel_id=1, source_target_pairs={{1,2},{2,1},{3,4},{4,3},{5,6},{6,5},{7,8},{8,7},{9,10},{10,9},{11,... | collective-permute-start | bytes 12296 | tf_op jit(solution)/shard_map/ppermute | solution.py:50
  222.4 5.8 %collective-permute-start.83 = (f32[8,128]{1,0:T(8,128)S(1)}, f32[8,128]{1,0:T(8,128)S(1)}, u32[]{:S(2)}, u32[]{:S(2)}) collective-permute-start(f32[8,128]{1,0:T(8,128)S(1)} %get-tuple-element.158.refs_3_), channel_id=1, source_target_pairs={{1,2},{2,1},{3,4},{4,3},{5,6},{6,5},{7,8},{8,7},{9,10},{10,9},{11,... | collective-permute-start | bytes 12296 | tf_op jit(solution)/shard_map/ppermute | solution.py:50
  230.1 5.8 %collective-permute-start.86 = (f32[8,128]{1,0:T(8,128)S(1)}, f32[8,128]{1,0:T(8,128)S(1)}, u32[]{:S(2)}, u32[]{:S(2)}) collective-permute-start(f32[8,128]{1,0:T(8,128)S(1)} %get-tuple-element.161.refs_3_), channel_id=1, source_target_pairs={{1,2},{2,1},{3,4},{4,3},{5,6},{6,5},{7,8},{8,7},{9,10},{10,9},{11,... | collective-permute-start | bytes 12296 | tf_op jit(solution)/shard_map/ppermute | solution.py:50
  237.9 5.8 %collective-permute-start.89 = (f32[8,128]{1,0:T(8,128)S(1)}, f32[8,128]{1,0:T(8,128)S(1)}, u32[]{:S(2)}, u32[]{:S(2)}) collective-permute-start(f32[8,128]{1,0:T(8,128)S(1)} %get-tuple-element.164.refs_3_), channel_id=1, source_target_pairs={{1,2},{2,1},{3,4},{4,3},{5,6},{6,5},{7,8},{8,7},{9,10},{10,9},{11,... | collective-permute-start | bytes 12296 | tf_op jit(solution)/shard_map/ppermute | solution.py:50
  245.6 5.8 %collective-permute-start.92 = (f32[8,128]{1,0:T(8,128)S(1)}, f32[8,128]{1,0:T(8,128)S(1)}, u32[]{:S(2)}, u32[]{:S(2)}) collective-permute-start(f32[8,128]{1,0:T(8,128)S(1)} %get-tuple-element.167.refs_3_), channel_id=1, source_target_pairs={{1,2},{2,1},{3,4},{4,3},{5,6},{6,5},{7,8},{8,7},{9,10},{10,9},{11,... | collective-permute-start | bytes 12296 | tf_op jit(solution)/shard_map/ppermute | solution.py:50
  253.3 5.8 %collective-permute-start.95 = (f32[8,128]{1,0:T(8,128)S(1)}, f32[8,128]{1,0:T(8,128)S(1)}, u32[]{:S(2)}, u32[]{:S(2)}) collective-permute-start(f32[8,128]{1,0:T(8,128)S(1)} %get-tuple-element.170.refs_3_), channel_id=1, source_target_pairs={{1,2},{2,1},{3,4},{4,3},{5,6},{6,5},{7,8},{8,7},{9,10},{10,9},{11,... | collective-permute-start | bytes 12296 | tf_op jit(solution)/shard_map/ppermute | solution.py:50
  (53 other events, 179.2 us)

commit v2 on v1

--- a/solution.py
+++ b/solution.py
@@ -123,17 +123,8 @@
             outs[0][...] = estimate
 
 
-def shards(own_block, neighbor_block, pattern, capacity, initial, currents, slot_tile):
-    tile_rows, tile_cols, width = initial.shape
-    tiles = tile_rows * tile_cols
-    n_col = lax.axis_size("col")
-    slots = currents.shape[3]
-    frames = currents.shape[4]
-    flags = jnp.stack([lax.axis_index("row") % 2, lax.axis_index("col") % 2]).astype(jnp.int32)
-
-    voltage = initial.reshape(tiles, width)
-    halos = exchange(voltage)
-
+def collect(currents, slot_tile, tiles, width):
+    slots, frames = currents.shape[3:]
     names = jnp.pad(slot_tile.astype(jnp.float32)[..., None, :],
                     ((0, 0), (0, 0), (0, 0), (0, 0), (0, frames - slots)))
     packed = jnp.concatenate([currents, names], axis=3)
@@ -141,7 +132,18 @@
     targets = arrived[:, slots, :slots]
     chooser = (targets[..., None] == jnp.arange(tiles, dtype=jnp.float32)).astype(jnp.float32)
     injected = jnp.einsum("skt,skf->tf", chooser, arrived[:, :slots], precision=lax.Precision.HIGHEST)
-    injected = injected.reshape(tiles, STEPS, width)
+    return injected.reshape(tiles, STEPS, width)
+
+
+def shards_general(own_block, neighbor_block, pattern, capacity, initial, currents, slot_tile):
+    tile_rows, tile_cols, width = initial.shape
+    tiles = tile_rows * tile_cols
+    flags = jnp.stack([lax.axis_index("row") % 2, lax.axis_index("col") % 2]).astype(jnp.int32)
+
+    voltage = initial.reshape(tiles, width)
+    halos = exchange(voltage)
+
+    injected = collect(currents, slot_tile, tiles, width)
 
     own = own_block.reshape(tiles, width, width)
     nb = neighbor_block.reshape(4, tiles, width, width)
@@ -185,9 +187,246 @@
     return jnp.stack(frames_out).reshape(STEPS, tile_rows, tile_cols, width)
 
 
+ROWS, HALF = 2, 2
+OWN, SIDE_A, SIDE_B, INNER, OUTER, FACING = 0, 4, 8, 12, 16, 18
+
+
+def ordered(x, row_dim, flip_row, flip_col, col_dim):
+    x = jnp.where(flip_row, jnp.flip(x, row_dim), x)
+    return jnp.where(flip_col, jnp.flip(x, col_dim), x)
+
+
+def tile_terms(keep, recv, j, b):
+    half, k = (keep, j) if j < ROWS else (recv, j - ROWS)
+    terms = [(half, OWN + k * HALF + b, (j, b))]
+    if j < ROWS:
+        terms.append((half, INNER + k * HALF + b, (j + 1, b)))
+        if k == 1:
+            terms.append((half, OUTER + b, (j - 1, b)))
+    else:
+        terms.append((half, INNER + k * HALF + b, (j - 1, b)))
+        if k == 0:
+            terms.append((half, OUTER + b, (j + 1, b)))
+    terms.append((half, (SIDE_A if b == 0 else SIDE_B) + k * HALF + b, (j, 1 - b)))
+    return terms
+
+
+def halo_term(keep, recv, j, b):
+    half, k = (keep, j) if j < ROWS else (recv, j - ROWS)
+    return half, (SIDE_B if b == 0 else SIDE_A) + k * HALF + b
+
+
+def facing_term(keep, recv, beyond, j, b):
+    if b == 0:
+        return beyond, j
+    return (keep, FACING + j) if j < ROWS else (recv, FACING + j - ROWS)
+
+
+def matvec(terms, chunk=32):
+    width = terms[0][2].shape[1]
+    lane = lax.broadcasted_iota(jnp.int32, (chunk, width), 1)
+    sub = lax.broadcasted_iota(jnp.int32, (chunk, width), 0)
+    spread = jnp.zeros((chunk, width), jnp.float32)
+    for g in range(0, width, chunk):
+        acc = None
+        for ref, index, vec in terms:
+            part = ref[index, g:g + chunk, :] * vec
+            acc = part if acc is None else acc + part
+        total = jnp.sum(acc, axis=1, keepdims=True)
+        spread = jnp.where(lane == sub + g, total, spread)
+    return jnp.sum(spread, axis=0, keepdims=True)
+
+
+TILES = [(j, b) for j in range(2 * ROWS) for b in range(HALF)]
+
+
+def row_of(x, j, b):
+    i = j * HALF + b
+    return x[i:i + 1]
+
+
+def inner_product(f, keep, recv):
+    return jnp.concatenate(
+        [matvec([(r, i, row_of(f, *at)) for r, i, at in tile_terms(keep, recv, j, b)]) for j, b in TILES], axis=0
+    )
+
+
+def messages(f, g):
+    def column(x, b, rows):
+        return [row_of(x, j, b) for j in rows]
+
+    rows = range(2 * ROWS)
+    to_a = jnp.concatenate(column(f, 1, rows[::-1]) + column(g, 1, rows[::-1]), axis=0)
+    to_b = jnp.concatenate(column(f, 0, rows) + column(g, 0, rows), axis=0)
+    return to_a, to_b
+
+
+def ahead(first, sweep, f, q, residue, capacity, injected):
+    if first:
+        return injected - q
+    return residue - STRIDES[sweep] * (q + capacity * f) + MOMENTA[sweep + 1] * f
+
+
+def start_kernel(keep, recv, field, injected, msg_a, msg_b, q_out):
+    f = field[...]
+    q = inner_product(f, keep, recv)
+    q_out[...] = q
+    msg_a[...], msg_b[...] = messages(f, ahead(True, 0, f, q, None, None, injected[...]))
+
+
+def pair_kernel(pair, last, keep, recv, beyond, capacity_ref, injected_ref, got_a, got_b, f_ref, q_ref, *refs):
+    first = pair == 0
+    capacity = capacity_ref[...]
+    f, q = f_ref[...], q_ref[...]
+    if not first:
+        residue, estimate, refs = refs[0][...], refs[1][...], refs[2:]
+    got = (got_b, got_a)
+    sweep = 2 * pair - 1
+    n = 2 * ROWS
+
+    extra = []
+    for j, b in TILES:
+        r, i = halo_term(keep, recv, j, b)
+        extra.append(matvec([(r, i, got[b][j:j + 1, :])]))
+    product = q + jnp.concatenate(extra, axis=0)
+    if first:
+        residue = injected_ref[...] - product
+        f2 = residue
+        estimate = f + STRIDES[0] * f2
+        scale = 1.0
+    else:
+        residue = residue - STRIDES[sweep] * (product + capacity * f)
+        f2 = residue + MOMENTA[sweep + 1] * f
+        estimate = estimate + STRIDES[sweep + 1] * f2
+        scale = STRIDES[sweep]
+
+    beside2 = {}
+    for j, b in TILES:
+        r, i = facing_term(keep, recv, beyond, j, b)
+        beside2[j, b] = got[b][n + j:n + j + 1, :] - scale * matvec([(r, i, row_of(f, j, b))])
+
+    outs = []
+    for j, b in TILES:
+        terms = [(r, i, row_of(f2, *at)) for r, i, at in tile_terms(keep, recv, j, b)]
+        r, i = halo_term(keep, recv, j, b)
+        outs.append(matvec(terms + [(r, i, beside2[j, b])]))
+    sweep = 2 * pair
+    residue = residue - STRIDES[sweep] * (jnp.concatenate(outs, axis=0) + capacity * f2)
+    f3 = residue + MOMENTA[sweep + 1] * f2
+    estimate = estimate + STRIDES[sweep + 1] * f3
+    closing = sweep + 2 == ITERS
+    if closing:
+        f3 = estimate
+    f_out, refs = refs[0], refs[1:]
+    f_out[...] = f3
+    if last:
+        return
+    q = inner_product(f3, keep, recv)
+    q_out, msg_a, msg_b = refs[:3]
+    q_out[...] = q
+    msg_a[...], msg_b[...] = messages(f3, ahead(closing, sweep + 1, f3, q, residue, capacity, injected_ref[...]))
+    if not closing:
+        refs[3][...] = residue
+        refs[4][...] = estimate
+
+
+def shards_chain(own_block, neighbor_block, pattern, capacity, initial, currents, slot_tile):
+    tile_rows, tile_cols, width = initial.shape
+    n_col = lax.axis_size("col")
+    row, col = lax.axis_index("row"), lax.axis_index("col")
+    flip_row = row == 1
+    flip_col = (row + col) % 2 == 1
+
+    def trade_row(x):
+        return lax.ppermute(x, "row", [(0, 1), (1, 0)])
+
+    b_pairs = []
+    for c in range(n_col - 1):
+        r = (c + 1) % 2
+        b_pairs += [(r * n_col + c, r * n_col + c + 1), (r * n_col + c + 1, r * n_col + c)]
+
+    def trade_next(x):
+        return lax.ppermute(x, ("row", "col"), b_pairs)
+
+    def in_order(x):
+        return ordered(x, 0, flip_row, flip_col, 1)
+
+    def split(x):
+        return x[:, :HALF], jnp.flip(x, (0, 1))[:, :HALF]
+
+    flat = (ROWS * HALF, width, width)
+    own = in_order(own_block)
+    weighted = neighbor_block * jnp.moveaxis(pattern, 2, 0).astype(jnp.float32)[..., None, None]
+    up, down, left, right = [weighted[d] for d in range(4)]
+    up, down = jnp.where(flip_row, down, up), jnp.where(flip_row, up, down)
+    side_b, side_a = jnp.where(flip_col, right, left), jnp.where(flip_col, left, right)
+    up, down, side_b, side_a = [in_order(x) for x in (up, down, side_b, side_a)]
+    own_k, own_s = split(own)
+    up_k, down_s = split(up)
+    down_k, up_s = split(down)
+    b_k, a_s = split(side_b)
+    a_k, b_s = split(side_a)
+    keep = jnp.concatenate(
+        [own_k.reshape(flat), a_k.reshape(flat), b_k.reshape(flat), down_k.reshape(flat), up_k[1], side_b[:, HALF]]
+    )
+    send = jnp.concatenate(
+        [own_s.reshape(flat), a_s.reshape(flat), b_s.reshape(flat), up_s.reshape(flat), down_s[0],
+         jnp.flip(side_a[:, HALF - 1], 0)]
+    )
+    recv = trade_row(send)
+
+    injected = collect(currents, slot_tile, tile_rows * tile_cols, width)
+    small = jnp.concatenate(
+        [injected.reshape(tile_rows, tile_cols, STEPS * width), capacity, initial], axis=2
+    )
+    small_k, small_s = split(in_order(small))
+    small = jnp.concatenate([small_k, trade_row(small_s)], axis=0).reshape(2 * ROWS * HALF, STEPS + 2, width)
+    injected, cap, field = small[:, :STEPS], small[:, STEPS], small[:, STEPS + 1]
+    beyond = trade_next(jnp.concatenate([keep[SIDE_B:SIDE_B + ROWS * HALF:HALF], recv[SIDE_B:SIDE_B + ROWS * HALF:HALF]]))
+
+    tiles = 2 * ROWS * HALF
+    shape = jax.ShapeDtypeStruct((tiles, width), jnp.float32)
+    vmem = pl.BlockSpec(memory_space=pltpu.VMEM)
+
+    def call(body, n_out, blocks, *ins):
+        return pl.pallas_call(
+            body,
+            out_shape=(shape,) * n_out,
+            in_specs=[vmem] * len(ins),
+            out_specs=(vmem,) * n_out,
+            compiler_params=pltpu.CompilerParams(vmem_limit_bytes=8 * 2**20),
+            cost_estimate=pl.CostEstimate(flops=2 * blocks * width * width, bytes_accessed=blocks * width * width * 4,
+                                          transcendentals=0),
+            name="pair",
+        )(*ins)
+
+    msg_a, msg_b, q = call(start_kernel, 3, 28, keep, recv, field, injected[:, 0])
+    frames = []
+    for instant in range(STEPS):
+        state = ()
+        for pair in range(ITERS // 2):
+            closing = pair + 1 == ITERS // 2
+            last = closing and instant + 1 == STEPS
+            got_b, got_a = trade_next(msg_b), trade_row(msg_a)
+            feed = injected[:, min(instant + closing, STEPS - 1)]
+            out = call(functools.partial(pair_kernel, pair, last), 1 if last else 4 if closing else 6, 80,
+                       keep, recv, beyond, cap, feed, got_a, got_b, field, q, *state)
+            field = out[0]
+            if not last:
+                q, msg_a, msg_b = out[1:4]
+                state = tuple(out[4:])
+        frames.append(field)
+
+    done = jnp.stack(frames).reshape(STEPS, 2 * ROWS, HALF, width)
+    got = trade_row(done[:, ROWS:])
+    done = jnp.concatenate([done[:, :ROWS], jnp.flip(got, (1, 2))], axis=2)
+    return ordered(done, 1, flip_row, flip_col, 2)
+
+
 def solution(mesh):
+    rows, cols = mesh.shape["row"], mesh.shape["col"]
     return jax.shard_map(
-        shards,
+        shards_chain if rows == 2 and cols % 2 == 0 else shards_general,
         mesh=mesh,
         in_specs=(
             P("row", "col", None, None),

time: 262 us -> 159 us (0.61)
  starting transfers between devices: 108 us -> 52.4 us
  waiting for transfers between devices: 118 us -> 75.8 us
  Pallas kernels: 26.6 us -> 11.6 us
  local copies, waits for them, and re-layouts: 4.72 us -> 12.5 us
    ppermute x96 -> x36, starting transfers between devices: 102 us -> 46.1 us  [the longest x17 41.3 us: trade_next(): return lax.ppermute(x, ('row', 'col'), b_pairs)]
    ppermute x96 -> x36, waiting for transfers between devices: 118 us -> 72.1 us  [the longest x17 36.7 us: trade_next(): return lax.ppermute(x, ('row', 'col'), b_pairs)]
    pallas_call x32 -> x17, Pallas kernels: 26.6 us -> 11.6 us  [call(): pl.pallas_call(body, out_shape=(shape,) * n_out, in_specs=[vmem] * len(in...]
    slice x2 -> x25, local copies, waits for them, and re-layouts: 0.08 us -> 5.16 us  [the longest x18 5.02 us: split(): return (x[:, :HALF], jnp.flip(x, (0, 1))[:, :HALF])]
    all_to_all x1, waiting for transfers between devices: 0.01 us -> 3.68 us  [collect(): lax.all_to_all(packed, 'col', split_axis=2, concat_axis=1, tiled=True)]
    unnamed x10 -> x35, local copies, waits for them, and re-layouts: 4.46 us -> 5.27 us
  transfers between devices with their start and end apart: 97 -> 37, of which waited for: 61 -> 34; matrix products, arithmetic and copies ran while one was open for 0% -> 3% of each run, Pallas kernels for 0% -> 0%
where the time goes in v2:
time: 159 us; the launch traced here: 158 us
  waiting for transfers between devices  75.8 us (48%)
  starting transfers between devices  52.4 us (33%)
  local copies, waits for them, and re-layouts  12.5 us (8%)
  Pallas kernels  11.6 us (7%)
  other arithmetic  4.53 us (3%)
    ppermute x17, starting transfers between devices, trade_next(): return lax.ppermute(x, ('row', 'col'), b_pairs)  41.3 us
    ppermute x17, waiting for transfers between devices, trade_next(): return lax.ppermute(x, ('row', 'col'), b_pairs)  36.7 us
    ppermute x19, waiting for transfers between devices, trade_row(): return lax.ppermute(x, 'row', [(0, 1), (1, 0)])  35.4 us
    pallas_call x17, Pallas kernels, call(): pl.pallas_call(body, out_shape=(shape,) * n_out, in_specs=[vmem] * len(in...  11.6 us
    all_to_all x1, starting transfers between devices, collect(): lax.all_to_all(packed, 'col', split_axis=2, concat_axis=1, tiled=True)  6.27 us
    unnamed x35, local copies, waits for them, and re-layouts  5.27 us
    slice x18, local copies, waits for them, and re-layouts, split(): return (x[:, :HALF], jnp.flip(x, (0, 1))[:, :HALF])  5.02 us
    ppermute x19, starting transfers between devices, trade_row(): return lax.ppermute(x, 'row', [(0, 1), (1, 0)])  4.81 us
  transfers between devices with their start and end apart: 37, of which 34 were waited for; matrix products, arithmetic and copies ran while one was open for 3% of the time, Pallas kernels for 0%

profile of v2, /device:TPU:8, one launch (start us, length us, event | category | flops | bytes accessed | tf_op | source)
XLA Modules:
  0.0 157.8 jit_solution(11655099483805972109)
XLA Ops:
  0.8 1.8 %copy_multiply_fusion = f32[4,2,4,128,128]{4,3,1,2,0:T(8,128)S(1)} fusion(f32[4,2,4,128,128]{4,3,2,1,0:T(8,128)} %param.8, f32[4,2,4]{1,2,0:T(4,128)S(1)} %copy.61), kind=kLoop, calls=%fused_computation | loop fusion | flops 524288 | bytes 4194432 | tf_op jit(solution)/shard_map/mul | solution.py:359
  11.8 1.5 collective-permute-start
  14.4 6.3 %all-to-all-start = ((f32[1,1,16,5,512]{4,1,3,0,2:T(1,128)}), f32[1,1,16,5,512]{4,1,3,0,2:T(1,128)}, u32[]{:S(2)}, u32[]{:S(2)}) async-start(f32[1,1,16,5,512]{4,1,3,0,2:T(1,128)} %fusion), calls=%async_computation | async-start | bytes 327680 | tf_op jit(solution)/shard_map/all_to_all | solution.py:131
  22.8 3.7 %all-to-all-done = f32[1,1,16,5,512]{4,1,3,0,2:T(1,128)} async-done(((f32[1,1,16,5,512]{4,1,3,0,2:T(1,128)}), f32[1,1,16,5,512]{4,1,3,0,2:T(1,128)}, u32[]{:S(2)}, u32[]{:S(2)}) %all-to-all-start) | async-done | bytes 163872 | tf_op jit(solution)/shard_map/all_to_all | solution.py:131
  28.9 13.8 %collective-permute-done.recv = f32[20,128,128]{2,1,0:T(8,128)S(1)} collective-permute-done((f32[20,128,128]{2,1,0:T(8,128)}, f32[20,128,128]{2,1,0:T(8,128)S(1)}, u32[]{:S(2)}, u32[]{:S(2)}) %collective-permute-start) | collective-permute-done | bytes 1310752 | tf_op jit(solution)/shard_map/ppermute | solution.py:341
  42.7 1.9 %collective-permute-start.1 = (f32[4,128,128]{2,1,0:T(8,128)S(1)}, f32[4,128,128]{2,1,0:T(8,128)S(1)}, u32[]{:S(2)}, u32[]{:S(2)}) collective-permute-start(f32[4,128,128]{2,1,0:T(8,128)S(1)} %pad_maximum_fusion), channel_id=1, source_target_pairs={{16,17},{17,16},{1,2},{2,1},{18,19},{19,18},{3,4},{4,3},{20,21},{2... | collective-permute-start | bytes 786440 | tf_op jit(solution)/shard_map/ppermute | solution.py:349
  45.0 1.6 %collective-permute-start.3 = (f32[8,128]{1,0:T(8,128)S(1)}, f32[8,128]{1,0:T(8,128)S(1)}, u32[]{:S(2)}, u32[]{:S(2)}) collective-permute-start(f32[8,128]{1,0:T(8,128)S(1)} %get-tuple-element.92), channel_id=1, source_target_pairs={{0,16},{16,0},{1,17},{17,1},{2,18},{18,2},{3,19},{19,3},{4,20},{20... | collective-permute-start | bytes 12296 | tf_op jit(solution)/shard_map/ppermute | solution.py:341
  46.6 3.1 %collective-permute-start.4 = (f32[8,128]{1,0:T(8,128)S(1)}, f32[8,128]{1,0:T(8,128)S(1)}, u32[]{:S(2)}, u32[]{:S(2)}) collective-permute-start(f32[8,128]{1,0:T(8,128)S(1)} %get-tuple-element.93), channel_id=1, source_target_pairs={{16,17},{17,16},{1,2},{2,1},{18,19},{19,18},{3,4},{4,3},{20,21},{2... | collective-permute-start | bytes 12296 | tf_op jit(solution)/shard_map/ppermute | solution.py:349
  49.7 2.8 %collective-permute-done.4.got_b = f32[8,128]{1,0:T(8,128)S(1)} collective-permute-done((f32[8,128]{1,0:T(8,128)S(1)}, f32[8,128]{1,0:T(8,128)S(1)}, u32[]{:S(2)}, u32[]{:S(2)}) %collective-permute-start.4) | collective-permute-done | bytes 4128 | tf_op jit(solution)/shard_map/ppermute | solution.py:349
  53.3 3.1 %collective-permute-start.6 = (f32[8,128]{1,0:T(8,128)S(1)}, f32[8,128]{1,0:T(8,128)S(1)}, u32[]{:S(2)}, u32[]{:S(2)}) collective-permute-start(f32[8,128]{1,0:T(8,128)S(1)} %get-tuple-element.96), channel_id=1, source_target_pairs={{16,17},{17,16},{1,2},{2,1},{18,19},{19,18},{3,4},{4,3},{20,21},{2... | collective-permute-start | bytes 12296 | tf_op jit(solution)/shard_map/ppermute | solution.py:349
  56.9 2.3 %collective-permute-done.6.got_b = f32[8,128]{1,0:T(8,128)S(1)} collective-permute-done((f32[8,128]{1,0:T(8,128)S(1)}, f32[8,128]{1,0:T(8,128)S(1)}, u32[]{:S(2)}, u32[]{:S(2)}) %collective-permute-start.6) | collective-permute-done | bytes 4128 | tf_op jit(solution)/shard_map/ppermute | solution.py:349
  60.0 3.1 %collective-permute-start.8 = (f32[8,128]{1,0:T(8,128)S(1)}, f32[8,128]{1,0:T(8,128)S(1)}, u32[]{:S(2)}, u32[]{:S(2)}) collective-permute-start(f32[8,128]{1,0:T(8,128)S(1)} %get-tuple-element.102), channel_id=1, source_target_pairs={{16,17},{17,16},{1,2},{2,1},{18,19},{19,18},{3,4},{4,3},{20,21},{2... | collective-permute-start | bytes 12296 | tf_op jit(solution)/shard_map/ppermute | solution.py:349
  63.6 2.2 %collective-permute-done.8.got_b = f32[8,128]{1,0:T(8,128)S(1)} collective-permute-done((f32[8,128]{1,0:T(8,128)S(1)}, f32[8,128]{1,0:T(8,128)S(1)}, u32[]{:S(2)}, u32[]{:S(2)}) %collective-permute-start.8) | collective-permute-done | bytes 4128 | tf_op jit(solution)/shard_map/ppermute | solution.py:349
  66.5 3.1 %collective-permute-start.10 = (f32[8,128]{1,0:T(8,128)S(1)}, f32[8,128]{1,0:T(8,128)S(1)}, u32[]{:S(2)}, u32[]{:S(2)}) collective-permute-start(f32[8,128]{1,0:T(8,128)S(1)} %get-tuple-element.108), channel_id=1, source_target_pairs={{16,17},{17,16},{1,2},{2,1},{18,19},{19,18},{3,4},{4,3},{20,21},{2... | collective-permute-start | bytes 12296 | tf_op jit(solution)/shard_map/ppermute | solution.py:349
  69.7 2.7 %collective-permute-done.10.got_b = f32[8,128]{1,0:T(8,128)S(1)} collective-permute-done((f32[8,128]{1,0:T(8,128)S(1)}, f32[8,128]{1,0:T(8,128)S(1)}, u32[]{:S(2)}, u32[]{:S(2)}) %collective-permute-start.10) | collective-permute-done | bytes 4128 | tf_op jit(solution)/shard_map/ppermute | solution.py:349
  74.1 2.2 %collective-permute-start.12 = (f32[8,128]{1,0:T(8,128)S(1)}, f32[8,128]{1,0:T(8,128)S(1)}, u32[]{:S(2)}, u32[]{:S(2)}) collective-permute-start(f32[8,128]{1,0:T(8,128)S(1)} %get-tuple-element.115), channel_id=1, source_target_pairs={{16,17},{17,16},{1,2},{2,1},{18,19},{19,18},{3,4},{4,3},{20,21},{2... | collective-permute-start | bytes 12296 | tf_op jit(solution)/shard_map/ppermute | solution.py:349
  76.3 1.3 collective-permute-done.11.got_a
  77.7 2.2 %collective-permute-done.12.got_b = f32[8,128]{1,0:T(8,128)S(1)} collective-permute-done((f32[8,128]{1,0:T(8,128)S(1)}, f32[8,128]{1,0:T(8,128)S(1)}, u32[]{:S(2)}, u32[]{:S(2)}) %collective-permute-start.12) | collective-permute-done | bytes 4128 | tf_op jit(solution)/shard_map/ppermute | solution.py:349
  80.7 2.2 %collective-permute-start.14 = (f32[8,128]{1,0:T(8,128)S(1)}, f32[8,128]{1,0:T(8,128)S(1)}, u32[]{:S(2)}, u32[]{:S(2)}) collective-permute-start(f32[8,128]{1,0:T(8,128)S(1)} %get-tuple-element.118), channel_id=1, source_target_pairs={{16,17},{17,16},{1,2},{2,1},{18,19},{19,18},{3,4},{4,3},{20,21},{2... | collective-permute-start | bytes 12296 | tf_op jit(solution)/shard_map/ppermute | solution.py:349
  82.9 1.3 collective-permute-done.13.got_a
  84.3 2.2 %collective-permute-done.14.got_b = f32[8,128]{1,0:T(8,128)S(1)} collective-permute-done((f32[8,128]{1,0:T(8,128)S(1)}, f32[8,128]{1,0:T(8,128)S(1)}, u32[]{:S(2)}, u32[]{:S(2)}) %collective-permute-start.14) | collective-permute-done | bytes 4128 | tf_op jit(solution)/shard_map/ppermute | solution.py:349
  87.3 2.2 %collective-permute-start.16 = (f32[8,128]{1,0:T(8,128)S(1)}, f32[8,128]{1,0:T(8,128)S(1)}, u32[]{:S(2)}, u32[]{:S(2)}) collective-permute-start(f32[8,128]{1,0:T(8,128)S(1)} %get-tuple-element.124), channel_id=1, source_target_pairs={{16,17},{17,16},{1,2},{2,1},{18,19},{19,18},{3,4},{4,3},{20,21},{2... | collective-permute-start | bytes 12296 | tf_op jit(solution)/shard_map/ppermute | solution.py:349
  89.6 1.3 collective-permute-done.15.got_a
  90.9 2.2 %collective-permute-done.16.got_b = f32[8,128]{1,0:T(8,128)S(1)} collective-permute-done((f32[8,128]{1,0:T(8,128)S(1)}, f32[8,128]{1,0:T(8,128)S(1)}, u32[]{:S(2)}, u32[]{:S(2)}) %collective-permute-start.16) | collective-permute-done | bytes 4128 | tf_op jit(solution)/shard_map/ppermute | solution.py:349
  94.0 2.2 %collective-permute-start.18 = (f32[8,128]{1,0:T(8,128)S(1)}, f32[8,128]{1,0:T(8,128)S(1)}, u32[]{:S(2)}, u32[]{:S(2)}) collective-permute-start(f32[8,128]{1,0:T(8,128)S(1)} %get-tuple-element.130), channel_id=1, source_target_pairs={{16,17},{17,16},{1,2},{2,1},{18,19},{19,18},{3,4},{4,3},{20,21},{2... | collective-permute-start | bytes 12296 | tf_op jit(solution)/shard_map/ppermute | solution.py:349
  96.2 1.3 collective-permute-done.17.got_a
  97.6 2.2 %collective-permute-done.18.got_b = f32[8,128]{1,0:T(8,128)S(1)} collective-permute-done((f32[8,128]{1,0:T(8,128)S(1)}, f32[8,128]{1,0:T(8,128)S(1)}, u32[]{:S(2)}, u32[]{:S(2)}) %collective-permute-start.18) | collective-permute-done | bytes 4128 | tf_op jit(solution)/shard_map/ppermute | solution.py:349
  100.6 2.2 %collective-permute-start.20 = (f32[8,128]{1,0:T(8,128)S(1)}, f32[8,128]{1,0:T(8,128)S(1)}, u32[]{:S(2)}, u32[]{:S(2)}) collective-permute-start(f32[8,128]{1,0:T(8,128)S(1)} %get-tuple-element.137), channel_id=1, source_target_pairs={{16,17},{17,16},{1,2},{2,1},{18,19},{19,18},{3,4},{4,3},{20,21},{2... | collective-permute-start | bytes 12296 | tf_op jit(solution)/shard_map/ppermute | solution.py:349
  102.8 1.3 collective-permute-done.19.got_a
  104.2 2.2 %collective-permute-done.20.got_b = f32[8,128]{1,0:T(8,128)S(1)} collective-permute-done((f32[8,128]{1,0:T(8,128)S(1)}, f32[8,128]{1,0:T(8,128)S(1)}, u32[]{:S(2)}, u32[]{:S(2)}) %collective-permute-start.20) | collective-permute-done | bytes 4128 | tf_op jit(solution)/shard_map/ppermute | solution.py:349
  107.2 2.2 %collective-permute-start.22 = (f32[8,128]{1,0:T(8,128)S(1)}, f32[8,128]{1,0:T(8,128)S(1)}, u32[]{:S(2)}, u32[]{:S(2)}) collective-permute-start(f32[8,128]{1,0:T(8,128)S(1)} %get-tuple-element.140), channel_id=1, source_target_pairs={{16,17},{17,16},{1,2},{2,1},{18,19},{19,18},{3,4},{4,3},{20,21},{2... | collective-permute-start | bytes 12296 | tf_op jit(solution)/shard_map/ppermute | solution.py:349
  110.8 2.2 %collective-permute-done.22.got_b = f32[8,128]{1,0:T(8,128)S(1)} collective-permute-done((f32[8,128]{1,0:T(8,128)S(1)}, f32[8,128]{1,0:T(8,128)S(1)}, u32[]{:S(2)}, u32[]{:S(2)}) %collective-permute-start.22) | collective-permute-done | bytes 4128 | tf_op jit(solution)/shard_map/ppermute | solution.py:349
  113.9 2.4 %collective-permute-start.24 = (f32[8,128]{1,0:T(8,128)S(1)}, f32[8,128]{1,0:T(8,128)S(1)}, u32[]{:S(2)}, u32[]{:S(2)}) collective-permute-start(f32[8,128]{1,0:T(8,128)S(1)} %get-tuple-element.146), channel_id=1, source_target_pairs={{16,17},{17,16},{1,2},{2,1},{18,19},{19,18},{3,4},{4,3},{20,21},{2... | collective-permute-start | bytes 12296 | tf_op jit(solution)/shard_map/ppermute | solution.py:349
  117.4 2.2 %collective-permute-done.24.got_b = f32[8,128]{1,0:T(8,128)S(1)} collective-permute-done((f32[8,128]{1,0:T(8,128)S(1)}, f32[8,128]{1,0:T(8,128)S(1)}, u32[]{:S(2)}, u32[]{:S(2)}) %collective-permute-start.24) | collective-permute-done | bytes 4128 | tf_op jit(solution)/shard_map/ppermute | solution.py:349
  120.5 2.2 %collective-permute-start.26 = (f32[8,128]{1,0:T(8,128)S(1)}, f32[8,128]{1,0:T(8,128)S(1)}, u32[]{:S(2)}, u32[]{:S(2)}) collective-permute-start(f32[8,128]{1,0:T(8,128)S(1)} %get-tuple-element.152), channel_id=1, source_target_pairs={{16,17},{17,16},{1,2},{2,1},{18,19},{19,18},{3,4},{4,3},{20,21},{2... | collective-permute-start | bytes 12296 | tf_op jit(solution)/shard_map/ppermute | solution.py:349
  122.7 1.3 collective-permute-done.25.got_a
  124.1 2.2 %collective-permute-done.26.got_b = f32[8,128]{1,0:T(8,128)S(1)} collective-permute-done((f32[8,128]{1,0:T(8,128)S(1)}, f32[8,128]{1,0:T(8,128)S(1)}, u32[]{:S(2)}, u32[]{:S(2)}) %collective-permute-start.26) | collective-permute-done | bytes 4128 | tf_op jit(solution)/shard_map/ppermute | solution.py:349
  127.1 2.2 %collective-permute-start.28 = (f32[8,128]{1,0:T(8,128)S(1)}, f32[8,128]{1,0:T(8,128)S(1)}, u32[]{:S(2)}, u32[]{:S(2)}) collective-permute-start(f32[8,128]{1,0:T(8,128)S(1)} %get-tuple-element.159), channel_id=1, source_target_pairs={{16,17},{17,16},{1,2},{2,1},{18,19},{19,18},{3,4},{4,3},{20,21},{2... | collective-permute-start | bytes 12296 | tf_op jit(solution)/shard_map/ppermute | solution.py:349
  130.7 2.2 %collective-permute-done.28.got_b = f32[8,128]{1,0:T(8,128)S(1)} collective-permute-done((f32[8,128]{1,0:T(8,128)S(1)}, f32[8,128]{1,0:T(8,128)S(1)}, u32[]{:S(2)}, u32[]{:S(2)}) %collective-permute-start.28) | collective-permute-done | bytes 4128 | tf_op jit(solution)/shard_map/ppermute | solution.py:349
  133.7 2.2 %collective-permute-start.30 = (f32[8,128]{1,0:T(8,128)S(1)}, f32[8,128]{1,0:T(8,128)S(1)}, u32[]{:S(2)}, u32[]{:S(2)}) collective-permute-start(f32[8,128]{1,0:T(8,128)S(1)} %get-tuple-element.162), channel_id=1, source_target_pairs={{16,17},{17,16},{1,2},{2,1},{18,19},{19,18},{3,4},{4,3},{20,21},{2... | collective-permute-start | bytes 12296 | tf_op jit(solution)/shard_map/ppermute | solution.py:349
  136.0 1.3 collective-permute-done.29.got_a
  137.3 2.2 %collective-permute-done.30.got_b = f32[8,128]{1,0:T(8,128)S(1)} collective-permute-done((f32[8,128]{1,0:T(8,128)S(1)}, f32[8,128]{1,0:T(8,128)S(1)}, u32[]{:S(2)}, u32[]{:S(2)}) %collective-permute-start.30) | collective-permute-done | bytes 4128 | tf_op jit(solution)/shard_map/ppermute | solution.py:349
  140.4 2.2 %collective-permute-start.32 = (f32[8,128]{1,0:T(8,128)S(1)}, f32[8,128]{1,0:T(8,128)S(1)}, u32[]{:S(2)}, u32[]{:S(2)}) collective-permute-start(f32[8,128]{1,0:T(8,128)S(1)} %get-tuple-element.168), channel_id=1, source_target_pairs={{16,17},{17,16},{1,2},{2,1},{18,19},{19,18},{3,4},{4,3},{20,21},{2... | collective-permute-start | bytes 12296 | tf_op jit(solution)/shard_map/ppermute | solution.py:349
  144.0 2.2 %collective-permute-done.32.got_b = f32[8,128]{1,0:T(8,128)S(1)} collective-permute-done((f32[8,128]{1,0:T(8,128)S(1)}, f32[8,128]{1,0:T(8,128)S(1)}, u32[]{:S(2)}, u32[]{:S(2)}) %collective-permute-start.32) | collective-permute-done | bytes 4128 | tf_op jit(solution)/shard_map/ppermute | solution.py:349
  147.0 2.2 %collective-permute-start.34 = (f32[8,128]{1,0:T(8,128)S(1)}, f32[8,128]{1,0:T(8,128)S(1)}, u32[]{:S(2)}, u32[]{:S(2)}) collective-permute-start(f32[8,128]{1,0:T(8,128)S(1)} %get-tuple-element.174), channel_id=1, source_target_pairs={{16,17},{17,16},{1,2},{2,1},{18,19},{19,18},{3,4},{4,3},{20,21},{2... | collective-permute-start | bytes 12296 | tf_op jit(solution)/shard_map/ppermute | solution.py:349
  149.2 1.3 collective-permute-done.33.got_a
  150.6 2.2 %collective-permute-done.34.got_b = f32[8,128]{1,0:T(8,128)S(1)} collective-permute-done((f32[8,128]{1,0:T(8,128)S(1)}, f32[8,128]{1,0:T(8,128)S(1)}, u32[]{:S(2)}, u32[]{:S(2)}) %collective-permute-start.34) | collective-permute-done | bytes 4128 | tf_op jit(solution)/shard_map/ppermute | solution.py:349
  153.4 3.6 %collective-permute-done.35 = f32[4,2,2,128]{3,2,1,0:T(2,128)S(1)} collective-permute-done((f32[4,2,2,128]{3,2,1,0:T(2,128)S(1)}, f32[4,2,2,128]{3,2,1,0:T(2,128)S(1)}, u32[]{:S(2)}, u32[]{:S(2)}) %collective-permute-start.35) | collective-permute-done | bytes 8224 | tf_op jit(solution)/shard_map/ppermute | solution.py:341
  (136 shorter events, 35.8 us)
Async XLA Ops:
  3.7 1.1 copy-start.5
  8.1 1.0 copy-start.1
  8.2 3.0 %copy-start = (f32[2,4,128,128]{3,2,0,1:T(8,128)}, f32[2,4,128,128]{3,2,0,1:T(8,128)S(1)}, u32[]{:S(2)}) copy-start(f32[2,4,128,128]{3,2,0,1:T(8,128)S(1)} %reverse_select_fusion) | copy-start | bytes 1572868
  8.2 5.1 %copy-start.6 = (f32[1,1,16,4,512]{4,3,2,1,0:T(4,128)S(1)}, f32[1,1,16,4,512]{4,3,2,1,0:T(4,128)}, u32[]{:S(2)}) copy-start(f32[1,1,16,4,512]{4,3,2,1,0:T(4,128)} %param.12) | copy-start | bytes 393220
  8.2 5.3 %copy-start.9 = (s32[1,1,16,4]{2,3,1,0:T(4,128)S(1)}, s32[1,1,16,4]{2,3,1,0:T(4,128)}, u32[]{:S(2)}) copy-start(s32[1,1,16,4]{2,3,1,0:T(4,128)} %param.13) | copy-start | bytes 772
  9.0 11.7 %copy-start.2 = (f32[2,2,128,128]{3,2,0,1:T(8,128)S(1)}, f32[2,2,128,128]{3,2,0,1:T(8,128)}, u32[]{:S(2)}) copy-start(f32[2,2,128,128]{3,2,0,1:T(8,128)} %get-tuple-element.186) | copy-start | bytes 786436
  9.8 10.9 %copy-start.4 = (f32[2,2,128,128]{3,2,0,1:T(8,128)S(1)}, f32[2,2,128,128]{3,2,0,1:T(8,128)}, u32[]{:S(2)}) copy-start(f32[2,2,128,128]{3,2,0,1:T(8,128)} %get-tuple-element.190) | copy-start | bytes 786436
  11.2 9.6 %copy-start.3 = (f32[2,2,128,128]{3,2,0,1:T(8,128)S(1)}, f32[2,2,128,128]{3,2,0,1:T(8,128)}, u32[]{:S(2)}) copy-start(f32[2,2,128,128]{3,2,0,1:T(8,128)} %get-tuple-element.188) | copy-start | bytes 786436
  11.8 30.9 %collective-permute-start = (f32[20,128,128]{2,1,0:T(8,128)}, f32[20,128,128]{2,1,0:T(8,128)S(1)}, u32[]{:S(2)}, u32[]{:S(2)}) collective-permute-start(f32[20,128,128]{2,1,0:T(8,128)} %reverse_dynamic-update-slice_fusion), channel_id=1, source_target_pairs={{0,16},{16,0},{1,17},{17,1},{2,18},{18,2},{3,19},{19,3},{4,20},{20... | collective-permute-start | bytes 3932168 | tf_op jit(solution)/shard_map/ppermute | solution.py:341
  14.4 12.1 %all-to-all-start = ((f32[1,1,16,5,512]{4,1,3,0,2:T(1,128)}), f32[1,1,16,5,512]{4,1,3,0,2:T(1,128)}, u32[]{:S(2)}, u32[]{:S(2)}) async-start(f32[1,1,16,5,512]{4,1,3,0,2:T(1,128)} %fusion), calls=%async_computation | async-start | bytes 327680 | tf_op jit(solution)/shard_map/all_to_all | solution.py:131
  21.8 6.0 %copy-start.7 = (f32[2,4,128]{2,1,0:T(4,128)S(1)}, f32[2,4,128]{2,1,0:T(4,128)}, u32[]{:S(2)}) copy-start(f32[2,4,128]{2,1,0:T(4,128)} %param.10) | copy-start | bytes 12292
  21.8 6.0 %copy-start.8 = (f32[2,4,128]{2,1,0:T(4,128)S(1)}, f32[2,4,128]{2,1,0:T(4,128)}, u32[]{:S(2)}) copy-start(f32[2,4,128]{2,1,0:T(4,128)} %param.11) | copy-start | bytes 12292
  28.3 16.4 %collective-permute-start.2 = (f32[2,2,768]{2,1,0:T(2,128)S(1)}, f32[2,2,768]{2,1,0:T(2,128)S(1)}, u32[]{:S(2)}, u32[]{:S(2)}) collective-permute-start(f32[2,2,768]{2,1,0:T(2,128)S(1)} %slice.158), channel_id=1, source_target_pairs={{0,16},{16,0},{1,17},{17,1},{2,18},{18,2},{3,19},{19,3},{4,20},{20... | collective-permute-start | bytes 36872 | tf_op jit(solution)/shard_map/ppermute | solution.py:341
  42.7 9.8 %collective-permute-start.1 = (f32[4,128,128]{2,1,0:T(8,128)S(1)}, f32[4,128,128]{2,1,0:T(8,128)S(1)}, u32[]{:S(2)}, u32[]{:S(2)}) collective-permute-start(f32[4,128,128]{2,1,0:T(8,128)S(1)} %pad_maximum_fusion), channel_id=1, source_target_pairs={{16,17},{17,16},{1,2},{2,1},{18,19},{19,18},{3,4},{4,3},{20,21},{2... | collective-permute-start | bytes 786440 | tf_op jit(solution)/shard_map/ppermute | solution.py:349
  45.0 4.7 %collective-permute-start.3 = (f32[8,128]{1,0:T(8,128)S(1)}, f32[8,128]{1,0:T(8,128)S(1)}, u32[]{:S(2)}, u32[]{:S(2)}) collective-permute-start(f32[8,128]{1,0:T(8,128)S(1)} %get-tuple-element.92), channel_id=1, source_target_pairs={{0,16},{16,0},{1,17},{17,1},{2,18},{18,2},{3,19},{19,3},{4,20},{20... | collective-permute-start | bytes 12296 | tf_op jit(solution)/shard_map/ppermute | solution.py:341
  46.6 5.9 %collective-permute-start.4 = (f32[8,128]{1,0:T(8,128)S(1)}, f32[8,128]{1,0:T(8,128)S(1)}, u32[]{:S(2)}, u32[]{:S(2)}) collective-permute-start(f32[8,128]{1,0:T(8,128)S(1)} %get-tuple-element.93), channel_id=1, source_target_pairs={{16,17},{17,16},{1,2},{2,1},{18,19},{19,18},{3,4},{4,3},{20,21},{2... | collective-permute-start | bytes 12296 | tf_op jit(solution)/shard_map/ppermute | solution.py:349
  53.2 3.7 %collective-permute-start.5 = (f32[8,128]{1,0:T(8,128)S(1)}, f32[8,128]{1,0:T(8,128)S(1)}, u32[]{:S(2)}, u32[]{:S(2)}) collective-permute-start(f32[8,128]{1,0:T(8,128)S(1)} %get-tuple-element.95), channel_id=1, source_target_pairs={{0,16},{16,0},{1,17},{17,1},{2,18},{18,2},{3,19},{19,3},{4,20},{20... | collective-permute-start | bytes 12296 | tf_op jit(solution)/shard_map/ppermute | solution.py:341
  53.3 5.9 %collective-permute-start.6 = (f32[8,128]{1,0:T(8,128)S(1)}, f32[8,128]{1,0:T(8,128)S(1)}, u32[]{:S(2)}, u32[]{:S(2)}) collective-permute-start(f32[8,128]{1,0:T(8,128)S(1)} %get-tuple-element.96), channel_id=1, source_target_pairs={{16,17},{17,16},{1,2},{2,1},{18,19},{19,18},{3,4},{4,3},{20,21},{2... | collective-permute-start | bytes 12296 | tf_op jit(solution)/shard_map/ppermute | solution.py:349
  59.9 3.7 %collective-permute-start.7 = (f32[8,128]{1,0:T(8,128)S(1)}, f32[8,128]{1,0:T(8,128)S(1)}, u32[]{:S(2)}, u32[]{:S(2)}) collective-permute-start(f32[8,128]{1,0:T(8,128)S(1)} %get-tuple-element.101), channel_id=1, source_target_pairs={{0,16},{16,0},{1,17},{17,1},{2,18},{18,2},{3,19},{19,3},{4,20},{20... | collective-permute-start | bytes 12296 | tf_op jit(solution)/shard_map/ppermute | solution.py:341
  60.0 5.8 %collective-permute-start.8 = (f32[8,128]{1,0:T(8,128)S(1)}, f32[8,128]{1,0:T(8,128)S(1)}, u32[]{:S(2)}, u32[]{:S(2)}) collective-permute-start(f32[8,128]{1,0:T(8,128)S(1)} %get-tuple-element.102), channel_id=1, source_target_pairs={{16,17},{17,16},{1,2},{2,1},{18,19},{19,18},{3,4},{4,3},{20,21},{2... | collective-permute-start | bytes 12296 | tf_op jit(solution)/shard_map/ppermute | solution.py:349
  66.5 5.8 %collective-permute-start.10 = (f32[8,128]{1,0:T(8,128)S(1)}, f32[8,128]{1,0:T(8,128)S(1)}, u32[]{:S(2)}, u32[]{:S(2)}) collective-permute-start(f32[8,128]{1,0:T(8,128)S(1)} %get-tuple-element.108), channel_id=1, source_target_pairs={{16,17},{17,16},{1,2},{2,1},{18,19},{19,18},{3,4},{4,3},{20,21},{2... | collective-permute-start | bytes 12296 | tf_op jit(solution)/shard_map/ppermute | solution.py:349
  69.6 3.7 %collective-permute-start.9 = (f32[8,128]{1,0:T(8,128)S(1)}, f32[8,128]{1,0:T(8,128)S(1)}, u32[]{:S(2)}, u32[]{:S(2)}) collective-permute-start(f32[8,128]{1,0:T(8,128)S(1)} %get-tuple-element.107), channel_id=1, source_target_pairs={{0,16},{16,0},{1,17},{17,1},{2,18},{18,2},{3,19},{19,3},{4,20},{20... | collective-permute-start | bytes 12296 | tf_op jit(solution)/shard_map/ppermute | solution.py:341
  74.0 3.7 %collective-permute-start.11 = (f32[8,128]{1,0:T(8,128)S(1)}, f32[8,128]{1,0:T(8,128)S(1)}, u32[]{:S(2)}, u32[]{:S(2)}) collective-permute-start(f32[8,128]{1,0:T(8,128)S(1)} %get-tuple-element.114), channel_id=1, source_target_pairs={{0,16},{16,0},{1,17},{17,1},{2,18},{18,2},{3,19},{19,3},{4,20},{20... | collective-permute-start | bytes 12296 | tf_op jit(solution)/shard_map/ppermute | solution.py:341
  74.1 5.8 %collective-permute-start.12 = (f32[8,128]{1,0:T(8,128)S(1)}, f32[8,128]{1,0:T(8,128)S(1)}, u32[]{:S(2)}, u32[]{:S(2)}) collective-permute-start(f32[8,128]{1,0:T(8,128)S(1)} %get-tuple-element.115), channel_id=1, source_target_pairs={{16,17},{17,16},{1,2},{2,1},{18,19},{19,18},{3,4},{4,3},{20,21},{2... | collective-permute-start | bytes 12296 | tf_op jit(solution)/shard_map/ppermute | solution.py:349
  80.6 3.7 %collective-permute-start.13 = (f32[8,128]{1,0:T(8,128)S(1)}, f32[8,128]{1,0:T(8,128)S(1)}, u32[]{:S(2)}, u32[]{:S(2)}) collective-permute-start(f32[8,128]{1,0:T(8,128)S(1)} %get-tuple-element.117), channel_id=1, source_target_pairs={{0,16},{16,0},{1,17},{17,1},{2,18},{18,2},{3,19},{19,3},{4,20},{20... | collective-permute-start | bytes 12296 | tf_op jit(solution)/shard_map/ppermute | solution.py:341
  80.7 5.8 %collective-permute-start.14 = (f32[8,128]{1,0:T(8,128)S(1)}, f32[8,128]{1,0:T(8,128)S(1)}, u32[]{:S(2)}, u32[]{:S(2)}) collective-permute-start(f32[8,128]{1,0:T(8,128)S(1)} %get-tuple-element.118), channel_id=1, source_target_pairs={{16,17},{17,16},{1,2},{2,1},{18,19},{19,18},{3,4},{4,3},{20,21},{2... | collective-permute-start | bytes 12296 | tf_op jit(solution)/shard_map/ppermute | solution.py:349
  87.3 3.7 %collective-permute-start.15 = (f32[8,128]{1,0:T(8,128)S(1)}, f32[8,128]{1,0:T(8,128)S(1)}, u32[]{:S(2)}, u32[]{:S(2)}) collective-permute-start(f32[8,128]{1,0:T(8,128)S(1)} %get-tuple-element.123), channel_id=1, source_target_pairs={{0,16},{16,0},{1,17},{17,1},{2,18},{18,2},{3,19},{19,3},{4,20},{20... | collective-permute-start | bytes 12296 | tf_op jit(solution)/shard_map/ppermute | solution.py:341
  87.3 5.8 %collective-permute-start.16 = (f32[8,128]{1,0:T(8,128)S(1)}, f32[8,128]{1,0:T(8,128)S(1)}, u32[]{:S(2)}, u32[]{:S(2)}) collective-permute-start(f32[8,128]{1,0:T(8,128)S(1)} %get-tuple-element.124), channel_id=1, source_target_pairs={{16,17},{17,16},{1,2},{2,1},{18,19},{19,18},{3,4},{4,3},{20,21},{2... | collective-permute-start | bytes 12296 | tf_op jit(solution)/shard_map/ppermute | solution.py:349
  93.9 3.7 %collective-permute-start.17 = (f32[8,128]{1,0:T(8,128)S(1)}, f32[8,128]{1,0:T(8,128)S(1)}, u32[]{:S(2)}, u32[]{:S(2)}) collective-permute-start(f32[8,128]{1,0:T(8,128)S(1)} %get-tuple-element.129), channel_id=1, source_target_pairs={{0,16},{16,0},{1,17},{17,1},{2,18},{18,2},{3,19},{19,3},{4,20},{20... | collective-permute-start | bytes 12296 | tf_op jit(solution)/shard_map/ppermute | solution.py:341
  94.0 5.8 %collective-permute-start.18 = (f32[8,128]{1,0:T(8,128)S(1)}, f32[8,128]{1,0:T(8,128)S(1)}, u32[]{:S(2)}, u32[]{:S(2)}) collective-permute-start(f32[8,128]{1,0:T(8,128)S(1)} %get-tuple-element.130), channel_id=1, source_target_pairs={{16,17},{17,16},{1,2},{2,1},{18,19},{19,18},{3,4},{4,3},{20,21},{2... | collective-permute-start | bytes 12296 | tf_op jit(solution)/shard_map/ppermute | solution.py:349
  100.5 3.7 %collective-permute-start.19 = (f32[8,128]{1,0:T(8,128)S(1)}, f32[8,128]{1,0:T(8,128)S(1)}, u32[]{:S(2)}, u32[]{:S(2)}) collective-permute-start(f32[8,128]{1,0:T(8,128)S(1)} %get-tuple-element.136), channel_id=1, source_target_pairs={{0,16},{16,0},{1,17},{17,1},{2,18},{18,2},{3,19},{19,3},{4,20},{20... | collective-permute-start | bytes 12296 | tf_op jit(solution)/shard_map/ppermute | solution.py:341
  100.6 5.8 %collective-permute-start.20 = (f32[8,128]{1,0:T(8,128)S(1)}, f32[8,128]{1,0:T(8,128)S(1)}, u32[]{:S(2)}, u32[]{:S(2)}) collective-permute-start(f32[8,128]{1,0:T(8,128)S(1)} %get-tuple-element.137), channel_id=1, source_target_pairs={{16,17},{17,16},{1,2},{2,1},{18,19},{19,18},{3,4},{4,3},{20,21},{2... | collective-permute-start | bytes 12296 | tf_op jit(solution)/shard_map/ppermute | solution.py:349
  107.1 3.7 %collective-permute-start.21 = (f32[8,128]{1,0:T(8,128)S(1)}, f32[8,128]{1,0:T(8,128)S(1)}, u32[]{:S(2)}, u32[]{:S(2)}) collective-permute-start(f32[8,128]{1,0:T(8,128)S(1)} %get-tuple-element.139), channel_id=1, source_target_pairs={{0,16},{16,0},{1,17},{17,1},{2,18},{18,2},{3,19},{19,3},{4,20},{20... | collective-permute-start | bytes 12296 | tf_op jit(solution)/shard_map/ppermute | solution.py:341
  107.2 5.8 %collective-permute-start.22 = (f32[8,128]{1,0:T(8,128)S(1)}, f32[8,128]{1,0:T(8,128)S(1)}, u32[]{:S(2)}, u32[]{:S(2)}) collective-permute-start(f32[8,128]{1,0:T(8,128)S(1)} %get-tuple-element.140), channel_id=1, source_target_pairs={{16,17},{17,16},{1,2},{2,1},{18,19},{19,18},{3,4},{4,3},{20,21},{2... | collective-permute-start | bytes 12296 | tf_op jit(solution)/shard_map/ppermute | solution.py:349
  113.8 3.7 %collective-permute-start.23 = (f32[8,128]{1,0:T(8,128)S(1)}, f32[8,128]{1,0:T(8,128)S(1)}, u32[]{:S(2)}, u32[]{:S(2)}) collective-permute-start(f32[8,128]{1,0:T(8,128)S(1)} %get-tuple-element.145), channel_id=1, source_target_pairs={{0,16},{16,0},{1,17},{17,1},{2,18},{18,2},{3,19},{19,3},{4,20},{20... | collective-permute-start | bytes 12296 | tf_op jit(solution)/shard_map/ppermute | solution.py:341
  113.9 5.8 %collective-permute-start.24 = (f32[8,128]{1,0:T(8,128)S(1)}, f32[8,128]{1,0:T(8,128)S(1)}, u32[]{:S(2)}, u32[]{:S(2)}) collective-permute-start(f32[8,128]{1,0:T(8,128)S(1)} %get-tuple-element.146), channel_id=1, source_target_pairs={{16,17},{17,16},{1,2},{2,1},{18,19},{19,18},{3,4},{4,3},{20,21},{2... | collective-permute-start | bytes 12296 | tf_op jit(solution)/shard_map/ppermute | solution.py:349
  120.4 3.7 %collective-permute-start.25 = (f32[8,128]{1,0:T(8,128)S(1)}, f32[8,128]{1,0:T(8,128)S(1)}, u32[]{:S(2)}, u32[]{:S(2)}) collective-permute-start(f32[8,128]{1,0:T(8,128)S(1)} %get-tuple-element.151), channel_id=1, source_target_pairs={{0,16},{16,0},{1,17},{17,1},{2,18},{18,2},{3,19},{19,3},{4,20},{20... | collective-permute-start | bytes 12296 | tf_op jit(solution)/shard_map/ppermute | solution.py:341
  120.5 5.8 %collective-permute-start.26 = (f32[8,128]{1,0:T(8,128)S(1)}, f32[8,128]{1,0:T(8,128)S(1)}, u32[]{:S(2)}, u32[]{:S(2)}) collective-permute-start(f32[8,128]{1,0:T(8,128)S(1)} %get-tuple-element.152), channel_id=1, source_target_pairs={{16,17},{17,16},{1,2},{2,1},{18,19},{19,18},{3,4},{4,3},{20,21},{2... | collective-permute-start | bytes 12296 | tf_op jit(solution)/shard_map/ppermute | solution.py:349
  127.0 3.7 %collective-permute-start.27 = (f32[8,128]{1,0:T(8,128)S(1)}, f32[8,128]{1,0:T(8,128)S(1)}, u32[]{:S(2)}, u32[]{:S(2)}) collective-permute-start(f32[8,128]{1,0:T(8,128)S(1)} %get-tuple-element.158), channel_id=1, source_target_pairs={{0,16},{16,0},{1,17},{17,1},{2,18},{18,2},{3,19},{19,3},{4,20},{20... | collective-permute-start | bytes 12296 | tf_op jit(solution)/shard_map/ppermute | solution.py:341
  127.1 5.8 %collective-permute-start.28 = (f32[8,128]{1,0:T(8,128)S(1)}, f32[8,128]{1,0:T(8,128)S(1)}, u32[]{:S(2)}, u32[]{:S(2)}) collective-permute-start(f32[8,128]{1,0:T(8,128)S(1)} %get-tuple-element.159), channel_id=1, source_target_pairs={{16,17},{17,16},{1,2},{2,1},{18,19},{19,18},{3,4},{4,3},{20,21},{2... | collective-permute-start | bytes 12296 | tf_op jit(solution)/shard_map/ppermute | solution.py:349
  133.7 3.7 %collective-permute-start.29 = (f32[8,128]{1,0:T(8,128)S(1)}, f32[8,128]{1,0:T(8,128)S(1)}, u32[]{:S(2)}, u32[]{:S(2)}) collective-permute-start(f32[8,128]{1,0:T(8,128)S(1)} %get-tuple-element.161), channel_id=1, source_target_pairs={{0,16},{16,0},{1,17},{17,1},{2,18},{18,2},{3,19},{19,3},{4,20},{20... | collective-permute-start | bytes 12296 | tf_op jit(solution)/shard_map/ppermute | solution.py:341
  133.7 5.8 %collective-permute-start.30 = (f32[8,128]{1,0:T(8,128)S(1)}, f32[8,128]{1,0:T(8,128)S(1)}, u32[]{:S(2)}, u32[]{:S(2)}) collective-permute-start(f32[8,128]{1,0:T(8,128)S(1)} %get-tuple-element.162), channel_id=1, source_target_pairs={{16,17},{17,16},{1,2},{2,1},{18,19},{19,18},{3,4},{4,3},{20,21},{2... | collective-permute-start | bytes 12296 | tf_op jit(solution)/shard_map/ppermute | solution.py:349
  140.3 3.7 %collective-permute-start.31 = (f32[8,128]{1,0:T(8,128)S(1)}, f32[8,128]{1,0:T(8,128)S(1)}, u32[]{:S(2)}, u32[]{:S(2)}) collective-permute-start(f32[8,128]{1,0:T(8,128)S(1)} %get-tuple-element.167), channel_id=1, source_target_pairs={{0,16},{16,0},{1,17},{17,1},{2,18},{18,2},{3,19},{19,3},{4,20},{20... | collective-permute-start | bytes 12296 | tf_op jit(solution)/shard_map/ppermute | solution.py:341
  140.4 5.8 %collective-permute-start.32 = (f32[8,128]{1,0:T(8,128)S(1)}, f32[8,128]{1,0:T(8,128)S(1)}, u32[]{:S(2)}, u32[]{:S(2)}) collective-permute-start(f32[8,128]{1,0:T(8,128)S(1)} %get-tuple-element.168), channel_id=1, source_target_pairs={{16,17},{17,16},{1,2},{2,1},{18,19},{19,18},{3,4},{4,3},{20,21},{2... | collective-permute-start | bytes 12296 | tf_op jit(solution)/shard_map/ppermute | solution.py:349
  146.9 3.7 %collective-permute-start.33 = (f32[8,128]{1,0:T(8,128)S(1)}, f32[8,128]{1,0:T(8,128)S(1)}, u32[]{:S(2)}, u32[]{:S(2)}) collective-permute-start(f32[8,128]{1,0:T(8,128)S(1)} %get-tuple-element.173), channel_id=1, source_target_pairs={{0,16},{16,0},{1,17},{17,1},{2,18},{18,2},{3,19},{19,3},{4,20},{20... | collective-permute-start | bytes 12296 | tf_op jit(solution)/shard_map/ppermute | solution.py:341
  147.0 5.8 %collective-permute-start.34 = (f32[8,128]{1,0:T(8,128)S(1)}, f32[8,128]{1,0:T(8,128)S(1)}, u32[]{:S(2)}, u32[]{:S(2)}) collective-permute-start(f32[8,128]{1,0:T(8,128)S(1)} %get-tuple-element.174), channel_id=1, source_target_pairs={{16,17},{17,16},{1,2},{2,1},{18,19},{19,18},{3,4},{4,3},{20,21},{2... | collective-permute-start | bytes 12296 | tf_op jit(solution)/shard_map/ppermute | solution.py:349
  153.4 3.7 %collective-permute-start.35 = (f32[4,2,2,128]{3,2,1,0:T(2,128)S(1)}, f32[4,2,2,128]{3,2,1,0:T(2,128)S(1)}, u32[]{:S(2)}, u32[]{:S(2)}) collective-permute-start(f32[4,2,2,128]{3,2,1,0:T(2,128)S(1)} %get-tuple-element.200), channel_id=1, source_target_pairs={{0,16},{16,0},{1,17},{17,1},{2,18},{18,2},{3,19},{19,3},{4,20},{20... | collective-permute-start | bytes 24584 | tf_op jit(solution)/shard_map/ppermute | solution.py:341

commit v3 on v2

--- a/solution.py
+++ b/solution.py
@@ -188,38 +188,80 @@
 
 
 ROWS, HALF = 2, 2
-OWN, SIDE_A, SIDE_B, INNER, OUTER, FACING = 0, 4, 8, 12, 16, 18
-
-
-def ordered(x, row_dim, flip_row, flip_col, col_dim):
-    x = jnp.where(flip_row, jnp.flip(x, row_dim), x)
-    return jnp.where(flip_col, jnp.flip(x, col_dim), x)
-
-
-def tile_terms(keep, recv, j, b):
-    half, k = (keep, j) if j < ROWS else (recv, j - ROWS)
-    terms = [(half, OWN + k * HALF + b, (j, b))]
-    if j < ROWS:
-        terms.append((half, INNER + k * HALF + b, (j + 1, b)))
-        if k == 1:
-            terms.append((half, OUTER + b, (j - 1, b)))
+N = 2 * ROWS
+OWN, SIDE_A, SIDE_B, OUT_IN, IN_OUT, IN_IN, FACING, PACKED = 0, 4, 8, 12, 14, 16, 18, 20
+TILES = [(j, b) for j in range(N) for b in range(HALF)]
+ORIGIN = [(0, 0), (0, 1), (1, 1), (1, 0)]
+
+
+def unit_device(unit, n_col):
+    group, place = divmod(unit // 2, 4)
+    x, row = ((0, 0), (1, 0), (1, 1), (0, 1))[place]
+    return (row + group) % 2 * n_col + 4 * group + 2 * x + unit % 2
+
+
+def deal_pairs(n_col, which):
+    rounds = []
+    for i in (0, 1):
+        pairs = []
+        for row in (0, 1):
+            for col in range(n_col):
+                k = row ^ i
+                unit = 2 * col + k if which == 0 else 2 * col + (2 if k == 0 else -1)
+                if 0 <= unit < 2 * n_col:
+                    pairs.append((row * n_col + col, unit_device(unit, n_col)))
+        rounds.append(pairs)
+    return rounds
+
+
+def pack_kernel(row_ref, pattern_ref, own_ref, nb_ref, send_0, send_1, facing_0, facing_1):
+    y = row_ref[0]
+    rows = (y, 1 - y)
+    inward, outward = 1 - y, y
+    cols = own_ref.shape[1]
+
+    def coupling(direction, row, col):
+        weight = pattern_ref[(row * cols + col) * 4 + direction].astype(jnp.float32)
+        return nb_ref[direction, row, col] * weight
+
+    for i, (send, facing) in enumerate(((send_0, facing_0), (send_1, facing_1))):
+        k = (y + i) % 2
+        at = [b + k * (cols - 1 - 2 * b) for b in range(HALF)]
+        side_a, side_b = 3 - k, 2 + k
+        for h in range(ROWS):
+            for b in range(HALF):
+                send[OWN + h * HALF + b] = own_ref[rows[h], at[b]]
+                send[SIDE_A + h * HALF + b] = coupling(side_a, rows[h], at[b])
+                send[SIDE_B + h * HALF + b] = coupling(side_b, rows[h], at[b])
+            send[FACING + h] = coupling(2 + k, rows[h], HALF - k)
+            facing[h] = coupling(3 - k, rows[h], (cols - 1) * (1 - k))
+        for b in range(HALF):
+            send[OUT_IN + b] = coupling(inward, rows[0], at[b])
+            send[IN_OUT + b] = coupling(outward, rows[1], at[b])
+            send[IN_IN + b] = coupling(inward, rows[1], at[b])
+
+
+def tile_terms(halves, j, b):
+    i, h = ORIGIN[j]
+    half = halves[i]
+    terms = [(half, OWN + h * HALF + b, (j, b))]
+    if h == 0:
+        terms.append((half, OUT_IN + b, ((1, 2)[i], b)))
     else:
-        terms.append((half, INNER + k * HALF + b, (j - 1, b)))
-        if k == 0:
-            terms.append((half, OUTER + b, (j + 1, b)))
-    terms.append((half, (SIDE_A if b == 0 else SIDE_B) + k * HALF + b, (j, 1 - b)))
+        terms.append((half, IN_OUT + b, ((0, 3)[i], b)))
+        terms.append((half, IN_IN + b, ((2, 1)[i], b)))
+    terms.append((half, (SIDE_A if b == 0 else SIDE_B) + h * HALF + b, (j, 1 - b)))
     return terms
 
 
-def halo_term(keep, recv, j, b):
-    half, k = (keep, j) if j < ROWS else (recv, j - ROWS)
-    return half, (SIDE_B if b == 0 else SIDE_A) + k * HALF + b
-
-
-def facing_term(keep, recv, beyond, j, b):
-    if b == 0:
-        return beyond, j
-    return (keep, FACING + j) if j < ROWS else (recv, FACING + j - ROWS)
+def halo_term(halves, j, b):
+    i, h = ORIGIN[j]
+    return halves[i], (SIDE_B if b == 0 else SIDE_A) + h * HALF + b
+
+
+def facing_term(halves, beyond, j, b):
+    i, h = ORIGIN[j]
+    return (beyond[i], h) if b == 0 else (halves[i], FACING + h)
 
 
 def matvec(terms, chunk=32):
@@ -237,28 +279,21 @@
     return jnp.sum(spread, axis=0, keepdims=True)
 
 
-TILES = [(j, b) for j in range(2 * ROWS) for b in range(HALF)]
-
-
 def row_of(x, j, b):
     i = j * HALF + b
     return x[i:i + 1]
 
 
-def inner_product(f, keep, recv):
+def inner_product(f, halves):
     return jnp.concatenate(
-        [matvec([(r, i, row_of(f, *at)) for r, i, at in tile_terms(keep, recv, j, b)]) for j, b in TILES], axis=0
+        [matvec([(r, i, row_of(f, *at)) for r, i, at in tile_terms(halves, j, b)]) for j, b in TILES], axis=0
     )
 
 
 def messages(f, g):
-    def column(x, b, rows):
-        return [row_of(x, j, b) for j in rows]
-
-    rows = range(2 * ROWS)
-    to_a = jnp.concatenate(column(f, 1, rows[::-1]) + column(g, 1, rows[::-1]), axis=0)
-    to_b = jnp.concatenate(column(f, 0, rows) + column(g, 0, rows), axis=0)
-    return to_a, to_b
+    return [
+        jnp.concatenate([row_of(x, j, b) for x in (f, g) for j in reversed(range(N))], axis=0) for b in (1, 0)
+    ]
 
 
 def ahead(first, sweep, f, q, residue, capacity, injected):
@@ -267,14 +302,16 @@
     return residue - STRIDES[sweep] * (q + capacity * f) + MOMENTA[sweep + 1] * f
 
 
-def start_kernel(keep, recv, field, injected, msg_a, msg_b, q_out):
+def start_kernel(half_0, half_1, field, injected, msg_a, msg_b, q_out):
     f = field[...]
-    q = inner_product(f, keep, recv)
+    q = inner_product(f, (half_0, half_1))
     q_out[...] = q
     msg_a[...], msg_b[...] = messages(f, ahead(True, 0, f, q, None, None, injected[...]))
 
 
-def pair_kernel(pair, last, keep, recv, beyond, capacity_ref, injected_ref, got_a, got_b, f_ref, q_ref, *refs):
+def pair_kernel(pair, last, half_0, half_1, beyond_0, beyond_1, capacity_ref, injected_ref, got_a, got_b, f_ref, q_ref,
+                *refs):
+    halves, beyond = (half_0, half_1), (beyond_0, beyond_1)
     first = pair == 0
     capacity = capacity_ref[...]
     f, q = f_ref[...], q_ref[...]
@@ -282,11 +319,10 @@
         residue, estimate, refs = refs[0][...], refs[1][...], refs[2:]
     got = (got_b, got_a)
     sweep = 2 * pair - 1
-    n = 2 * ROWS
 
     extra = []
     for j, b in TILES:
-        r, i = halo_term(keep, recv, j, b)
+        r, i = halo_term(halves, j, b)
         extra.append(matvec([(r, i, got[b][j:j + 1, :])]))
     product = q + jnp.concatenate(extra, axis=0)
     if first:
@@ -302,13 +338,13 @@
 
     beside2 = {}
     for j, b in TILES:
-        r, i = facing_term(keep, recv, beyond, j, b)
-        beside2[j, b] = got[b][n + j:n + j + 1, :] - scale * matvec([(r, i, row_of(f, j, b))])
+        r, i = facing_term(halves, beyond, j, b)
+        beside2[j, b] = got[b][N + j:N + j + 1, :] - scale * matvec([(r, i, row_of(f, j, b))])
 
     outs = []
     for j, b in TILES:
-        terms = [(r, i, row_of(f2, *at)) for r, i, at in tile_terms(keep, recv, j, b)]
-        r, i = halo_term(keep, recv, j, b)
+        terms = [(r, i, row_of(f2, *at)) for r, i, at in tile_terms(halves, j, b)]
+        r, i = halo_term(halves, j, b)
         outs.append(matvec(terms + [(r, i, beside2[j, b])]))
     sweep = 2 * pair
     residue = residue - STRIDES[sweep] * (jnp.concatenate(outs, axis=0) + capacity * f2)
@@ -321,7 +357,7 @@
     f_out[...] = f3
     if last:
         return
-    q = inner_product(f3, keep, recv)
+    q = inner_product(f3, halves)
     q_out, msg_a, msg_b = refs[:3]
     q_out[...] = q
     msg_a[...], msg_b[...] = messages(f3, ahead(closing, sweep + 1, f3, q, residue, capacity, injected_ref[...]))
@@ -333,60 +369,46 @@
 def shards_chain(own_block, neighbor_block, pattern, capacity, initial, currents, slot_tile):
     tile_rows, tile_cols, width = initial.shape
     n_col = lax.axis_size("col")
-    row, col = lax.axis_index("row"), lax.axis_index("col")
-    flip_row = row == 1
-    flip_col = (row + col) % 2 == 1
-
-    def trade_row(x):
-        return lax.ppermute(x, "row", [(0, 1), (1, 0)])
-
+    row = lax.axis_index("row")
+    both = ("row", "col")
+    deal = deal_pairs(n_col, 0)
+    deal_b = deal_pairs(n_col, 1)
+    a_pairs = [(c, c ^ 1) for c in range(n_col)]
     b_pairs = []
-    for c in range(n_col - 1):
-        r = (c + 1) % 2
-        b_pairs += [(r * n_col + c, r * n_col + c + 1), (r * n_col + c + 1, r * n_col + c)]
-
-    def trade_next(x):
-        return lax.ppermute(x, ("row", "col"), b_pairs)
-
-    def in_order(x):
-        return ordered(x, 0, flip_row, flip_col, 1)
-
-    def split(x):
-        return x[:, :HALF], jnp.flip(x, (0, 1))[:, :HALF]
-
-    flat = (ROWS * HALF, width, width)
-    own = in_order(own_block)
-    weighted = neighbor_block * jnp.moveaxis(pattern, 2, 0).astype(jnp.float32)[..., None, None]
-    up, down, left, right = [weighted[d] for d in range(4)]
-    up, down = jnp.where(flip_row, down, up), jnp.where(flip_row, up, down)
-    side_b, side_a = jnp.where(flip_col, right, left), jnp.where(flip_col, left, right)
-    up, down, side_b, side_a = [in_order(x) for x in (up, down, side_b, side_a)]
-    own_k, own_s = split(own)
-    up_k, down_s = split(up)
-    down_k, up_s = split(down)
-    b_k, a_s = split(side_b)
-    a_k, b_s = split(side_a)
-    keep = jnp.concatenate(
-        [own_k.reshape(flat), a_k.reshape(flat), b_k.reshape(flat), down_k.reshape(flat), up_k[1], side_b[:, HALF]]
-    )
-    send = jnp.concatenate(
-        [own_s.reshape(flat), a_s.reshape(flat), b_s.reshape(flat), up_s.reshape(flat), down_s[0],
-         jnp.flip(side_a[:, HALF - 1], 0)]
-    )
-    recv = trade_row(send)
+    for unit in range(1, 2 * n_col - 1, 2):
+        one, two = unit_device(unit, n_col), unit_device(unit + 1, n_col)
+        b_pairs += [(one, two), (two, one)]
+
+    vmem = pl.BlockSpec(memory_space=pltpu.VMEM)
+    smem = pl.BlockSpec(memory_space=pltpu.SMEM)
+    limit = pltpu.CompilerParams(vmem_limit_bytes=16 * 2**20)
+    packed = jax.ShapeDtypeStruct((PACKED, width, width), jnp.float32)
+    facing = jax.ShapeDtypeStruct((ROWS, width, width), jnp.float32)
+    send_0, send_1, facing_0, facing_1 = pl.pallas_call(
+        pack_kernel,
+        out_shape=(packed, packed, facing, facing),
+        in_specs=[smem, smem, vmem, vmem],
+        out_specs=(vmem,) * 4,
+        compiler_params=limit,
+        name="pack",
+    )(row.astype(jnp.int32).reshape(1), pattern.reshape(-1), own_block, neighbor_block)
+    half_0 = lax.ppermute(send_0, both, deal[0])
+    half_1 = lax.ppermute(send_1, both, deal[1])
+    beyond_0 = lax.ppermute(facing_0, both, deal_b[0])
+    beyond_1 = lax.ppermute(facing_1, both, deal_b[1])
 
     injected = collect(currents, slot_tile, tile_rows * tile_cols, width)
     small = jnp.concatenate(
         [injected.reshape(tile_rows, tile_cols, STEPS * width), capacity, initial], axis=2
     )
-    small_k, small_s = split(in_order(small))
-    small = jnp.concatenate([small_k, trade_row(small_s)], axis=0).reshape(2 * ROWS * HALF, STEPS + 2, width)
+    small = jnp.where(row == 1, jnp.flip(small, 0), small)
+    unit_0, unit_1 = small[:, :HALF], jnp.flip(small, 1)[:, :HALF]
+    got_0 = lax.ppermute(jnp.where(row == 1, unit_1, unit_0), both, deal[0])
+    got_1 = lax.ppermute(jnp.where(row == 1, unit_0, unit_1), both, deal[1])
+    small = jnp.concatenate([got_0, jnp.flip(got_1, 0)], axis=0).reshape(N * HALF, STEPS + 2, width)
     injected, cap, field = small[:, :STEPS], small[:, STEPS], small[:, STEPS + 1]
-    beyond = trade_next(jnp.concatenate([keep[SIDE_B:SIDE_B + ROWS * HALF:HALF], recv[SIDE_B:SIDE_B + ROWS * HALF:HALF]]))
-
-    tiles = 2 * ROWS * HALF
-    shape = jax.ShapeDtypeStruct((tiles, width), jnp.float32)
-    vmem = pl.BlockSpec(memory_space=pltpu.VMEM)
+
+    shape = jax.ShapeDtypeStruct((N * HALF, width), jnp.float32)
 
     def call(body, n_out, blocks, *ins):
         return pl.pallas_call(
@@ -394,39 +416,42 @@
             out_shape=(shape,) * n_out,
             in_specs=[vmem] * len(ins),
             out_specs=(vmem,) * n_out,
-            compiler_params=pltpu.CompilerParams(vmem_limit_bytes=8 * 2**20),
+            compiler_params=limit,
             cost_estimate=pl.CostEstimate(flops=2 * blocks * width * width, bytes_accessed=blocks * width * width * 4,
                                           transcendentals=0),
             name="pair",
         )(*ins)
 
-    msg_a, msg_b, q = call(start_kernel, 3, 28, keep, recv, field, injected[:, 0])
+    msg_a, msg_b, q = call(start_kernel, 3, 28, half_0, half_1, field, injected[:, 0])
     frames = []
     for instant in range(STEPS):
         state = ()
         for pair in range(ITERS // 2):
             closing = pair + 1 == ITERS // 2
             last = closing and instant + 1 == STEPS
-            got_b, got_a = trade_next(msg_b), trade_row(msg_a)
+            got_b = lax.ppermute(msg_b, both, b_pairs)
+            got_a = lax.ppermute(msg_a, "col", a_pairs)
             feed = injected[:, min(instant + closing, STEPS - 1)]
             out = call(functools.partial(pair_kernel, pair, last), 1 if last else 4 if closing else 6, 80,
-                       keep, recv, beyond, cap, feed, got_a, got_b, field, q, *state)
+                       half_0, half_1, beyond_0, beyond_1, cap, feed, got_a, got_b, field, q, *state)
             field = out[0]
             if not last:
                 q, msg_a, msg_b = out[1:4]
                 state = tuple(out[4:])
         frames.append(field)
 
-    done = jnp.stack(frames).reshape(STEPS, 2 * ROWS, HALF, width)
-    got = trade_row(done[:, ROWS:])
-    done = jnp.concatenate([done[:, :ROWS], jnp.flip(got, (1, 2))], axis=2)
-    return ordered(done, 1, flip_row, flip_col, 2)
+    done = jnp.stack(frames).reshape(STEPS, N, HALF, width)
+    got_0 = lax.ppermute(done[:, :ROWS], both, [(b, a) for a, b in deal[0]])
+    got_1 = lax.ppermute(jnp.flip(done[:, ROWS:], 1), both, [(b, a) for a, b in deal[1]])
+    unit_0, unit_1 = jnp.where(row == 1, got_1, got_0), jnp.where(row == 1, got_0, got_1)
+    done = jnp.concatenate([unit_0, jnp.flip(unit_1, 2)], axis=2)
+    return jnp.where(row == 1, jnp.flip(done, 1), done)
 
 
 def solution(mesh):
     rows, cols = mesh.shape["row"], mesh.shape["col"]
     return jax.shard_map(
-        shards_chain if rows == 2 and cols % 2 == 0 else shards_general,
+        shards_chain if rows == 2 and cols % 4 == 0 else shards_general,
         mesh=mesh,
         in_specs=(
             P("row", "col", None, None),

time: 159 us -> 160 us (level)
  starting transfers between devices: 52.4 us -> 92.4 us
  waiting for transfers between devices: 75.8 us -> 44.6 us
  local copies, waits for them, and re-layouts: 12.5 us -> 4.96 us
  other arithmetic: 4.53 us -> 2.16 us
  Pallas kernels: 11.6 us -> 13.8 us
    ppermute x36 -> x40, starting transfers between devices: 46.1 us -> 86.2 us  [the longest x16 57.3 us: shards_chain(): got_b = lax.ppermute(msg_b, both, b_pairs)]
    ppermute x36 -> x40, waiting for transfers between devices: 72.1 us -> 44.6 us  [the longest x16 20.4 us: shards_chain(): got_b = lax.ppermute(msg_b, both, b_pairs)]
    slice x22 -> x3, local copies, waits for them, and re-layouts: 5.05 us -> 0.21 us  [the longest x2 0.2 us: shards_chain(): unit_0, unit_1 = (small[:, :HALF], jnp.flip(small, 1)[:, :HALF])]
    all_to_all x1, waiting for transfers between devices: 3.68 us -> 0.01 us  [collect(): lax.all_to_all(packed, 'col', split_axis=2, concat_axis=1, tiled=True)]
    pallas_call x0 -> x1, Pallas kernels: none -> 2.2 us  [shards_chain(): pl.pallas_call(pack_kernel, out_shape=(packed, packed, facing, facing), i...]
    mul x1 -> x0, other arithmetic: 1.79 us -> none  [shards_chain(): neighbor_block * jnp.moveaxis(pattern, 2, 0).astype(jnp.float32)[..., Non...]
    unnamed x35 -> x12, local copies, waits for them, and re-layouts: 5.27 us -> 3.78 us
  transfers between devices with their start and end apart: 37 -> 41, of which waited for: 34 -> 19; matrix products, arithmetic and copies ran while one was open for 3% -> 1% of each run, Pallas kernels for 0% -> 2%
where the time goes in v3:
time: 160 us; the launch traced here: 159 us
  starting transfers between devices  92.4 us (58%)
  waiting for transfers between devices  44.6 us (28%)
  Pallas kernels  13.8 us (9%)
  local copies, waits for them, and re-layouts  4.96 us (3%)
  other arithmetic  2.16 us (1%)
    ppermute x16, starting transfers between devices, shards_chain(): got_b = lax.ppermute(msg_b, both, b_pairs)  57.3 us
    ppermute x16, waiting for transfers between devices, shards_chain(): got_b = lax.ppermute(msg_b, both, b_pairs)  20.4 us
    ppermute x1, waiting for transfers between devices, shards_chain(): got_1 = lax.ppermute(jnp.where(row == 1, unit_0, unit_1), both, deal[1])  19.8 us
    pallas_call x17, Pallas kernels, call(): pl.pallas_call(body, out_shape=(shape,) * n_out, in_specs=[vmem] * len(in...  11.6 us
    all_to_all x1, starting transfers between devices, collect(): lax.all_to_all(packed, 'col', split_axis=2, concat_axis=1, tiled=True)  6.27 us
    ppermute x16, starting transfers between devices, shards_chain(): got_a = lax.ppermute(msg_a, 'col', a_pairs)  5.04 us
    ppermute x1, starting transfers between devices, shards_chain(): lax.ppermute(jnp.flip(done[:, ROWS:], 1), both, [(b, a) for a, b in deal[...  4.4 us
    ppermute x1, starting transfers between devices, shards_chain(): beyond_0 = lax.ppermute(facing_0, both, deal_b[0])  4.29 us
  transfers between devices with their start and end apart: 41, of which 19 were waited for; matrix products, arithmetic and copies ran while one was open for 1% of the time, Pallas kernels for 2%

profile of v3, /device:TPU:8, one launch (start us, length us, event | category | flops | bytes accessed | tf_op | source)
XLA Modules:
  0.0 158.7 jit_solution(14465113019943849058)
XLA Ops:
  0.8 1.0 copy.30
  1.8 0.8 fusion
  2.6 6.3 %all-to-all-start = ((f32[1,1,16,5,512]{4,1,3,0,2:T(1,128)}), f32[1,1,16,5,512]{4,1,3,0,2:T(1,128)S(1)}, u32[]{:S(2)}, u32[]{:S(2)}) async-start(f32[1,1,16,5,512]{4,1,3,0,2:T(1,128)} %fusion), calls=%async_computation | async-start | bytes 327680 | tf_op jit(solution)/shard_map/all_to_all | solution.py:131
  8.9 0.8 reshape.24.pattern_ref
  9.6 1.6 %copy-done = f32[4,2,4,128,128]{4,3,2,1,0:T(8,128)S(1)} copy-done((f32[4,2,4,128,128]{4,3,2,1,0:T(8,128)S(1)}, f32[4,2,4,128,128]{4,3,2,1,0:T(8,128)}, u32[]{:S(2)}) %copy-start) | copy-done | bytes 2097176
  11.2 1.0 copy-done.1
  12.3 2.2 %pack.1 = (f32[20,128,128]{2,1,0:T(8,128)}, f32[20,128,128]{2,1,0:T(8,128)}, f32[2,128,128]{2,1,0:T(8,128)S(1)}, f32[2,128,128]{2,1,0:T(8,128)S(1)}) custom-call(s32[1]{0:T(128)} %bitcast.row_ref, s32[32]{0:T(128)S(1)} %reshape.24.pattern_ref, f32[2,4,128,128]{3,2,1,0:T(8,128)S(1)} %copy-done.1, f32[4,2,4,128,128]{4,3,2,1,0:T(8,128)S(1)} %copy-done), custom_call_target="tpu_custom_call" | custom-call | tf_op jit(solution)/shard_map/pack/pallas_call | solution.py:387
  14.5 3.4 %collective-permute-start = (f32[20,128,128]{2,1,0:T(8,128)}, f32[20,128,128]{2,1,0:T(8,128)S(1)}, u32[]{:S(2)}, u32[]{:S(2)}) collective-permute-start(f32[20,128,128]{2,1,0:T(8,128)} %get-tuple-element.96), channel_id=1, source_target_pairs={{0,0},{1,2},{2,18},{3,16},{4,20},{5,22},{6,6},{7,4},{8,8},{9,10},{... | collective-permute-start | bytes 3932168 | tf_op jit(solution)/shard_map/ppermute | solution.py:395
  17.9 2.8 %collective-permute-start.1 = (f32[20,128,128]{2,1,0:T(8,128)}, f32[20,128,128]{2,1,0:T(8,128)S(1)}, u32[]{:S(2)}, u32[]{:S(2)}) collective-permute-start(f32[20,128,128]{2,1,0:T(8,128)} %get-tuple-element.97), channel_id=1, source_target_pairs={{0,1},{1,3},{2,19},{3,17},{4,21},{5,23},{6,7},{7,5},{8,9},{9,11},{... | collective-permute-start | bytes 3932168 | tf_op jit(solution)/shard_map/ppermute | solution.py:396
  21.4 2.4 %collective-permute-start.5 = (f32[2,2,768]{2,1,0:T(2,128)S(1)}, f32[2,2,768]{2,1,0:T(2,128)S(1)}, u32[]{:S(2)}, u32[]{:S(2)}) collective-permute-start(f32[2,2,768]{2,1,0:T(2,128)S(1)} %get-tuple-element.188), channel_id=1, source_target_pairs={{0,1},{1,3},{2,19},{3,17},{4,21},{5,23},{6,7},{7,5},{8,9},{9,11},{... | collective-permute-start | bytes 36872 | tf_op jit(solution)/shard_map/ppermute | solution.py:407
  23.9 1.9 %collective-permute-start.4 = (f32[2,2,768]{2,1,0:T(2,128)S(1)}, f32[2,2,768]{2,1,0:T(2,128)S(1)}, u32[]{:S(2)}, u32[]{:S(2)}) collective-permute-start(f32[2,2,768]{2,1,0:T(2,128)S(1)} %get-tuple-element.187), channel_id=1, source_target_pairs={{0,0},{1,2},{2,18},{3,16},{4,20},{5,22},{6,6},{7,4},{8,8},{9,10},{... | collective-permute-start | bytes 36872 | tf_op jit(solution)/shard_map/ppermute | solution.py:406
  25.8 4.3 %collective-permute-start.2 = (f32[2,128,128]{2,1,0:T(8,128)S(1)}, f32[2,128,128]{2,1,0:T(8,128)S(1)}, u32[]{:S(2)}, u32[]{:S(2)}) collective-permute-start(f32[2,128,128]{2,1,0:T(8,128)S(1)} %get-tuple-element.98), channel_id=1, source_target_pairs={{0,2},{1,18},{2,16},{3,20},{4,22},{5,6},{6,4},{7,8},{8,10},{9,26},... | collective-permute-start | bytes 393224 | tf_op jit(solution)/shard_map/ppermute | solution.py:397
  30.1 19.8 %collective-permute-done.5 = f32[2,2,768]{2,1,0:T(2,128)S(1)} collective-permute-done((f32[2,2,768]{2,1,0:T(2,128)S(1)}, f32[2,2,768]{2,1,0:T(2,128)S(1)}, u32[]{:S(2)}, u32[]{:S(2)}) %collective-permute-start.5) | collective-permute-done | bytes 12320 | tf_op jit(solution)/shard_map/ppermute | solution.py:407
  49.8 2.6 %collective-permute-start.3 = (f32[2,128,128]{2,1,0:T(8,128)S(1)}, f32[2,128,128]{2,1,0:T(8,128)S(1)}, u32[]{:S(2)}, u32[]{:S(2)}) collective-permute-start(f32[2,128,128]{2,1,0:T(8,128)S(1)} %get-tuple-element.99), channel_id=1, source_target_pairs={{1,1},{2,3},{3,19},{4,17},{5,21},{6,23},{7,7},{8,5},{9,9},{10,11},... | collective-permute-start | bytes 393224 | tf_op jit(solution)/shard_map/ppermute | solution.py:398
  53.2 3.7 %collective-permute-start.7 = (f32[8,128]{1,0:T(8,128)S(1)}, f32[8,128]{1,0:T(8,128)S(1)}, u32[]{:S(2)}, u32[]{:S(2)}) collective-permute-start(f32[8,128]{1,0:T(8,128)S(1)} %get-tuple-element.101), channel_id=1, source_target_pairs={{1,2},{2,1},{3,18},{18,3},{19,16},{16,19},{17,20},{20,17},{21,22},... | collective-permute-start | bytes 12296 | tf_op jit(solution)/shard_map/ppermute | solution.py:432
  59.1 3.4 %collective-permute-start.9 = (f32[8,128]{1,0:T(8,128)S(1)}, f32[8,128]{1,0:T(8,128)S(1)}, u32[]{:S(2)}, u32[]{:S(2)}) collective-permute-start(f32[8,128]{1,0:T(8,128)S(1)} %get-tuple-element.104), channel_id=1, source_target_pairs={{1,2},{2,1},{3,18},{18,3},{19,16},{16,19},{17,20},{20,17},{21,22},... | collective-permute-start | bytes 12296 | tf_op jit(solution)/shard_map/ppermute | solution.py:432
  62.6 1.4 collective-permute-done.9.got_b
  65.2 3.6 %collective-permute-start.11 = (f32[8,128]{1,0:T(8,128)S(1)}, f32[8,128]{1,0:T(8,128)S(1)}, u32[]{:S(2)}, u32[]{:S(2)}) collective-permute-start(f32[8,128]{1,0:T(8,128)S(1)} %get-tuple-element.110), channel_id=1, source_target_pairs={{1,2},{2,1},{3,18},{18,3},{19,16},{16,19},{17,20},{20,17},{21,22},... | collective-permute-start | bytes 12296 | tf_op jit(solution)/shard_map/ppermute | solution.py:432
  68.8 1.3 collective-permute-done.11.got_b
  71.0 3.5 %collective-permute-start.13 = (f32[8,128]{1,0:T(8,128)S(1)}, f32[8,128]{1,0:T(8,128)S(1)}, u32[]{:S(2)}, u32[]{:S(2)}) collective-permute-start(f32[8,128]{1,0:T(8,128)S(1)} %get-tuple-element.116), channel_id=1, source_target_pairs={{1,2},{2,1},{3,18},{18,3},{19,16},{16,19},{17,20},{20,17},{21,22},... | collective-permute-start | bytes 12296 | tf_op jit(solution)/shard_map/ppermute | solution.py:432
  74.6 1.4 collective-permute-done.13.got_b
  77.1 3.6 %collective-permute-start.15 = (f32[8,128]{1,0:T(8,128)S(1)}, f32[8,128]{1,0:T(8,128)S(1)}, u32[]{:S(2)}, u32[]{:S(2)}) collective-permute-start(f32[8,128]{1,0:T(8,128)S(1)} %get-tuple-element.123), channel_id=1, source_target_pairs={{1,2},{2,1},{3,18},{18,3},{19,16},{16,19},{17,20},{20,17},{21,22},... | collective-permute-start | bytes 12296 | tf_op jit(solution)/shard_map/ppermute | solution.py:432
  80.7 1.3 collective-permute-done.15.got_b
  83.0 3.5 %collective-permute-start.17 = (f32[8,128]{1,0:T(8,128)S(1)}, f32[8,128]{1,0:T(8,128)S(1)}, u32[]{:S(2)}, u32[]{:S(2)}) collective-permute-start(f32[8,128]{1,0:T(8,128)S(1)} %get-tuple-element.126), channel_id=1, source_target_pairs={{1,2},{2,1},{3,18},{18,3},{19,16},{16,19},{17,20},{20,17},{21,22},... | collective-permute-start | bytes 12296 | tf_op jit(solution)/shard_map/ppermute | solution.py:432
  86.5 1.4 collective-permute-done.17.got_b
  89.0 3.6 %collective-permute-start.19 = (f32[8,128]{1,0:T(8,128)S(1)}, f32[8,128]{1,0:T(8,128)S(1)}, u32[]{:S(2)}, u32[]{:S(2)}) collective-permute-start(f32[8,128]{1,0:T(8,128)S(1)} %get-tuple-element.132), channel_id=1, source_target_pairs={{1,2},{2,1},{3,18},{18,3},{19,16},{16,19},{17,20},{20,17},{21,22},... | collective-permute-start | bytes 12296 | tf_op jit(solution)/shard_map/ppermute | solution.py:432
  92.6 1.3 collective-permute-done.19.got_b
  94.9 3.5 %collective-permute-start.21 = (f32[8,128]{1,0:T(8,128)S(1)}, f32[8,128]{1,0:T(8,128)S(1)}, u32[]{:S(2)}, u32[]{:S(2)}) collective-permute-start(f32[8,128]{1,0:T(8,128)S(1)} %get-tuple-element.138), channel_id=1, source_target_pairs={{1,2},{2,1},{3,18},{18,3},{19,16},{16,19},{17,20},{20,17},{21,22},... | collective-permute-start | bytes 12296 | tf_op jit(solution)/shard_map/ppermute | solution.py:432
  98.4 1.4 collective-permute-done.21.got_b
  100.9 3.6 %collective-permute-start.23 = (f32[8,128]{1,0:T(8,128)S(1)}, f32[8,128]{1,0:T(8,128)S(1)}, u32[]{:S(2)}, u32[]{:S(2)}) collective-permute-start(f32[8,128]{1,0:T(8,128)S(1)} %get-tuple-element.145), channel_id=1, source_target_pairs={{1,2},{2,1},{3,18},{18,3},{19,16},{16,19},{17,20},{20,17},{21,22},... | collective-permute-start | bytes 12296 | tf_op jit(solution)/shard_map/ppermute | solution.py:432
  104.5 1.3 collective-permute-done.23.got_b
  106.8 3.5 %collective-permute-start.25 = (f32[8,128]{1,0:T(8,128)S(1)}, f32[8,128]{1,0:T(8,128)S(1)}, u32[]{:S(2)}, u32[]{:S(2)}) collective-permute-start(f32[8,128]{1,0:T(8,128)S(1)} %get-tuple-element.148), channel_id=1, source_target_pairs={{1,2},{2,1},{3,18},{18,3},{19,16},{16,19},{17,20},{20,17},{21,22},... | collective-permute-start | bytes 12296 | tf_op jit(solution)/shard_map/ppermute | solution.py:432
  110.4 1.4 collective-permute-done.25.got_b
  112.8 3.6 %collective-permute-start.27 = (f32[8,128]{1,0:T(8,128)S(1)}, f32[8,128]{1,0:T(8,128)S(1)}, u32[]{:S(2)}, u32[]{:S(2)}) collective-permute-start(f32[8,128]{1,0:T(8,128)S(1)} %get-tuple-element.154), channel_id=1, source_target_pairs={{1,2},{2,1},{3,18},{18,3},{19,16},{16,19},{17,20},{20,17},{21,22},... | collective-permute-start | bytes 12296 | tf_op jit(solution)/shard_map/ppermute | solution.py:432
  116.5 1.3 collective-permute-done.27.got_b
  118.7 3.7 %collective-permute-start.29 = (f32[8,128]{1,0:T(8,128)S(1)}, f32[8,128]{1,0:T(8,128)S(1)}, u32[]{:S(2)}, u32[]{:S(2)}) collective-permute-start(f32[8,128]{1,0:T(8,128)S(1)} %get-tuple-element.160), channel_id=1, source_target_pairs={{1,2},{2,1},{3,18},{18,3},{19,16},{16,19},{17,20},{20,17},{21,22},... | collective-permute-start | bytes 12296 | tf_op jit(solution)/shard_map/ppermute | solution.py:432
  122.5 1.2 collective-permute-done.29.got_b
  124.8 3.6 %collective-permute-start.31 = (f32[8,128]{1,0:T(8,128)S(1)}, f32[8,128]{1,0:T(8,128)S(1)}, u32[]{:S(2)}, u32[]{:S(2)}) collective-permute-start(f32[8,128]{1,0:T(8,128)S(1)} %get-tuple-element.167), channel_id=1, source_target_pairs={{1,2},{2,1},{3,18},{18,3},{19,16},{16,19},{17,20},{20,17},{21,22},... | collective-permute-start | bytes 12296 | tf_op jit(solution)/shard_map/ppermute | solution.py:432
  128.4 1.3 collective-permute-done.31.got_b
  130.7 3.5 %collective-permute-start.33 = (f32[8,128]{1,0:T(8,128)S(1)}, f32[8,128]{1,0:T(8,128)S(1)}, u32[]{:S(2)}, u32[]{:S(2)}) collective-permute-start(f32[8,128]{1,0:T(8,128)S(1)} %get-tuple-element.170), channel_id=1, source_target_pairs={{1,2},{2,1},{3,18},{18,3},{19,16},{16,19},{17,20},{20,17},{21,22},... | collective-permute-start | bytes 12296 | tf_op jit(solution)/shard_map/ppermute | solution.py:432
  134.2 1.4 collective-permute-done.33.got_b
  136.7 3.6 %collective-permute-start.35 = (f32[8,128]{1,0:T(8,128)S(1)}, f32[8,128]{1,0:T(8,128)S(1)}, u32[]{:S(2)}, u32[]{:S(2)}) collective-permute-start(f32[8,128]{1,0:T(8,128)S(1)} %get-tuple-element.176), channel_id=1, source_target_pairs={{1,2},{2,1},{3,18},{18,3},{19,16},{16,19},{17,20},{20,17},{21,22},... | collective-permute-start | bytes 12296 | tf_op jit(solution)/shard_map/ppermute | solution.py:432
  140.3 1.3 collective-permute-done.35.got_b
  142.6 3.5 %collective-permute-start.37 = (f32[8,128]{1,0:T(8,128)S(1)}, f32[8,128]{1,0:T(8,128)S(1)}, u32[]{:S(2)}, u32[]{:S(2)}) collective-permute-start(f32[8,128]{1,0:T(8,128)S(1)} %get-tuple-element.182), channel_id=1, source_target_pairs={{1,2},{2,1},{3,18},{18,3},{19,16},{16,19},{17,20},{20,17},{21,22},... | collective-permute-start | bytes 12296 | tf_op jit(solution)/shard_map/ppermute | solution.py:432
  146.1 1.4 collective-permute-done.37.got_b
  148.0 4.4 %collective-permute-start.38 = (f32[4,2,2,128]{3,2,1,0:T(2,128)S(1)}, f32[4,2,2,128]{3,2,1,0:T(2,128)S(1)}, u32[]{:S(2)}, u32[]{:S(2)}) collective-permute-start(f32[4,2,2,128]{3,2,1,0:T(2,128)S(1)} %rev.24), channel_id=1, source_target_pairs={{1,0},{3,1},{19,2},{17,3},{21,4},{23,5},{7,6},{5,7},{9,8},{11,9},{... | collective-permute-start | bytes 24584 | tf_op jit(solution)/shard_map/ppermute | solution.py:445
  152.4 1.9 %collective-permute-start.39 = (f32[4,2,2,128]{3,2,1,0:T(2,128)S(1)}, f32[4,2,2,128]{3,2,1,0:T(2,128)S(1)}, u32[]{:S(2)}, u32[]{:S(2)}) collective-permute-start(f32[4,2,2,128]{3,2,1,0:T(2,128)S(1)} %get-tuple-element.198), channel_id=1, source_target_pairs={{0,0},{2,1},{18,2},{16,3},{20,4},{22,5},{6,6},{4,7},{8,8},{10,9},{... | collective-permute-start | bytes 24584 | tf_op jit(solution)/shard_map/ppermute | solution.py:444
  154.4 3.6 %collective-permute-done.39 = f32[4,2,2,128]{3,2,1,0:T(2,128)S(1)} collective-permute-done((f32[4,2,2,128]{3,2,1,0:T(2,128)S(1)}, f32[4,2,2,128]{3,2,1,0:T(2,128)S(1)}, u32[]{:S(2)}, u32[]{:S(2)}) %collective-permute-start.39) | collective-permute-done | bytes 8224 | tf_op jit(solution)/shard_map/ppermute | solution.py:444
  (88 shorter events, 20.0 us)
Async XLA Ops:
  2.6 18.2 %all-to-all-start = ((f32[1,1,16,5,512]{4,1,3,0,2:T(1,128)}), f32[1,1,16,5,512]{4,1,3,0,2:T(1,128)S(1)}, u32[]{:S(2)}, u32[]{:S(2)}) async-start(f32[1,1,16,5,512]{4,1,3,0,2:T(1,128)} %fusion), calls=%async_computation | async-start | bytes 327680 | tf_op jit(solution)/shard_map/all_to_all | solution.py:131
  9.6 1.6 %copy-start = (f32[4,2,4,128,128]{4,3,2,1,0:T(8,128)S(1)}, f32[4,2,4,128,128]{4,3,2,1,0:T(8,128)}, u32[]{:S(2)}) copy-start(f32[4,2,4,128,128]{4,3,2,1,0:T(8,128)} %nb_ref.1) | copy-start | bytes 6291460
  11.2 1.0 copy-start.1
  12.3 8.9 %copy-start.2 = (f32[2,4,128]{2,1,0:T(4,128)S(1)}, f32[2,4,128]{2,1,0:T(4,128)}, u32[]{:S(2)}) copy-start(f32[2,4,128]{2,1,0:T(4,128)} %param.10) | copy-start | bytes 12292
  12.3 8.9 %copy-start.3 = (f32[2,4,128]{2,1,0:T(4,128)S(1)}, f32[2,4,128]{2,1,0:T(4,128)}, u32[]{:S(2)}) copy-start(f32[2,4,128]{2,1,0:T(4,128)} %param.11) | copy-start | bytes 12292
  14.5 38.1 %collective-permute-start = (f32[20,128,128]{2,1,0:T(8,128)}, f32[20,128,128]{2,1,0:T(8,128)S(1)}, u32[]{:S(2)}, u32[]{:S(2)}) collective-permute-start(f32[20,128,128]{2,1,0:T(8,128)} %get-tuple-element.96), channel_id=1, source_target_pairs={{0,0},{1,2},{2,18},{3,16},{4,20},{5,22},{6,6},{7,4},{8,8},{9,10},{... | collective-permute-start | bytes 3932168 | tf_op jit(solution)/shard_map/ppermute | solution.py:395
  17.9 34.7 %collective-permute-start.1 = (f32[20,128,128]{2,1,0:T(8,128)}, f32[20,128,128]{2,1,0:T(8,128)S(1)}, u32[]{:S(2)}, u32[]{:S(2)}) collective-permute-start(f32[20,128,128]{2,1,0:T(8,128)} %get-tuple-element.97), channel_id=1, source_target_pairs={{0,1},{1,3},{2,19},{3,17},{4,21},{5,23},{6,7},{7,5},{8,9},{9,11},{... | collective-permute-start | bytes 3932168 | tf_op jit(solution)/shard_map/ppermute | solution.py:396
  21.4 28.4 %collective-permute-start.5 = (f32[2,2,768]{2,1,0:T(2,128)S(1)}, f32[2,2,768]{2,1,0:T(2,128)S(1)}, u32[]{:S(2)}, u32[]{:S(2)}) collective-permute-start(f32[2,2,768]{2,1,0:T(2,128)S(1)} %get-tuple-element.188), channel_id=1, source_target_pairs={{0,1},{1,3},{2,19},{3,17},{4,21},{5,23},{6,7},{7,5},{8,9},{9,11},{... | collective-permute-start | bytes 36872 | tf_op jit(solution)/shard_map/ppermute | solution.py:407
  23.9 28.6 %collective-permute-start.4 = (f32[2,2,768]{2,1,0:T(2,128)S(1)}, f32[2,2,768]{2,1,0:T(2,128)S(1)}, u32[]{:S(2)}, u32[]{:S(2)}) collective-permute-start(f32[2,2,768]{2,1,0:T(2,128)S(1)} %get-tuple-element.187), channel_id=1, source_target_pairs={{0,0},{1,2},{2,18},{3,16},{4,20},{5,22},{6,6},{7,4},{8,8},{9,10},{... | collective-permute-start | bytes 36872 | tf_op jit(solution)/shard_map/ppermute | solution.py:406
  25.8 31.1 %collective-permute-start.2 = (f32[2,128,128]{2,1,0:T(8,128)S(1)}, f32[2,128,128]{2,1,0:T(8,128)S(1)}, u32[]{:S(2)}, u32[]{:S(2)}) collective-permute-start(f32[2,128,128]{2,1,0:T(8,128)S(1)} %get-tuple-element.98), channel_id=1, source_target_pairs={{0,2},{1,18},{2,16},{3,20},{4,22},{5,6},{6,4},{7,8},{8,10},{9,26},... | collective-permute-start | bytes 393224 | tf_op jit(solution)/shard_map/ppermute | solution.py:397
  49.8 7.7 %collective-permute-start.3 = (f32[2,128,128]{2,1,0:T(8,128)S(1)}, f32[2,128,128]{2,1,0:T(8,128)S(1)}, u32[]{:S(2)}, u32[]{:S(2)}) collective-permute-start(f32[2,128,128]{2,1,0:T(8,128)S(1)} %get-tuple-element.99), channel_id=1, source_target_pairs={{1,1},{2,3},{3,19},{4,17},{5,21},{6,23},{7,7},{8,5},{9,9},{10,11},... | collective-permute-start | bytes 393224 | tf_op jit(solution)/shard_map/ppermute | solution.py:398
  52.8 4.8 %collective-permute-start.6 = (f32[8,128]{1,0:T(8,128)S(1)}, f32[8,128]{1,0:T(8,128)S(1)}, u32[]{:S(2)}, u32[]{:S(2)}) collective-permute-start(f32[8,128]{1,0:T(8,128)S(1)} %get-tuple-element.100), channel_id=1, source_target_pairs={{0,1},{1,0},{2,3},{3,2},{4,5},{5,4},{6,7},{7,6},{8,9},{9,8},{10,11... | collective-permute-start | bytes 12296 | tf_op jit(solution)/shard_map/ppermute | solution.py:433
  53.2 5.0 %collective-permute-start.7 = (f32[8,128]{1,0:T(8,128)S(1)}, f32[8,128]{1,0:T(8,128)S(1)}, u32[]{:S(2)}, u32[]{:S(2)}) collective-permute-start(f32[8,128]{1,0:T(8,128)S(1)} %get-tuple-element.101), channel_id=1, source_target_pairs={{1,2},{2,1},{3,18},{18,3},{19,16},{16,19},{17,20},{20,17},{21,22},... | collective-permute-start | bytes 12296 | tf_op jit(solution)/shard_map/ppermute | solution.py:432
  58.9 3.7 %collective-permute-start.8 = (f32[8,128]{1,0:T(8,128)S(1)}, f32[8,128]{1,0:T(8,128)S(1)}, u32[]{:S(2)}, u32[]{:S(2)}) collective-permute-start(f32[8,128]{1,0:T(8,128)S(1)} %get-tuple-element.103), channel_id=1, source_target_pairs={{0,1},{1,0},{2,3},{3,2},{4,5},{5,4},{6,7},{7,6},{8,9},{9,8},{10,11... | collective-permute-start | bytes 12296 | tf_op jit(solution)/shard_map/ppermute | solution.py:433
  59.1 4.9 %collective-permute-start.9 = (f32[8,128]{1,0:T(8,128)S(1)}, f32[8,128]{1,0:T(8,128)S(1)}, u32[]{:S(2)}, u32[]{:S(2)}) collective-permute-start(f32[8,128]{1,0:T(8,128)S(1)} %get-tuple-element.104), channel_id=1, source_target_pairs={{1,2},{2,1},{3,18},{18,3},{19,16},{16,19},{17,20},{20,17},{21,22},... | collective-permute-start | bytes 12296 | tf_op jit(solution)/shard_map/ppermute | solution.py:432
  64.8 4.0 %collective-permute-start.10 = (f32[8,128]{1,0:T(8,128)S(1)}, f32[8,128]{1,0:T(8,128)S(1)}, u32[]{:S(2)}, u32[]{:S(2)}) collective-permute-start(f32[8,128]{1,0:T(8,128)S(1)} %get-tuple-element.109), channel_id=1, source_target_pairs={{0,1},{1,0},{2,3},{3,2},{4,5},{5,4},{6,7},{7,6},{8,9},{9,8},{10,11... | collective-permute-start | bytes 12296 | tf_op jit(solution)/shard_map/ppermute | solution.py:433
  65.2 4.9 %collective-permute-start.11 = (f32[8,128]{1,0:T(8,128)S(1)}, f32[8,128]{1,0:T(8,128)S(1)}, u32[]{:S(2)}, u32[]{:S(2)}) collective-permute-start(f32[8,128]{1,0:T(8,128)S(1)} %get-tuple-element.110), channel_id=1, source_target_pairs={{1,2},{2,1},{3,18},{18,3},{19,16},{16,19},{17,20},{20,17},{21,22},... | collective-permute-start | bytes 12296 | tf_op jit(solution)/shard_map/ppermute | solution.py:432
  70.8 3.8 %collective-permute-start.12 = (f32[8,128]{1,0:T(8,128)S(1)}, f32[8,128]{1,0:T(8,128)S(1)}, u32[]{:S(2)}, u32[]{:S(2)}) collective-permute-start(f32[8,128]{1,0:T(8,128)S(1)} %get-tuple-element.115), channel_id=1, source_target_pairs={{0,1},{1,0},{2,3},{3,2},{4,5},{5,4},{6,7},{7,6},{8,9},{9,8},{10,11... | collective-permute-start | bytes 12296 | tf_op jit(solution)/shard_map/ppermute | solution.py:433
  71.0 4.9 %collective-permute-start.13 = (f32[8,128]{1,0:T(8,128)S(1)}, f32[8,128]{1,0:T(8,128)S(1)}, u32[]{:S(2)}, u32[]{:S(2)}) collective-permute-start(f32[8,128]{1,0:T(8,128)S(1)} %get-tuple-element.116), channel_id=1, source_target_pairs={{1,2},{2,1},{3,18},{18,3},{19,16},{16,19},{17,20},{20,17},{21,22},... | collective-permute-start | bytes 12296 | tf_op jit(solution)/shard_map/ppermute | solution.py:432
  76.7 4.0 %collective-permute-start.14 = (f32[8,128]{1,0:T(8,128)S(1)}, f32[8,128]{1,0:T(8,128)S(1)}, u32[]{:S(2)}, u32[]{:S(2)}) collective-permute-start(f32[8,128]{1,0:T(8,128)S(1)} %get-tuple-element.122), channel_id=1, source_target_pairs={{0,1},{1,0},{2,3},{3,2},{4,5},{5,4},{6,7},{7,6},{8,9},{9,8},{10,11... | collective-permute-start | bytes 12296 | tf_op jit(solution)/shard_map/ppermute | solution.py:433
  77.1 4.9 %collective-permute-start.15 = (f32[8,128]{1,0:T(8,128)S(1)}, f32[8,128]{1,0:T(8,128)S(1)}, u32[]{:S(2)}, u32[]{:S(2)}) collective-permute-start(f32[8,128]{1,0:T(8,128)S(1)} %get-tuple-element.123), channel_id=1, source_target_pairs={{1,2},{2,1},{3,18},{18,3},{19,16},{16,19},{17,20},{20,17},{21,22},... | collective-permute-start | bytes 12296 | tf_op jit(solution)/shard_map/ppermute | solution.py:432
  82.7 3.8 %collective-permute-start.16 = (f32[8,128]{1,0:T(8,128)S(1)}, f32[8,128]{1,0:T(8,128)S(1)}, u32[]{:S(2)}, u32[]{:S(2)}) collective-permute-start(f32[8,128]{1,0:T(8,128)S(1)} %get-tuple-element.125), channel_id=1, source_target_pairs={{0,1},{1,0},{2,3},{3,2},{4,5},{5,4},{6,7},{7,6},{8,9},{9,8},{10,11... | collective-permute-start | bytes 12296 | tf_op jit(solution)/shard_map/ppermute | solution.py:433
  83.0 4.9 %collective-permute-start.17 = (f32[8,128]{1,0:T(8,128)S(1)}, f32[8,128]{1,0:T(8,128)S(1)}, u32[]{:S(2)}, u32[]{:S(2)}) collective-permute-start(f32[8,128]{1,0:T(8,128)S(1)} %get-tuple-element.126), channel_id=1, source_target_pairs={{1,2},{2,1},{3,18},{18,3},{19,16},{16,19},{17,20},{20,17},{21,22},... | collective-permute-start | bytes 12296 | tf_op jit(solution)/shard_map/ppermute | solution.py:432
  88.6 4.0 %collective-permute-start.18 = (f32[8,128]{1,0:T(8,128)S(1)}, f32[8,128]{1,0:T(8,128)S(1)}, u32[]{:S(2)}, u32[]{:S(2)}) collective-permute-start(f32[8,128]{1,0:T(8,128)S(1)} %get-tuple-element.131), channel_id=1, source_target_pairs={{0,1},{1,0},{2,3},{3,2},{4,5},{5,4},{6,7},{7,6},{8,9},{9,8},{10,11... | collective-permute-start | bytes 12296 | tf_op jit(solution)/shard_map/ppermute | solution.py:433
  89.0 4.9 %collective-permute-start.19 = (f32[8,128]{1,0:T(8,128)S(1)}, f32[8,128]{1,0:T(8,128)S(1)}, u32[]{:S(2)}, u32[]{:S(2)}) collective-permute-start(f32[8,128]{1,0:T(8,128)S(1)} %get-tuple-element.132), channel_id=1, source_target_pairs={{1,2},{2,1},{3,18},{18,3},{19,16},{16,19},{17,20},{20,17},{21,22},... | collective-permute-start | bytes 12296 | tf_op jit(solution)/shard_map/ppermute | solution.py:432
  94.6 3.8 %collective-permute-start.20 = (f32[8,128]{1,0:T(8,128)S(1)}, f32[8,128]{1,0:T(8,128)S(1)}, u32[]{:S(2)}, u32[]{:S(2)}) collective-permute-start(f32[8,128]{1,0:T(8,128)S(1)} %get-tuple-element.137), channel_id=1, source_target_pairs={{0,1},{1,0},{2,3},{3,2},{4,5},{5,4},{6,7},{7,6},{8,9},{9,8},{10,11... | collective-permute-start | bytes 12296 | tf_op jit(solution)/shard_map/ppermute | solution.py:433
  94.9 4.9 %collective-permute-start.21 = (f32[8,128]{1,0:T(8,128)S(1)}, f32[8,128]{1,0:T(8,128)S(1)}, u32[]{:S(2)}, u32[]{:S(2)}) collective-permute-start(f32[8,128]{1,0:T(8,128)S(1)} %get-tuple-element.138), channel_id=1, source_target_pairs={{1,2},{2,1},{3,18},{18,3},{19,16},{16,19},{17,20},{20,17},{21,22},... | collective-permute-start | bytes 12296 | tf_op jit(solution)/shard_map/ppermute | solution.py:432
  100.5 4.0 %collective-permute-start.22 = (f32[8,128]{1,0:T(8,128)S(1)}, f32[8,128]{1,0:T(8,128)S(1)}, u32[]{:S(2)}, u32[]{:S(2)}) collective-permute-start(f32[8,128]{1,0:T(8,128)S(1)} %get-tuple-element.144), channel_id=1, source_target_pairs={{0,1},{1,0},{2,3},{3,2},{4,5},{5,4},{6,7},{7,6},{8,9},{9,8},{10,11... | collective-permute-start | bytes 12296 | tf_op jit(solution)/shard_map/ppermute | solution.py:433
  100.9 4.9 %collective-permute-start.23 = (f32[8,128]{1,0:T(8,128)S(1)}, f32[8,128]{1,0:T(8,128)S(1)}, u32[]{:S(2)}, u32[]{:S(2)}) collective-permute-start(f32[8,128]{1,0:T(8,128)S(1)} %get-tuple-element.145), channel_id=1, source_target_pairs={{1,2},{2,1},{3,18},{18,3},{19,16},{16,19},{17,20},{20,17},{21,22},... | collective-permute-start | bytes 12296 | tf_op jit(solution)/shard_map/ppermute | solution.py:432
  106.6 3.8 %collective-permute-start.24 = (f32[8,128]{1,0:T(8,128)S(1)}, f32[8,128]{1,0:T(8,128)S(1)}, u32[]{:S(2)}, u32[]{:S(2)}) collective-permute-start(f32[8,128]{1,0:T(8,128)S(1)} %get-tuple-element.147), channel_id=1, source_target_pairs={{0,1},{1,0},{2,3},{3,2},{4,5},{5,4},{6,7},{7,6},{8,9},{9,8},{10,11... | collective-permute-start | bytes 12296 | tf_op jit(solution)/shard_map/ppermute | solution.py:433
  106.8 4.9 %collective-permute-start.25 = (f32[8,128]{1,0:T(8,128)S(1)}, f32[8,128]{1,0:T(8,128)S(1)}, u32[]{:S(2)}, u32[]{:S(2)}) collective-permute-start(f32[8,128]{1,0:T(8,128)S(1)} %get-tuple-element.148), channel_id=1, source_target_pairs={{1,2},{2,1},{3,18},{18,3},{19,16},{16,19},{17,20},{20,17},{21,22},... | collective-permute-start | bytes 12296 | tf_op jit(solution)/shard_map/ppermute | solution.py:432
  112.4 4.0 %collective-permute-start.26 = (f32[8,128]{1,0:T(8,128)S(1)}, f32[8,128]{1,0:T(8,128)S(1)}, u32[]{:S(2)}, u32[]{:S(2)}) collective-permute-start(f32[8,128]{1,0:T(8,128)S(1)} %get-tuple-element.153), channel_id=1, source_target_pairs={{0,1},{1,0},{2,3},{3,2},{4,5},{5,4},{6,7},{7,6},{8,9},{9,8},{10,11... | collective-permute-start | bytes 12296 | tf_op jit(solution)/shard_map/ppermute | solution.py:433
  112.8 4.9 %collective-permute-start.27 = (f32[8,128]{1,0:T(8,128)S(1)}, f32[8,128]{1,0:T(8,128)S(1)}, u32[]{:S(2)}, u32[]{:S(2)}) collective-permute-start(f32[8,128]{1,0:T(8,128)S(1)} %get-tuple-element.154), channel_id=1, source_target_pairs={{1,2},{2,1},{3,18},{18,3},{19,16},{16,19},{17,20},{20,17},{21,22},... | collective-permute-start | bytes 12296 | tf_op jit(solution)/shard_map/ppermute | solution.py:432
  118.5 4.0 %collective-permute-start.28 = (f32[8,128]{1,0:T(8,128)S(1)}, f32[8,128]{1,0:T(8,128)S(1)}, u32[]{:S(2)}, u32[]{:S(2)}) collective-permute-start(f32[8,128]{1,0:T(8,128)S(1)} %get-tuple-element.159), channel_id=1, source_target_pairs={{0,1},{1,0},{2,3},{3,2},{4,5},{5,4},{6,7},{7,6},{8,9},{9,8},{10,11... | collective-permute-start | bytes 12296 | tf_op jit(solution)/shard_map/ppermute | solution.py:433
  118.7 4.9 %collective-permute-start.29 = (f32[8,128]{1,0:T(8,128)S(1)}, f32[8,128]{1,0:T(8,128)S(1)}, u32[]{:S(2)}, u32[]{:S(2)}) collective-permute-start(f32[8,128]{1,0:T(8,128)S(1)} %get-tuple-element.160), channel_id=1, source_target_pairs={{1,2},{2,1},{3,18},{18,3},{19,16},{16,19},{17,20},{20,17},{21,22},... | collective-permute-start | bytes 12296 | tf_op jit(solution)/shard_map/ppermute | solution.py:432
  124.4 4.0 %collective-permute-start.30 = (f32[8,128]{1,0:T(8,128)S(1)}, f32[8,128]{1,0:T(8,128)S(1)}, u32[]{:S(2)}, u32[]{:S(2)}) collective-permute-start(f32[8,128]{1,0:T(8,128)S(1)} %get-tuple-element.166), channel_id=1, source_target_pairs={{0,1},{1,0},{2,3},{3,2},{4,5},{5,4},{6,7},{7,6},{8,9},{9,8},{10,11... | collective-permute-start | bytes 12296 | tf_op jit(solution)/shard_map/ppermute | solution.py:433
  124.8 4.9 %collective-permute-start.31 = (f32[8,128]{1,0:T(8,128)S(1)}, f32[8,128]{1,0:T(8,128)S(1)}, u32[]{:S(2)}, u32[]{:S(2)}) collective-permute-start(f32[8,128]{1,0:T(8,128)S(1)} %get-tuple-element.167), channel_id=1, source_target_pairs={{1,2},{2,1},{3,18},{18,3},{19,16},{16,19},{17,20},{20,17},{21,22},... | collective-permute-start | bytes 12296 | tf_op jit(solution)/shard_map/ppermute | solution.py:432
  130.4 3.8 %collective-permute-start.32 = (f32[8,128]{1,0:T(8,128)S(1)}, f32[8,128]{1,0:T(8,128)S(1)}, u32[]{:S(2)}, u32[]{:S(2)}) collective-permute-start(f32[8,128]{1,0:T(8,128)S(1)} %get-tuple-element.169), channel_id=1, source_target_pairs={{0,1},{1,0},{2,3},{3,2},{4,5},{5,4},{6,7},{7,6},{8,9},{9,8},{10,11... | collective-permute-start | bytes 12296 | tf_op jit(solution)/shard_map/ppermute | solution.py:433
  130.7 4.9 %collective-permute-start.33 = (f32[8,128]{1,0:T(8,128)S(1)}, f32[8,128]{1,0:T(8,128)S(1)}, u32[]{:S(2)}, u32[]{:S(2)}) collective-permute-start(f32[8,128]{1,0:T(8,128)S(1)} %get-tuple-element.170), channel_id=1, source_target_pairs={{1,2},{2,1},{3,18},{18,3},{19,16},{16,19},{17,20},{20,17},{21,22},... | collective-permute-start | bytes 12296 | tf_op jit(solution)/shard_map/ppermute | solution.py:432
  136.3 4.0 %collective-permute-start.34 = (f32[8,128]{1,0:T(8,128)S(1)}, f32[8,128]{1,0:T(8,128)S(1)}, u32[]{:S(2)}, u32[]{:S(2)}) collective-permute-start(f32[8,128]{1,0:T(8,128)S(1)} %get-tuple-element.175), channel_id=1, source_target_pairs={{0,1},{1,0},{2,3},{3,2},{4,5},{5,4},{6,7},{7,6},{8,9},{9,8},{10,11... | collective-permute-start | bytes 12296 | tf_op jit(solution)/shard_map/ppermute | solution.py:433
  136.7 4.9 %collective-permute-start.35 = (f32[8,128]{1,0:T(8,128)S(1)}, f32[8,128]{1,0:T(8,128)S(1)}, u32[]{:S(2)}, u32[]{:S(2)}) collective-permute-start(f32[8,128]{1,0:T(8,128)S(1)} %get-tuple-element.176), channel_id=1, source_target_pairs={{1,2},{2,1},{3,18},{18,3},{19,16},{16,19},{17,20},{20,17},{21,22},... | collective-permute-start | bytes 12296 | tf_op jit(solution)/shard_map/ppermute | solution.py:432
  142.3 3.8 %collective-permute-start.36 = (f32[8,128]{1,0:T(8,128)S(1)}, f32[8,128]{1,0:T(8,128)S(1)}, u32[]{:S(2)}, u32[]{:S(2)}) collective-permute-start(f32[8,128]{1,0:T(8,128)S(1)} %get-tuple-element.181), channel_id=1, source_target_pairs={{0,1},{1,0},{2,3},{3,2},{4,5},{5,4},{6,7},{7,6},{8,9},{9,8},{10,11... | collective-permute-start | bytes 12296 | tf_op jit(solution)/shard_map/ppermute | solution.py:433
  142.6 4.9 %collective-permute-start.37 = (f32[8,128]{1,0:T(8,128)S(1)}, f32[8,128]{1,0:T(8,128)S(1)}, u32[]{:S(2)}, u32[]{:S(2)}) collective-permute-start(f32[8,128]{1,0:T(8,128)S(1)} %get-tuple-element.182), channel_id=1, source_target_pairs={{1,2},{2,1},{3,18},{18,3},{19,16},{16,19},{17,20},{20,17},{21,22},... | collective-permute-start | bytes 12296 | tf_op jit(solution)/shard_map/ppermute | solution.py:432
  148.0 6.3 %collective-permute-start.38 = (f32[4,2,2,128]{3,2,1,0:T(2,128)S(1)}, f32[4,2,2,128]{3,2,1,0:T(2,128)S(1)}, u32[]{:S(2)}, u32[]{:S(2)}) collective-permute-start(f32[4,2,2,128]{3,2,1,0:T(2,128)S(1)} %rev.24), channel_id=1, source_target_pairs={{1,0},{3,1},{19,2},{17,3},{21,4},{23,5},{7,6},{5,7},{9,8},{11,9},{... | collective-permute-start | bytes 24584 | tf_op jit(solution)/shard_map/ppermute | solution.py:445
  152.4 5.5 %collective-permute-start.39 = (f32[4,2,2,128]{3,2,1,0:T(2,128)S(1)}, f32[4,2,2,128]{3,2,1,0:T(2,128)S(1)}, u32[]{:S(2)}, u32[]{:S(2)}) collective-permute-start(f32[4,2,2,128]{3,2,1,0:T(2,128)S(1)} %get-tuple-element.198), channel_id=1, source_target_pairs={{0,0},{2,1},{18,2},{16,3},{20,4},{22,5},{6,6},{4,7},{8,8},{10,9},{... | collective-permute-start | bytes 24584 | tf_op jit(solution)/shard_map/ppermute | solution.py:444

commit v4 on v3

--- a/solution.py
+++ b/solution.py
@@ -214,8 +214,8 @@
     return rounds
 
 
-def pack_kernel(row_ref, pattern_ref, own_ref, nb_ref, send_0, send_1, facing_0, facing_1):
-    y = row_ref[0]
+def pack_kernel(n_col, place_ref, pattern_ref, own_ref, nb_ref, send_0, send_1, facing_0, facing_1):
+    y, col = place_ref[0], place_ref[1]
     rows = (y, 1 - y)
     inward, outward = 1 - y, y
     cols = own_ref.shape[1]
@@ -228,11 +228,13 @@
         k = (y + i) % 2
         at = [b + k * (cols - 1 - 2 * b) for b in range(HALF)]
         side_a, side_b = 3 - k, 2 + k
+        inside = jnp.where(col == k * (n_col - 1), 0.0, 1.0)
         for h in range(ROWS):
             for b in range(HALF):
                 send[OWN + h * HALF + b] = own_ref[rows[h], at[b]]
                 send[SIDE_A + h * HALF + b] = coupling(side_a, rows[h], at[b])
-                send[SIDE_B + h * HALF + b] = coupling(side_b, rows[h], at[b])
+                block = coupling(side_b, rows[h], at[b])
+                send[SIDE_B + h * HALF + b] = block * inside if b == 0 else block
             send[FACING + h] = coupling(2 + k, rows[h], HALF - k)
             facing[h] = coupling(3 - k, rows[h], (cols - 1) * (1 - k))
         for b in range(HALF):
@@ -374,7 +376,7 @@
     deal = deal_pairs(n_col, 0)
     deal_b = deal_pairs(n_col, 1)
     a_pairs = [(c, c ^ 1) for c in range(n_col)]
-    b_pairs = []
+    b_pairs = [(unit_device(unit, n_col),) * 2 for unit in (0, 2 * n_col - 1)]
     for unit in range(1, 2 * n_col - 1, 2):
         one, two = unit_device(unit, n_col), unit_device(unit + 1, n_col)
         b_pairs += [(one, two), (two, one)]
@@ -385,13 +387,14 @@
     packed = jax.ShapeDtypeStruct((PACKED, width, width), jnp.float32)
     facing = jax.ShapeDtypeStruct((ROWS, width, width), jnp.float32)
     send_0, send_1, facing_0, facing_1 = pl.pallas_call(
-        pack_kernel,
+        functools.partial(pack_kernel, n_col),
         out_shape=(packed, packed, facing, facing),
         in_specs=[smem, smem, vmem, vmem],
         out_specs=(vmem,) * 4,
         compiler_params=limit,
         name="pack",
-    )(row.astype(jnp.int32).reshape(1), pattern.reshape(-1), own_block, neighbor_block)
+    )(jnp.stack([row, lax.axis_index("col")]).astype(jnp.int32), pattern.reshape(-1), own_block, neighbor_block)
+    currents, slot_tile, facing_0, facing_1 = lax.optimization_barrier((currents, slot_tile, facing_0, facing_1))
     half_0 = lax.ppermute(send_0, both, deal[0])
     half_1 = lax.ppermute(send_1, both, deal[1])
     beyond_0 = lax.ppermute(facing_0, both, deal_b[0])

time: 160 us -> 159 us (level)
  waiting for transfers between devices: 44.6 us -> 50.2 us
  starting transfers between devices: 92.4 us -> 86.9 us
    ppermute x16, starting transfers between devices: 57.3 us -> 51.9 us  [shards_chain(): got_b = lax.ppermute(msg_b, both, b_pairs)]
    ppermute x16, waiting for transfers between devices: 20.4 us -> 25 us  [shards_chain(): got_b = lax.ppermute(msg_b, both, b_pairs)]
    unnamed x12 -> x17, local copies, waits for them, and re-layouts: 3.78 us -> 3.83 us
  transfers between devices with their start and end apart: 41 -> 41, of which waited for: 19 -> 19; matrix products, arithmetic and copies ran while one was open for 1% -> 0% of each run, Pallas kernels for 2% -> 0%
where the time goes in v4:
time: 159 us; the launch traced here: 158 us
  starting transfers between devices  86.9 us (55%)
  waiting for transfers between devices  50.2 us (32%)
  Pallas kernels  13.4 us (8%)
  local copies, waits for them, and re-layouts  5.14 us (3%)
    ppermute x16, starting transfers between devices, shards_chain(): got_b = lax.ppermute(msg_b, both, b_pairs)  51.9 us
    ppermute x16, waiting for transfers between devices, shards_chain(): got_b = lax.ppermute(msg_b, both, b_pairs)  25 us
    ppermute x1, waiting for transfers between devices, shards_chain(): got_1 = lax.ppermute(jnp.where(row == 1, unit_0, unit_1), both, deal[1])  20.2 us
    pallas_call x17, Pallas kernels, call(): pl.pallas_call(body, out_shape=(shape,) * n_out, in_specs=[vmem] * len(in...  11.6 us
    all_to_all x1, starting transfers between devices, collect(): lax.all_to_all(packed, 'col', split_axis=2, concat_axis=1, tiled=True)  6.27 us
    ppermute x16, starting transfers between devices, shards_chain(): got_a = lax.ppermute(msg_a, 'col', a_pairs)  5.1 us
    ppermute x1, starting transfers between devices, shards_chain(): lax.ppermute(jnp.flip(done[:, ROWS:], 1), both, [(b, a) for a, b in deal[...  3.99 us
    unnamed x17, local copies, waits for them, and re-layouts  3.83 us
  transfers between devices with their start and end apart: 41, of which 19 were waited for; matrix products, arithmetic and copies ran while one was open for 0% of the time, Pallas kernels for 0%

profile of v4, /device:TPU:8, one launch (start us, length us, event | category | flops | bytes accessed | tf_op | source)
XLA Modules:
  0.0 158.0 jit_solution(541268327916123814)
XLA Ops:
  0.8 1.6 %copy-done = f32[4,2,4,128,128]{4,3,2,1,0:T(8,128)S(1)} copy-done((f32[4,2,4,128,128]{4,3,2,1,0:T(8,128)S(1)}, f32[4,2,4,128,128]{4,3,2,1,0:T(8,128)}, u32[]{:S(2)}) %copy-start) | copy-done | bytes 2097176
  2.4 1.0 copy-done.1
  3.5 1.8 %pack.1 = (f32[20,128,128]{2,1,0:T(8,128)}, f32[20,128,128]{2,1,0:T(8,128)S(1)}, f32[2,128,128]{2,1,0:T(8,128)S(1)}, f32[2,128,128]{2,1,0:T(8,128)S(1)}) custom-call(s32[2]{0:T(128)S(1)} %pad_add_fusion.place_ref, s32[32]{0:T(128)S(1)} %reshape.20.pattern_ref, f32[2,4,128,128]{3,2,1,0:T(8,128)S(1)} %copy-done.1, f32[4,2,4,128,128]{4,3,2,1,0:T(8,128)S(1)} %copy-done), custom_call_target="tpu_custom_call" | custom-call | tf_op jit(solution)/shard_map/pack/pallas_call | solution.py:389
  5.3 1.1 copy-done.2
  6.6 0.8 fusion
  7.4 6.3 %all-to-all-start = ((f32[1,1,16,5,512]{4,1,3,0,2:T(1,128)}), f32[1,1,16,5,512]{4,1,3,0,2:T(1,128)S(1)}, u32[]{:S(2)}, u32[]{:S(2)}) async-start(f32[1,1,16,5,512]{4,1,3,0,2:T(1,128)} %fusion), calls=%async_computation | async-start | bytes 327680 | tf_op jit(solution)/shard_map/all_to_all | solution.py:131
  13.7 3.4 %collective-permute-start = (f32[20,128,128]{2,1,0:T(8,128)}, f32[20,128,128]{2,1,0:T(8,128)S(1)}, u32[]{:S(2)}, u32[]{:S(2)}) collective-permute-start(f32[20,128,128]{2,1,0:T(8,128)} %get-tuple-element.100), channel_id=1, source_target_pairs={{0,0},{1,2},{2,18},{3,16},{4,20},{5,22},{6,6},{7,4},{8,8},{9,10},{... | collective-permute-start | bytes 3932168 | tf_op jit(solution)/shard_map/ppermute | solution.py:398
  17.1 2.8 %collective-permute-start.1 = (f32[20,128,128]{2,1,0:T(8,128)}, f32[20,128,128]{2,1,0:T(8,128)S(1)}, u32[]{:S(2)}, u32[]{:S(2)}) collective-permute-start(f32[20,128,128]{2,1,0:T(8,128)} %copy-done.2), channel_id=1, source_target_pairs={{0,1},{1,3},{2,19},{3,17},{4,21},{5,23},{6,7},{7,5},{8,9},{9,11},{... | collective-permute-start | bytes 3932168 | tf_op jit(solution)/shard_map/ppermute | solution.py:399
  20.6 3.4 %collective-permute-start.5 = (f32[2,2,768]{2,1,0:T(2,128)S(1)}, f32[2,2,768]{2,1,0:T(2,128)S(1)}, u32[]{:S(2)}, u32[]{:S(2)}) collective-permute-start(f32[2,2,768]{2,1,0:T(2,128)S(1)} %get-tuple-element.196), channel_id=1, source_target_pairs={{0,1},{1,3},{2,19},{3,17},{4,21},{5,23},{6,7},{7,5},{8,9},{9,11},{... | collective-permute-start | bytes 36872 | tf_op jit(solution)/shard_map/ppermute | solution.py:410
  24.1 1.9 %collective-permute-start.4 = (f32[2,2,768]{2,1,0:T(2,128)S(1)}, f32[2,2,768]{2,1,0:T(2,128)S(1)}, u32[]{:S(2)}, u32[]{:S(2)}) collective-permute-start(f32[2,2,768]{2,1,0:T(2,128)S(1)} %get-tuple-element.195), channel_id=1, source_target_pairs={{0,0},{1,2},{2,18},{3,16},{4,20},{5,22},{6,6},{7,4},{8,8},{9,10},{... | collective-permute-start | bytes 36872 | tf_op jit(solution)/shard_map/ppermute | solution.py:409
  26.0 3.6 %collective-permute-start.2 = (f32[2,128,128]{2,1,0:T(8,128)S(1)}, f32[2,128,128]{2,1,0:T(8,128)S(1)}, u32[]{:S(2)}, u32[]{:S(2)}) collective-permute-start(f32[2,128,128]{2,1,0:T(8,128)S(1)} %get-tuple-element.104), channel_id=1, source_target_pairs={{0,2},{1,18},{2,16},{3,20},{4,22},{5,6},{6,4},{7,8},{8,10},{9,26},... | collective-permute-start | bytes 393224 | tf_op jit(solution)/shard_map/ppermute | solution.py:400
  29.6 20.2 %collective-permute-done.5 = f32[2,2,768]{2,1,0:T(2,128)S(1)} collective-permute-done((f32[2,2,768]{2,1,0:T(2,128)S(1)}, f32[2,2,768]{2,1,0:T(2,128)S(1)}, u32[]{:S(2)}, u32[]{:S(2)}) %collective-permute-start.5) | collective-permute-done | bytes 12320 | tf_op jit(solution)/shard_map/ppermute | solution.py:410
  49.8 2.5 %collective-permute-start.3 = (f32[2,128,128]{2,1,0:T(8,128)S(1)}, f32[2,128,128]{2,1,0:T(8,128)S(1)}, u32[]{:S(2)}, u32[]{:S(2)}) collective-permute-start(f32[2,128,128]{2,1,0:T(8,128)S(1)} %get-tuple-element.105), channel_id=1, source_target_pairs={{1,1},{2,3},{3,19},{4,17},{5,21},{6,23},{7,7},{8,5},{9,9},{10,11},... | collective-permute-start | bytes 393224 | tf_op jit(solution)/shard_map/ppermute | solution.py:401
  52.7 3.5 %collective-permute-start.7 = (f32[8,128]{1,0:T(8,128)S(1)}, f32[8,128]{1,0:T(8,128)S(1)}, u32[]{:S(2)}, u32[]{:S(2)}) collective-permute-start(f32[8,128]{1,0:T(8,128)S(1)} %get-tuple-element.109), channel_id=1, source_target_pairs={{0,0},{13,13},{1,2},{2,1},{3,18},{18,3},{19,16},{16,19},{17,20},{2... | collective-permute-start | bytes 12296 | tf_op jit(solution)/shard_map/ppermute | solution.py:435
  56.2 1.4 collective-permute-done.3.beyond_1
  58.9 3.0 %collective-permute-start.9 = (f32[8,128]{1,0:T(8,128)S(1)}, f32[8,128]{1,0:T(8,128)S(1)}, u32[]{:S(2)}, u32[]{:S(2)}) collective-permute-start(f32[8,128]{1,0:T(8,128)S(1)} %get-tuple-element.112), channel_id=1, source_target_pairs={{0,0},{13,13},{1,2},{2,1},{3,18},{18,3},{19,16},{16,19},{17,20},{2... | collective-permute-start | bytes 12296 | tf_op jit(solution)/shard_map/ppermute | solution.py:435
  61.9 1.9 %collective-permute-done.9.got_b = f32[8,128]{1,0:T(8,128)S(1)} collective-permute-done((f32[8,128]{1,0:T(8,128)S(1)}, f32[8,128]{1,0:T(8,128)S(1)}, u32[]{:S(2)}, u32[]{:S(2)}) %collective-permute-start.9) | collective-permute-done | bytes 4128 | tf_op jit(solution)/shard_map/ppermute | solution.py:435
  64.7 3.4 %collective-permute-start.11 = (f32[8,128]{1,0:T(8,128)S(1)}, f32[8,128]{1,0:T(8,128)S(1)}, u32[]{:S(2)}, u32[]{:S(2)}) collective-permute-start(f32[8,128]{1,0:T(8,128)S(1)} %get-tuple-element.118), channel_id=1, source_target_pairs={{0,0},{13,13},{1,2},{2,1},{3,18},{18,3},{19,16},{16,19},{17,20},{2... | collective-permute-start | bytes 12296 | tf_op jit(solution)/shard_map/ppermute | solution.py:435
  68.1 1.5 collective-permute-done.11.got_b
  70.8 3.1 %collective-permute-start.13 = (f32[8,128]{1,0:T(8,128)S(1)}, f32[8,128]{1,0:T(8,128)S(1)}, u32[]{:S(2)}, u32[]{:S(2)}) collective-permute-start(f32[8,128]{1,0:T(8,128)S(1)} %get-tuple-element.124), channel_id=1, source_target_pairs={{0,0},{13,13},{1,2},{2,1},{3,18},{18,3},{19,16},{16,19},{17,20},{2... | collective-permute-start | bytes 12296 | tf_op jit(solution)/shard_map/ppermute | solution.py:435
  73.9 1.8 %collective-permute-done.13.got_b = f32[8,128]{1,0:T(8,128)S(1)} collective-permute-done((f32[8,128]{1,0:T(8,128)S(1)}, f32[8,128]{1,0:T(8,128)S(1)}, u32[]{:S(2)}, u32[]{:S(2)}) %collective-permute-start.13) | collective-permute-done | bytes 4128 | tf_op jit(solution)/shard_map/ppermute | solution.py:435
  76.6 3.4 %collective-permute-start.15 = (f32[8,128]{1,0:T(8,128)S(1)}, f32[8,128]{1,0:T(8,128)S(1)}, u32[]{:S(2)}, u32[]{:S(2)}) collective-permute-start(f32[8,128]{1,0:T(8,128)S(1)} %get-tuple-element.131), channel_id=1, source_target_pairs={{0,0},{13,13},{1,2},{2,1},{3,18},{18,3},{19,16},{16,19},{17,20},{2... | collective-permute-start | bytes 12296 | tf_op jit(solution)/shard_map/ppermute | solution.py:435
  80.0 1.5 collective-permute-done.15.got_b
  82.7 3.1 %collective-permute-start.17 = (f32[8,128]{1,0:T(8,128)S(1)}, f32[8,128]{1,0:T(8,128)S(1)}, u32[]{:S(2)}, u32[]{:S(2)}) collective-permute-start(f32[8,128]{1,0:T(8,128)S(1)} %get-tuple-element.134), channel_id=1, source_target_pairs={{0,0},{13,13},{1,2},{2,1},{3,18},{18,3},{19,16},{16,19},{17,20},{2... | collective-permute-start | bytes 12296 | tf_op jit(solution)/shard_map/ppermute | solution.py:435
  85.8 1.8 %collective-permute-done.17.got_b = f32[8,128]{1,0:T(8,128)S(1)} collective-permute-done((f32[8,128]{1,0:T(8,128)S(1)}, f32[8,128]{1,0:T(8,128)S(1)}, u32[]{:S(2)}, u32[]{:S(2)}) %collective-permute-start.17) | collective-permute-done | bytes 4128 | tf_op jit(solution)/shard_map/ppermute | solution.py:435
  88.5 3.4 %collective-permute-start.19 = (f32[8,128]{1,0:T(8,128)S(1)}, f32[8,128]{1,0:T(8,128)S(1)}, u32[]{:S(2)}, u32[]{:S(2)}) collective-permute-start(f32[8,128]{1,0:T(8,128)S(1)} %get-tuple-element.140), channel_id=1, source_target_pairs={{0,0},{13,13},{1,2},{2,1},{3,18},{18,3},{19,16},{16,19},{17,20},{2... | collective-permute-start | bytes 12296 | tf_op jit(solution)/shard_map/ppermute | solution.py:435
  91.9 1.5 collective-permute-done.19.got_b
  94.6 3.1 %collective-permute-start.21 = (f32[8,128]{1,0:T(8,128)S(1)}, f32[8,128]{1,0:T(8,128)S(1)}, u32[]{:S(2)}, u32[]{:S(2)}) collective-permute-start(f32[8,128]{1,0:T(8,128)S(1)} %get-tuple-element.146), channel_id=1, source_target_pairs={{0,0},{13,13},{1,2},{2,1},{3,18},{18,3},{19,16},{16,19},{17,20},{2... | collective-permute-start | bytes 12296 | tf_op jit(solution)/shard_map/ppermute | solution.py:435
  97.8 1.8 %collective-permute-done.21.got_b = f32[8,128]{1,0:T(8,128)S(1)} collective-permute-done((f32[8,128]{1,0:T(8,128)S(1)}, f32[8,128]{1,0:T(8,128)S(1)}, u32[]{:S(2)}, u32[]{:S(2)}) %collective-permute-start.21) | collective-permute-done | bytes 4128 | tf_op jit(solution)/shard_map/ppermute | solution.py:435
  100.5 3.4 %collective-permute-start.23 = (f32[8,128]{1,0:T(8,128)S(1)}, f32[8,128]{1,0:T(8,128)S(1)}, u32[]{:S(2)}, u32[]{:S(2)}) collective-permute-start(f32[8,128]{1,0:T(8,128)S(1)} %get-tuple-element.153), channel_id=1, source_target_pairs={{0,0},{13,13},{1,2},{2,1},{3,18},{18,3},{19,16},{16,19},{17,20},{2... | collective-permute-start | bytes 12296 | tf_op jit(solution)/shard_map/ppermute | solution.py:435
  103.9 1.5 collective-permute-done.23.got_b
  106.6 3.1 %collective-permute-start.25 = (f32[8,128]{1,0:T(8,128)S(1)}, f32[8,128]{1,0:T(8,128)S(1)}, u32[]{:S(2)}, u32[]{:S(2)}) collective-permute-start(f32[8,128]{1,0:T(8,128)S(1)} %get-tuple-element.156), channel_id=1, source_target_pairs={{0,0},{13,13},{1,2},{2,1},{3,18},{18,3},{19,16},{16,19},{17,20},{2... | collective-permute-start | bytes 12296 | tf_op jit(solution)/shard_map/ppermute | solution.py:435
  109.7 1.8 %collective-permute-done.25.got_b = f32[8,128]{1,0:T(8,128)S(1)} collective-permute-done((f32[8,128]{1,0:T(8,128)S(1)}, f32[8,128]{1,0:T(8,128)S(1)}, u32[]{:S(2)}, u32[]{:S(2)}) %collective-permute-start.25) | collective-permute-done | bytes 4128 | tf_op jit(solution)/shard_map/ppermute | solution.py:435
  112.4 3.4 %collective-permute-start.27 = (f32[8,128]{1,0:T(8,128)S(1)}, f32[8,128]{1,0:T(8,128)S(1)}, u32[]{:S(2)}, u32[]{:S(2)}) collective-permute-start(f32[8,128]{1,0:T(8,128)S(1)} %get-tuple-element.162), channel_id=1, source_target_pairs={{0,0},{13,13},{1,2},{2,1},{3,18},{18,3},{19,16},{16,19},{17,20},{2... | collective-permute-start | bytes 12296 | tf_op jit(solution)/shard_map/ppermute | solution.py:435
  115.8 1.5 collective-permute-done.27.got_b
  118.5 3.3 %collective-permute-start.29 = (f32[8,128]{1,0:T(8,128)S(1)}, f32[8,128]{1,0:T(8,128)S(1)}, u32[]{:S(2)}, u32[]{:S(2)}) collective-permute-start(f32[8,128]{1,0:T(8,128)S(1)} %get-tuple-element.168), channel_id=1, source_target_pairs={{0,0},{13,13},{1,2},{2,1},{3,18},{18,3},{19,16},{16,19},{17,20},{2... | collective-permute-start | bytes 12296 | tf_op jit(solution)/shard_map/ppermute | solution.py:435
  121.8 1.6 %collective-permute-done.29.got_b = f32[8,128]{1,0:T(8,128)S(1)} collective-permute-done((f32[8,128]{1,0:T(8,128)S(1)}, f32[8,128]{1,0:T(8,128)S(1)}, u32[]{:S(2)}, u32[]{:S(2)}) %collective-permute-start.29) | collective-permute-done | bytes 4128 | tf_op jit(solution)/shard_map/ppermute | solution.py:435
  124.3 3.4 %collective-permute-start.31 = (f32[8,128]{1,0:T(8,128)S(1)}, f32[8,128]{1,0:T(8,128)S(1)}, u32[]{:S(2)}, u32[]{:S(2)}) collective-permute-start(f32[8,128]{1,0:T(8,128)S(1)} %get-tuple-element.175), channel_id=1, source_target_pairs={{0,0},{13,13},{1,2},{2,1},{3,18},{18,3},{19,16},{16,19},{17,20},{2... | collective-permute-start | bytes 12296 | tf_op jit(solution)/shard_map/ppermute | solution.py:435
  127.7 1.5 collective-permute-done.31.got_b
  130.4 3.1 %collective-permute-start.33 = (f32[8,128]{1,0:T(8,128)S(1)}, f32[8,128]{1,0:T(8,128)S(1)}, u32[]{:S(2)}, u32[]{:S(2)}) collective-permute-start(f32[8,128]{1,0:T(8,128)S(1)} %get-tuple-element.178), channel_id=1, source_target_pairs={{0,0},{13,13},{1,2},{2,1},{3,18},{18,3},{19,16},{16,19},{17,20},{2... | collective-permute-start | bytes 12296 | tf_op jit(solution)/shard_map/ppermute | solution.py:435
  133.5 1.8 %collective-permute-done.33.got_b = f32[8,128]{1,0:T(8,128)S(1)} collective-permute-done((f32[8,128]{1,0:T(8,128)S(1)}, f32[8,128]{1,0:T(8,128)S(1)}, u32[]{:S(2)}, u32[]{:S(2)}) %collective-permute-start.33) | collective-permute-done | bytes 4128 | tf_op jit(solution)/shard_map/ppermute | solution.py:435
  136.2 3.4 %collective-permute-start.35 = (f32[8,128]{1,0:T(8,128)S(1)}, f32[8,128]{1,0:T(8,128)S(1)}, u32[]{:S(2)}, u32[]{:S(2)}) collective-permute-start(f32[8,128]{1,0:T(8,128)S(1)} %get-tuple-element.184), channel_id=1, source_target_pairs={{0,0},{13,13},{1,2},{2,1},{3,18},{18,3},{19,16},{16,19},{17,20},{2... | collective-permute-start | bytes 12296 | tf_op jit(solution)/shard_map/ppermute | solution.py:435
  139.6 1.5 collective-permute-done.35.got_b
  142.3 3.1 %collective-permute-start.37 = (f32[8,128]{1,0:T(8,128)S(1)}, f32[8,128]{1,0:T(8,128)S(1)}, u32[]{:S(2)}, u32[]{:S(2)}) collective-permute-start(f32[8,128]{1,0:T(8,128)S(1)} %get-tuple-element.190), channel_id=1, source_target_pairs={{0,0},{13,13},{1,2},{2,1},{3,18},{18,3},{19,16},{16,19},{17,20},{2... | collective-permute-start | bytes 12296 | tf_op jit(solution)/shard_map/ppermute | solution.py:435
  145.4 1.8 %collective-permute-done.37.got_b = f32[8,128]{1,0:T(8,128)S(1)} collective-permute-done((f32[8,128]{1,0:T(8,128)S(1)}, f32[8,128]{1,0:T(8,128)S(1)}, u32[]{:S(2)}, u32[]{:S(2)}) %collective-permute-start.37) | collective-permute-done | bytes 4128 | tf_op jit(solution)/shard_map/ppermute | solution.py:435
  147.8 4.0 %collective-permute-start.38 = (f32[4,2,2,128]{3,2,1,0:T(2,128)S(1)}, f32[4,2,2,128]{3,2,1,0:T(2,128)S(1)}, u32[]{:S(2)}, u32[]{:S(2)}) collective-permute-start(f32[4,2,2,128]{3,2,1,0:T(2,128)S(1)} %rev.24), channel_id=1, source_target_pairs={{1,0},{3,1},{19,2},{17,3},{21,4},{23,5},{7,6},{5,7},{9,8},{11,9},{... | collective-permute-start | bytes 24584 | tf_op jit(solution)/shard_map/ppermute | solution.py:448
  151.8 1.9 %collective-permute-start.39 = (f32[4,2,2,128]{3,2,1,0:T(2,128)S(1)}, f32[4,2,2,128]{3,2,1,0:T(2,128)S(1)}, u32[]{:S(2)}, u32[]{:S(2)}) collective-permute-start(f32[4,2,2,128]{3,2,1,0:T(2,128)S(1)} %get-tuple-element.206), channel_id=1, source_target_pairs={{0,0},{2,1},{18,2},{16,3},{20,4},{22,5},{6,6},{4,7},{8,8},{10,9},{... | collective-permute-start | bytes 24584 | tf_op jit(solution)/shard_map/ppermute | solution.py:447
  153.7 3.6 %collective-permute-done.39 = f32[4,2,2,128]{3,2,1,0:T(2,128)S(1)} collective-permute-done((f32[4,2,2,128]{3,2,1,0:T(2,128)S(1)}, f32[4,2,2,128]{3,2,1,0:T(2,128)S(1)}, u32[]{:S(2)}, u32[]{:S(2)}) %collective-permute-start.39) | collective-permute-done | bytes 8224 | tf_op jit(solution)/shard_map/ppermute | solution.py:447
  (95 shorter events, 19.2 us)
Async XLA Ops:
  0.8 1.6 %copy-start = (f32[4,2,4,128,128]{4,3,2,1,0:T(8,128)S(1)}, f32[4,2,4,128,128]{4,3,2,1,0:T(8,128)}, u32[]{:S(2)}) copy-start(f32[4,2,4,128,128]{4,3,2,1,0:T(8,128)} %nb_ref.1) | copy-start | bytes 6291460
  2.4 1.0 copy-start.1
  3.5 2.9 %copy-start.6 = (s32[1,1,16,4]{2,3,1,0:T(4,128)S(1)}, s32[1,1,16,4]{2,3,1,0:T(4,128)}, u32[]{:S(2)}) copy-start(s32[1,1,16,4]{2,3,1,0:T(4,128)} %param.13) | copy-start | bytes 772
  3.5 3.0 %copy-start.3 = (f32[1,1,16,4,512]{4,3,2,1,0:T(4,128)S(1)}, f32[1,1,16,4,512]{4,3,2,1,0:T(4,128)}, u32[]{:S(2)}) copy-start(f32[1,1,16,4,512]{4,3,2,1,0:T(4,128)} %param.12) | copy-start | bytes 393220
  5.3 1.1 copy-start.2
  6.4 14.0 %copy-start.4 = (f32[2,4,128]{2,1,0:T(4,128)S(1)}, f32[2,4,128]{2,1,0:T(4,128)}, u32[]{:S(2)}) copy-start(f32[2,4,128]{2,1,0:T(4,128)} %param.10) | copy-start | bytes 12292
  6.4 14.0 %copy-start.5 = (f32[2,4,128]{2,1,0:T(4,128)S(1)}, f32[2,4,128]{2,1,0:T(4,128)}, u32[]{:S(2)}) copy-start(f32[2,4,128]{2,1,0:T(4,128)} %param.11) | copy-start | bytes 12292
  7.4 12.5 %all-to-all-start = ((f32[1,1,16,5,512]{4,1,3,0,2:T(1,128)}), f32[1,1,16,5,512]{4,1,3,0,2:T(1,128)S(1)}, u32[]{:S(2)}, u32[]{:S(2)}) async-start(f32[1,1,16,5,512]{4,1,3,0,2:T(1,128)} %fusion), calls=%async_computation | async-start | bytes 327680 | tf_op jit(solution)/shard_map/all_to_all | solution.py:131
  13.7 38.7 %collective-permute-start = (f32[20,128,128]{2,1,0:T(8,128)}, f32[20,128,128]{2,1,0:T(8,128)S(1)}, u32[]{:S(2)}, u32[]{:S(2)}) collective-permute-start(f32[20,128,128]{2,1,0:T(8,128)} %get-tuple-element.100), channel_id=1, source_target_pairs={{0,0},{1,2},{2,18},{3,16},{4,20},{5,22},{6,6},{7,4},{8,8},{9,10},{... | collective-permute-start | bytes 3932168 | tf_op jit(solution)/shard_map/ppermute | solution.py:398
  17.1 35.2 %collective-permute-start.1 = (f32[20,128,128]{2,1,0:T(8,128)}, f32[20,128,128]{2,1,0:T(8,128)S(1)}, u32[]{:S(2)}, u32[]{:S(2)}) collective-permute-start(f32[20,128,128]{2,1,0:T(8,128)} %copy-done.2), channel_id=1, source_target_pairs={{0,1},{1,3},{2,19},{3,17},{4,21},{5,23},{6,7},{7,5},{8,9},{9,11},{... | collective-permute-start | bytes 3932168 | tf_op jit(solution)/shard_map/ppermute | solution.py:399
  20.6 29.1 %collective-permute-start.5 = (f32[2,2,768]{2,1,0:T(2,128)S(1)}, f32[2,2,768]{2,1,0:T(2,128)S(1)}, u32[]{:S(2)}, u32[]{:S(2)}) collective-permute-start(f32[2,2,768]{2,1,0:T(2,128)S(1)} %get-tuple-element.196), channel_id=1, source_target_pairs={{0,1},{1,3},{2,19},{3,17},{4,21},{5,23},{6,7},{7,5},{8,9},{9,11},{... | collective-permute-start | bytes 36872 | tf_op jit(solution)/shard_map/ppermute | solution.py:410
  24.1 28.2 %collective-permute-start.4 = (f32[2,2,768]{2,1,0:T(2,128)S(1)}, f32[2,2,768]{2,1,0:T(2,128)S(1)}, u32[]{:S(2)}, u32[]{:S(2)}) collective-permute-start(f32[2,2,768]{2,1,0:T(2,128)S(1)} %get-tuple-element.195), channel_id=1, source_target_pairs={{0,0},{1,2},{2,18},{3,16},{4,20},{5,22},{6,6},{7,4},{8,8},{9,10},{... | collective-permute-start | bytes 36872 | tf_op jit(solution)/shard_map/ppermute | solution.py:409
  26.0 30.2 %collective-permute-start.2 = (f32[2,128,128]{2,1,0:T(8,128)S(1)}, f32[2,128,128]{2,1,0:T(8,128)S(1)}, u32[]{:S(2)}, u32[]{:S(2)}) collective-permute-start(f32[2,128,128]{2,1,0:T(8,128)S(1)} %get-tuple-element.104), channel_id=1, source_target_pairs={{0,2},{1,18},{2,16},{3,20},{4,22},{5,6},{6,4},{7,8},{8,10},{9,26},... | collective-permute-start | bytes 393224 | tf_op jit(solution)/shard_map/ppermute | solution.py:400
  49.8 7.7 %collective-permute-start.3 = (f32[2,128,128]{2,1,0:T(8,128)S(1)}, f32[2,128,128]{2,1,0:T(8,128)S(1)}, u32[]{:S(2)}, u32[]{:S(2)}) collective-permute-start(f32[2,128,128]{2,1,0:T(8,128)S(1)} %get-tuple-element.105), channel_id=1, source_target_pairs={{1,1},{2,3},{3,19},{4,17},{5,21},{6,23},{7,7},{8,5},{9,9},{10,11},... | collective-permute-start | bytes 393224 | tf_op jit(solution)/shard_map/ppermute | solution.py:401
  52.6 4.9 %collective-permute-start.6 = (f32[8,128]{1,0:T(8,128)S(1)}, f32[8,128]{1,0:T(8,128)S(1)}, u32[]{:S(2)}, u32[]{:S(2)}) collective-permute-start(f32[8,128]{1,0:T(8,128)S(1)} %get-tuple-element.108), channel_id=1, source_target_pairs={{0,1},{1,0},{2,3},{3,2},{4,5},{5,4},{6,7},{7,6},{8,9},{9,8},{10,11... | collective-permute-start | bytes 12296 | tf_op jit(solution)/shard_map/ppermute | solution.py:436
  52.7 4.9 %collective-permute-start.7 = (f32[8,128]{1,0:T(8,128)S(1)}, f32[8,128]{1,0:T(8,128)S(1)}, u32[]{:S(2)}, u32[]{:S(2)}) collective-permute-start(f32[8,128]{1,0:T(8,128)S(1)} %get-tuple-element.109), channel_id=1, source_target_pairs={{0,0},{13,13},{1,2},{2,1},{3,18},{18,3},{19,16},{16,19},{17,20},{2... | collective-permute-start | bytes 12296 | tf_op jit(solution)/shard_map/ppermute | solution.py:435
  58.3 3.6 %collective-permute-start.8 = (f32[8,128]{1,0:T(8,128)S(1)}, f32[8,128]{1,0:T(8,128)S(1)}, u32[]{:S(2)}, u32[]{:S(2)}) collective-permute-start(f32[8,128]{1,0:T(8,128)S(1)} %get-tuple-element.111), channel_id=1, source_target_pairs={{0,1},{1,0},{2,3},{3,2},{4,5},{5,4},{6,7},{7,6},{8,9},{9,8},{10,11... | collective-permute-start | bytes 12296 | tf_op jit(solution)/shard_map/ppermute | solution.py:436
  58.9 4.9 %collective-permute-start.9 = (f32[8,128]{1,0:T(8,128)S(1)}, f32[8,128]{1,0:T(8,128)S(1)}, u32[]{:S(2)}, u32[]{:S(2)}) collective-permute-start(f32[8,128]{1,0:T(8,128)S(1)} %get-tuple-element.112), channel_id=1, source_target_pairs={{0,0},{13,13},{1,2},{2,1},{3,18},{18,3},{19,16},{16,19},{17,20},{2... | collective-permute-start | bytes 12296 | tf_op jit(solution)/shard_map/ppermute | solution.py:435
  64.5 3.6 %collective-permute-start.10 = (f32[8,128]{1,0:T(8,128)S(1)}, f32[8,128]{1,0:T(8,128)S(1)}, u32[]{:S(2)}, u32[]{:S(2)}) collective-permute-start(f32[8,128]{1,0:T(8,128)S(1)} %get-tuple-element.117), channel_id=1, source_target_pairs={{0,1},{1,0},{2,3},{3,2},{4,5},{5,4},{6,7},{7,6},{8,9},{9,8},{10,11... | collective-permute-start | bytes 12296 | tf_op jit(solution)/shard_map/ppermute | solution.py:436
  64.7 4.9 %collective-permute-start.11 = (f32[8,128]{1,0:T(8,128)S(1)}, f32[8,128]{1,0:T(8,128)S(1)}, u32[]{:S(2)}, u32[]{:S(2)}) collective-permute-start(f32[8,128]{1,0:T(8,128)S(1)} %get-tuple-element.118), channel_id=1, source_target_pairs={{0,0},{13,13},{1,2},{2,1},{3,18},{18,3},{19,16},{16,19},{17,20},{2... | collective-permute-start | bytes 12296 | tf_op jit(solution)/shard_map/ppermute | solution.py:435
  70.3 3.6 %collective-permute-start.12 = (f32[8,128]{1,0:T(8,128)S(1)}, f32[8,128]{1,0:T(8,128)S(1)}, u32[]{:S(2)}, u32[]{:S(2)}) collective-permute-start(f32[8,128]{1,0:T(8,128)S(1)} %get-tuple-element.123), channel_id=1, source_target_pairs={{0,1},{1,0},{2,3},{3,2},{4,5},{5,4},{6,7},{7,6},{8,9},{9,8},{10,11... | collective-permute-start | bytes 12296 | tf_op jit(solution)/shard_map/ppermute | solution.py:436
  70.8 4.9 %collective-permute-start.13 = (f32[8,128]{1,0:T(8,128)S(1)}, f32[8,128]{1,0:T(8,128)S(1)}, u32[]{:S(2)}, u32[]{:S(2)}) collective-permute-start(f32[8,128]{1,0:T(8,128)S(1)} %get-tuple-element.124), channel_id=1, source_target_pairs={{0,0},{13,13},{1,2},{2,1},{3,18},{18,3},{19,16},{16,19},{17,20},{2... | collective-permute-start | bytes 12296 | tf_op jit(solution)/shard_map/ppermute | solution.py:435
  76.4 3.6 %collective-permute-start.14 = (f32[8,128]{1,0:T(8,128)S(1)}, f32[8,128]{1,0:T(8,128)S(1)}, u32[]{:S(2)}, u32[]{:S(2)}) collective-permute-start(f32[8,128]{1,0:T(8,128)S(1)} %get-tuple-element.130), channel_id=1, source_target_pairs={{0,1},{1,0},{2,3},{3,2},{4,5},{5,4},{6,7},{7,6},{8,9},{9,8},{10,11... | collective-permute-start | bytes 12296 | tf_op jit(solution)/shard_map/ppermute | solution.py:436
  76.6 4.9 %collective-permute-start.15 = (f32[8,128]{1,0:T(8,128)S(1)}, f32[8,128]{1,0:T(8,128)S(1)}, u32[]{:S(2)}, u32[]{:S(2)}) collective-permute-start(f32[8,128]{1,0:T(8,128)S(1)} %get-tuple-element.131), channel_id=1, source_target_pairs={{0,0},{13,13},{1,2},{2,1},{3,18},{18,3},{19,16},{16,19},{17,20},{2... | collective-permute-start | bytes 12296 | tf_op jit(solution)/shard_map/ppermute | solution.py:435
  82.3 3.6 %collective-permute-start.16 = (f32[8,128]{1,0:T(8,128)S(1)}, f32[8,128]{1,0:T(8,128)S(1)}, u32[]{:S(2)}, u32[]{:S(2)}) collective-permute-start(f32[8,128]{1,0:T(8,128)S(1)} %get-tuple-element.133), channel_id=1, source_target_pairs={{0,1},{1,0},{2,3},{3,2},{4,5},{5,4},{6,7},{7,6},{8,9},{9,8},{10,11... | collective-permute-start | bytes 12296 | tf_op jit(solution)/shard_map/ppermute | solution.py:436
  82.7 4.9 %collective-permute-start.17 = (f32[8,128]{1,0:T(8,128)S(1)}, f32[8,128]{1,0:T(8,128)S(1)}, u32[]{:S(2)}, u32[]{:S(2)}) collective-permute-start(f32[8,128]{1,0:T(8,128)S(1)} %get-tuple-element.134), channel_id=1, source_target_pairs={{0,0},{13,13},{1,2},{2,1},{3,18},{18,3},{19,16},{16,19},{17,20},{2... | collective-permute-start | bytes 12296 | tf_op jit(solution)/shard_map/ppermute | solution.py:435
  88.4 3.6 %collective-permute-start.18 = (f32[8,128]{1,0:T(8,128)S(1)}, f32[8,128]{1,0:T(8,128)S(1)}, u32[]{:S(2)}, u32[]{:S(2)}) collective-permute-start(f32[8,128]{1,0:T(8,128)S(1)} %get-tuple-element.139), channel_id=1, source_target_pairs={{0,1},{1,0},{2,3},{3,2},{4,5},{5,4},{6,7},{7,6},{8,9},{9,8},{10,11... | collective-permute-start | bytes 12296 | tf_op jit(solution)/shard_map/ppermute | solution.py:436
  88.5 4.9 %collective-permute-start.19 = (f32[8,128]{1,0:T(8,128)S(1)}, f32[8,128]{1,0:T(8,128)S(1)}, u32[]{:S(2)}, u32[]{:S(2)}) collective-permute-start(f32[8,128]{1,0:T(8,128)S(1)} %get-tuple-element.140), channel_id=1, source_target_pairs={{0,0},{13,13},{1,2},{2,1},{3,18},{18,3},{19,16},{16,19},{17,20},{2... | collective-permute-start | bytes 12296 | tf_op jit(solution)/shard_map/ppermute | solution.py:435
  94.2 3.6 %collective-permute-start.20 = (f32[8,128]{1,0:T(8,128)S(1)}, f32[8,128]{1,0:T(8,128)S(1)}, u32[]{:S(2)}, u32[]{:S(2)}) collective-permute-start(f32[8,128]{1,0:T(8,128)S(1)} %get-tuple-element.145), channel_id=1, source_target_pairs={{0,1},{1,0},{2,3},{3,2},{4,5},{5,4},{6,7},{7,6},{8,9},{9,8},{10,11... | collective-permute-start | bytes 12296 | tf_op jit(solution)/shard_map/ppermute | solution.py:436
  94.6 4.9 %collective-permute-start.21 = (f32[8,128]{1,0:T(8,128)S(1)}, f32[8,128]{1,0:T(8,128)S(1)}, u32[]{:S(2)}, u32[]{:S(2)}) collective-permute-start(f32[8,128]{1,0:T(8,128)S(1)} %get-tuple-element.146), channel_id=1, source_target_pairs={{0,0},{13,13},{1,2},{2,1},{3,18},{18,3},{19,16},{16,19},{17,20},{2... | collective-permute-start | bytes 12296 | tf_op jit(solution)/shard_map/ppermute | solution.py:435
  100.3 3.6 %collective-permute-start.22 = (f32[8,128]{1,0:T(8,128)S(1)}, f32[8,128]{1,0:T(8,128)S(1)}, u32[]{:S(2)}, u32[]{:S(2)}) collective-permute-start(f32[8,128]{1,0:T(8,128)S(1)} %get-tuple-element.152), channel_id=1, source_target_pairs={{0,1},{1,0},{2,3},{3,2},{4,5},{5,4},{6,7},{7,6},{8,9},{9,8},{10,11... | collective-permute-start | bytes 12296 | tf_op jit(solution)/shard_map/ppermute | solution.py:436
  100.5 4.9 %collective-permute-start.23 = (f32[8,128]{1,0:T(8,128)S(1)}, f32[8,128]{1,0:T(8,128)S(1)}, u32[]{:S(2)}, u32[]{:S(2)}) collective-permute-start(f32[8,128]{1,0:T(8,128)S(1)} %get-tuple-element.153), channel_id=1, source_target_pairs={{0,0},{13,13},{1,2},{2,1},{3,18},{18,3},{19,16},{16,19},{17,20},{2... | collective-permute-start | bytes 12296 | tf_op jit(solution)/shard_map/ppermute | solution.py:435
  106.1 3.6 %collective-permute-start.24 = (f32[8,128]{1,0:T(8,128)S(1)}, f32[8,128]{1,0:T(8,128)S(1)}, u32[]{:S(2)}, u32[]{:S(2)}) collective-permute-start(f32[8,128]{1,0:T(8,128)S(1)} %get-tuple-element.155), channel_id=1, source_target_pairs={{0,1},{1,0},{2,3},{3,2},{4,5},{5,4},{6,7},{7,6},{8,9},{9,8},{10,11... | collective-permute-start | bytes 12296 | tf_op jit(solution)/shard_map/ppermute | solution.py:436
  106.6 4.9 %collective-permute-start.25 = (f32[8,128]{1,0:T(8,128)S(1)}, f32[8,128]{1,0:T(8,128)S(1)}, u32[]{:S(2)}, u32[]{:S(2)}) collective-permute-start(f32[8,128]{1,0:T(8,128)S(1)} %get-tuple-element.156), channel_id=1, source_target_pairs={{0,0},{13,13},{1,2},{2,1},{3,18},{18,3},{19,16},{16,19},{17,20},{2... | collective-permute-start | bytes 12296 | tf_op jit(solution)/shard_map/ppermute | solution.py:435
  112.2 3.6 %collective-permute-start.26 = (f32[8,128]{1,0:T(8,128)S(1)}, f32[8,128]{1,0:T(8,128)S(1)}, u32[]{:S(2)}, u32[]{:S(2)}) collective-permute-start(f32[8,128]{1,0:T(8,128)S(1)} %get-tuple-element.161), channel_id=1, source_target_pairs={{0,1},{1,0},{2,3},{3,2},{4,5},{5,4},{6,7},{7,6},{8,9},{9,8},{10,11... | collective-permute-start | bytes 12296 | tf_op jit(solution)/shard_map/ppermute | solution.py:436
  112.4 4.9 %collective-permute-start.27 = (f32[8,128]{1,0:T(8,128)S(1)}, f32[8,128]{1,0:T(8,128)S(1)}, u32[]{:S(2)}, u32[]{:S(2)}) collective-permute-start(f32[8,128]{1,0:T(8,128)S(1)} %get-tuple-element.162), channel_id=1, source_target_pairs={{0,0},{13,13},{1,2},{2,1},{3,18},{18,3},{19,16},{16,19},{17,20},{2... | collective-permute-start | bytes 12296 | tf_op jit(solution)/shard_map/ppermute | solution.py:435
  118.0 3.7 %collective-permute-start.28 = (f32[8,128]{1,0:T(8,128)S(1)}, f32[8,128]{1,0:T(8,128)S(1)}, u32[]{:S(2)}, u32[]{:S(2)}) collective-permute-start(f32[8,128]{1,0:T(8,128)S(1)} %get-tuple-element.167), channel_id=1, source_target_pairs={{0,1},{1,0},{2,3},{3,2},{4,5},{5,4},{6,7},{7,6},{8,9},{9,8},{10,11... | collective-permute-start | bytes 12296 | tf_op jit(solution)/shard_map/ppermute | solution.py:436
  118.5 4.9 %collective-permute-start.29 = (f32[8,128]{1,0:T(8,128)S(1)}, f32[8,128]{1,0:T(8,128)S(1)}, u32[]{:S(2)}, u32[]{:S(2)}) collective-permute-start(f32[8,128]{1,0:T(8,128)S(1)} %get-tuple-element.168), channel_id=1, source_target_pairs={{0,0},{13,13},{1,2},{2,1},{3,18},{18,3},{19,16},{16,19},{17,20},{2... | collective-permute-start | bytes 12296 | tf_op jit(solution)/shard_map/ppermute | solution.py:435
  124.1 3.6 %collective-permute-start.30 = (f32[8,128]{1,0:T(8,128)S(1)}, f32[8,128]{1,0:T(8,128)S(1)}, u32[]{:S(2)}, u32[]{:S(2)}) collective-permute-start(f32[8,128]{1,0:T(8,128)S(1)} %get-tuple-element.174), channel_id=1, source_target_pairs={{0,1},{1,0},{2,3},{3,2},{4,5},{5,4},{6,7},{7,6},{8,9},{9,8},{10,11... | collective-permute-start | bytes 12296 | tf_op jit(solution)/shard_map/ppermute | solution.py:436
  124.3 4.9 %collective-permute-start.31 = (f32[8,128]{1,0:T(8,128)S(1)}, f32[8,128]{1,0:T(8,128)S(1)}, u32[]{:S(2)}, u32[]{:S(2)}) collective-permute-start(f32[8,128]{1,0:T(8,128)S(1)} %get-tuple-element.175), channel_id=1, source_target_pairs={{0,0},{13,13},{1,2},{2,1},{3,18},{18,3},{19,16},{16,19},{17,20},{2... | collective-permute-start | bytes 12296 | tf_op jit(solution)/shard_map/ppermute | solution.py:435
  129.9 3.6 %collective-permute-start.32 = (f32[8,128]{1,0:T(8,128)S(1)}, f32[8,128]{1,0:T(8,128)S(1)}, u32[]{:S(2)}, u32[]{:S(2)}) collective-permute-start(f32[8,128]{1,0:T(8,128)S(1)} %get-tuple-element.177), channel_id=1, source_target_pairs={{0,1},{1,0},{2,3},{3,2},{4,5},{5,4},{6,7},{7,6},{8,9},{9,8},{10,11... | collective-permute-start | bytes 12296 | tf_op jit(solution)/shard_map/ppermute | solution.py:436
  130.4 4.9 %collective-permute-start.33 = (f32[8,128]{1,0:T(8,128)S(1)}, f32[8,128]{1,0:T(8,128)S(1)}, u32[]{:S(2)}, u32[]{:S(2)}) collective-permute-start(f32[8,128]{1,0:T(8,128)S(1)} %get-tuple-element.178), channel_id=1, source_target_pairs={{0,0},{13,13},{1,2},{2,1},{3,18},{18,3},{19,16},{16,19},{17,20},{2... | collective-permute-start | bytes 12296 | tf_op jit(solution)/shard_map/ppermute | solution.py:435
  136.0 3.6 %collective-permute-start.34 = (f32[8,128]{1,0:T(8,128)S(1)}, f32[8,128]{1,0:T(8,128)S(1)}, u32[]{:S(2)}, u32[]{:S(2)}) collective-permute-start(f32[8,128]{1,0:T(8,128)S(1)} %get-tuple-element.183), channel_id=1, source_target_pairs={{0,1},{1,0},{2,3},{3,2},{4,5},{5,4},{6,7},{7,6},{8,9},{9,8},{10,11... | collective-permute-start | bytes 12296 | tf_op jit(solution)/shard_map/ppermute | solution.py:436
  136.2 4.9 %collective-permute-start.35 = (f32[8,128]{1,0:T(8,128)S(1)}, f32[8,128]{1,0:T(8,128)S(1)}, u32[]{:S(2)}, u32[]{:S(2)}) collective-permute-start(f32[8,128]{1,0:T(8,128)S(1)} %get-tuple-element.184), channel_id=1, source_target_pairs={{0,0},{13,13},{1,2},{2,1},{3,18},{18,3},{19,16},{16,19},{17,20},{2... | collective-permute-start | bytes 12296 | tf_op jit(solution)/shard_map/ppermute | solution.py:435
  141.9 3.6 %collective-permute-start.36 = (f32[8,128]{1,0:T(8,128)S(1)}, f32[8,128]{1,0:T(8,128)S(1)}, u32[]{:S(2)}, u32[]{:S(2)}) collective-permute-start(f32[8,128]{1,0:T(8,128)S(1)} %get-tuple-element.189), channel_id=1, source_target_pairs={{0,1},{1,0},{2,3},{3,2},{4,5},{5,4},{6,7},{7,6},{8,9},{9,8},{10,11... | collective-permute-start | bytes 12296 | tf_op jit(solution)/shard_map/ppermute | solution.py:436
  142.3 4.9 %collective-permute-start.37 = (f32[8,128]{1,0:T(8,128)S(1)}, f32[8,128]{1,0:T(8,128)S(1)}, u32[]{:S(2)}, u32[]{:S(2)}) collective-permute-start(f32[8,128]{1,0:T(8,128)S(1)} %get-tuple-element.190), channel_id=1, source_target_pairs={{0,0},{13,13},{1,2},{2,1},{3,18},{18,3},{19,16},{16,19},{17,20},{2... | collective-permute-start | bytes 12296 | tf_op jit(solution)/shard_map/ppermute | solution.py:435
  147.8 5.9 %collective-permute-start.38 = (f32[4,2,2,128]{3,2,1,0:T(2,128)S(1)}, f32[4,2,2,128]{3,2,1,0:T(2,128)S(1)}, u32[]{:S(2)}, u32[]{:S(2)}) collective-permute-start(f32[4,2,2,128]{3,2,1,0:T(2,128)S(1)} %rev.24), channel_id=1, source_target_pairs={{1,0},{3,1},{19,2},{17,3},{21,4},{23,5},{7,6},{5,7},{9,8},{11,9},{... | collective-permute-start | bytes 24584 | tf_op jit(solution)/shard_map/ppermute | solution.py:448
  151.8 5.5 %collective-permute-start.39 = (f32[4,2,2,128]{3,2,1,0:T(2,128)S(1)}, f32[4,2,2,128]{3,2,1,0:T(2,128)S(1)}, u32[]{:S(2)}, u32[]{:S(2)}) collective-permute-start(f32[4,2,2,128]{3,2,1,0:T(2,128)S(1)} %get-tuple-element.206), channel_id=1, source_target_pairs={{0,0},{2,1},{18,2},{16,3},{20,4},{22,5},{6,6},{4,7},{8,8},{10,9},{... | collective-permute-start | bytes 24584 | tf_op jit(solution)/shard_map/ppermute | solution.py:447

commit v5 on v4

--- a/solution.py
+++ b/solution.py
@@ -197,7 +197,7 @@
 def unit_device(unit, n_col):
     group, place = divmod(unit // 2, 4)
     x, row = ((0, 0), (1, 0), (1, 1), (0, 1))[place]
-    return (row + group) % 2 * n_col + 4 * group + 2 * x + unit % 2
+    return (row + group) % 2 * n_col + 4 * group + 2 * x + (unit + place) % 2
 
 
 def deal_pairs(n_col, which):
@@ -311,7 +311,7 @@
     msg_a[...], msg_b[...] = messages(f, ahead(True, 0, f, q, None, None, injected[...]))
 
 
-def pair_kernel(pair, last, half_0, half_1, beyond_0, beyond_1, capacity_ref, injected_ref, got_a, got_b, f_ref, q_ref,
+def pair_kernel(pair, last, half_0, half_1, beyond_0, beyond_1, capacity_ref, injected_ref, got_b, got_a, f_ref, q_ref,
                 *refs):
     halves, beyond = (half_0, half_1), (beyond_0, beyond_1)
     first = pair == 0
@@ -394,21 +394,28 @@
         compiler_params=limit,
         name="pack",
     )(jnp.stack([row, lax.axis_index("col")]).astype(jnp.int32), pattern.reshape(-1), own_block, neighbor_block)
-    currents, slot_tile, facing_0, facing_1 = lax.optimization_barrier((currents, slot_tile, facing_0, facing_1))
     half_0 = lax.ppermute(send_0, both, deal[0])
     half_1 = lax.ppermute(send_1, both, deal[1])
     beyond_0 = lax.ppermute(facing_0, both, deal_b[0])
     beyond_1 = lax.ppermute(facing_1, both, deal_b[1])
 
-    injected = collect(currents, slot_tile, tile_rows * tile_cols, width)
-    small = jnp.concatenate(
-        [injected.reshape(tile_rows, tile_cols, STEPS * width), capacity, initial], axis=2
+    def deal_small(currents, slot_tile, capacity, initial):
+        injected = collect(currents, slot_tile, tile_rows * tile_cols, width)
+        small = jnp.concatenate(
+            [injected.reshape(tile_rows, tile_cols, STEPS * width), capacity, initial], axis=2
+        )
+        small = jnp.where(row == 1, jnp.flip(small, 0), small)
+        unit_0, unit_1 = small[:, :HALF], jnp.flip(small, 1)[:, :HALF]
+        got_0 = lax.ppermute(jnp.where(row == 1, unit_1, unit_0), both, deal[0])
+        got_1 = lax.ppermute(jnp.where(row == 1, unit_0, unit_1), both, deal[1])
+        return jnp.concatenate([got_0, jnp.flip(got_1, 0)], axis=0).reshape(N * HALF, STEPS + 2, width)
+
+    small = lax.cond(
+        row < lax.axis_size("row"),
+        deal_small,
+        lambda *_: jnp.zeros((N * HALF, STEPS + 2, width), jnp.float32),
+        currents, slot_tile, capacity, initial,
     )
-    small = jnp.where(row == 1, jnp.flip(small, 0), small)
-    unit_0, unit_1 = small[:, :HALF], jnp.flip(small, 1)[:, :HALF]
-    got_0 = lax.ppermute(jnp.where(row == 1, unit_1, unit_0), both, deal[0])
-    got_1 = lax.ppermute(jnp.where(row == 1, unit_0, unit_1), both, deal[1])
-    small = jnp.concatenate([got_0, jnp.flip(got_1, 0)], axis=0).reshape(N * HALF, STEPS + 2, width)
     injected, cap, field = small[:, :STEPS], small[:, STEPS], small[:, STEPS + 1]
 
     shape = jax.ShapeDtypeStruct((N * HALF, width), jnp.float32)
@@ -436,7 +443,7 @@
             got_a = lax.ppermute(msg_a, "col", a_pairs)
             feed = injected[:, min(instant + closing, STEPS - 1)]
             out = call(functools.partial(pair_kernel, pair, last), 1 if last else 4 if closing else 6, 80,
-                       half_0, half_1, beyond_0, beyond_1, cap, feed, got_a, got_b, field, q, *state)
+                       half_0, half_1, beyond_0, beyond_1, cap, feed, got_b, got_a, field, q, *state)
             field = out[0]
             if not last:
                 q, msg_a, msg_b = out[1:4]

time: 159 us -> 171 us (1.075)
  waiting for transfers between devices: 50.2 us -> 59.3 us
  local copies, waits for them, and re-layouts: 5.14 us -> 10.4 us
  starting transfers between devices: 86.9 us -> 82.6 us
    all_to_all x1, waiting for transfers between devices: 0.01 us -> 20.8 us  [collect(): lax.all_to_all(packed, 'col', split_axis=2, concat_axis=1, tiled=True)]
    ppermute x2, waiting for transfers between devices: 20.2 us -> 3.98 us  [the longest x1 2.5 us: deal_small(): got_0 = lax.ppermute(jnp.where(row == 1, unit_1, unit_0), both, deal[0])]
    ppermute x16, waiting for transfers between devices: 25 us -> 31.7 us  [shards_chain(): got_b = lax.ppermute(msg_b, both, b_pairs)]
    cond x0 -> x9, local copies, waits for them, and re-layouts: none -> 4.17 us
    ppermute x16, starting transfers between devices: 5.1 us -> 1.14 us  [shards_chain(): got_a = lax.ppermute(msg_a, 'col', a_pairs)]
    ppermute x16, starting transfers between devices: 51.9 us -> 54.3 us  [shards_chain(): got_b = lax.ppermute(msg_b, both, b_pairs)]
    ppermute x1, starting transfers between devices: 3.99 us -> 2.23 us  [shards_chain(): lax.ppermute(jnp.flip(done[:, ROWS:], 1), both, [(b, a) for a, b in deal[...]
    unnamed x17 -> x12, local copies, waits for them, and re-layouts: 3.83 us -> 2.65 us
  transfers between devices with their start and end apart: 41 -> 41, of which waited for: 19 -> 21; matrix products, arithmetic and copies ran while one was open for 0% -> 5% of each run, Pallas kernels for 0% -> 0%
where the time goes in v5:
time: 171 us; the launch traced here: 168 us
  starting transfers between devices  82.6 us (48%)
  waiting for transfers between devices  59.3 us (35%)
  Pallas kernels  13.8 us (8%)
  local copies, waits for them, and re-layouts  10.4 us (6%)
    ppermute x16, starting transfers between devices, shards_chain(): got_b = lax.ppermute(msg_b, both, b_pairs)  54.3 us
    ppermute x16, waiting for transfers between devices, shards_chain(): got_b = lax.ppermute(msg_b, both, b_pairs)  31.7 us
    all_to_all x1, waiting for transfers between devices, collect(): lax.all_to_all(packed, 'col', split_axis=2, concat_axis=1, tiled=True)  20.8 us
    pallas_call x17, Pallas kernels, call(): pl.pallas_call(body, out_shape=(shape,) * n_out, in_specs=[vmem] * len(in...  11.6 us
    all_to_all x1, starting transfers between devices, collect(): lax.all_to_all(packed, 'col', split_axis=2, concat_axis=1, tiled=True)  5.34 us
    cond x9, local copies, waits for them, and re-layouts  4.17 us
    ppermute x1, starting transfers between devices, shards_chain(): beyond_0 = lax.ppermute(facing_0, both, deal_b[0])  3.43 us
  transfers between devices with their start and end apart: 41, of which 21 were waited for; matrix products, arithmetic and copies ran while one was open for 5% of the time, Pallas kernels for 0%

profile of v5, /device:TPU:8, one launch (start us, length us, event | category | flops | bytes accessed | tf_op | source)
XLA Modules:
  0.0 168.5 jit_solution(7142695993200912888)
XLA Ops:
  0.8 1.6 copy-done
  3.5 2.2 %pack.1 = (f32[20,128,128]{2,1,0:T(8,128)}, f32[20,128,128]{2,1,0:T(8,128)}, f32[2,128,128]{2,1,0:T(8,128)S(1)}, f32[2,128,128]{2,1,0:T(8,128)S(1)}) custom-call(s32[2]{0:T(128)S(1)} %pad_add_fusion.place_ref, s32[32]{0:T(128)S(1)} %reshape.23.pattern_ref, f32[2,4,128,128]{3,2,1,0:T(8,128)S(1)} %copy-done.1, f32[4,2,4,128,128]{4,3,2,1,0:T(8,128)S(1)} %copy-done), custom_call_target="tpu_custom_call" | custom-call | tf_op jit(solution)/shard_map/pack/pallas_call | solution.py:389
  5.7 3.4 %collective-permute-start.2 = (f32[20,128,128]{2,1,0:T(8,128)}, f32[20,128,128]{2,1,0:T(8,128)S(1)}, u32[]{:S(2)}, u32[]{:S(2)}) collective-permute-start(f32[20,128,128]{2,1,0:T(8,128)} %get-tuple-element.130), channel_id=1, source_target_pairs={{0,0},{1,3},{2,18},{3,17},{4,20},{5,23},{6,6},{7,5},{8,8},{9,11},{... | collective-permute-start | bytes 3932168 | tf_op jit(solution)/shard_map/ppermute | solution.py:397
  9.1 3.1 %collective-permute-start.3 = (f32[20,128,128]{2,1,0:T(8,128)}, f32[20,128,128]{2,1,0:T(8,128)S(1)}, u32[]{:S(2)}, u32[]{:S(2)}) collective-permute-start(f32[20,128,128]{2,1,0:T(8,128)} %get-tuple-element.131), channel_id=1, source_target_pairs={{0,1},{1,2},{2,19},{3,16},{4,21},{5,22},{6,7},{7,4},{8,9},{9,10},{... | collective-permute-start | bytes 3932168 | tf_op jit(solution)/shard_map/ppermute | solution.py:398
  12.3 3.4 %collective-permute-start.4 = (f32[2,128,128]{2,1,0:T(8,128)S(1)}, f32[2,128,128]{2,1,0:T(8,128)S(1)}, u32[]{:S(2)}, u32[]{:S(2)}) collective-permute-start(f32[2,128,128]{2,1,0:T(8,128)S(1)} %get-tuple-element.132), channel_id=1, source_target_pairs={{0,3},{1,18},{2,17},{3,20},{4,23},{5,6},{6,5},{7,8},{8,11},{9,26},... | collective-permute-start | bytes 393224 | tf_op jit(solution)/shard_map/ppermute | solution.py:399
  15.7 42.1 %conditional.1 = (f32[8,6,128]{2,1,0:T(8,128)}, f32[8,1,128]{2,1,0:T(1,128)}, f32[8,1,128]{2,1,0:T(1,128)}, f32[8,1,128]{2,1,0:T(1,128)}, f32[8,1,128]{2,1,0:T(1...) conditional(s32[]{:T(128)} %convert_element_type.9, () %tuple.15, ...), branch_computations={%region_0.0_spmd, %region_1.2_spmd} | conditional | flops 3287617 | bytes 2077155 | solution.py:413
  16.8 5.3 %all-to-all-start = ((f32[1,1,16,5,512]{4,1,3,0,2:T(1,128)}), f32[1,1,16,5,512]{4,1,3,0,2:T(1,128)S(1)}, u32[]{:S(2)}, u32[]{:S(2)}) async-start(f32[1,1,16,5,512]{4,1,3,0,2:T(1,128)} %fusion), calls=%async_computation | async-start | bytes 327680 | tf_op jit(solution)/shard_map/cond/branch_1_fun/all_to_all | solution.py:131
  22.1 20.8 %all-to-all-done = f32[1,1,16,5,512]{4,1,3,0,2:T(1,128)S(1)} async-done(((f32[1,1,16,5,512]{4,1,3,0,2:T(1,128)}), f32[1,1,16,5,512]{4,1,3,0,2:T(1,128)S(1)}, u32[]{:S(2)}, u32[]{:S(2)}) %all-to-all-start) | async-done | bytes 163872 | tf_op jit(solution)/shard_map/cond/branch_1_fun/all_to_all | solution.py:131
  43.5 1.9 %collective-permute-start.1 = (f32[2,2,768]{2,1,0:T(2,128)S(1)}, f32[2,2,768]{2,1,0:T(2,128)S(1)}, u32[]{:S(2)}, u32[]{:S(2)}) collective-permute-start(f32[2,2,768]{2,1,0:T(2,128)S(1)} %get-tuple-element.256), channel_id=1, source_target_pairs={{0,1},{1,2},{2,19},{3,16},{4,21},{5,22},{6,7},{7,4},{8,9},{9,10},{... | collective-permute-start | bytes 36872 | tf_op jit(solution)/shard_map/cond/branch_1_fun/ppermute | solution.py:410
  45.5 1.9 %collective-permute-start = (f32[2,2,768]{2,1,0:T(2,128)S(1)}, f32[2,2,768]{2,1,0:T(2,128)S(1)}, u32[]{:S(2)}, u32[]{:S(2)}) collective-permute-start(f32[2,2,768]{2,1,0:T(2,128)S(1)} %get-tuple-element.255), channel_id=1, source_target_pairs={{0,0},{1,3},{2,18},{3,17},{4,20},{5,23},{6,6},{7,5},{8,8},{9,11},{... | collective-permute-start | bytes 36872 | tf_op jit(solution)/shard_map/cond/branch_1_fun/ppermute | solution.py:409
  47.4 1.5 collective-permute-done.1
  48.9 2.5 %collective-permute-done = f32[2,2,768]{2,1,0:T(2,128)S(1)} collective-permute-done((f32[2,2,768]{2,1,0:T(2,128)S(1)}, f32[2,2,768]{2,1,0:T(2,128)S(1)}, u32[]{:S(2)}, u32[]{:S(2)}) %collective-permute-start) | collective-permute-done | bytes 12320 | tf_op jit(solution)/shard_map/cond/branch_1_fun/ppermute | solution.py:409
  52.0 1.7 %fusion.3 = (f32[8,1,128]{2,1,0:T(1,128)}, f32[8,1,128]{2,1,0:T(1,128)}, f32[8,1,128]{2,1,0:T(1,128)}, f32[8,1,128]{2,1,0:T(1,128)}, f32[8,1,128]{2,1,0:T(1,128)}, /*index=5*/f32[8,1,128]{2,1,0:T(1,128)}) fusion(f32[8,6,128]{2,1,0:T(8,128)} %reshape.21), kind=kLoop, calls=%fused_computation.21 | loop fusion | bytes 49152 | tf_op jit(solution)/shard_map/slice | solution.py:444
  57.8 2.4 %collective-permute-start.5 = (f32[2,128,128]{2,1,0:T(8,128)S(1)}, f32[2,128,128]{2,1,0:T(8,128)S(1)}, u32[]{:S(2)}, u32[]{:S(2)}) collective-permute-start(f32[2,128,128]{2,1,0:T(8,128)S(1)} %get-tuple-element.133), channel_id=1, source_target_pairs={{1,1},{2,2},{3,19},{4,16},{5,21},{6,22},{7,7},{8,4},{9,9},{10,10},... | collective-permute-start | bytes 393224 | tf_op jit(solution)/shard_map/ppermute | solution.py:400
  60.5 3.4 %collective-permute-start.6 = (f32[8,128]{1,0:T(8,128)S(1)}, f32[8,128]{1,0:T(8,128)S(1)}, u32[]{:S(2)}, u32[]{:S(2)}) collective-permute-start(f32[8,128]{1,0:T(8,128)S(1)} %get-tuple-element.138), channel_id=1, source_target_pairs={{0,0},{12,12},{1,3},{3,1},{2,18},{18,2},{19,17},{17,19},{16,20},{2... | collective-permute-start | bytes 12296 | tf_op jit(solution)/shard_map/ppermute | solution.py:442
  66.7 3.4 %collective-permute-start.8 = (f32[8,128]{1,0:T(8,128)S(1)}, f32[8,128]{1,0:T(8,128)S(1)}, u32[]{:S(2)}, u32[]{:S(2)}) collective-permute-start(f32[8,128]{1,0:T(8,128)S(1)} %get-tuple-element.141), channel_id=1, source_target_pairs={{0,0},{12,12},{1,3},{3,1},{2,18},{18,2},{19,17},{17,19},{16,20},{2... | collective-permute-start | bytes 12296 | tf_op jit(solution)/shard_map/ppermute | solution.py:442
  70.2 2.0 %collective-permute-done.8.got_b = f32[8,128]{1,0:T(8,128)S(1)} collective-permute-done((f32[8,128]{1,0:T(8,128)S(1)}, f32[8,128]{1,0:T(8,128)S(1)}, u32[]{:S(2)}, u32[]{:S(2)}) %collective-permute-start.8) | collective-permute-done | bytes 4128 | tf_op jit(solution)/shard_map/ppermute | solution.py:442
  73.0 3.4 %collective-permute-start.10 = (f32[8,128]{1,0:T(8,128)S(1)}, f32[8,128]{1,0:T(8,128)S(1)}, u32[]{:S(2)}, u32[]{:S(2)}) collective-permute-start(f32[8,128]{1,0:T(8,128)S(1)} %get-tuple-element.147), channel_id=1, source_target_pairs={{0,0},{12,12},{1,3},{3,1},{2,18},{18,2},{19,17},{17,19},{16,20},{2... | collective-permute-start | bytes 12296 | tf_op jit(solution)/shard_map/ppermute | solution.py:442
  76.4 2.0 %collective-permute-done.10.got_b = f32[8,128]{1,0:T(8,128)S(1)} collective-permute-done((f32[8,128]{1,0:T(8,128)S(1)}, f32[8,128]{1,0:T(8,128)S(1)}, u32[]{:S(2)}, u32[]{:S(2)}) %collective-permute-start.10) | collective-permute-done | bytes 4128 | tf_op jit(solution)/shard_map/ppermute | solution.py:442
  79.2 3.4 %collective-permute-start.12 = (f32[8,128]{1,0:T(8,128)S(1)}, f32[8,128]{1,0:T(8,128)S(1)}, u32[]{:S(2)}, u32[]{:S(2)}) collective-permute-start(f32[8,128]{1,0:T(8,128)S(1)} %get-tuple-element.153), channel_id=1, source_target_pairs={{0,0},{12,12},{1,3},{3,1},{2,18},{18,2},{19,17},{17,19},{16,20},{2... | collective-permute-start | bytes 12296 | tf_op jit(solution)/shard_map/ppermute | solution.py:442
  82.7 2.0 %collective-permute-done.12.got_b = f32[8,128]{1,0:T(8,128)S(1)} collective-permute-done((f32[8,128]{1,0:T(8,128)S(1)}, f32[8,128]{1,0:T(8,128)S(1)}, u32[]{:S(2)}, u32[]{:S(2)}) %collective-permute-start.12) | collective-permute-done | bytes 4128 | tf_op jit(solution)/shard_map/ppermute | solution.py:442
  85.4 3.4 %collective-permute-start.14 = (f32[8,128]{1,0:T(8,128)S(1)}, f32[8,128]{1,0:T(8,128)S(1)}, u32[]{:S(2)}, u32[]{:S(2)}) collective-permute-start(f32[8,128]{1,0:T(8,128)S(1)} %get-tuple-element.161), channel_id=1, source_target_pairs={{0,0},{12,12},{1,3},{3,1},{2,18},{18,2},{19,17},{17,19},{16,20},{2... | collective-permute-start | bytes 12296 | tf_op jit(solution)/shard_map/ppermute | solution.py:442
  88.9 2.0 %collective-permute-done.14.got_b = f32[8,128]{1,0:T(8,128)S(1)} collective-permute-done((f32[8,128]{1,0:T(8,128)S(1)}, f32[8,128]{1,0:T(8,128)S(1)}, u32[]{:S(2)}, u32[]{:S(2)}) %collective-permute-start.14) | collective-permute-done | bytes 4128 | tf_op jit(solution)/shard_map/ppermute | solution.py:442
  91.7 3.4 %collective-permute-start.16 = (f32[8,128]{1,0:T(8,128)S(1)}, f32[8,128]{1,0:T(8,128)S(1)}, u32[]{:S(2)}, u32[]{:S(2)}) collective-permute-start(f32[8,128]{1,0:T(8,128)S(1)} %get-tuple-element.164), channel_id=1, source_target_pairs={{0,0},{12,12},{1,3},{3,1},{2,18},{18,2},{19,17},{17,19},{16,20},{2... | collective-permute-start | bytes 12296 | tf_op jit(solution)/shard_map/ppermute | solution.py:442
  95.1 2.0 %collective-permute-done.16.got_b = f32[8,128]{1,0:T(8,128)S(1)} collective-permute-done((f32[8,128]{1,0:T(8,128)S(1)}, f32[8,128]{1,0:T(8,128)S(1)}, u32[]{:S(2)}, u32[]{:S(2)}) %collective-permute-start.16) | collective-permute-done | bytes 4128 | tf_op jit(solution)/shard_map/ppermute | solution.py:442
  97.9 3.4 %collective-permute-start.18 = (f32[8,128]{1,0:T(8,128)S(1)}, f32[8,128]{1,0:T(8,128)S(1)}, u32[]{:S(2)}, u32[]{:S(2)}) collective-permute-start(f32[8,128]{1,0:T(8,128)S(1)} %get-tuple-element.170), channel_id=1, source_target_pairs={{0,0},{12,12},{1,3},{3,1},{2,18},{18,2},{19,17},{17,19},{16,20},{2... | collective-permute-start | bytes 12296 | tf_op jit(solution)/shard_map/ppermute | solution.py:442
  101.4 2.0 %collective-permute-done.18.got_b = f32[8,128]{1,0:T(8,128)S(1)} collective-permute-done((f32[8,128]{1,0:T(8,128)S(1)}, f32[8,128]{1,0:T(8,128)S(1)}, u32[]{:S(2)}, u32[]{:S(2)}) %collective-permute-start.18) | collective-permute-done | bytes 4128 | tf_op jit(solution)/shard_map/ppermute | solution.py:442
  104.1 3.4 %collective-permute-start.20 = (f32[8,128]{1,0:T(8,128)S(1)}, f32[8,128]{1,0:T(8,128)S(1)}, u32[]{:S(2)}, u32[]{:S(2)}) collective-permute-start(f32[8,128]{1,0:T(8,128)S(1)} %get-tuple-element.176), channel_id=1, source_target_pairs={{0,0},{12,12},{1,3},{3,1},{2,18},{18,2},{19,17},{17,19},{16,20},{2... | collective-permute-start | bytes 12296 | tf_op jit(solution)/shard_map/ppermute | solution.py:442
  107.6 2.0 %collective-permute-done.20.got_b = f32[8,128]{1,0:T(8,128)S(1)} collective-permute-done((f32[8,128]{1,0:T(8,128)S(1)}, f32[8,128]{1,0:T(8,128)S(1)}, u32[]{:S(2)}, u32[]{:S(2)}) %collective-permute-start.20) | collective-permute-done | bytes 4128 | tf_op jit(solution)/shard_map/ppermute | solution.py:442
  110.3 3.4 %collective-permute-start.22 = (f32[8,128]{1,0:T(8,128)S(1)}, f32[8,128]{1,0:T(8,128)S(1)}, u32[]{:S(2)}, u32[]{:S(2)}) collective-permute-start(f32[8,128]{1,0:T(8,128)S(1)} %get-tuple-element.184), channel_id=1, source_target_pairs={{0,0},{12,12},{1,3},{3,1},{2,18},{18,2},{19,17},{17,19},{16,20},{2... | collective-permute-start | bytes 12296 | tf_op jit(solution)/shard_map/ppermute | solution.py:442
  113.8 2.0 %collective-permute-done.22.got_b = f32[8,128]{1,0:T(8,128)S(1)} collective-permute-done((f32[8,128]{1,0:T(8,128)S(1)}, f32[8,128]{1,0:T(8,128)S(1)}, u32[]{:S(2)}, u32[]{:S(2)}) %collective-permute-start.22) | collective-permute-done | bytes 4128 | tf_op jit(solution)/shard_map/ppermute | solution.py:442
  116.6 3.4 %collective-permute-start.24 = (f32[8,128]{1,0:T(8,128)S(1)}, f32[8,128]{1,0:T(8,128)S(1)}, u32[]{:S(2)}, u32[]{:S(2)}) collective-permute-start(f32[8,128]{1,0:T(8,128)S(1)} %get-tuple-element.187), channel_id=1, source_target_pairs={{0,0},{12,12},{1,3},{3,1},{2,18},{18,2},{19,17},{17,19},{16,20},{2... | collective-permute-start | bytes 12296 | tf_op jit(solution)/shard_map/ppermute | solution.py:442
  120.0 2.0 %collective-permute-done.24.got_b = f32[8,128]{1,0:T(8,128)S(1)} collective-permute-done((f32[8,128]{1,0:T(8,128)S(1)}, f32[8,128]{1,0:T(8,128)S(1)}, u32[]{:S(2)}, u32[]{:S(2)}) %collective-permute-start.24) | collective-permute-done | bytes 4128 | tf_op jit(solution)/shard_map/ppermute | solution.py:442
  122.8 3.4 %collective-permute-start.26 = (f32[8,128]{1,0:T(8,128)S(1)}, f32[8,128]{1,0:T(8,128)S(1)}, u32[]{:S(2)}, u32[]{:S(2)}) collective-permute-start(f32[8,128]{1,0:T(8,128)S(1)} %get-tuple-element.193), channel_id=1, source_target_pairs={{0,0},{12,12},{1,3},{3,1},{2,18},{18,2},{19,17},{17,19},{16,20},{2... | collective-permute-start | bytes 12296 | tf_op jit(solution)/shard_map/ppermute | solution.py:442
  126.3 2.0 %collective-permute-done.26.got_b = f32[8,128]{1,0:T(8,128)S(1)} collective-permute-done((f32[8,128]{1,0:T(8,128)S(1)}, f32[8,128]{1,0:T(8,128)S(1)}, u32[]{:S(2)}, u32[]{:S(2)}) %collective-permute-start.26) | collective-permute-done | bytes 4128 | tf_op jit(solution)/shard_map/ppermute | solution.py:442
  129.0 3.6 %collective-permute-start.28 = (f32[8,128]{1,0:T(8,128)S(1)}, f32[8,128]{1,0:T(8,128)S(1)}, u32[]{:S(2)}, u32[]{:S(2)}) collective-permute-start(f32[8,128]{1,0:T(8,128)S(1)} %get-tuple-element.199), channel_id=1, source_target_pairs={{0,0},{12,12},{1,3},{3,1},{2,18},{18,2},{19,17},{17,19},{16,20},{2... | collective-permute-start | bytes 12296 | tf_op jit(solution)/shard_map/ppermute | solution.py:442
  132.7 1.9 %collective-permute-done.28.got_b = f32[8,128]{1,0:T(8,128)S(1)} collective-permute-done((f32[8,128]{1,0:T(8,128)S(1)}, f32[8,128]{1,0:T(8,128)S(1)}, u32[]{:S(2)}, u32[]{:S(2)}) %collective-permute-start.28) | collective-permute-done | bytes 4128 | tf_op jit(solution)/shard_map/ppermute | solution.py:442
  135.3 3.4 %collective-permute-start.30 = (f32[8,128]{1,0:T(8,128)S(1)}, f32[8,128]{1,0:T(8,128)S(1)}, u32[]{:S(2)}, u32[]{:S(2)}) collective-permute-start(f32[8,128]{1,0:T(8,128)S(1)} %get-tuple-element.206), channel_id=1, source_target_pairs={{0,0},{12,12},{1,3},{3,1},{2,18},{18,2},{19,17},{17,19},{16,20},{2... | collective-permute-start | bytes 12296 | tf_op jit(solution)/shard_map/ppermute | solution.py:442
  138.7 2.0 %collective-permute-done.30.got_b = f32[8,128]{1,0:T(8,128)S(1)} collective-permute-done((f32[8,128]{1,0:T(8,128)S(1)}, f32[8,128]{1,0:T(8,128)S(1)}, u32[]{:S(2)}, u32[]{:S(2)}) %collective-permute-start.30) | collective-permute-done | bytes 4128 | tf_op jit(solution)/shard_map/ppermute | solution.py:442
  141.5 3.4 %collective-permute-start.32 = (f32[8,128]{1,0:T(8,128)S(1)}, f32[8,128]{1,0:T(8,128)S(1)}, u32[]{:S(2)}, u32[]{:S(2)}) collective-permute-start(f32[8,128]{1,0:T(8,128)S(1)} %get-tuple-element.209), channel_id=1, source_target_pairs={{0,0},{12,12},{1,3},{3,1},{2,18},{18,2},{19,17},{17,19},{16,20},{2... | collective-permute-start | bytes 12296 | tf_op jit(solution)/shard_map/ppermute | solution.py:442
  145.0 2.0 %collective-permute-done.32.got_b = f32[8,128]{1,0:T(8,128)S(1)} collective-permute-done((f32[8,128]{1,0:T(8,128)S(1)}, f32[8,128]{1,0:T(8,128)S(1)}, u32[]{:S(2)}, u32[]{:S(2)}) %collective-permute-start.32) | collective-permute-done | bytes 4128 | tf_op jit(solution)/shard_map/ppermute | solution.py:442
  147.7 3.4 %collective-permute-start.34 = (f32[8,128]{1,0:T(8,128)S(1)}, f32[8,128]{1,0:T(8,128)S(1)}, u32[]{:S(2)}, u32[]{:S(2)}) collective-permute-start(f32[8,128]{1,0:T(8,128)S(1)} %get-tuple-element.215), channel_id=1, source_target_pairs={{0,0},{12,12},{1,3},{3,1},{2,18},{18,2},{19,17},{17,19},{16,20},{2... | collective-permute-start | bytes 12296 | tf_op jit(solution)/shard_map/ppermute | solution.py:442
  151.2 2.0 %collective-permute-done.34.got_b = f32[8,128]{1,0:T(8,128)S(1)} collective-permute-done((f32[8,128]{1,0:T(8,128)S(1)}, f32[8,128]{1,0:T(8,128)S(1)}, u32[]{:S(2)}, u32[]{:S(2)}) %collective-permute-start.34) | collective-permute-done | bytes 4128 | tf_op jit(solution)/shard_map/ppermute | solution.py:442
  154.0 3.4 %collective-permute-start.36 = (f32[8,128]{1,0:T(8,128)S(1)}, f32[8,128]{1,0:T(8,128)S(1)}, u32[]{:S(2)}, u32[]{:S(2)}) collective-permute-start(f32[8,128]{1,0:T(8,128)S(1)} %get-tuple-element.221), channel_id=1, source_target_pairs={{0,0},{12,12},{1,3},{3,1},{2,18},{18,2},{19,17},{17,19},{16,20},{2... | collective-permute-start | bytes 12296 | tf_op jit(solution)/shard_map/ppermute | solution.py:442
  157.4 2.0 %collective-permute-done.36.got_b = f32[8,128]{1,0:T(8,128)S(1)} collective-permute-done((f32[8,128]{1,0:T(8,128)S(1)}, f32[8,128]{1,0:T(8,128)S(1)}, u32[]{:S(2)}, u32[]{:S(2)}) %collective-permute-start.36) | collective-permute-done | bytes 4128 | tf_op jit(solution)/shard_map/ppermute | solution.py:442
  160.0 2.2 %collective-permute-start.38 = (f32[4,2,2,128]{3,2,1,0:T(2,128)S(1)}, f32[4,2,2,128]{3,2,1,0:T(2,128)S(1)}, u32[]{:S(2)}, u32[]{:S(2)}) collective-permute-start(f32[4,2,2,128]{3,2,1,0:T(2,128)S(1)} %rev.22), channel_id=1, source_target_pairs={{1,0},{2,1},{19,2},{16,3},{21,4},{22,5},{7,6},{4,7},{9,8},{10,9},{... | collective-permute-start | bytes 24584 | tf_op jit(solution)/shard_map/ppermute | solution.py:455
  162.2 3.4 %collective-permute-start.39 = (f32[4,2,2,128]{3,2,1,0:T(2,128)S(1)}, f32[4,2,2,128]{3,2,1,0:T(2,128)S(1)}, u32[]{:S(2)}, u32[]{:S(2)}) collective-permute-start(f32[4,2,2,128]{3,2,1,0:T(2,128)S(1)} %get-tuple-element.266), channel_id=1, source_target_pairs={{0,0},{3,1},{18,2},{17,3},{20,4},{23,5},{6,6},{5,7},{8,8},{11,9},{... | collective-permute-start | bytes 24584 | tf_op jit(solution)/shard_map/ppermute | solution.py:454
  165.6 2.2 %collective-permute-done.39 = f32[4,2,2,128]{3,2,1,0:T(2,128)S(1)} collective-permute-done((f32[4,2,2,128]{3,2,1,0:T(2,128)S(1)}, f32[4,2,2,128]{3,2,1,0:T(2,128)S(1)}, u32[]{:S(2)}, u32[]{:S(2)}) %collective-permute-start.39) | collective-permute-done | bytes 8224 | tf_op jit(solution)/shard_map/ppermute | solution.py:454
  (100 shorter events, 23.7 us)
Async XLA Ops:
  0.8 1.6 copy-start
  2.4 1.0 copy-start.1
  3.5 12.2 %copy-start.2 = (f32[1,1,16,4,512]{4,3,2,1,0:T(4,128)S(1)}, f32[1,1,16,4,512]{4,3,2,1,0:T(4,128)}, u32[]{:S(2)}) copy-start(f32[1,1,16,4,512]{4,3,2,1,0:T(4,128)} %param.14) | copy-start | bytes 393220
  3.5 12.2 %copy-start.3 = (f32[2,4,128]{2,1,0:T(4,128)S(1)}, f32[2,4,128]{2,1,0:T(4,128)}, u32[]{:S(2)}) copy-start(f32[2,4,128]{2,1,0:T(4,128)} %param.12) | copy-start | bytes 12292
  3.5 12.2 %copy-start.4 = (f32[2,4,128]{2,1,0:T(4,128)S(1)}, f32[2,4,128]{2,1,0:T(4,128)}, u32[]{:S(2)}) copy-start(f32[2,4,128]{2,1,0:T(4,128)} %param.13) | copy-start | bytes 12292
  3.5 12.2 %copy-start.5 = (s32[1,1,16,4]{2,3,1,0:T(4,128)S(1)}, s32[1,1,16,4]{2,3,1,0:T(4,128)}, u32[]{:S(2)}) copy-start(s32[1,1,16,4]{2,3,1,0:T(4,128)} %param.15) | copy-start | bytes 772
  5.7 54.5 %collective-permute-start.2 = (f32[20,128,128]{2,1,0:T(8,128)}, f32[20,128,128]{2,1,0:T(8,128)S(1)}, u32[]{:S(2)}, u32[]{:S(2)}) collective-permute-start(f32[20,128,128]{2,1,0:T(8,128)} %get-tuple-element.130), channel_id=1, source_target_pairs={{0,0},{1,3},{2,18},{3,17},{4,20},{5,23},{6,6},{7,5},{8,8},{9,11},{... | collective-permute-start | bytes 3932168 | tf_op jit(solution)/shard_map/ppermute | solution.py:397
  9.1 51.1 %collective-permute-start.3 = (f32[20,128,128]{2,1,0:T(8,128)}, f32[20,128,128]{2,1,0:T(8,128)S(1)}, u32[]{:S(2)}, u32[]{:S(2)}) collective-permute-start(f32[20,128,128]{2,1,0:T(8,128)} %get-tuple-element.131), channel_id=1, source_target_pairs={{0,1},{1,2},{2,19},{3,16},{4,21},{5,22},{6,7},{7,4},{8,9},{9,10},{... | collective-permute-start | bytes 3932168 | tf_op jit(solution)/shard_map/ppermute | solution.py:398
  12.3 51.7 %collective-permute-start.4 = (f32[2,128,128]{2,1,0:T(8,128)S(1)}, f32[2,128,128]{2,1,0:T(8,128)S(1)}, u32[]{:S(2)}, u32[]{:S(2)}) collective-permute-start(f32[2,128,128]{2,1,0:T(8,128)S(1)} %get-tuple-element.132), channel_id=1, source_target_pairs={{0,3},{1,18},{2,17},{3,20},{4,23},{5,6},{6,5},{7,8},{8,11},{9,26},... | collective-permute-start | bytes 393224 | tf_op jit(solution)/shard_map/ppermute | solution.py:399
  16.8 26.1 %all-to-all-start = ((f32[1,1,16,5,512]{4,1,3,0,2:T(1,128)}), f32[1,1,16,5,512]{4,1,3,0,2:T(1,128)S(1)}, u32[]{:S(2)}, u32[]{:S(2)}) async-start(f32[1,1,16,5,512]{4,1,3,0,2:T(1,128)} %fusion), calls=%async_computation | async-start | bytes 327680 | tf_op jit(solution)/shard_map/cond/branch_1_fun/all_to_all | solution.py:131
  43.5 5.3 %collective-permute-start.1 = (f32[2,2,768]{2,1,0:T(2,128)S(1)}, f32[2,2,768]{2,1,0:T(2,128)S(1)}, u32[]{:S(2)}, u32[]{:S(2)}) collective-permute-start(f32[2,2,768]{2,1,0:T(2,128)S(1)} %get-tuple-element.256), channel_id=1, source_target_pairs={{0,1},{1,2},{2,19},{3,16},{4,21},{5,22},{6,7},{7,4},{8,9},{9,10},{... | collective-permute-start | bytes 36872 | tf_op jit(solution)/shard_map/cond/branch_1_fun/ppermute | solution.py:410
  45.5 5.9 %collective-permute-start = (f32[2,2,768]{2,1,0:T(2,128)S(1)}, f32[2,2,768]{2,1,0:T(2,128)S(1)}, u32[]{:S(2)}, u32[]{:S(2)}) collective-permute-start(f32[2,2,768]{2,1,0:T(2,128)S(1)} %get-tuple-element.255), channel_id=1, source_target_pairs={{0,0},{1,3},{2,18},{3,17},{4,20},{5,23},{6,6},{7,5},{8,8},{9,11},{... | collective-permute-start | bytes 36872 | tf_op jit(solution)/shard_map/cond/branch_1_fun/ppermute | solution.py:409
  57.8 6.8 %collective-permute-start.5 = (f32[2,128,128]{2,1,0:T(8,128)S(1)}, f32[2,128,128]{2,1,0:T(8,128)S(1)}, u32[]{:S(2)}, u32[]{:S(2)}) collective-permute-start(f32[2,128,128]{2,1,0:T(8,128)S(1)} %get-tuple-element.133), channel_id=1, source_target_pairs={{1,1},{2,2},{3,19},{4,16},{5,21},{6,22},{7,7},{8,4},{9,9},{10,10},... | collective-permute-start | bytes 393224 | tf_op jit(solution)/shard_map/ppermute | solution.py:400
  60.5 5.5 %collective-permute-start.6 = (f32[8,128]{1,0:T(8,128)S(1)}, f32[8,128]{1,0:T(8,128)S(1)}, u32[]{:S(2)}, u32[]{:S(2)}) collective-permute-start(f32[8,128]{1,0:T(8,128)S(1)} %get-tuple-element.138), channel_id=1, source_target_pairs={{0,0},{12,12},{1,3},{3,1},{2,18},{18,2},{19,17},{17,19},{16,20},{2... | collective-permute-start | bytes 12296 | tf_op jit(solution)/shard_map/ppermute | solution.py:442
  63.9 2.1 %collective-permute-start.7 = (f32[8,128]{1,0:T(8,128)S(1)}, f32[8,128]{1,0:T(8,128)S(1)}, u32[]{:S(2)}, u32[]{:S(2)}) collective-permute-start(f32[8,128]{1,0:T(8,128)S(1)} %get-tuple-element.139), channel_id=1, source_target_pairs={{0,1},{1,0},{2,3},{3,2},{4,5},{5,4},{6,7},{7,6},{8,9},{9,8},{10,11... | collective-permute-start | bytes 12296 | tf_op jit(solution)/shard_map/ppermute | solution.py:443
  66.7 5.5 %collective-permute-start.8 = (f32[8,128]{1,0:T(8,128)S(1)}, f32[8,128]{1,0:T(8,128)S(1)}, u32[]{:S(2)}, u32[]{:S(2)}) collective-permute-start(f32[8,128]{1,0:T(8,128)S(1)} %get-tuple-element.141), channel_id=1, source_target_pairs={{0,0},{12,12},{1,3},{3,1},{2,18},{18,2},{19,17},{17,19},{16,20},{2... | collective-permute-start | bytes 12296 | tf_op jit(solution)/shard_map/ppermute | solution.py:442
  70.1 2.1 %collective-permute-start.9 = (f32[8,128]{1,0:T(8,128)S(1)}, f32[8,128]{1,0:T(8,128)S(1)}, u32[]{:S(2)}, u32[]{:S(2)}) collective-permute-start(f32[8,128]{1,0:T(8,128)S(1)} %get-tuple-element.142), channel_id=1, source_target_pairs={{0,1},{1,0},{2,3},{3,2},{4,5},{5,4},{6,7},{7,6},{8,9},{9,8},{10,11... | collective-permute-start | bytes 12296 | tf_op jit(solution)/shard_map/ppermute | solution.py:443
  73.0 5.5 %collective-permute-start.10 = (f32[8,128]{1,0:T(8,128)S(1)}, f32[8,128]{1,0:T(8,128)S(1)}, u32[]{:S(2)}, u32[]{:S(2)}) collective-permute-start(f32[8,128]{1,0:T(8,128)S(1)} %get-tuple-element.147), channel_id=1, source_target_pairs={{0,0},{12,12},{1,3},{3,1},{2,18},{18,2},{19,17},{17,19},{16,20},{2... | collective-permute-start | bytes 12296 | tf_op jit(solution)/shard_map/ppermute | solution.py:442
  76.4 2.1 %collective-permute-start.11 = (f32[8,128]{1,0:T(8,128)S(1)}, f32[8,128]{1,0:T(8,128)S(1)}, u32[]{:S(2)}, u32[]{:S(2)}) collective-permute-start(f32[8,128]{1,0:T(8,128)S(1)} %get-tuple-element.148), channel_id=1, source_target_pairs={{0,1},{1,0},{2,3},{3,2},{4,5},{5,4},{6,7},{7,6},{8,9},{9,8},{10,11... | collective-permute-start | bytes 12296 | tf_op jit(solution)/shard_map/ppermute | solution.py:443
  79.2 5.5 %collective-permute-start.12 = (f32[8,128]{1,0:T(8,128)S(1)}, f32[8,128]{1,0:T(8,128)S(1)}, u32[]{:S(2)}, u32[]{:S(2)}) collective-permute-start(f32[8,128]{1,0:T(8,128)S(1)} %get-tuple-element.153), channel_id=1, source_target_pairs={{0,0},{12,12},{1,3},{3,1},{2,18},{18,2},{19,17},{17,19},{16,20},{2... | collective-permute-start | bytes 12296 | tf_op jit(solution)/shard_map/ppermute | solution.py:442
  82.6 2.1 %collective-permute-start.13 = (f32[8,128]{1,0:T(8,128)S(1)}, f32[8,128]{1,0:T(8,128)S(1)}, u32[]{:S(2)}, u32[]{:S(2)}) collective-permute-start(f32[8,128]{1,0:T(8,128)S(1)} %get-tuple-element.154), channel_id=1, source_target_pairs={{0,1},{1,0},{2,3},{3,2},{4,5},{5,4},{6,7},{7,6},{8,9},{9,8},{10,11... | collective-permute-start | bytes 12296 | tf_op jit(solution)/shard_map/ppermute | solution.py:443
  85.4 5.5 %collective-permute-start.14 = (f32[8,128]{1,0:T(8,128)S(1)}, f32[8,128]{1,0:T(8,128)S(1)}, u32[]{:S(2)}, u32[]{:S(2)}) collective-permute-start(f32[8,128]{1,0:T(8,128)S(1)} %get-tuple-element.161), channel_id=1, source_target_pairs={{0,0},{12,12},{1,3},{3,1},{2,18},{18,2},{19,17},{17,19},{16,20},{2... | collective-permute-start | bytes 12296 | tf_op jit(solution)/shard_map/ppermute | solution.py:442
  88.8 2.1 %collective-permute-start.15 = (f32[8,128]{1,0:T(8,128)S(1)}, f32[8,128]{1,0:T(8,128)S(1)}, u32[]{:S(2)}, u32[]{:S(2)}) collective-permute-start(f32[8,128]{1,0:T(8,128)S(1)} %get-tuple-element.162), channel_id=1, source_target_pairs={{0,1},{1,0},{2,3},{3,2},{4,5},{5,4},{6,7},{7,6},{8,9},{9,8},{10,11... | collective-permute-start | bytes 12296 | tf_op jit(solution)/shard_map/ppermute | solution.py:443
  91.7 5.5 %collective-permute-start.16 = (f32[8,128]{1,0:T(8,128)S(1)}, f32[8,128]{1,0:T(8,128)S(1)}, u32[]{:S(2)}, u32[]{:S(2)}) collective-permute-start(f32[8,128]{1,0:T(8,128)S(1)} %get-tuple-element.164), channel_id=1, source_target_pairs={{0,0},{12,12},{1,3},{3,1},{2,18},{18,2},{19,17},{17,19},{16,20},{2... | collective-permute-start | bytes 12296 | tf_op jit(solution)/shard_map/ppermute | solution.py:442
  95.0 2.1 %collective-permute-start.17 = (f32[8,128]{1,0:T(8,128)S(1)}, f32[8,128]{1,0:T(8,128)S(1)}, u32[]{:S(2)}, u32[]{:S(2)}) collective-permute-start(f32[8,128]{1,0:T(8,128)S(1)} %get-tuple-element.165), channel_id=1, source_target_pairs={{0,1},{1,0},{2,3},{3,2},{4,5},{5,4},{6,7},{7,6},{8,9},{9,8},{10,11... | collective-permute-start | bytes 12296 | tf_op jit(solution)/shard_map/ppermute | solution.py:443
  97.9 5.5 %collective-permute-start.18 = (f32[8,128]{1,0:T(8,128)S(1)}, f32[8,128]{1,0:T(8,128)S(1)}, u32[]{:S(2)}, u32[]{:S(2)}) collective-permute-start(f32[8,128]{1,0:T(8,128)S(1)} %get-tuple-element.170), channel_id=1, source_target_pairs={{0,0},{12,12},{1,3},{3,1},{2,18},{18,2},{19,17},{17,19},{16,20},{2... | collective-permute-start | bytes 12296 | tf_op jit(solution)/shard_map/ppermute | solution.py:442
  101.3 2.1 %collective-permute-start.19 = (f32[8,128]{1,0:T(8,128)S(1)}, f32[8,128]{1,0:T(8,128)S(1)}, u32[]{:S(2)}, u32[]{:S(2)}) collective-permute-start(f32[8,128]{1,0:T(8,128)S(1)} %get-tuple-element.171), channel_id=1, source_target_pairs={{0,1},{1,0},{2,3},{3,2},{4,5},{5,4},{6,7},{7,6},{8,9},{9,8},{10,11... | collective-permute-start | bytes 12296 | tf_op jit(solution)/shard_map/ppermute | solution.py:443
  104.1 5.5 %collective-permute-start.20 = (f32[8,128]{1,0:T(8,128)S(1)}, f32[8,128]{1,0:T(8,128)S(1)}, u32[]{:S(2)}, u32[]{:S(2)}) collective-permute-start(f32[8,128]{1,0:T(8,128)S(1)} %get-tuple-element.176), channel_id=1, source_target_pairs={{0,0},{12,12},{1,3},{3,1},{2,18},{18,2},{19,17},{17,19},{16,20},{2... | collective-permute-start | bytes 12296 | tf_op jit(solution)/shard_map/ppermute | solution.py:442
  107.5 2.1 %collective-permute-start.21 = (f32[8,128]{1,0:T(8,128)S(1)}, f32[8,128]{1,0:T(8,128)S(1)}, u32[]{:S(2)}, u32[]{:S(2)}) collective-permute-start(f32[8,128]{1,0:T(8,128)S(1)} %get-tuple-element.177), channel_id=1, source_target_pairs={{0,1},{1,0},{2,3},{3,2},{4,5},{5,4},{6,7},{7,6},{8,9},{9,8},{10,11... | collective-permute-start | bytes 12296 | tf_op jit(solution)/shard_map/ppermute | solution.py:443
  110.3 5.5 %collective-permute-start.22 = (f32[8,128]{1,0:T(8,128)S(1)}, f32[8,128]{1,0:T(8,128)S(1)}, u32[]{:S(2)}, u32[]{:S(2)}) collective-permute-start(f32[8,128]{1,0:T(8,128)S(1)} %get-tuple-element.184), channel_id=1, source_target_pairs={{0,0},{12,12},{1,3},{3,1},{2,18},{18,2},{19,17},{17,19},{16,20},{2... | collective-permute-start | bytes 12296 | tf_op jit(solution)/shard_map/ppermute | solution.py:442
  113.7 2.1 %collective-permute-start.23 = (f32[8,128]{1,0:T(8,128)S(1)}, f32[8,128]{1,0:T(8,128)S(1)}, u32[]{:S(2)}, u32[]{:S(2)}) collective-permute-start(f32[8,128]{1,0:T(8,128)S(1)} %get-tuple-element.185), channel_id=1, source_target_pairs={{0,1},{1,0},{2,3},{3,2},{4,5},{5,4},{6,7},{7,6},{8,9},{9,8},{10,11... | collective-permute-start | bytes 12296 | tf_op jit(solution)/shard_map/ppermute | solution.py:443
  116.6 5.5 %collective-permute-start.24 = (f32[8,128]{1,0:T(8,128)S(1)}, f32[8,128]{1,0:T(8,128)S(1)}, u32[]{:S(2)}, u32[]{:S(2)}) collective-permute-start(f32[8,128]{1,0:T(8,128)S(1)} %get-tuple-element.187), channel_id=1, source_target_pairs={{0,0},{12,12},{1,3},{3,1},{2,18},{18,2},{19,17},{17,19},{16,20},{2... | collective-permute-start | bytes 12296 | tf_op jit(solution)/shard_map/ppermute | solution.py:442
  120.0 2.1 %collective-permute-start.25 = (f32[8,128]{1,0:T(8,128)S(1)}, f32[8,128]{1,0:T(8,128)S(1)}, u32[]{:S(2)}, u32[]{:S(2)}) collective-permute-start(f32[8,128]{1,0:T(8,128)S(1)} %get-tuple-element.188), channel_id=1, source_target_pairs={{0,1},{1,0},{2,3},{3,2},{4,5},{5,4},{6,7},{7,6},{8,9},{9,8},{10,11... | collective-permute-start | bytes 12296 | tf_op jit(solution)/shard_map/ppermute | solution.py:443
  122.8 5.5 %collective-permute-start.26 = (f32[8,128]{1,0:T(8,128)S(1)}, f32[8,128]{1,0:T(8,128)S(1)}, u32[]{:S(2)}, u32[]{:S(2)}) collective-permute-start(f32[8,128]{1,0:T(8,128)S(1)} %get-tuple-element.193), channel_id=1, source_target_pairs={{0,0},{12,12},{1,3},{3,1},{2,18},{18,2},{19,17},{17,19},{16,20},{2... | collective-permute-start | bytes 12296 | tf_op jit(solution)/shard_map/ppermute | solution.py:442
  126.2 2.1 %collective-permute-start.27 = (f32[8,128]{1,0:T(8,128)S(1)}, f32[8,128]{1,0:T(8,128)S(1)}, u32[]{:S(2)}, u32[]{:S(2)}) collective-permute-start(f32[8,128]{1,0:T(8,128)S(1)} %get-tuple-element.194), channel_id=1, source_target_pairs={{0,1},{1,0},{2,3},{3,2},{4,5},{5,4},{6,7},{7,6},{8,9},{9,8},{10,11... | collective-permute-start | bytes 12296 | tf_op jit(solution)/shard_map/ppermute | solution.py:443
  129.0 5.5 %collective-permute-start.28 = (f32[8,128]{1,0:T(8,128)S(1)}, f32[8,128]{1,0:T(8,128)S(1)}, u32[]{:S(2)}, u32[]{:S(2)}) collective-permute-start(f32[8,128]{1,0:T(8,128)S(1)} %get-tuple-element.199), channel_id=1, source_target_pairs={{0,0},{12,12},{1,3},{3,1},{2,18},{18,2},{19,17},{17,19},{16,20},{2... | collective-permute-start | bytes 12296 | tf_op jit(solution)/shard_map/ppermute | solution.py:442
  132.6 1.9 %collective-permute-start.29 = (f32[8,128]{1,0:T(8,128)S(1)}, f32[8,128]{1,0:T(8,128)S(1)}, u32[]{:S(2)}, u32[]{:S(2)}) collective-permute-start(f32[8,128]{1,0:T(8,128)S(1)} %get-tuple-element.200), channel_id=1, source_target_pairs={{0,1},{1,0},{2,3},{3,2},{4,5},{5,4},{6,7},{7,6},{8,9},{9,8},{10,11... | collective-permute-start | bytes 12296 | tf_op jit(solution)/shard_map/ppermute | solution.py:443
  135.3 5.5 %collective-permute-start.30 = (f32[8,128]{1,0:T(8,128)S(1)}, f32[8,128]{1,0:T(8,128)S(1)}, u32[]{:S(2)}, u32[]{:S(2)}) collective-permute-start(f32[8,128]{1,0:T(8,128)S(1)} %get-tuple-element.206), channel_id=1, source_target_pairs={{0,0},{12,12},{1,3},{3,1},{2,18},{18,2},{19,17},{17,19},{16,20},{2... | collective-permute-start | bytes 12296 | tf_op jit(solution)/shard_map/ppermute | solution.py:442
  138.7 2.1 %collective-permute-start.31 = (f32[8,128]{1,0:T(8,128)S(1)}, f32[8,128]{1,0:T(8,128)S(1)}, u32[]{:S(2)}, u32[]{:S(2)}) collective-permute-start(f32[8,128]{1,0:T(8,128)S(1)} %get-tuple-element.207), channel_id=1, source_target_pairs={{0,1},{1,0},{2,3},{3,2},{4,5},{5,4},{6,7},{7,6},{8,9},{9,8},{10,11... | collective-permute-start | bytes 12296 | tf_op jit(solution)/shard_map/ppermute | solution.py:443
  141.5 5.5 %collective-permute-start.32 = (f32[8,128]{1,0:T(8,128)S(1)}, f32[8,128]{1,0:T(8,128)S(1)}, u32[]{:S(2)}, u32[]{:S(2)}) collective-permute-start(f32[8,128]{1,0:T(8,128)S(1)} %get-tuple-element.209), channel_id=1, source_target_pairs={{0,0},{12,12},{1,3},{3,1},{2,18},{18,2},{19,17},{17,19},{16,20},{2... | collective-permute-start | bytes 12296 | tf_op jit(solution)/shard_map/ppermute | solution.py:442
  144.9 2.1 %collective-permute-start.33 = (f32[8,128]{1,0:T(8,128)S(1)}, f32[8,128]{1,0:T(8,128)S(1)}, u32[]{:S(2)}, u32[]{:S(2)}) collective-permute-start(f32[8,128]{1,0:T(8,128)S(1)} %get-tuple-element.210), channel_id=1, source_target_pairs={{0,1},{1,0},{2,3},{3,2},{4,5},{5,4},{6,7},{7,6},{8,9},{9,8},{10,11... | collective-permute-start | bytes 12296 | tf_op jit(solution)/shard_map/ppermute | solution.py:443
  147.7 5.5 %collective-permute-start.34 = (f32[8,128]{1,0:T(8,128)S(1)}, f32[8,128]{1,0:T(8,128)S(1)}, u32[]{:S(2)}, u32[]{:S(2)}) collective-permute-start(f32[8,128]{1,0:T(8,128)S(1)} %get-tuple-element.215), channel_id=1, source_target_pairs={{0,0},{12,12},{1,3},{3,1},{2,18},{18,2},{19,17},{17,19},{16,20},{2... | collective-permute-start | bytes 12296 | tf_op jit(solution)/shard_map/ppermute | solution.py:442
  151.1 2.1 %collective-permute-start.35 = (f32[8,128]{1,0:T(8,128)S(1)}, f32[8,128]{1,0:T(8,128)S(1)}, u32[]{:S(2)}, u32[]{:S(2)}) collective-permute-start(f32[8,128]{1,0:T(8,128)S(1)} %get-tuple-element.216), channel_id=1, source_target_pairs={{0,1},{1,0},{2,3},{3,2},{4,5},{5,4},{6,7},{7,6},{8,9},{9,8},{10,11... | collective-permute-start | bytes 12296 | tf_op jit(solution)/shard_map/ppermute | solution.py:443
  154.0 5.5 %collective-permute-start.36 = (f32[8,128]{1,0:T(8,128)S(1)}, f32[8,128]{1,0:T(8,128)S(1)}, u32[]{:S(2)}, u32[]{:S(2)}) collective-permute-start(f32[8,128]{1,0:T(8,128)S(1)} %get-tuple-element.221), channel_id=1, source_target_pairs={{0,0},{12,12},{1,3},{3,1},{2,18},{18,2},{19,17},{17,19},{16,20},{2... | collective-permute-start | bytes 12296 | tf_op jit(solution)/shard_map/ppermute | solution.py:442
  157.3 2.1 %collective-permute-start.37 = (f32[8,128]{1,0:T(8,128)S(1)}, f32[8,128]{1,0:T(8,128)S(1)}, u32[]{:S(2)}, u32[]{:S(2)}) collective-permute-start(f32[8,128]{1,0:T(8,128)S(1)} %get-tuple-element.222), channel_id=1, source_target_pairs={{0,1},{1,0},{2,3},{3,2},{4,5},{5,4},{6,7},{7,6},{8,9},{9,8},{10,11... | collective-permute-start | bytes 12296 | tf_op jit(solution)/shard_map/ppermute | solution.py:443
  160.0 5.6 %collective-permute-start.38 = (f32[4,2,2,128]{3,2,1,0:T(2,128)S(1)}, f32[4,2,2,128]{3,2,1,0:T(2,128)S(1)}, u32[]{:S(2)}, u32[]{:S(2)}) collective-permute-start(f32[4,2,2,128]{3,2,1,0:T(2,128)S(1)} %rev.22), channel_id=1, source_target_pairs={{1,0},{2,1},{19,2},{16,3},{21,4},{22,5},{7,6},{4,7},{9,8},{10,9},{... | collective-permute-start | bytes 24584 | tf_op jit(solution)/shard_map/ppermute | solution.py:455
  162.2 5.5 %collective-permute-start.39 = (f32[4,2,2,128]{3,2,1,0:T(2,128)S(1)}, f32[4,2,2,128]{3,2,1,0:T(2,128)S(1)}, u32[]{:S(2)}, u32[]{:S(2)}) collective-permute-start(f32[4,2,2,128]{3,2,1,0:T(2,128)S(1)} %get-tuple-element.266), channel_id=1, source_target_pairs={{0,0},{3,1},{18,2},{17,3},{20,4},{23,5},{6,6},{5,7},{8,8},{11,9},{... | collective-permute-start | bytes 24584 | tf_op jit(solution)/shard_map/ppermute | solution.py:454

commit v6 on v4

--- a/solution.py
+++ b/solution.py
@@ -195,52 +195,53 @@
 
 
 def unit_device(unit, n_col):
-    group, place = divmod(unit // 2, 4)
-    x, row = ((0, 0), (1, 0), (1, 1), (0, 1))[place]
-    return (row + group) % 2 * n_col + 4 * group + 2 * x + unit % 2
-
-
-def deal_pairs(n_col, which):
-    rounds = []
-    for i in (0, 1):
-        pairs = []
-        for row in (0, 1):
-            for col in range(n_col):
-                k = row ^ i
-                unit = 2 * col + k if which == 0 else 2 * col + (2 if k == 0 else -1)
-                if 0 <= unit < 2 * n_col:
-                    pairs.append((row * n_col + col, unit_device(unit, n_col)))
-        rounds.append(pairs)
-    return rounds
-
-
-def pack_kernel(n_col, place_ref, pattern_ref, own_ref, nb_ref, send_0, send_1, facing_0, facing_1):
+    col = unit // 2
+    return (unit + col) % 2, col
+
+
+def pack_kernel(n_col, place_ref, pattern_ref, own_hbm, nb_hbm, keep, send, facing_0, facing_1, own_ref, nb_ref, sems):
     y, col = place_ref[0], place_ref[1]
+    copies = [pltpu.make_async_copy(own_hbm, own_ref, sems.at[4])]
+    copies += [pltpu.make_async_copy(nb_hbm.at[d], nb_ref.at[d], sems.at[d]) for d in (2, 3, 0, 1)]
+    for copy in copies:
+        copy.start()
     rows = (y, 1 - y)
     inward, outward = 1 - y, y
     cols = own_ref.shape[1]
 
-    def coupling(direction, row, col):
-        weight = pattern_ref[(row * cols + col) * 4 + direction].astype(jnp.float32)
-        return nb_ref[direction, row, col] * weight
-
-    for i, (send, facing) in enumerate(((send_0, facing_0), (send_1, facing_1))):
-        k = (y + i) % 2
-        at = [b + k * (cols - 1 - 2 * b) for b in range(HALF)]
-        side_a, side_b = 3 - k, 2 + k
+    def coupling(direction, row, at_col):
+        weight = pattern_ref[(row * cols + at_col) * 4 + direction].astype(jnp.float32)
+        return nb_ref[direction, row, at_col] * weight
+
+    halves = []
+    for i, (half, facing) in enumerate(((keep, facing_0), (send, facing_1))):
+        k = (y + col + i) % 2
+        halves.append((half, facing, k, [b + k * (cols - 1 - 2 * b) for b in range(HALF)]))
+    copies[0].wait()
+    for half, facing, k, at in halves:
+        for h in range(ROWS):
+            for b in range(HALF):
+                half[OWN + h * HALF + b] = own_ref[rows[h], at[b]]
+    for copy in copies[1:3]:
+        copy.wait()
+    for half, facing, k, at in halves:
         inside = jnp.where(col == k * (n_col - 1), 0.0, 1.0)
         for h in range(ROWS):
             for b in range(HALF):
-                send[OWN + h * HALF + b] = own_ref[rows[h], at[b]]
-                send[SIDE_A + h * HALF + b] = coupling(side_a, rows[h], at[b])
-                block = coupling(side_b, rows[h], at[b])
-                send[SIDE_B + h * HALF + b] = block * inside if b == 0 else block
-            send[FACING + h] = coupling(2 + k, rows[h], HALF - k)
-            facing[h] = coupling(3 - k, rows[h], (cols - 1) * (1 - k))
+                half[SIDE_A + h * HALF + b] = coupling(3 - k, rows[h], at[b])
+                block = coupling(2 + k, rows[h], at[b])
+                if b == 0:
+                    block = block * inside
+                    facing[h] = block
+                half[SIDE_B + h * HALF + b] = block
+            half[FACING + h] = coupling(2 + k, rows[h], HALF - k)
+    for copy in copies[3:]:
+        copy.wait()
+    for half, facing, k, at in halves:
         for b in range(HALF):
-            send[OUT_IN + b] = coupling(inward, rows[0], at[b])
-            send[IN_OUT + b] = coupling(outward, rows[1], at[b])
-            send[IN_IN + b] = coupling(inward, rows[1], at[b])
+            half[OUT_IN + b] = coupling(inward, rows[0], at[b])
+            half[IN_OUT + b] = coupling(outward, rows[1], at[b])
+            half[IN_IN + b] = coupling(inward, rows[1], at[b])
 
 
 def tile_terms(halves, j, b):
@@ -294,7 +295,8 @@
 
 def messages(f, g):
     return [
-        jnp.concatenate([row_of(x, j, b) for x in (f, g) for j in reversed(range(N))], axis=0) for b in (1, 0)
+        jnp.concatenate([row_of(x, j, b) for x in (f, g) for j in order], axis=0)
+        for b, order in ((1, range(N)[::-1]), (0, range(N)))
     ]
 
 
@@ -304,7 +306,7 @@
     return residue - STRIDES[sweep] * (q + capacity * f) + MOMENTA[sweep + 1] * f
 
 
-def start_kernel(half_0, half_1, field, injected, msg_a, msg_b, q_out):
+def start_kernel(half_0, half_1, beyond_0, beyond_1, field, injected, msg_a, msg_b, q_out):
     f = field[...]
     q = inner_product(f, (half_0, half_1))
     q_out[...] = q
@@ -371,34 +373,39 @@
 def shards_chain(own_block, neighbor_block, pattern, capacity, initial, currents, slot_tile):
     tile_rows, tile_cols, width = initial.shape
     n_col = lax.axis_size("col")
-    row = lax.axis_index("row")
+    row, col = lax.axis_index("row"), lax.axis_index("col")
     both = ("row", "col")
-    deal = deal_pairs(n_col, 0)
-    deal_b = deal_pairs(n_col, 1)
-    a_pairs = [(c, c ^ 1) for c in range(n_col)]
-    b_pairs = [(unit_device(unit, n_col),) * 2 for unit in (0, 2 * n_col - 1)]
+    swap = [(0, 1), (1, 0)]
+    b_pairs, b_cross = [], []
     for unit in range(1, 2 * n_col - 1, 2):
-        one, two = unit_device(unit, n_col), unit_device(unit + 1, n_col)
-        b_pairs += [(one, two), (two, one)]
+        ends = unit_device(unit, n_col), unit_device(unit + 1, n_col)
+        for (r, c), (to_r, to_c) in (ends, ends[::-1]):
+            b_pairs.append((r * n_col + c, to_r * n_col + to_c))
+            b_cross.append(((1 - r) * n_col + c, to_r * n_col + to_c))
+    parity = (row + col) % 2
 
     vmem = pl.BlockSpec(memory_space=pltpu.VMEM)
     smem = pl.BlockSpec(memory_space=pltpu.SMEM)
+    hbm = pl.BlockSpec(memory_space=pltpu.HBM)
     limit = pltpu.CompilerParams(vmem_limit_bytes=16 * 2**20)
     packed = jax.ShapeDtypeStruct((PACKED, width, width), jnp.float32)
     facing = jax.ShapeDtypeStruct((ROWS, width, width), jnp.float32)
-    send_0, send_1, facing_0, facing_1 = pl.pallas_call(
+    half_0, send, facing_0, facing_1 = pl.pallas_call(
         functools.partial(pack_kernel, n_col),
         out_shape=(packed, packed, facing, facing),
-        in_specs=[smem, smem, vmem, vmem],
+        in_specs=[smem, smem, hbm, hbm],
         out_specs=(vmem,) * 4,
-        compiler_params=limit,
+        scratch_shapes=[
+            pltpu.VMEM(own_block.shape, jnp.float32),
+            pltpu.VMEM(neighbor_block.shape, jnp.float32),
+            pltpu.SemaphoreType.DMA((5,)),
+        ],
+        compiler_params=pltpu.CompilerParams(vmem_limit_bytes=48 * 2**20),
         name="pack",
-    )(jnp.stack([row, lax.axis_index("col")]).astype(jnp.int32), pattern.reshape(-1), own_block, neighbor_block)
-    currents, slot_tile, facing_0, facing_1 = lax.optimization_barrier((currents, slot_tile, facing_0, facing_1))
-    half_0 = lax.ppermute(send_0, both, deal[0])
-    half_1 = lax.ppermute(send_1, both, deal[1])
-    beyond_0 = lax.ppermute(facing_0, both, deal_b[0])
-    beyond_1 = lax.ppermute(facing_1, both, deal_b[1])
+    )(jnp.stack([row, col]).astype(jnp.int32), pattern.reshape(-1), own_block, neighbor_block)
+    half_1 = lax.ppermute(send, "row", swap)
+    beyond_0 = lax.ppermute(facing_0, both, b_pairs)
+    beyond_1 = lax.ppermute(facing_1, both, b_cross)
 
     injected = collect(currents, slot_tile, tile_rows * tile_cols, width)
     small = jnp.concatenate(
@@ -406,9 +413,9 @@
     )
     small = jnp.where(row == 1, jnp.flip(small, 0), small)
     unit_0, unit_1 = small[:, :HALF], jnp.flip(small, 1)[:, :HALF]
-    got_0 = lax.ppermute(jnp.where(row == 1, unit_1, unit_0), both, deal[0])
-    got_1 = lax.ppermute(jnp.where(row == 1, unit_0, unit_1), both, deal[1])
-    small = jnp.concatenate([got_0, jnp.flip(got_1, 0)], axis=0).reshape(N * HALF, STEPS + 2, width)
+    got = lax.ppermute(jnp.where(parity == 1, unit_0, unit_1), "row", swap)
+    small = jnp.concatenate([jnp.where(parity == 1, unit_1, unit_0), jnp.flip(got, 0)], axis=0)
+    small = small.reshape(N * HALF, STEPS + 2, width)
     injected, cap, field = small[:, :STEPS], small[:, STEPS], small[:, STEPS + 1]
 
     shape = jax.ShapeDtypeStruct((N * HALF, width), jnp.float32)
@@ -425,7 +432,7 @@
             name="pair",
         )(*ins)
 
-    msg_a, msg_b, q = call(start_kernel, 3, 28, half_0, half_1, field, injected[:, 0])
+    msg_a, msg_b, q = call(start_kernel, 3, 28, half_0, half_1, beyond_0, beyond_1, field, injected[:, 0])
     frames = []
     for instant in range(STEPS):
         state = ()
@@ -433,7 +440,7 @@
             closing = pair + 1 == ITERS // 2
             last = closing and instant + 1 == STEPS
             got_b = lax.ppermute(msg_b, both, b_pairs)
-            got_a = lax.ppermute(msg_a, "col", a_pairs)
+            got_a = lax.ppermute(msg_a, "row", swap)
             feed = injected[:, min(instant + closing, STEPS - 1)]
             out = call(functools.partial(pair_kernel, pair, last), 1 if last else 4 if closing else 6, 80,
                        half_0, half_1, beyond_0, beyond_1, cap, feed, got_a, got_b, field, q, *state)
@@ -444,9 +451,9 @@
         frames.append(field)
 
     done = jnp.stack(frames).reshape(STEPS, N, HALF, width)
-    got_0 = lax.ppermute(done[:, :ROWS], both, [(b, a) for a, b in deal[0]])
-    got_1 = lax.ppermute(jnp.flip(done[:, ROWS:], 1), both, [(b, a) for a, b in deal[1]])
-    unit_0, unit_1 = jnp.where(row == 1, got_1, got_0), jnp.where(row == 1, got_0, got_1)
+    got = lax.ppermute(jnp.flip(done[:, ROWS:], 1), "row", swap)
+    mine = done[:, :ROWS]
+    unit_0, unit_1 = jnp.where(parity == 1, got, mine), jnp.where(parity == 1, mine, got)
     done = jnp.concatenate([unit_0, jnp.flip(unit_1, 2)], axis=2)
     return jnp.where(row == 1, jnp.flip(done, 1), done)
 
@@ -454,7 +461,7 @@
 def solution(mesh):
     rows, cols = mesh.shape["row"], mesh.shape["col"]
     return jax.shard_map(
-        shards_chain if rows == 2 and cols % 4 == 0 else shards_general,
+        shards_chain if rows == 2 else shards_general,
         mesh=mesh,
         in_specs=(
             P("row", "col", None, None),

time: 159 us -> 161 us (1.013)
  waiting for transfers between devices: 50.2 us -> 69.5 us
  starting transfers between devices: 86.9 us -> 68.8 us
    ppermute x24 -> x21, starting transfers between devices: 28.7 us -> 9.41 us  [the longest x1 3.02 us: shards_chain(): beyond_0 = lax.ppermute(facing_0, both, b_pairs)]
    ppermute x16, waiting for transfers between devices: 25 us -> 36 us  [shards_chain(): got_b = lax.ppermute(msg_b, both, b_pairs)]
    ppermute x24 -> x21, waiting for transfers between devices: 25.2 us -> 33.5 us  [the longest x1 25.9 us: shards_chain(): got = lax.ppermute(jnp.where(parity == 1, unit_0, unit_1), 'row', swap)]
    unnamed x17 -> x12, local copies, waits for them, and re-layouts: 3.83 us -> 3.78 us
  transfers between devices with their start and end apart: 41 -> 38, of which waited for: 19 -> 33; matrix products, arithmetic and copies ran while one was open for 0% -> 1% of each run, Pallas kernels for 0% -> 1%
where the time goes in v6:
time: 161 us; the launch traced here: 160 us
  waiting for transfers between devices  69.5 us (43%)
  starting transfers between devices  68.8 us (43%)
  Pallas kernels  13.6 us (8%)
  local copies, waits for them, and re-layouts  4.95 us (3%)
  other arithmetic  2.23 us (1%)
    ppermute x16, starting transfers between devices, shards_chain(): got_b = lax.ppermute(msg_b, both, b_pairs)  53.1 us
    ppermute x16, waiting for transfers between devices, shards_chain(): got_b = lax.ppermute(msg_b, both, b_pairs)  36 us
    ppermute x1, waiting for transfers between devices, shards_chain(): got = lax.ppermute(jnp.where(parity == 1, unit_0, unit_1), 'row', swap)  25.9 us
    pallas_call x17, Pallas kernels, call(): pl.pallas_call(body, out_shape=(shape,) * n_out, in_specs=[vmem] * len(in...  11.6 us
    all_to_all x1, starting transfers between devices, collect(): lax.all_to_all(packed, 'col', split_axis=2, concat_axis=1, tiled=True)  6.27 us
    ppermute x16, waiting for transfers between devices, shards_chain(): got_a = lax.ppermute(msg_a, 'row', swap)  3.95 us
    unnamed x12, local copies, waits for them, and re-layouts  3.78 us
    ppermute x1, waiting for transfers between devices, shards_chain(): got = lax.ppermute(jnp.flip(done[:, ROWS:], 1), 'row', swap)  3.64 us
  transfers between devices with their start and end apart: 38, of which 33 were waited for; matrix products, arithmetic and copies ran while one was open for 1% of the time, Pallas kernels for 1%

profile of v6, /device:TPU:8, one launch (start us, length us, event | category | flops | bytes accessed | tf_op | source)
XLA Modules:
  0.0 159.9 jit_solution(1336694737737881418)
XLA Ops:
  0.8 1.0 copy.30
  1.8 0.8 fusion
  2.6 6.3 %all-to-all-start = ((f32[1,1,16,5,512]{4,1,3,0,2:T(1,128)}), f32[1,1,16,5,512]{4,1,3,0,2:T(1,128)S(1)}, u32[]{:S(2)}, u32[]{:S(2)}) async-start(f32[1,1,16,5,512]{4,1,3,0,2:T(1,128)} %fusion), calls=%async_computation | async-start | bytes 327680 | tf_op jit(solution)/shard_map/all_to_all | solution.py:131
  8.9 0.8 reshape.20.pattern_ref
  9.7 1.6 copy-done
  11.3 1.0 copy-done.1
  12.4 2.1 %pack.1 = (f32[20,128,128]{2,1,0:T(8,128)S(1)}, f32[20,128,128]{2,1,0:T(8,128)}, f32[2,128,128]{2,1,0:T(8,128)S(1)}, f32[2,128,128]{2,1,0:T(8,128)S(1)}) custom-call(s32[2]{0:T(128)S(1)} %pad_add_fusion.place_ref, s32[32]{0:T(128)S(1)} %reshape.20.pattern_ref, f32[2,4,128,128]{3,2,1,0:T(8,128)S(1)} %copy-done.1, f32[4,2,4,128,128]{4,3,2,1,0:T(8,128)S(1)} %copy-done), custom_call_target="tpu_custom_call" | custom-call | tf_op jit(solution)/shard_map/pack/pallas_call | solution.py:393
  14.5 1.6 collective-permute-start
  17.3 3.0 %collective-permute-start.1 = (f32[2,128,128]{2,1,0:T(8,128)S(1)}, f32[2,128,128]{2,1,0:T(8,128)S(1)}, u32[]{:S(2)}, u32[]{:S(2)}) collective-permute-start(f32[2,128,128]{2,1,0:T(8,128)S(1)} %get-tuple-element.98), channel_id=1, source_target_pairs={{16,17},{17,16},{1,2},{2,1},{18,19},{19,18},{3,4},{4,3},{20,21},{2... | collective-permute-start | bytes 393224 | tf_op jit(solution)/shard_map/ppermute | solution.py:407
  20.3 2.4 %collective-permute-start.2 = (f32[2,128,128]{2,1,0:T(8,128)S(1)}, f32[2,128,128]{2,1,0:T(8,128)S(1)}, u32[]{:S(2)}, u32[]{:S(2)}) collective-permute-start(f32[2,128,128]{2,1,0:T(8,128)S(1)} %get-tuple-element.99), channel_id=1, source_target_pairs={{0,17},{1,16},{17,2},{18,1},{2,19},{3,18},{19,4},{20,3},{4,21},{5,... | collective-permute-start | bytes 393224 | tf_op jit(solution)/shard_map/ppermute | solution.py:408
  22.7 25.9 %collective-permute-done.3 = f32[2,2,768]{2,1,0:T(2,128)S(1)} collective-permute-done((f32[2,2,768]{2,1,0:T(2,128)S(1)}, f32[2,2,768]{2,1,0:T(2,128)S(1)}, u32[]{:S(2)}, u32[]{:S(2)}) %collective-permute-start.3) | collective-permute-done | bytes 12320 | tf_op jit(solution)/shard_map/ppermute | solution.py:416
  49.7 3.3 %collective-permute-start.5 = (f32[8,128]{1,0:T(8,128)S(1)}, f32[8,128]{1,0:T(8,128)S(1)}, u32[]{:S(2)}, u32[]{:S(2)}) collective-permute-start(f32[8,128]{1,0:T(8,128)S(1)} %get-tuple-element.101), channel_id=1, source_target_pairs={{16,17},{17,16},{1,2},{2,1},{18,19},{19,18},{3,4},{4,3},{20,21},{2... | collective-permute-start | bytes 12296 | tf_op jit(solution)/shard_map/ppermute | solution.py:442
  53.0 2.5 %collective-permute-done.5.got_b = f32[8,128]{1,0:T(8,128)S(1)} collective-permute-done((f32[8,128]{1,0:T(8,128)S(1)}, f32[8,128]{1,0:T(8,128)S(1)}, u32[]{:S(2)}, u32[]{:S(2)}) %collective-permute-start.5) | collective-permute-done | bytes 4128 | tf_op jit(solution)/shard_map/ppermute | solution.py:442
  56.3 3.3 %collective-permute-start.7 = (f32[8,128]{1,0:T(8,128)S(1)}, f32[8,128]{1,0:T(8,128)S(1)}, u32[]{:S(2)}, u32[]{:S(2)}) collective-permute-start(f32[8,128]{1,0:T(8,128)S(1)} %get-tuple-element.104), channel_id=1, source_target_pairs={{16,17},{17,16},{1,2},{2,1},{18,19},{19,18},{3,4},{4,3},{20,21},{2... | collective-permute-start | bytes 12296 | tf_op jit(solution)/shard_map/ppermute | solution.py:442
  59.9 2.2 %collective-permute-done.7.got_b = f32[8,128]{1,0:T(8,128)S(1)} collective-permute-done((f32[8,128]{1,0:T(8,128)S(1)}, f32[8,128]{1,0:T(8,128)S(1)}, u32[]{:S(2)}, u32[]{:S(2)}) %collective-permute-start.7) | collective-permute-done | bytes 4128 | tf_op jit(solution)/shard_map/ppermute | solution.py:442
  62.9 3.3 %collective-permute-start.9 = (f32[8,128]{1,0:T(8,128)S(1)}, f32[8,128]{1,0:T(8,128)S(1)}, u32[]{:S(2)}, u32[]{:S(2)}) collective-permute-start(f32[8,128]{1,0:T(8,128)S(1)} %get-tuple-element.110), channel_id=1, source_target_pairs={{16,17},{17,16},{1,2},{2,1},{18,19},{19,18},{3,4},{4,3},{20,21},{2... | collective-permute-start | bytes 12296 | tf_op jit(solution)/shard_map/ppermute | solution.py:442
  66.5 2.2 %collective-permute-done.9.got_b = f32[8,128]{1,0:T(8,128)S(1)} collective-permute-done((f32[8,128]{1,0:T(8,128)S(1)}, f32[8,128]{1,0:T(8,128)S(1)}, u32[]{:S(2)}, u32[]{:S(2)}) %collective-permute-start.9) | collective-permute-done | bytes 4128 | tf_op jit(solution)/shard_map/ppermute | solution.py:442
  69.5 3.3 %collective-permute-start.11 = (f32[8,128]{1,0:T(8,128)S(1)}, f32[8,128]{1,0:T(8,128)S(1)}, u32[]{:S(2)}, u32[]{:S(2)}) collective-permute-start(f32[8,128]{1,0:T(8,128)S(1)} %get-tuple-element.116), channel_id=1, source_target_pairs={{16,17},{17,16},{1,2},{2,1},{18,19},{19,18},{3,4},{4,3},{20,21},{2... | collective-permute-start | bytes 12296 | tf_op jit(solution)/shard_map/ppermute | solution.py:442
  73.1 2.2 %collective-permute-done.11.got_b = f32[8,128]{1,0:T(8,128)S(1)} collective-permute-done((f32[8,128]{1,0:T(8,128)S(1)}, f32[8,128]{1,0:T(8,128)S(1)}, u32[]{:S(2)}, u32[]{:S(2)}) %collective-permute-start.11) | collective-permute-done | bytes 4128 | tf_op jit(solution)/shard_map/ppermute | solution.py:442
  76.2 3.3 %collective-permute-start.13 = (f32[8,128]{1,0:T(8,128)S(1)}, f32[8,128]{1,0:T(8,128)S(1)}, u32[]{:S(2)}, u32[]{:S(2)}) collective-permute-start(f32[8,128]{1,0:T(8,128)S(1)} %get-tuple-element.123), channel_id=1, source_target_pairs={{16,17},{17,16},{1,2},{2,1},{18,19},{19,18},{3,4},{4,3},{20,21},{2... | collective-permute-start | bytes 12296 | tf_op jit(solution)/shard_map/ppermute | solution.py:442
  79.8 2.2 %collective-permute-done.13.got_b = f32[8,128]{1,0:T(8,128)S(1)} collective-permute-done((f32[8,128]{1,0:T(8,128)S(1)}, f32[8,128]{1,0:T(8,128)S(1)}, u32[]{:S(2)}, u32[]{:S(2)}) %collective-permute-start.13) | collective-permute-done | bytes 4128 | tf_op jit(solution)/shard_map/ppermute | solution.py:442
  82.0 0.7 pair.22
  82.8 3.3 %collective-permute-start.15 = (f32[8,128]{1,0:T(8,128)S(1)}, f32[8,128]{1,0:T(8,128)S(1)}, u32[]{:S(2)}, u32[]{:S(2)}) collective-permute-start(f32[8,128]{1,0:T(8,128)S(1)} %get-tuple-element.126), channel_id=1, source_target_pairs={{16,17},{17,16},{1,2},{2,1},{18,19},{19,18},{3,4},{4,3},{20,21},{2... | collective-permute-start | bytes 12296 | tf_op jit(solution)/shard_map/ppermute | solution.py:442
  86.4 2.2 %collective-permute-done.15.got_b = f32[8,128]{1,0:T(8,128)S(1)} collective-permute-done((f32[8,128]{1,0:T(8,128)S(1)}, f32[8,128]{1,0:T(8,128)S(1)}, u32[]{:S(2)}, u32[]{:S(2)}) %collective-permute-start.15) | collective-permute-done | bytes 4128 | tf_op jit(solution)/shard_map/ppermute | solution.py:442
  89.4 3.3 %collective-permute-start.17 = (f32[8,128]{1,0:T(8,128)S(1)}, f32[8,128]{1,0:T(8,128)S(1)}, u32[]{:S(2)}, u32[]{:S(2)}) collective-permute-start(f32[8,128]{1,0:T(8,128)S(1)} %get-tuple-element.132), channel_id=1, source_target_pairs={{16,17},{17,16},{1,2},{2,1},{18,19},{19,18},{3,4},{4,3},{20,21},{2... | collective-permute-start | bytes 12296 | tf_op jit(solution)/shard_map/ppermute | solution.py:442
  93.0 2.2 %collective-permute-done.17.got_b = f32[8,128]{1,0:T(8,128)S(1)} collective-permute-done((f32[8,128]{1,0:T(8,128)S(1)}, f32[8,128]{1,0:T(8,128)S(1)}, u32[]{:S(2)}, u32[]{:S(2)}) %collective-permute-start.17) | collective-permute-done | bytes 4128 | tf_op jit(solution)/shard_map/ppermute | solution.py:442
  96.0 3.3 %collective-permute-start.19 = (f32[8,128]{1,0:T(8,128)S(1)}, f32[8,128]{1,0:T(8,128)S(1)}, u32[]{:S(2)}, u32[]{:S(2)}) collective-permute-start(f32[8,128]{1,0:T(8,128)S(1)} %get-tuple-element.138), channel_id=1, source_target_pairs={{16,17},{17,16},{1,2},{2,1},{18,19},{19,18},{3,4},{4,3},{20,21},{2... | collective-permute-start | bytes 12296 | tf_op jit(solution)/shard_map/ppermute | solution.py:442
  99.6 2.2 %collective-permute-done.19.got_b = f32[8,128]{1,0:T(8,128)S(1)} collective-permute-done((f32[8,128]{1,0:T(8,128)S(1)}, f32[8,128]{1,0:T(8,128)S(1)}, u32[]{:S(2)}, u32[]{:S(2)}) %collective-permute-start.19) | collective-permute-done | bytes 4128 | tf_op jit(solution)/shard_map/ppermute | solution.py:442
  102.7 3.3 %collective-permute-start.21 = (f32[8,128]{1,0:T(8,128)S(1)}, f32[8,128]{1,0:T(8,128)S(1)}, u32[]{:S(2)}, u32[]{:S(2)}) collective-permute-start(f32[8,128]{1,0:T(8,128)S(1)} %get-tuple-element.145), channel_id=1, source_target_pairs={{16,17},{17,16},{1,2},{2,1},{18,19},{19,18},{3,4},{4,3},{20,21},{2... | collective-permute-start | bytes 12296 | tf_op jit(solution)/shard_map/ppermute | solution.py:442
  106.3 2.2 %collective-permute-done.21.got_b = f32[8,128]{1,0:T(8,128)S(1)} collective-permute-done((f32[8,128]{1,0:T(8,128)S(1)}, f32[8,128]{1,0:T(8,128)S(1)}, u32[]{:S(2)}, u32[]{:S(2)}) %collective-permute-start.21) | collective-permute-done | bytes 4128 | tf_op jit(solution)/shard_map/ppermute | solution.py:442
  108.5 0.7 pair.26
  109.3 3.3 %collective-permute-start.23 = (f32[8,128]{1,0:T(8,128)S(1)}, f32[8,128]{1,0:T(8,128)S(1)}, u32[]{:S(2)}, u32[]{:S(2)}) collective-permute-start(f32[8,128]{1,0:T(8,128)S(1)} %get-tuple-element.148), channel_id=1, source_target_pairs={{16,17},{17,16},{1,2},{2,1},{18,19},{19,18},{3,4},{4,3},{20,21},{2... | collective-permute-start | bytes 12296 | tf_op jit(solution)/shard_map/ppermute | solution.py:442
  112.9 2.2 %collective-permute-done.23.got_b = f32[8,128]{1,0:T(8,128)S(1)} collective-permute-done((f32[8,128]{1,0:T(8,128)S(1)}, f32[8,128]{1,0:T(8,128)S(1)}, u32[]{:S(2)}, u32[]{:S(2)}) %collective-permute-start.23) | collective-permute-done | bytes 4128 | tf_op jit(solution)/shard_map/ppermute | solution.py:442
  115.9 3.3 %collective-permute-start.25 = (f32[8,128]{1,0:T(8,128)S(1)}, f32[8,128]{1,0:T(8,128)S(1)}, u32[]{:S(2)}, u32[]{:S(2)}) collective-permute-start(f32[8,128]{1,0:T(8,128)S(1)} %get-tuple-element.154), channel_id=1, source_target_pairs={{16,17},{17,16},{1,2},{2,1},{18,19},{19,18},{3,4},{4,3},{20,21},{2... | collective-permute-start | bytes 12296 | tf_op jit(solution)/shard_map/ppermute | solution.py:442
  119.5 2.2 %collective-permute-done.25.got_b = f32[8,128]{1,0:T(8,128)S(1)} collective-permute-done((f32[8,128]{1,0:T(8,128)S(1)}, f32[8,128]{1,0:T(8,128)S(1)}, u32[]{:S(2)}, u32[]{:S(2)}) %collective-permute-start.25) | collective-permute-done | bytes 4128 | tf_op jit(solution)/shard_map/ppermute | solution.py:442
  122.6 3.5 %collective-permute-start.27 = (f32[8,128]{1,0:T(8,128)S(1)}, f32[8,128]{1,0:T(8,128)S(1)}, u32[]{:S(2)}, u32[]{:S(2)}) collective-permute-start(f32[8,128]{1,0:T(8,128)S(1)} %get-tuple-element.160), channel_id=1, source_target_pairs={{16,17},{17,16},{1,2},{2,1},{18,19},{19,18},{3,4},{4,3},{20,21},{2... | collective-permute-start | bytes 12296 | tf_op jit(solution)/shard_map/ppermute | solution.py:442
  126.2 2.2 %collective-permute-done.27.got_b = f32[8,128]{1,0:T(8,128)S(1)} collective-permute-done((f32[8,128]{1,0:T(8,128)S(1)}, f32[8,128]{1,0:T(8,128)S(1)}, u32[]{:S(2)}, u32[]{:S(2)}) %collective-permute-start.27) | collective-permute-done | bytes 4128 | tf_op jit(solution)/shard_map/ppermute | solution.py:442
  129.2 3.3 %collective-permute-start.29 = (f32[8,128]{1,0:T(8,128)S(1)}, f32[8,128]{1,0:T(8,128)S(1)}, u32[]{:S(2)}, u32[]{:S(2)}) collective-permute-start(f32[8,128]{1,0:T(8,128)S(1)} %get-tuple-element.167), channel_id=1, source_target_pairs={{16,17},{17,16},{1,2},{2,1},{18,19},{19,18},{3,4},{4,3},{20,21},{2... | collective-permute-start | bytes 12296 | tf_op jit(solution)/shard_map/ppermute | solution.py:442
  132.8 2.2 %collective-permute-done.29.got_b = f32[8,128]{1,0:T(8,128)S(1)} collective-permute-done((f32[8,128]{1,0:T(8,128)S(1)}, f32[8,128]{1,0:T(8,128)S(1)}, u32[]{:S(2)}, u32[]{:S(2)}) %collective-permute-start.29) | collective-permute-done | bytes 4128 | tf_op jit(solution)/shard_map/ppermute | solution.py:442
  135.0 0.7 pair.30
  135.8 3.3 %collective-permute-start.31 = (f32[8,128]{1,0:T(8,128)S(1)}, f32[8,128]{1,0:T(8,128)S(1)}, u32[]{:S(2)}, u32[]{:S(2)}) collective-permute-start(f32[8,128]{1,0:T(8,128)S(1)} %get-tuple-element.170), channel_id=1, source_target_pairs={{16,17},{17,16},{1,2},{2,1},{18,19},{19,18},{3,4},{4,3},{20,21},{2... | collective-permute-start | bytes 12296 | tf_op jit(solution)/shard_map/ppermute | solution.py:442
  139.4 2.2 %collective-permute-done.31.got_b = f32[8,128]{1,0:T(8,128)S(1)} collective-permute-done((f32[8,128]{1,0:T(8,128)S(1)}, f32[8,128]{1,0:T(8,128)S(1)}, u32[]{:S(2)}, u32[]{:S(2)}) %collective-permute-start.31) | collective-permute-done | bytes 4128 | tf_op jit(solution)/shard_map/ppermute | solution.py:442
  142.5 3.3 %collective-permute-start.33 = (f32[8,128]{1,0:T(8,128)S(1)}, f32[8,128]{1,0:T(8,128)S(1)}, u32[]{:S(2)}, u32[]{:S(2)}) collective-permute-start(f32[8,128]{1,0:T(8,128)S(1)} %get-tuple-element.176), channel_id=1, source_target_pairs={{16,17},{17,16},{1,2},{2,1},{18,19},{19,18},{3,4},{4,3},{20,21},{2... | collective-permute-start | bytes 12296 | tf_op jit(solution)/shard_map/ppermute | solution.py:442
  146.1 2.2 %collective-permute-done.33.got_b = f32[8,128]{1,0:T(8,128)S(1)} collective-permute-done((f32[8,128]{1,0:T(8,128)S(1)}, f32[8,128]{1,0:T(8,128)S(1)}, u32[]{:S(2)}, u32[]{:S(2)}) %collective-permute-start.33) | collective-permute-done | bytes 4128 | tf_op jit(solution)/shard_map/ppermute | solution.py:442
  148.3 0.7 pair.32
  149.1 3.3 %collective-permute-start.35 = (f32[8,128]{1,0:T(8,128)S(1)}, f32[8,128]{1,0:T(8,128)S(1)}, u32[]{:S(2)}, u32[]{:S(2)}) collective-permute-start(f32[8,128]{1,0:T(8,128)S(1)} %get-tuple-element.182), channel_id=1, source_target_pairs={{16,17},{17,16},{1,2},{2,1},{18,19},{19,18},{3,4},{4,3},{20,21},{2... | collective-permute-start | bytes 12296 | tf_op jit(solution)/shard_map/ppermute | solution.py:442
  152.7 2.2 %collective-permute-done.35.got_b = f32[8,128]{1,0:T(8,128)S(1)} collective-permute-done((f32[8,128]{1,0:T(8,128)S(1)}, f32[8,128]{1,0:T(8,128)S(1)}, u32[]{:S(2)}, u32[]{:S(2)}) %collective-permute-start.35) | collective-permute-done | bytes 4128 | tf_op jit(solution)/shard_map/ppermute | solution.py:442
  155.5 3.6 %collective-permute-done.36 = f32[4,2,2,128]{3,2,1,0:T(2,128)S(1)} collective-permute-done((f32[4,2,2,128]{3,2,1,0:T(2,128)S(1)}, f32[4,2,2,128]{3,2,1,0:T(2,128)S(1)}, u32[]{:S(2)}, u32[]{:S(2)}) %collective-permute-start.36) | collective-permute-done | bytes 8224 | tf_op jit(solution)/shard_map/ppermute | solution.py:454
  (83 shorter events, 17.2 us)
Async XLA Ops:
  2.6 13.4 %all-to-all-start = ((f32[1,1,16,5,512]{4,1,3,0,2:T(1,128)}), f32[1,1,16,5,512]{4,1,3,0,2:T(1,128)S(1)}, u32[]{:S(2)}, u32[]{:S(2)}) async-start(f32[1,1,16,5,512]{4,1,3,0,2:T(1,128)} %fusion), calls=%async_computation | async-start | bytes 327680 | tf_op jit(solution)/shard_map/all_to_all | solution.py:131
  9.7 1.6 copy-start
  11.3 1.0 copy-start.1
  12.4 4.0 %copy-start.2 = (f32[2,4,128]{2,1,0:T(4,128)S(1)}, f32[2,4,128]{2,1,0:T(4,128)}, u32[]{:S(2)}) copy-start(f32[2,4,128]{2,1,0:T(4,128)} %param.10) | copy-start | bytes 12292
  12.4 4.1 %copy-start.3 = (f32[2,4,128]{2,1,0:T(4,128)S(1)}, f32[2,4,128]{2,1,0:T(4,128)}, u32[]{:S(2)}) copy-start(f32[2,4,128]{2,1,0:T(4,128)} %param.11) | copy-start | bytes 12292
  14.5 34.3 %collective-permute-start = (f32[20,128,128]{2,1,0:T(8,128)}, f32[20,128,128]{2,1,0:T(8,128)S(1)}, u32[]{:S(2)}, u32[]{:S(2)}) collective-permute-start(f32[20,128,128]{2,1,0:T(8,128)} %get-tuple-element.97), channel_id=1, source_target_pairs={{0,16},{16,0},{1,17},{17,1},{2,18},{18,2},{3,19},{19,3},{4,20},{20... | collective-permute-start | bytes 3932168 | tf_op jit(solution)/shard_map/ppermute | solution.py:406
  16.7 31.9 %collective-permute-start.3 = (f32[2,2,768]{2,1,0:T(2,128)S(1)}, f32[2,2,768]{2,1,0:T(2,128)S(1)}, u32[]{:S(2)}, u32[]{:S(2)}) collective-permute-start(f32[2,2,768]{2,1,0:T(2,128)S(1)} %get-tuple-element.188), channel_id=1, source_target_pairs={{0,16},{16,0},{1,17},{17,1},{2,18},{18,2},{3,19},{19,3},{4,20},{20... | collective-permute-start | bytes 36872 | tf_op jit(solution)/shard_map/ppermute | solution.py:416
  17.3 31.4 %collective-permute-start.1 = (f32[2,128,128]{2,1,0:T(8,128)S(1)}, f32[2,128,128]{2,1,0:T(8,128)S(1)}, u32[]{:S(2)}, u32[]{:S(2)}) collective-permute-start(f32[2,128,128]{2,1,0:T(8,128)S(1)} %get-tuple-element.98), channel_id=1, source_target_pairs={{16,17},{17,16},{1,2},{2,1},{18,19},{19,18},{3,4},{4,3},{20,21},{2... | collective-permute-start | bytes 393224 | tf_op jit(solution)/shard_map/ppermute | solution.py:407
  20.3 28.4 %collective-permute-start.2 = (f32[2,128,128]{2,1,0:T(8,128)S(1)}, f32[2,128,128]{2,1,0:T(8,128)S(1)}, u32[]{:S(2)}, u32[]{:S(2)}) collective-permute-start(f32[2,128,128]{2,1,0:T(8,128)S(1)} %get-tuple-element.99), channel_id=1, source_target_pairs={{0,17},{1,16},{17,2},{18,1},{2,19},{3,18},{19,4},{20,3},{4,21},{5,... | collective-permute-start | bytes 393224 | tf_op jit(solution)/shard_map/ppermute | solution.py:408
  49.0 4.0 %collective-permute-start.4 = (f32[8,128]{1,0:T(8,128)S(1)}, f32[8,128]{1,0:T(8,128)S(1)}, u32[]{:S(2)}, u32[]{:S(2)}) collective-permute-start(f32[8,128]{1,0:T(8,128)S(1)} %get-tuple-element.100), channel_id=1, source_target_pairs={{0,16},{16,0},{1,17},{17,1},{2,18},{18,2},{3,19},{19,3},{4,20},{20... | collective-permute-start | bytes 12296 | tf_op jit(solution)/shard_map/ppermute | solution.py:443
  49.7 5.8 %collective-permute-start.5 = (f32[8,128]{1,0:T(8,128)S(1)}, f32[8,128]{1,0:T(8,128)S(1)}, u32[]{:S(2)}, u32[]{:S(2)}) collective-permute-start(f32[8,128]{1,0:T(8,128)S(1)} %get-tuple-element.101), channel_id=1, source_target_pairs={{16,17},{17,16},{1,2},{2,1},{18,19},{19,18},{3,4},{4,3},{20,21},{2... | collective-permute-start | bytes 12296 | tf_op jit(solution)/shard_map/ppermute | solution.py:442
  56.2 3.7 %collective-permute-start.6 = (f32[8,128]{1,0:T(8,128)S(1)}, f32[8,128]{1,0:T(8,128)S(1)}, u32[]{:S(2)}, u32[]{:S(2)}) collective-permute-start(f32[8,128]{1,0:T(8,128)S(1)} %get-tuple-element.103), channel_id=1, source_target_pairs={{0,16},{16,0},{1,17},{17,1},{2,18},{18,2},{3,19},{19,3},{4,20},{20... | collective-permute-start | bytes 12296 | tf_op jit(solution)/shard_map/ppermute | solution.py:443
  56.3 5.8 %collective-permute-start.7 = (f32[8,128]{1,0:T(8,128)S(1)}, f32[8,128]{1,0:T(8,128)S(1)}, u32[]{:S(2)}, u32[]{:S(2)}) collective-permute-start(f32[8,128]{1,0:T(8,128)S(1)} %get-tuple-element.104), channel_id=1, source_target_pairs={{16,17},{17,16},{1,2},{2,1},{18,19},{19,18},{3,4},{4,3},{20,21},{2... | collective-permute-start | bytes 12296 | tf_op jit(solution)/shard_map/ppermute | solution.py:442
  62.8 3.7 %collective-permute-start.8 = (f32[8,128]{1,0:T(8,128)S(1)}, f32[8,128]{1,0:T(8,128)S(1)}, u32[]{:S(2)}, u32[]{:S(2)}) collective-permute-start(f32[8,128]{1,0:T(8,128)S(1)} %get-tuple-element.109), channel_id=1, source_target_pairs={{0,16},{16,0},{1,17},{17,1},{2,18},{18,2},{3,19},{19,3},{4,20},{20... | collective-permute-start | bytes 12296 | tf_op jit(solution)/shard_map/ppermute | solution.py:443
  62.9 5.8 %collective-permute-start.9 = (f32[8,128]{1,0:T(8,128)S(1)}, f32[8,128]{1,0:T(8,128)S(1)}, u32[]{:S(2)}, u32[]{:S(2)}) collective-permute-start(f32[8,128]{1,0:T(8,128)S(1)} %get-tuple-element.110), channel_id=1, source_target_pairs={{16,17},{17,16},{1,2},{2,1},{18,19},{19,18},{3,4},{4,3},{20,21},{2... | collective-permute-start | bytes 12296 | tf_op jit(solution)/shard_map/ppermute | solution.py:442
  69.5 3.7 %collective-permute-start.10 = (f32[8,128]{1,0:T(8,128)S(1)}, f32[8,128]{1,0:T(8,128)S(1)}, u32[]{:S(2)}, u32[]{:S(2)}) collective-permute-start(f32[8,128]{1,0:T(8,128)S(1)} %get-tuple-element.115), channel_id=1, source_target_pairs={{0,16},{16,0},{1,17},{17,1},{2,18},{18,2},{3,19},{19,3},{4,20},{20... | collective-permute-start | bytes 12296 | tf_op jit(solution)/shard_map/ppermute | solution.py:443
  69.5 5.8 %collective-permute-start.11 = (f32[8,128]{1,0:T(8,128)S(1)}, f32[8,128]{1,0:T(8,128)S(1)}, u32[]{:S(2)}, u32[]{:S(2)}) collective-permute-start(f32[8,128]{1,0:T(8,128)S(1)} %get-tuple-element.116), channel_id=1, source_target_pairs={{16,17},{17,16},{1,2},{2,1},{18,19},{19,18},{3,4},{4,3},{20,21},{2... | collective-permute-start | bytes 12296 | tf_op jit(solution)/shard_map/ppermute | solution.py:442
  76.1 3.7 %collective-permute-start.12 = (f32[8,128]{1,0:T(8,128)S(1)}, f32[8,128]{1,0:T(8,128)S(1)}, u32[]{:S(2)}, u32[]{:S(2)}) collective-permute-start(f32[8,128]{1,0:T(8,128)S(1)} %get-tuple-element.122), channel_id=1, source_target_pairs={{0,16},{16,0},{1,17},{17,1},{2,18},{18,2},{3,19},{19,3},{4,20},{20... | collective-permute-start | bytes 12296 | tf_op jit(solution)/shard_map/ppermute | solution.py:443
  76.2 5.8 %collective-permute-start.13 = (f32[8,128]{1,0:T(8,128)S(1)}, f32[8,128]{1,0:T(8,128)S(1)}, u32[]{:S(2)}, u32[]{:S(2)}) collective-permute-start(f32[8,128]{1,0:T(8,128)S(1)} %get-tuple-element.123), channel_id=1, source_target_pairs={{16,17},{17,16},{1,2},{2,1},{18,19},{19,18},{3,4},{4,3},{20,21},{2... | collective-permute-start | bytes 12296 | tf_op jit(solution)/shard_map/ppermute | solution.py:442
  82.7 3.7 %collective-permute-start.14 = (f32[8,128]{1,0:T(8,128)S(1)}, f32[8,128]{1,0:T(8,128)S(1)}, u32[]{:S(2)}, u32[]{:S(2)}) collective-permute-start(f32[8,128]{1,0:T(8,128)S(1)} %get-tuple-element.125), channel_id=1, source_target_pairs={{0,16},{16,0},{1,17},{17,1},{2,18},{18,2},{3,19},{19,3},{4,20},{20... | collective-permute-start | bytes 12296 | tf_op jit(solution)/shard_map/ppermute | solution.py:443
  82.8 5.8 %collective-permute-start.15 = (f32[8,128]{1,0:T(8,128)S(1)}, f32[8,128]{1,0:T(8,128)S(1)}, u32[]{:S(2)}, u32[]{:S(2)}) collective-permute-start(f32[8,128]{1,0:T(8,128)S(1)} %get-tuple-element.126), channel_id=1, source_target_pairs={{16,17},{17,16},{1,2},{2,1},{18,19},{19,18},{3,4},{4,3},{20,21},{2... | collective-permute-start | bytes 12296 | tf_op jit(solution)/shard_map/ppermute | solution.py:442
  89.3 3.7 %collective-permute-start.16 = (f32[8,128]{1,0:T(8,128)S(1)}, f32[8,128]{1,0:T(8,128)S(1)}, u32[]{:S(2)}, u32[]{:S(2)}) collective-permute-start(f32[8,128]{1,0:T(8,128)S(1)} %get-tuple-element.131), channel_id=1, source_target_pairs={{0,16},{16,0},{1,17},{17,1},{2,18},{18,2},{3,19},{19,3},{4,20},{20... | collective-permute-start | bytes 12296 | tf_op jit(solution)/shard_map/ppermute | solution.py:443
  89.4 5.8 %collective-permute-start.17 = (f32[8,128]{1,0:T(8,128)S(1)}, f32[8,128]{1,0:T(8,128)S(1)}, u32[]{:S(2)}, u32[]{:S(2)}) collective-permute-start(f32[8,128]{1,0:T(8,128)S(1)} %get-tuple-element.132), channel_id=1, source_target_pairs={{16,17},{17,16},{1,2},{2,1},{18,19},{19,18},{3,4},{4,3},{20,21},{2... | collective-permute-start | bytes 12296 | tf_op jit(solution)/shard_map/ppermute | solution.py:442
  96.0 3.7 %collective-permute-start.18 = (f32[8,128]{1,0:T(8,128)S(1)}, f32[8,128]{1,0:T(8,128)S(1)}, u32[]{:S(2)}, u32[]{:S(2)}) collective-permute-start(f32[8,128]{1,0:T(8,128)S(1)} %get-tuple-element.137), channel_id=1, source_target_pairs={{0,16},{16,0},{1,17},{17,1},{2,18},{18,2},{3,19},{19,3},{4,20},{20... | collective-permute-start | bytes 12296 | tf_op jit(solution)/shard_map/ppermute | solution.py:443
  96.0 5.8 %collective-permute-start.19 = (f32[8,128]{1,0:T(8,128)S(1)}, f32[8,128]{1,0:T(8,128)S(1)}, u32[]{:S(2)}, u32[]{:S(2)}) collective-permute-start(f32[8,128]{1,0:T(8,128)S(1)} %get-tuple-element.138), channel_id=1, source_target_pairs={{16,17},{17,16},{1,2},{2,1},{18,19},{19,18},{3,4},{4,3},{20,21},{2... | collective-permute-start | bytes 12296 | tf_op jit(solution)/shard_map/ppermute | solution.py:442
  102.6 3.7 %collective-permute-start.20 = (f32[8,128]{1,0:T(8,128)S(1)}, f32[8,128]{1,0:T(8,128)S(1)}, u32[]{:S(2)}, u32[]{:S(2)}) collective-permute-start(f32[8,128]{1,0:T(8,128)S(1)} %get-tuple-element.144), channel_id=1, source_target_pairs={{0,16},{16,0},{1,17},{17,1},{2,18},{18,2},{3,19},{19,3},{4,20},{20... | collective-permute-start | bytes 12296 | tf_op jit(solution)/shard_map/ppermute | solution.py:443
  102.7 5.8 %collective-permute-start.21 = (f32[8,128]{1,0:T(8,128)S(1)}, f32[8,128]{1,0:T(8,128)S(1)}, u32[]{:S(2)}, u32[]{:S(2)}) collective-permute-start(f32[8,128]{1,0:T(8,128)S(1)} %get-tuple-element.145), channel_id=1, source_target_pairs={{16,17},{17,16},{1,2},{2,1},{18,19},{19,18},{3,4},{4,3},{20,21},{2... | collective-permute-start | bytes 12296 | tf_op jit(solution)/shard_map/ppermute | solution.py:442
  109.2 3.7 %collective-permute-start.22 = (f32[8,128]{1,0:T(8,128)S(1)}, f32[8,128]{1,0:T(8,128)S(1)}, u32[]{:S(2)}, u32[]{:S(2)}) collective-permute-start(f32[8,128]{1,0:T(8,128)S(1)} %get-tuple-element.147), channel_id=1, source_target_pairs={{0,16},{16,0},{1,17},{17,1},{2,18},{18,2},{3,19},{19,3},{4,20},{20... | collective-permute-start | bytes 12296 | tf_op jit(solution)/shard_map/ppermute | solution.py:443
  109.3 5.8 %collective-permute-start.23 = (f32[8,128]{1,0:T(8,128)S(1)}, f32[8,128]{1,0:T(8,128)S(1)}, u32[]{:S(2)}, u32[]{:S(2)}) collective-permute-start(f32[8,128]{1,0:T(8,128)S(1)} %get-tuple-element.148), channel_id=1, source_target_pairs={{16,17},{17,16},{1,2},{2,1},{18,19},{19,18},{3,4},{4,3},{20,21},{2... | collective-permute-start | bytes 12296 | tf_op jit(solution)/shard_map/ppermute | solution.py:442
  115.9 3.7 %collective-permute-start.24 = (f32[8,128]{1,0:T(8,128)S(1)}, f32[8,128]{1,0:T(8,128)S(1)}, u32[]{:S(2)}, u32[]{:S(2)}) collective-permute-start(f32[8,128]{1,0:T(8,128)S(1)} %get-tuple-element.153), channel_id=1, source_target_pairs={{0,16},{16,0},{1,17},{17,1},{2,18},{18,2},{3,19},{19,3},{4,20},{20... | collective-permute-start | bytes 12296 | tf_op jit(solution)/shard_map/ppermute | solution.py:443
  115.9 5.8 %collective-permute-start.25 = (f32[8,128]{1,0:T(8,128)S(1)}, f32[8,128]{1,0:T(8,128)S(1)}, u32[]{:S(2)}, u32[]{:S(2)}) collective-permute-start(f32[8,128]{1,0:T(8,128)S(1)} %get-tuple-element.154), channel_id=1, source_target_pairs={{16,17},{17,16},{1,2},{2,1},{18,19},{19,18},{3,4},{4,3},{20,21},{2... | collective-permute-start | bytes 12296 | tf_op jit(solution)/shard_map/ppermute | solution.py:442
  122.5 3.7 %collective-permute-start.26 = (f32[8,128]{1,0:T(8,128)S(1)}, f32[8,128]{1,0:T(8,128)S(1)}, u32[]{:S(2)}, u32[]{:S(2)}) collective-permute-start(f32[8,128]{1,0:T(8,128)S(1)} %get-tuple-element.159), channel_id=1, source_target_pairs={{0,16},{16,0},{1,17},{17,1},{2,18},{18,2},{3,19},{19,3},{4,20},{20... | collective-permute-start | bytes 12296 | tf_op jit(solution)/shard_map/ppermute | solution.py:443
  122.6 5.8 %collective-permute-start.27 = (f32[8,128]{1,0:T(8,128)S(1)}, f32[8,128]{1,0:T(8,128)S(1)}, u32[]{:S(2)}, u32[]{:S(2)}) collective-permute-start(f32[8,128]{1,0:T(8,128)S(1)} %get-tuple-element.160), channel_id=1, source_target_pairs={{16,17},{17,16},{1,2},{2,1},{18,19},{19,18},{3,4},{4,3},{20,21},{2... | collective-permute-start | bytes 12296 | tf_op jit(solution)/shard_map/ppermute | solution.py:442
  129.1 3.7 %collective-permute-start.28 = (f32[8,128]{1,0:T(8,128)S(1)}, f32[8,128]{1,0:T(8,128)S(1)}, u32[]{:S(2)}, u32[]{:S(2)}) collective-permute-start(f32[8,128]{1,0:T(8,128)S(1)} %get-tuple-element.166), channel_id=1, source_target_pairs={{0,16},{16,0},{1,17},{17,1},{2,18},{18,2},{3,19},{19,3},{4,20},{20... | collective-permute-start | bytes 12296 | tf_op jit(solution)/shard_map/ppermute | solution.py:443
  129.2 5.8 %collective-permute-start.29 = (f32[8,128]{1,0:T(8,128)S(1)}, f32[8,128]{1,0:T(8,128)S(1)}, u32[]{:S(2)}, u32[]{:S(2)}) collective-permute-start(f32[8,128]{1,0:T(8,128)S(1)} %get-tuple-element.167), channel_id=1, source_target_pairs={{16,17},{17,16},{1,2},{2,1},{18,19},{19,18},{3,4},{4,3},{20,21},{2... | collective-permute-start | bytes 12296 | tf_op jit(solution)/shard_map/ppermute | solution.py:442
  135.8 3.7 %collective-permute-start.30 = (f32[8,128]{1,0:T(8,128)S(1)}, f32[8,128]{1,0:T(8,128)S(1)}, u32[]{:S(2)}, u32[]{:S(2)}) collective-permute-start(f32[8,128]{1,0:T(8,128)S(1)} %get-tuple-element.169), channel_id=1, source_target_pairs={{0,16},{16,0},{1,17},{17,1},{2,18},{18,2},{3,19},{19,3},{4,20},{20... | collective-permute-start | bytes 12296 | tf_op jit(solution)/shard_map/ppermute | solution.py:443
  135.8 5.8 %collective-permute-start.31 = (f32[8,128]{1,0:T(8,128)S(1)}, f32[8,128]{1,0:T(8,128)S(1)}, u32[]{:S(2)}, u32[]{:S(2)}) collective-permute-start(f32[8,128]{1,0:T(8,128)S(1)} %get-tuple-element.170), channel_id=1, source_target_pairs={{16,17},{17,16},{1,2},{2,1},{18,19},{19,18},{3,4},{4,3},{20,21},{2... | collective-permute-start | bytes 12296 | tf_op jit(solution)/shard_map/ppermute | solution.py:442
  142.4 3.7 %collective-permute-start.32 = (f32[8,128]{1,0:T(8,128)S(1)}, f32[8,128]{1,0:T(8,128)S(1)}, u32[]{:S(2)}, u32[]{:S(2)}) collective-permute-start(f32[8,128]{1,0:T(8,128)S(1)} %get-tuple-element.175), channel_id=1, source_target_pairs={{0,16},{16,0},{1,17},{17,1},{2,18},{18,2},{3,19},{19,3},{4,20},{20... | collective-permute-start | bytes 12296 | tf_op jit(solution)/shard_map/ppermute | solution.py:443
  142.5 5.8 %collective-permute-start.33 = (f32[8,128]{1,0:T(8,128)S(1)}, f32[8,128]{1,0:T(8,128)S(1)}, u32[]{:S(2)}, u32[]{:S(2)}) collective-permute-start(f32[8,128]{1,0:T(8,128)S(1)} %get-tuple-element.176), channel_id=1, source_target_pairs={{16,17},{17,16},{1,2},{2,1},{18,19},{19,18},{3,4},{4,3},{20,21},{2... | collective-permute-start | bytes 12296 | tf_op jit(solution)/shard_map/ppermute | solution.py:442
  149.0 3.7 %collective-permute-start.34 = (f32[8,128]{1,0:T(8,128)S(1)}, f32[8,128]{1,0:T(8,128)S(1)}, u32[]{:S(2)}, u32[]{:S(2)}) collective-permute-start(f32[8,128]{1,0:T(8,128)S(1)} %get-tuple-element.181), channel_id=1, source_target_pairs={{0,16},{16,0},{1,17},{17,1},{2,18},{18,2},{3,19},{19,3},{4,20},{20... | collective-permute-start | bytes 12296 | tf_op jit(solution)/shard_map/ppermute | solution.py:443
  149.1 5.8 %collective-permute-start.35 = (f32[8,128]{1,0:T(8,128)S(1)}, f32[8,128]{1,0:T(8,128)S(1)}, u32[]{:S(2)}, u32[]{:S(2)}) collective-permute-start(f32[8,128]{1,0:T(8,128)S(1)} %get-tuple-element.182), channel_id=1, source_target_pairs={{16,17},{17,16},{1,2},{2,1},{18,19},{19,18},{3,4},{4,3},{20,21},{2... | collective-permute-start | bytes 12296 | tf_op jit(solution)/shard_map/ppermute | solution.py:442
  155.5 3.7 %collective-permute-start.36 = (f32[4,2,2,128]{3,2,1,0:T(2,128)S(1)}, f32[4,2,2,128]{3,2,1,0:T(2,128)S(1)}, u32[]{:S(2)}, u32[]{:S(2)}) collective-permute-start(f32[4,2,2,128]{3,2,1,0:T(2,128)S(1)} %rev.24), channel_id=1, source_target_pairs={{0,16},{16,0},{1,17},{17,1},{2,18},{18,2},{3,19},{19,3},{4,20},{20... | collective-permute-start | bytes 24584 | tf_op jit(solution)/shard_map/ppermute | solution.py:454

commit v7 on v6

--- a/solution.py
+++ b/solution.py
@@ -192,6 +192,7 @@
 OWN, SIDE_A, SIDE_B, OUT_IN, IN_OUT, IN_IN, FACING, PACKED = 0, 4, 8, 12, 14, 16, 18, 20
 TILES = [(j, b) for j in range(N) for b in range(HALF)]
 ORIGIN = [(0, 0), (0, 1), (1, 1), (1, 0)]
+CAPACITY, INITIAL = STEPS, STEPS + 1
 
 
 def unit_device(unit, n_col):
@@ -210,7 +211,7 @@
     cols = own_ref.shape[1]
 
     def coupling(direction, row, at_col):
-        weight = pattern_ref[(row * cols + at_col) * 4 + direction].astype(jnp.float32)
+        weight = pattern_ref[row, at_col, direction].astype(jnp.float32)
         return nb_ref[direction, row, at_col] * weight
 
     halves = []
@@ -306,19 +307,27 @@
     return residue - STRIDES[sweep] * (q + capacity * f) + MOMENTA[sweep + 1] * f
 
 
-def start_kernel(half_0, half_1, beyond_0, beyond_1, field, injected, msg_a, msg_b, q_out):
-    f = field[...]
+def small_part(small, index):
+    n = N * HALF
+    return small[index * n:(index + 1) * n, :]
+
+
+def start_kernel(half_0, half_1, small, msg_a, msg_b, q_out):
+    f = small_part(small, INITIAL)
     q = inner_product(f, (half_0, half_1))
     q_out[...] = q
-    msg_a[...], msg_b[...] = messages(f, ahead(True, 0, f, q, None, None, injected[...]))
-
-
-def pair_kernel(pair, last, half_0, half_1, beyond_0, beyond_1, capacity_ref, injected_ref, got_a, got_b, f_ref, q_ref,
-                *refs):
+    msg_a[...], msg_b[...] = messages(f, ahead(True, 0, f, q, None, None, small_part(small, 0)))
+
+
+def pair_kernel(instant, pair, last, half_0, half_1, beyond_0, beyond_1, small, got_a, got_b, q_ref, *refs):
     halves, beyond = (half_0, half_1), (beyond_0, beyond_1)
     first = pair == 0
-    capacity = capacity_ref[...]
-    f, q = f_ref[...], q_ref[...]
+    capacity = small_part(small, CAPACITY)
+    q = q_ref[...]
+    if first and instant == 0:
+        f = small_part(small, INITIAL)
+    else:
+        f, refs = refs[0][...], refs[1:]
     if not first:
         residue, estimate, refs = refs[0][...], refs[1][...], refs[2:]
     got = (got_b, got_a)
@@ -330,7 +339,7 @@
         extra.append(matvec([(r, i, got[b][j:j + 1, :])]))
     product = q + jnp.concatenate(extra, axis=0)
     if first:
-        residue = injected_ref[...] - product
+        residue = small_part(small, instant) - product
         f2 = residue
         estimate = f + STRIDES[0] * f2
         scale = 1.0
@@ -364,7 +373,8 @@
     q = inner_product(f3, halves)
     q_out, msg_a, msg_b = refs[:3]
     q_out[...] = q
-    msg_a[...], msg_b[...] = messages(f3, ahead(closing, sweep + 1, f3, q, residue, capacity, injected_ref[...]))
+    upcoming = small_part(small, instant + 1) if closing else None
+    msg_a[...], msg_b[...] = messages(f3, ahead(closing, sweep + 1, f3, q, residue, capacity, upcoming))
     if not closing:
         refs[3][...] = residue
         refs[4][...] = estimate
@@ -402,21 +412,32 @@
         ],
         compiler_params=pltpu.CompilerParams(vmem_limit_bytes=48 * 2**20),
         name="pack",
-    )(jnp.stack([row, col]).astype(jnp.int32), pattern.reshape(-1), own_block, neighbor_block)
+    )(jnp.stack([row, col]).astype(jnp.int32), pattern,
+      pltpu.with_memory_space_constraint(own_block, pltpu.HBM),
+      pltpu.with_memory_space_constraint(neighbor_block, pltpu.HBM))
     half_1 = lax.ppermute(send, "row", swap)
-    beyond_0 = lax.ppermute(facing_0, both, b_pairs)
-    beyond_1 = lax.ppermute(facing_1, both, b_cross)
-
-    injected = collect(currents, slot_tile, tile_rows * tile_cols, width)
-    small = jnp.concatenate(
-        [injected.reshape(tile_rows, tile_cols, STEPS * width), capacity, initial], axis=2
+
+    def beside(currents, slot_tile, capacity, initial, facing_0, facing_1):
+        beyond_0 = lax.ppermute(facing_0, both, b_pairs)
+        beyond_1 = lax.ppermute(facing_1, both, b_cross)
+        injected = collect(currents, slot_tile, tile_rows * tile_cols, width)
+        small = jnp.concatenate(
+            [jnp.moveaxis(injected, 1, 0).reshape(STEPS, tile_rows, tile_cols, width), capacity[None], initial[None]]
+        )
+        small = jnp.where(row == 1, jnp.flip(small, 1), small)
+        unit_0, unit_1 = small[:, :, :HALF], jnp.flip(small, 2)[:, :, :HALF]
+        got = lax.ppermute(jnp.where(parity == 1, unit_0, unit_1), "row", swap)
+        small = jnp.concatenate([jnp.where(parity == 1, unit_1, unit_0), jnp.flip(got, 1)], axis=1)
+        return small.reshape((STEPS + 2) * N * HALF, width), beyond_0, beyond_1
+
+    small, beyond_0, beyond_1 = lax.cond(
+        row < lax.axis_size("row"),
+        beside,
+        lambda currents, slot_tile, capacity, initial, *blocks: (
+            jnp.zeros(((STEPS + 2) * N * HALF, width), jnp.float32), *blocks
+        ),
+        currents, slot_tile, capacity, initial, facing_0, facing_1,
     )
-    small = jnp.where(row == 1, jnp.flip(small, 0), small)
-    unit_0, unit_1 = small[:, :HALF], jnp.flip(small, 1)[:, :HALF]
-    got = lax.ppermute(jnp.where(parity == 1, unit_0, unit_1), "row", swap)
-    small = jnp.concatenate([jnp.where(parity == 1, unit_1, unit_0), jnp.flip(got, 0)], axis=0)
-    small = small.reshape(N * HALF, STEPS + 2, width)
-    injected, cap, field = small[:, :STEPS], small[:, STEPS], small[:, STEPS + 1]
 
     shape = jax.ShapeDtypeStruct((N * HALF, width), jnp.float32)
 
@@ -432,23 +453,21 @@
             name="pair",
         )(*ins)
 
-    msg_a, msg_b, q = call(start_kernel, 3, 28, half_0, half_1, beyond_0, beyond_1, field, injected[:, 0])
+    msg_a, msg_b, q = call(start_kernel, 3, 28, half_0, half_1, small)
     frames = []
+    state = ()
     for instant in range(STEPS):
-        state = ()
         for pair in range(ITERS // 2):
             closing = pair + 1 == ITERS // 2
             last = closing and instant + 1 == STEPS
             got_b = lax.ppermute(msg_b, both, b_pairs)
             got_a = lax.ppermute(msg_a, "row", swap)
-            feed = injected[:, min(instant + closing, STEPS - 1)]
-            out = call(functools.partial(pair_kernel, pair, last), 1 if last else 4 if closing else 6, 80,
-                       half_0, half_1, beyond_0, beyond_1, cap, feed, got_a, got_b, field, q, *state)
-            field = out[0]
+            out = call(functools.partial(pair_kernel, instant, pair, last), 1 if last else 4 if closing else 6, 80,
+                       half_0, half_1, beyond_0, beyond_1, small, got_a, got_b, q, *state)
             if not last:
                 q, msg_a, msg_b = out[1:4]
-                state = tuple(out[4:])
-        frames.append(field)
+                state = (out[0], *out[4:])
+        frames.append(out[0])
 
     done = jnp.stack(frames).reshape(STEPS, N, HALF, width)
     got = lax.ppermute(jnp.flip(done[:, ROWS:], 1), "row", swap)

time: 161 us -> 151 us (0.938)
  starting transfers between devices: 68.8 us -> 55.4 us
  waiting for transfers between devices: 69.5 us -> 76.5 us
  local copies, waits for them, and re-layouts: 4.95 us -> 1.12 us
    ppermute x16, starting transfers between devices: 53.1 us -> 37.5 us  [shards_chain(): got_b = lax.ppermute(msg_b, both, b_pairs)]
    ppermute x16, waiting for transfers between devices: 3.95 us -> 18.6 us  [shards_chain(): got_a = lax.ppermute(msg_a, 'row', swap)]
    ppermute x3, waiting for transfers between devices: 25.9 us -> 16.5 us  [the longest x1 15.4 us: beside(): beyond_1 = lax.ppermute(facing_1, both, b_cross)]
    unnamed x12 -> x10, local copies, waits for them, and re-layouts: 3.78 us -> 0.7 us
  transfers between devices with their start and end apart: 38 -> 38, of which waited for: 33 -> 35; matrix products, arithmetic and copies ran while one was open for 1% -> 1% of each run, Pallas kernels for 1% -> 0%
where the time goes in v7:
time: 151 us; the launch traced here: 150 us
  waiting for transfers between devices  76.5 us (51%)
  starting transfers between devices  55.4 us (37%)
  Pallas kernels  15 us (10%)
  other arithmetic  1.56 us (1%)
    ppermute x16, starting transfers between devices, shards_chain(): got_b = lax.ppermute(msg_b, both, b_pairs)  37.5 us
    ppermute x16, waiting for transfers between devices, shards_chain(): got_b = lax.ppermute(msg_b, both, b_pairs)  37.1 us
    ppermute x16, waiting for transfers between devices, shards_chain(): got_a = lax.ppermute(msg_a, 'row', swap)  18.6 us
    ppermute x1, waiting for transfers between devices, beside(): beyond_1 = lax.ppermute(facing_1, both, b_cross)  15.4 us
    pallas_call x17, Pallas kernels, call(): pl.pallas_call(body, out_shape=(shape,) * n_out, in_specs=[vmem] * len(in...  11.5 us
    all_to_all x1, starting transfers between devices, collect(): lax.all_to_all(packed, 'col', split_axis=2, concat_axis=1, tiled=True)  6.27 us
    ppermute x1, waiting for transfers between devices, shards_chain(): got = lax.ppermute(jnp.flip(done[:, ROWS:], 1), 'row', swap)  3.63 us
    pallas_call x1, Pallas kernels, shards_chain(): pl.pallas_call(functools.partial(pack_kernel, n_col), out_shape=(packed,...  3.47 us
  transfers between devices with their start and end apart: 38, of which 35 were waited for; matrix products, arithmetic and copies ran while one was open for 1% of the time, Pallas kernels for 0%

profile of v7, /device:TPU:8, one launch (start us, length us, event | category | flops | bytes accessed | tf_op | source)
XLA Modules:
  0.0 150.3 jit_solution(5713716149378564396)
XLA Ops:
  0.8 3.5 %pack.1 = (f32[20,128,128]{2,1,0:T(8,128)S(1)}, f32[20,128,128]{2,1,0:T(8,128)}, f32[2,128,128]{2,1,0:T(8,128)S(1)}, f32[2,128,128]{2,1,0:T(8,128)S(1)}) custom-call(s32[2]{0:T(128)S(1)} %pad_add_fusion.place_ref, s32[2,4,4]{2,1,0:T(4,128)S(1)} %copy-done, f32[2,4,128,128]{3,2,1,0:T(8,128)} %own_hbm.1, f32[4,2,4,128,128]{4,3,2,1,0:T(8,128)} %nb_hbm.1), custom_call_target="tpu_custom_call" | custom-call | tf_op jit(solution)/shard_map/pack/pallas_call | solution.py:403
  4.3 1.6 %collective-permute-start.3 = (f32[20,128,128]{2,1,0:T(8,128)}, f32[20,128,128]{2,1,0:T(8,128)S(1)}, u32[]{:S(2)}, u32[]{:S(2)}) collective-permute-start(f32[20,128,128]{2,1,0:T(8,128)} %get-tuple-element.130), channel_id=1, source_target_pairs={{0,16},{16,0},{1,17},{17,1},{2,18},{18,2},{3,19},{19,3},{4,20},{20... | collective-permute-start | bytes 3932168 | tf_op jit(solution)/shard_map/ppermute | solution.py:418
  5.9 32.3 %conditional.1 = (f32[48,128]{1,0:T(8,128)S(1)}, f32[2,128,128]{2,1,0:T(8,128)S(1)}, f32[2,128,128]{2,1,0:T(8,128)S(1)}) conditional(s32[]{:T(128)} %convert_element_type.9, (f32[2,128,128]{2,1,0:T(8,128)S(1)}, f32[2,128,128]{2,1,0:T(8,128)S(1)}) %tuple.13, (s32[]{:T(128)}, s32[]{:T(128)}, s32[1,1,16,4]{2,3,1,0:T(4,128)S(1)}, ...), branch_computations={%region_0.1_spmd, %region_1.2_spmd} | conditional | flops 3299906 | bytes 3420612 | solution.py:433
  6.9 6.3 %all-to-all-start = ((f32[1,1,16,5,512]{4,1,3,0,2:T(1,128)}), f32[1,1,16,5,512]{4,1,3,0,2:T(1,128)S(1)}, u32[]{:S(2)}, u32[]{:S(2)}) async-start(f32[1,1,16,5,512]{4,1,3,0,2:T(1,128)} %fusion), calls=%async_computation | async-start | bytes 327680 | tf_op jit(solution)/shard_map/cond/branch_1_fun/all_to_all | solution.py:131
  13.2 3.1 %collective-permute-start.1 = (f32[2,128,128]{2,1,0:T(8,128)S(1)}, f32[2,128,128]{2,1,0:T(8,128)S(1)}, u32[]{:S(2)}, u32[]{:S(2)}) collective-permute-start(f32[2,128,128]{2,1,0:T(8,128)S(1)} %get-tuple-element.33), channel_id=1, source_target_pairs={{16,17},{17,16},{1,2},{2,1},{18,19},{19,18},{3,4},{4,3},{20,21},{2... | collective-permute-start | bytes 393224 | tf_op jit(solution)/shard_map/cond/branch_1_fun/ppermute | solution.py:421
  16.3 1.9 %collective-permute-start.2 = (f32[2,128,128]{2,1,0:T(8,128)S(1)}, f32[2,128,128]{2,1,0:T(8,128)S(1)}, u32[]{:S(2)}, u32[]{:S(2)}) collective-permute-start(f32[2,128,128]{2,1,0:T(8,128)S(1)} %get-tuple-element.34), channel_id=1, source_target_pairs={{0,17},{1,16},{17,2},{18,1},{2,19},{3,18},{19,4},{20,3},{4,21},{5,... | collective-permute-start | bytes 393224 | tf_op jit(solution)/shard_map/cond/branch_1_fun/ppermute | solution.py:422
  19.3 2.3 %collective-permute-start = (f32[6,2,2,128]{3,2,1,0:T(2,128)S(1)}, f32[6,2,2,128]{3,2,1,0:T(2,128)S(1)}, u32[]{:S(2)}, u32[]{:S(2)}) collective-permute-start(f32[6,2,2,128]{3,2,1,0:T(2,128)S(1)} %get-tuple-element.256), channel_id=1, source_target_pairs={{0,16},{16,0},{1,17},{17,1},{2,18},{18,2},{3,19},{19,3},{4,20},{20... | collective-permute-start | bytes 36872 | tf_op jit(solution)/shard_map/cond/branch_1_fun/ppermute | solution.py:429
  21.6 15.4 %collective-permute-done.2 = f32[2,128,128]{2,1,0:T(8,128)S(1)} collective-permute-done((f32[2,128,128]{2,1,0:T(8,128)S(1)}, f32[2,128,128]{2,1,0:T(8,128)S(1)}, u32[]{:S(2)}, u32[]{:S(2)}) %collective-permute-start.2) | collective-permute-done | bytes 131104 | tf_op jit(solution)/shard_map/cond/branch_1_fun/ppermute | solution.py:422
  38.4 1.6 %collective-permute-start.4 = (f32[8,128]{1,0:T(8,128)S(1)}, f32[8,128]{1,0:T(8,128)S(1)}, u32[]{:S(2)}, u32[]{:S(2)}) collective-permute-start(f32[8,128]{1,0:T(8,128)S(1)} %get-tuple-element.136), channel_id=1, source_target_pairs={{0,16},{16,0},{1,17},{17,1},{2,18},{18,2},{3,19},{19,3},{4,20},{20... | collective-permute-start | bytes 12296 | tf_op jit(solution)/shard_map/ppermute | solution.py:464
  40.0 2.3 %collective-permute-start.5 = (f32[8,128]{1,0:T(8,128)S(1)}, f32[8,128]{1,0:T(8,128)S(1)}, u32[]{:S(2)}, u32[]{:S(2)}) collective-permute-start(f32[8,128]{1,0:T(8,128)S(1)} %get-tuple-element.137), channel_id=1, source_target_pairs={{16,17},{17,16},{1,2},{2,1},{18,19},{19,18},{3,4},{4,3},{20,21},{2... | collective-permute-start | bytes 12296 | tf_op jit(solution)/shard_map/ppermute | solution.py:463
  42.3 3.5 %collective-permute-done.5.got_b = f32[8,128]{1,0:T(8,128)S(1)} collective-permute-done((f32[8,128]{1,0:T(8,128)S(1)}, f32[8,128]{1,0:T(8,128)S(1)}, u32[]{:S(2)}, u32[]{:S(2)}) %collective-permute-start.5) | collective-permute-done | bytes 4128 | tf_op jit(solution)/shard_map/ppermute | solution.py:463
  46.6 2.3 %collective-permute-start.7 = (f32[8,128]{1,0:T(8,128)S(1)}, f32[8,128]{1,0:T(8,128)S(1)}, u32[]{:S(2)}, u32[]{:S(2)}) collective-permute-start(f32[8,128]{1,0:T(8,128)S(1)} %get-tuple-element.140), channel_id=1, source_target_pairs={{16,17},{17,16},{1,2},{2,1},{18,19},{19,18},{3,4},{4,3},{20,21},{2... | collective-permute-start | bytes 12296 | tf_op jit(solution)/shard_map/ppermute | solution.py:463
  48.9 1.2 collective-permute-done.6.got_a
  50.2 2.2 %collective-permute-done.7.got_b = f32[8,128]{1,0:T(8,128)S(1)} collective-permute-done((f32[8,128]{1,0:T(8,128)S(1)}, f32[8,128]{1,0:T(8,128)S(1)}, u32[]{:S(2)}, u32[]{:S(2)}) %collective-permute-start.7) | collective-permute-done | bytes 4128 | tf_op jit(solution)/shard_map/ppermute | solution.py:463
  53.2 2.3 %collective-permute-start.9 = (f32[8,128]{1,0:T(8,128)S(1)}, f32[8,128]{1,0:T(8,128)S(1)}, u32[]{:S(2)}, u32[]{:S(2)}) collective-permute-start(f32[8,128]{1,0:T(8,128)S(1)} %get-tuple-element.146), channel_id=1, source_target_pairs={{16,17},{17,16},{1,2},{2,1},{18,19},{19,18},{3,4},{4,3},{20,21},{2... | collective-permute-start | bytes 12296 | tf_op jit(solution)/shard_map/ppermute | solution.py:463
  55.6 1.2 collective-permute-done.8.got_a
  56.8 2.2 %collective-permute-done.9.got_b = f32[8,128]{1,0:T(8,128)S(1)} collective-permute-done((f32[8,128]{1,0:T(8,128)S(1)}, f32[8,128]{1,0:T(8,128)S(1)}, u32[]{:S(2)}, u32[]{:S(2)}) %collective-permute-start.9) | collective-permute-done | bytes 4128 | tf_op jit(solution)/shard_map/ppermute | solution.py:463
  59.8 2.3 %collective-permute-start.11 = (f32[8,128]{1,0:T(8,128)S(1)}, f32[8,128]{1,0:T(8,128)S(1)}, u32[]{:S(2)}, u32[]{:S(2)}) collective-permute-start(f32[8,128]{1,0:T(8,128)S(1)} %get-tuple-element.152), channel_id=1, source_target_pairs={{16,17},{17,16},{1,2},{2,1},{18,19},{19,18},{3,4},{4,3},{20,21},{2... | collective-permute-start | bytes 12296 | tf_op jit(solution)/shard_map/ppermute | solution.py:463
  62.2 1.2 collective-permute-done.10.got_a
  63.4 2.2 %collective-permute-done.11.got_b = f32[8,128]{1,0:T(8,128)S(1)} collective-permute-done((f32[8,128]{1,0:T(8,128)S(1)}, f32[8,128]{1,0:T(8,128)S(1)}, u32[]{:S(2)}, u32[]{:S(2)}) %collective-permute-start.11) | collective-permute-done | bytes 4128 | tf_op jit(solution)/shard_map/ppermute | solution.py:463
  66.5 2.3 %collective-permute-start.13 = (f32[8,128]{1,0:T(8,128)S(1)}, f32[8,128]{1,0:T(8,128)S(1)}, u32[]{:S(2)}, u32[]{:S(2)}) collective-permute-start(f32[8,128]{1,0:T(8,128)S(1)} %get-tuple-element.159), channel_id=1, source_target_pairs={{16,17},{17,16},{1,2},{2,1},{18,19},{19,18},{3,4},{4,3},{20,21},{2... | collective-permute-start | bytes 12296 | tf_op jit(solution)/shard_map/ppermute | solution.py:463
  70.1 2.2 %collective-permute-done.13.got_b = f32[8,128]{1,0:T(8,128)S(1)} collective-permute-done((f32[8,128]{1,0:T(8,128)S(1)}, f32[8,128]{1,0:T(8,128)S(1)}, u32[]{:S(2)}, u32[]{:S(2)}) %collective-permute-start.13) | collective-permute-done | bytes 4128 | tf_op jit(solution)/shard_map/ppermute | solution.py:463
  73.1 2.3 %collective-permute-start.15 = (f32[8,128]{1,0:T(8,128)S(1)}, f32[8,128]{1,0:T(8,128)S(1)}, u32[]{:S(2)}, u32[]{:S(2)}) collective-permute-start(f32[8,128]{1,0:T(8,128)S(1)} %get-tuple-element.162), channel_id=1, source_target_pairs={{16,17},{17,16},{1,2},{2,1},{18,19},{19,18},{3,4},{4,3},{20,21},{2... | collective-permute-start | bytes 12296 | tf_op jit(solution)/shard_map/ppermute | solution.py:463
  75.4 1.2 collective-permute-done.14.got_a
  76.7 2.2 %collective-permute-done.15.got_b = f32[8,128]{1,0:T(8,128)S(1)} collective-permute-done((f32[8,128]{1,0:T(8,128)S(1)}, f32[8,128]{1,0:T(8,128)S(1)}, u32[]{:S(2)}, u32[]{:S(2)}) %collective-permute-start.15) | collective-permute-done | bytes 4128 | tf_op jit(solution)/shard_map/ppermute | solution.py:463
  79.7 2.3 %collective-permute-start.17 = (f32[8,128]{1,0:T(8,128)S(1)}, f32[8,128]{1,0:T(8,128)S(1)}, u32[]{:S(2)}, u32[]{:S(2)}) collective-permute-start(f32[8,128]{1,0:T(8,128)S(1)} %get-tuple-element.168), channel_id=1, source_target_pairs={{16,17},{17,16},{1,2},{2,1},{18,19},{19,18},{3,4},{4,3},{20,21},{2... | collective-permute-start | bytes 12296 | tf_op jit(solution)/shard_map/ppermute | solution.py:463
  82.1 1.2 collective-permute-done.16.got_a
  83.3 2.2 %collective-permute-done.17.got_b = f32[8,128]{1,0:T(8,128)S(1)} collective-permute-done((f32[8,128]{1,0:T(8,128)S(1)}, f32[8,128]{1,0:T(8,128)S(1)}, u32[]{:S(2)}, u32[]{:S(2)}) %collective-permute-start.17) | collective-permute-done | bytes 4128 | tf_op jit(solution)/shard_map/ppermute | solution.py:463
  86.4 2.3 %collective-permute-start.19 = (f32[8,128]{1,0:T(8,128)S(1)}, f32[8,128]{1,0:T(8,128)S(1)}, u32[]{:S(2)}, u32[]{:S(2)}) collective-permute-start(f32[8,128]{1,0:T(8,128)S(1)} %get-tuple-element.174), channel_id=1, source_target_pairs={{16,17},{17,16},{1,2},{2,1},{18,19},{19,18},{3,4},{4,3},{20,21},{2... | collective-permute-start | bytes 12296 | tf_op jit(solution)/shard_map/ppermute | solution.py:463
  88.7 1.2 collective-permute-done.18.got_a
  90.0 2.2 %collective-permute-done.19.got_b = f32[8,128]{1,0:T(8,128)S(1)} collective-permute-done((f32[8,128]{1,0:T(8,128)S(1)}, f32[8,128]{1,0:T(8,128)S(1)}, u32[]{:S(2)}, u32[]{:S(2)}) %collective-permute-start.19) | collective-permute-done | bytes 4128 | tf_op jit(solution)/shard_map/ppermute | solution.py:463
  93.0 2.3 %collective-permute-start.21 = (f32[8,128]{1,0:T(8,128)S(1)}, f32[8,128]{1,0:T(8,128)S(1)}, u32[]{:S(2)}, u32[]{:S(2)}) collective-permute-start(f32[8,128]{1,0:T(8,128)S(1)} %get-tuple-element.181), channel_id=1, source_target_pairs={{16,17},{17,16},{1,2},{2,1},{18,19},{19,18},{3,4},{4,3},{20,21},{2... | collective-permute-start | bytes 12296 | tf_op jit(solution)/shard_map/ppermute | solution.py:463
  96.6 2.2 %collective-permute-done.21.got_b = f32[8,128]{1,0:T(8,128)S(1)} collective-permute-done((f32[8,128]{1,0:T(8,128)S(1)}, f32[8,128]{1,0:T(8,128)S(1)}, u32[]{:S(2)}, u32[]{:S(2)}) %collective-permute-start.21) | collective-permute-done | bytes 4128 | tf_op jit(solution)/shard_map/ppermute | solution.py:463
  99.6 2.3 %collective-permute-start.23 = (f32[8,128]{1,0:T(8,128)S(1)}, f32[8,128]{1,0:T(8,128)S(1)}, u32[]{:S(2)}, u32[]{:S(2)}) collective-permute-start(f32[8,128]{1,0:T(8,128)S(1)} %get-tuple-element.184), channel_id=1, source_target_pairs={{16,17},{17,16},{1,2},{2,1},{18,19},{19,18},{3,4},{4,3},{20,21},{2... | collective-permute-start | bytes 12296 | tf_op jit(solution)/shard_map/ppermute | solution.py:463
  103.2 2.2 %collective-permute-done.23.got_b = f32[8,128]{1,0:T(8,128)S(1)} collective-permute-done((f32[8,128]{1,0:T(8,128)S(1)}, f32[8,128]{1,0:T(8,128)S(1)}, u32[]{:S(2)}, u32[]{:S(2)}) %collective-permute-start.23) | collective-permute-done | bytes 4128 | tf_op jit(solution)/shard_map/ppermute | solution.py:463
  106.2 2.3 %collective-permute-start.25 = (f32[8,128]{1,0:T(8,128)S(1)}, f32[8,128]{1,0:T(8,128)S(1)}, u32[]{:S(2)}, u32[]{:S(2)}) collective-permute-start(f32[8,128]{1,0:T(8,128)S(1)} %get-tuple-element.190), channel_id=1, source_target_pairs={{16,17},{17,16},{1,2},{2,1},{18,19},{19,18},{3,4},{4,3},{20,21},{2... | collective-permute-start | bytes 12296 | tf_op jit(solution)/shard_map/ppermute | solution.py:463
  109.8 2.2 %collective-permute-done.25.got_b = f32[8,128]{1,0:T(8,128)S(1)} collective-permute-done((f32[8,128]{1,0:T(8,128)S(1)}, f32[8,128]{1,0:T(8,128)S(1)}, u32[]{:S(2)}, u32[]{:S(2)}) %collective-permute-start.25) | collective-permute-done | bytes 4128 | tf_op jit(solution)/shard_map/ppermute | solution.py:463
  112.9 2.3 %collective-permute-start.27 = (f32[8,128]{1,0:T(8,128)S(1)}, f32[8,128]{1,0:T(8,128)S(1)}, u32[]{:S(2)}, u32[]{:S(2)}) collective-permute-start(f32[8,128]{1,0:T(8,128)S(1)} %get-tuple-element.196), channel_id=1, source_target_pairs={{16,17},{17,16},{1,2},{2,1},{18,19},{19,18},{3,4},{4,3},{20,21},{2... | collective-permute-start | bytes 12296 | tf_op jit(solution)/shard_map/ppermute | solution.py:463
  116.5 2.2 %collective-permute-done.27.got_b = f32[8,128]{1,0:T(8,128)S(1)} collective-permute-done((f32[8,128]{1,0:T(8,128)S(1)}, f32[8,128]{1,0:T(8,128)S(1)}, u32[]{:S(2)}, u32[]{:S(2)}) %collective-permute-start.27) | collective-permute-done | bytes 4128 | tf_op jit(solution)/shard_map/ppermute | solution.py:463
  119.5 2.5 %collective-permute-start.29 = (f32[8,128]{1,0:T(8,128)S(1)}, f32[8,128]{1,0:T(8,128)S(1)}, u32[]{:S(2)}, u32[]{:S(2)}) collective-permute-start(f32[8,128]{1,0:T(8,128)S(1)} %get-tuple-element.203), channel_id=1, source_target_pairs={{16,17},{17,16},{1,2},{2,1},{18,19},{19,18},{3,4},{4,3},{20,21},{2... | collective-permute-start | bytes 12296 | tf_op jit(solution)/shard_map/ppermute | solution.py:463
  123.1 2.4 %collective-permute-done.29.got_b = f32[8,128]{1,0:T(8,128)S(1)} collective-permute-done((f32[8,128]{1,0:T(8,128)S(1)}, f32[8,128]{1,0:T(8,128)S(1)}, u32[]{:S(2)}, u32[]{:S(2)}) %collective-permute-start.29) | collective-permute-done | bytes 4128 | tf_op jit(solution)/shard_map/ppermute | solution.py:463
  126.3 2.3 %collective-permute-start.31 = (f32[8,128]{1,0:T(8,128)S(1)}, f32[8,128]{1,0:T(8,128)S(1)}, u32[]{:S(2)}, u32[]{:S(2)}) collective-permute-start(f32[8,128]{1,0:T(8,128)S(1)} %get-tuple-element.206), channel_id=1, source_target_pairs={{16,17},{17,16},{1,2},{2,1},{18,19},{19,18},{3,4},{4,3},{20,21},{2... | collective-permute-start | bytes 12296 | tf_op jit(solution)/shard_map/ppermute | solution.py:463
  129.9 2.2 %collective-permute-done.31.got_b = f32[8,128]{1,0:T(8,128)S(1)} collective-permute-done((f32[8,128]{1,0:T(8,128)S(1)}, f32[8,128]{1,0:T(8,128)S(1)}, u32[]{:S(2)}, u32[]{:S(2)}) %collective-permute-start.31) | collective-permute-done | bytes 4128 | tf_op jit(solution)/shard_map/ppermute | solution.py:463
  132.9 2.3 %collective-permute-start.33 = (f32[8,128]{1,0:T(8,128)S(1)}, f32[8,128]{1,0:T(8,128)S(1)}, u32[]{:S(2)}, u32[]{:S(2)}) collective-permute-start(f32[8,128]{1,0:T(8,128)S(1)} %get-tuple-element.212), channel_id=1, source_target_pairs={{16,17},{17,16},{1,2},{2,1},{18,19},{19,18},{3,4},{4,3},{20,21},{2... | collective-permute-start | bytes 12296 | tf_op jit(solution)/shard_map/ppermute | solution.py:463
  136.5 2.2 %collective-permute-done.33.got_b = f32[8,128]{1,0:T(8,128)S(1)} collective-permute-done((f32[8,128]{1,0:T(8,128)S(1)}, f32[8,128]{1,0:T(8,128)S(1)}, u32[]{:S(2)}, u32[]{:S(2)}) %collective-permute-start.33) | collective-permute-done | bytes 4128 | tf_op jit(solution)/shard_map/ppermute | solution.py:463
  139.6 2.3 %collective-permute-start.35 = (f32[8,128]{1,0:T(8,128)S(1)}, f32[8,128]{1,0:T(8,128)S(1)}, u32[]{:S(2)}, u32[]{:S(2)}) collective-permute-start(f32[8,128]{1,0:T(8,128)S(1)} %get-tuple-element.218), channel_id=1, source_target_pairs={{16,17},{17,16},{1,2},{2,1},{18,19},{19,18},{3,4},{4,3},{20,21},{2... | collective-permute-start | bytes 12296 | tf_op jit(solution)/shard_map/ppermute | solution.py:463
  143.2 2.2 %collective-permute-done.35.got_b = f32[8,128]{1,0:T(8,128)S(1)} collective-permute-done((f32[8,128]{1,0:T(8,128)S(1)}, f32[8,128]{1,0:T(8,128)S(1)}, u32[]{:S(2)}, u32[]{:S(2)}) %collective-permute-start.35) | collective-permute-done | bytes 4128 | tf_op jit(solution)/shard_map/ppermute | solution.py:463
  146.0 3.6 %collective-permute-done.36 = f32[4,2,2,128]{3,2,1,0:T(2,128)S(1)} collective-permute-done((f32[4,2,2,128]{3,2,1,0:T(2,128)S(1)}, f32[4,2,2,128]{3,2,1,0:T(2,128)S(1)}, u32[]{:S(2)}, u32[]{:S(2)}) %collective-permute-start.36) | collective-permute-done | bytes 8224 | tf_op jit(solution)/shard_map/ppermute | solution.py:473
  (82 shorter events, 28.4 us)
Async XLA Ops:
  0.1 0.7 copy-start
  0.8 5.1 %copy-start.1 = (f32[1,1,16,4,512]{4,3,2,1,0:T(4,128)S(1)}, f32[1,1,16,4,512]{4,3,2,1,0:T(4,128)}, u32[]{:S(2)}) copy-start(f32[1,1,16,4,512]{4,3,2,1,0:T(4,128)} %param.14) | copy-start | bytes 393220
  0.8 5.1 %copy-start.2 = (f32[2,4,128]{2,1,0:T(4,128)S(1)}, f32[2,4,128]{2,1,0:T(4,128)}, u32[]{:S(2)}) copy-start(f32[2,4,128]{2,1,0:T(4,128)} %param.12) | copy-start | bytes 12292
  0.8 5.1 %copy-start.3 = (f32[2,4,128]{2,1,0:T(4,128)S(1)}, f32[2,4,128]{2,1,0:T(4,128)}, u32[]{:S(2)}) copy-start(f32[2,4,128]{2,1,0:T(4,128)} %param.13) | copy-start | bytes 12292
  0.8 5.1 %copy-start.4 = (s32[1,1,16,4]{2,3,1,0:T(4,128)S(1)}, s32[1,1,16,4]{2,3,1,0:T(4,128)}, u32[]{:S(2)}) copy-start(s32[1,1,16,4]{2,3,1,0:T(4,128)} %param.15) | copy-start | bytes 772
  4.3 33.9 %collective-permute-start.3 = (f32[20,128,128]{2,1,0:T(8,128)}, f32[20,128,128]{2,1,0:T(8,128)S(1)}, u32[]{:S(2)}, u32[]{:S(2)}) collective-permute-start(f32[20,128,128]{2,1,0:T(8,128)} %get-tuple-element.130), channel_id=1, source_target_pairs={{0,16},{16,0},{1,17},{17,1},{2,18},{18,2},{3,19},{19,3},{4,20},{20... | collective-permute-start | bytes 3932168 | tf_op jit(solution)/shard_map/ppermute | solution.py:418
  6.9 12.0 %all-to-all-start = ((f32[1,1,16,5,512]{4,1,3,0,2:T(1,128)}), f32[1,1,16,5,512]{4,1,3,0,2:T(1,128)S(1)}, u32[]{:S(2)}, u32[]{:S(2)}) async-start(f32[1,1,16,5,512]{4,1,3,0,2:T(1,128)} %fusion), calls=%async_computation | async-start | bytes 327680 | tf_op jit(solution)/shard_map/cond/branch_1_fun/all_to_all | solution.py:131
  13.2 8.5 %collective-permute-start.1 = (f32[2,128,128]{2,1,0:T(8,128)S(1)}, f32[2,128,128]{2,1,0:T(8,128)S(1)}, u32[]{:S(2)}, u32[]{:S(2)}) collective-permute-start(f32[2,128,128]{2,1,0:T(8,128)S(1)} %get-tuple-element.33), channel_id=1, source_target_pairs={{16,17},{17,16},{1,2},{2,1},{18,19},{19,18},{3,4},{4,3},{20,21},{2... | collective-permute-start | bytes 393224 | tf_op jit(solution)/shard_map/cond/branch_1_fun/ppermute | solution.py:421
  16.3 20.8 %collective-permute-start.2 = (f32[2,128,128]{2,1,0:T(8,128)S(1)}, f32[2,128,128]{2,1,0:T(8,128)S(1)}, u32[]{:S(2)}, u32[]{:S(2)}) collective-permute-start(f32[2,128,128]{2,1,0:T(8,128)S(1)} %get-tuple-element.34), channel_id=1, source_target_pairs={{0,17},{1,16},{17,2},{18,1},{2,19},{3,18},{19,4},{20,3},{4,21},{5,... | collective-permute-start | bytes 393224 | tf_op jit(solution)/shard_map/cond/branch_1_fun/ppermute | solution.py:422
  19.3 18.8 %collective-permute-start = (f32[6,2,2,128]{3,2,1,0:T(2,128)S(1)}, f32[6,2,2,128]{3,2,1,0:T(2,128)S(1)}, u32[]{:S(2)}, u32[]{:S(2)}) collective-permute-start(f32[6,2,2,128]{3,2,1,0:T(2,128)S(1)} %get-tuple-element.256), channel_id=1, source_target_pairs={{0,16},{16,0},{1,17},{17,1},{2,18},{18,2},{3,19},{19,3},{4,20},{20... | collective-permute-start | bytes 36872 | tf_op jit(solution)/shard_map/cond/branch_1_fun/ppermute | solution.py:429
  38.4 3.9 %collective-permute-start.4 = (f32[8,128]{1,0:T(8,128)S(1)}, f32[8,128]{1,0:T(8,128)S(1)}, u32[]{:S(2)}, u32[]{:S(2)}) collective-permute-start(f32[8,128]{1,0:T(8,128)S(1)} %get-tuple-element.136), channel_id=1, source_target_pairs={{0,16},{16,0},{1,17},{17,1},{2,18},{18,2},{3,19},{19,3},{4,20},{20... | collective-permute-start | bytes 12296 | tf_op jit(solution)/shard_map/ppermute | solution.py:464
  40.0 5.8 %collective-permute-start.5 = (f32[8,128]{1,0:T(8,128)S(1)}, f32[8,128]{1,0:T(8,128)S(1)}, u32[]{:S(2)}, u32[]{:S(2)}) collective-permute-start(f32[8,128]{1,0:T(8,128)S(1)} %get-tuple-element.137), channel_id=1, source_target_pairs={{16,17},{17,16},{1,2},{2,1},{18,19},{19,18},{3,4},{4,3},{20,21},{2... | collective-permute-start | bytes 12296 | tf_op jit(solution)/shard_map/ppermute | solution.py:463
  46.5 3.7 %collective-permute-start.6 = (f32[8,128]{1,0:T(8,128)S(1)}, f32[8,128]{1,0:T(8,128)S(1)}, u32[]{:S(2)}, u32[]{:S(2)}) collective-permute-start(f32[8,128]{1,0:T(8,128)S(1)} %get-tuple-element.139), channel_id=1, source_target_pairs={{0,16},{16,0},{1,17},{17,1},{2,18},{18,2},{3,19},{19,3},{4,20},{20... | collective-permute-start | bytes 12296 | tf_op jit(solution)/shard_map/ppermute | solution.py:464
  46.6 5.8 %collective-permute-start.7 = (f32[8,128]{1,0:T(8,128)S(1)}, f32[8,128]{1,0:T(8,128)S(1)}, u32[]{:S(2)}, u32[]{:S(2)}) collective-permute-start(f32[8,128]{1,0:T(8,128)S(1)} %get-tuple-element.140), channel_id=1, source_target_pairs={{16,17},{17,16},{1,2},{2,1},{18,19},{19,18},{3,4},{4,3},{20,21},{2... | collective-permute-start | bytes 12296 | tf_op jit(solution)/shard_map/ppermute | solution.py:463
  53.1 3.7 %collective-permute-start.8 = (f32[8,128]{1,0:T(8,128)S(1)}, f32[8,128]{1,0:T(8,128)S(1)}, u32[]{:S(2)}, u32[]{:S(2)}) collective-permute-start(f32[8,128]{1,0:T(8,128)S(1)} %get-tuple-element.145), channel_id=1, source_target_pairs={{0,16},{16,0},{1,17},{17,1},{2,18},{18,2},{3,19},{19,3},{4,20},{20... | collective-permute-start | bytes 12296 | tf_op jit(solution)/shard_map/ppermute | solution.py:464
  53.2 5.8 %collective-permute-start.9 = (f32[8,128]{1,0:T(8,128)S(1)}, f32[8,128]{1,0:T(8,128)S(1)}, u32[]{:S(2)}, u32[]{:S(2)}) collective-permute-start(f32[8,128]{1,0:T(8,128)S(1)} %get-tuple-element.146), channel_id=1, source_target_pairs={{16,17},{17,16},{1,2},{2,1},{18,19},{19,18},{3,4},{4,3},{20,21},{2... | collective-permute-start | bytes 12296 | tf_op jit(solution)/shard_map/ppermute | solution.py:463
  59.8 3.7 %collective-permute-start.10 = (f32[8,128]{1,0:T(8,128)S(1)}, f32[8,128]{1,0:T(8,128)S(1)}, u32[]{:S(2)}, u32[]{:S(2)}) collective-permute-start(f32[8,128]{1,0:T(8,128)S(1)} %get-tuple-element.151), channel_id=1, source_target_pairs={{0,16},{16,0},{1,17},{17,1},{2,18},{18,2},{3,19},{19,3},{4,20},{20... | collective-permute-start | bytes 12296 | tf_op jit(solution)/shard_map/ppermute | solution.py:464
  59.8 5.8 %collective-permute-start.11 = (f32[8,128]{1,0:T(8,128)S(1)}, f32[8,128]{1,0:T(8,128)S(1)}, u32[]{:S(2)}, u32[]{:S(2)}) collective-permute-start(f32[8,128]{1,0:T(8,128)S(1)} %get-tuple-element.152), channel_id=1, source_target_pairs={{16,17},{17,16},{1,2},{2,1},{18,19},{19,18},{3,4},{4,3},{20,21},{2... | collective-permute-start | bytes 12296 | tf_op jit(solution)/shard_map/ppermute | solution.py:463
  66.4 3.7 %collective-permute-start.12 = (f32[8,128]{1,0:T(8,128)S(1)}, f32[8,128]{1,0:T(8,128)S(1)}, u32[]{:S(2)}, u32[]{:S(2)}) collective-permute-start(f32[8,128]{1,0:T(8,128)S(1)} %get-tuple-element.158), channel_id=1, source_target_pairs={{0,16},{16,0},{1,17},{17,1},{2,18},{18,2},{3,19},{19,3},{4,20},{20... | collective-permute-start | bytes 12296 | tf_op jit(solution)/shard_map/ppermute | solution.py:464
  66.5 5.8 %collective-permute-start.13 = (f32[8,128]{1,0:T(8,128)S(1)}, f32[8,128]{1,0:T(8,128)S(1)}, u32[]{:S(2)}, u32[]{:S(2)}) collective-permute-start(f32[8,128]{1,0:T(8,128)S(1)} %get-tuple-element.159), channel_id=1, source_target_pairs={{16,17},{17,16},{1,2},{2,1},{18,19},{19,18},{3,4},{4,3},{20,21},{2... | collective-permute-start | bytes 12296 | tf_op jit(solution)/shard_map/ppermute | solution.py:463
  73.0 3.7 %collective-permute-start.14 = (f32[8,128]{1,0:T(8,128)S(1)}, f32[8,128]{1,0:T(8,128)S(1)}, u32[]{:S(2)}, u32[]{:S(2)}) collective-permute-start(f32[8,128]{1,0:T(8,128)S(1)} %get-tuple-element.161), channel_id=1, source_target_pairs={{0,16},{16,0},{1,17},{17,1},{2,18},{18,2},{3,19},{19,3},{4,20},{20... | collective-permute-start | bytes 12296 | tf_op jit(solution)/shard_map/ppermute | solution.py:464
  73.1 5.8 %collective-permute-start.15 = (f32[8,128]{1,0:T(8,128)S(1)}, f32[8,128]{1,0:T(8,128)S(1)}, u32[]{:S(2)}, u32[]{:S(2)}) collective-permute-start(f32[8,128]{1,0:T(8,128)S(1)} %get-tuple-element.162), channel_id=1, source_target_pairs={{16,17},{17,16},{1,2},{2,1},{18,19},{19,18},{3,4},{4,3},{20,21},{2... | collective-permute-start | bytes 12296 | tf_op jit(solution)/shard_map/ppermute | solution.py:463
  79.6 3.7 %collective-permute-start.16 = (f32[8,128]{1,0:T(8,128)S(1)}, f32[8,128]{1,0:T(8,128)S(1)}, u32[]{:S(2)}, u32[]{:S(2)}) collective-permute-start(f32[8,128]{1,0:T(8,128)S(1)} %get-tuple-element.167), channel_id=1, source_target_pairs={{0,16},{16,0},{1,17},{17,1},{2,18},{18,2},{3,19},{19,3},{4,20},{20... | collective-permute-start | bytes 12296 | tf_op jit(solution)/shard_map/ppermute | solution.py:464
  79.7 5.8 %collective-permute-start.17 = (f32[8,128]{1,0:T(8,128)S(1)}, f32[8,128]{1,0:T(8,128)S(1)}, u32[]{:S(2)}, u32[]{:S(2)}) collective-permute-start(f32[8,128]{1,0:T(8,128)S(1)} %get-tuple-element.168), channel_id=1, source_target_pairs={{16,17},{17,16},{1,2},{2,1},{18,19},{19,18},{3,4},{4,3},{20,21},{2... | collective-permute-start | bytes 12296 | tf_op jit(solution)/shard_map/ppermute | solution.py:463
  86.3 3.7 %collective-permute-start.18 = (f32[8,128]{1,0:T(8,128)S(1)}, f32[8,128]{1,0:T(8,128)S(1)}, u32[]{:S(2)}, u32[]{:S(2)}) collective-permute-start(f32[8,128]{1,0:T(8,128)S(1)} %get-tuple-element.173), channel_id=1, source_target_pairs={{0,16},{16,0},{1,17},{17,1},{2,18},{18,2},{3,19},{19,3},{4,20},{20... | collective-permute-start | bytes 12296 | tf_op jit(solution)/shard_map/ppermute | solution.py:464
  86.4 5.8 %collective-permute-start.19 = (f32[8,128]{1,0:T(8,128)S(1)}, f32[8,128]{1,0:T(8,128)S(1)}, u32[]{:S(2)}, u32[]{:S(2)}) collective-permute-start(f32[8,128]{1,0:T(8,128)S(1)} %get-tuple-element.174), channel_id=1, source_target_pairs={{16,17},{17,16},{1,2},{2,1},{18,19},{19,18},{3,4},{4,3},{20,21},{2... | collective-permute-start | bytes 12296 | tf_op jit(solution)/shard_map/ppermute | solution.py:463
  92.9 3.7 %collective-permute-start.20 = (f32[8,128]{1,0:T(8,128)S(1)}, f32[8,128]{1,0:T(8,128)S(1)}, u32[]{:S(2)}, u32[]{:S(2)}) collective-permute-start(f32[8,128]{1,0:T(8,128)S(1)} %get-tuple-element.180), channel_id=1, source_target_pairs={{0,16},{16,0},{1,17},{17,1},{2,18},{18,2},{3,19},{19,3},{4,20},{20... | collective-permute-start | bytes 12296 | tf_op jit(solution)/shard_map/ppermute | solution.py:464
  93.0 5.8 %collective-permute-start.21 = (f32[8,128]{1,0:T(8,128)S(1)}, f32[8,128]{1,0:T(8,128)S(1)}, u32[]{:S(2)}, u32[]{:S(2)}) collective-permute-start(f32[8,128]{1,0:T(8,128)S(1)} %get-tuple-element.181), channel_id=1, source_target_pairs={{16,17},{17,16},{1,2},{2,1},{18,19},{19,18},{3,4},{4,3},{20,21},{2... | collective-permute-start | bytes 12296 | tf_op jit(solution)/shard_map/ppermute | solution.py:463
  99.5 3.7 %collective-permute-start.22 = (f32[8,128]{1,0:T(8,128)S(1)}, f32[8,128]{1,0:T(8,128)S(1)}, u32[]{:S(2)}, u32[]{:S(2)}) collective-permute-start(f32[8,128]{1,0:T(8,128)S(1)} %get-tuple-element.183), channel_id=1, source_target_pairs={{0,16},{16,0},{1,17},{17,1},{2,18},{18,2},{3,19},{19,3},{4,20},{20... | collective-permute-start | bytes 12296 | tf_op jit(solution)/shard_map/ppermute | solution.py:464
  99.6 5.8 %collective-permute-start.23 = (f32[8,128]{1,0:T(8,128)S(1)}, f32[8,128]{1,0:T(8,128)S(1)}, u32[]{:S(2)}, u32[]{:S(2)}) collective-permute-start(f32[8,128]{1,0:T(8,128)S(1)} %get-tuple-element.184), channel_id=1, source_target_pairs={{16,17},{17,16},{1,2},{2,1},{18,19},{19,18},{3,4},{4,3},{20,21},{2... | collective-permute-start | bytes 12296 | tf_op jit(solution)/shard_map/ppermute | solution.py:463
  106.2 3.7 %collective-permute-start.24 = (f32[8,128]{1,0:T(8,128)S(1)}, f32[8,128]{1,0:T(8,128)S(1)}, u32[]{:S(2)}, u32[]{:S(2)}) collective-permute-start(f32[8,128]{1,0:T(8,128)S(1)} %get-tuple-element.189), channel_id=1, source_target_pairs={{0,16},{16,0},{1,17},{17,1},{2,18},{18,2},{3,19},{19,3},{4,20},{20... | collective-permute-start | bytes 12296 | tf_op jit(solution)/shard_map/ppermute | solution.py:464
  106.2 5.8 %collective-permute-start.25 = (f32[8,128]{1,0:T(8,128)S(1)}, f32[8,128]{1,0:T(8,128)S(1)}, u32[]{:S(2)}, u32[]{:S(2)}) collective-permute-start(f32[8,128]{1,0:T(8,128)S(1)} %get-tuple-element.190), channel_id=1, source_target_pairs={{16,17},{17,16},{1,2},{2,1},{18,19},{19,18},{3,4},{4,3},{20,21},{2... | collective-permute-start | bytes 12296 | tf_op jit(solution)/shard_map/ppermute | solution.py:463
  112.8 3.7 %collective-permute-start.26 = (f32[8,128]{1,0:T(8,128)S(1)}, f32[8,128]{1,0:T(8,128)S(1)}, u32[]{:S(2)}, u32[]{:S(2)}) collective-permute-start(f32[8,128]{1,0:T(8,128)S(1)} %get-tuple-element.195), channel_id=1, source_target_pairs={{0,16},{16,0},{1,17},{17,1},{2,18},{18,2},{3,19},{19,3},{4,20},{20... | collective-permute-start | bytes 12296 | tf_op jit(solution)/shard_map/ppermute | solution.py:464
  112.9 5.8 %collective-permute-start.27 = (f32[8,128]{1,0:T(8,128)S(1)}, f32[8,128]{1,0:T(8,128)S(1)}, u32[]{:S(2)}, u32[]{:S(2)}) collective-permute-start(f32[8,128]{1,0:T(8,128)S(1)} %get-tuple-element.196), channel_id=1, source_target_pairs={{16,17},{17,16},{1,2},{2,1},{18,19},{19,18},{3,4},{4,3},{20,21},{2... | collective-permute-start | bytes 12296 | tf_op jit(solution)/shard_map/ppermute | solution.py:463
  119.4 3.7 %collective-permute-start.28 = (f32[8,128]{1,0:T(8,128)S(1)}, f32[8,128]{1,0:T(8,128)S(1)}, u32[]{:S(2)}, u32[]{:S(2)}) collective-permute-start(f32[8,128]{1,0:T(8,128)S(1)} %get-tuple-element.202), channel_id=1, source_target_pairs={{0,16},{16,0},{1,17},{17,1},{2,18},{18,2},{3,19},{19,3},{4,20},{20... | collective-permute-start | bytes 12296 | tf_op jit(solution)/shard_map/ppermute | solution.py:464
  119.5 6.0 %collective-permute-start.29 = (f32[8,128]{1,0:T(8,128)S(1)}, f32[8,128]{1,0:T(8,128)S(1)}, u32[]{:S(2)}, u32[]{:S(2)}) collective-permute-start(f32[8,128]{1,0:T(8,128)S(1)} %get-tuple-element.203), channel_id=1, source_target_pairs={{16,17},{17,16},{1,2},{2,1},{18,19},{19,18},{3,4},{4,3},{20,21},{2... | collective-permute-start | bytes 12296 | tf_op jit(solution)/shard_map/ppermute | solution.py:463
  126.2 3.7 %collective-permute-start.30 = (f32[8,128]{1,0:T(8,128)S(1)}, f32[8,128]{1,0:T(8,128)S(1)}, u32[]{:S(2)}, u32[]{:S(2)}) collective-permute-start(f32[8,128]{1,0:T(8,128)S(1)} %get-tuple-element.205), channel_id=1, source_target_pairs={{0,16},{16,0},{1,17},{17,1},{2,18},{18,2},{3,19},{19,3},{4,20},{20... | collective-permute-start | bytes 12296 | tf_op jit(solution)/shard_map/ppermute | solution.py:464
  126.3 5.8 %collective-permute-start.31 = (f32[8,128]{1,0:T(8,128)S(1)}, f32[8,128]{1,0:T(8,128)S(1)}, u32[]{:S(2)}, u32[]{:S(2)}) collective-permute-start(f32[8,128]{1,0:T(8,128)S(1)} %get-tuple-element.206), channel_id=1, source_target_pairs={{16,17},{17,16},{1,2},{2,1},{18,19},{19,18},{3,4},{4,3},{20,21},{2... | collective-permute-start | bytes 12296 | tf_op jit(solution)/shard_map/ppermute | solution.py:463
  132.9 3.7 %collective-permute-start.32 = (f32[8,128]{1,0:T(8,128)S(1)}, f32[8,128]{1,0:T(8,128)S(1)}, u32[]{:S(2)}, u32[]{:S(2)}) collective-permute-start(f32[8,128]{1,0:T(8,128)S(1)} %get-tuple-element.211), channel_id=1, source_target_pairs={{0,16},{16,0},{1,17},{17,1},{2,18},{18,2},{3,19},{19,3},{4,20},{20... | collective-permute-start | bytes 12296 | tf_op jit(solution)/shard_map/ppermute | solution.py:464
  132.9 5.8 %collective-permute-start.33 = (f32[8,128]{1,0:T(8,128)S(1)}, f32[8,128]{1,0:T(8,128)S(1)}, u32[]{:S(2)}, u32[]{:S(2)}) collective-permute-start(f32[8,128]{1,0:T(8,128)S(1)} %get-tuple-element.212), channel_id=1, source_target_pairs={{16,17},{17,16},{1,2},{2,1},{18,19},{19,18},{3,4},{4,3},{20,21},{2... | collective-permute-start | bytes 12296 | tf_op jit(solution)/shard_map/ppermute | solution.py:463
  139.5 3.7 %collective-permute-start.34 = (f32[8,128]{1,0:T(8,128)S(1)}, f32[8,128]{1,0:T(8,128)S(1)}, u32[]{:S(2)}, u32[]{:S(2)}) collective-permute-start(f32[8,128]{1,0:T(8,128)S(1)} %get-tuple-element.217), channel_id=1, source_target_pairs={{0,16},{16,0},{1,17},{17,1},{2,18},{18,2},{3,19},{19,3},{4,20},{20... | collective-permute-start | bytes 12296 | tf_op jit(solution)/shard_map/ppermute | solution.py:464
  139.6 5.8 %collective-permute-start.35 = (f32[8,128]{1,0:T(8,128)S(1)}, f32[8,128]{1,0:T(8,128)S(1)}, u32[]{:S(2)}, u32[]{:S(2)}) collective-permute-start(f32[8,128]{1,0:T(8,128)S(1)} %get-tuple-element.218), channel_id=1, source_target_pairs={{16,17},{17,16},{1,2},{2,1},{18,19},{19,18},{3,4},{4,3},{20,21},{2... | collective-permute-start | bytes 12296 | tf_op jit(solution)/shard_map/ppermute | solution.py:463
  145.9 3.7 %collective-permute-start.36 = (f32[4,2,2,128]{3,2,1,0:T(2,128)S(1)}, f32[4,2,2,128]{3,2,1,0:T(2,128)S(1)}, u32[]{:S(2)}, u32[]{:S(2)}) collective-permute-start(f32[4,2,2,128]{3,2,1,0:T(2,128)S(1)} %rev.22), channel_id=1, source_target_pairs={{0,16},{16,0},{1,17},{17,1},{2,18},{18,2},{3,19},{19,3},{4,20},{20... | collective-permute-start | bytes 24584 | tf_op jit(solution)/shard_map/ppermute | solution.py:473

commit v8 on v7

--- a/solution.py
+++ b/solution.py
@@ -193,6 +193,7 @@
 TILES = [(j, b) for j in range(N) for b in range(HALF)]
 ORIGIN = [(0, 0), (0, 1), (1, 1), (1, 0)]
 CAPACITY, INITIAL = STEPS, STEPS + 1
+SPLIT = ((PACKED,), (OUT_IN, PACKED - OUT_IN))
 
 
 def unit_device(unit, n_col):
@@ -200,83 +201,94 @@
     return (unit + col) % 2, col
 
 
-def pack_kernel(n_col, place_ref, pattern_ref, own_hbm, nb_hbm, keep, send, facing_0, facing_1, own_ref, nb_ref, sems):
-    y, col = place_ref[0], place_ref[1]
-    copies = [pltpu.make_async_copy(own_hbm, own_ref, sems.at[4])]
-    copies += [pltpu.make_async_copy(nb_hbm.at[d], nb_ref.at[d], sems.at[d]) for d in (2, 3, 0, 1)]
+def half_tiles(y, col, n_col, cols, sent):
+    k = (y + col + sent) % 2
+    rows = (y, 1 - y)
+    inward, outward = 1 - y, y
+    at = [b + k * (cols - 1 - 2 * b) for b in range(HALF)]
+    inside = jnp.where(col == k * (n_col - 1), 0.0, 1.0)
+    tiles = [None] * PACKED
+    for h in range(ROWS):
+        for b in range(HALF):
+            tiles[OWN + h * HALF + b] = (None, rows[h], at[b], None)
+            tiles[SIDE_A + h * HALF + b] = (3 - k, rows[h], at[b], None)
+            tiles[SIDE_B + h * HALF + b] = (2 + k, rows[h], at[b], inside if b == 0 else None)
+        tiles[FACING + h] = (2 + k, rows[h], HALF - k, None)
+    for b in range(HALF):
+        tiles[OUT_IN + b] = (inward, rows[0], at[b], None)
+        tiles[IN_OUT + b] = (outward, rows[1], at[b], None)
+        tiles[IN_IN + b] = (inward, rows[1], at[b], None)
+    return tiles
+
+
+def pack_kernel(n_col, sent, first, count, place_ref, pattern_ref, own_hbm, nb_hbm, out, *rest):
+    sems = rest[-1]
+    tiles = half_tiles(place_ref[0], place_ref[1], n_col, own_hbm.shape[1], sent)
+    copies = []
+    for i in range(count):
+        direction, row, at, _ = tiles[first + i]
+        source = own_hbm.at[row, at] if direction is None else nb_hbm.at[direction, row, at]
+        copies.append(pltpu.make_async_copy(source, out.at[i], sems.at[i]))
     for copy in copies:
         copy.start()
-    rows = (y, 1 - y)
-    inward, outward = 1 - y, y
-    cols = own_ref.shape[1]
-
-    def coupling(direction, row, at_col):
-        weight = pattern_ref[row, at_col, direction].astype(jnp.float32)
-        return nb_ref[direction, row, at_col] * weight
-
-    halves = []
-    for i, (half, facing) in enumerate(((keep, facing_0), (send, facing_1))):
-        k = (y + col + i) % 2
-        halves.append((half, facing, k, [b + k * (cols - 1 - 2 * b) for b in range(HALF)]))
-    copies[0].wait()
-    for half, facing, k, at in halves:
+    for i in range(count):
+        direction, row, at, weight = tiles[first + i]
+        copies[i].wait()
+        if direction is not None:
+            scale = pattern_ref[row, at, direction].astype(jnp.float32)
+            out[i] = out[i] * (scale if weight is None else scale * weight)
+    if not sent:
         for h in range(ROWS):
-            for b in range(HALF):
-                half[OWN + h * HALF + b] = own_ref[rows[h], at[b]]
-    for copy in copies[1:3]:
-        copy.wait()
-    for half, facing, k, at in halves:
-        inside = jnp.where(col == k * (n_col - 1), 0.0, 1.0)
-        for h in range(ROWS):
-            for b in range(HALF):
-                half[SIDE_A + h * HALF + b] = coupling(3 - k, rows[h], at[b])
-                block = coupling(2 + k, rows[h], at[b])
-                if b == 0:
-                    block = block * inside
-                    facing[h] = block
-                half[SIDE_B + h * HALF + b] = block
-            half[FACING + h] = coupling(2 + k, rows[h], HALF - k)
-    for copy in copies[3:]:
-        copy.wait()
-    for half, facing, k, at in halves:
-        for b in range(HALF):
-            half[OUT_IN + b] = coupling(inward, rows[0], at[b])
-            half[IN_OUT + b] = coupling(outward, rows[1], at[b])
-            half[IN_IN + b] = coupling(inward, rows[1], at[b])
+            rest[0][h] = out[SIDE_B + h * HALF]
+
+
+def block_of(refs, sizes, slot):
+    for ref, size in zip(refs, sizes):
+        if slot < size:
+            return lambda g, n: ref[slot, g:g + n, :]
+        slot -= size
+
+
+def half_block(halves, i, slot):
+    return block_of(halves[i], SPLIT[i], slot)
 
 
 def tile_terms(halves, j, b):
     i, h = ORIGIN[j]
-    half = halves[i]
-    terms = [(half, OWN + h * HALF + b, (j, b))]
+    terms = [(OWN + h * HALF + b, (j, b))]
     if h == 0:
-        terms.append((half, OUT_IN + b, ((1, 2)[i], b)))
+        terms.append((OUT_IN + b, ((1, 2)[i], b)))
     else:
-        terms.append((half, IN_OUT + b, ((0, 3)[i], b)))
-        terms.append((half, IN_IN + b, ((2, 1)[i], b)))
-    terms.append((half, (SIDE_A if b == 0 else SIDE_B) + h * HALF + b, (j, 1 - b)))
-    return terms
-
-
-def halo_term(halves, j, b):
+        terms.append((IN_OUT + b, ((0, 3)[i], b)))
+        terms.append((IN_IN + b, ((2, 1)[i], b)))
+    terms.append(((SIDE_A if b == 0 else SIDE_B) + h * HALF + b, (j, 1 - b)))
+    return [(half_block(halves, i, slot), at) for slot, at in terms]
+
+
+def halo_block(halves, j, b):
     i, h = ORIGIN[j]
-    return halves[i], (SIDE_B if b == 0 else SIDE_A) + h * HALF + b
-
-
-def facing_term(halves, beyond, j, b):
+    return half_block(halves, i, (SIDE_B if b == 0 else SIDE_A) + h * HALF + b)
+
+
+def facing_block(halves, beyond_0, first_b, j, b):
     i, h = ORIGIN[j]
-    return (beyond[i], h) if b == 0 else (halves[i], FACING + h)
+    if b == 1:
+        return half_block(halves, i, FACING + h)
+    if i == 0:
+        return lambda g, n: beyond_0[h, g:g + n, :]
+    start = 2 * N + h * first_b.shape[1]
+    return lambda g, n: first_b[start + g:start + g + n, :]
 
 
 def matvec(terms, chunk=32):
-    width = terms[0][2].shape[1]
+    width = terms[0][1].shape[1]
     lane = lax.broadcasted_iota(jnp.int32, (chunk, width), 1)
     sub = lax.broadcasted_iota(jnp.int32, (chunk, width), 0)
     spread = jnp.zeros((chunk, width), jnp.float32)
     for g in range(0, width, chunk):
         acc = None
-        for ref, index, vec in terms:
-            part = ref[index, g:g + chunk, :] * vec
+        for block, vec in terms:
+            part = block(g, chunk) * vec
             acc = part if acc is None else acc + part
         total = jnp.sum(acc, axis=1, keepdims=True)
         spread = jnp.where(lane == sub + g, total, spread)
@@ -290,7 +302,7 @@
 
 def inner_product(f, halves):
     return jnp.concatenate(
-        [matvec([(r, i, row_of(f, *at)) for r, i, at in tile_terms(halves, j, b)]) for j, b in TILES], axis=0
+        [matvec([(block, row_of(f, *at)) for block, at in tile_terms(halves, j, b)]) for j, b in TILES], axis=0
     )
 
 
@@ -312,32 +324,55 @@
     return small[index * n:(index + 1) * n, :]
 
 
-def start_kernel(half_0, half_1, small, msg_a, msg_b, q_out):
+def start_kernel(keep, recv_0, recv_1, small, msg_a, msg_b, q_out):
+    halves = ((keep,), (recv_0, recv_1))
     f = small_part(small, INITIAL)
-    q = inner_product(f, (half_0, half_1))
+    q = inner_product(f, halves)
     q_out[...] = q
-    msg_a[...], msg_b[...] = messages(f, ahead(True, 0, f, q, None, None, small_part(small, 0)))
-
-
-def pair_kernel(instant, pair, last, half_0, half_1, beyond_0, beyond_1, small, got_a, got_b, q_ref, *refs):
-    halves, beyond = (half_0, half_1), (beyond_0, beyond_1)
+    msg_a[...], to_b = messages(f, ahead(True, 0, f, q, None, None, small_part(small, 0)))
+    msg_b[:2 * N, :] = to_b
+    width = f.shape[1]
+    for h in range(ROWS):
+        start = 2 * N + h * width
+        msg_b[start:start + width, :] = recv_0[SIDE_B + h * HALF]
+
+
+def small_part(small, index):
+    n = N * HALF
+    return small[index * n:(index + 1) * n, :]
+
+
+def beside_kernel(keep, recv_0, recv_1, beyond_0, first_b, got_a, f_ref, q_ref, response_out, q_out):
+    halves = ((keep,), (recv_0, recv_1))
+    f, q = f_ref[...], q_ref[...]
+    response, total = [], []
+    for j, b in TILES:
+        response.append(matvec([(facing_block(halves, beyond_0, first_b, j, b), row_of(f, j, b))]))
+        mine = row_of(q, j, b)
+        if b == 1:
+            mine = mine + matvec([(halo_block(halves, j, b), got_a[j:j + 1, :])])
+        total.append(mine)
+    response_out[...] = jnp.concatenate(response, axis=0)
+    q_out[...] = jnp.concatenate(total, axis=0)
+
+
+def pair_kernel(instant, pair, last, keep, recv_0, recv_1, small, got_a, got_b, response_ref, q_ref, f_ref, *refs):
+    halves = ((keep,), (recv_0, recv_1))
     first = pair == 0
     capacity = small_part(small, CAPACITY)
-    q = q_ref[...]
-    if first and instant == 0:
-        f = small_part(small, INITIAL)
-    else:
-        f, refs = refs[0][...], refs[1:]
+    f, q, response = f_ref[...], q_ref[...], response_ref[...]
     if not first:
         residue, estimate, refs = refs[0][...], refs[1][...], refs[2:]
     got = (got_b, got_a)
     sweep = 2 * pair - 1
 
-    extra = []
+    product = []
     for j, b in TILES:
-        r, i = halo_term(halves, j, b)
-        extra.append(matvec([(r, i, got[b][j:j + 1, :])]))
-    product = q + jnp.concatenate(extra, axis=0)
+        mine = row_of(q, j, b)
+        if b == 0:
+            mine = mine + matvec([(halo_block(halves, j, b), got_b[j:j + 1, :])])
+        product.append(mine)
+    product = jnp.concatenate(product, axis=0)
     if first:
         residue = small_part(small, instant) - product
         f2 = residue
@@ -349,16 +384,11 @@
         estimate = estimate + STRIDES[sweep + 1] * f2
         scale = STRIDES[sweep]
 
-    beside2 = {}
-    for j, b in TILES:
-        r, i = facing_term(halves, beyond, j, b)
-        beside2[j, b] = got[b][N + j:N + j + 1, :] - scale * matvec([(r, i, row_of(f, j, b))])
-
     outs = []
     for j, b in TILES:
-        terms = [(r, i, row_of(f2, *at)) for r, i, at in tile_terms(halves, j, b)]
-        r, i = halo_term(halves, j, b)
-        outs.append(matvec(terms + [(r, i, beside2[j, b])]))
+        beside = got[b][N + j:N + j + 1, :] - scale * row_of(response, j, b)
+        terms = [(block, row_of(f2, *at)) for block, at in tile_terms(halves, j, b)]
+        outs.append(matvec(terms + [(halo_block(halves, j, b), beside)]))
     sweep = 2 * pair
     residue = residue - STRIDES[sweep] * (jnp.concatenate(outs, axis=0) + capacity * f2)
     f3 = residue + MOMENTA[sweep + 1] * f2
@@ -386,40 +416,38 @@
     row, col = lax.axis_index("row"), lax.axis_index("col")
     both = ("row", "col")
     swap = [(0, 1), (1, 0)]
-    b_pairs, b_cross = [], []
+    b_pairs = []
     for unit in range(1, 2 * n_col - 1, 2):
-        ends = unit_device(unit, n_col), unit_device(unit + 1, n_col)
-        for (r, c), (to_r, to_c) in (ends, ends[::-1]):
-            b_pairs.append((r * n_col + c, to_r * n_col + to_c))
-            b_cross.append(((1 - r) * n_col + c, to_r * n_col + to_c))
+        ends = [r * n_col + c for r, c in (unit_device(unit, n_col), unit_device(unit + 1, n_col))]
+        b_pairs += [tuple(ends), tuple(ends[::-1])]
     parity = (row + col) % 2
 
     vmem = pl.BlockSpec(memory_space=pltpu.VMEM)
     smem = pl.BlockSpec(memory_space=pltpu.SMEM)
     hbm = pl.BlockSpec(memory_space=pltpu.HBM)
     limit = pltpu.CompilerParams(vmem_limit_bytes=16 * 2**20)
-    packed = jax.ShapeDtypeStruct((PACKED, width, width), jnp.float32)
-    facing = jax.ShapeDtypeStruct((ROWS, width, width), jnp.float32)
-    half_0, send, facing_0, facing_1 = pl.pallas_call(
-        functools.partial(pack_kernel, n_col),
-        out_shape=(packed, packed, facing, facing),
-        in_specs=[smem, smem, hbm, hbm],
-        out_specs=(vmem,) * 4,
-        scratch_shapes=[
-            pltpu.VMEM(own_block.shape, jnp.float32),
-            pltpu.VMEM(neighbor_block.shape, jnp.float32),
-            pltpu.SemaphoreType.DMA((5,)),
-        ],
-        compiler_params=pltpu.CompilerParams(vmem_limit_bytes=48 * 2**20),
-        name="pack",
-    )(jnp.stack([row, col]).astype(jnp.int32), pattern,
-      pltpu.with_memory_space_constraint(own_block, pltpu.HBM),
-      pltpu.with_memory_space_constraint(neighbor_block, pltpu.HBM))
-    half_1 = lax.ppermute(send, "row", swap)
-
-    def beside(currents, slot_tile, capacity, initial, facing_0, facing_1):
+    place = jnp.stack([row, col]).astype(jnp.int32)
+    blocks = [pltpu.with_memory_space_constraint(x, pltpu.HBM) for x in (own_block, neighbor_block)]
+
+    def pack(sent, first, count, extra=()):
+        return pl.pallas_call(
+            functools.partial(pack_kernel, n_col, sent, first, count),
+            out_shape=[jax.ShapeDtypeStruct((n, width, width), jnp.float32) for n in (count, *extra)],
+            in_specs=[smem, smem, hbm, hbm],
+            out_specs=[vmem] * (1 + len(extra)),
+            scratch_shapes=[pltpu.SemaphoreType.DMA((count,))],
+            compiler_params=limit,
+            name="pack",
+        )(place, pattern, *blocks)
+
+    recv = []
+    for first, count in ((0, SPLIT[1][0]), SPLIT[1]):
+        (send,) = pack(1, first, count)
+        recv.append(lax.ppermute(send, "row", swap))
+    keep, facing_0 = pack(0, 0, PACKED, (ROWS,))
+
+    def beside(currents, slot_tile, capacity, initial, facing_0):
         beyond_0 = lax.ppermute(facing_0, both, b_pairs)
-        beyond_1 = lax.ppermute(facing_1, both, b_cross)
         injected = collect(currents, slot_tile, tile_rows * tile_cols, width)
         small = jnp.concatenate(
             [jnp.moveaxis(injected, 1, 0).reshape(STEPS, tile_rows, tile_cols, width), capacity[None], initial[None]]
@@ -428,32 +456,35 @@
         unit_0, unit_1 = small[:, :, :HALF], jnp.flip(small, 2)[:, :, :HALF]
         got = lax.ppermute(jnp.where(parity == 1, unit_0, unit_1), "row", swap)
         small = jnp.concatenate([jnp.where(parity == 1, unit_1, unit_0), jnp.flip(got, 1)], axis=1)
-        return small.reshape((STEPS + 2) * N * HALF, width), beyond_0, beyond_1
-
-    small, beyond_0, beyond_1 = lax.cond(
+        return small.reshape((STEPS + 2) * N * HALF, width), beyond_0
+
+    small, beyond_0 = lax.cond(
         row < lax.axis_size("row"),
         beside,
-        lambda currents, slot_tile, capacity, initial, *blocks: (
-            jnp.zeros(((STEPS + 2) * N * HALF, width), jnp.float32), *blocks
+        lambda currents, slot_tile, capacity, initial, facing_0: (
+            jnp.zeros(((STEPS + 2) * N * HALF, width), jnp.float32), facing_0
         ),
-        currents, slot_tile, capacity, initial, facing_0, facing_1,
+        currents, slot_tile, capacity, initial, facing_0,
     )
 
     shape = jax.ShapeDtypeStruct((N * HALF, width), jnp.float32)
-
-    def call(body, n_out, blocks, *ins):
+    halves = (keep, *recv)
+
+    def call(body, outs, blocks, *ins):
         return pl.pallas_call(
             body,
-            out_shape=(shape,) * n_out,
+            out_shape=outs,
             in_specs=[vmem] * len(ins),
-            out_specs=(vmem,) * n_out,
+            out_specs=(vmem,) * len(outs),
             compiler_params=limit,
             cost_estimate=pl.CostEstimate(flops=2 * blocks * width * width, bytes_accessed=blocks * width * width * 4,
                                           transcendentals=0),
             name="pair",
         )(*ins)
 
-    msg_a, msg_b, q = call(start_kernel, 3, 28, half_0, half_1, small)
+    first_shape = jax.ShapeDtypeStruct((2 * N + ROWS * width, width), jnp.float32)
+    msg_a, msg_b, q = call(start_kernel, (shape, first_shape, shape), 28, *halves, small)
+    field, first_b = small[INITIAL * N * HALF:(INITIAL + 1) * N * HALF], None
     frames = []
     state = ()
     for instant in range(STEPS):
@@ -462,12 +493,16 @@
             last = closing and instant + 1 == STEPS
             got_b = lax.ppermute(msg_b, both, b_pairs)
             got_a = lax.ppermute(msg_a, "row", swap)
-            out = call(functools.partial(pair_kernel, instant, pair, last), 1 if last else 4 if closing else 6, 80,
-                       half_0, half_1, beyond_0, beyond_1, small, got_a, got_b, q, *state)
+            if first_b is None:
+                first_b = got_b
+            response, q = call(beside_kernel, (shape,) * 2, 12, *halves, beyond_0, first_b, got_a, field, q)
+            out = call(functools.partial(pair_kernel, instant, pair, last), (shape,) * (1 if last else 4 if closing else 6),
+                       68, *halves, small, got_a, got_b, response, q, field, *state)
+            field = out[0]
             if not last:
                 q, msg_a, msg_b = out[1:4]
-                state = (out[0], *out[4:])
-        frames.append(out[0])
+                state = out[4:]
+        frames.append(field)
 
     done = jnp.stack(frames).reshape(STEPS, N, HALF, width)
     got = lax.ppermute(jnp.flip(done[:, ROWS:], 1), "row", swap)

time: 151 us -> 151 us (level)
  waiting for transfers between devices: 76.5 us -> 54.3 us
  Pallas kernels: 15 us -> 21.8 us
  local copies, waits for them, and re-layouts: 1.12 us -> 7.68 us
  other arithmetic: 1.56 us -> 5.7 us
  starting transfers between devices: 55.4 us -> 57.8 us
    ppermute x2, waiting for transfers between devices: 15.4 us -> 0.01 us  [shards_chain(): recv.append(lax.ppermute(send, 'row', swap))]
    ppermute x16, waiting for transfers between devices: 37.1 us -> 30.1 us  [shards_chain(): got_b = lax.ppermute(msg_b, both, b_pairs)]
    pallas_call x18 -> x36, Pallas kernels: 15 us -> 21.8 us  [the longest x33 15.2 us: call(): pl.pallas_call(body, out_shape=outs, in_specs=[vmem] * len(ins), out_spec...]
    ppermute x16, starting transfers between devices: 37.5 us -> 42.7 us  [shards_chain(): got_b = lax.ppermute(msg_b, both, b_pairs)]
    ppermute x16, waiting for transfers between devices: 18.6 us -> 16.5 us  [shards_chain(): got_a = lax.ppermute(msg_a, 'row', swap)]
    all_to_all x1, waiting for transfers between devices: 0.7 us -> 2.73 us  [collect(): lax.all_to_all(packed, 'col', split_axis=2, concat_axis=1, tiled=True)]
    all_to_all x1, local copies, waits for them, and re-layouts: 0.01 us -> 1.59 us  [collect(): lax.all_to_all(packed, 'col', split_axis=2, concat_axis=1, tiled=True)]
  transfers between devices with their start and end apart: 38 -> 38, of which waited for: 35 -> 35; matrix products, arithmetic and copies ran while one was open for 1% -> 8% of each run, Pallas kernels for 0% -> 6%
where the time goes in v8:
time: 151 us; the launch traced here: 149 us
  starting transfers between devices  57.8 us (38%)
  waiting for transfers between devices  54.3 us (36%)
  Pallas kernels  21.8 us (14%)
  local copies, waits for them, and re-layouts  7.68 us (5%)
  other arithmetic  5.7 us (4%)
    ppermute x16, starting transfers between devices, shards_chain(): got_b = lax.ppermute(msg_b, both, b_pairs)  42.7 us
    ppermute x16, waiting for transfers between devices, shards_chain(): got_b = lax.ppermute(msg_b, both, b_pairs)  30.1 us
    ppermute x16, waiting for transfers between devices, shards_chain(): got_a = lax.ppermute(msg_a, 'row', swap)  16.5 us
    pallas_call x33, Pallas kernels, call(): pl.pallas_call(body, out_shape=outs, in_specs=[vmem] * len(ins), out_spec...  15.2 us
    pallas_call x3, Pallas kernels, pack(): pl.pallas_call(functools.partial(pack_kernel, n_col, sent, first, count),...  6.58 us
    all_to_all x1, starting transfers between devices, collect(): lax.all_to_all(packed, 'col', split_axis=2, concat_axis=1, tiled=True)  6.27 us
    ppermute x1, waiting for transfers between devices, shards_chain(): got = lax.ppermute(jnp.flip(done[:, ROWS:], 1), 'row', swap)  3.63 us
    ppermute x1, starting transfers between devices, beside(): beyond_0 = lax.ppermute(facing_0, both, b_pairs)  3.11 us
  transfers between devices with their start and end apart: 38, of which 35 were waited for; matrix products, arithmetic and copies ran while one was open for 8% of the time, Pallas kernels for 6%

profile of v8, /device:TPU:8, one launch (start us, length us, event | category | flops | bytes accessed | tf_op | source)
XLA Modules:
  0.0 149.1 jit_solution(17222660987543853174)
XLA Ops:
  0.8 1.9 %pack.4 = f32[12,128,128]{2,1,0:T(8,128)S(1)} custom-call(s32[2]{0:T(128)S(1)} %pad_add_fusion.place_ref, s32[2,4,4]{2,1,0:T(4,128)S(1)} %copy-done, f32[2,4,128,128]{3,2,1,0:T(8,128)} %own_hbm.5, f32[4,2,4,128,128]{4,3,2,1,0:T(8,128)} %nb_hbm.5), custom_call_target="tpu_custom_call" | custom-call | tf_op jit(solution)/shard_map/pack/pallas_call | solution.py:433
  2.7 1.6 %collective-permute-start.2 = (f32[12,128,128]{2,1,0:T(8,128)S(1)}, f32[12,128,128]{2,1,0:T(8,128)S(1)}, u32[]{:S(2)}, u32[]{:S(2)}) collective-permute-start(f32[12,128,128]{2,1,0:T(8,128)S(1)} %pack.4), channel_id=1, source_target_pairs={{0,16},{16,0},{1,17},{17,1},{2,18},{18,2},{3,19},{19,3},{4,20},{20... | collective-permute-start | bytes 2359304 | tf_op jit(solution)/shard_map/ppermute | solution.py:446
  4.2 2.6 %pack.5 = f32[8,128,128]{2,1,0:T(8,128)} custom-call(s32[2]{0:T(128)S(1)} %pad_add_fusion.place_ref, s32[2,4,4]{2,1,0:T(4,128)S(1)} %copy-done, f32[2,4,128,128]{3,2,1,0:T(8,128)} %own_hbm.5, f32[4,2,4,128,128]{4,3,2,1,0:T(8,128)} %nb_hbm.5), custom_call_target="tpu_custom_call" | custom-call | tf_op jit(solution)/shard_map/pack/pallas_call | solution.py:433
  7.4 2.1 %pack.3 = (f32[20,128,128]{2,1,0:T(8,128)S(1)}, f32[2,128,128]{2,1,0:T(8,128)S(1)}) custom-call(s32[2]{0:T(128)S(1)} %pad_add_fusion.place_ref, s32[2,4,4]{2,1,0:T(4,128)S(1)} %copy-done.1, f32[2,4,128,128]{3,2,1,0:T(8,128)} %own_hbm.5, f32[4,2,4,128,128]{4,3,2,1,0:T(8,128)} %nb_hbm.5), custom_call_target="tpu_custom_call" | custom-call | tf_op jit(solution)/shard_map/pack/pallas_call | solution.py:433
  9.5 27.5 %conditional.1 = (f32[48,128]{1,0:T(8,128)S(1)}, f32[2,128,128]{2,1,0:T(8,128)S(1)}, f32[8,128]{1,0:T(8,128)S(1)}) conditional(s32[]{:T(128)} %convert_element_type.9, f32[2,128,128]{2,1,0:T(8,128)S(1)} %get-tuple-element.153, (s32[]{:T(128)}, s32[]{:T(128)}, s32[1,1,16,4]{2,3,1,0:T(4,128)}, f32[1,1,16,4,512]{4,3,2,1,0:T(4,128)}, ...), branch_computations={%region_0.1_spmd, %region_1.2_spmd} | conditional | flops 3300930 | bytes 2759352 | solution.py:461
  10.3 1.0 copy.22
  12.2 6.3 %all-to-all-start = ((f32[1,1,16,5,512]{4,1,3,0,2:T(1,128)}), f32[1,1,16,5,512]{4,1,3,0,2:T(1,128)}, u32[]{:S(2)}, u32[]{:S(2)}) async-start(f32[1,1,16,5,512]{4,1,3,0,2:T(1,128)} %fusion), calls=%async_computation | async-start | bytes 327680 | tf_op jit(solution)/shard_map/cond/branch_1_fun/all_to_all | solution.py:131
  18.4 3.1 %collective-permute-start.1 = (f32[2,128,128]{2,1,0:T(8,128)S(1)}, f32[2,128,128]{2,1,0:T(8,128)}, u32[]{:S(2)}, u32[]{:S(2)}) collective-permute-start(f32[2,128,128]{2,1,0:T(8,128)S(1)} %get-tuple-element.27), channel_id=1, source_target_pairs={{16,17},{17,16},{1,2},{2,1},{18,19},{19,18},{3,4},{4,3},{20,21},{2... | collective-permute-start | bytes 393224 | tf_op jit(solution)/shard_map/cond/branch_1_fun/ppermute | solution.py:450
  21.6 2.7 %all-to-all-done = f32[1,1,16,5,512]{4,1,3,0,2:T(1,128)} async-done(((f32[1,1,16,5,512]{4,1,3,0,2:T(1,128)}), f32[1,1,16,5,512]{4,1,3,0,2:T(1,128)}, u32[]{:S(2)}, u32[]{:S(2)}) %all-to-all-start) | async-done | bytes 163872 | tf_op jit(solution)/shard_map/cond/branch_1_fun/all_to_all | solution.py:131
  24.3 1.6 %copy.25 = f32[1,1,16,5,512]{4,2,3,1,0:T(8,128)} copy(f32[1,1,16,5,512]{4,1,3,0,2:T(1,128)} %all-to-all-done) | data formatting | bytes 327680 | tf_op jit(solution)/shard_map/cond/branch_1_fun/all_to_all | solution.py:131
  26.7 1.1 fusion.1
  29.8 1.4 broadcast_select_fusion.1
  31.1 1.5 %collective-permute-start = (f32[6,2,2,128]{3,2,1,0:T(2,128)S(1)}, f32[6,2,2,128]{3,2,1,0:T(2,128)}, u32[]{:S(2)}, u32[]{:S(2)}) collective-permute-start(f32[6,2,2,128]{3,2,1,0:T(2,128)S(1)} %get-tuple-element.306), channel_id=1, source_target_pairs={{0,16},{16,0},{1,17},{17,1},{2,18},{18,2},{3,19},{19,3},{4,20},{20... | collective-permute-start | bytes 36872 | tf_op jit(solution)/shard_map/cond/branch_1_fun/ppermute | solution.py:457
  33.6 1.4 collective-permute-done
  38.7 2.7 %collective-permute-start.5 = (f32[264,128]{1,0:T(8,128)S(1)}, f32[264,128]{1,0:T(8,128)S(1)}, u32[]{:S(2)}, u32[]{:S(2)}) collective-permute-start(f32[264,128]{1,0:T(8,128)S(1)} %get-tuple-element.156), channel_id=1, source_target_pairs={{16,17},{17,16},{1,2},{2,1},{18,19},{19,18},{3,4},{4,3},{20,21},{2... | collective-permute-start | bytes 405512 | tf_op jit(solution)/shard_map/ppermute | solution.py:494
  42.3 2.7 %collective-permute-done.4.got_a = f32[8,128]{1,0:T(8,128)S(1)} collective-permute-done((f32[8,128]{1,0:T(8,128)S(1)}, f32[8,128]{1,0:T(8,128)S(1)}, u32[]{:S(2)}, u32[]{:S(2)}) %collective-permute-start.4) | collective-permute-done | bytes 4128 | tf_op jit(solution)/shard_map/ppermute | solution.py:495
  45.0 1.0 collective-permute-done.5.first_b.got_b
  47.0 2.7 %collective-permute-start.7 = (f32[8,128]{1,0:T(8,128)S(1)}, f32[8,128]{1,0:T(8,128)S(1)}, u32[]{:S(2)}, u32[]{:S(2)}) collective-permute-start(f32[8,128]{1,0:T(8,128)S(1)} %get-tuple-element.163), channel_id=1, source_target_pairs={{16,17},{17,16},{1,2},{2,1},{18,19},{19,18},{3,4},{4,3},{20,21},{2... | collective-permute-start | bytes 12296 | tf_op jit(solution)/shard_map/ppermute | solution.py:494
  50.9 1.9 %collective-permute-done.7.got_b = f32[8,128]{1,0:T(8,128)S(1)} collective-permute-done((f32[8,128]{1,0:T(8,128)S(1)}, f32[8,128]{1,0:T(8,128)S(1)}, u32[]{:S(2)}, u32[]{:S(2)}) %collective-permute-start.7) | collective-permute-done | bytes 4128 | tf_op jit(solution)/shard_map/ppermute | solution.py:494
  53.5 2.7 %collective-permute-start.9 = (f32[8,128]{1,0:T(8,128)S(1)}, f32[8,128]{1,0:T(8,128)S(1)}, u32[]{:S(2)}, u32[]{:S(2)}) collective-permute-start(f32[8,128]{1,0:T(8,128)S(1)} %get-tuple-element.171), channel_id=1, source_target_pairs={{16,17},{17,16},{1,2},{2,1},{18,19},{19,18},{3,4},{4,3},{20,21},{2... | collective-permute-start | bytes 12296 | tf_op jit(solution)/shard_map/ppermute | solution.py:494
  57.4 1.9 %collective-permute-done.9.got_b = f32[8,128]{1,0:T(8,128)S(1)} collective-permute-done((f32[8,128]{1,0:T(8,128)S(1)}, f32[8,128]{1,0:T(8,128)S(1)}, u32[]{:S(2)}, u32[]{:S(2)}) %collective-permute-start.9) | collective-permute-done | bytes 4128 | tf_op jit(solution)/shard_map/ppermute | solution.py:494
  60.1 2.7 %collective-permute-start.11 = (f32[8,128]{1,0:T(8,128)S(1)}, f32[8,128]{1,0:T(8,128)S(1)}, u32[]{:S(2)}, u32[]{:S(2)}) collective-permute-start(f32[8,128]{1,0:T(8,128)S(1)} %get-tuple-element.179), channel_id=1, source_target_pairs={{16,17},{17,16},{1,2},{2,1},{18,19},{19,18},{3,4},{4,3},{20,21},{2... | collective-permute-start | bytes 12296 | tf_op jit(solution)/shard_map/ppermute | solution.py:494
  63.9 1.9 %collective-permute-done.11.got_b = f32[8,128]{1,0:T(8,128)S(1)} collective-permute-done((f32[8,128]{1,0:T(8,128)S(1)}, f32[8,128]{1,0:T(8,128)S(1)}, u32[]{:S(2)}, u32[]{:S(2)}) %collective-permute-start.11) | collective-permute-done | bytes 4128 | tf_op jit(solution)/shard_map/ppermute | solution.py:494
  66.6 2.7 %collective-permute-start.13 = (f32[8,128]{1,0:T(8,128)S(1)}, f32[8,128]{1,0:T(8,128)S(1)}, u32[]{:S(2)}, u32[]{:S(2)}) collective-permute-start(f32[8,128]{1,0:T(8,128)S(1)} %get-tuple-element.188), channel_id=1, source_target_pairs={{16,17},{17,16},{1,2},{2,1},{18,19},{19,18},{3,4},{4,3},{20,21},{2... | collective-permute-start | bytes 12296 | tf_op jit(solution)/shard_map/ppermute | solution.py:494
  70.5 1.9 %collective-permute-done.13.got_b = f32[8,128]{1,0:T(8,128)S(1)} collective-permute-done((f32[8,128]{1,0:T(8,128)S(1)}, f32[8,128]{1,0:T(8,128)S(1)}, u32[]{:S(2)}, u32[]{:S(2)}) %collective-permute-start.13) | collective-permute-done | bytes 4128 | tf_op jit(solution)/shard_map/ppermute | solution.py:494
  73.1 2.7 %collective-permute-start.15 = (f32[8,128]{1,0:T(8,128)S(1)}, f32[8,128]{1,0:T(8,128)S(1)}, u32[]{:S(2)}, u32[]{:S(2)}) collective-permute-start(f32[8,128]{1,0:T(8,128)S(1)} %get-tuple-element.193), channel_id=1, source_target_pairs={{16,17},{17,16},{1,2},{2,1},{18,19},{19,18},{3,4},{4,3},{20,21},{2... | collective-permute-start | bytes 12296 | tf_op jit(solution)/shard_map/ppermute | solution.py:494
  77.0 1.9 %collective-permute-done.15.got_b = f32[8,128]{1,0:T(8,128)S(1)} collective-permute-done((f32[8,128]{1,0:T(8,128)S(1)}, f32[8,128]{1,0:T(8,128)S(1)}, u32[]{:S(2)}, u32[]{:S(2)}) %collective-permute-start.15) | collective-permute-done | bytes 4128 | tf_op jit(solution)/shard_map/ppermute | solution.py:494
  79.6 2.7 %collective-permute-start.17 = (f32[8,128]{1,0:T(8,128)S(1)}, f32[8,128]{1,0:T(8,128)S(1)}, u32[]{:S(2)}, u32[]{:S(2)}) collective-permute-start(f32[8,128]{1,0:T(8,128)S(1)} %get-tuple-element.201), channel_id=1, source_target_pairs={{16,17},{17,16},{1,2},{2,1},{18,19},{19,18},{3,4},{4,3},{20,21},{2... | collective-permute-start | bytes 12296 | tf_op jit(solution)/shard_map/ppermute | solution.py:494
  83.5 1.9 %collective-permute-done.17.got_b = f32[8,128]{1,0:T(8,128)S(1)} collective-permute-done((f32[8,128]{1,0:T(8,128)S(1)}, f32[8,128]{1,0:T(8,128)S(1)}, u32[]{:S(2)}, u32[]{:S(2)}) %collective-permute-start.17) | collective-permute-done | bytes 4128 | tf_op jit(solution)/shard_map/ppermute | solution.py:494
  86.2 2.7 %collective-permute-start.19 = (f32[8,128]{1,0:T(8,128)S(1)}, f32[8,128]{1,0:T(8,128)S(1)}, u32[]{:S(2)}, u32[]{:S(2)}) collective-permute-start(f32[8,128]{1,0:T(8,128)S(1)} %get-tuple-element.209), channel_id=1, source_target_pairs={{16,17},{17,16},{1,2},{2,1},{18,19},{19,18},{3,4},{4,3},{20,21},{2... | collective-permute-start | bytes 12296 | tf_op jit(solution)/shard_map/ppermute | solution.py:494
  90.1 1.9 %collective-permute-done.19.got_b = f32[8,128]{1,0:T(8,128)S(1)} collective-permute-done((f32[8,128]{1,0:T(8,128)S(1)}, f32[8,128]{1,0:T(8,128)S(1)}, u32[]{:S(2)}, u32[]{:S(2)}) %collective-permute-start.19) | collective-permute-done | bytes 4128 | tf_op jit(solution)/shard_map/ppermute | solution.py:494
  92.7 2.7 %collective-permute-start.21 = (f32[8,128]{1,0:T(8,128)S(1)}, f32[8,128]{1,0:T(8,128)S(1)}, u32[]{:S(2)}, u32[]{:S(2)}) collective-permute-start(f32[8,128]{1,0:T(8,128)S(1)} %get-tuple-element.218), channel_id=1, source_target_pairs={{16,17},{17,16},{1,2},{2,1},{18,19},{19,18},{3,4},{4,3},{20,21},{2... | collective-permute-start | bytes 12296 | tf_op jit(solution)/shard_map/ppermute | solution.py:494
  96.6 1.9 %collective-permute-done.21.got_b = f32[8,128]{1,0:T(8,128)S(1)} collective-permute-done((f32[8,128]{1,0:T(8,128)S(1)}, f32[8,128]{1,0:T(8,128)S(1)}, u32[]{:S(2)}, u32[]{:S(2)}) %collective-permute-start.21) | collective-permute-done | bytes 4128 | tf_op jit(solution)/shard_map/ppermute | solution.py:494
  99.2 2.8 %collective-permute-start.23 = (f32[8,128]{1,0:T(8,128)S(1)}, f32[8,128]{1,0:T(8,128)S(1)}, u32[]{:S(2)}, u32[]{:S(2)}) collective-permute-start(f32[8,128]{1,0:T(8,128)S(1)} %get-tuple-element.223), channel_id=1, source_target_pairs={{16,17},{17,16},{1,2},{2,1},{18,19},{19,18},{3,4},{4,3},{20,21},{2... | collective-permute-start | bytes 12296 | tf_op jit(solution)/shard_map/ppermute | solution.py:494
  103.1 1.9 %collective-permute-done.23.got_b = f32[8,128]{1,0:T(8,128)S(1)} collective-permute-done((f32[8,128]{1,0:T(8,128)S(1)}, f32[8,128]{1,0:T(8,128)S(1)}, u32[]{:S(2)}, u32[]{:S(2)}) %collective-permute-start.23) | collective-permute-done | bytes 4128 | tf_op jit(solution)/shard_map/ppermute | solution.py:494
  105.8 2.7 %collective-permute-start.25 = (f32[8,128]{1,0:T(8,128)S(1)}, f32[8,128]{1,0:T(8,128)S(1)}, u32[]{:S(2)}, u32[]{:S(2)}) collective-permute-start(f32[8,128]{1,0:T(8,128)S(1)} %get-tuple-element.231), channel_id=1, source_target_pairs={{16,17},{17,16},{1,2},{2,1},{18,19},{19,18},{3,4},{4,3},{20,21},{2... | collective-permute-start | bytes 12296 | tf_op jit(solution)/shard_map/ppermute | solution.py:494
  109.6 1.9 %collective-permute-done.25.got_b = f32[8,128]{1,0:T(8,128)S(1)} collective-permute-done((f32[8,128]{1,0:T(8,128)S(1)}, f32[8,128]{1,0:T(8,128)S(1)}, u32[]{:S(2)}, u32[]{:S(2)}) %collective-permute-start.25) | collective-permute-done | bytes 4128 | tf_op jit(solution)/shard_map/ppermute | solution.py:494
  112.3 2.7 %collective-permute-start.27 = (f32[8,128]{1,0:T(8,128)S(1)}, f32[8,128]{1,0:T(8,128)S(1)}, u32[]{:S(2)}, u32[]{:S(2)}) collective-permute-start(f32[8,128]{1,0:T(8,128)S(1)} %get-tuple-element.239), channel_id=1, source_target_pairs={{16,17},{17,16},{1,2},{2,1},{18,19},{19,18},{3,4},{4,3},{20,21},{2... | collective-permute-start | bytes 12296 | tf_op jit(solution)/shard_map/ppermute | solution.py:494
  116.2 1.9 %collective-permute-done.27.got_b = f32[8,128]{1,0:T(8,128)S(1)} collective-permute-done((f32[8,128]{1,0:T(8,128)S(1)}, f32[8,128]{1,0:T(8,128)S(1)}, u32[]{:S(2)}, u32[]{:S(2)}) %collective-permute-start.27) | collective-permute-done | bytes 4128 | tf_op jit(solution)/shard_map/ppermute | solution.py:494
  118.8 2.7 %collective-permute-start.29 = (f32[8,128]{1,0:T(8,128)S(1)}, f32[8,128]{1,0:T(8,128)S(1)}, u32[]{:S(2)}, u32[]{:S(2)}) collective-permute-start(f32[8,128]{1,0:T(8,128)S(1)} %get-tuple-element.248), channel_id=1, source_target_pairs={{16,17},{17,16},{1,2},{2,1},{18,19},{19,18},{3,4},{4,3},{20,21},{2... | collective-permute-start | bytes 12296 | tf_op jit(solution)/shard_map/ppermute | solution.py:494
  122.7 1.9 %collective-permute-done.29.got_b = f32[8,128]{1,0:T(8,128)S(1)} collective-permute-done((f32[8,128]{1,0:T(8,128)S(1)}, f32[8,128]{1,0:T(8,128)S(1)}, u32[]{:S(2)}, u32[]{:S(2)}) %collective-permute-start.29) | collective-permute-done | bytes 4128 | tf_op jit(solution)/shard_map/ppermute | solution.py:494
  125.3 2.7 %collective-permute-start.31 = (f32[8,128]{1,0:T(8,128)S(1)}, f32[8,128]{1,0:T(8,128)S(1)}, u32[]{:S(2)}, u32[]{:S(2)}) collective-permute-start(f32[8,128]{1,0:T(8,128)S(1)} %get-tuple-element.253), channel_id=1, source_target_pairs={{16,17},{17,16},{1,2},{2,1},{18,19},{19,18},{3,4},{4,3},{20,21},{2... | collective-permute-start | bytes 12296 | tf_op jit(solution)/shard_map/ppermute | solution.py:494
  129.2 1.9 %collective-permute-done.31.got_b = f32[8,128]{1,0:T(8,128)S(1)} collective-permute-done((f32[8,128]{1,0:T(8,128)S(1)}, f32[8,128]{1,0:T(8,128)S(1)}, u32[]{:S(2)}, u32[]{:S(2)}) %collective-permute-start.31) | collective-permute-done | bytes 4128 | tf_op jit(solution)/shard_map/ppermute | solution.py:494
  131.9 2.7 %collective-permute-start.33 = (f32[8,128]{1,0:T(8,128)S(1)}, f32[8,128]{1,0:T(8,128)S(1)}, u32[]{:S(2)}, u32[]{:S(2)}) collective-permute-start(f32[8,128]{1,0:T(8,128)S(1)} %get-tuple-element.261), channel_id=1, source_target_pairs={{16,17},{17,16},{1,2},{2,1},{18,19},{19,18},{3,4},{4,3},{20,21},{2... | collective-permute-start | bytes 12296 | tf_op jit(solution)/shard_map/ppermute | solution.py:494
  135.8 1.9 %collective-permute-done.33.got_b = f32[8,128]{1,0:T(8,128)S(1)} collective-permute-done((f32[8,128]{1,0:T(8,128)S(1)}, f32[8,128]{1,0:T(8,128)S(1)}, u32[]{:S(2)}, u32[]{:S(2)}) %collective-permute-start.33) | collective-permute-done | bytes 4128 | tf_op jit(solution)/shard_map/ppermute | solution.py:494
  138.4 2.7 %collective-permute-start.35 = (f32[8,128]{1,0:T(8,128)S(1)}, f32[8,128]{1,0:T(8,128)S(1)}, u32[]{:S(2)}, u32[]{:S(2)}) collective-permute-start(f32[8,128]{1,0:T(8,128)S(1)} %get-tuple-element.269), channel_id=1, source_target_pairs={{16,17},{17,16},{1,2},{2,1},{18,19},{19,18},{3,4},{4,3},{20,21},{2... | collective-permute-start | bytes 12296 | tf_op jit(solution)/shard_map/ppermute | solution.py:494
  142.3 1.9 %collective-permute-done.35.got_b = f32[8,128]{1,0:T(8,128)S(1)} collective-permute-done((f32[8,128]{1,0:T(8,128)S(1)}, f32[8,128]{1,0:T(8,128)S(1)}, u32[]{:S(2)}, u32[]{:S(2)}) %collective-permute-start.35) | collective-permute-done | bytes 4128 | tf_op jit(solution)/shard_map/ppermute | solution.py:494
  144.7 3.6 %collective-permute-done.36 = f32[4,2,2,128]{3,2,1,0:T(2,128)S(1)} collective-permute-done((f32[4,2,2,128]{3,2,1,0:T(2,128)S(1)}, f32[4,2,2,128]{3,2,1,0:T(2,128)S(1)}, u32[]{:S(2)}, u32[]{:S(2)}) %collective-permute-start.36) | collective-permute-done | bytes 8224 | tf_op jit(solution)/shard_map/ppermute | solution.py:508
  (100 shorter events, 41.1 us)
Async XLA Ops:
  0.1 0.7 copy-start
  2.7 4.8 %copy-start.1 = (s32[2,4,4]{2,1,0:T(4,128)S(1)}, s32[2,4,4]{2,1,0:T(4,128)}, u32[]{:S(2)}) copy-start(s32[2,4,4]{2,1,0:T(4,128)} %pattern_ref.5) | copy-start | bytes 388
  2.7 34.4 %collective-permute-start.2 = (f32[12,128,128]{2,1,0:T(8,128)S(1)}, f32[12,128,128]{2,1,0:T(8,128)S(1)}, u32[]{:S(2)}, u32[]{:S(2)}) collective-permute-start(f32[12,128,128]{2,1,0:T(8,128)S(1)} %pack.4), channel_id=1, source_target_pairs={{0,16},{16,0},{1,17},{17,1},{2,18},{18,2},{3,19},{19,3},{4,20},{20... | collective-permute-start | bytes 2359304 | tf_op jit(solution)/shard_map/ppermute | solution.py:446
  6.8 30.2 %collective-permute-start.3 = (f32[8,128,128]{2,1,0:T(8,128)}, f32[8,128,128]{2,1,0:T(8,128)S(1)}, u32[]{:S(2)}, u32[]{:S(2)}) collective-permute-start(f32[8,128,128]{2,1,0:T(8,128)} %pack.5), channel_id=1, source_target_pairs={{0,16},{16,0},{1,17},{17,1},{2,18},{18,2},{3,19},{19,3},{4,20},{20... | collective-permute-start | bytes 1572872 | tf_op jit(solution)/shard_map/ppermute | solution.py:446
  12.2 12.1 %all-to-all-start = ((f32[1,1,16,5,512]{4,1,3,0,2:T(1,128)}), f32[1,1,16,5,512]{4,1,3,0,2:T(1,128)}, u32[]{:S(2)}, u32[]{:S(2)}) async-start(f32[1,1,16,5,512]{4,1,3,0,2:T(1,128)} %fusion), calls=%async_computation | async-start | bytes 327680 | tf_op jit(solution)/shard_map/cond/branch_1_fun/all_to_all | solution.py:131
  18.4 14.2 %collective-permute-start.1 = (f32[2,128,128]{2,1,0:T(8,128)S(1)}, f32[2,128,128]{2,1,0:T(8,128)}, u32[]{:S(2)}, u32[]{:S(2)}) collective-permute-start(f32[2,128,128]{2,1,0:T(8,128)S(1)} %get-tuple-element.27), channel_id=1, source_target_pairs={{16,17},{17,16},{1,2},{2,1},{18,19},{19,18},{3,4},{4,3},{20,21},{2... | collective-permute-start | bytes 393224 | tf_op jit(solution)/shard_map/cond/branch_1_fun/ppermute | solution.py:450
  28.5 0.6 copy-start.4
  31.1 3.8 %collective-permute-start = (f32[6,2,2,128]{3,2,1,0:T(2,128)S(1)}, f32[6,2,2,128]{3,2,1,0:T(2,128)}, u32[]{:S(2)}, u32[]{:S(2)}) collective-permute-start(f32[6,2,2,128]{3,2,1,0:T(2,128)S(1)} %get-tuple-element.306), channel_id=1, source_target_pairs={{0,16},{16,0},{1,17},{17,1},{2,18},{18,2},{3,19},{19,3},{4,20},{20... | collective-permute-start | bytes 36872 | tf_op jit(solution)/shard_map/cond/branch_1_fun/ppermute | solution.py:457
  37.1 0.6 copy-start.2
  38.6 7.6 %copy-start.3 = (f32[48,128]{1,0:T(8,128)S(1)}, f32[48,128]{1,0:T(8,128)}, u32[]{:S(2)}) copy-start(f32[48,128]{1,0:T(8,128)} %copy-done.2) | copy-start | bytes 73732
  38.7 7.3 %collective-permute-start.5 = (f32[264,128]{1,0:T(8,128)S(1)}, f32[264,128]{1,0:T(8,128)S(1)}, u32[]{:S(2)}, u32[]{:S(2)}) collective-permute-start(f32[264,128]{1,0:T(8,128)S(1)} %get-tuple-element.156), channel_id=1, source_target_pairs={{16,17},{17,16},{1,2},{2,1},{18,19},{19,18},{3,4},{4,3},{20,21},{2... | collective-permute-start | bytes 405512 | tf_op jit(solution)/shard_map/ppermute | solution.py:494
  41.3 3.7 %collective-permute-start.4 = (f32[8,128]{1,0:T(8,128)S(1)}, f32[8,128]{1,0:T(8,128)S(1)}, u32[]{:S(2)}, u32[]{:S(2)}) collective-permute-start(f32[8,128]{1,0:T(8,128)S(1)} %get-tuple-element.155), channel_id=1, source_target_pairs={{0,16},{16,0},{1,17},{17,1},{2,18},{18,2},{3,19},{19,3},{4,20},{20... | collective-permute-start | bytes 12296 | tf_op jit(solution)/shard_map/ppermute | solution.py:495
  46.9 3.7 %collective-permute-start.6 = (f32[8,128]{1,0:T(8,128)S(1)}, f32[8,128]{1,0:T(8,128)S(1)}, u32[]{:S(2)}, u32[]{:S(2)}) collective-permute-start(f32[8,128]{1,0:T(8,128)S(1)} %get-tuple-element.162), channel_id=1, source_target_pairs={{0,16},{16,0},{1,17},{17,1},{2,18},{18,2},{3,19},{19,3},{4,20},{20... | collective-permute-start | bytes 12296 | tf_op jit(solution)/shard_map/ppermute | solution.py:495
  47.0 5.8 %collective-permute-start.7 = (f32[8,128]{1,0:T(8,128)S(1)}, f32[8,128]{1,0:T(8,128)S(1)}, u32[]{:S(2)}, u32[]{:S(2)}) collective-permute-start(f32[8,128]{1,0:T(8,128)S(1)} %get-tuple-element.163), channel_id=1, source_target_pairs={{16,17},{17,16},{1,2},{2,1},{18,19},{19,18},{3,4},{4,3},{20,21},{2... | collective-permute-start | bytes 12296 | tf_op jit(solution)/shard_map/ppermute | solution.py:494
  53.4 3.7 %collective-permute-start.8 = (f32[8,128]{1,0:T(8,128)S(1)}, f32[8,128]{1,0:T(8,128)S(1)}, u32[]{:S(2)}, u32[]{:S(2)}) collective-permute-start(f32[8,128]{1,0:T(8,128)S(1)} %get-tuple-element.170), channel_id=1, source_target_pairs={{0,16},{16,0},{1,17},{17,1},{2,18},{18,2},{3,19},{19,3},{4,20},{20... | collective-permute-start | bytes 12296 | tf_op jit(solution)/shard_map/ppermute | solution.py:495
  53.5 5.8 %collective-permute-start.9 = (f32[8,128]{1,0:T(8,128)S(1)}, f32[8,128]{1,0:T(8,128)S(1)}, u32[]{:S(2)}, u32[]{:S(2)}) collective-permute-start(f32[8,128]{1,0:T(8,128)S(1)} %get-tuple-element.171), channel_id=1, source_target_pairs={{16,17},{17,16},{1,2},{2,1},{18,19},{19,18},{3,4},{4,3},{20,21},{2... | collective-permute-start | bytes 12296 | tf_op jit(solution)/shard_map/ppermute | solution.py:494
  60.0 3.7 %collective-permute-start.10 = (f32[8,128]{1,0:T(8,128)S(1)}, f32[8,128]{1,0:T(8,128)S(1)}, u32[]{:S(2)}, u32[]{:S(2)}) collective-permute-start(f32[8,128]{1,0:T(8,128)S(1)} %get-tuple-element.178), channel_id=1, source_target_pairs={{0,16},{16,0},{1,17},{17,1},{2,18},{18,2},{3,19},{19,3},{4,20},{20... | collective-permute-start | bytes 12296 | tf_op jit(solution)/shard_map/ppermute | solution.py:495
  60.1 5.8 %collective-permute-start.11 = (f32[8,128]{1,0:T(8,128)S(1)}, f32[8,128]{1,0:T(8,128)S(1)}, u32[]{:S(2)}, u32[]{:S(2)}) collective-permute-start(f32[8,128]{1,0:T(8,128)S(1)} %get-tuple-element.179), channel_id=1, source_target_pairs={{16,17},{17,16},{1,2},{2,1},{18,19},{19,18},{3,4},{4,3},{20,21},{2... | collective-permute-start | bytes 12296 | tf_op jit(solution)/shard_map/ppermute | solution.py:494
  66.5 3.7 %collective-permute-start.12 = (f32[8,128]{1,0:T(8,128)S(1)}, f32[8,128]{1,0:T(8,128)S(1)}, u32[]{:S(2)}, u32[]{:S(2)}) collective-permute-start(f32[8,128]{1,0:T(8,128)S(1)} %get-tuple-element.187), channel_id=1, source_target_pairs={{0,16},{16,0},{1,17},{17,1},{2,18},{18,2},{3,19},{19,3},{4,20},{20... | collective-permute-start | bytes 12296 | tf_op jit(solution)/shard_map/ppermute | solution.py:495
  66.6 5.8 %collective-permute-start.13 = (f32[8,128]{1,0:T(8,128)S(1)}, f32[8,128]{1,0:T(8,128)S(1)}, u32[]{:S(2)}, u32[]{:S(2)}) collective-permute-start(f32[8,128]{1,0:T(8,128)S(1)} %get-tuple-element.188), channel_id=1, source_target_pairs={{16,17},{17,16},{1,2},{2,1},{18,19},{19,18},{3,4},{4,3},{20,21},{2... | collective-permute-start | bytes 12296 | tf_op jit(solution)/shard_map/ppermute | solution.py:494
  73.0 3.7 %collective-permute-start.14 = (f32[8,128]{1,0:T(8,128)S(1)}, f32[8,128]{1,0:T(8,128)S(1)}, u32[]{:S(2)}, u32[]{:S(2)}) collective-permute-start(f32[8,128]{1,0:T(8,128)S(1)} %get-tuple-element.192), channel_id=1, source_target_pairs={{0,16},{16,0},{1,17},{17,1},{2,18},{18,2},{3,19},{19,3},{4,20},{20... | collective-permute-start | bytes 12296 | tf_op jit(solution)/shard_map/ppermute | solution.py:495
  73.1 5.8 %collective-permute-start.15 = (f32[8,128]{1,0:T(8,128)S(1)}, f32[8,128]{1,0:T(8,128)S(1)}, u32[]{:S(2)}, u32[]{:S(2)}) collective-permute-start(f32[8,128]{1,0:T(8,128)S(1)} %get-tuple-element.193), channel_id=1, source_target_pairs={{16,17},{17,16},{1,2},{2,1},{18,19},{19,18},{3,4},{4,3},{20,21},{2... | collective-permute-start | bytes 12296 | tf_op jit(solution)/shard_map/ppermute | solution.py:494
  79.6 3.7 %collective-permute-start.16 = (f32[8,128]{1,0:T(8,128)S(1)}, f32[8,128]{1,0:T(8,128)S(1)}, u32[]{:S(2)}, u32[]{:S(2)}) collective-permute-start(f32[8,128]{1,0:T(8,128)S(1)} %get-tuple-element.200), channel_id=1, source_target_pairs={{0,16},{16,0},{1,17},{17,1},{2,18},{18,2},{3,19},{19,3},{4,20},{20... | collective-permute-start | bytes 12296 | tf_op jit(solution)/shard_map/ppermute | solution.py:495
  79.6 5.8 %collective-permute-start.17 = (f32[8,128]{1,0:T(8,128)S(1)}, f32[8,128]{1,0:T(8,128)S(1)}, u32[]{:S(2)}, u32[]{:S(2)}) collective-permute-start(f32[8,128]{1,0:T(8,128)S(1)} %get-tuple-element.201), channel_id=1, source_target_pairs={{16,17},{17,16},{1,2},{2,1},{18,19},{19,18},{3,4},{4,3},{20,21},{2... | collective-permute-start | bytes 12296 | tf_op jit(solution)/shard_map/ppermute | solution.py:494
  86.1 3.7 %collective-permute-start.18 = (f32[8,128]{1,0:T(8,128)S(1)}, f32[8,128]{1,0:T(8,128)S(1)}, u32[]{:S(2)}, u32[]{:S(2)}) collective-permute-start(f32[8,128]{1,0:T(8,128)S(1)} %get-tuple-element.208), channel_id=1, source_target_pairs={{0,16},{16,0},{1,17},{17,1},{2,18},{18,2},{3,19},{19,3},{4,20},{20... | collective-permute-start | bytes 12296 | tf_op jit(solution)/shard_map/ppermute | solution.py:495
  86.2 5.8 %collective-permute-start.19 = (f32[8,128]{1,0:T(8,128)S(1)}, f32[8,128]{1,0:T(8,128)S(1)}, u32[]{:S(2)}, u32[]{:S(2)}) collective-permute-start(f32[8,128]{1,0:T(8,128)S(1)} %get-tuple-element.209), channel_id=1, source_target_pairs={{16,17},{17,16},{1,2},{2,1},{18,19},{19,18},{3,4},{4,3},{20,21},{2... | collective-permute-start | bytes 12296 | tf_op jit(solution)/shard_map/ppermute | solution.py:494
  92.6 3.7 %collective-permute-start.20 = (f32[8,128]{1,0:T(8,128)S(1)}, f32[8,128]{1,0:T(8,128)S(1)}, u32[]{:S(2)}, u32[]{:S(2)}) collective-permute-start(f32[8,128]{1,0:T(8,128)S(1)} %get-tuple-element.217), channel_id=1, source_target_pairs={{0,16},{16,0},{1,17},{17,1},{2,18},{18,2},{3,19},{19,3},{4,20},{20... | collective-permute-start | bytes 12296 | tf_op jit(solution)/shard_map/ppermute | solution.py:495
  92.7 5.8 %collective-permute-start.21 = (f32[8,128]{1,0:T(8,128)S(1)}, f32[8,128]{1,0:T(8,128)S(1)}, u32[]{:S(2)}, u32[]{:S(2)}) collective-permute-start(f32[8,128]{1,0:T(8,128)S(1)} %get-tuple-element.218), channel_id=1, source_target_pairs={{16,17},{17,16},{1,2},{2,1},{18,19},{19,18},{3,4},{4,3},{20,21},{2... | collective-permute-start | bytes 12296 | tf_op jit(solution)/shard_map/ppermute | solution.py:494
  99.1 3.7 %collective-permute-start.22 = (f32[8,128]{1,0:T(8,128)S(1)}, f32[8,128]{1,0:T(8,128)S(1)}, u32[]{:S(2)}, u32[]{:S(2)}) collective-permute-start(f32[8,128]{1,0:T(8,128)S(1)} %get-tuple-element.222), channel_id=1, source_target_pairs={{0,16},{16,0},{1,17},{17,1},{2,18},{18,2},{3,19},{19,3},{4,20},{20... | collective-permute-start | bytes 12296 | tf_op jit(solution)/shard_map/ppermute | solution.py:495
  99.2 5.8 %collective-permute-start.23 = (f32[8,128]{1,0:T(8,128)S(1)}, f32[8,128]{1,0:T(8,128)S(1)}, u32[]{:S(2)}, u32[]{:S(2)}) collective-permute-start(f32[8,128]{1,0:T(8,128)S(1)} %get-tuple-element.223), channel_id=1, source_target_pairs={{16,17},{17,16},{1,2},{2,1},{18,19},{19,18},{3,4},{4,3},{20,21},{2... | collective-permute-start | bytes 12296 | tf_op jit(solution)/shard_map/ppermute | solution.py:494
  105.7 3.7 %collective-permute-start.24 = (f32[8,128]{1,0:T(8,128)S(1)}, f32[8,128]{1,0:T(8,128)S(1)}, u32[]{:S(2)}, u32[]{:S(2)}) collective-permute-start(f32[8,128]{1,0:T(8,128)S(1)} %get-tuple-element.230), channel_id=1, source_target_pairs={{0,16},{16,0},{1,17},{17,1},{2,18},{18,2},{3,19},{19,3},{4,20},{20... | collective-permute-start | bytes 12296 | tf_op jit(solution)/shard_map/ppermute | solution.py:495
  105.8 5.8 %collective-permute-start.25 = (f32[8,128]{1,0:T(8,128)S(1)}, f32[8,128]{1,0:T(8,128)S(1)}, u32[]{:S(2)}, u32[]{:S(2)}) collective-permute-start(f32[8,128]{1,0:T(8,128)S(1)} %get-tuple-element.231), channel_id=1, source_target_pairs={{16,17},{17,16},{1,2},{2,1},{18,19},{19,18},{3,4},{4,3},{20,21},{2... | collective-permute-start | bytes 12296 | tf_op jit(solution)/shard_map/ppermute | solution.py:494
  112.2 3.7 %collective-permute-start.26 = (f32[8,128]{1,0:T(8,128)S(1)}, f32[8,128]{1,0:T(8,128)S(1)}, u32[]{:S(2)}, u32[]{:S(2)}) collective-permute-start(f32[8,128]{1,0:T(8,128)S(1)} %get-tuple-element.238), channel_id=1, source_target_pairs={{0,16},{16,0},{1,17},{17,1},{2,18},{18,2},{3,19},{19,3},{4,20},{20... | collective-permute-start | bytes 12296 | tf_op jit(solution)/shard_map/ppermute | solution.py:495
  112.3 5.8 %collective-permute-start.27 = (f32[8,128]{1,0:T(8,128)S(1)}, f32[8,128]{1,0:T(8,128)S(1)}, u32[]{:S(2)}, u32[]{:S(2)}) collective-permute-start(f32[8,128]{1,0:T(8,128)S(1)} %get-tuple-element.239), channel_id=1, source_target_pairs={{16,17},{17,16},{1,2},{2,1},{18,19},{19,18},{3,4},{4,3},{20,21},{2... | collective-permute-start | bytes 12296 | tf_op jit(solution)/shard_map/ppermute | solution.py:494
  118.7 3.7 %collective-permute-start.28 = (f32[8,128]{1,0:T(8,128)S(1)}, f32[8,128]{1,0:T(8,128)S(1)}, u32[]{:S(2)}, u32[]{:S(2)}) collective-permute-start(f32[8,128]{1,0:T(8,128)S(1)} %get-tuple-element.247), channel_id=1, source_target_pairs={{0,16},{16,0},{1,17},{17,1},{2,18},{18,2},{3,19},{19,3},{4,20},{20... | collective-permute-start | bytes 12296 | tf_op jit(solution)/shard_map/ppermute | solution.py:495
  118.8 5.8 %collective-permute-start.29 = (f32[8,128]{1,0:T(8,128)S(1)}, f32[8,128]{1,0:T(8,128)S(1)}, u32[]{:S(2)}, u32[]{:S(2)}) collective-permute-start(f32[8,128]{1,0:T(8,128)S(1)} %get-tuple-element.248), channel_id=1, source_target_pairs={{16,17},{17,16},{1,2},{2,1},{18,19},{19,18},{3,4},{4,3},{20,21},{2... | collective-permute-start | bytes 12296 | tf_op jit(solution)/shard_map/ppermute | solution.py:494
  125.3 3.7 %collective-permute-start.30 = (f32[8,128]{1,0:T(8,128)S(1)}, f32[8,128]{1,0:T(8,128)S(1)}, u32[]{:S(2)}, u32[]{:S(2)}) collective-permute-start(f32[8,128]{1,0:T(8,128)S(1)} %get-tuple-element.252), channel_id=1, source_target_pairs={{0,16},{16,0},{1,17},{17,1},{2,18},{18,2},{3,19},{19,3},{4,20},{20... | collective-permute-start | bytes 12296 | tf_op jit(solution)/shard_map/ppermute | solution.py:495
  125.3 5.8 %collective-permute-start.31 = (f32[8,128]{1,0:T(8,128)S(1)}, f32[8,128]{1,0:T(8,128)S(1)}, u32[]{:S(2)}, u32[]{:S(2)}) collective-permute-start(f32[8,128]{1,0:T(8,128)S(1)} %get-tuple-element.253), channel_id=1, source_target_pairs={{16,17},{17,16},{1,2},{2,1},{18,19},{19,18},{3,4},{4,3},{20,21},{2... | collective-permute-start | bytes 12296 | tf_op jit(solution)/shard_map/ppermute | solution.py:494
  131.8 3.7 %collective-permute-start.32 = (f32[8,128]{1,0:T(8,128)S(1)}, f32[8,128]{1,0:T(8,128)S(1)}, u32[]{:S(2)}, u32[]{:S(2)}) collective-permute-start(f32[8,128]{1,0:T(8,128)S(1)} %get-tuple-element.260), channel_id=1, source_target_pairs={{0,16},{16,0},{1,17},{17,1},{2,18},{18,2},{3,19},{19,3},{4,20},{20... | collective-permute-start | bytes 12296 | tf_op jit(solution)/shard_map/ppermute | solution.py:495
  131.9 5.8 %collective-permute-start.33 = (f32[8,128]{1,0:T(8,128)S(1)}, f32[8,128]{1,0:T(8,128)S(1)}, u32[]{:S(2)}, u32[]{:S(2)}) collective-permute-start(f32[8,128]{1,0:T(8,128)S(1)} %get-tuple-element.261), channel_id=1, source_target_pairs={{16,17},{17,16},{1,2},{2,1},{18,19},{19,18},{3,4},{4,3},{20,21},{2... | collective-permute-start | bytes 12296 | tf_op jit(solution)/shard_map/ppermute | solution.py:494
  138.3 3.7 %collective-permute-start.34 = (f32[8,128]{1,0:T(8,128)S(1)}, f32[8,128]{1,0:T(8,128)S(1)}, u32[]{:S(2)}, u32[]{:S(2)}) collective-permute-start(f32[8,128]{1,0:T(8,128)S(1)} %get-tuple-element.268), channel_id=1, source_target_pairs={{0,16},{16,0},{1,17},{17,1},{2,18},{18,2},{3,19},{19,3},{4,20},{20... | collective-permute-start | bytes 12296 | tf_op jit(solution)/shard_map/ppermute | solution.py:495
  138.4 5.8 %collective-permute-start.35 = (f32[8,128]{1,0:T(8,128)S(1)}, f32[8,128]{1,0:T(8,128)S(1)}, u32[]{:S(2)}, u32[]{:S(2)}) collective-permute-start(f32[8,128]{1,0:T(8,128)S(1)} %get-tuple-element.269), channel_id=1, source_target_pairs={{16,17},{17,16},{1,2},{2,1},{18,19},{19,18},{3,4},{4,3},{20,21},{2... | collective-permute-start | bytes 12296 | tf_op jit(solution)/shard_map/ppermute | solution.py:494
  144.7 3.7 %collective-permute-start.36 = (f32[4,2,2,128]{3,2,1,0:T(2,128)S(1)}, f32[4,2,2,128]{3,2,1,0:T(2,128)S(1)}, u32[]{:S(2)}, u32[]{:S(2)}) collective-permute-start(f32[4,2,2,128]{3,2,1,0:T(2,128)S(1)} %rev.22), channel_id=1, source_target_pairs={{0,16},{16,0},{1,17},{17,1},{2,18},{18,2},{3,19},{19,3},{4,20},{20... | collective-permute-start | bytes 24584 | tf_op jit(solution)/shard_map/ppermute | solution.py:508

commit v9 on v8

--- a/solution.py
+++ b/solution.py
@@ -320,11 +320,14 @@
 
 
 def small_part(small, index):
-    n = N * HALF
-    return small[index * n:(index + 1) * n, :]
-
-
-def start_kernel(keep, recv_0, recv_1, small, msg_a, msg_b, q_out):
+    keep, recv = small
+    n = ROWS * HALF
+    i = index * n
+    return jnp.concatenate([keep[i:i + n, :], recv[i + HALF:i + n, :], recv[i:i + HALF, :]], axis=0)
+
+
+def start_kernel(keep, recv_0, recv_1, small_keep, small_recv, msg_a, msg_b, q_out):
+    small = (small_keep, small_recv)
     halves = ((keep,), (recv_0, recv_1))
     f = small_part(small, INITIAL)
     q = inner_product(f, halves)
@@ -337,14 +340,36 @@
         msg_b[start:start + width, :] = recv_0[SIDE_B + h * HALF]
 
 
-def small_part(small, index):
-    n = N * HALF
-    return small[index * n:(index + 1) * n, :]
-
-
-def beside_kernel(keep, recv_0, recv_1, beyond_0, first_b, got_a, f_ref, q_ref, response_out, q_out):
+def small_kernel(place_ref, arrived, capacity, initial, keep, send, injected):
+    y, col = place_ref[0], place_ref[1]
+    tiles, frames = injected.shape
+    _, cols, width = capacity.shape
+    slots = (arrived.shape[1] - width) // frames
+    for t in range(tiles):
+        total = jnp.zeros((arrived.shape[0], frames), jnp.float32)
+        for k in range(slots):
+            feeds = arrived[:, slots * frames + k:slots * frames + k + 1] == float(t)
+            total = total + jnp.where(feeds, 1.0, 0.0) * arrived[:, k * frames:(k + 1) * frames]
+        injected[t:t + 1, :] = jnp.sum(total, axis=0, keepdims=True)
+    for sent, out in ((0, keep), (1, send)):
+        parity = (y + col + sent) % 2
+        for h in range(ROWS):
+            row = y if h == 0 else 1 - y
+            for b in range(HALF):
+                at = b + parity * (cols - 1 - 2 * b)
+                currents = injected[pl.ds(row * cols + at, 1), :]
+                parts = [currents[:, n * width:(n + 1) * width] for n in range(STEPS)]
+                parts += [x[row, pl.ds(at, 1), :] for x in (capacity, initial)]
+                for n, part in enumerate(parts):
+                    i = n * ROWS * HALF + h * HALF + b
+                    out[i:i + 1, :] = part
+
+
+def beside_kernel(begin, keep, recv_0, recv_1, beyond_0, first_b, got_a, q_ref, *refs):
     halves = ((keep,), (recv_0, recv_1))
-    f, q = f_ref[...], q_ref[...]
+    response_out, q_out = refs[-2:]
+    f = small_part(refs[:2], INITIAL) if begin else refs[0][...]
+    q = q_ref[...]
     response, total = [], []
     for j, b in TILES:
         response.append(matvec([(facing_block(halves, beyond_0, first_b, j, b), row_of(f, j, b))]))
@@ -356,11 +381,17 @@
     q_out[...] = jnp.concatenate(total, axis=0)
 
 
-def pair_kernel(instant, pair, last, keep, recv_0, recv_1, small, got_a, got_b, response_ref, q_ref, f_ref, *refs):
+def pair_kernel(instant, pair, last, keep, recv_0, recv_1, small_keep, small_recv, got_a, got_b, response_ref, q_ref,
+                *refs):
+    small = (small_keep, small_recv)
     halves = ((keep,), (recv_0, recv_1))
     first = pair == 0
     capacity = small_part(small, CAPACITY)
-    f, q, response = f_ref[...], q_ref[...], response_ref[...]
+    q, response = q_ref[...], response_ref[...]
+    if first and instant == 0:
+        f = small_part(small, INITIAL)
+    else:
+        f, refs = refs[0][...], refs[1:]
     if not first:
         residue, estimate, refs = refs[0][...], refs[1][...], refs[2:]
     got = (got_b, got_a)
@@ -427,7 +458,7 @@
     hbm = pl.BlockSpec(memory_space=pltpu.HBM)
     limit = pltpu.CompilerParams(vmem_limit_bytes=16 * 2**20)
     place = jnp.stack([row, col]).astype(jnp.int32)
-    blocks = [pltpu.with_memory_space_constraint(x, pltpu.HBM) for x in (own_block, neighbor_block)]
+    blocks = [pltpu.with_memory_space_constraint(x, pltpu.HBM) for x in (pattern, own_block, neighbor_block)]
 
     def pack(sent, first, count, extra=()):
         return pl.pallas_call(
@@ -438,7 +469,7 @@
             scratch_shapes=[pltpu.SemaphoreType.DMA((count,))],
             compiler_params=limit,
             name="pack",
-        )(place, pattern, *blocks)
+        )(place, *blocks)
 
     recv = []
     for first, count in ((0, SPLIT[1][0]), SPLIT[1]):
@@ -448,21 +479,27 @@
 
     def beside(currents, slot_tile, capacity, initial, facing_0):
         beyond_0 = lax.ppermute(facing_0, both, b_pairs)
-        injected = collect(currents, slot_tile, tile_rows * tile_cols, width)
-        small = jnp.concatenate(
-            [jnp.moveaxis(injected, 1, 0).reshape(STEPS, tile_rows, tile_cols, width), capacity[None], initial[None]]
-        )
-        small = jnp.where(row == 1, jnp.flip(small, 1), small)
-        unit_0, unit_1 = small[:, :, :HALF], jnp.flip(small, 2)[:, :, :HALF]
-        got = lax.ppermute(jnp.where(parity == 1, unit_0, unit_1), "row", swap)
-        small = jnp.concatenate([jnp.where(parity == 1, unit_1, unit_0), jnp.flip(got, 1)], axis=1)
-        return small.reshape((STEPS + 2) * N * HALF, width), beyond_0
-
-    small, beyond_0 = lax.cond(
+        slots, frames = currents.shape[3:]
+        names = jnp.pad(slot_tile.astype(jnp.float32), ((0, 0), (0, 0), (0, 0), (0, width - slots)))
+        packed = jnp.concatenate([currents.reshape(*currents.shape[:3], slots * frames), names], axis=3)
+        arrived = lax.all_to_all(packed, "col", split_axis=2, concat_axis=1, tiled=True)
+        half = jax.ShapeDtypeStruct(((STEPS + 2) * ROWS * HALF, width), jnp.float32)
+        small, send = pl.pallas_call(
+            small_kernel,
+            out_shape=(half, half),
+            in_specs=[smem, vmem, vmem, vmem],
+            out_specs=(vmem, vmem),
+            scratch_shapes=[pltpu.VMEM((tile_rows * tile_cols, frames), jnp.float32)],
+            compiler_params=limit,
+            name="small",
+        )(place, arrived.reshape(n_col, slots * frames + width), capacity, initial)
+        return small, lax.ppermute(send, "row", swap), beyond_0
+
+    *small, beyond_0 = lax.cond(
         row < lax.axis_size("row"),
         beside,
         lambda currents, slot_tile, capacity, initial, facing_0: (
-            jnp.zeros(((STEPS + 2) * N * HALF, width), jnp.float32), facing_0
+            *jnp.zeros((2, (STEPS + 2) * ROWS * HALF, width), jnp.float32), facing_0
         ),
         currents, slot_tile, capacity, initial, facing_0,
     )
@@ -483,8 +520,8 @@
         )(*ins)
 
     first_shape = jax.ShapeDtypeStruct((2 * N + ROWS * width, width), jnp.float32)
-    msg_a, msg_b, q = call(start_kernel, (shape, first_shape, shape), 28, *halves, small)
-    field, first_b = small[INITIAL * N * HALF:(INITIAL + 1) * N * HALF], None
+    msg_a, msg_b, q = call(start_kernel, (shape, first_shape, shape), 28, *halves, *small)
+    field, first_b = (), None
     frames = []
     state = ()
     for instant in range(STEPS):
@@ -495,14 +532,15 @@
             got_a = lax.ppermute(msg_a, "row", swap)
             if first_b is None:
                 first_b = got_b
-            response, q = call(beside_kernel, (shape,) * 2, 12, *halves, beyond_0, first_b, got_a, field, q)
+            response, q = call(functools.partial(beside_kernel, not field), (shape,) * 2, 12, *halves, beyond_0, first_b,
+                               got_a, q, *(field or small))
             out = call(functools.partial(pair_kernel, instant, pair, last), (shape,) * (1 if last else 4 if closing else 6),
-                       68, *halves, small, got_a, got_b, response, q, field, *state)
-            field = out[0]
+                       68, *halves, *small, got_a, got_b, response, q, *field, *state)
+            field = out[:1]
             if not last:
                 q, msg_a, msg_b = out[1:4]
                 state = out[4:]
-        frames.append(field)
+        frames.append(out[0])
 
     done = jnp.stack(frames).reshape(STEPS, N, HALF, width)
     got = lax.ppermute(jnp.flip(done[:, ROWS:], 1), "row", swap)

time: 151 us -> 159 us (1.053)
  Pallas kernels: 21.8 us -> 35.1 us
  waiting for transfers between devices: 54.3 us -> 60.1 us
  starting transfers between devices: 57.8 us -> 53.9 us
  local copies, waits for them, and re-layouts: 7.68 us -> 4.36 us
  other arithmetic: 5.7 us -> 2.4 us
    pallas_call x33, Pallas kernels: 15.2 us -> 27.2 us  [call(): pl.pallas_call(body, out_shape=outs, in_specs=[vmem] * len(ins), out_spec...]
    ppermute x16, starting transfers between devices: 42.7 us -> 38.1 us  [shards_chain(): got_b = lax.ppermute(msg_b, both, b_pairs)]
    ppermute x16, waiting for transfers between devices: 16.5 us -> 19.7 us  [shards_chain(): got_a = lax.ppermute(msg_a, 'row', swap)]
    ppermute x1, waiting for transfers between devices: 1.37 us -> 3.41 us  [beside(): return (small, lax.ppermute(send, 'row', swap), beyond_0)]
    reshape x0 -> x1, local copies, waits for them, and re-layouts: none -> 1.73 us  [beside(): currents.reshape(*currents.shape[:3], slots * frames)]
    all_to_all x1 -> x0, local copies, waits for them, and re-layouts: 1.59 us -> none  [collect(): lax.all_to_all(packed, 'col', split_axis=2, concat_axis=1, tiled=True)]
  transfers between devices with their start and end apart: 38 -> 38, of which waited for: 35 -> 35; matrix products, arithmetic and copies ran while one was open for 8% -> 4% of each run, Pallas kernels for 6% -> 6%
where the time goes in v9:
time: 159 us; the launch traced here: 156 us
  waiting for transfers between devices  60.1 us (38%)
  starting transfers between devices  53.9 us (34%)
  Pallas kernels  35.1 us (22%)
  local copies, waits for them, and re-layouts  4.36 us (3%)
  other arithmetic  2.4 us (2%)
    ppermute x16, starting transfers between devices, shards_chain(): got_b = lax.ppermute(msg_b, both, b_pairs)  38.1 us
    ppermute x16, waiting for transfers between devices, shards_chain(): got_b = lax.ppermute(msg_b, both, b_pairs)  30.8 us
    pallas_call x33, Pallas kernels, call(): pl.pallas_call(body, out_shape=outs, in_specs=[vmem] * len(ins), out_spec...  27.2 us
    ppermute x16, waiting for transfers between devices, shards_chain(): got_a = lax.ppermute(msg_a, 'row', swap)  19.7 us
    pallas_call x3, Pallas kernels, pack(): pl.pallas_call(functools.partial(pack_kernel, n_col, sent, first, count),...  6.99 us
    all_to_all x1, starting transfers between devices, beside(): lax.all_to_all(packed, 'col', split_axis=2, concat_axis=1, tiled=True)  6.27 us
    ppermute x1, waiting for transfers between devices, shards_chain(): got = lax.ppermute(jnp.flip(done[:, ROWS:], 1), 'row', swap)  3.63 us
    ppermute x1, waiting for transfers between devices, beside(): return (small, lax.ppermute(send, 'row', swap), beyond_0)  3.41 us
  transfers between devices with their start and end apart: 38, of which 35 were waited for; matrix products, arithmetic and copies ran while one was open for 4% of the time, Pallas kernels for 6%

profile of v9, /device:TPU:8, one launch (start us, length us, event | category | flops | bytes accessed | tf_op | source)
XLA Modules:
  0.0 156.4 jit_solution(15488726664651627936)
XLA Ops:
  0.1 2.0 %pack.4 = f32[12,128,128]{2,1,0:T(8,128)S(1)} custom-call(s32[2]{0:T(128)S(1)} %pad_add_fusion.place_ref, s32[2,4,4]{2,1,0:T(4,128)} %pattern_ref.5, f32[2,4,128,128]{3,2,1,0:T(8,128)} %own_hbm.5, f32[4,2,4,128,128]{4,3,2,1,0:T(8,128)} %nb_hbm.5), custom_call_target="tpu_custom_call" | custom-call | tf_op jit(solution)/shard_map/pack/pallas_call | solution.py:464
  2.1 1.6 %collective-permute-start.2 = (f32[12,128,128]{2,1,0:T(8,128)S(1)}, f32[12,128,128]{2,1,0:T(8,128)S(1)}, u32[]{:S(2)}, u32[]{:S(2)}) collective-permute-start(f32[12,128,128]{2,1,0:T(8,128)S(1)} %pack.4), channel_id=1, source_target_pairs={{0,16},{16,0},{1,17},{17,1},{2,18},{18,2},{3,19},{19,3},{4,20},{20... | collective-permute-start | bytes 2359304 | tf_op jit(solution)/shard_map/ppermute | solution.py:477
  3.7 2.7 %pack.5 = f32[8,128,128]{2,1,0:T(8,128)} custom-call(s32[2]{0:T(128)S(1)} %pad_add_fusion.place_ref, s32[2,4,4]{2,1,0:T(4,128)} %pattern_ref.5, f32[2,4,128,128]{3,2,1,0:T(8,128)} %own_hbm.5, f32[4,2,4,128,128]{4,3,2,1,0:T(8,128)} %nb_hbm.5), custom_call_target="tpu_custom_call" | custom-call | tf_op jit(solution)/shard_map/pack/pallas_call | solution.py:464
  7.0 2.3 %pack.3 = (f32[20,128,128]{2,1,0:T(8,128)S(1)}, f32[2,128,128]{2,1,0:T(8,128)S(1)}) custom-call(s32[2]{0:T(128)S(1)} %pad_add_fusion.place_ref, s32[2,4,4]{2,1,0:T(4,128)} %pattern_ref.5, f32[2,4,128,128]{3,2,1,0:T(8,128)} %own_hbm.5, f32[4,2,4,128,128]{4,3,2,1,0:T(8,128)} %nb_hbm.5), custom_call_target="tpu_custom_call" | custom-call | tf_op jit(solution)/shard_map/pack/pallas_call | solution.py:464
  9.2 23.8 %conditional.1 = (f32[24,128]{1,0:T(8,128)S(1)}, f32[24,128]{1,0:T(8,128)}, f32[2,128,128]{2,1,0:T(8,128)S(1)}) conditional(s32[]{:T(128)} %convert_element_type.8, f32[2,128,128]{2,1,0:T(8,128)S(1)} %get-tuple-element.151, (f32[1,1,16,4,512]{4,3,2,1,0:T(4,128)}, s32[1,1,16,4]{2,3,1,0:T(4,128)}, s32[2]{0:T(128)}, f32[2,4,128]{2,1,0:T(4,128)}, ...), branch_computations={%region_0.1_spmd, %region_1.2_spmd} | conditional | flops 104512 | bytes 2065800 | solution.py:498
  10.0 1.7 %reshape.17 = f32[1,1,16,2048]{3,1,0,2:T(1,128)} reshape(f32[1,1,16,4,512]{4,3,2,1,0:T(4,128)} %get-tuple-element.278) | data formatting | bytes 262144 | tf_op jit(solution)/shard_map/cond/branch_1_fun/reshape | solution.py:484
  11.8 1.7 %fusion = f32[1,1,16,2176]{3,1,0,2:T(1,128)} fusion(f32[1,1,16,4]{3,1,0,2:T(1,128)S(1)} %convert_element_type.6, f32[1,1,16,2048]{3,1,0,2:T(1,128)} %reshape.17), kind=kLoop, calls=%fused_computation.1 | loop fusion | flops 104448 | bytes 270592 | tf_op jit(solution)/shard_map/cond/branch_1_fun/concatenate | solution.py:484
  13.4 6.3 %all-to-all-start = ((f32[1,1,16,2176]{3,1,0,2:T(1,128)}), f32[1,1,16,2176]{3,1,0,2:T(1,128)}, u32[]{:S(2)}, u32[]{:S(2)}) async-start(f32[1,1,16,2176]{3,1,0,2:T(1,128)} %fusion), calls=%async_computation | async-start | bytes 278528 | tf_op jit(solution)/shard_map/cond/branch_1_fun/all_to_all | solution.py:485
  19.7 3.1 %collective-permute-start.1 = (f32[2,128,128]{2,1,0:T(8,128)S(1)}, f32[2,128,128]{2,1,0:T(8,128)}, u32[]{:S(2)}, u32[]{:S(2)}) collective-permute-start(f32[2,128,128]{2,1,0:T(8,128)S(1)} %get-tuple-element.25), channel_id=1, source_target_pairs={{16,17},{17,16},{1,2},{2,1},{18,19},{19,18},{3,4},{4,3},{20,21},{2... | collective-permute-start | bytes 393224 | tf_op jit(solution)/shard_map/cond/branch_1_fun/ppermute | solution.py:481
  22.8 2.5 %all-to-all-done = f32[1,1,16,2176]{3,1,0,2:T(1,128)} async-done(((f32[1,1,16,2176]{3,1,0,2:T(1,128)}), f32[1,1,16,2176]{3,1,0,2:T(1,128)}, u32[]{:S(2)}, u32[]{:S(2)}) %all-to-all-start) | async-done | bytes 139296 | tf_op jit(solution)/shard_map/cond/branch_1_fun/all_to_all | solution.py:485
  27.2 1.6 %collective-permute-start = (f32[24,128]{1,0:T(8,128)S(1)}, f32[24,128]{1,0:T(8,128)}, u32[]{:S(2)}, u32[]{:S(2)}) collective-permute-start(f32[24,128]{1,0:T(8,128)S(1)} %get-tuple-element.24), channel_id=1, source_target_pairs={{0,16},{16,0},{1,17},{17,1},{2,18},{18,2},{3,19},{19,3},{4,20},{20... | collective-permute-start | bytes 36872 | tf_op jit(solution)/shard_map/cond/branch_1_fun/ppermute | solution.py:496
  29.6 3.4 %collective-permute-done = f32[24,128]{1,0:T(8,128)} collective-permute-done((f32[24,128]{1,0:T(8,128)S(1)}, f32[24,128]{1,0:T(8,128)}, u32[]{:S(2)}, u32[]{:S(2)}) %collective-permute-start) | collective-permute-done | bytes 12320 | tf_op jit(solution)/shard_map/cond/branch_1_fun/ppermute | solution.py:496
  34.0 1.9 %collective-permute-start.5 = (f32[264,128]{1,0:T(8,128)S(1)}, f32[264,128]{1,0:T(8,128)S(1)}, u32[]{:S(2)}, u32[]{:S(2)}) collective-permute-start(f32[264,128]{1,0:T(8,128)S(1)} %get-tuple-element.155), channel_id=1, source_target_pairs={{16,17},{17,16},{1,2},{2,1},{18,19},{19,18},{3,4},{4,3},{20,21},{2... | collective-permute-start | bytes 405512 | tf_op jit(solution)/shard_map/ppermute | solution.py:531
  35.9 1.6 %collective-permute-start.4 = (f32[8,128]{1,0:T(8,128)S(1)}, f32[8,128]{1,0:T(8,128)S(1)}, u32[]{:S(2)}, u32[]{:S(2)}) collective-permute-start(f32[8,128]{1,0:T(8,128)S(1)} %get-tuple-element.154), channel_id=1, source_target_pairs={{0,16},{16,0},{1,17},{17,1},{2,18},{18,2},{3,19},{19,3},{4,20},{20... | collective-permute-start | bytes 12296 | tf_op jit(solution)/shard_map/ppermute | solution.py:532
  37.5 2.1 %collective-permute-done.4.got_a = f32[8,128]{1,0:T(8,128)S(1)} collective-permute-done((f32[8,128]{1,0:T(8,128)S(1)}, f32[8,128]{1,0:T(8,128)S(1)}, u32[]{:S(2)}, u32[]{:S(2)}) %collective-permute-start.4) | collective-permute-done | bytes 4128 | tf_op jit(solution)/shard_map/ppermute | solution.py:532
  39.6 1.7 %collective-permute-done.5.first_b.got_b = f32[264,128]{1,0:T(8,128)S(1)} collective-permute-done((f32[264,128]{1,0:T(8,128)S(1)}, f32[264,128]{1,0:T(8,128)S(1)}, u32[]{:S(2)}, u32[]{:S(2)}) %collective-permute-start.5) | collective-permute-done | bytes 135200 | tf_op jit(solution)/shard_map/ppermute | solution.py:531
  43.8 2.0 %collective-permute-start.7 = (f32[8,128]{1,0:T(8,128)S(1)}, f32[8,128]{1,0:T(8,128)S(1)}, u32[]{:S(2)}, u32[]{:S(2)}) collective-permute-start(f32[8,128]{1,0:T(8,128)S(1)} %get-tuple-element.161), channel_id=1, source_target_pairs={{16,17},{17,16},{1,2},{2,1},{18,19},{19,18},{3,4},{4,3},{20,21},{2... | collective-permute-start | bytes 12296 | tf_op jit(solution)/shard_map/ppermute | solution.py:531
  45.7 1.6 %collective-permute-done.6.got_a = f32[8,128]{1,0:T(8,128)S(1)} collective-permute-done((f32[8,128]{1,0:T(8,128)S(1)}, f32[8,128]{1,0:T(8,128)S(1)}, u32[]{:S(2)}, u32[]{:S(2)}) %collective-permute-start.6) | collective-permute-done | bytes 4128 | tf_op jit(solution)/shard_map/ppermute | solution.py:532
  47.6 1.9 %collective-permute-done.7.got_b = f32[8,128]{1,0:T(8,128)S(1)} collective-permute-done((f32[8,128]{1,0:T(8,128)S(1)}, f32[8,128]{1,0:T(8,128)S(1)}, u32[]{:S(2)}, u32[]{:S(2)}) %collective-permute-start.7) | collective-permute-done | bytes 4128 | tf_op jit(solution)/shard_map/ppermute | solution.py:531
  51.0 2.4 %collective-permute-start.9 = (f32[8,128]{1,0:T(8,128)S(1)}, f32[8,128]{1,0:T(8,128)S(1)}, u32[]{:S(2)}, u32[]{:S(2)}) collective-permute-start(f32[8,128]{1,0:T(8,128)S(1)} %get-tuple-element.169), channel_id=1, source_target_pairs={{16,17},{17,16},{1,2},{2,1},{18,19},{19,18},{3,4},{4,3},{20,21},{2... | collective-permute-start | bytes 12296 | tf_op jit(solution)/shard_map/ppermute | solution.py:531
  54.9 1.9 %collective-permute-done.9.got_b = f32[8,128]{1,0:T(8,128)S(1)} collective-permute-done((f32[8,128]{1,0:T(8,128)S(1)}, f32[8,128]{1,0:T(8,128)S(1)}, u32[]{:S(2)}, u32[]{:S(2)}) %collective-permute-start.9) | collective-permute-done | bytes 4128 | tf_op jit(solution)/shard_map/ppermute | solution.py:531
  58.2 2.4 %collective-permute-start.11 = (f32[8,128]{1,0:T(8,128)S(1)}, f32[8,128]{1,0:T(8,128)S(1)}, u32[]{:S(2)}, u32[]{:S(2)}) collective-permute-start(f32[8,128]{1,0:T(8,128)S(1)} %get-tuple-element.177), channel_id=1, source_target_pairs={{16,17},{17,16},{1,2},{2,1},{18,19},{19,18},{3,4},{4,3},{20,21},{2... | collective-permute-start | bytes 12296 | tf_op jit(solution)/shard_map/ppermute | solution.py:531
  62.1 1.9 %collective-permute-done.11.got_b = f32[8,128]{1,0:T(8,128)S(1)} collective-permute-done((f32[8,128]{1,0:T(8,128)S(1)}, f32[8,128]{1,0:T(8,128)S(1)}, u32[]{:S(2)}, u32[]{:S(2)}) %collective-permute-start.11) | collective-permute-done | bytes 4128 | tf_op jit(solution)/shard_map/ppermute | solution.py:531
  65.5 2.4 %collective-permute-start.13 = (f32[8,128]{1,0:T(8,128)S(1)}, f32[8,128]{1,0:T(8,128)S(1)}, u32[]{:S(2)}, u32[]{:S(2)}) collective-permute-start(f32[8,128]{1,0:T(8,128)S(1)} %get-tuple-element.186), channel_id=1, source_target_pairs={{16,17},{17,16},{1,2},{2,1},{18,19},{19,18},{3,4},{4,3},{20,21},{2... | collective-permute-start | bytes 12296 | tf_op jit(solution)/shard_map/ppermute | solution.py:531
  69.4 1.9 %collective-permute-done.13.got_b = f32[8,128]{1,0:T(8,128)S(1)} collective-permute-done((f32[8,128]{1,0:T(8,128)S(1)}, f32[8,128]{1,0:T(8,128)S(1)}, u32[]{:S(2)}, u32[]{:S(2)}) %collective-permute-start.13) | collective-permute-done | bytes 4128 | tf_op jit(solution)/shard_map/ppermute | solution.py:531
  72.7 2.4 %collective-permute-start.15 = (f32[8,128]{1,0:T(8,128)S(1)}, f32[8,128]{1,0:T(8,128)S(1)}, u32[]{:S(2)}, u32[]{:S(2)}) collective-permute-start(f32[8,128]{1,0:T(8,128)S(1)} %get-tuple-element.191), channel_id=1, source_target_pairs={{16,17},{17,16},{1,2},{2,1},{18,19},{19,18},{3,4},{4,3},{20,21},{2... | collective-permute-start | bytes 12296 | tf_op jit(solution)/shard_map/ppermute | solution.py:531
  76.6 1.9 %collective-permute-done.15.got_b = f32[8,128]{1,0:T(8,128)S(1)} collective-permute-done((f32[8,128]{1,0:T(8,128)S(1)}, f32[8,128]{1,0:T(8,128)S(1)}, u32[]{:S(2)}, u32[]{:S(2)}) %collective-permute-start.15) | collective-permute-done | bytes 4128 | tf_op jit(solution)/shard_map/ppermute | solution.py:531
  79.9 2.4 %collective-permute-start.17 = (f32[8,128]{1,0:T(8,128)S(1)}, f32[8,128]{1,0:T(8,128)S(1)}, u32[]{:S(2)}, u32[]{:S(2)}) collective-permute-start(f32[8,128]{1,0:T(8,128)S(1)} %get-tuple-element.199), channel_id=1, source_target_pairs={{16,17},{17,16},{1,2},{2,1},{18,19},{19,18},{3,4},{4,3},{20,21},{2... | collective-permute-start | bytes 12296 | tf_op jit(solution)/shard_map/ppermute | solution.py:531
  83.8 1.9 %collective-permute-done.17.got_b = f32[8,128]{1,0:T(8,128)S(1)} collective-permute-done((f32[8,128]{1,0:T(8,128)S(1)}, f32[8,128]{1,0:T(8,128)S(1)}, u32[]{:S(2)}, u32[]{:S(2)}) %collective-permute-start.17) | collective-permute-done | bytes 4128 | tf_op jit(solution)/shard_map/ppermute | solution.py:531
  87.2 2.4 %collective-permute-start.19 = (f32[8,128]{1,0:T(8,128)S(1)}, f32[8,128]{1,0:T(8,128)S(1)}, u32[]{:S(2)}, u32[]{:S(2)}) collective-permute-start(f32[8,128]{1,0:T(8,128)S(1)} %get-tuple-element.207), channel_id=1, source_target_pairs={{16,17},{17,16},{1,2},{2,1},{18,19},{19,18},{3,4},{4,3},{20,21},{2... | collective-permute-start | bytes 12296 | tf_op jit(solution)/shard_map/ppermute | solution.py:531
  91.1 1.9 %collective-permute-done.19.got_b = f32[8,128]{1,0:T(8,128)S(1)} collective-permute-done((f32[8,128]{1,0:T(8,128)S(1)}, f32[8,128]{1,0:T(8,128)S(1)}, u32[]{:S(2)}, u32[]{:S(2)}) %collective-permute-start.19) | collective-permute-done | bytes 4128 | tf_op jit(solution)/shard_map/ppermute | solution.py:531
  94.4 2.4 %collective-permute-start.21 = (f32[8,128]{1,0:T(8,128)S(1)}, f32[8,128]{1,0:T(8,128)S(1)}, u32[]{:S(2)}, u32[]{:S(2)}) collective-permute-start(f32[8,128]{1,0:T(8,128)S(1)} %get-tuple-element.216), channel_id=1, source_target_pairs={{16,17},{17,16},{1,2},{2,1},{18,19},{19,18},{3,4},{4,3},{20,21},{2... | collective-permute-start | bytes 12296 | tf_op jit(solution)/shard_map/ppermute | solution.py:531
  98.3 1.9 %collective-permute-done.21.got_b = f32[8,128]{1,0:T(8,128)S(1)} collective-permute-done((f32[8,128]{1,0:T(8,128)S(1)}, f32[8,128]{1,0:T(8,128)S(1)}, u32[]{:S(2)}, u32[]{:S(2)}) %collective-permute-start.21) | collective-permute-done | bytes 4128 | tf_op jit(solution)/shard_map/ppermute | solution.py:531
  101.6 2.6 %collective-permute-start.23 = (f32[8,128]{1,0:T(8,128)S(1)}, f32[8,128]{1,0:T(8,128)S(1)}, u32[]{:S(2)}, u32[]{:S(2)}) collective-permute-start(f32[8,128]{1,0:T(8,128)S(1)} %get-tuple-element.221), channel_id=1, source_target_pairs={{16,17},{17,16},{1,2},{2,1},{18,19},{19,18},{3,4},{4,3},{20,21},{2... | collective-permute-start | bytes 12296 | tf_op jit(solution)/shard_map/ppermute | solution.py:531
  105.5 1.9 %collective-permute-done.23.got_b = f32[8,128]{1,0:T(8,128)S(1)} collective-permute-done((f32[8,128]{1,0:T(8,128)S(1)}, f32[8,128]{1,0:T(8,128)S(1)}, u32[]{:S(2)}, u32[]{:S(2)}) %collective-permute-start.23) | collective-permute-done | bytes 4128 | tf_op jit(solution)/shard_map/ppermute | solution.py:531
  108.9 2.4 %collective-permute-start.25 = (f32[8,128]{1,0:T(8,128)S(1)}, f32[8,128]{1,0:T(8,128)S(1)}, u32[]{:S(2)}, u32[]{:S(2)}) collective-permute-start(f32[8,128]{1,0:T(8,128)S(1)} %get-tuple-element.229), channel_id=1, source_target_pairs={{16,17},{17,16},{1,2},{2,1},{18,19},{19,18},{3,4},{4,3},{20,21},{2... | collective-permute-start | bytes 12296 | tf_op jit(solution)/shard_map/ppermute | solution.py:531
  112.8 1.9 %collective-permute-done.25.got_b = f32[8,128]{1,0:T(8,128)S(1)} collective-permute-done((f32[8,128]{1,0:T(8,128)S(1)}, f32[8,128]{1,0:T(8,128)S(1)}, u32[]{:S(2)}, u32[]{:S(2)}) %collective-permute-start.25) | collective-permute-done | bytes 4128 | tf_op jit(solution)/shard_map/ppermute | solution.py:531
  116.1 2.4 %collective-permute-start.27 = (f32[8,128]{1,0:T(8,128)S(1)}, f32[8,128]{1,0:T(8,128)S(1)}, u32[]{:S(2)}, u32[]{:S(2)}) collective-permute-start(f32[8,128]{1,0:T(8,128)S(1)} %get-tuple-element.237), channel_id=1, source_target_pairs={{16,17},{17,16},{1,2},{2,1},{18,19},{19,18},{3,4},{4,3},{20,21},{2... | collective-permute-start | bytes 12296 | tf_op jit(solution)/shard_map/ppermute | solution.py:531
  120.0 1.9 %collective-permute-done.27.got_b = f32[8,128]{1,0:T(8,128)S(1)} collective-permute-done((f32[8,128]{1,0:T(8,128)S(1)}, f32[8,128]{1,0:T(8,128)S(1)}, u32[]{:S(2)}, u32[]{:S(2)}) %collective-permute-start.27) | collective-permute-done | bytes 4128 | tf_op jit(solution)/shard_map/ppermute | solution.py:531
  123.3 2.4 %collective-permute-start.29 = (f32[8,128]{1,0:T(8,128)S(1)}, f32[8,128]{1,0:T(8,128)S(1)}, u32[]{:S(2)}, u32[]{:S(2)}) collective-permute-start(f32[8,128]{1,0:T(8,128)S(1)} %get-tuple-element.246), channel_id=1, source_target_pairs={{16,17},{17,16},{1,2},{2,1},{18,19},{19,18},{3,4},{4,3},{20,21},{2... | collective-permute-start | bytes 12296 | tf_op jit(solution)/shard_map/ppermute | solution.py:531
  127.2 1.9 %collective-permute-done.29.got_b = f32[8,128]{1,0:T(8,128)S(1)} collective-permute-done((f32[8,128]{1,0:T(8,128)S(1)}, f32[8,128]{1,0:T(8,128)S(1)}, u32[]{:S(2)}, u32[]{:S(2)}) %collective-permute-start.29) | collective-permute-done | bytes 4128 | tf_op jit(solution)/shard_map/ppermute | solution.py:531
  130.6 2.4 %collective-permute-start.31 = (f32[8,128]{1,0:T(8,128)S(1)}, f32[8,128]{1,0:T(8,128)S(1)}, u32[]{:S(2)}, u32[]{:S(2)}) collective-permute-start(f32[8,128]{1,0:T(8,128)S(1)} %get-tuple-element.251), channel_id=1, source_target_pairs={{16,17},{17,16},{1,2},{2,1},{18,19},{19,18},{3,4},{4,3},{20,21},{2... | collective-permute-start | bytes 12296 | tf_op jit(solution)/shard_map/ppermute | solution.py:531
  134.5 1.9 %collective-permute-done.31.got_b = f32[8,128]{1,0:T(8,128)S(1)} collective-permute-done((f32[8,128]{1,0:T(8,128)S(1)}, f32[8,128]{1,0:T(8,128)S(1)}, u32[]{:S(2)}, u32[]{:S(2)}) %collective-permute-start.31) | collective-permute-done | bytes 4128 | tf_op jit(solution)/shard_map/ppermute | solution.py:531
  137.8 2.4 %collective-permute-start.33 = (f32[8,128]{1,0:T(8,128)S(1)}, f32[8,128]{1,0:T(8,128)S(1)}, u32[]{:S(2)}, u32[]{:S(2)}) collective-permute-start(f32[8,128]{1,0:T(8,128)S(1)} %get-tuple-element.259), channel_id=1, source_target_pairs={{16,17},{17,16},{1,2},{2,1},{18,19},{19,18},{3,4},{4,3},{20,21},{2... | collective-permute-start | bytes 12296 | tf_op jit(solution)/shard_map/ppermute | solution.py:531
  141.7 1.9 %collective-permute-done.33.got_b = f32[8,128]{1,0:T(8,128)S(1)} collective-permute-done((f32[8,128]{1,0:T(8,128)S(1)}, f32[8,128]{1,0:T(8,128)S(1)}, u32[]{:S(2)}, u32[]{:S(2)}) %collective-permute-start.33) | collective-permute-done | bytes 4128 | tf_op jit(solution)/shard_map/ppermute | solution.py:531
  145.0 2.4 %collective-permute-start.35 = (f32[8,128]{1,0:T(8,128)S(1)}, f32[8,128]{1,0:T(8,128)S(1)}, u32[]{:S(2)}, u32[]{:S(2)}) collective-permute-start(f32[8,128]{1,0:T(8,128)S(1)} %get-tuple-element.267), channel_id=1, source_target_pairs={{16,17},{17,16},{1,2},{2,1},{18,19},{19,18},{3,4},{4,3},{20,21},{2... | collective-permute-start | bytes 12296 | tf_op jit(solution)/shard_map/ppermute | solution.py:531
  148.9 1.9 %collective-permute-done.35.got_b = f32[8,128]{1,0:T(8,128)S(1)} collective-permute-done((f32[8,128]{1,0:T(8,128)S(1)}, f32[8,128]{1,0:T(8,128)S(1)}, u32[]{:S(2)}, u32[]{:S(2)}) %collective-permute-start.35) | collective-permute-done | bytes 4128 | tf_op jit(solution)/shard_map/ppermute | solution.py:531
  152.1 3.6 %collective-permute-done.36 = f32[4,2,2,128]{3,2,1,0:T(2,128)S(1)} collective-permute-done((f32[4,2,2,128]{3,2,1,0:T(2,128)S(1)}, f32[4,2,2,128]{3,2,1,0:T(2,128)S(1)}, u32[]{:S(2)}, u32[]{:S(2)}) %collective-permute-start.36) | collective-permute-done | bytes 8224 | tf_op jit(solution)/shard_map/ppermute | solution.py:546
  (82 shorter events, 49.2 us)
Async XLA Ops:
  0.1 6.9 %copy-start = (s32[2]{0:T(128)}, s32[2]{0:T(128)S(1)}, u32[]{:S(2)}) copy-start(s32[2]{0:T(128)S(1)} %pad_add_fusion.place_ref) | copy-start | bytes 28
  2.1 31.0 %collective-permute-start.2 = (f32[12,128,128]{2,1,0:T(8,128)S(1)}, f32[12,128,128]{2,1,0:T(8,128)S(1)}, u32[]{:S(2)}, u32[]{:S(2)}) collective-permute-start(f32[12,128,128]{2,1,0:T(8,128)S(1)} %pack.4), channel_id=1, source_target_pairs={{0,16},{16,0},{1,17},{17,1},{2,18},{18,2},{3,19},{19,3},{4,20},{20... | collective-permute-start | bytes 2359304 | tf_op jit(solution)/shard_map/ppermute | solution.py:477
  6.4 26.7 %collective-permute-start.3 = (f32[8,128,128]{2,1,0:T(8,128)}, f32[8,128,128]{2,1,0:T(8,128)S(1)}, u32[]{:S(2)}, u32[]{:S(2)}) collective-permute-start(f32[8,128,128]{2,1,0:T(8,128)} %pack.5), channel_id=1, source_target_pairs={{0,16},{16,0},{1,17},{17,1},{2,18},{18,2},{3,19},{19,3},{4,20},{20... | collective-permute-start | bytes 1572872 | tf_op jit(solution)/shard_map/ppermute | solution.py:477
  13.4 11.9 %all-to-all-start = ((f32[1,1,16,2176]{3,1,0,2:T(1,128)}), f32[1,1,16,2176]{3,1,0,2:T(1,128)}, u32[]{:S(2)}, u32[]{:S(2)}) async-start(f32[1,1,16,2176]{3,1,0,2:T(1,128)} %fusion), calls=%async_computation | async-start | bytes 278528 | tf_op jit(solution)/shard_map/cond/branch_1_fun/all_to_all | solution.py:485
  19.7 9.0 %collective-permute-start.1 = (f32[2,128,128]{2,1,0:T(8,128)S(1)}, f32[2,128,128]{2,1,0:T(8,128)}, u32[]{:S(2)}, u32[]{:S(2)}) collective-permute-start(f32[2,128,128]{2,1,0:T(8,128)S(1)} %get-tuple-element.25), channel_id=1, source_target_pairs={{16,17},{17,16},{1,2},{2,1},{18,19},{19,18},{3,4},{4,3},{20,21},{2... | collective-permute-start | bytes 393224 | tf_op jit(solution)/shard_map/cond/branch_1_fun/ppermute | solution.py:481
  27.2 5.9 %collective-permute-start = (f32[24,128]{1,0:T(8,128)S(1)}, f32[24,128]{1,0:T(8,128)}, u32[]{:S(2)}, u32[]{:S(2)}) collective-permute-start(f32[24,128]{1,0:T(8,128)S(1)} %get-tuple-element.24), channel_id=1, source_target_pairs={{0,16},{16,0},{1,17},{17,1},{2,18},{18,2},{3,19},{19,3},{4,20},{20... | collective-permute-start | bytes 36872 | tf_op jit(solution)/shard_map/cond/branch_1_fun/ppermute | solution.py:496
  34.0 7.3 %collective-permute-start.5 = (f32[264,128]{1,0:T(8,128)S(1)}, f32[264,128]{1,0:T(8,128)S(1)}, u32[]{:S(2)}, u32[]{:S(2)}) collective-permute-start(f32[264,128]{1,0:T(8,128)S(1)} %get-tuple-element.155), channel_id=1, source_target_pairs={{16,17},{17,16},{1,2},{2,1},{18,19},{19,18},{3,4},{4,3},{20,21},{2... | collective-permute-start | bytes 405512 | tf_op jit(solution)/shard_map/ppermute | solution.py:531
  35.9 3.7 %collective-permute-start.4 = (f32[8,128]{1,0:T(8,128)S(1)}, f32[8,128]{1,0:T(8,128)S(1)}, u32[]{:S(2)}, u32[]{:S(2)}) collective-permute-start(f32[8,128]{1,0:T(8,128)S(1)} %get-tuple-element.154), channel_id=1, source_target_pairs={{0,16},{16,0},{1,17},{17,1},{2,18},{18,2},{3,19},{19,3},{4,20},{20... | collective-permute-start | bytes 12296 | tf_op jit(solution)/shard_map/ppermute | solution.py:532
  43.7 3.7 %collective-permute-start.6 = (f32[8,128]{1,0:T(8,128)S(1)}, f32[8,128]{1,0:T(8,128)S(1)}, u32[]{:S(2)}, u32[]{:S(2)}) collective-permute-start(f32[8,128]{1,0:T(8,128)S(1)} %get-tuple-element.160), channel_id=1, source_target_pairs={{0,16},{16,0},{1,17},{17,1},{2,18},{18,2},{3,19},{19,3},{4,20},{20... | collective-permute-start | bytes 12296 | tf_op jit(solution)/shard_map/ppermute | solution.py:532
  43.8 5.8 %collective-permute-start.7 = (f32[8,128]{1,0:T(8,128)S(1)}, f32[8,128]{1,0:T(8,128)S(1)}, u32[]{:S(2)}, u32[]{:S(2)}) collective-permute-start(f32[8,128]{1,0:T(8,128)S(1)} %get-tuple-element.161), channel_id=1, source_target_pairs={{16,17},{17,16},{1,2},{2,1},{18,19},{19,18},{3,4},{4,3},{20,21},{2... | collective-permute-start | bytes 12296 | tf_op jit(solution)/shard_map/ppermute | solution.py:531
  50.9 3.7 %collective-permute-start.8 = (f32[8,128]{1,0:T(8,128)S(1)}, f32[8,128]{1,0:T(8,128)S(1)}, u32[]{:S(2)}, u32[]{:S(2)}) collective-permute-start(f32[8,128]{1,0:T(8,128)S(1)} %get-tuple-element.168), channel_id=1, source_target_pairs={{0,16},{16,0},{1,17},{17,1},{2,18},{18,2},{3,19},{19,3},{4,20},{20... | collective-permute-start | bytes 12296 | tf_op jit(solution)/shard_map/ppermute | solution.py:532
  51.0 5.8 %collective-permute-start.9 = (f32[8,128]{1,0:T(8,128)S(1)}, f32[8,128]{1,0:T(8,128)S(1)}, u32[]{:S(2)}, u32[]{:S(2)}) collective-permute-start(f32[8,128]{1,0:T(8,128)S(1)} %get-tuple-element.169), channel_id=1, source_target_pairs={{16,17},{17,16},{1,2},{2,1},{18,19},{19,18},{3,4},{4,3},{20,21},{2... | collective-permute-start | bytes 12296 | tf_op jit(solution)/shard_map/ppermute | solution.py:531
  58.2 3.7 %collective-permute-start.10 = (f32[8,128]{1,0:T(8,128)S(1)}, f32[8,128]{1,0:T(8,128)S(1)}, u32[]{:S(2)}, u32[]{:S(2)}) collective-permute-start(f32[8,128]{1,0:T(8,128)S(1)} %get-tuple-element.176), channel_id=1, source_target_pairs={{0,16},{16,0},{1,17},{17,1},{2,18},{18,2},{3,19},{19,3},{4,20},{20... | collective-permute-start | bytes 12296 | tf_op jit(solution)/shard_map/ppermute | solution.py:532
  58.2 5.8 %collective-permute-start.11 = (f32[8,128]{1,0:T(8,128)S(1)}, f32[8,128]{1,0:T(8,128)S(1)}, u32[]{:S(2)}, u32[]{:S(2)}) collective-permute-start(f32[8,128]{1,0:T(8,128)S(1)} %get-tuple-element.177), channel_id=1, source_target_pairs={{16,17},{17,16},{1,2},{2,1},{18,19},{19,18},{3,4},{4,3},{20,21},{2... | collective-permute-start | bytes 12296 | tf_op jit(solution)/shard_map/ppermute | solution.py:531
  65.4 3.7 %collective-permute-start.12 = (f32[8,128]{1,0:T(8,128)S(1)}, f32[8,128]{1,0:T(8,128)S(1)}, u32[]{:S(2)}, u32[]{:S(2)}) collective-permute-start(f32[8,128]{1,0:T(8,128)S(1)} %get-tuple-element.185), channel_id=1, source_target_pairs={{0,16},{16,0},{1,17},{17,1},{2,18},{18,2},{3,19},{19,3},{4,20},{20... | collective-permute-start | bytes 12296 | tf_op jit(solution)/shard_map/ppermute | solution.py:532
  65.5 5.8 %collective-permute-start.13 = (f32[8,128]{1,0:T(8,128)S(1)}, f32[8,128]{1,0:T(8,128)S(1)}, u32[]{:S(2)}, u32[]{:S(2)}) collective-permute-start(f32[8,128]{1,0:T(8,128)S(1)} %get-tuple-element.186), channel_id=1, source_target_pairs={{16,17},{17,16},{1,2},{2,1},{18,19},{19,18},{3,4},{4,3},{20,21},{2... | collective-permute-start | bytes 12296 | tf_op jit(solution)/shard_map/ppermute | solution.py:531
  72.6 3.7 %collective-permute-start.14 = (f32[8,128]{1,0:T(8,128)S(1)}, f32[8,128]{1,0:T(8,128)S(1)}, u32[]{:S(2)}, u32[]{:S(2)}) collective-permute-start(f32[8,128]{1,0:T(8,128)S(1)} %get-tuple-element.190), channel_id=1, source_target_pairs={{0,16},{16,0},{1,17},{17,1},{2,18},{18,2},{3,19},{19,3},{4,20},{20... | collective-permute-start | bytes 12296 | tf_op jit(solution)/shard_map/ppermute | solution.py:532
  72.7 5.8 %collective-permute-start.15 = (f32[8,128]{1,0:T(8,128)S(1)}, f32[8,128]{1,0:T(8,128)S(1)}, u32[]{:S(2)}, u32[]{:S(2)}) collective-permute-start(f32[8,128]{1,0:T(8,128)S(1)} %get-tuple-element.191), channel_id=1, source_target_pairs={{16,17},{17,16},{1,2},{2,1},{18,19},{19,18},{3,4},{4,3},{20,21},{2... | collective-permute-start | bytes 12296 | tf_op jit(solution)/shard_map/ppermute | solution.py:531
  79.9 3.7 %collective-permute-start.16 = (f32[8,128]{1,0:T(8,128)S(1)}, f32[8,128]{1,0:T(8,128)S(1)}, u32[]{:S(2)}, u32[]{:S(2)}) collective-permute-start(f32[8,128]{1,0:T(8,128)S(1)} %get-tuple-element.198), channel_id=1, source_target_pairs={{0,16},{16,0},{1,17},{17,1},{2,18},{18,2},{3,19},{19,3},{4,20},{20... | collective-permute-start | bytes 12296 | tf_op jit(solution)/shard_map/ppermute | solution.py:532
  79.9 5.8 %collective-permute-start.17 = (f32[8,128]{1,0:T(8,128)S(1)}, f32[8,128]{1,0:T(8,128)S(1)}, u32[]{:S(2)}, u32[]{:S(2)}) collective-permute-start(f32[8,128]{1,0:T(8,128)S(1)} %get-tuple-element.199), channel_id=1, source_target_pairs={{16,17},{17,16},{1,2},{2,1},{18,19},{19,18},{3,4},{4,3},{20,21},{2... | collective-permute-start | bytes 12296 | tf_op jit(solution)/shard_map/ppermute | solution.py:531
  87.1 3.7 %collective-permute-start.18 = (f32[8,128]{1,0:T(8,128)S(1)}, f32[8,128]{1,0:T(8,128)S(1)}, u32[]{:S(2)}, u32[]{:S(2)}) collective-permute-start(f32[8,128]{1,0:T(8,128)S(1)} %get-tuple-element.206), channel_id=1, source_target_pairs={{0,16},{16,0},{1,17},{17,1},{2,18},{18,2},{3,19},{19,3},{4,20},{20... | collective-permute-start | bytes 12296 | tf_op jit(solution)/shard_map/ppermute | solution.py:532
  87.2 5.8 %collective-permute-start.19 = (f32[8,128]{1,0:T(8,128)S(1)}, f32[8,128]{1,0:T(8,128)S(1)}, u32[]{:S(2)}, u32[]{:S(2)}) collective-permute-start(f32[8,128]{1,0:T(8,128)S(1)} %get-tuple-element.207), channel_id=1, source_target_pairs={{16,17},{17,16},{1,2},{2,1},{18,19},{19,18},{3,4},{4,3},{20,21},{2... | collective-permute-start | bytes 12296 | tf_op jit(solution)/shard_map/ppermute | solution.py:531
  94.3 3.7 %collective-permute-start.20 = (f32[8,128]{1,0:T(8,128)S(1)}, f32[8,128]{1,0:T(8,128)S(1)}, u32[]{:S(2)}, u32[]{:S(2)}) collective-permute-start(f32[8,128]{1,0:T(8,128)S(1)} %get-tuple-element.215), channel_id=1, source_target_pairs={{0,16},{16,0},{1,17},{17,1},{2,18},{18,2},{3,19},{19,3},{4,20},{20... | collective-permute-start | bytes 12296 | tf_op jit(solution)/shard_map/ppermute | solution.py:532
  94.4 5.8 %collective-permute-start.21 = (f32[8,128]{1,0:T(8,128)S(1)}, f32[8,128]{1,0:T(8,128)S(1)}, u32[]{:S(2)}, u32[]{:S(2)}) collective-permute-start(f32[8,128]{1,0:T(8,128)S(1)} %get-tuple-element.216), channel_id=1, source_target_pairs={{16,17},{17,16},{1,2},{2,1},{18,19},{19,18},{3,4},{4,3},{20,21},{2... | collective-permute-start | bytes 12296 | tf_op jit(solution)/shard_map/ppermute | solution.py:531
  101.6 3.7 %collective-permute-start.22 = (f32[8,128]{1,0:T(8,128)S(1)}, f32[8,128]{1,0:T(8,128)S(1)}, u32[]{:S(2)}, u32[]{:S(2)}) collective-permute-start(f32[8,128]{1,0:T(8,128)S(1)} %get-tuple-element.220), channel_id=1, source_target_pairs={{0,16},{16,0},{1,17},{17,1},{2,18},{18,2},{3,19},{19,3},{4,20},{20... | collective-permute-start | bytes 12296 | tf_op jit(solution)/shard_map/ppermute | solution.py:532
  101.6 5.8 %collective-permute-start.23 = (f32[8,128]{1,0:T(8,128)S(1)}, f32[8,128]{1,0:T(8,128)S(1)}, u32[]{:S(2)}, u32[]{:S(2)}) collective-permute-start(f32[8,128]{1,0:T(8,128)S(1)} %get-tuple-element.221), channel_id=1, source_target_pairs={{16,17},{17,16},{1,2},{2,1},{18,19},{19,18},{3,4},{4,3},{20,21},{2... | collective-permute-start | bytes 12296 | tf_op jit(solution)/shard_map/ppermute | solution.py:531
  108.8 3.7 %collective-permute-start.24 = (f32[8,128]{1,0:T(8,128)S(1)}, f32[8,128]{1,0:T(8,128)S(1)}, u32[]{:S(2)}, u32[]{:S(2)}) collective-permute-start(f32[8,128]{1,0:T(8,128)S(1)} %get-tuple-element.228), channel_id=1, source_target_pairs={{0,16},{16,0},{1,17},{17,1},{2,18},{18,2},{3,19},{19,3},{4,20},{20... | collective-permute-start | bytes 12296 | tf_op jit(solution)/shard_map/ppermute | solution.py:532
  108.9 5.8 %collective-permute-start.25 = (f32[8,128]{1,0:T(8,128)S(1)}, f32[8,128]{1,0:T(8,128)S(1)}, u32[]{:S(2)}, u32[]{:S(2)}) collective-permute-start(f32[8,128]{1,0:T(8,128)S(1)} %get-tuple-element.229), channel_id=1, source_target_pairs={{16,17},{17,16},{1,2},{2,1},{18,19},{19,18},{3,4},{4,3},{20,21},{2... | collective-permute-start | bytes 12296 | tf_op jit(solution)/shard_map/ppermute | solution.py:531
  116.0 3.7 %collective-permute-start.26 = (f32[8,128]{1,0:T(8,128)S(1)}, f32[8,128]{1,0:T(8,128)S(1)}, u32[]{:S(2)}, u32[]{:S(2)}) collective-permute-start(f32[8,128]{1,0:T(8,128)S(1)} %get-tuple-element.236), channel_id=1, source_target_pairs={{0,16},{16,0},{1,17},{17,1},{2,18},{18,2},{3,19},{19,3},{4,20},{20... | collective-permute-start | bytes 12296 | tf_op jit(solution)/shard_map/ppermute | solution.py:532
  116.1 5.8 %collective-permute-start.27 = (f32[8,128]{1,0:T(8,128)S(1)}, f32[8,128]{1,0:T(8,128)S(1)}, u32[]{:S(2)}, u32[]{:S(2)}) collective-permute-start(f32[8,128]{1,0:T(8,128)S(1)} %get-tuple-element.237), channel_id=1, source_target_pairs={{16,17},{17,16},{1,2},{2,1},{18,19},{19,18},{3,4},{4,3},{20,21},{2... | collective-permute-start | bytes 12296 | tf_op jit(solution)/shard_map/ppermute | solution.py:531
  123.3 3.7 %collective-permute-start.28 = (f32[8,128]{1,0:T(8,128)S(1)}, f32[8,128]{1,0:T(8,128)S(1)}, u32[]{:S(2)}, u32[]{:S(2)}) collective-permute-start(f32[8,128]{1,0:T(8,128)S(1)} %get-tuple-element.245), channel_id=1, source_target_pairs={{0,16},{16,0},{1,17},{17,1},{2,18},{18,2},{3,19},{19,3},{4,20},{20... | collective-permute-start | bytes 12296 | tf_op jit(solution)/shard_map/ppermute | solution.py:532
  123.3 5.8 %collective-permute-start.29 = (f32[8,128]{1,0:T(8,128)S(1)}, f32[8,128]{1,0:T(8,128)S(1)}, u32[]{:S(2)}, u32[]{:S(2)}) collective-permute-start(f32[8,128]{1,0:T(8,128)S(1)} %get-tuple-element.246), channel_id=1, source_target_pairs={{16,17},{17,16},{1,2},{2,1},{18,19},{19,18},{3,4},{4,3},{20,21},{2... | collective-permute-start | bytes 12296 | tf_op jit(solution)/shard_map/ppermute | solution.py:531
  130.5 3.7 %collective-permute-start.30 = (f32[8,128]{1,0:T(8,128)S(1)}, f32[8,128]{1,0:T(8,128)S(1)}, u32[]{:S(2)}, u32[]{:S(2)}) collective-permute-start(f32[8,128]{1,0:T(8,128)S(1)} %get-tuple-element.250), channel_id=1, source_target_pairs={{0,16},{16,0},{1,17},{17,1},{2,18},{18,2},{3,19},{19,3},{4,20},{20... | collective-permute-start | bytes 12296 | tf_op jit(solution)/shard_map/ppermute | solution.py:532
  130.6 5.8 %collective-permute-start.31 = (f32[8,128]{1,0:T(8,128)S(1)}, f32[8,128]{1,0:T(8,128)S(1)}, u32[]{:S(2)}, u32[]{:S(2)}) collective-permute-start(f32[8,128]{1,0:T(8,128)S(1)} %get-tuple-element.251), channel_id=1, source_target_pairs={{16,17},{17,16},{1,2},{2,1},{18,19},{19,18},{3,4},{4,3},{20,21},{2... | collective-permute-start | bytes 12296 | tf_op jit(solution)/shard_map/ppermute | solution.py:531
  137.7 3.7 %collective-permute-start.32 = (f32[8,128]{1,0:T(8,128)S(1)}, f32[8,128]{1,0:T(8,128)S(1)}, u32[]{:S(2)}, u32[]{:S(2)}) collective-permute-start(f32[8,128]{1,0:T(8,128)S(1)} %get-tuple-element.258), channel_id=1, source_target_pairs={{0,16},{16,0},{1,17},{17,1},{2,18},{18,2},{3,19},{19,3},{4,20},{20... | collective-permute-start | bytes 12296 | tf_op jit(solution)/shard_map/ppermute | solution.py:532
  137.8 5.8 %collective-permute-start.33 = (f32[8,128]{1,0:T(8,128)S(1)}, f32[8,128]{1,0:T(8,128)S(1)}, u32[]{:S(2)}, u32[]{:S(2)}) collective-permute-start(f32[8,128]{1,0:T(8,128)S(1)} %get-tuple-element.259), channel_id=1, source_target_pairs={{16,17},{17,16},{1,2},{2,1},{18,19},{19,18},{3,4},{4,3},{20,21},{2... | collective-permute-start | bytes 12296 | tf_op jit(solution)/shard_map/ppermute | solution.py:531
  145.0 3.7 %collective-permute-start.34 = (f32[8,128]{1,0:T(8,128)S(1)}, f32[8,128]{1,0:T(8,128)S(1)}, u32[]{:S(2)}, u32[]{:S(2)}) collective-permute-start(f32[8,128]{1,0:T(8,128)S(1)} %get-tuple-element.266), channel_id=1, source_target_pairs={{0,16},{16,0},{1,17},{17,1},{2,18},{18,2},{3,19},{19,3},{4,20},{20... | collective-permute-start | bytes 12296 | tf_op jit(solution)/shard_map/ppermute | solution.py:532
  145.0 5.8 %collective-permute-start.35 = (f32[8,128]{1,0:T(8,128)S(1)}, f32[8,128]{1,0:T(8,128)S(1)}, u32[]{:S(2)}, u32[]{:S(2)}) collective-permute-start(f32[8,128]{1,0:T(8,128)S(1)} %get-tuple-element.267), channel_id=1, source_target_pairs={{16,17},{17,16},{1,2},{2,1},{18,19},{19,18},{3,4},{4,3},{20,21},{2... | collective-permute-start | bytes 12296 | tf_op jit(solution)/shard_map/ppermute | solution.py:531
  152.0 3.7 %collective-permute-start.36 = (f32[4,2,2,128]{3,2,1,0:T(2,128)S(1)}, f32[4,2,2,128]{3,2,1,0:T(2,128)S(1)}, u32[]{:S(2)}, u32[]{:S(2)}) collective-permute-start(f32[4,2,2,128]{3,2,1,0:T(2,128)S(1)} %rev.12), channel_id=1, source_target_pairs={{0,16},{16,0},{1,17},{17,1},{2,18},{18,2},{3,19},{19,3},{4,20},{20... | collective-permute-start | bytes 24584 | tf_op jit(solution)/shard_map/ppermute | solution.py:546

commit v10 on v9

--- a/solution.py
+++ b/solution.py
@@ -320,14 +320,16 @@
 
 
 def small_part(small, index):
-    keep, recv = small
+    n = N * HALF
+    return small[index * n:(index + 1) * n, :]
+
+
+def start_kernel(keep, recv_0, recv_1, small_keep, small_recv, msg_a, msg_b, q_out, small):
     n = ROWS * HALF
-    i = index * n
-    return jnp.concatenate([keep[i:i + n, :], recv[i + HALF:i + n, :], recv[i:i + HALF, :]], axis=0)
-
-
-def start_kernel(keep, recv_0, recv_1, small_keep, small_recv, msg_a, msg_b, q_out):
-    small = (small_keep, small_recv)
+    for i in range(0, small_keep.shape[0], n):
+        small[2 * i:2 * i + n, :] = small_keep[i:i + n, :]
+        small[2 * i + n:2 * i + n + HALF, :] = small_recv[i + HALF:i + n, :]
+        small[2 * i + n + HALF:2 * i + 2 * n, :] = small_recv[i:i + HALF, :]
     halves = ((keep,), (recv_0, recv_1))
     f = small_part(small, INITIAL)
     q = inner_product(f, halves)
@@ -368,7 +370,7 @@
 def beside_kernel(begin, keep, recv_0, recv_1, beyond_0, first_b, got_a, q_ref, *refs):
     halves = ((keep,), (recv_0, recv_1))
     response_out, q_out = refs[-2:]
-    f = small_part(refs[:2], INITIAL) if begin else refs[0][...]
+    f = small_part(refs[0], INITIAL) if begin else refs[0][...]
     q = q_ref[...]
     response, total = [], []
     for j, b in TILES:
@@ -381,9 +383,7 @@
     q_out[...] = jnp.concatenate(total, axis=0)
 
 
-def pair_kernel(instant, pair, last, keep, recv_0, recv_1, small_keep, small_recv, got_a, got_b, response_ref, q_ref,
-                *refs):
-    small = (small_keep, small_recv)
+def pair_kernel(instant, pair, last, keep, recv_0, recv_1, small, got_a, got_b, response_ref, q_ref, *refs):
     halves = ((keep,), (recv_0, recv_1))
     first = pair == 0
     capacity = small_part(small, CAPACITY)
@@ -520,7 +520,8 @@
         )(*ins)
 
     first_shape = jax.ShapeDtypeStruct((2 * N + ROWS * width, width), jnp.float32)
-    msg_a, msg_b, q = call(start_kernel, (shape, first_shape, shape), 28, *halves, *small)
+    unit_small = jax.ShapeDtypeStruct(((STEPS + 2) * N * HALF, width), jnp.float32)
+    msg_a, msg_b, q, small = call(start_kernel, (shape, first_shape, shape, unit_small), 28, *halves, *small)
     field, first_b = (), None
     frames = []
     state = ()
@@ -533,9 +534,9 @@
             if first_b is None:
                 first_b = got_b
             response, q = call(functools.partial(beside_kernel, not field), (shape,) * 2, 12, *halves, beyond_0, first_b,
-                               got_a, q, *(field or small))
+                               got_a, q, *(field or (small,)))
             out = call(functools.partial(pair_kernel, instant, pair, last), (shape,) * (1 if last else 4 if closing else 6),
-                       68, *halves, *small, got_a, got_b, response, q, *field, *state)
+                       68, *halves, small, got_a, got_b, response, q, *field, *state)
             field = out[:1]
             if not last:
                 q, msg_a, msg_b = out[1:4]

time: 159 us -> 145 us (0.912); the launches traced: 156 us -> 144 us
  Pallas kernels: 35.1 us -> 23.1 us
    pallas_call x33, Pallas kernels: 27.2 us -> 15.2 us  [call(): pl.pallas_call(body, out_shape=outs, in_specs=[vmem] * len(ins), out_spec...]
  transfers between devices with their start and end apart: 38 -> 38, of which waited for: 35 -> 35; matrix products, arithmetic and copies ran while one was open for 4% -> 4% of each run, Pallas kernels for 6% -> 7%
where the time goes in v10:
time: 145 us; the launch traced here: 144 us
  waiting for transfers between devices  60.1 us (41%)
  starting transfers between devices  53.9 us (37%)
  Pallas kernels  23.1 us (16%)
  local copies, waits for them, and re-layouts  4.36 us (3%)
  other arithmetic  2.4 us (2%)
    ppermute x16, starting transfers between devices, shards_chain(): got_b = lax.ppermute(msg_b, both, b_pairs)  38.1 us
    ppermute x16, waiting for transfers between devices, shards_chain(): got_b = lax.ppermute(msg_b, both, b_pairs)  30.8 us
    ppermute x16, waiting for transfers between devices, shards_chain(): got_a = lax.ppermute(msg_a, 'row', swap)  19.7 us
    pallas_call x33, Pallas kernels, call(): pl.pallas_call(body, out_shape=outs, in_specs=[vmem] * len(ins), out_spec...  15.2 us
    pallas_call x3, Pallas kernels, pack(): pl.pallas_call(functools.partial(pack_kernel, n_col, sent, first, count),...  6.99 us
    all_to_all x1, starting transfers between devices, beside(): lax.all_to_all(packed, 'col', split_axis=2, concat_axis=1, tiled=True)  6.27 us
    ppermute x1, waiting for transfers between devices, shards_chain(): got = lax.ppermute(jnp.flip(done[:, ROWS:], 1), 'row', swap)  3.63 us
    ppermute x1, waiting for transfers between devices, beside(): return (small, lax.ppermute(send, 'row', swap), beyond_0)  3.41 us
  transfers between devices with their start and end apart: 38, of which 35 were waited for; matrix products, arithmetic and copies ran while one was open for 4% of the time, Pallas kernels for 7%

profile of v10, /device:TPU:8, one launch (start us, length us, event | category | flops | bytes accessed | tf_op | source)
XLA Modules:
  0.0 144.4 jit_solution(13287680660857183577)
XLA Ops:
  0.1 2.0 %pack.4 = f32[12,128,128]{2,1,0:T(8,128)S(1)} custom-call(s32[2]{0:T(128)S(1)} %pad_add_fusion.place_ref, s32[2,4,4]{2,1,0:T(4,128)} %pattern_ref.5, f32[2,4,128,128]{3,2,1,0:T(8,128)} %own_hbm.5, f32[4,2,4,128,128]{4,3,2,1,0:T(8,128)} %nb_hbm.5), custom_call_target="tpu_custom_call" | custom-call | tf_op jit(solution)/shard_map/pack/pallas_call | solution.py:464
  2.1 1.6 %collective-permute-start.2 = (f32[12,128,128]{2,1,0:T(8,128)S(1)}, f32[12,128,128]{2,1,0:T(8,128)S(1)}, u32[]{:S(2)}, u32[]{:S(2)}) collective-permute-start(f32[12,128,128]{2,1,0:T(8,128)S(1)} %pack.4), channel_id=1, source_target_pairs={{0,16},{16,0},{1,17},{17,1},{2,18},{18,2},{3,19},{19,3},{4,20},{20... | collective-permute-start | bytes 2359304 | tf_op jit(solution)/shard_map/ppermute | solution.py:477
  3.7 2.7 %pack.5 = f32[8,128,128]{2,1,0:T(8,128)} custom-call(s32[2]{0:T(128)S(1)} %pad_add_fusion.place_ref, s32[2,4,4]{2,1,0:T(4,128)} %pattern_ref.5, f32[2,4,128,128]{3,2,1,0:T(8,128)} %own_hbm.5, f32[4,2,4,128,128]{4,3,2,1,0:T(8,128)} %nb_hbm.5), custom_call_target="tpu_custom_call" | custom-call | tf_op jit(solution)/shard_map/pack/pallas_call | solution.py:464
  7.0 2.3 %pack.3 = (f32[20,128,128]{2,1,0:T(8,128)S(1)}, f32[2,128,128]{2,1,0:T(8,128)S(1)}) custom-call(s32[2]{0:T(128)S(1)} %pad_add_fusion.place_ref, s32[2,4,4]{2,1,0:T(4,128)} %pattern_ref.5, f32[2,4,128,128]{3,2,1,0:T(8,128)} %own_hbm.5, f32[4,2,4,128,128]{4,3,2,1,0:T(8,128)} %nb_hbm.5), custom_call_target="tpu_custom_call" | custom-call | tf_op jit(solution)/shard_map/pack/pallas_call | solution.py:464
  9.2 23.8 %conditional.1 = (f32[24,128]{1,0:T(8,128)S(1)}, f32[24,128]{1,0:T(8,128)}, f32[2,128,128]{2,1,0:T(8,128)S(1)}) conditional(s32[]{:T(128)} %convert_element_type.8, f32[2,128,128]{2,1,0:T(8,128)S(1)} %get-tuple-element.152, (f32[1,1,16,4,512]{4,3,2,1,0:T(4,128)}, s32[1,1,16,4]{2,3,1,0:T(4,128)}, s32[2]{0:T(128)}, f32[2,4,128]{2,1,0:T(4,128)}, ...), branch_computations={%region_0.1_spmd, %region_1.2_spmd} | conditional | flops 104512 | bytes 2065800 | solution.py:498
  10.0 1.7 %reshape.17 = f32[1,1,16,2048]{3,1,0,2:T(1,128)} reshape(f32[1,1,16,4,512]{4,3,2,1,0:T(4,128)} %get-tuple-element.280) | data formatting | bytes 262144 | tf_op jit(solution)/shard_map/cond/branch_1_fun/reshape | solution.py:484
  11.8 1.7 %fusion = f32[1,1,16,2176]{3,1,0,2:T(1,128)} fusion(f32[1,1,16,4]{3,1,0,2:T(1,128)S(1)} %convert_element_type.6, f32[1,1,16,2048]{3,1,0,2:T(1,128)} %reshape.17), kind=kLoop, calls=%fused_computation.1 | loop fusion | flops 104448 | bytes 270592 | tf_op jit(solution)/shard_map/cond/branch_1_fun/concatenate | solution.py:484
  13.4 6.3 %all-to-all-start = ((f32[1,1,16,2176]{3,1,0,2:T(1,128)}), f32[1,1,16,2176]{3,1,0,2:T(1,128)}, u32[]{:S(2)}, u32[]{:S(2)}) async-start(f32[1,1,16,2176]{3,1,0,2:T(1,128)} %fusion), calls=%async_computation | async-start | bytes 278528 | tf_op jit(solution)/shard_map/cond/branch_1_fun/all_to_all | solution.py:485
  19.7 3.1 %collective-permute-start.1 = (f32[2,128,128]{2,1,0:T(8,128)S(1)}, f32[2,128,128]{2,1,0:T(8,128)}, u32[]{:S(2)}, u32[]{:S(2)}) collective-permute-start(f32[2,128,128]{2,1,0:T(8,128)S(1)} %get-tuple-element.25), channel_id=1, source_target_pairs={{16,17},{17,16},{1,2},{2,1},{18,19},{19,18},{3,4},{4,3},{20,21},{2... | collective-permute-start | bytes 393224 | tf_op jit(solution)/shard_map/cond/branch_1_fun/ppermute | solution.py:481
  22.8 2.5 %all-to-all-done = f32[1,1,16,2176]{3,1,0,2:T(1,128)} async-done(((f32[1,1,16,2176]{3,1,0,2:T(1,128)}), f32[1,1,16,2176]{3,1,0,2:T(1,128)}, u32[]{:S(2)}, u32[]{:S(2)}) %all-to-all-start) | async-done | bytes 139296 | tf_op jit(solution)/shard_map/cond/branch_1_fun/all_to_all | solution.py:485
  27.2 1.6 %collective-permute-start = (f32[24,128]{1,0:T(8,128)S(1)}, f32[24,128]{1,0:T(8,128)}, u32[]{:S(2)}, u32[]{:S(2)}) collective-permute-start(f32[24,128]{1,0:T(8,128)S(1)} %get-tuple-element.24), channel_id=1, source_target_pairs={{0,16},{16,0},{1,17},{17,1},{2,18},{18,2},{3,19},{19,3},{4,20},{20... | collective-permute-start | bytes 36872 | tf_op jit(solution)/shard_map/cond/branch_1_fun/ppermute | solution.py:496
  29.6 3.4 %collective-permute-done = f32[24,128]{1,0:T(8,128)} collective-permute-done((f32[24,128]{1,0:T(8,128)S(1)}, f32[24,128]{1,0:T(8,128)}, u32[]{:S(2)}, u32[]{:S(2)}) %collective-permute-start) | collective-permute-done | bytes 12320 | tf_op jit(solution)/shard_map/cond/branch_1_fun/ppermute | solution.py:496
  34.0 1.9 %collective-permute-start.5 = (f32[264,128]{1,0:T(8,128)S(1)}, f32[264,128]{1,0:T(8,128)S(1)}, u32[]{:S(2)}, u32[]{:S(2)}) collective-permute-start(f32[264,128]{1,0:T(8,128)S(1)} %get-tuple-element.157), channel_id=1, source_target_pairs={{16,17},{17,16},{1,2},{2,1},{18,19},{19,18},{3,4},{4,3},{20,21},{2... | collective-permute-start | bytes 405512 | tf_op jit(solution)/shard_map/ppermute | solution.py:532
  36.0 1.6 %collective-permute-start.4 = (f32[8,128]{1,0:T(8,128)S(1)}, f32[8,128]{1,0:T(8,128)S(1)}, u32[]{:S(2)}, u32[]{:S(2)}) collective-permute-start(f32[8,128]{1,0:T(8,128)S(1)} %get-tuple-element.156), channel_id=1, source_target_pairs={{0,16},{16,0},{1,17},{17,1},{2,18},{18,2},{3,19},{19,3},{4,20},{20... | collective-permute-start | bytes 12296 | tf_op jit(solution)/shard_map/ppermute | solution.py:533
  37.5 2.1 %collective-permute-done.4.got_a = f32[8,128]{1,0:T(8,128)S(1)} collective-permute-done((f32[8,128]{1,0:T(8,128)S(1)}, f32[8,128]{1,0:T(8,128)S(1)}, u32[]{:S(2)}, u32[]{:S(2)}) %collective-permute-start.4) | collective-permute-done | bytes 4128 | tf_op jit(solution)/shard_map/ppermute | solution.py:533
  39.6 1.7 %collective-permute-done.5.first_b.got_b = f32[264,128]{1,0:T(8,128)S(1)} collective-permute-done((f32[264,128]{1,0:T(8,128)S(1)}, f32[264,128]{1,0:T(8,128)S(1)}, u32[]{:S(2)}, u32[]{:S(2)}) %collective-permute-start.5) | collective-permute-done | bytes 135200 | tf_op jit(solution)/shard_map/ppermute | solution.py:532
  42.4 2.0 %collective-permute-start.7 = (f32[8,128]{1,0:T(8,128)S(1)}, f32[8,128]{1,0:T(8,128)S(1)}, u32[]{:S(2)}, u32[]{:S(2)}) collective-permute-start(f32[8,128]{1,0:T(8,128)S(1)} %get-tuple-element.163), channel_id=1, source_target_pairs={{16,17},{17,16},{1,2},{2,1},{18,19},{19,18},{3,4},{4,3},{20,21},{2... | collective-permute-start | bytes 12296 | tf_op jit(solution)/shard_map/ppermute | solution.py:532
  44.3 1.6 %collective-permute-done.6.got_a = f32[8,128]{1,0:T(8,128)S(1)} collective-permute-done((f32[8,128]{1,0:T(8,128)S(1)}, f32[8,128]{1,0:T(8,128)S(1)}, u32[]{:S(2)}, u32[]{:S(2)}) %collective-permute-start.6) | collective-permute-done | bytes 4128 | tf_op jit(solution)/shard_map/ppermute | solution.py:533
  46.2 1.9 %collective-permute-done.7.got_b = f32[8,128]{1,0:T(8,128)S(1)} collective-permute-done((f32[8,128]{1,0:T(8,128)S(1)}, f32[8,128]{1,0:T(8,128)S(1)}, u32[]{:S(2)}, u32[]{:S(2)}) %collective-permute-start.7) | collective-permute-done | bytes 4128 | tf_op jit(solution)/shard_map/ppermute | solution.py:532
  48.9 2.4 %collective-permute-start.9 = (f32[8,128]{1,0:T(8,128)S(1)}, f32[8,128]{1,0:T(8,128)S(1)}, u32[]{:S(2)}, u32[]{:S(2)}) collective-permute-start(f32[8,128]{1,0:T(8,128)S(1)} %get-tuple-element.171), channel_id=1, source_target_pairs={{16,17},{17,16},{1,2},{2,1},{18,19},{19,18},{3,4},{4,3},{20,21},{2... | collective-permute-start | bytes 12296 | tf_op jit(solution)/shard_map/ppermute | solution.py:532
  52.8 1.9 %collective-permute-done.9.got_b = f32[8,128]{1,0:T(8,128)S(1)} collective-permute-done((f32[8,128]{1,0:T(8,128)S(1)}, f32[8,128]{1,0:T(8,128)S(1)}, u32[]{:S(2)}, u32[]{:S(2)}) %collective-permute-start.9) | collective-permute-done | bytes 4128 | tf_op jit(solution)/shard_map/ppermute | solution.py:532
  55.4 2.4 %collective-permute-start.11 = (f32[8,128]{1,0:T(8,128)S(1)}, f32[8,128]{1,0:T(8,128)S(1)}, u32[]{:S(2)}, u32[]{:S(2)}) collective-permute-start(f32[8,128]{1,0:T(8,128)S(1)} %get-tuple-element.179), channel_id=1, source_target_pairs={{16,17},{17,16},{1,2},{2,1},{18,19},{19,18},{3,4},{4,3},{20,21},{2... | collective-permute-start | bytes 12296 | tf_op jit(solution)/shard_map/ppermute | solution.py:532
  59.3 1.9 %collective-permute-done.11.got_b = f32[8,128]{1,0:T(8,128)S(1)} collective-permute-done((f32[8,128]{1,0:T(8,128)S(1)}, f32[8,128]{1,0:T(8,128)S(1)}, u32[]{:S(2)}, u32[]{:S(2)}) %collective-permute-start.11) | collective-permute-done | bytes 4128 | tf_op jit(solution)/shard_map/ppermute | solution.py:532
  61.9 2.4 %collective-permute-start.13 = (f32[8,128]{1,0:T(8,128)S(1)}, f32[8,128]{1,0:T(8,128)S(1)}, u32[]{:S(2)}, u32[]{:S(2)}) collective-permute-start(f32[8,128]{1,0:T(8,128)S(1)} %get-tuple-element.188), channel_id=1, source_target_pairs={{16,17},{17,16},{1,2},{2,1},{18,19},{19,18},{3,4},{4,3},{20,21},{2... | collective-permute-start | bytes 12296 | tf_op jit(solution)/shard_map/ppermute | solution.py:532
  65.8 1.9 %collective-permute-done.13.got_b = f32[8,128]{1,0:T(8,128)S(1)} collective-permute-done((f32[8,128]{1,0:T(8,128)S(1)}, f32[8,128]{1,0:T(8,128)S(1)}, u32[]{:S(2)}, u32[]{:S(2)}) %collective-permute-start.13) | collective-permute-done | bytes 4128 | tf_op jit(solution)/shard_map/ppermute | solution.py:532
  68.5 2.4 %collective-permute-start.15 = (f32[8,128]{1,0:T(8,128)S(1)}, f32[8,128]{1,0:T(8,128)S(1)}, u32[]{:S(2)}, u32[]{:S(2)}) collective-permute-start(f32[8,128]{1,0:T(8,128)S(1)} %get-tuple-element.193), channel_id=1, source_target_pairs={{16,17},{17,16},{1,2},{2,1},{18,19},{19,18},{3,4},{4,3},{20,21},{2... | collective-permute-start | bytes 12296 | tf_op jit(solution)/shard_map/ppermute | solution.py:532
  72.4 1.9 %collective-permute-done.15.got_b = f32[8,128]{1,0:T(8,128)S(1)} collective-permute-done((f32[8,128]{1,0:T(8,128)S(1)}, f32[8,128]{1,0:T(8,128)S(1)}, u32[]{:S(2)}, u32[]{:S(2)}) %collective-permute-start.15) | collective-permute-done | bytes 4128 | tf_op jit(solution)/shard_map/ppermute | solution.py:532
  75.0 2.4 %collective-permute-start.17 = (f32[8,128]{1,0:T(8,128)S(1)}, f32[8,128]{1,0:T(8,128)S(1)}, u32[]{:S(2)}, u32[]{:S(2)}) collective-permute-start(f32[8,128]{1,0:T(8,128)S(1)} %get-tuple-element.201), channel_id=1, source_target_pairs={{16,17},{17,16},{1,2},{2,1},{18,19},{19,18},{3,4},{4,3},{20,21},{2... | collective-permute-start | bytes 12296 | tf_op jit(solution)/shard_map/ppermute | solution.py:532
  78.9 1.9 %collective-permute-done.17.got_b = f32[8,128]{1,0:T(8,128)S(1)} collective-permute-done((f32[8,128]{1,0:T(8,128)S(1)}, f32[8,128]{1,0:T(8,128)S(1)}, u32[]{:S(2)}, u32[]{:S(2)}) %collective-permute-start.17) | collective-permute-done | bytes 4128 | tf_op jit(solution)/shard_map/ppermute | solution.py:532
  81.5 2.4 %collective-permute-start.19 = (f32[8,128]{1,0:T(8,128)S(1)}, f32[8,128]{1,0:T(8,128)S(1)}, u32[]{:S(2)}, u32[]{:S(2)}) collective-permute-start(f32[8,128]{1,0:T(8,128)S(1)} %get-tuple-element.209), channel_id=1, source_target_pairs={{16,17},{17,16},{1,2},{2,1},{18,19},{19,18},{3,4},{4,3},{20,21},{2... | collective-permute-start | bytes 12296 | tf_op jit(solution)/shard_map/ppermute | solution.py:532
  85.4 1.9 %collective-permute-done.19.got_b = f32[8,128]{1,0:T(8,128)S(1)} collective-permute-done((f32[8,128]{1,0:T(8,128)S(1)}, f32[8,128]{1,0:T(8,128)S(1)}, u32[]{:S(2)}, u32[]{:S(2)}) %collective-permute-start.19) | collective-permute-done | bytes 4128 | tf_op jit(solution)/shard_map/ppermute | solution.py:532
  88.1 2.4 %collective-permute-start.21 = (f32[8,128]{1,0:T(8,128)S(1)}, f32[8,128]{1,0:T(8,128)S(1)}, u32[]{:S(2)}, u32[]{:S(2)}) collective-permute-start(f32[8,128]{1,0:T(8,128)S(1)} %get-tuple-element.218), channel_id=1, source_target_pairs={{16,17},{17,16},{1,2},{2,1},{18,19},{19,18},{3,4},{4,3},{20,21},{2... | collective-permute-start | bytes 12296 | tf_op jit(solution)/shard_map/ppermute | solution.py:532
  91.9 1.9 %collective-permute-done.21.got_b = f32[8,128]{1,0:T(8,128)S(1)} collective-permute-done((f32[8,128]{1,0:T(8,128)S(1)}, f32[8,128]{1,0:T(8,128)S(1)}, u32[]{:S(2)}, u32[]{:S(2)}) %collective-permute-start.21) | collective-permute-done | bytes 4128 | tf_op jit(solution)/shard_map/ppermute | solution.py:532
  94.6 2.6 %collective-permute-start.23 = (f32[8,128]{1,0:T(8,128)S(1)}, f32[8,128]{1,0:T(8,128)S(1)}, u32[]{:S(2)}, u32[]{:S(2)}) collective-permute-start(f32[8,128]{1,0:T(8,128)S(1)} %get-tuple-element.223), channel_id=1, source_target_pairs={{16,17},{17,16},{1,2},{2,1},{18,19},{19,18},{3,4},{4,3},{20,21},{2... | collective-permute-start | bytes 12296 | tf_op jit(solution)/shard_map/ppermute | solution.py:532
  98.5 1.9 %collective-permute-done.23.got_b = f32[8,128]{1,0:T(8,128)S(1)} collective-permute-done((f32[8,128]{1,0:T(8,128)S(1)}, f32[8,128]{1,0:T(8,128)S(1)}, u32[]{:S(2)}, u32[]{:S(2)}) %collective-permute-start.23) | collective-permute-done | bytes 4128 | tf_op jit(solution)/shard_map/ppermute | solution.py:532
  101.1 2.4 %collective-permute-start.25 = (f32[8,128]{1,0:T(8,128)S(1)}, f32[8,128]{1,0:T(8,128)S(1)}, u32[]{:S(2)}, u32[]{:S(2)}) collective-permute-start(f32[8,128]{1,0:T(8,128)S(1)} %get-tuple-element.231), channel_id=1, source_target_pairs={{16,17},{17,16},{1,2},{2,1},{18,19},{19,18},{3,4},{4,3},{20,21},{2... | collective-permute-start | bytes 12296 | tf_op jit(solution)/shard_map/ppermute | solution.py:532
  105.0 1.9 %collective-permute-done.25.got_b = f32[8,128]{1,0:T(8,128)S(1)} collective-permute-done((f32[8,128]{1,0:T(8,128)S(1)}, f32[8,128]{1,0:T(8,128)S(1)}, u32[]{:S(2)}, u32[]{:S(2)}) %collective-permute-start.25) | collective-permute-done | bytes 4128 | tf_op jit(solution)/shard_map/ppermute | solution.py:532
  107.6 2.4 %collective-permute-start.27 = (f32[8,128]{1,0:T(8,128)S(1)}, f32[8,128]{1,0:T(8,128)S(1)}, u32[]{:S(2)}, u32[]{:S(2)}) collective-permute-start(f32[8,128]{1,0:T(8,128)S(1)} %get-tuple-element.239), channel_id=1, source_target_pairs={{16,17},{17,16},{1,2},{2,1},{18,19},{19,18},{3,4},{4,3},{20,21},{2... | collective-permute-start | bytes 12296 | tf_op jit(solution)/shard_map/ppermute | solution.py:532
  111.5 1.9 %collective-permute-done.27.got_b = f32[8,128]{1,0:T(8,128)S(1)} collective-permute-done((f32[8,128]{1,0:T(8,128)S(1)}, f32[8,128]{1,0:T(8,128)S(1)}, u32[]{:S(2)}, u32[]{:S(2)}) %collective-permute-start.27) | collective-permute-done | bytes 4128 | tf_op jit(solution)/shard_map/ppermute | solution.py:532
  114.2 2.4 %collective-permute-start.29 = (f32[8,128]{1,0:T(8,128)S(1)}, f32[8,128]{1,0:T(8,128)S(1)}, u32[]{:S(2)}, u32[]{:S(2)}) collective-permute-start(f32[8,128]{1,0:T(8,128)S(1)} %get-tuple-element.248), channel_id=1, source_target_pairs={{16,17},{17,16},{1,2},{2,1},{18,19},{19,18},{3,4},{4,3},{20,21},{2... | collective-permute-start | bytes 12296 | tf_op jit(solution)/shard_map/ppermute | solution.py:532
  118.1 1.9 %collective-permute-done.29.got_b = f32[8,128]{1,0:T(8,128)S(1)} collective-permute-done((f32[8,128]{1,0:T(8,128)S(1)}, f32[8,128]{1,0:T(8,128)S(1)}, u32[]{:S(2)}, u32[]{:S(2)}) %collective-permute-start.29) | collective-permute-done | bytes 4128 | tf_op jit(solution)/shard_map/ppermute | solution.py:532
  120.7 2.4 %collective-permute-start.31 = (f32[8,128]{1,0:T(8,128)S(1)}, f32[8,128]{1,0:T(8,128)S(1)}, u32[]{:S(2)}, u32[]{:S(2)}) collective-permute-start(f32[8,128]{1,0:T(8,128)S(1)} %get-tuple-element.253), channel_id=1, source_target_pairs={{16,17},{17,16},{1,2},{2,1},{18,19},{19,18},{3,4},{4,3},{20,21},{2... | collective-permute-start | bytes 12296 | tf_op jit(solution)/shard_map/ppermute | solution.py:532
  124.6 1.9 %collective-permute-done.31.got_b = f32[8,128]{1,0:T(8,128)S(1)} collective-permute-done((f32[8,128]{1,0:T(8,128)S(1)}, f32[8,128]{1,0:T(8,128)S(1)}, u32[]{:S(2)}, u32[]{:S(2)}) %collective-permute-start.31) | collective-permute-done | bytes 4128 | tf_op jit(solution)/shard_map/ppermute | solution.py:532
  127.2 2.4 %collective-permute-start.33 = (f32[8,128]{1,0:T(8,128)S(1)}, f32[8,128]{1,0:T(8,128)S(1)}, u32[]{:S(2)}, u32[]{:S(2)}) collective-permute-start(f32[8,128]{1,0:T(8,128)S(1)} %get-tuple-element.261), channel_id=1, source_target_pairs={{16,17},{17,16},{1,2},{2,1},{18,19},{19,18},{3,4},{4,3},{20,21},{2... | collective-permute-start | bytes 12296 | tf_op jit(solution)/shard_map/ppermute | solution.py:532
  131.1 1.9 %collective-permute-done.33.got_b = f32[8,128]{1,0:T(8,128)S(1)} collective-permute-done((f32[8,128]{1,0:T(8,128)S(1)}, f32[8,128]{1,0:T(8,128)S(1)}, u32[]{:S(2)}, u32[]{:S(2)}) %collective-permute-start.33) | collective-permute-done | bytes 4128 | tf_op jit(solution)/shard_map/ppermute | solution.py:532
  133.8 2.4 %collective-permute-start.35 = (f32[8,128]{1,0:T(8,128)S(1)}, f32[8,128]{1,0:T(8,128)S(1)}, u32[]{:S(2)}, u32[]{:S(2)}) collective-permute-start(f32[8,128]{1,0:T(8,128)S(1)} %get-tuple-element.269), channel_id=1, source_target_pairs={{16,17},{17,16},{1,2},{2,1},{18,19},{19,18},{3,4},{4,3},{20,21},{2... | collective-permute-start | bytes 12296 | tf_op jit(solution)/shard_map/ppermute | solution.py:532
  137.6 1.9 %collective-permute-done.35.got_b = f32[8,128]{1,0:T(8,128)S(1)} collective-permute-done((f32[8,128]{1,0:T(8,128)S(1)}, f32[8,128]{1,0:T(8,128)S(1)}, u32[]{:S(2)}, u32[]{:S(2)}) %collective-permute-start.35) | collective-permute-done | bytes 4128 | tf_op jit(solution)/shard_map/ppermute | solution.py:532
  140.1 3.6 %collective-permute-done.36 = f32[4,2,2,128]{3,2,1,0:T(2,128)S(1)} collective-permute-done((f32[4,2,2,128]{3,2,1,0:T(2,128)S(1)}, f32[4,2,2,128]{3,2,1,0:T(2,128)S(1)}, u32[]{:S(2)}, u32[]{:S(2)}) %collective-permute-start.36) | collective-permute-done | bytes 8224 | tf_op jit(solution)/shard_map/ppermute | solution.py:547
  (82 shorter events, 37.2 us)
Async XLA Ops:
  0.1 6.9 %copy-start = (s32[2]{0:T(128)}, s32[2]{0:T(128)S(1)}, u32[]{:S(2)}) copy-start(s32[2]{0:T(128)S(1)} %pad_add_fusion.place_ref) | copy-start | bytes 28
  2.1 31.0 %collective-permute-start.2 = (f32[12,128,128]{2,1,0:T(8,128)S(1)}, f32[12,128,128]{2,1,0:T(8,128)S(1)}, u32[]{:S(2)}, u32[]{:S(2)}) collective-permute-start(f32[12,128,128]{2,1,0:T(8,128)S(1)} %pack.4), channel_id=1, source_target_pairs={{0,16},{16,0},{1,17},{17,1},{2,18},{18,2},{3,19},{19,3},{4,20},{20... | collective-permute-start | bytes 2359304 | tf_op jit(solution)/shard_map/ppermute | solution.py:477
  6.4 26.7 %collective-permute-start.3 = (f32[8,128,128]{2,1,0:T(8,128)}, f32[8,128,128]{2,1,0:T(8,128)S(1)}, u32[]{:S(2)}, u32[]{:S(2)}) collective-permute-start(f32[8,128,128]{2,1,0:T(8,128)} %pack.5), channel_id=1, source_target_pairs={{0,16},{16,0},{1,17},{17,1},{2,18},{18,2},{3,19},{19,3},{4,20},{20... | collective-permute-start | bytes 1572872 | tf_op jit(solution)/shard_map/ppermute | solution.py:477
  13.4 11.9 %all-to-all-start = ((f32[1,1,16,2176]{3,1,0,2:T(1,128)}), f32[1,1,16,2176]{3,1,0,2:T(1,128)}, u32[]{:S(2)}, u32[]{:S(2)}) async-start(f32[1,1,16,2176]{3,1,0,2:T(1,128)} %fusion), calls=%async_computation | async-start | bytes 278528 | tf_op jit(solution)/shard_map/cond/branch_1_fun/all_to_all | solution.py:485
  19.7 9.0 %collective-permute-start.1 = (f32[2,128,128]{2,1,0:T(8,128)S(1)}, f32[2,128,128]{2,1,0:T(8,128)}, u32[]{:S(2)}, u32[]{:S(2)}) collective-permute-start(f32[2,128,128]{2,1,0:T(8,128)S(1)} %get-tuple-element.25), channel_id=1, source_target_pairs={{16,17},{17,16},{1,2},{2,1},{18,19},{19,18},{3,4},{4,3},{20,21},{2... | collective-permute-start | bytes 393224 | tf_op jit(solution)/shard_map/cond/branch_1_fun/ppermute | solution.py:481
  27.2 5.9 %collective-permute-start = (f32[24,128]{1,0:T(8,128)S(1)}, f32[24,128]{1,0:T(8,128)}, u32[]{:S(2)}, u32[]{:S(2)}) collective-permute-start(f32[24,128]{1,0:T(8,128)S(1)} %get-tuple-element.24), channel_id=1, source_target_pairs={{0,16},{16,0},{1,17},{17,1},{2,18},{18,2},{3,19},{19,3},{4,20},{20... | collective-permute-start | bytes 36872 | tf_op jit(solution)/shard_map/cond/branch_1_fun/ppermute | solution.py:496
  34.0 7.3 %collective-permute-start.5 = (f32[264,128]{1,0:T(8,128)S(1)}, f32[264,128]{1,0:T(8,128)S(1)}, u32[]{:S(2)}, u32[]{:S(2)}) collective-permute-start(f32[264,128]{1,0:T(8,128)S(1)} %get-tuple-element.157), channel_id=1, source_target_pairs={{16,17},{17,16},{1,2},{2,1},{18,19},{19,18},{3,4},{4,3},{20,21},{2... | collective-permute-start | bytes 405512 | tf_op jit(solution)/shard_map/ppermute | solution.py:532
  36.0 3.7 %collective-permute-start.4 = (f32[8,128]{1,0:T(8,128)S(1)}, f32[8,128]{1,0:T(8,128)S(1)}, u32[]{:S(2)}, u32[]{:S(2)}) collective-permute-start(f32[8,128]{1,0:T(8,128)S(1)} %get-tuple-element.156), channel_id=1, source_target_pairs={{0,16},{16,0},{1,17},{17,1},{2,18},{18,2},{3,19},{19,3},{4,20},{20... | collective-permute-start | bytes 12296 | tf_op jit(solution)/shard_map/ppermute | solution.py:533
  42.3 3.7 %collective-permute-start.6 = (f32[8,128]{1,0:T(8,128)S(1)}, f32[8,128]{1,0:T(8,128)S(1)}, u32[]{:S(2)}, u32[]{:S(2)}) collective-permute-start(f32[8,128]{1,0:T(8,128)S(1)} %get-tuple-element.162), channel_id=1, source_target_pairs={{0,16},{16,0},{1,17},{17,1},{2,18},{18,2},{3,19},{19,3},{4,20},{20... | collective-permute-start | bytes 12296 | tf_op jit(solution)/shard_map/ppermute | solution.py:533
  42.4 5.8 %collective-permute-start.7 = (f32[8,128]{1,0:T(8,128)S(1)}, f32[8,128]{1,0:T(8,128)S(1)}, u32[]{:S(2)}, u32[]{:S(2)}) collective-permute-start(f32[8,128]{1,0:T(8,128)S(1)} %get-tuple-element.163), channel_id=1, source_target_pairs={{16,17},{17,16},{1,2},{2,1},{18,19},{19,18},{3,4},{4,3},{20,21},{2... | collective-permute-start | bytes 12296 | tf_op jit(solution)/shard_map/ppermute | solution.py:532
  48.8 3.7 %collective-permute-start.8 = (f32[8,128]{1,0:T(8,128)S(1)}, f32[8,128]{1,0:T(8,128)S(1)}, u32[]{:S(2)}, u32[]{:S(2)}) collective-permute-start(f32[8,128]{1,0:T(8,128)S(1)} %get-tuple-element.170), channel_id=1, source_target_pairs={{0,16},{16,0},{1,17},{17,1},{2,18},{18,2},{3,19},{19,3},{4,20},{20... | collective-permute-start | bytes 12296 | tf_op jit(solution)/shard_map/ppermute | solution.py:533
  48.9 5.8 %collective-permute-start.9 = (f32[8,128]{1,0:T(8,128)S(1)}, f32[8,128]{1,0:T(8,128)S(1)}, u32[]{:S(2)}, u32[]{:S(2)}) collective-permute-start(f32[8,128]{1,0:T(8,128)S(1)} %get-tuple-element.171), channel_id=1, source_target_pairs={{16,17},{17,16},{1,2},{2,1},{18,19},{19,18},{3,4},{4,3},{20,21},{2... | collective-permute-start | bytes 12296 | tf_op jit(solution)/shard_map/ppermute | solution.py:532
  55.3 3.7 %collective-permute-start.10 = (f32[8,128]{1,0:T(8,128)S(1)}, f32[8,128]{1,0:T(8,128)S(1)}, u32[]{:S(2)}, u32[]{:S(2)}) collective-permute-start(f32[8,128]{1,0:T(8,128)S(1)} %get-tuple-element.178), channel_id=1, source_target_pairs={{0,16},{16,0},{1,17},{17,1},{2,18},{18,2},{3,19},{19,3},{4,20},{20... | collective-permute-start | bytes 12296 | tf_op jit(solution)/shard_map/ppermute | solution.py:533
  55.4 5.8 %collective-permute-start.11 = (f32[8,128]{1,0:T(8,128)S(1)}, f32[8,128]{1,0:T(8,128)S(1)}, u32[]{:S(2)}, u32[]{:S(2)}) collective-permute-start(f32[8,128]{1,0:T(8,128)S(1)} %get-tuple-element.179), channel_id=1, source_target_pairs={{16,17},{17,16},{1,2},{2,1},{18,19},{19,18},{3,4},{4,3},{20,21},{2... | collective-permute-start | bytes 12296 | tf_op jit(solution)/shard_map/ppermute | solution.py:532
  61.9 3.7 %collective-permute-start.12 = (f32[8,128]{1,0:T(8,128)S(1)}, f32[8,128]{1,0:T(8,128)S(1)}, u32[]{:S(2)}, u32[]{:S(2)}) collective-permute-start(f32[8,128]{1,0:T(8,128)S(1)} %get-tuple-element.187), channel_id=1, source_target_pairs={{0,16},{16,0},{1,17},{17,1},{2,18},{18,2},{3,19},{19,3},{4,20},{20... | collective-permute-start | bytes 12296 | tf_op jit(solution)/shard_map/ppermute | solution.py:533
  61.9 5.8 %collective-permute-start.13 = (f32[8,128]{1,0:T(8,128)S(1)}, f32[8,128]{1,0:T(8,128)S(1)}, u32[]{:S(2)}, u32[]{:S(2)}) collective-permute-start(f32[8,128]{1,0:T(8,128)S(1)} %get-tuple-element.188), channel_id=1, source_target_pairs={{16,17},{17,16},{1,2},{2,1},{18,19},{19,18},{3,4},{4,3},{20,21},{2... | collective-permute-start | bytes 12296 | tf_op jit(solution)/shard_map/ppermute | solution.py:532
  68.4 3.7 %collective-permute-start.14 = (f32[8,128]{1,0:T(8,128)S(1)}, f32[8,128]{1,0:T(8,128)S(1)}, u32[]{:S(2)}, u32[]{:S(2)}) collective-permute-start(f32[8,128]{1,0:T(8,128)S(1)} %get-tuple-element.192), channel_id=1, source_target_pairs={{0,16},{16,0},{1,17},{17,1},{2,18},{18,2},{3,19},{19,3},{4,20},{20... | collective-permute-start | bytes 12296 | tf_op jit(solution)/shard_map/ppermute | solution.py:533
  68.5 5.8 %collective-permute-start.15 = (f32[8,128]{1,0:T(8,128)S(1)}, f32[8,128]{1,0:T(8,128)S(1)}, u32[]{:S(2)}, u32[]{:S(2)}) collective-permute-start(f32[8,128]{1,0:T(8,128)S(1)} %get-tuple-element.193), channel_id=1, source_target_pairs={{16,17},{17,16},{1,2},{2,1},{18,19},{19,18},{3,4},{4,3},{20,21},{2... | collective-permute-start | bytes 12296 | tf_op jit(solution)/shard_map/ppermute | solution.py:532
  74.9 3.7 %collective-permute-start.16 = (f32[8,128]{1,0:T(8,128)S(1)}, f32[8,128]{1,0:T(8,128)S(1)}, u32[]{:S(2)}, u32[]{:S(2)}) collective-permute-start(f32[8,128]{1,0:T(8,128)S(1)} %get-tuple-element.200), channel_id=1, source_target_pairs={{0,16},{16,0},{1,17},{17,1},{2,18},{18,2},{3,19},{19,3},{4,20},{20... | collective-permute-start | bytes 12296 | tf_op jit(solution)/shard_map/ppermute | solution.py:533
  75.0 5.8 %collective-permute-start.17 = (f32[8,128]{1,0:T(8,128)S(1)}, f32[8,128]{1,0:T(8,128)S(1)}, u32[]{:S(2)}, u32[]{:S(2)}) collective-permute-start(f32[8,128]{1,0:T(8,128)S(1)} %get-tuple-element.201), channel_id=1, source_target_pairs={{16,17},{17,16},{1,2},{2,1},{18,19},{19,18},{3,4},{4,3},{20,21},{2... | collective-permute-start | bytes 12296 | tf_op jit(solution)/shard_map/ppermute | solution.py:532
  81.4 3.7 %collective-permute-start.18 = (f32[8,128]{1,0:T(8,128)S(1)}, f32[8,128]{1,0:T(8,128)S(1)}, u32[]{:S(2)}, u32[]{:S(2)}) collective-permute-start(f32[8,128]{1,0:T(8,128)S(1)} %get-tuple-element.208), channel_id=1, source_target_pairs={{0,16},{16,0},{1,17},{17,1},{2,18},{18,2},{3,19},{19,3},{4,20},{20... | collective-permute-start | bytes 12296 | tf_op jit(solution)/shard_map/ppermute | solution.py:533
  81.5 5.8 %collective-permute-start.19 = (f32[8,128]{1,0:T(8,128)S(1)}, f32[8,128]{1,0:T(8,128)S(1)}, u32[]{:S(2)}, u32[]{:S(2)}) collective-permute-start(f32[8,128]{1,0:T(8,128)S(1)} %get-tuple-element.209), channel_id=1, source_target_pairs={{16,17},{17,16},{1,2},{2,1},{18,19},{19,18},{3,4},{4,3},{20,21},{2... | collective-permute-start | bytes 12296 | tf_op jit(solution)/shard_map/ppermute | solution.py:532
  88.0 3.7 %collective-permute-start.20 = (f32[8,128]{1,0:T(8,128)S(1)}, f32[8,128]{1,0:T(8,128)S(1)}, u32[]{:S(2)}, u32[]{:S(2)}) collective-permute-start(f32[8,128]{1,0:T(8,128)S(1)} %get-tuple-element.217), channel_id=1, source_target_pairs={{0,16},{16,0},{1,17},{17,1},{2,18},{18,2},{3,19},{19,3},{4,20},{20... | collective-permute-start | bytes 12296 | tf_op jit(solution)/shard_map/ppermute | solution.py:533
  88.1 5.8 %collective-permute-start.21 = (f32[8,128]{1,0:T(8,128)S(1)}, f32[8,128]{1,0:T(8,128)S(1)}, u32[]{:S(2)}, u32[]{:S(2)}) collective-permute-start(f32[8,128]{1,0:T(8,128)S(1)} %get-tuple-element.218), channel_id=1, source_target_pairs={{16,17},{17,16},{1,2},{2,1},{18,19},{19,18},{3,4},{4,3},{20,21},{2... | collective-permute-start | bytes 12296 | tf_op jit(solution)/shard_map/ppermute | solution.py:532
  94.5 3.7 %collective-permute-start.22 = (f32[8,128]{1,0:T(8,128)S(1)}, f32[8,128]{1,0:T(8,128)S(1)}, u32[]{:S(2)}, u32[]{:S(2)}) collective-permute-start(f32[8,128]{1,0:T(8,128)S(1)} %get-tuple-element.222), channel_id=1, source_target_pairs={{0,16},{16,0},{1,17},{17,1},{2,18},{18,2},{3,19},{19,3},{4,20},{20... | collective-permute-start | bytes 12296 | tf_op jit(solution)/shard_map/ppermute | solution.py:533
  94.6 5.8 %collective-permute-start.23 = (f32[8,128]{1,0:T(8,128)S(1)}, f32[8,128]{1,0:T(8,128)S(1)}, u32[]{:S(2)}, u32[]{:S(2)}) collective-permute-start(f32[8,128]{1,0:T(8,128)S(1)} %get-tuple-element.223), channel_id=1, source_target_pairs={{16,17},{17,16},{1,2},{2,1},{18,19},{19,18},{3,4},{4,3},{20,21},{2... | collective-permute-start | bytes 12296 | tf_op jit(solution)/shard_map/ppermute | solution.py:532
  101.0 3.7 %collective-permute-start.24 = (f32[8,128]{1,0:T(8,128)S(1)}, f32[8,128]{1,0:T(8,128)S(1)}, u32[]{:S(2)}, u32[]{:S(2)}) collective-permute-start(f32[8,128]{1,0:T(8,128)S(1)} %get-tuple-element.230), channel_id=1, source_target_pairs={{0,16},{16,0},{1,17},{17,1},{2,18},{18,2},{3,19},{19,3},{4,20},{20... | collective-permute-start | bytes 12296 | tf_op jit(solution)/shard_map/ppermute | solution.py:533
  101.1 5.8 %collective-permute-start.25 = (f32[8,128]{1,0:T(8,128)S(1)}, f32[8,128]{1,0:T(8,128)S(1)}, u32[]{:S(2)}, u32[]{:S(2)}) collective-permute-start(f32[8,128]{1,0:T(8,128)S(1)} %get-tuple-element.231), channel_id=1, source_target_pairs={{16,17},{17,16},{1,2},{2,1},{18,19},{19,18},{3,4},{4,3},{20,21},{2... | collective-permute-start | bytes 12296 | tf_op jit(solution)/shard_map/ppermute | solution.py:532
  107.6 3.7 %collective-permute-start.26 = (f32[8,128]{1,0:T(8,128)S(1)}, f32[8,128]{1,0:T(8,128)S(1)}, u32[]{:S(2)}, u32[]{:S(2)}) collective-permute-start(f32[8,128]{1,0:T(8,128)S(1)} %get-tuple-element.238), channel_id=1, source_target_pairs={{0,16},{16,0},{1,17},{17,1},{2,18},{18,2},{3,19},{19,3},{4,20},{20... | collective-permute-start | bytes 12296 | tf_op jit(solution)/shard_map/ppermute | solution.py:533
  107.6 5.8 %collective-permute-start.27 = (f32[8,128]{1,0:T(8,128)S(1)}, f32[8,128]{1,0:T(8,128)S(1)}, u32[]{:S(2)}, u32[]{:S(2)}) collective-permute-start(f32[8,128]{1,0:T(8,128)S(1)} %get-tuple-element.239), channel_id=1, source_target_pairs={{16,17},{17,16},{1,2},{2,1},{18,19},{19,18},{3,4},{4,3},{20,21},{2... | collective-permute-start | bytes 12296 | tf_op jit(solution)/shard_map/ppermute | solution.py:532
  114.1 3.7 %collective-permute-start.28 = (f32[8,128]{1,0:T(8,128)S(1)}, f32[8,128]{1,0:T(8,128)S(1)}, u32[]{:S(2)}, u32[]{:S(2)}) collective-permute-start(f32[8,128]{1,0:T(8,128)S(1)} %get-tuple-element.247), channel_id=1, source_target_pairs={{0,16},{16,0},{1,17},{17,1},{2,18},{18,2},{3,19},{19,3},{4,20},{20... | collective-permute-start | bytes 12296 | tf_op jit(solution)/shard_map/ppermute | solution.py:533
  114.2 5.8 %collective-permute-start.29 = (f32[8,128]{1,0:T(8,128)S(1)}, f32[8,128]{1,0:T(8,128)S(1)}, u32[]{:S(2)}, u32[]{:S(2)}) collective-permute-start(f32[8,128]{1,0:T(8,128)S(1)} %get-tuple-element.248), channel_id=1, source_target_pairs={{16,17},{17,16},{1,2},{2,1},{18,19},{19,18},{3,4},{4,3},{20,21},{2... | collective-permute-start | bytes 12296 | tf_op jit(solution)/shard_map/ppermute | solution.py:532
  120.6 3.7 %collective-permute-start.30 = (f32[8,128]{1,0:T(8,128)S(1)}, f32[8,128]{1,0:T(8,128)S(1)}, u32[]{:S(2)}, u32[]{:S(2)}) collective-permute-start(f32[8,128]{1,0:T(8,128)S(1)} %get-tuple-element.252), channel_id=1, source_target_pairs={{0,16},{16,0},{1,17},{17,1},{2,18},{18,2},{3,19},{19,3},{4,20},{20... | collective-permute-start | bytes 12296 | tf_op jit(solution)/shard_map/ppermute | solution.py:533
  120.7 5.8 %collective-permute-start.31 = (f32[8,128]{1,0:T(8,128)S(1)}, f32[8,128]{1,0:T(8,128)S(1)}, u32[]{:S(2)}, u32[]{:S(2)}) collective-permute-start(f32[8,128]{1,0:T(8,128)S(1)} %get-tuple-element.253), channel_id=1, source_target_pairs={{16,17},{17,16},{1,2},{2,1},{18,19},{19,18},{3,4},{4,3},{20,21},{2... | collective-permute-start | bytes 12296 | tf_op jit(solution)/shard_map/ppermute | solution.py:532
  127.1 3.7 %collective-permute-start.32 = (f32[8,128]{1,0:T(8,128)S(1)}, f32[8,128]{1,0:T(8,128)S(1)}, u32[]{:S(2)}, u32[]{:S(2)}) collective-permute-start(f32[8,128]{1,0:T(8,128)S(1)} %get-tuple-element.260), channel_id=1, source_target_pairs={{0,16},{16,0},{1,17},{17,1},{2,18},{18,2},{3,19},{19,3},{4,20},{20... | collective-permute-start | bytes 12296 | tf_op jit(solution)/shard_map/ppermute | solution.py:533
  127.2 5.8 %collective-permute-start.33 = (f32[8,128]{1,0:T(8,128)S(1)}, f32[8,128]{1,0:T(8,128)S(1)}, u32[]{:S(2)}, u32[]{:S(2)}) collective-permute-start(f32[8,128]{1,0:T(8,128)S(1)} %get-tuple-element.261), channel_id=1, source_target_pairs={{16,17},{17,16},{1,2},{2,1},{18,19},{19,18},{3,4},{4,3},{20,21},{2... | collective-permute-start | bytes 12296 | tf_op jit(solution)/shard_map/ppermute | solution.py:532
  133.7 3.7 %collective-permute-start.34 = (f32[8,128]{1,0:T(8,128)S(1)}, f32[8,128]{1,0:T(8,128)S(1)}, u32[]{:S(2)}, u32[]{:S(2)}) collective-permute-start(f32[8,128]{1,0:T(8,128)S(1)} %get-tuple-element.268), channel_id=1, source_target_pairs={{0,16},{16,0},{1,17},{17,1},{2,18},{18,2},{3,19},{19,3},{4,20},{20... | collective-permute-start | bytes 12296 | tf_op jit(solution)/shard_map/ppermute | solution.py:533
  133.8 5.8 %collective-permute-start.35 = (f32[8,128]{1,0:T(8,128)S(1)}, f32[8,128]{1,0:T(8,128)S(1)}, u32[]{:S(2)}, u32[]{:S(2)}) collective-permute-start(f32[8,128]{1,0:T(8,128)S(1)} %get-tuple-element.269), channel_id=1, source_target_pairs={{16,17},{17,16},{1,2},{2,1},{18,19},{19,18},{3,4},{4,3},{20,21},{2... | collective-permute-start | bytes 12296 | tf_op jit(solution)/shard_map/ppermute | solution.py:532
  140.0 3.7 %collective-permute-start.36 = (f32[4,2,2,128]{3,2,1,0:T(2,128)S(1)}, f32[4,2,2,128]{3,2,1,0:T(2,128)S(1)}, u32[]{:S(2)}, u32[]{:S(2)}) collective-permute-start(f32[4,2,2,128]{3,2,1,0:T(2,128)S(1)} %rev.12), channel_id=1, source_target_pairs={{0,16},{16,0},{1,17},{17,1},{2,18},{18,2},{3,19},{19,3},{4,20},{20... | collective-permute-start | bytes 24584 | tf_op jit(solution)/shard_map/ppermute | solution.py:547

commit v11 on v10

--- a/solution.py
+++ b/solution.py
@@ -193,7 +193,7 @@
 TILES = [(j, b) for j in range(N) for b in range(HALF)]
 ORIGIN = [(0, 0), (0, 1), (1, 1), (1, 0)]
 CAPACITY, INITIAL = STEPS, STEPS + 1
-SPLIT = ((PACKED,), (OUT_IN, PACKED - OUT_IN))
+SPLIT = ((PACKED,), (OUT_IN, FACING - OUT_IN))
 
 
 def unit_device(unit, n_col):
@@ -270,14 +270,13 @@
     return half_block(halves, i, (SIDE_B if b == 0 else SIDE_A) + h * HALF + b)
 
 
-def facing_block(halves, beyond_0, first_b, j, b):
+def facing_block(halves, beyond_0, first_a, first_b, j, b):
     i, h = ORIGIN[j]
-    if b == 1:
-        return half_block(halves, i, FACING + h)
     if i == 0:
-        return lambda g, n: beyond_0[h, g:g + n, :]
-    start = 2 * N + h * first_b.shape[1]
-    return lambda g, n: first_b[start + g:start + g + n, :]
+        return half_block(halves, i, FACING + h) if b == 1 else lambda g, n: beyond_0[h, g:g + n, :]
+    first = first_a if b == 1 else first_b
+    start = 2 * N + h * first.shape[1]
+    return lambda g, n: first[start + g:start + g + n, :]
 
 
 def matvec(terms, chunk=32):
@@ -334,12 +333,24 @@
     f = small_part(small, INITIAL)
     q = inner_product(f, halves)
     q_out[...] = q
-    msg_a[...], to_b = messages(f, ahead(True, 0, f, q, None, None, small_part(small, 0)))
-    msg_b[:2 * N, :] = to_b
+    to_a, to_b = messages(f, ahead(True, 0, f, q, None, None, small_part(small, 0)))
+    msg_a[:2 * N, :], msg_b[:2 * N, :] = to_a, to_b
     width = f.shape[1]
     for h in range(ROWS):
         start = 2 * N + h * width
+        msg_a[start:start + width, :] = keep[SIDE_A + h * HALF + 1]
         msg_b[start:start + width, :] = recv_0[SIDE_B + h * HALF]
+
+
+def by_target_kernel(currents, slot_tile, out):
+    targets, slots, frames = currents.shape
+    width = out.shape[2] - slots * frames
+    names = slot_tile[...].astype(jnp.float32)
+    names = jnp.concatenate([names, jnp.zeros((targets, width - slots), jnp.float32)], axis=1)
+    for d in range(targets):
+        for k in range(slots):
+            out[d, :, k * frames:(k + 1) * frames] = currents[d, k:k + 1, :]
+        out[d, :, slots * frames:] = names[d:d + 1, :]
 
 
 def small_kernel(place_ref, arrived, capacity, initial, keep, send, injected):
@@ -367,14 +378,14 @@
                     out[i:i + 1, :] = part
 
 
-def beside_kernel(begin, keep, recv_0, recv_1, beyond_0, first_b, got_a, q_ref, *refs):
+def beside_kernel(begin, keep, recv_0, recv_1, beyond_0, first_a, first_b, got_a, q_ref, *refs):
     halves = ((keep,), (recv_0, recv_1))
     response_out, q_out = refs[-2:]
     f = small_part(refs[0], INITIAL) if begin else refs[0][...]
     q = q_ref[...]
     response, total = [], []
     for j, b in TILES:
-        response.append(matvec([(facing_block(halves, beyond_0, first_b, j, b), row_of(f, j, b))]))
+        response.append(matvec([(facing_block(halves, beyond_0, first_a, first_b, j, b), row_of(f, j, b))]))
         mine = row_of(q, j, b)
         if b == 1:
             mine = mine + matvec([(halo_block(halves, j, b), got_a[j:j + 1, :])])
@@ -480,9 +491,15 @@
     def beside(currents, slot_tile, capacity, initial, facing_0):
         beyond_0 = lax.ppermute(facing_0, both, b_pairs)
         slots, frames = currents.shape[3:]
-        names = jnp.pad(slot_tile.astype(jnp.float32), ((0, 0), (0, 0), (0, 0), (0, width - slots)))
-        packed = jnp.concatenate([currents.reshape(*currents.shape[:3], slots * frames), names], axis=3)
-        arrived = lax.all_to_all(packed, "col", split_axis=2, concat_axis=1, tiled=True)
+        by_target = pl.pallas_call(
+            by_target_kernel,
+            out_shape=jax.ShapeDtypeStruct((n_col, 1, slots * frames + width), jnp.float32),
+            in_specs=[vmem, vmem],
+            out_specs=vmem,
+            compiler_params=limit,
+            name="by_target",
+        )(currents.reshape(n_col, slots, frames), slot_tile.reshape(n_col, slots))
+        arrived = lax.all_to_all(by_target, "col", split_axis=0, concat_axis=0, tiled=True)
         half = jax.ShapeDtypeStruct(((STEPS + 2) * ROWS * HALF, width), jnp.float32)
         small, send = pl.pallas_call(
             small_kernel,
@@ -521,8 +538,8 @@
 
     first_shape = jax.ShapeDtypeStruct((2 * N + ROWS * width, width), jnp.float32)
     unit_small = jax.ShapeDtypeStruct(((STEPS + 2) * N * HALF, width), jnp.float32)
-    msg_a, msg_b, q, small = call(start_kernel, (shape, first_shape, shape, unit_small), 28, *halves, *small)
-    field, first_b = (), None
+    msg_a, msg_b, q, small = call(start_kernel, (first_shape, first_shape, shape, unit_small), 28, *halves, *small)
+    field, first_a, first_b = (), None, None
     frames = []
     state = ()
     for instant in range(STEPS):
@@ -532,8 +549,8 @@
             got_b = lax.ppermute(msg_b, both, b_pairs)
             got_a = lax.ppermute(msg_a, "row", swap)
             if first_b is None:
-                first_b = got_b
-            response, q = call(functools.partial(beside_kernel, not field), (shape,) * 2, 12, *halves, beyond_0, first_b,
+                first_a, first_b = got_a, got_b
+            response, q = call(functools.partial(beside_kernel, not field), (shape,) * 2, 12, *halves, beyond_0, first_a, first_b,
                                got_a, q, *(field or (small,)))
             out = call(functools.partial(pair_kernel, instant, pair, last), (shape,) * (1 if last else 4 if closing else 6),
                        68, *halves, small, got_a, got_b, response, q, *field, *state)

time: 145 us -> 144 us (level)
  local copies, waits for them, and re-layouts: 4.36 us -> 1.62 us
  waiting for transfers between devices: 60.1 us -> 62.2 us
  other arithmetic: 2.4 us -> 0.72 us
    ppermute x16, waiting for transfers between devices: 30.8 us -> 32.9 us  [shards_chain(): got_b = lax.ppermute(msg_b, both, b_pairs)]
    concatenate x1 -> x0, other arithmetic: 1.67 us -> none  [beside(): jnp.concatenate([currents.reshape(*currents.shape[:3], slots * frames), n...]
    reshape x1, local copies, waits for them, and re-layouts: 1.73 us -> 0.08 us  [beside(): slot_tile.reshape(n_col, slots)]
  transfers between devices with their start and end apart: 38 -> 38, of which waited for: 35 -> 35; matrix products, arithmetic and copies ran while one was open for 4% -> 1% of each run, Pallas kernels for 7% -> 8%
where the time goes in v11:
time: 144 us; the launch traced here: 143 us
  waiting for transfers between devices  62.2 us (43%)
  starting transfers between devices  53.8 us (37%)
  Pallas kernels  24.3 us (17%)
  local copies, waits for them, and re-layouts  1.62 us (1%)
    ppermute x16, starting transfers between devices, shards_chain(): got_b = lax.ppermute(msg_b, both, b_pairs)  38 us
    ppermute x16, waiting for transfers between devices, shards_chain(): got_b = lax.ppermute(msg_b, both, b_pairs)  32.9 us
    ppermute x16, waiting for transfers between devices, shards_chain(): got_a = lax.ppermute(msg_a, 'row', swap)  19.3 us
    pallas_call x33, Pallas kernels, call(): pl.pallas_call(body, out_shape=outs, in_specs=[vmem] * len(ins), out_spec...  15.2 us
    pallas_call x3, Pallas kernels, pack(): pl.pallas_call(functools.partial(pack_kernel, n_col, sent, first, count),...  6.85 us
    all_to_all x1, starting transfers between devices, beside(): lax.all_to_all(by_target, 'col', split_axis=0, concat_axis=0, tiled=True)  6.27 us
    ppermute x1, waiting for transfers between devices, beside(): return (small, lax.ppermute(send, 'row', swap), beyond_0)  4.02 us
    ppermute x1, waiting for transfers between devices, shards_chain(): got = lax.ppermute(jnp.flip(done[:, ROWS:], 1), 'row', swap)  3.63 us
  transfers between devices with their start and end apart: 38, of which 35 were waited for; matrix products, arithmetic and copies ran while one was open for 1% of the time, Pallas kernels for 8%

profile of v11, /device:TPU:8, one launch (start us, length us, event | category | flops | bytes accessed | tf_op | source)
XLA Modules:
  0.0 143.2 jit_solution(9068063152745112883)
XLA Ops:
  0.1 2.0 %pack.4 = f32[12,128,128]{2,1,0:T(8,128)S(1)} custom-call(s32[2]{0:T(128)S(1)} %pad_add_fusion.place_ref, s32[2,4,4]{2,1,0:T(4,128)} %pattern_ref.5, f32[2,4,128,128]{3,2,1,0:T(8,128)} %own_hbm.5, f32[4,2,4,128,128]{4,3,2,1,0:T(8,128)} %nb_hbm.5), custom_call_target="tpu_custom_call" | custom-call | tf_op jit(solution)/shard_map/pack/pallas_call | solution.py:475
  2.1 1.6 %collective-permute-start.2 = (f32[12,128,128]{2,1,0:T(8,128)S(1)}, f32[12,128,128]{2,1,0:T(8,128)S(1)}, u32[]{:S(2)}, u32[]{:S(2)}) collective-permute-start(f32[12,128,128]{2,1,0:T(8,128)S(1)} %pack.4), channel_id=1, source_target_pairs={{0,16},{16,0},{1,17},{17,1},{2,18},{18,2},{3,19},{19,3},{4,20},{20... | collective-permute-start | bytes 2359304 | tf_op jit(solution)/shard_map/ppermute | solution.py:488
  3.7 2.6 %pack.5 = f32[6,128,128]{2,1,0:T(8,128)} custom-call(s32[2]{0:T(128)S(1)} %pad_add_fusion.place_ref, s32[2,4,4]{2,1,0:T(4,128)} %pattern_ref.5, f32[2,4,128,128]{3,2,1,0:T(8,128)} %own_hbm.5, f32[4,2,4,128,128]{4,3,2,1,0:T(8,128)} %nb_hbm.5), custom_call_target="tpu_custom_call" | custom-call | tf_op jit(solution)/shard_map/pack/pallas_call | solution.py:475
  6.9 2.3 %pack.3 = (f32[20,128,128]{2,1,0:T(8,128)S(1)}, f32[2,128,128]{2,1,0:T(8,128)S(1)}) custom-call(s32[2]{0:T(128)S(1)} %pad_add_fusion.place_ref, s32[2,4,4]{2,1,0:T(4,128)} %pattern_ref.5, f32[2,4,128,128]{3,2,1,0:T(8,128)} %own_hbm.5, f32[4,2,4,128,128]{4,3,2,1,0:T(8,128)} %nb_hbm.5), custom_call_target="tpu_custom_call" | custom-call | tf_op jit(solution)/shard_map/pack/pallas_call | solution.py:475
  9.2 21.1 %conditional.1 = (f32[24,128]{1,0:T(8,128)}, f32[24,128]{1,0:T(8,128)}, f32[2,128,128]{2,1,0:T(8,128)S(1)}) conditional(s32[]{:T(128)} %convert_element_type.3, f32[2,128,128]{2,1,0:T(8,128)S(1)} %get-tuple-element.152, (f32[1,1,16,4,512]{4,3,2,1,0:T(4,128)S(1)}, s32[1,1,16,4]{2,3,1,0:T(4,128)S(1)}, s32[2]{0:T(128)S(1)}, f32[2,4,128]{2,1,0:T(4,128)}, ...), branch_computations={%region_0.1_spmd, %region_1.2_spmd} | conditional | bytes 1532612 | solution.py:515
  10.5 6.3 %all-to-all-start = ((f32[16,1,2176]{2,1,0:T(1,128)}), f32[16,1,2176]{2,1,0:T(1,128)S(1)}, u32[]{:S(2)}, u32[]{:S(2)}) async-start(f32[16,1,2176]{2,1,0:T(1,128)} %by_target.1), calls=%async_computation | async-start | bytes 278528 | tf_op jit(solution)/shard_map/cond/branch_1_fun/all_to_all | solution.py:502
  16.8 3.1 %collective-permute-start.1 = (f32[2,128,128]{2,1,0:T(8,128)S(1)}, f32[2,128,128]{2,1,0:T(8,128)}, u32[]{:S(2)}, u32[]{:S(2)}) collective-permute-start(f32[2,128,128]{2,1,0:T(8,128)S(1)} %get-tuple-element.25), channel_id=1, source_target_pairs={{16,17},{17,16},{1,2},{2,1},{18,19},{19,18},{3,4},{4,3},{20,21},{2... | collective-permute-start | bytes 393224 | tf_op jit(solution)/shard_map/cond/branch_1_fun/ppermute | solution.py:492
  19.9 2.4 %all-to-all-done = f32[16,1,2176]{2,1,0:T(1,128)S(1)} async-done(((f32[16,1,2176]{2,1,0:T(1,128)}), f32[16,1,2176]{2,1,0:T(1,128)S(1)}, u32[]{:S(2)}, u32[]{:S(2)}) %all-to-all-start) | async-done | bytes 139296 | tf_op jit(solution)/shard_map/cond/branch_1_fun/all_to_all | solution.py:502
  22.3 1.5 %small.1 = (f32[24,128]{1,0:T(8,128)}, f32[24,128]{1,0:T(8,128)S(1)}) custom-call(s32[2]{0:T(128)} %copy-done.1, f32[16,2176]{1,0:T(8,128)S(1)} %bitcast.11, f32[2,4,128]{2,1,0:T(4,128)} %get-tuple-element.282.capacity, f32[2,4,128]{2,1,0:T(4,128)} %get-tuple-element.283.initial), custom_call_target="tpu_custom_call" | custom-call | tf_op jit(solution)/shard_map/cond/branch_1_fun/small/pallas_call | solution.py:504
  23.8 1.5 %collective-permute-start = (f32[24,128]{1,0:T(8,128)S(1)}, f32[24,128]{1,0:T(8,128)}, u32[]{:S(2)}, u32[]{:S(2)}) collective-permute-start(f32[24,128]{1,0:T(8,128)S(1)} %get-tuple-element.24), channel_id=1, source_target_pairs={{0,16},{16,0},{1,17},{17,1},{2,18},{18,2},{3,19},{19,3},{4,20},{20... | collective-permute-start | bytes 36872 | tf_op jit(solution)/shard_map/cond/branch_1_fun/ppermute | solution.py:513
  26.3 4.0 %collective-permute-done = f32[24,128]{1,0:T(8,128)} collective-permute-done((f32[24,128]{1,0:T(8,128)S(1)}, f32[24,128]{1,0:T(8,128)}, u32[]{:S(2)}, u32[]{:S(2)}) %collective-permute-start) | collective-permute-done | bytes 12320 | tf_op jit(solution)/shard_map/cond/branch_1_fun/ppermute | solution.py:513
  31.3 1.6 %collective-permute-start.4 = (f32[264,128]{1,0:T(8,128)S(1)}, f32[264,128]{1,0:T(8,128)S(1)}, u32[]{:S(2)}, u32[]{:S(2)}) collective-permute-start(f32[264,128]{1,0:T(8,128)S(1)} %get-tuple-element.156), channel_id=1, source_target_pairs={{0,16},{16,0},{1,17},{17,1},{2,18},{18,2},{3,19},{19,3},{4,20},{20... | collective-permute-start | bytes 405512 | tf_op jit(solution)/shard_map/ppermute | solution.py:550
  32.8 1.9 %collective-permute-start.5 = (f32[264,128]{1,0:T(8,128)S(1)}, f32[264,128]{1,0:T(8,128)S(1)}, u32[]{:S(2)}, u32[]{:S(2)}) collective-permute-start(f32[264,128]{1,0:T(8,128)S(1)} %get-tuple-element.157), channel_id=1, source_target_pairs={{16,17},{17,16},{1,2},{2,1},{18,19},{19,18},{3,4},{4,3},{20,21},{2... | collective-permute-start | bytes 405512 | tf_op jit(solution)/shard_map/ppermute | solution.py:549
  34.8 1.6 %collective-permute-done.4.first_a.got_a = f32[264,128]{1,0:T(8,128)S(1)} collective-permute-done((f32[264,128]{1,0:T(8,128)S(1)}, f32[264,128]{1,0:T(8,128)S(1)}, u32[]{:S(2)}, u32[]{:S(2)}) %collective-permute-start.4) | collective-permute-done | bytes 135200 | tf_op jit(solution)/shard_map/ppermute | solution.py:550
  36.3 3.8 %collective-permute-done.5.first_b.got_b = f32[264,128]{1,0:T(8,128)S(1)} collective-permute-done((f32[264,128]{1,0:T(8,128)S(1)}, f32[264,128]{1,0:T(8,128)S(1)}, u32[]{:S(2)}, u32[]{:S(2)}) %collective-permute-start.5) | collective-permute-done | bytes 135200 | tf_op jit(solution)/shard_map/ppermute | solution.py:549
  41.2 1.9 %collective-permute-start.7 = (f32[8,128]{1,0:T(8,128)S(1)}, f32[8,128]{1,0:T(8,128)S(1)}, u32[]{:S(2)}, u32[]{:S(2)}) collective-permute-start(f32[8,128]{1,0:T(8,128)S(1)} %get-tuple-element.163), channel_id=1, source_target_pairs={{16,17},{17,16},{1,2},{2,1},{18,19},{19,18},{3,4},{4,3},{20,21},{2... | collective-permute-start | bytes 12296 | tf_op jit(solution)/shard_map/ppermute | solution.py:549
  43.1 1.7 %collective-permute-done.6.got_a = f32[8,128]{1,0:T(8,128)S(1)} collective-permute-done((f32[8,128]{1,0:T(8,128)S(1)}, f32[8,128]{1,0:T(8,128)S(1)}, u32[]{:S(2)}, u32[]{:S(2)}) %collective-permute-start.6) | collective-permute-done | bytes 4128 | tf_op jit(solution)/shard_map/ppermute | solution.py:550
  45.1 1.9 %collective-permute-done.7.got_b = f32[8,128]{1,0:T(8,128)S(1)} collective-permute-done((f32[8,128]{1,0:T(8,128)S(1)}, f32[8,128]{1,0:T(8,128)S(1)}, u32[]{:S(2)}, u32[]{:S(2)}) %collective-permute-start.7) | collective-permute-done | bytes 4128 | tf_op jit(solution)/shard_map/ppermute | solution.py:549
  47.7 2.4 %collective-permute-start.9 = (f32[8,128]{1,0:T(8,128)S(1)}, f32[8,128]{1,0:T(8,128)S(1)}, u32[]{:S(2)}, u32[]{:S(2)}) collective-permute-start(f32[8,128]{1,0:T(8,128)S(1)} %get-tuple-element.171), channel_id=1, source_target_pairs={{16,17},{17,16},{1,2},{2,1},{18,19},{19,18},{3,4},{4,3},{20,21},{2... | collective-permute-start | bytes 12296 | tf_op jit(solution)/shard_map/ppermute | solution.py:549
  51.6 1.9 %collective-permute-done.9.got_b = f32[8,128]{1,0:T(8,128)S(1)} collective-permute-done((f32[8,128]{1,0:T(8,128)S(1)}, f32[8,128]{1,0:T(8,128)S(1)}, u32[]{:S(2)}, u32[]{:S(2)}) %collective-permute-start.9) | collective-permute-done | bytes 4128 | tf_op jit(solution)/shard_map/ppermute | solution.py:549
  54.2 2.4 %collective-permute-start.11 = (f32[8,128]{1,0:T(8,128)S(1)}, f32[8,128]{1,0:T(8,128)S(1)}, u32[]{:S(2)}, u32[]{:S(2)}) collective-permute-start(f32[8,128]{1,0:T(8,128)S(1)} %get-tuple-element.179), channel_id=1, source_target_pairs={{16,17},{17,16},{1,2},{2,1},{18,19},{19,18},{3,4},{4,3},{20,21},{2... | collective-permute-start | bytes 12296 | tf_op jit(solution)/shard_map/ppermute | solution.py:549
  58.1 1.9 %collective-permute-done.11.got_b = f32[8,128]{1,0:T(8,128)S(1)} collective-permute-done((f32[8,128]{1,0:T(8,128)S(1)}, f32[8,128]{1,0:T(8,128)S(1)}, u32[]{:S(2)}, u32[]{:S(2)}) %collective-permute-start.11) | collective-permute-done | bytes 4128 | tf_op jit(solution)/shard_map/ppermute | solution.py:549
  60.8 2.4 %collective-permute-start.13 = (f32[8,128]{1,0:T(8,128)S(1)}, f32[8,128]{1,0:T(8,128)S(1)}, u32[]{:S(2)}, u32[]{:S(2)}) collective-permute-start(f32[8,128]{1,0:T(8,128)S(1)} %get-tuple-element.188), channel_id=1, source_target_pairs={{16,17},{17,16},{1,2},{2,1},{18,19},{19,18},{3,4},{4,3},{20,21},{2... | collective-permute-start | bytes 12296 | tf_op jit(solution)/shard_map/ppermute | solution.py:549
  64.6 1.9 %collective-permute-done.13.got_b = f32[8,128]{1,0:T(8,128)S(1)} collective-permute-done((f32[8,128]{1,0:T(8,128)S(1)}, f32[8,128]{1,0:T(8,128)S(1)}, u32[]{:S(2)}, u32[]{:S(2)}) %collective-permute-start.13) | collective-permute-done | bytes 4128 | tf_op jit(solution)/shard_map/ppermute | solution.py:549
  67.3 2.4 %collective-permute-start.15 = (f32[8,128]{1,0:T(8,128)S(1)}, f32[8,128]{1,0:T(8,128)S(1)}, u32[]{:S(2)}, u32[]{:S(2)}) collective-permute-start(f32[8,128]{1,0:T(8,128)S(1)} %get-tuple-element.193), channel_id=1, source_target_pairs={{16,17},{17,16},{1,2},{2,1},{18,19},{19,18},{3,4},{4,3},{20,21},{2... | collective-permute-start | bytes 12296 | tf_op jit(solution)/shard_map/ppermute | solution.py:549
  69.7 1.2 collective-permute-done.14.got_a
  71.2 1.9 %collective-permute-done.15.got_b = f32[8,128]{1,0:T(8,128)S(1)} collective-permute-done((f32[8,128]{1,0:T(8,128)S(1)}, f32[8,128]{1,0:T(8,128)S(1)}, u32[]{:S(2)}, u32[]{:S(2)}) %collective-permute-start.15) | collective-permute-done | bytes 4128 | tf_op jit(solution)/shard_map/ppermute | solution.py:549
  73.8 2.4 %collective-permute-start.17 = (f32[8,128]{1,0:T(8,128)S(1)}, f32[8,128]{1,0:T(8,128)S(1)}, u32[]{:S(2)}, u32[]{:S(2)}) collective-permute-start(f32[8,128]{1,0:T(8,128)S(1)} %get-tuple-element.201), channel_id=1, source_target_pairs={{16,17},{17,16},{1,2},{2,1},{18,19},{19,18},{3,4},{4,3},{20,21},{2... | collective-permute-start | bytes 12296 | tf_op jit(solution)/shard_map/ppermute | solution.py:549
  77.7 1.9 %collective-permute-done.17.got_b = f32[8,128]{1,0:T(8,128)S(1)} collective-permute-done((f32[8,128]{1,0:T(8,128)S(1)}, f32[8,128]{1,0:T(8,128)S(1)}, u32[]{:S(2)}, u32[]{:S(2)}) %collective-permute-start.17) | collective-permute-done | bytes 4128 | tf_op jit(solution)/shard_map/ppermute | solution.py:549
  80.3 2.4 %collective-permute-start.19 = (f32[8,128]{1,0:T(8,128)S(1)}, f32[8,128]{1,0:T(8,128)S(1)}, u32[]{:S(2)}, u32[]{:S(2)}) collective-permute-start(f32[8,128]{1,0:T(8,128)S(1)} %get-tuple-element.209), channel_id=1, source_target_pairs={{16,17},{17,16},{1,2},{2,1},{18,19},{19,18},{3,4},{4,3},{20,21},{2... | collective-permute-start | bytes 12296 | tf_op jit(solution)/shard_map/ppermute | solution.py:549
  84.2 1.9 %collective-permute-done.19.got_b = f32[8,128]{1,0:T(8,128)S(1)} collective-permute-done((f32[8,128]{1,0:T(8,128)S(1)}, f32[8,128]{1,0:T(8,128)S(1)}, u32[]{:S(2)}, u32[]{:S(2)}) %collective-permute-start.19) | collective-permute-done | bytes 4128 | tf_op jit(solution)/shard_map/ppermute | solution.py:549
  86.9 2.4 %collective-permute-start.21 = (f32[8,128]{1,0:T(8,128)S(1)}, f32[8,128]{1,0:T(8,128)S(1)}, u32[]{:S(2)}, u32[]{:S(2)}) collective-permute-start(f32[8,128]{1,0:T(8,128)S(1)} %get-tuple-element.218), channel_id=1, source_target_pairs={{16,17},{17,16},{1,2},{2,1},{18,19},{19,18},{3,4},{4,3},{20,21},{2... | collective-permute-start | bytes 12296 | tf_op jit(solution)/shard_map/ppermute | solution.py:549
  90.8 1.9 %collective-permute-done.21.got_b = f32[8,128]{1,0:T(8,128)S(1)} collective-permute-done((f32[8,128]{1,0:T(8,128)S(1)}, f32[8,128]{1,0:T(8,128)S(1)}, u32[]{:S(2)}, u32[]{:S(2)}) %collective-permute-start.21) | collective-permute-done | bytes 4128 | tf_op jit(solution)/shard_map/ppermute | solution.py:549
  93.4 2.4 %collective-permute-start.23 = (f32[8,128]{1,0:T(8,128)S(1)}, f32[8,128]{1,0:T(8,128)S(1)}, u32[]{:S(2)}, u32[]{:S(2)}) collective-permute-start(f32[8,128]{1,0:T(8,128)S(1)} %get-tuple-element.223), channel_id=1, source_target_pairs={{16,17},{17,16},{1,2},{2,1},{18,19},{19,18},{3,4},{4,3},{20,21},{2... | collective-permute-start | bytes 12296 | tf_op jit(solution)/shard_map/ppermute | solution.py:549
  97.3 1.9 %collective-permute-done.23.got_b = f32[8,128]{1,0:T(8,128)S(1)} collective-permute-done((f32[8,128]{1,0:T(8,128)S(1)}, f32[8,128]{1,0:T(8,128)S(1)}, u32[]{:S(2)}, u32[]{:S(2)}) %collective-permute-start.23) | collective-permute-done | bytes 4128 | tf_op jit(solution)/shard_map/ppermute | solution.py:549
  99.9 2.6 %collective-permute-start.25 = (f32[8,128]{1,0:T(8,128)S(1)}, f32[8,128]{1,0:T(8,128)S(1)}, u32[]{:S(2)}, u32[]{:S(2)}) collective-permute-start(f32[8,128]{1,0:T(8,128)S(1)} %get-tuple-element.231), channel_id=1, source_target_pairs={{16,17},{17,16},{1,2},{2,1},{18,19},{19,18},{3,4},{4,3},{20,21},{2... | collective-permute-start | bytes 12296 | tf_op jit(solution)/shard_map/ppermute | solution.py:549
  103.8 1.9 %collective-permute-done.25.got_b = f32[8,128]{1,0:T(8,128)S(1)} collective-permute-done((f32[8,128]{1,0:T(8,128)S(1)}, f32[8,128]{1,0:T(8,128)S(1)}, u32[]{:S(2)}, u32[]{:S(2)}) %collective-permute-start.25) | collective-permute-done | bytes 4128 | tf_op jit(solution)/shard_map/ppermute | solution.py:549
  106.4 2.4 %collective-permute-start.27 = (f32[8,128]{1,0:T(8,128)S(1)}, f32[8,128]{1,0:T(8,128)S(1)}, u32[]{:S(2)}, u32[]{:S(2)}) collective-permute-start(f32[8,128]{1,0:T(8,128)S(1)} %get-tuple-element.239), channel_id=1, source_target_pairs={{16,17},{17,16},{1,2},{2,1},{18,19},{19,18},{3,4},{4,3},{20,21},{2... | collective-permute-start | bytes 12296 | tf_op jit(solution)/shard_map/ppermute | solution.py:549
  110.3 1.9 %collective-permute-done.27.got_b = f32[8,128]{1,0:T(8,128)S(1)} collective-permute-done((f32[8,128]{1,0:T(8,128)S(1)}, f32[8,128]{1,0:T(8,128)S(1)}, u32[]{:S(2)}, u32[]{:S(2)}) %collective-permute-start.27) | collective-permute-done | bytes 4128 | tf_op jit(solution)/shard_map/ppermute | solution.py:549
  113.0 2.4 %collective-permute-start.29 = (f32[8,128]{1,0:T(8,128)S(1)}, f32[8,128]{1,0:T(8,128)S(1)}, u32[]{:S(2)}, u32[]{:S(2)}) collective-permute-start(f32[8,128]{1,0:T(8,128)S(1)} %get-tuple-element.248), channel_id=1, source_target_pairs={{16,17},{17,16},{1,2},{2,1},{18,19},{19,18},{3,4},{4,3},{20,21},{2... | collective-permute-start | bytes 12296 | tf_op jit(solution)/shard_map/ppermute | solution.py:549
  116.9 1.9 %collective-permute-done.29.got_b = f32[8,128]{1,0:T(8,128)S(1)} collective-permute-done((f32[8,128]{1,0:T(8,128)S(1)}, f32[8,128]{1,0:T(8,128)S(1)}, u32[]{:S(2)}, u32[]{:S(2)}) %collective-permute-start.29) | collective-permute-done | bytes 4128 | tf_op jit(solution)/shard_map/ppermute | solution.py:549
  119.5 2.4 %collective-permute-start.31 = (f32[8,128]{1,0:T(8,128)S(1)}, f32[8,128]{1,0:T(8,128)S(1)}, u32[]{:S(2)}, u32[]{:S(2)}) collective-permute-start(f32[8,128]{1,0:T(8,128)S(1)} %get-tuple-element.253), channel_id=1, source_target_pairs={{16,17},{17,16},{1,2},{2,1},{18,19},{19,18},{3,4},{4,3},{20,21},{2... | collective-permute-start | bytes 12296 | tf_op jit(solution)/shard_map/ppermute | solution.py:549
  123.4 1.9 %collective-permute-done.31.got_b = f32[8,128]{1,0:T(8,128)S(1)} collective-permute-done((f32[8,128]{1,0:T(8,128)S(1)}, f32[8,128]{1,0:T(8,128)S(1)}, u32[]{:S(2)}, u32[]{:S(2)}) %collective-permute-start.31) | collective-permute-done | bytes 4128 | tf_op jit(solution)/shard_map/ppermute | solution.py:549
  126.0 2.4 %collective-permute-start.33 = (f32[8,128]{1,0:T(8,128)S(1)}, f32[8,128]{1,0:T(8,128)S(1)}, u32[]{:S(2)}, u32[]{:S(2)}) collective-permute-start(f32[8,128]{1,0:T(8,128)S(1)} %get-tuple-element.261), channel_id=1, source_target_pairs={{16,17},{17,16},{1,2},{2,1},{18,19},{19,18},{3,4},{4,3},{20,21},{2... | collective-permute-start | bytes 12296 | tf_op jit(solution)/shard_map/ppermute | solution.py:549
  129.9 1.9 %collective-permute-done.33.got_b = f32[8,128]{1,0:T(8,128)S(1)} collective-permute-done((f32[8,128]{1,0:T(8,128)S(1)}, f32[8,128]{1,0:T(8,128)S(1)}, u32[]{:S(2)}, u32[]{:S(2)}) %collective-permute-start.33) | collective-permute-done | bytes 4128 | tf_op jit(solution)/shard_map/ppermute | solution.py:549
  132.6 2.4 %collective-permute-start.35 = (f32[8,128]{1,0:T(8,128)S(1)}, f32[8,128]{1,0:T(8,128)S(1)}, u32[]{:S(2)}, u32[]{:S(2)}) collective-permute-start(f32[8,128]{1,0:T(8,128)S(1)} %get-tuple-element.269), channel_id=1, source_target_pairs={{16,17},{17,16},{1,2},{2,1},{18,19},{19,18},{3,4},{4,3},{20,21},{2... | collective-permute-start | bytes 12296 | tf_op jit(solution)/shard_map/ppermute | solution.py:549
  136.4 1.9 %collective-permute-done.35.got_b = f32[8,128]{1,0:T(8,128)S(1)} collective-permute-done((f32[8,128]{1,0:T(8,128)S(1)}, f32[8,128]{1,0:T(8,128)S(1)}, u32[]{:S(2)}, u32[]{:S(2)}) %collective-permute-start.35) | collective-permute-done | bytes 4128 | tf_op jit(solution)/shard_map/ppermute | solution.py:549
  138.9 3.6 %collective-permute-done.36 = f32[4,2,2,128]{3,2,1,0:T(2,128)S(1)} collective-permute-done((f32[4,2,2,128]{3,2,1,0:T(2,128)S(1)}, f32[4,2,2,128]{3,2,1,0:T(2,128)S(1)}, u32[]{:S(2)}, u32[]{:S(2)}) %collective-permute-start.36) | collective-permute-done | bytes 8224 | tf_op jit(solution)/shard_map/ppermute | solution.py:564
  (84 shorter events, 34.8 us)
Async XLA Ops:
  2.1 7.0 %copy-start = (f32[1,1,16,4,512]{4,3,2,1,0:T(4,128)S(1)}, f32[1,1,16,4,512]{4,3,2,1,0:T(4,128)}, u32[]{:S(2)}) copy-start(f32[1,1,16,4,512]{4,3,2,1,0:T(4,128)} %param.14) | copy-start | bytes 393220
  2.1 7.0 %copy-start.2 = (s32[1,1,16,4]{2,3,1,0:T(4,128)S(1)}, s32[1,1,16,4]{2,3,1,0:T(4,128)}, u32[]{:S(2)}) copy-start(s32[1,1,16,4]{2,3,1,0:T(4,128)} %param.15) | copy-start | bytes 772
  2.1 28.1 %collective-permute-start.2 = (f32[12,128,128]{2,1,0:T(8,128)S(1)}, f32[12,128,128]{2,1,0:T(8,128)S(1)}, u32[]{:S(2)}, u32[]{:S(2)}) collective-permute-start(f32[12,128,128]{2,1,0:T(8,128)S(1)} %pack.4), channel_id=1, source_target_pairs={{0,16},{16,0},{1,17},{17,1},{2,18},{18,2},{3,19},{19,3},{4,20},{20... | collective-permute-start | bytes 2359304 | tf_op jit(solution)/shard_map/ppermute | solution.py:488
  6.3 24.0 %collective-permute-start.3 = (f32[6,128,128]{2,1,0:T(8,128)}, f32[6,128,128]{2,1,0:T(8,128)S(1)}, u32[]{:S(2)}, u32[]{:S(2)}) collective-permute-start(f32[6,128,128]{2,1,0:T(8,128)} %pack.5), channel_id=1, source_target_pairs={{0,16},{16,0},{1,17},{17,1},{2,18},{18,2},{3,19},{19,3},{4,20},{20... | collective-permute-start | bytes 1179656 | tf_op jit(solution)/shard_map/ppermute | solution.py:488
  9.2 0.6 copy-start.1
  10.5 11.8 %all-to-all-start = ((f32[16,1,2176]{2,1,0:T(1,128)}), f32[16,1,2176]{2,1,0:T(1,128)S(1)}, u32[]{:S(2)}, u32[]{:S(2)}) async-start(f32[16,1,2176]{2,1,0:T(1,128)} %by_target.1), calls=%async_computation | async-start | bytes 278528 | tf_op jit(solution)/shard_map/cond/branch_1_fun/all_to_all | solution.py:502
  16.8 8.6 %collective-permute-start.1 = (f32[2,128,128]{2,1,0:T(8,128)S(1)}, f32[2,128,128]{2,1,0:T(8,128)}, u32[]{:S(2)}, u32[]{:S(2)}) collective-permute-start(f32[2,128,128]{2,1,0:T(8,128)S(1)} %get-tuple-element.25), channel_id=1, source_target_pairs={{16,17},{17,16},{1,2},{2,1},{18,19},{19,18},{3,4},{4,3},{20,21},{2... | collective-permute-start | bytes 393224 | tf_op jit(solution)/shard_map/cond/branch_1_fun/ppermute | solution.py:492
  23.8 6.4 %collective-permute-start = (f32[24,128]{1,0:T(8,128)S(1)}, f32[24,128]{1,0:T(8,128)}, u32[]{:S(2)}, u32[]{:S(2)}) collective-permute-start(f32[24,128]{1,0:T(8,128)S(1)} %get-tuple-element.24), channel_id=1, source_target_pairs={{0,16},{16,0},{1,17},{17,1},{2,18},{18,2},{3,19},{19,3},{4,20},{20... | collective-permute-start | bytes 36872 | tf_op jit(solution)/shard_map/cond/branch_1_fun/ppermute | solution.py:513
  31.3 5.1 %collective-permute-start.4 = (f32[264,128]{1,0:T(8,128)S(1)}, f32[264,128]{1,0:T(8,128)S(1)}, u32[]{:S(2)}, u32[]{:S(2)}) collective-permute-start(f32[264,128]{1,0:T(8,128)S(1)} %get-tuple-element.156), channel_id=1, source_target_pairs={{0,16},{16,0},{1,17},{17,1},{2,18},{18,2},{3,19},{19,3},{4,20},{20... | collective-permute-start | bytes 405512 | tf_op jit(solution)/shard_map/ppermute | solution.py:550
  32.8 7.3 %collective-permute-start.5 = (f32[264,128]{1,0:T(8,128)S(1)}, f32[264,128]{1,0:T(8,128)S(1)}, u32[]{:S(2)}, u32[]{:S(2)}) collective-permute-start(f32[264,128]{1,0:T(8,128)S(1)} %get-tuple-element.157), channel_id=1, source_target_pairs={{16,17},{17,16},{1,2},{2,1},{18,19},{19,18},{3,4},{4,3},{20,21},{2... | collective-permute-start | bytes 405512 | tf_op jit(solution)/shard_map/ppermute | solution.py:549
  41.1 3.7 %collective-permute-start.6 = (f32[8,128]{1,0:T(8,128)S(1)}, f32[8,128]{1,0:T(8,128)S(1)}, u32[]{:S(2)}, u32[]{:S(2)}) collective-permute-start(f32[8,128]{1,0:T(8,128)S(1)} %get-tuple-element.162), channel_id=1, source_target_pairs={{0,16},{16,0},{1,17},{17,1},{2,18},{18,2},{3,19},{19,3},{4,20},{20... | collective-permute-start | bytes 12296 | tf_op jit(solution)/shard_map/ppermute | solution.py:550
  41.2 5.8 %collective-permute-start.7 = (f32[8,128]{1,0:T(8,128)S(1)}, f32[8,128]{1,0:T(8,128)S(1)}, u32[]{:S(2)}, u32[]{:S(2)}) collective-permute-start(f32[8,128]{1,0:T(8,128)S(1)} %get-tuple-element.163), channel_id=1, source_target_pairs={{16,17},{17,16},{1,2},{2,1},{18,19},{19,18},{3,4},{4,3},{20,21},{2... | collective-permute-start | bytes 12296 | tf_op jit(solution)/shard_map/ppermute | solution.py:549
  47.6 3.7 %collective-permute-start.8 = (f32[8,128]{1,0:T(8,128)S(1)}, f32[8,128]{1,0:T(8,128)S(1)}, u32[]{:S(2)}, u32[]{:S(2)}) collective-permute-start(f32[8,128]{1,0:T(8,128)S(1)} %get-tuple-element.170), channel_id=1, source_target_pairs={{0,16},{16,0},{1,17},{17,1},{2,18},{18,2},{3,19},{19,3},{4,20},{20... | collective-permute-start | bytes 12296 | tf_op jit(solution)/shard_map/ppermute | solution.py:550
  47.7 5.8 %collective-permute-start.9 = (f32[8,128]{1,0:T(8,128)S(1)}, f32[8,128]{1,0:T(8,128)S(1)}, u32[]{:S(2)}, u32[]{:S(2)}) collective-permute-start(f32[8,128]{1,0:T(8,128)S(1)} %get-tuple-element.171), channel_id=1, source_target_pairs={{16,17},{17,16},{1,2},{2,1},{18,19},{19,18},{3,4},{4,3},{20,21},{2... | collective-permute-start | bytes 12296 | tf_op jit(solution)/shard_map/ppermute | solution.py:549
  54.1 3.7 %collective-permute-start.10 = (f32[8,128]{1,0:T(8,128)S(1)}, f32[8,128]{1,0:T(8,128)S(1)}, u32[]{:S(2)}, u32[]{:S(2)}) collective-permute-start(f32[8,128]{1,0:T(8,128)S(1)} %get-tuple-element.178), channel_id=1, source_target_pairs={{0,16},{16,0},{1,17},{17,1},{2,18},{18,2},{3,19},{19,3},{4,20},{20... | collective-permute-start | bytes 12296 | tf_op jit(solution)/shard_map/ppermute | solution.py:550
  54.2 5.8 %collective-permute-start.11 = (f32[8,128]{1,0:T(8,128)S(1)}, f32[8,128]{1,0:T(8,128)S(1)}, u32[]{:S(2)}, u32[]{:S(2)}) collective-permute-start(f32[8,128]{1,0:T(8,128)S(1)} %get-tuple-element.179), channel_id=1, source_target_pairs={{16,17},{17,16},{1,2},{2,1},{18,19},{19,18},{3,4},{4,3},{20,21},{2... | collective-permute-start | bytes 12296 | tf_op jit(solution)/shard_map/ppermute | solution.py:549
  60.7 3.7 %collective-permute-start.12 = (f32[8,128]{1,0:T(8,128)S(1)}, f32[8,128]{1,0:T(8,128)S(1)}, u32[]{:S(2)}, u32[]{:S(2)}) collective-permute-start(f32[8,128]{1,0:T(8,128)S(1)} %get-tuple-element.187), channel_id=1, source_target_pairs={{0,16},{16,0},{1,17},{17,1},{2,18},{18,2},{3,19},{19,3},{4,20},{20... | collective-permute-start | bytes 12296 | tf_op jit(solution)/shard_map/ppermute | solution.py:550
  60.8 5.8 %collective-permute-start.13 = (f32[8,128]{1,0:T(8,128)S(1)}, f32[8,128]{1,0:T(8,128)S(1)}, u32[]{:S(2)}, u32[]{:S(2)}) collective-permute-start(f32[8,128]{1,0:T(8,128)S(1)} %get-tuple-element.188), channel_id=1, source_target_pairs={{16,17},{17,16},{1,2},{2,1},{18,19},{19,18},{3,4},{4,3},{20,21},{2... | collective-permute-start | bytes 12296 | tf_op jit(solution)/shard_map/ppermute | solution.py:549
  67.2 3.7 %collective-permute-start.14 = (f32[8,128]{1,0:T(8,128)S(1)}, f32[8,128]{1,0:T(8,128)S(1)}, u32[]{:S(2)}, u32[]{:S(2)}) collective-permute-start(f32[8,128]{1,0:T(8,128)S(1)} %get-tuple-element.192), channel_id=1, source_target_pairs={{0,16},{16,0},{1,17},{17,1},{2,18},{18,2},{3,19},{19,3},{4,20},{20... | collective-permute-start | bytes 12296 | tf_op jit(solution)/shard_map/ppermute | solution.py:550
  67.3 5.8 %collective-permute-start.15 = (f32[8,128]{1,0:T(8,128)S(1)}, f32[8,128]{1,0:T(8,128)S(1)}, u32[]{:S(2)}, u32[]{:S(2)}) collective-permute-start(f32[8,128]{1,0:T(8,128)S(1)} %get-tuple-element.193), channel_id=1, source_target_pairs={{16,17},{17,16},{1,2},{2,1},{18,19},{19,18},{3,4},{4,3},{20,21},{2... | collective-permute-start | bytes 12296 | tf_op jit(solution)/shard_map/ppermute | solution.py:549
  73.7 3.7 %collective-permute-start.16 = (f32[8,128]{1,0:T(8,128)S(1)}, f32[8,128]{1,0:T(8,128)S(1)}, u32[]{:S(2)}, u32[]{:S(2)}) collective-permute-start(f32[8,128]{1,0:T(8,128)S(1)} %get-tuple-element.200), channel_id=1, source_target_pairs={{0,16},{16,0},{1,17},{17,1},{2,18},{18,2},{3,19},{19,3},{4,20},{20... | collective-permute-start | bytes 12296 | tf_op jit(solution)/shard_map/ppermute | solution.py:550
  73.8 5.8 %collective-permute-start.17 = (f32[8,128]{1,0:T(8,128)S(1)}, f32[8,128]{1,0:T(8,128)S(1)}, u32[]{:S(2)}, u32[]{:S(2)}) collective-permute-start(f32[8,128]{1,0:T(8,128)S(1)} %get-tuple-element.201), channel_id=1, source_target_pairs={{16,17},{17,16},{1,2},{2,1},{18,19},{19,18},{3,4},{4,3},{20,21},{2... | collective-permute-start | bytes 12296 | tf_op jit(solution)/shard_map/ppermute | solution.py:549
  80.3 3.7 %collective-permute-start.18 = (f32[8,128]{1,0:T(8,128)S(1)}, f32[8,128]{1,0:T(8,128)S(1)}, u32[]{:S(2)}, u32[]{:S(2)}) collective-permute-start(f32[8,128]{1,0:T(8,128)S(1)} %get-tuple-element.208), channel_id=1, source_target_pairs={{0,16},{16,0},{1,17},{17,1},{2,18},{18,2},{3,19},{19,3},{4,20},{20... | collective-permute-start | bytes 12296 | tf_op jit(solution)/shard_map/ppermute | solution.py:550
  80.3 5.8 %collective-permute-start.19 = (f32[8,128]{1,0:T(8,128)S(1)}, f32[8,128]{1,0:T(8,128)S(1)}, u32[]{:S(2)}, u32[]{:S(2)}) collective-permute-start(f32[8,128]{1,0:T(8,128)S(1)} %get-tuple-element.209), channel_id=1, source_target_pairs={{16,17},{17,16},{1,2},{2,1},{18,19},{19,18},{3,4},{4,3},{20,21},{2... | collective-permute-start | bytes 12296 | tf_op jit(solution)/shard_map/ppermute | solution.py:549
  86.8 3.7 %collective-permute-start.20 = (f32[8,128]{1,0:T(8,128)S(1)}, f32[8,128]{1,0:T(8,128)S(1)}, u32[]{:S(2)}, u32[]{:S(2)}) collective-permute-start(f32[8,128]{1,0:T(8,128)S(1)} %get-tuple-element.217), channel_id=1, source_target_pairs={{0,16},{16,0},{1,17},{17,1},{2,18},{18,2},{3,19},{19,3},{4,20},{20... | collective-permute-start | bytes 12296 | tf_op jit(solution)/shard_map/ppermute | solution.py:550
  86.9 5.8 %collective-permute-start.21 = (f32[8,128]{1,0:T(8,128)S(1)}, f32[8,128]{1,0:T(8,128)S(1)}, u32[]{:S(2)}, u32[]{:S(2)}) collective-permute-start(f32[8,128]{1,0:T(8,128)S(1)} %get-tuple-element.218), channel_id=1, source_target_pairs={{16,17},{17,16},{1,2},{2,1},{18,19},{19,18},{3,4},{4,3},{20,21},{2... | collective-permute-start | bytes 12296 | tf_op jit(solution)/shard_map/ppermute | solution.py:549
  93.3 3.7 %collective-permute-start.22 = (f32[8,128]{1,0:T(8,128)S(1)}, f32[8,128]{1,0:T(8,128)S(1)}, u32[]{:S(2)}, u32[]{:S(2)}) collective-permute-start(f32[8,128]{1,0:T(8,128)S(1)} %get-tuple-element.222), channel_id=1, source_target_pairs={{0,16},{16,0},{1,17},{17,1},{2,18},{18,2},{3,19},{19,3},{4,20},{20... | collective-permute-start | bytes 12296 | tf_op jit(solution)/shard_map/ppermute | solution.py:550
  93.4 5.8 %collective-permute-start.23 = (f32[8,128]{1,0:T(8,128)S(1)}, f32[8,128]{1,0:T(8,128)S(1)}, u32[]{:S(2)}, u32[]{:S(2)}) collective-permute-start(f32[8,128]{1,0:T(8,128)S(1)} %get-tuple-element.223), channel_id=1, source_target_pairs={{16,17},{17,16},{1,2},{2,1},{18,19},{19,18},{3,4},{4,3},{20,21},{2... | collective-permute-start | bytes 12296 | tf_op jit(solution)/shard_map/ppermute | solution.py:549
  99.8 3.7 %collective-permute-start.24 = (f32[8,128]{1,0:T(8,128)S(1)}, f32[8,128]{1,0:T(8,128)S(1)}, u32[]{:S(2)}, u32[]{:S(2)}) collective-permute-start(f32[8,128]{1,0:T(8,128)S(1)} %get-tuple-element.230), channel_id=1, source_target_pairs={{0,16},{16,0},{1,17},{17,1},{2,18},{18,2},{3,19},{19,3},{4,20},{20... | collective-permute-start | bytes 12296 | tf_op jit(solution)/shard_map/ppermute | solution.py:550
  99.9 5.8 %collective-permute-start.25 = (f32[8,128]{1,0:T(8,128)S(1)}, f32[8,128]{1,0:T(8,128)S(1)}, u32[]{:S(2)}, u32[]{:S(2)}) collective-permute-start(f32[8,128]{1,0:T(8,128)S(1)} %get-tuple-element.231), channel_id=1, source_target_pairs={{16,17},{17,16},{1,2},{2,1},{18,19},{19,18},{3,4},{4,3},{20,21},{2... | collective-permute-start | bytes 12296 | tf_op jit(solution)/shard_map/ppermute | solution.py:549
  106.4 3.7 %collective-permute-start.26 = (f32[8,128]{1,0:T(8,128)S(1)}, f32[8,128]{1,0:T(8,128)S(1)}, u32[]{:S(2)}, u32[]{:S(2)}) collective-permute-start(f32[8,128]{1,0:T(8,128)S(1)} %get-tuple-element.238), channel_id=1, source_target_pairs={{0,16},{16,0},{1,17},{17,1},{2,18},{18,2},{3,19},{19,3},{4,20},{20... | collective-permute-start | bytes 12296 | tf_op jit(solution)/shard_map/ppermute | solution.py:550
  106.4 5.8 %collective-permute-start.27 = (f32[8,128]{1,0:T(8,128)S(1)}, f32[8,128]{1,0:T(8,128)S(1)}, u32[]{:S(2)}, u32[]{:S(2)}) collective-permute-start(f32[8,128]{1,0:T(8,128)S(1)} %get-tuple-element.239), channel_id=1, source_target_pairs={{16,17},{17,16},{1,2},{2,1},{18,19},{19,18},{3,4},{4,3},{20,21},{2... | collective-permute-start | bytes 12296 | tf_op jit(solution)/shard_map/ppermute | solution.py:549
  112.9 3.7 %collective-permute-start.28 = (f32[8,128]{1,0:T(8,128)S(1)}, f32[8,128]{1,0:T(8,128)S(1)}, u32[]{:S(2)}, u32[]{:S(2)}) collective-permute-start(f32[8,128]{1,0:T(8,128)S(1)} %get-tuple-element.247), channel_id=1, source_target_pairs={{0,16},{16,0},{1,17},{17,1},{2,18},{18,2},{3,19},{19,3},{4,20},{20... | collective-permute-start | bytes 12296 | tf_op jit(solution)/shard_map/ppermute | solution.py:550
  113.0 5.8 %collective-permute-start.29 = (f32[8,128]{1,0:T(8,128)S(1)}, f32[8,128]{1,0:T(8,128)S(1)}, u32[]{:S(2)}, u32[]{:S(2)}) collective-permute-start(f32[8,128]{1,0:T(8,128)S(1)} %get-tuple-element.248), channel_id=1, source_target_pairs={{16,17},{17,16},{1,2},{2,1},{18,19},{19,18},{3,4},{4,3},{20,21},{2... | collective-permute-start | bytes 12296 | tf_op jit(solution)/shard_map/ppermute | solution.py:549
  119.4 3.7 %collective-permute-start.30 = (f32[8,128]{1,0:T(8,128)S(1)}, f32[8,128]{1,0:T(8,128)S(1)}, u32[]{:S(2)}, u32[]{:S(2)}) collective-permute-start(f32[8,128]{1,0:T(8,128)S(1)} %get-tuple-element.252), channel_id=1, source_target_pairs={{0,16},{16,0},{1,17},{17,1},{2,18},{18,2},{3,19},{19,3},{4,20},{20... | collective-permute-start | bytes 12296 | tf_op jit(solution)/shard_map/ppermute | solution.py:550
  119.5 5.8 %collective-permute-start.31 = (f32[8,128]{1,0:T(8,128)S(1)}, f32[8,128]{1,0:T(8,128)S(1)}, u32[]{:S(2)}, u32[]{:S(2)}) collective-permute-start(f32[8,128]{1,0:T(8,128)S(1)} %get-tuple-element.253), channel_id=1, source_target_pairs={{16,17},{17,16},{1,2},{2,1},{18,19},{19,18},{3,4},{4,3},{20,21},{2... | collective-permute-start | bytes 12296 | tf_op jit(solution)/shard_map/ppermute | solution.py:549
  126.0 3.7 %collective-permute-start.32 = (f32[8,128]{1,0:T(8,128)S(1)}, f32[8,128]{1,0:T(8,128)S(1)}, u32[]{:S(2)}, u32[]{:S(2)}) collective-permute-start(f32[8,128]{1,0:T(8,128)S(1)} %get-tuple-element.260), channel_id=1, source_target_pairs={{0,16},{16,0},{1,17},{17,1},{2,18},{18,2},{3,19},{19,3},{4,20},{20... | collective-permute-start | bytes 12296 | tf_op jit(solution)/shard_map/ppermute | solution.py:550
  126.0 5.8 %collective-permute-start.33 = (f32[8,128]{1,0:T(8,128)S(1)}, f32[8,128]{1,0:T(8,128)S(1)}, u32[]{:S(2)}, u32[]{:S(2)}) collective-permute-start(f32[8,128]{1,0:T(8,128)S(1)} %get-tuple-element.261), channel_id=1, source_target_pairs={{16,17},{17,16},{1,2},{2,1},{18,19},{19,18},{3,4},{4,3},{20,21},{2... | collective-permute-start | bytes 12296 | tf_op jit(solution)/shard_map/ppermute | solution.py:549
  132.5 3.7 %collective-permute-start.34 = (f32[8,128]{1,0:T(8,128)S(1)}, f32[8,128]{1,0:T(8,128)S(1)}, u32[]{:S(2)}, u32[]{:S(2)}) collective-permute-start(f32[8,128]{1,0:T(8,128)S(1)} %get-tuple-element.268), channel_id=1, source_target_pairs={{0,16},{16,0},{1,17},{17,1},{2,18},{18,2},{3,19},{19,3},{4,20},{20... | collective-permute-start | bytes 12296 | tf_op jit(solution)/shard_map/ppermute | solution.py:550
  132.6 5.8 %collective-permute-start.35 = (f32[8,128]{1,0:T(8,128)S(1)}, f32[8,128]{1,0:T(8,128)S(1)}, u32[]{:S(2)}, u32[]{:S(2)}) collective-permute-start(f32[8,128]{1,0:T(8,128)S(1)} %get-tuple-element.269), channel_id=1, source_target_pairs={{16,17},{17,16},{1,2},{2,1},{18,19},{19,18},{3,4},{4,3},{20,21},{2... | collective-permute-start | bytes 12296 | tf_op jit(solution)/shard_map/ppermute | solution.py:549
  138.8 3.7 %collective-permute-start.36 = (f32[4,2,2,128]{3,2,1,0:T(2,128)S(1)}, f32[4,2,2,128]{3,2,1,0:T(2,128)S(1)}, u32[]{:S(2)}, u32[]{:S(2)}) collective-permute-start(f32[4,2,2,128]{3,2,1,0:T(2,128)S(1)} %rev.12), channel_id=1, source_target_pairs={{0,16},{16,0},{1,17},{17,1},{2,18},{18,2},{3,19},{19,3},{4,20},{20... | collective-permute-start | bytes 24584 | tf_op jit(solution)/shard_map/ppermute | solution.py:564

commit v12 on v11

--- a/solution.py
+++ b/solution.py
@@ -305,17 +305,15 @@
     )
 
 
-def messages(f, g):
-    return [
-        jnp.concatenate([row_of(x, j, b) for x in (f, g) for j in order], axis=0)
-        for b, order in ((1, range(N)[::-1]), (0, range(N)))
-    ]
-
-
-def ahead(first, sweep, f, q, residue, capacity, injected):
+def message(f, g, b):
+    order = range(N)[::-1] if b == 1 else range(N)
+    return jnp.concatenate([row_of(x, j, b) for x in (f, g) for j in order], axis=0)
+
+
+def ahead(first, sweep, f, residue, capacity, injected):
     if first:
-        return injected - q
-    return residue - STRIDES[sweep] * (q + capacity * f) + MOMENTA[sweep + 1] * f
+        return injected, 1.0
+    return residue - STRIDES[sweep] * (capacity * f) + MOMENTA[sweep + 1] * f, STRIDES[sweep]
 
 
 def small_part(small, index):
@@ -333,8 +331,8 @@
     f = small_part(small, INITIAL)
     q = inner_product(f, halves)
     q_out[...] = q
-    to_a, to_b = messages(f, ahead(True, 0, f, q, None, None, small_part(small, 0)))
-    msg_a[:2 * N, :], msg_b[:2 * N, :] = to_a, to_b
+    g = small_part(small, 0) - q
+    msg_a[:2 * N, :], msg_b[:2 * N, :] = message(f, g, 1), message(f, g, 0)
     width = f.shape[1]
     for h in range(ROWS):
         start = 2 * N + h * width
@@ -378,61 +376,100 @@
                     out[i:i + 1, :] = part
 
 
-def beside_kernel(begin, keep, recv_0, recv_1, beyond_0, first_a, first_b, got_a, q_ref, *refs):
+def stacked(rows):
+    return jnp.concatenate(rows, axis=0)
+
+
+def responses(halves, beyond_0, first_a, first_b, f):
+    return stacked([
+        matvec([(facing_block(halves, beyond_0, first_a, first_b, j, b), row_of(f, j, b))]) for j, b in TILES
+    ])
+
+
+def response_kernel(keep, recv_0, recv_1, beyond_0, first_a, first_b, small, out):
+    out[...] = responses(((keep,), (recv_0, recv_1)), beyond_0, first_a, first_b, small_part(small, INITIAL))
+
+
+def to_a_kernel(factor, keep, recv_0, recv_1, beyond_0, first_a, first_b, f_ref, q_ref, base, response_out, q_out, msg_a):
     halves = ((keep,), (recv_0, recv_1))
-    response_out, q_out = refs[-2:]
-    f = small_part(refs[0], INITIAL) if begin else refs[0][...]
-    q = q_ref[...]
-    response, total = [], []
+    f, q = f_ref[...], q_ref[...]
+    q = stacked([
+        matvec([(block, row_of(f, *at)) for block, at in tile_terms(halves, j, b)]) if b == 1 else row_of(q, j, b)
+        for j, b in TILES
+    ])
+    q_out[...] = q
+    msg_a[...] = message(f, base[...] - factor * q, 1)
+    response_out[...] = responses(halves, beyond_0, first_a, first_b, f)
+
+
+def advance(instant, pair, small, product, f, residue):
+    if pair == 0:
+        residue = small_part(small, instant) - product
+        return residue, residue, 1.0
+    sweep = 2 * pair - 1
+    residue = residue - STRIDES[sweep] * (product + small_part(small, CAPACITY) * f)
+    return residue, residue + MOMENTA[sweep + 1] * f, STRIDES[sweep]
+
+
+def inner_and_side(halves, j, b, f):
+    terms = [(block, row_of(f, *at)) for block, at in tile_terms(halves, j, b)]
+    return terms[:-1], terms[-1:]
+
+
+def beside_kernel(instant, pair, keep, recv_0, recv_1, small, got_a, response_ref, q_ref, *refs):
+    halves = ((keep,), (recv_0, recv_1))
+    product_out, part_out = refs[-2:]
+    f = small_part(small, INITIAL) if instant == pair == 0 else refs[0][...]
+    residue = None if pair == 0 else refs[1][...]
+    q, response = q_ref[...], response_ref[...]
+    product = stacked([
+        row_of(q, j, b) + matvec([(halo_block(halves, j, b), got_a[j:j + 1, :])]) if b == 1 else row_of(q, j, b)
+        for j, b in TILES
+    ])
+    product_out[...] = product
+    _, f2, scale = advance(instant, pair, small, product, f, residue)
+    part = []
     for j, b in TILES:
-        response.append(matvec([(facing_block(halves, beyond_0, first_a, first_b, j, b), row_of(f, j, b))]))
-        mine = row_of(q, j, b)
+        inner, side = inner_and_side(halves, j, b, f2)
         if b == 1:
-            mine = mine + matvec([(halo_block(halves, j, b), got_a[j:j + 1, :])])
-        total.append(mine)
-    response_out[...] = jnp.concatenate(response, axis=0)
-    q_out[...] = jnp.concatenate(total, axis=0)
-
-
-def pair_kernel(instant, pair, last, keep, recv_0, recv_1, small, got_a, got_b, response_ref, q_ref, *refs):
+            beside = got_a[N + j:N + j + 1, :] - scale * row_of(response, j, b)
+            part.append(matvec(inner + [(halo_block(halves, j, b), beside)]))
+        else:
+            part.append(matvec(side))
+    part_out[...] = stacked(part)
+
+
+def pair_kernel(instant, pair, last, keep, recv_0, recv_1, small, got_b, response_ref, product_ref, part_ref, *refs):
     halves = ((keep,), (recv_0, recv_1))
     first = pair == 0
     capacity = small_part(small, CAPACITY)
-    q, response = q_ref[...], response_ref[...]
     if first and instant == 0:
         f = small_part(small, INITIAL)
     else:
         f, refs = refs[0][...], refs[1:]
+    residue = estimate = None
     if not first:
         residue, estimate, refs = refs[0][...], refs[1][...], refs[2:]
-    got = (got_b, got_a)
-    sweep = 2 * pair - 1
-
-    product = []
-    for j, b in TILES:
-        mine = row_of(q, j, b)
-        if b == 0:
-            mine = mine + matvec([(halo_block(halves, j, b), got_b[j:j + 1, :])])
-        product.append(mine)
-    product = jnp.concatenate(product, axis=0)
-    if first:
-        residue = small_part(small, instant) - product
-        f2 = residue
-        estimate = f + STRIDES[0] * f2
-        scale = 1.0
-    else:
-        residue = residue - STRIDES[sweep] * (product + capacity * f)
-        f2 = residue + MOMENTA[sweep + 1] * f
-        estimate = estimate + STRIDES[sweep + 1] * f2
-        scale = STRIDES[sweep]
+    response, product, part = response_ref[...], product_ref[...], part_ref[...]
+
+    product = stacked([
+        row_of(product, j, b) + matvec([(halo_block(halves, j, b), got_b[j:j + 1, :])]) if b == 0
+        else row_of(product, j, b) for j, b in TILES
+    ])
+    residue, f2, scale = advance(instant, pair, small, product, f, residue)
+    estimate = f + STRIDES[0] * f2 if first else estimate + STRIDES[2 * pair] * f2
 
     outs = []
     for j, b in TILES:
-        beside = got[b][N + j:N + j + 1, :] - scale * row_of(response, j, b)
-        terms = [(block, row_of(f2, *at)) for block, at in tile_terms(halves, j, b)]
-        outs.append(matvec(terms + [(halo_block(halves, j, b), beside)]))
+        inner, side = inner_and_side(halves, j, b, f2)
+        if b == 0:
+            beside = got_b[N + j:N + j + 1, :] - scale * row_of(response, j, b)
+            rest = matvec(inner + [(halo_block(halves, j, b), beside)])
+        else:
+            rest = matvec(side)
+        outs.append(row_of(part, j, b) + rest)
     sweep = 2 * pair
-    residue = residue - STRIDES[sweep] * (jnp.concatenate(outs, axis=0) + capacity * f2)
+    residue = residue - STRIDES[sweep] * (stacked(outs) + capacity * f2)
     f3 = residue + MOMENTA[sweep + 1] * f2
     estimate = estimate + STRIDES[sweep + 1] * f3
     closing = sweep + 2 == ITERS
@@ -442,11 +479,17 @@
     f_out[...] = f3
     if last:
         return
-    q = inner_product(f3, halves)
-    q_out, msg_a, msg_b = refs[:3]
+    zero = jnp.zeros_like(f3[:1])
+    q = stacked([
+        matvec([(block, row_of(f3, *at)) for block, at in tile_terms(halves, j, b)]) if b == 0 else zero for j, b in TILES
+    ])
+    upcoming = small_part(small, instant + 1) if closing else None
+    base, factor = ahead(closing, sweep + 1, f3, residue, capacity, upcoming)
+    q_out, base_out, msg_b = refs[:3]
     q_out[...] = q
-    upcoming = small_part(small, instant + 1) if closing else None
-    msg_a[...], msg_b[...] = messages(f3, ahead(closing, sweep + 1, f3, q, residue, capacity, upcoming))
+    base_out[...] = base
+    to_b = message(f3, base - factor * q, 0)
+    msg_b[...] = stacked([to_b, jnp.zeros_like(to_b)])
     if not closing:
         refs[3][...] = residue
         refs[4][...] = estimate
@@ -539,26 +582,30 @@
     first_shape = jax.ShapeDtypeStruct((2 * N + ROWS * width, width), jnp.float32)
     unit_small = jax.ShapeDtypeStruct(((STEPS + 2) * N * HALF, width), jnp.float32)
     msg_a, msg_b, q, small = call(start_kernel, (first_shape, first_shape, shape, unit_small), 28, *halves, *small)
-    field, first_a, first_b = (), None, None
-    frames = []
-    state = ()
+    got_b = first_b = lax.ppermute(msg_b, both, b_pairs)
+    got_a = first_a = lax.ppermute(msg_a, "row", swap)
+    blocks = (*halves, beyond_0, first_a, first_b)
+    (response,) = call(response_kernel, (shape,), 8, *blocks, small)
+    b_shape = jax.ShapeDtypeStruct((4 * N, width), jnp.float32)
+    field, state, frames = (), (), []
     for instant in range(STEPS):
         for pair in range(ITERS // 2):
             closing = pair + 1 == ITERS // 2
             last = closing and instant + 1 == STEPS
+            product, part = call(functools.partial(beside_kernel, instant, pair), (shape,) * 2, 22,
+                                 *halves, small, got_a, response, q, *field, *state[:1])
+            out = call(functools.partial(pair_kernel, instant, pair, last), (shape,) if last else (shape,) * 3 + (b_shape,) + (shape,) * (0 if closing else 2),
+                       36, *halves, small, got_b, response, product, part, *field, *state)
+            field = out[:1]
+            if last:
+                break
+            q, base, msg_b = out[1:4]
+            state = out[4:]
             got_b = lax.ppermute(msg_b, both, b_pairs)
+            factor = 1.0 if closing else STRIDES[2 * pair + 1]
+            response, q, msg_a = call(functools.partial(to_a_kernel, factor), (shape,) * 3, 22, *blocks, *field, q, base)
             got_a = lax.ppermute(msg_a, "row", swap)
-            if first_b is None:
-                first_a, first_b = got_a, got_b
-            response, q = call(functools.partial(beside_kernel, not field), (shape,) * 2, 12, *halves, beyond_0, first_a, first_b,
-                               got_a, q, *(field or (small,)))
-            out = call(functools.partial(pair_kernel, instant, pair, last), (shape,) * (1 if last else 4 if closing else 6),
-                       68, *halves, small, got_a, got_b, response, q, *field, *state)
-            field = out[:1]
-            if not last:
-                q, msg_a, msg_b = out[1:4]
-                state = out[4:]
-        frames.append(out[0])
+        frames.append(field[0])
 
     done = jnp.stack(frames).reshape(STEPS, N, HALF, width)
     got = lax.ppermute(jnp.flip(done[:, ROWS:], 1), "row", swap)

time: 144 us -> 161 us (1.12)
  waiting for transfers between devices: 62.2 us -> 68 us
  Pallas kernels: 24.3 us -> 29.3 us
  starting transfers between devices: 53.8 us -> 58.7 us
    ppermute x16 -> x15, waiting for transfers between devices: 19.3 us -> 53.5 us  [shards_chain(): got_a = lax.ppermute(msg_a, 'row', swap)]
    ppermute x16 -> x15, waiting for transfers between devices: 32.9 us -> 0.04 us  [shards_chain(): got_b = lax.ppermute(msg_b, both, b_pairs)]
    pallas_call x33 -> x49, Pallas kernels: 15.2 us -> 20.3 us  [call(): pl.pallas_call(body, out_shape=outs, in_specs=[vmem] * len(ins), out_spec...]
    ppermute x0 -> x2, waiting for transfers between devices: none -> 4.37 us  [the longest x1 3.82 us: shards_chain(): got_b = first_b = lax.ppermute(msg_b, both, b_pairs)]
    ppermute x0 -> x2, starting transfers between devices: none -> 3.51 us  [the longest x1 1.92 us: shards_chain(): got_b = first_b = lax.ppermute(msg_b, both, b_pairs)]
    ppermute x16 -> x15, starting transfers between devices: 38 us -> 40.6 us  [shards_chain(): got_b = lax.ppermute(msg_b, both, b_pairs)]
  transfers between devices with their start and end apart: 38 -> 38, of which waited for: 35 -> 20; matrix products, arithmetic and copies ran while one was open for 1% -> 1% of each run, Pallas kernels for 8% -> 11%
where the time goes in v12:
time: 161 us; the launch traced here: 159 us
  waiting for transfers between devices  68 us (42%)
  starting transfers between devices  58.7 us (36%)
  Pallas kernels  29.3 us (18%)
  local copies, waits for them, and re-layouts  1.61 us (1%)
    ppermute x15, waiting for transfers between devices, shards_chain(): got_a = lax.ppermute(msg_a, 'row', swap)  53.5 us
    ppermute x15, starting transfers between devices, shards_chain(): got_b = lax.ppermute(msg_b, both, b_pairs)  40.6 us
    pallas_call x49, Pallas kernels, call(): pl.pallas_call(body, out_shape=outs, in_specs=[vmem] * len(ins), out_spec...  20.3 us
    pallas_call x3, Pallas kernels, pack(): pl.pallas_call(functools.partial(pack_kernel, n_col, sent, first, count),...  6.83 us
    all_to_all x1, starting transfers between devices, beside(): lax.all_to_all(by_target, 'col', split_axis=0, concat_axis=0, tiled=True)  6.27 us
    ppermute x1, waiting for transfers between devices, beside(): return (small, lax.ppermute(send, 'row', swap), beyond_0)  4.05 us
    ppermute x1, waiting for transfers between devices, shards_chain(): got_b = first_b = lax.ppermute(msg_b, both, b_pairs)  3.82 us
    ppermute x1, waiting for transfers between devices, shards_chain(): got = lax.ppermute(jnp.flip(done[:, ROWS:], 1), 'row', swap)  3.63 us
  transfers between devices with their start and end apart: 38, of which 20 were waited for; matrix products, arithmetic and copies ran while one was open for 1% of the time, Pallas kernels for 11%

profile of v12, /device:TPU:8, one launch (start us, length us, event | category | flops | bytes accessed | tf_op | source)
XLA Modules:
  0.0 159.1 jit_solution(1811156317503785818)
XLA Ops:
  0.1 2.0 %pack.4 = f32[12,128,128]{2,1,0:T(8,128)S(1)} custom-call(s32[2]{0:T(128)S(1)} %pad_add_fusion.place_ref, s32[2,4,4]{2,1,0:T(4,128)} %pattern_ref.5, f32[2,4,128,128]{3,2,1,0:T(8,128)} %own_hbm.5, f32[4,2,4,128,128]{4,3,2,1,0:T(8,128)} %nb_hbm.5), custom_call_target="tpu_custom_call" | custom-call | tf_op jit(solution)/shard_map/pack/pallas_call | solution.py:518
  2.1 1.6 collective-permute-start.2
  3.7 2.5 %pack.5 = f32[6,128,128]{2,1,0:T(8,128)} custom-call(s32[2]{0:T(128)S(1)} %pad_add_fusion.place_ref, s32[2,4,4]{2,1,0:T(4,128)} %pattern_ref.5, f32[2,4,128,128]{3,2,1,0:T(8,128)} %own_hbm.5, f32[4,2,4,128,128]{4,3,2,1,0:T(8,128)} %nb_hbm.5), custom_call_target="tpu_custom_call" | custom-call | tf_op jit(solution)/shard_map/pack/pallas_call | solution.py:518
  6.8 2.3 %pack.3 = (f32[20,128,128]{2,1,0:T(8,128)S(1)}, f32[2,128,128]{2,1,0:T(8,128)S(1)}) custom-call(s32[2]{0:T(128)S(1)} %pad_add_fusion.place_ref, s32[2,4,4]{2,1,0:T(4,128)} %pattern_ref.5, f32[2,4,128,128]{3,2,1,0:T(8,128)} %own_hbm.5, f32[4,2,4,128,128]{4,3,2,1,0:T(8,128)} %nb_hbm.5), custom_call_target="tpu_custom_call" | custom-call | tf_op jit(solution)/shard_map/pack/pallas_call | solution.py:518
  9.1 21.1 %conditional.1 = (f32[24,128]{1,0:T(8,128)}, f32[24,128]{1,0:T(8,128)}, f32[2,128,128]{2,1,0:T(8,128)S(1)}) conditional(s32[]{:T(128)} %convert_element_type.3, f32[2,128,128]{2,1,0:T(8,128)S(1)} %get-tuple-element.197, (f32[1,1,16,4,512]{4,3,2,1,0:T(4,128)S(1)}, s32[1,1,16,4]{2,3,1,0:T(4,128)S(1)}, s32[2]{0:T(128)S(1)}, f32[2,4,128]{2,1,0:T(4,128)}, ...), branch_computations={%region_0.1_spmd, %region_1.2_spmd} | conditional | bytes 1532612 | solution.py:558
  9.8 0.7 by_target.1
  10.5 6.3 %all-to-all-start = ((f32[16,1,2176]{2,1,0:T(1,128)}), f32[16,1,2176]{2,1,0:T(1,128)S(1)}, u32[]{:S(2)}, u32[]{:S(2)}) async-start(f32[16,1,2176]{2,1,0:T(1,128)} %by_target.1), calls=%async_computation | async-start | bytes 278528 | tf_op jit(solution)/shard_map/cond/branch_1_fun/all_to_all | solution.py:545
  16.8 3.1 %collective-permute-start.1 = (f32[2,128,128]{2,1,0:T(8,128)S(1)}, f32[2,128,128]{2,1,0:T(8,128)}, u32[]{:S(2)}, u32[]{:S(2)}) collective-permute-start(f32[2,128,128]{2,1,0:T(8,128)S(1)} %get-tuple-element.25), channel_id=1, source_target_pairs={{16,17},{17,16},{1,2},{2,1},{18,19},{19,18},{3,4},{4,3},{20,21},{2... | collective-permute-start | bytes 393224 | tf_op jit(solution)/shard_map/cond/branch_1_fun/ppermute | solution.py:535
  19.9 2.4 %all-to-all-done = f32[16,1,2176]{2,1,0:T(1,128)S(1)} async-done(((f32[16,1,2176]{2,1,0:T(1,128)}), f32[16,1,2176]{2,1,0:T(1,128)S(1)}, u32[]{:S(2)}, u32[]{:S(2)}) %all-to-all-start) | async-done | bytes 139296 | tf_op jit(solution)/shard_map/cond/branch_1_fun/all_to_all | solution.py:545
  22.3 1.5 small.1
  23.8 1.5 collective-permute-start
  25.3 0.9 copy.23
  26.2 4.0 %collective-permute-done = f32[24,128]{1,0:T(8,128)} collective-permute-done((f32[24,128]{1,0:T(8,128)S(1)}, f32[24,128]{1,0:T(8,128)}, u32[]{:S(2)}, u32[]{:S(2)}) %collective-permute-start) | collective-permute-done | bytes 12320 | tf_op jit(solution)/shard_map/cond/branch_1_fun/ppermute | solution.py:556
  30.3 1.0 pair.49
  31.3 1.9 %collective-permute-start.4 = (f32[264,128]{1,0:T(8,128)S(1)}, f32[264,128]{1,0:T(8,128)S(1)}, u32[]{:S(2)}, u32[]{:S(2)}) collective-permute-start(f32[264,128]{1,0:T(8,128)S(1)} %get-tuple-element.201), channel_id=1, source_target_pairs={{16,17},{17,16},{1,2},{2,1},{18,19},{19,18},{3,4},{4,3},{20,21},{2... | collective-permute-start | bytes 405512 | tf_op jit(solution)/shard_map/ppermute | solution.py:585
  33.2 1.6 collective-permute-start.5
  34.8 3.8 %collective-permute-done.4.first_b.got_b = f32[264,128]{1,0:T(8,128)S(1)} collective-permute-done((f32[264,128]{1,0:T(8,128)S(1)}, f32[264,128]{1,0:T(8,128)S(1)}, u32[]{:S(2)}, u32[]{:S(2)}) %collective-permute-start.4) | collective-permute-done | bytes 135200 | tf_op jit(solution)/shard_map/ppermute | solution.py:585
  40.3 3.3 %collective-permute-start.6 = (f32[16,128]{1,0:T(8,128)S(1)}, f32[16,128]{1,0:T(8,128)S(1)}, u32[]{:S(2)}, u32[]{:S(2)}) collective-permute-start(f32[16,128]{1,0:T(8,128)S(1)} %get-tuple-element.207), channel_id=1, source_target_pairs={{16,17},{17,16},{1,2},{2,1},{18,19},{19,18},{3,4},{4,3},{20,21},{2... | collective-permute-start | bytes 24584 | tf_op jit(solution)/shard_map/ppermute | solution.py:604
  44.2 3.3 %collective-permute-done.7.got_a = f32[8,128]{1,0:T(8,128)S(1)} collective-permute-done((f32[8,128]{1,0:T(8,128)S(1)}, f32[8,128]{1,0:T(8,128)S(1)}, u32[]{:S(2)}, u32[]{:S(2)}) %collective-permute-start.7) | collective-permute-done | bytes 4128 | tf_op jit(solution)/shard_map/ppermute | solution.py:607
  48.5 2.0 %collective-permute-start.8 = (f32[16,128]{1,0:T(8,128)S(1)}, f32[16,128]{1,0:T(8,128)S(1)}, u32[]{:S(2)}, u32[]{:S(2)}) collective-permute-start(f32[16,128]{1,0:T(8,128)S(1)} %get-tuple-element.218), channel_id=1, source_target_pairs={{16,17},{17,16},{1,2},{2,1},{18,19},{19,18},{3,4},{4,3},{20,21},{2... | collective-permute-start | bytes 24584 | tf_op jit(solution)/shard_map/ppermute | solution.py:604
  51.1 3.5 %collective-permute-done.9.got_a = f32[8,128]{1,0:T(8,128)S(1)} collective-permute-done((f32[8,128]{1,0:T(8,128)S(1)}, f32[8,128]{1,0:T(8,128)S(1)}, u32[]{:S(2)}, u32[]{:S(2)}) %collective-permute-start.9) | collective-permute-done | bytes 4128 | tf_op jit(solution)/shard_map/ppermute | solution.py:607
  55.5 3.3 %collective-permute-start.10 = (f32[16,128]{1,0:T(8,128)S(1)}, f32[16,128]{1,0:T(8,128)S(1)}, u32[]{:S(2)}, u32[]{:S(2)}) collective-permute-start(f32[16,128]{1,0:T(8,128)S(1)} %get-tuple-element.229), channel_id=1, source_target_pairs={{16,17},{17,16},{1,2},{2,1},{18,19},{19,18},{3,4},{4,3},{20,21},{2... | collective-permute-start | bytes 24584 | tf_op jit(solution)/shard_map/ppermute | solution.py:604
  59.1 3.6 %collective-permute-done.11.got_a = f32[8,128]{1,0:T(8,128)S(1)} collective-permute-done((f32[8,128]{1,0:T(8,128)S(1)}, f32[8,128]{1,0:T(8,128)S(1)}, u32[]{:S(2)}, u32[]{:S(2)}) %collective-permute-start.11) | collective-permute-done | bytes 4128 | tf_op jit(solution)/shard_map/ppermute | solution.py:607
  63.7 2.0 %collective-permute-start.12 = (f32[16,128]{1,0:T(8,128)S(1)}, f32[16,128]{1,0:T(8,128)S(1)}, u32[]{:S(2)}, u32[]{:S(2)}) collective-permute-start(f32[16,128]{1,0:T(8,128)S(1)} %get-tuple-element.241), channel_id=1, source_target_pairs={{16,17},{17,16},{1,2},{2,1},{18,19},{19,18},{3,4},{4,3},{20,21},{2... | collective-permute-start | bytes 24584 | tf_op jit(solution)/shard_map/ppermute | solution.py:604
  66.1 3.6 %collective-permute-done.13.got_a = f32[8,128]{1,0:T(8,128)S(1)} collective-permute-done((f32[8,128]{1,0:T(8,128)S(1)}, f32[8,128]{1,0:T(8,128)S(1)}, u32[]{:S(2)}, u32[]{:S(2)}) %collective-permute-start.13) | collective-permute-done | bytes 4128 | tf_op jit(solution)/shard_map/ppermute | solution.py:607
  70.6 3.3 %collective-permute-start.14 = (f32[16,128]{1,0:T(8,128)S(1)}, f32[16,128]{1,0:T(8,128)S(1)}, u32[]{:S(2)}, u32[]{:S(2)}) collective-permute-start(f32[16,128]{1,0:T(8,128)S(1)} %get-tuple-element.249), channel_id=1, source_target_pairs={{16,17},{17,16},{1,2},{2,1},{18,19},{19,18},{3,4},{4,3},{20,21},{2... | collective-permute-start | bytes 24584 | tf_op jit(solution)/shard_map/ppermute | solution.py:604
  74.3 3.6 %collective-permute-done.15.got_a = f32[8,128]{1,0:T(8,128)S(1)} collective-permute-done((f32[8,128]{1,0:T(8,128)S(1)}, f32[8,128]{1,0:T(8,128)S(1)}, u32[]{:S(2)}, u32[]{:S(2)}) %collective-permute-start.15) | collective-permute-done | bytes 4128 | tf_op jit(solution)/shard_map/ppermute | solution.py:607
  78.8 2.0 %collective-permute-start.16 = (f32[16,128]{1,0:T(8,128)S(1)}, f32[16,128]{1,0:T(8,128)S(1)}, u32[]{:S(2)}, u32[]{:S(2)}) collective-permute-start(f32[16,128]{1,0:T(8,128)S(1)} %get-tuple-element.260), channel_id=1, source_target_pairs={{16,17},{17,16},{1,2},{2,1},{18,19},{19,18},{3,4},{4,3},{20,21},{2... | collective-permute-start | bytes 24584 | tf_op jit(solution)/shard_map/ppermute | solution.py:604
  81.3 3.6 %collective-permute-done.17.got_a = f32[8,128]{1,0:T(8,128)S(1)} collective-permute-done((f32[8,128]{1,0:T(8,128)S(1)}, f32[8,128]{1,0:T(8,128)S(1)}, u32[]{:S(2)}, u32[]{:S(2)}) %collective-permute-start.17) | collective-permute-done | bytes 4128 | tf_op jit(solution)/shard_map/ppermute | solution.py:607
  85.8 3.3 %collective-permute-start.18 = (f32[16,128]{1,0:T(8,128)S(1)}, f32[16,128]{1,0:T(8,128)S(1)}, u32[]{:S(2)}, u32[]{:S(2)}) collective-permute-start(f32[16,128]{1,0:T(8,128)S(1)} %get-tuple-element.271), channel_id=1, source_target_pairs={{16,17},{17,16},{1,2},{2,1},{18,19},{19,18},{3,4},{4,3},{20,21},{2... | collective-permute-start | bytes 24584 | tf_op jit(solution)/shard_map/ppermute | solution.py:604
  89.5 3.6 %collective-permute-done.19.got_a = f32[8,128]{1,0:T(8,128)S(1)} collective-permute-done((f32[8,128]{1,0:T(8,128)S(1)}, f32[8,128]{1,0:T(8,128)S(1)}, u32[]{:S(2)}, u32[]{:S(2)}) %collective-permute-start.19) | collective-permute-done | bytes 4128 | tf_op jit(solution)/shard_map/ppermute | solution.py:607
  94.0 2.2 %collective-permute-start.20 = (f32[16,128]{1,0:T(8,128)S(1)}, f32[16,128]{1,0:T(8,128)S(1)}, u32[]{:S(2)}, u32[]{:S(2)}) collective-permute-start(f32[16,128]{1,0:T(8,128)S(1)} %get-tuple-element.283), channel_id=1, source_target_pairs={{16,17},{17,16},{1,2},{2,1},{18,19},{19,18},{3,4},{4,3},{20,21},{2... | collective-permute-start | bytes 24584 | tf_op jit(solution)/shard_map/ppermute | solution.py:604
  96.6 3.6 %collective-permute-done.21.got_a = f32[8,128]{1,0:T(8,128)S(1)} collective-permute-done((f32[8,128]{1,0:T(8,128)S(1)}, f32[8,128]{1,0:T(8,128)S(1)}, u32[]{:S(2)}, u32[]{:S(2)}) %collective-permute-start.21) | collective-permute-done | bytes 4128 | tf_op jit(solution)/shard_map/ppermute | solution.py:607
  101.2 3.3 %collective-permute-start.22 = (f32[16,128]{1,0:T(8,128)S(1)}, f32[16,128]{1,0:T(8,128)S(1)}, u32[]{:S(2)}, u32[]{:S(2)}) collective-permute-start(f32[16,128]{1,0:T(8,128)S(1)} %get-tuple-element.291), channel_id=1, source_target_pairs={{16,17},{17,16},{1,2},{2,1},{18,19},{19,18},{3,4},{4,3},{20,21},{2... | collective-permute-start | bytes 24584 | tf_op jit(solution)/shard_map/ppermute | solution.py:604
  104.8 3.6 %collective-permute-done.23.got_a = f32[8,128]{1,0:T(8,128)S(1)} collective-permute-done((f32[8,128]{1,0:T(8,128)S(1)}, f32[8,128]{1,0:T(8,128)S(1)}, u32[]{:S(2)}, u32[]{:S(2)}) %collective-permute-start.23) | collective-permute-done | bytes 4128 | tf_op jit(solution)/shard_map/ppermute | solution.py:607
  109.4 2.0 %collective-permute-start.24 = (f32[16,128]{1,0:T(8,128)S(1)}, f32[16,128]{1,0:T(8,128)S(1)}, u32[]{:S(2)}, u32[]{:S(2)}) collective-permute-start(f32[16,128]{1,0:T(8,128)S(1)} %get-tuple-element.302), channel_id=1, source_target_pairs={{16,17},{17,16},{1,2},{2,1},{18,19},{19,18},{3,4},{4,3},{20,21},{2... | collective-permute-start | bytes 24584 | tf_op jit(solution)/shard_map/ppermute | solution.py:604
  111.8 3.6 %collective-permute-done.25.got_a = f32[8,128]{1,0:T(8,128)S(1)} collective-permute-done((f32[8,128]{1,0:T(8,128)S(1)}, f32[8,128]{1,0:T(8,128)S(1)}, u32[]{:S(2)}, u32[]{:S(2)}) %collective-permute-start.25) | collective-permute-done | bytes 4128 | tf_op jit(solution)/shard_map/ppermute | solution.py:607
  116.3 3.3 %collective-permute-start.26 = (f32[16,128]{1,0:T(8,128)S(1)}, f32[16,128]{1,0:T(8,128)S(1)}, u32[]{:S(2)}, u32[]{:S(2)}) collective-permute-start(f32[16,128]{1,0:T(8,128)S(1)} %get-tuple-element.313), channel_id=1, source_target_pairs={{16,17},{17,16},{1,2},{2,1},{18,19},{19,18},{3,4},{4,3},{20,21},{2... | collective-permute-start | bytes 24584 | tf_op jit(solution)/shard_map/ppermute | solution.py:604
  120.0 3.6 %collective-permute-done.27.got_a = f32[8,128]{1,0:T(8,128)S(1)} collective-permute-done((f32[8,128]{1,0:T(8,128)S(1)}, f32[8,128]{1,0:T(8,128)S(1)}, u32[]{:S(2)}, u32[]{:S(2)}) %collective-permute-start.27) | collective-permute-done | bytes 4128 | tf_op jit(solution)/shard_map/ppermute | solution.py:607
  124.5 2.0 %collective-permute-start.28 = (f32[16,128]{1,0:T(8,128)S(1)}, f32[16,128]{1,0:T(8,128)S(1)}, u32[]{:S(2)}, u32[]{:S(2)}) collective-permute-start(f32[16,128]{1,0:T(8,128)S(1)} %get-tuple-element.325), channel_id=1, source_target_pairs={{16,17},{17,16},{1,2},{2,1},{18,19},{19,18},{3,4},{4,3},{20,21},{2... | collective-permute-start | bytes 24584 | tf_op jit(solution)/shard_map/ppermute | solution.py:604
  127.0 3.6 %collective-permute-done.29.got_a = f32[8,128]{1,0:T(8,128)S(1)} collective-permute-done((f32[8,128]{1,0:T(8,128)S(1)}, f32[8,128]{1,0:T(8,128)S(1)}, u32[]{:S(2)}, u32[]{:S(2)}) %collective-permute-start.29) | collective-permute-done | bytes 4128 | tf_op jit(solution)/shard_map/ppermute | solution.py:607
  131.5 3.3 %collective-permute-start.30 = (f32[16,128]{1,0:T(8,128)S(1)}, f32[16,128]{1,0:T(8,128)S(1)}, u32[]{:S(2)}, u32[]{:S(2)}) collective-permute-start(f32[16,128]{1,0:T(8,128)S(1)} %get-tuple-element.333), channel_id=1, source_target_pairs={{16,17},{17,16},{1,2},{2,1},{18,19},{19,18},{3,4},{4,3},{20,21},{2... | collective-permute-start | bytes 24584 | tf_op jit(solution)/shard_map/ppermute | solution.py:604
  135.2 3.6 %collective-permute-done.31.got_a = f32[8,128]{1,0:T(8,128)S(1)} collective-permute-done((f32[8,128]{1,0:T(8,128)S(1)}, f32[8,128]{1,0:T(8,128)S(1)}, u32[]{:S(2)}, u32[]{:S(2)}) %collective-permute-start.31) | collective-permute-done | bytes 4128 | tf_op jit(solution)/shard_map/ppermute | solution.py:607
  139.7 2.0 %collective-permute-start.32 = (f32[16,128]{1,0:T(8,128)S(1)}, f32[16,128]{1,0:T(8,128)S(1)}, u32[]{:S(2)}, u32[]{:S(2)}) collective-permute-start(f32[16,128]{1,0:T(8,128)S(1)} %get-tuple-element.344), channel_id=1, source_target_pairs={{16,17},{17,16},{1,2},{2,1},{18,19},{19,18},{3,4},{4,3},{20,21},{2... | collective-permute-start | bytes 24584 | tf_op jit(solution)/shard_map/ppermute | solution.py:604
  142.1 3.6 %collective-permute-done.33.got_a = f32[8,128]{1,0:T(8,128)S(1)} collective-permute-done((f32[8,128]{1,0:T(8,128)S(1)}, f32[8,128]{1,0:T(8,128)S(1)}, u32[]{:S(2)}, u32[]{:S(2)}) %collective-permute-start.33) | collective-permute-done | bytes 4128 | tf_op jit(solution)/shard_map/ppermute | solution.py:607
  146.7 3.3 %collective-permute-start.34 = (f32[16,128]{1,0:T(8,128)S(1)}, f32[16,128]{1,0:T(8,128)S(1)}, u32[]{:S(2)}, u32[]{:S(2)}) collective-permute-start(f32[16,128]{1,0:T(8,128)S(1)} %get-tuple-element.355), channel_id=1, source_target_pairs={{16,17},{17,16},{1,2},{2,1},{18,19},{19,18},{3,4},{4,3},{20,21},{2... | collective-permute-start | bytes 24584 | tf_op jit(solution)/shard_map/ppermute | solution.py:604
  150.3 3.6 %collective-permute-done.35.got_a = f32[8,128]{1,0:T(8,128)S(1)} collective-permute-done((f32[8,128]{1,0:T(8,128)S(1)}, f32[8,128]{1,0:T(8,128)S(1)}, u32[]{:S(2)}, u32[]{:S(2)}) %collective-permute-start.35) | collective-permute-done | bytes 4128 | tf_op jit(solution)/shard_map/ppermute | solution.py:607
  154.8 3.6 %collective-permute-done.36 = f32[4,2,2,128]{3,2,1,0:T(2,128)S(1)} collective-permute-done((f32[4,2,2,128]{3,2,1,0:T(2,128)S(1)}, f32[4,2,2,128]{3,2,1,0:T(2,128)S(1)}, u32[]{:S(2)}, u32[]{:S(2)}) %collective-permute-start.36) | collective-permute-done | bytes 8224 | tf_op jit(solution)/shard_map/ppermute | solution.py:611
  (100 shorter events, 23.4 us)
Async XLA Ops:
  2.1 7.0 %copy-start = (f32[1,1,16,4,512]{4,3,2,1,0:T(4,128)S(1)}, f32[1,1,16,4,512]{4,3,2,1,0:T(4,128)}, u32[]{:S(2)}) copy-start(f32[1,1,16,4,512]{4,3,2,1,0:T(4,128)} %param.14) | copy-start | bytes 393220
  2.1 7.0 %copy-start.2 = (s32[1,1,16,4]{2,3,1,0:T(4,128)S(1)}, s32[1,1,16,4]{2,3,1,0:T(4,128)}, u32[]{:S(2)}) copy-start(s32[1,1,16,4]{2,3,1,0:T(4,128)} %param.15) | copy-start | bytes 772
  2.1 28.1 %collective-permute-start.2 = (f32[12,128,128]{2,1,0:T(8,128)S(1)}, f32[12,128,128]{2,1,0:T(8,128)S(1)}, u32[]{:S(2)}, u32[]{:S(2)}) collective-permute-start(f32[12,128,128]{2,1,0:T(8,128)S(1)} %pack.4), channel_id=1, source_target_pairs={{0,16},{16,0},{1,17},{17,1},{2,18},{18,2},{3,19},{19,3},{4,20},{20... | collective-permute-start | bytes 2359304 | tf_op jit(solution)/shard_map/ppermute | solution.py:531
  6.3 24.0 %collective-permute-start.3 = (f32[6,128,128]{2,1,0:T(8,128)}, f32[6,128,128]{2,1,0:T(8,128)S(1)}, u32[]{:S(2)}, u32[]{:S(2)}) collective-permute-start(f32[6,128,128]{2,1,0:T(8,128)} %pack.5), channel_id=1, source_target_pairs={{0,16},{16,0},{1,17},{17,1},{2,18},{18,2},{3,19},{19,3},{4,20},{20... | collective-permute-start | bytes 1179656 | tf_op jit(solution)/shard_map/ppermute | solution.py:531
  9.1 0.6 copy-start.1
  10.5 11.8 %all-to-all-start = ((f32[16,1,2176]{2,1,0:T(1,128)}), f32[16,1,2176]{2,1,0:T(1,128)S(1)}, u32[]{:S(2)}, u32[]{:S(2)}) async-start(f32[16,1,2176]{2,1,0:T(1,128)} %by_target.1), calls=%async_computation | async-start | bytes 278528 | tf_op jit(solution)/shard_map/cond/branch_1_fun/all_to_all | solution.py:545
  16.8 8.6 %collective-permute-start.1 = (f32[2,128,128]{2,1,0:T(8,128)S(1)}, f32[2,128,128]{2,1,0:T(8,128)}, u32[]{:S(2)}, u32[]{:S(2)}) collective-permute-start(f32[2,128,128]{2,1,0:T(8,128)S(1)} %get-tuple-element.25), channel_id=1, source_target_pairs={{16,17},{17,16},{1,2},{2,1},{18,19},{19,18},{3,4},{4,3},{20,21},{2... | collective-permute-start | bytes 393224 | tf_op jit(solution)/shard_map/cond/branch_1_fun/ppermute | solution.py:535
  23.8 6.5 %collective-permute-start = (f32[24,128]{1,0:T(8,128)S(1)}, f32[24,128]{1,0:T(8,128)}, u32[]{:S(2)}, u32[]{:S(2)}) collective-permute-start(f32[24,128]{1,0:T(8,128)S(1)} %get-tuple-element.24), channel_id=1, source_target_pairs={{0,16},{16,0},{1,17},{17,1},{2,18},{18,2},{3,19},{19,3},{4,20},{20... | collective-permute-start | bytes 36872 | tf_op jit(solution)/shard_map/cond/branch_1_fun/ppermute | solution.py:556
  31.3 7.3 %collective-permute-start.4 = (f32[264,128]{1,0:T(8,128)S(1)}, f32[264,128]{1,0:T(8,128)S(1)}, u32[]{:S(2)}, u32[]{:S(2)}) collective-permute-start(f32[264,128]{1,0:T(8,128)S(1)} %get-tuple-element.201), channel_id=1, source_target_pairs={{16,17},{17,16},{1,2},{2,1},{18,19},{19,18},{3,4},{4,3},{20,21},{2... | collective-permute-start | bytes 405512 | tf_op jit(solution)/shard_map/ppermute | solution.py:585
  33.2 6.0 %collective-permute-start.5 = (f32[264,128]{1,0:T(8,128)S(1)}, f32[264,128]{1,0:T(8,128)S(1)}, u32[]{:S(2)}, u32[]{:S(2)}) collective-permute-start(f32[264,128]{1,0:T(8,128)S(1)} %get-tuple-element.203), channel_id=1, source_target_pairs={{0,16},{16,0},{1,17},{17,1},{2,18},{18,2},{3,19},{19,3},{4,20},{20... | collective-permute-start | bytes 405512 | tf_op jit(solution)/shard_map/ppermute | solution.py:586
  40.3 7.6 %collective-permute-start.6 = (f32[16,128]{1,0:T(8,128)S(1)}, f32[16,128]{1,0:T(8,128)S(1)}, u32[]{:S(2)}, u32[]{:S(2)}) collective-permute-start(f32[16,128]{1,0:T(8,128)S(1)} %get-tuple-element.207), channel_id=1, source_target_pairs={{16,17},{17,16},{1,2},{2,1},{18,19},{19,18},{3,4},{4,3},{20,21},{2... | collective-permute-start | bytes 24584 | tf_op jit(solution)/shard_map/ppermute | solution.py:604
  43.9 3.7 %collective-permute-start.7 = (f32[8,128]{1,0:T(8,128)S(1)}, f32[8,128]{1,0:T(8,128)S(1)}, u32[]{:S(2)}, u32[]{:S(2)}) collective-permute-start(f32[8,128]{1,0:T(8,128)S(1)} %get-tuple-element.212), channel_id=1, source_target_pairs={{0,16},{16,0},{1,17},{17,1},{2,18},{18,2},{3,19},{19,3},{4,20},{20... | collective-permute-start | bytes 12296 | tf_op jit(solution)/shard_map/ppermute | solution.py:607
  48.5 6.4 %collective-permute-start.8 = (f32[16,128]{1,0:T(8,128)S(1)}, f32[16,128]{1,0:T(8,128)S(1)}, u32[]{:S(2)}, u32[]{:S(2)}) collective-permute-start(f32[16,128]{1,0:T(8,128)S(1)} %get-tuple-element.218), channel_id=1, source_target_pairs={{16,17},{17,16},{1,2},{2,1},{18,19},{19,18},{3,4},{4,3},{20,21},{2... | collective-permute-start | bytes 24584 | tf_op jit(solution)/shard_map/ppermute | solution.py:604
  50.8 3.7 %collective-permute-start.9 = (f32[8,128]{1,0:T(8,128)S(1)}, f32[8,128]{1,0:T(8,128)S(1)}, u32[]{:S(2)}, u32[]{:S(2)}) collective-permute-start(f32[8,128]{1,0:T(8,128)S(1)} %get-tuple-element.223), channel_id=1, source_target_pairs={{0,16},{16,0},{1,17},{17,1},{2,18},{18,2},{3,19},{19,3},{4,20},{20... | collective-permute-start | bytes 12296 | tf_op jit(solution)/shard_map/ppermute | solution.py:607
  55.5 7.6 %collective-permute-start.10 = (f32[16,128]{1,0:T(8,128)S(1)}, f32[16,128]{1,0:T(8,128)S(1)}, u32[]{:S(2)}, u32[]{:S(2)}) collective-permute-start(f32[16,128]{1,0:T(8,128)S(1)} %get-tuple-element.229), channel_id=1, source_target_pairs={{16,17},{17,16},{1,2},{2,1},{18,19},{19,18},{3,4},{4,3},{20,21},{2... | collective-permute-start | bytes 24584 | tf_op jit(solution)/shard_map/ppermute | solution.py:604
  59.1 3.7 %collective-permute-start.11 = (f32[8,128]{1,0:T(8,128)S(1)}, f32[8,128]{1,0:T(8,128)S(1)}, u32[]{:S(2)}, u32[]{:S(2)}) collective-permute-start(f32[8,128]{1,0:T(8,128)S(1)} %get-tuple-element.234), channel_id=1, source_target_pairs={{0,16},{16,0},{1,17},{17,1},{2,18},{18,2},{3,19},{19,3},{4,20},{20... | collective-permute-start | bytes 12296 | tf_op jit(solution)/shard_map/ppermute | solution.py:607
  63.7 6.4 %collective-permute-start.12 = (f32[16,128]{1,0:T(8,128)S(1)}, f32[16,128]{1,0:T(8,128)S(1)}, u32[]{:S(2)}, u32[]{:S(2)}) collective-permute-start(f32[16,128]{1,0:T(8,128)S(1)} %get-tuple-element.241), channel_id=1, source_target_pairs={{16,17},{17,16},{1,2},{2,1},{18,19},{19,18},{3,4},{4,3},{20,21},{2... | collective-permute-start | bytes 24584 | tf_op jit(solution)/shard_map/ppermute | solution.py:604
  66.0 3.7 %collective-permute-start.13 = (f32[8,128]{1,0:T(8,128)S(1)}, f32[8,128]{1,0:T(8,128)S(1)}, u32[]{:S(2)}, u32[]{:S(2)}) collective-permute-start(f32[8,128]{1,0:T(8,128)S(1)} %get-tuple-element.245), channel_id=1, source_target_pairs={{0,16},{16,0},{1,17},{17,1},{2,18},{18,2},{3,19},{19,3},{4,20},{20... | collective-permute-start | bytes 12296 | tf_op jit(solution)/shard_map/ppermute | solution.py:607
  70.6 7.6 %collective-permute-start.14 = (f32[16,128]{1,0:T(8,128)S(1)}, f32[16,128]{1,0:T(8,128)S(1)}, u32[]{:S(2)}, u32[]{:S(2)}) collective-permute-start(f32[16,128]{1,0:T(8,128)S(1)} %get-tuple-element.249), channel_id=1, source_target_pairs={{16,17},{17,16},{1,2},{2,1},{18,19},{19,18},{3,4},{4,3},{20,21},{2... | collective-permute-start | bytes 24584 | tf_op jit(solution)/shard_map/ppermute | solution.py:604
  74.2 3.7 %collective-permute-start.15 = (f32[8,128]{1,0:T(8,128)S(1)}, f32[8,128]{1,0:T(8,128)S(1)}, u32[]{:S(2)}, u32[]{:S(2)}) collective-permute-start(f32[8,128]{1,0:T(8,128)S(1)} %get-tuple-element.254), channel_id=1, source_target_pairs={{0,16},{16,0},{1,17},{17,1},{2,18},{18,2},{3,19},{19,3},{4,20},{20... | collective-permute-start | bytes 12296 | tf_op jit(solution)/shard_map/ppermute | solution.py:607
  78.8 6.4 %collective-permute-start.16 = (f32[16,128]{1,0:T(8,128)S(1)}, f32[16,128]{1,0:T(8,128)S(1)}, u32[]{:S(2)}, u32[]{:S(2)}) collective-permute-start(f32[16,128]{1,0:T(8,128)S(1)} %get-tuple-element.260), channel_id=1, source_target_pairs={{16,17},{17,16},{1,2},{2,1},{18,19},{19,18},{3,4},{4,3},{20,21},{2... | collective-permute-start | bytes 24584 | tf_op jit(solution)/shard_map/ppermute | solution.py:604
  81.2 3.7 %collective-permute-start.17 = (f32[8,128]{1,0:T(8,128)S(1)}, f32[8,128]{1,0:T(8,128)S(1)}, u32[]{:S(2)}, u32[]{:S(2)}) collective-permute-start(f32[8,128]{1,0:T(8,128)S(1)} %get-tuple-element.265), channel_id=1, source_target_pairs={{0,16},{16,0},{1,17},{17,1},{2,18},{18,2},{3,19},{19,3},{4,20},{20... | collective-permute-start | bytes 12296 | tf_op jit(solution)/shard_map/ppermute | solution.py:607
  85.8 7.6 %collective-permute-start.18 = (f32[16,128]{1,0:T(8,128)S(1)}, f32[16,128]{1,0:T(8,128)S(1)}, u32[]{:S(2)}, u32[]{:S(2)}) collective-permute-start(f32[16,128]{1,0:T(8,128)S(1)} %get-tuple-element.271), channel_id=1, source_target_pairs={{16,17},{17,16},{1,2},{2,1},{18,19},{19,18},{3,4},{4,3},{20,21},{2... | collective-permute-start | bytes 24584 | tf_op jit(solution)/shard_map/ppermute | solution.py:604
  89.4 3.7 %collective-permute-start.19 = (f32[8,128]{1,0:T(8,128)S(1)}, f32[8,128]{1,0:T(8,128)S(1)}, u32[]{:S(2)}, u32[]{:S(2)}) collective-permute-start(f32[8,128]{1,0:T(8,128)S(1)} %get-tuple-element.276), channel_id=1, source_target_pairs={{0,16},{16,0},{1,17},{17,1},{2,18},{18,2},{3,19},{19,3},{4,20},{20... | collective-permute-start | bytes 12296 | tf_op jit(solution)/shard_map/ppermute | solution.py:607
  94.0 6.6 %collective-permute-start.20 = (f32[16,128]{1,0:T(8,128)S(1)}, f32[16,128]{1,0:T(8,128)S(1)}, u32[]{:S(2)}, u32[]{:S(2)}) collective-permute-start(f32[16,128]{1,0:T(8,128)S(1)} %get-tuple-element.283), channel_id=1, source_target_pairs={{16,17},{17,16},{1,2},{2,1},{18,19},{19,18},{3,4},{4,3},{20,21},{2... | collective-permute-start | bytes 24584 | tf_op jit(solution)/shard_map/ppermute | solution.py:604
  96.5 3.7 %collective-permute-start.21 = (f32[8,128]{1,0:T(8,128)S(1)}, f32[8,128]{1,0:T(8,128)S(1)}, u32[]{:S(2)}, u32[]{:S(2)}) collective-permute-start(f32[8,128]{1,0:T(8,128)S(1)} %get-tuple-element.287), channel_id=1, source_target_pairs={{0,16},{16,0},{1,17},{17,1},{2,18},{18,2},{3,19},{19,3},{4,20},{20... | collective-permute-start | bytes 12296 | tf_op jit(solution)/shard_map/ppermute | solution.py:607
  101.2 7.6 %collective-permute-start.22 = (f32[16,128]{1,0:T(8,128)S(1)}, f32[16,128]{1,0:T(8,128)S(1)}, u32[]{:S(2)}, u32[]{:S(2)}) collective-permute-start(f32[16,128]{1,0:T(8,128)S(1)} %get-tuple-element.291), channel_id=1, source_target_pairs={{16,17},{17,16},{1,2},{2,1},{18,19},{19,18},{3,4},{4,3},{20,21},{2... | collective-permute-start | bytes 24584 | tf_op jit(solution)/shard_map/ppermute | solution.py:604
  104.7 3.7 %collective-permute-start.23 = (f32[8,128]{1,0:T(8,128)S(1)}, f32[8,128]{1,0:T(8,128)S(1)}, u32[]{:S(2)}, u32[]{:S(2)}) collective-permute-start(f32[8,128]{1,0:T(8,128)S(1)} %get-tuple-element.296), channel_id=1, source_target_pairs={{0,16},{16,0},{1,17},{17,1},{2,18},{18,2},{3,19},{19,3},{4,20},{20... | collective-permute-start | bytes 12296 | tf_op jit(solution)/shard_map/ppermute | solution.py:607
  109.4 6.4 %collective-permute-start.24 = (f32[16,128]{1,0:T(8,128)S(1)}, f32[16,128]{1,0:T(8,128)S(1)}, u32[]{:S(2)}, u32[]{:S(2)}) collective-permute-start(f32[16,128]{1,0:T(8,128)S(1)} %get-tuple-element.302), channel_id=1, source_target_pairs={{16,17},{17,16},{1,2},{2,1},{18,19},{19,18},{3,4},{4,3},{20,21},{2... | collective-permute-start | bytes 24584 | tf_op jit(solution)/shard_map/ppermute | solution.py:604
  111.7 3.7 %collective-permute-start.25 = (f32[8,128]{1,0:T(8,128)S(1)}, f32[8,128]{1,0:T(8,128)S(1)}, u32[]{:S(2)}, u32[]{:S(2)}) collective-permute-start(f32[8,128]{1,0:T(8,128)S(1)} %get-tuple-element.307), channel_id=1, source_target_pairs={{0,16},{16,0},{1,17},{17,1},{2,18},{18,2},{3,19},{19,3},{4,20},{20... | collective-permute-start | bytes 12296 | tf_op jit(solution)/shard_map/ppermute | solution.py:607
  116.3 7.6 %collective-permute-start.26 = (f32[16,128]{1,0:T(8,128)S(1)}, f32[16,128]{1,0:T(8,128)S(1)}, u32[]{:S(2)}, u32[]{:S(2)}) collective-permute-start(f32[16,128]{1,0:T(8,128)S(1)} %get-tuple-element.313), channel_id=1, source_target_pairs={{16,17},{17,16},{1,2},{2,1},{18,19},{19,18},{3,4},{4,3},{20,21},{2... | collective-permute-start | bytes 24584 | tf_op jit(solution)/shard_map/ppermute | solution.py:604
  119.9 3.7 %collective-permute-start.27 = (f32[8,128]{1,0:T(8,128)S(1)}, f32[8,128]{1,0:T(8,128)S(1)}, u32[]{:S(2)}, u32[]{:S(2)}) collective-permute-start(f32[8,128]{1,0:T(8,128)S(1)} %get-tuple-element.318), channel_id=1, source_target_pairs={{0,16},{16,0},{1,17},{17,1},{2,18},{18,2},{3,19},{19,3},{4,20},{20... | collective-permute-start | bytes 12296 | tf_op jit(solution)/shard_map/ppermute | solution.py:607
  124.5 6.4 %collective-permute-start.28 = (f32[16,128]{1,0:T(8,128)S(1)}, f32[16,128]{1,0:T(8,128)S(1)}, u32[]{:S(2)}, u32[]{:S(2)}) collective-permute-start(f32[16,128]{1,0:T(8,128)S(1)} %get-tuple-element.325), channel_id=1, source_target_pairs={{16,17},{17,16},{1,2},{2,1},{18,19},{19,18},{3,4},{4,3},{20,21},{2... | collective-permute-start | bytes 24584 | tf_op jit(solution)/shard_map/ppermute | solution.py:604
  126.9 3.7 %collective-permute-start.29 = (f32[8,128]{1,0:T(8,128)S(1)}, f32[8,128]{1,0:T(8,128)S(1)}, u32[]{:S(2)}, u32[]{:S(2)}) collective-permute-start(f32[8,128]{1,0:T(8,128)S(1)} %get-tuple-element.329), channel_id=1, source_target_pairs={{0,16},{16,0},{1,17},{17,1},{2,18},{18,2},{3,19},{19,3},{4,20},{20... | collective-permute-start | bytes 12296 | tf_op jit(solution)/shard_map/ppermute | solution.py:607
  131.5 7.6 %collective-permute-start.30 = (f32[16,128]{1,0:T(8,128)S(1)}, f32[16,128]{1,0:T(8,128)S(1)}, u32[]{:S(2)}, u32[]{:S(2)}) collective-permute-start(f32[16,128]{1,0:T(8,128)S(1)} %get-tuple-element.333), channel_id=1, source_target_pairs={{16,17},{17,16},{1,2},{2,1},{18,19},{19,18},{3,4},{4,3},{20,21},{2... | collective-permute-start | bytes 24584 | tf_op jit(solution)/shard_map/ppermute | solution.py:604
  135.1 3.7 %collective-permute-start.31 = (f32[8,128]{1,0:T(8,128)S(1)}, f32[8,128]{1,0:T(8,128)S(1)}, u32[]{:S(2)}, u32[]{:S(2)}) collective-permute-start(f32[8,128]{1,0:T(8,128)S(1)} %get-tuple-element.338), channel_id=1, source_target_pairs={{0,16},{16,0},{1,17},{17,1},{2,18},{18,2},{3,19},{19,3},{4,20},{20... | collective-permute-start | bytes 12296 | tf_op jit(solution)/shard_map/ppermute | solution.py:607
  139.7 6.4 %collective-permute-start.32 = (f32[16,128]{1,0:T(8,128)S(1)}, f32[16,128]{1,0:T(8,128)S(1)}, u32[]{:S(2)}, u32[]{:S(2)}) collective-permute-start(f32[16,128]{1,0:T(8,128)S(1)} %get-tuple-element.344), channel_id=1, source_target_pairs={{16,17},{17,16},{1,2},{2,1},{18,19},{19,18},{3,4},{4,3},{20,21},{2... | collective-permute-start | bytes 24584 | tf_op jit(solution)/shard_map/ppermute | solution.py:604
  142.0 3.7 %collective-permute-start.33 = (f32[8,128]{1,0:T(8,128)S(1)}, f32[8,128]{1,0:T(8,128)S(1)}, u32[]{:S(2)}, u32[]{:S(2)}) collective-permute-start(f32[8,128]{1,0:T(8,128)S(1)} %get-tuple-element.349), channel_id=1, source_target_pairs={{0,16},{16,0},{1,17},{17,1},{2,18},{18,2},{3,19},{19,3},{4,20},{20... | collective-permute-start | bytes 12296 | tf_op jit(solution)/shard_map/ppermute | solution.py:607
  146.7 7.6 %collective-permute-start.34 = (f32[16,128]{1,0:T(8,128)S(1)}, f32[16,128]{1,0:T(8,128)S(1)}, u32[]{:S(2)}, u32[]{:S(2)}) collective-permute-start(f32[16,128]{1,0:T(8,128)S(1)} %get-tuple-element.355), channel_id=1, source_target_pairs={{16,17},{17,16},{1,2},{2,1},{18,19},{19,18},{3,4},{4,3},{20,21},{2... | collective-permute-start | bytes 24584 | tf_op jit(solution)/shard_map/ppermute | solution.py:604
  150.2 3.7 %collective-permute-start.35 = (f32[8,128]{1,0:T(8,128)S(1)}, f32[8,128]{1,0:T(8,128)S(1)}, u32[]{:S(2)}, u32[]{:S(2)}) collective-permute-start(f32[8,128]{1,0:T(8,128)S(1)} %get-tuple-element.360), channel_id=1, source_target_pairs={{0,16},{16,0},{1,17},{17,1},{2,18},{18,2},{3,19},{19,3},{4,20},{20... | collective-permute-start | bytes 12296 | tf_op jit(solution)/shard_map/ppermute | solution.py:607
  154.8 3.7 %collective-permute-start.36 = (f32[4,2,2,128]{3,2,1,0:T(2,128)S(1)}, f32[4,2,2,128]{3,2,1,0:T(2,128)S(1)}, u32[]{:S(2)}, u32[]{:S(2)}) collective-permute-start(f32[4,2,2,128]{3,2,1,0:T(2,128)S(1)} %rev.12), channel_id=1, source_target_pairs={{0,16},{16,0},{1,17},{17,1},{2,18},{18,2},{3,19},{19,3},{4,20},{20... | collective-permute-start | bytes 24584 | tf_op jit(solution)/shard_map/ppermute | solution.py:611

commit v13 on v12

--- a/solution.py
+++ b/solution.py
@@ -386,22 +386,6 @@
     ])
 
 
-def response_kernel(keep, recv_0, recv_1, beyond_0, first_a, first_b, small, out):
-    out[...] = responses(((keep,), (recv_0, recv_1)), beyond_0, first_a, first_b, small_part(small, INITIAL))
-
-
-def to_a_kernel(factor, keep, recv_0, recv_1, beyond_0, first_a, first_b, f_ref, q_ref, base, response_out, q_out, msg_a):
-    halves = ((keep,), (recv_0, recv_1))
-    f, q = f_ref[...], q_ref[...]
-    q = stacked([
-        matvec([(block, row_of(f, *at)) for block, at in tile_terms(halves, j, b)]) if b == 1 else row_of(q, j, b)
-        for j, b in TILES
-    ])
-    q_out[...] = q
-    msg_a[...] = message(f, base[...] - factor * q, 1)
-    response_out[...] = responses(halves, beyond_0, first_a, first_b, f)
-
-
 def advance(instant, pair, small, product, f, residue):
     if pair == 0:
         residue = small_part(small, instant) - product
@@ -416,12 +400,13 @@
     return terms[:-1], terms[-1:]
 
 
-def beside_kernel(instant, pair, keep, recv_0, recv_1, small, got_a, response_ref, q_ref, *refs):
+def beside_kernel(instant, pair, keep, recv_0, recv_1, beyond_0, first_a, first_b, small, got_a, q_ref, *refs):
     halves = ((keep,), (recv_0, recv_1))
-    product_out, part_out = refs[-2:]
+    response_out, product_out, part_out = refs[-3:]
     f = small_part(small, INITIAL) if instant == pair == 0 else refs[0][...]
     residue = None if pair == 0 else refs[1][...]
-    q, response = q_ref[...], response_ref[...]
+    q, response = q_ref[...], responses(halves, beyond_0, first_a, first_b, f)
+    response_out[...] = response
     product = stacked([
         row_of(q, j, b) + matvec([(halo_block(halves, j, b), got_a[j:j + 1, :])]) if b == 1 else row_of(q, j, b)
         for j, b in TILES
@@ -479,17 +464,13 @@
     f_out[...] = f3
     if last:
         return
-    zero = jnp.zeros_like(f3[:1])
-    q = stacked([
-        matvec([(block, row_of(f3, *at)) for block, at in tile_terms(halves, j, b)]) if b == 0 else zero for j, b in TILES
-    ])
+    q = inner_product(f3, halves)
     upcoming = small_part(small, instant + 1) if closing else None
     base, factor = ahead(closing, sweep + 1, f3, residue, capacity, upcoming)
-    q_out, base_out, msg_b = refs[:3]
+    g = base - factor * q
+    q_out, msg_a, msg_b = refs[:3]
     q_out[...] = q
-    base_out[...] = base
-    to_b = message(f3, base - factor * q, 0)
-    msg_b[...] = stacked([to_b, jnp.zeros_like(to_b)])
+    msg_a[...], msg_b[...] = message(f3, g, 1), message(f3, g, 0)
     if not closing:
         refs[3][...] = residue
         refs[4][...] = estimate
@@ -582,29 +563,22 @@
     first_shape = jax.ShapeDtypeStruct((2 * N + ROWS * width, width), jnp.float32)
     unit_small = jax.ShapeDtypeStruct(((STEPS + 2) * N * HALF, width), jnp.float32)
     msg_a, msg_b, q, small = call(start_kernel, (first_shape, first_shape, shape, unit_small), 28, *halves, *small)
-    got_b = first_b = lax.ppermute(msg_b, both, b_pairs)
-    got_a = first_a = lax.ppermute(msg_a, "row", swap)
-    blocks = (*halves, beyond_0, first_a, first_b)
-    (response,) = call(response_kernel, (shape,), 8, *blocks, small)
-    b_shape = jax.ShapeDtypeStruct((4 * N, width), jnp.float32)
-    field, state, frames = (), (), []
+    field, state, frames, first = (), (), [], None
     for instant in range(STEPS):
         for pair in range(ITERS // 2):
             closing = pair + 1 == ITERS // 2
             last = closing and instant + 1 == STEPS
-            product, part = call(functools.partial(beside_kernel, instant, pair), (shape,) * 2, 22,
-                                 *halves, small, got_a, response, q, *field, *state[:1])
-            out = call(functools.partial(pair_kernel, instant, pair, last), (shape,) if last else (shape,) * 3 + (b_shape,) + (shape,) * (0 if closing else 2),
-                       36, *halves, small, got_b, response, product, part, *field, *state)
+            got_b = lax.ppermute(msg_b, both, b_pairs)
+            got_a = lax.ppermute(msg_a, "row", swap)
+            first = first or (got_a, got_b)
+            response, product, part = call(functools.partial(beside_kernel, instant, pair), (shape,) * 3, 30,
+                                           *halves, beyond_0, *first, small, got_a, q, *field, *state[:1])
+            out = call(functools.partial(pair_kernel, instant, pair, last), (shape,) * (1 if last else 4 if closing else 6),
+                       50, *halves, small, got_b, response, product, part, *field, *state)
             field = out[:1]
-            if last:
-                break
-            q, base, msg_b = out[1:4]
-            state = out[4:]
-            got_b = lax.ppermute(msg_b, both, b_pairs)
-            factor = 1.0 if closing else STRIDES[2 * pair + 1]
-            response, q, msg_a = call(functools.partial(to_a_kernel, factor), (shape,) * 3, 22, *blocks, *field, q, base)
-            got_a = lax.ppermute(msg_a, "row", swap)
+            if not last:
+                q, msg_a, msg_b = out[1:4]
+                state = out[4:]
         frames.append(field[0])
 
     done = jnp.stack(frames).reshape(STEPS, N, HALF, width)

time: 161 us -> 145 us (0.901)
  waiting for transfers between devices: 68 us -> 58.9 us
  starting transfers between devices: 58.7 us -> 54.3 us
    ppermute x15 -> x16, waiting for transfers between devices: 53.5 us -> 18 us  [shards_chain(): got_a = lax.ppermute(msg_a, 'row', swap)]
    ppermute x15 -> x16, waiting for transfers between devices: 0.04 us -> 30.8 us  [shards_chain(): got_b = lax.ppermute(msg_b, both, b_pairs)]
    ppermute x2 -> x0, waiting for transfers between devices: 4.37 us -> none  [the longest x1 3.82 us: shards_chain(): got_b = first_b = lax.ppermute(msg_b, both, b_pairs)]
    ppermute x15 -> x16, starting transfers between devices: 40.6 us -> 37 us  [shards_chain(): got_b = lax.ppermute(msg_b, both, b_pairs)]
    ppermute x2 -> x0, starting transfers between devices: 3.51 us -> none  [the longest x1 1.92 us: shards_chain(): got_b = first_b = lax.ppermute(msg_b, both, b_pairs)]
    ppermute x15 -> x16, starting transfers between devices: 1.46 us -> 4.26 us  [shards_chain(): got_a = lax.ppermute(msg_a, 'row', swap)]
    pallas_call x49 -> x33, Pallas kernels: 20.3 us -> 18.8 us  [call(): pl.pallas_call(body, out_shape=outs, in_specs=[vmem] * len(ins), out_spec...]
  transfers between devices with their start and end apart: 38 -> 38, of which waited for: 20 -> 34; matrix products, arithmetic and copies ran while one was open for 1% -> 1% of each run, Pallas kernels for 11% -> 10%
where the time goes in v13:
time: 145 us; the launch traced here: 144 us
  waiting for transfers between devices  58.9 us (41%)
  starting transfers between devices  54.3 us (37%)
  Pallas kernels  27.8 us (19%)
  local copies, waits for them, and re-layouts  1.62 us (1%)
    ppermute x16, starting transfers between devices, shards_chain(): got_b = lax.ppermute(msg_b, both, b_pairs)  37 us
    ppermute x16, waiting for transfers between devices, shards_chain(): got_b = lax.ppermute(msg_b, both, b_pairs)  30.8 us
    pallas_call x33, Pallas kernels, call(): pl.pallas_call(body, out_shape=outs, in_specs=[vmem] * len(ins), out_spec...  18.8 us
    ppermute x16, waiting for transfers between devices, shards_chain(): got_a = lax.ppermute(msg_a, 'row', swap)  18 us
    pallas_call x3, Pallas kernels, pack(): pl.pallas_call(functools.partial(pack_kernel, n_col, sent, first, count),...  6.85 us
    all_to_all x1, starting transfers between devices, beside(): lax.all_to_all(by_target, 'col', split_axis=0, concat_axis=0, tiled=True)  6.27 us
    ppermute x16, starting transfers between devices, shards_chain(): got_a = lax.ppermute(msg_a, 'row', swap)  4.26 us
    ppermute x1, waiting for transfers between devices, beside(): return (small, lax.ppermute(send, 'row', swap), beyond_0)  4.02 us
  transfers between devices with their start and end apart: 38, of which 34 were waited for; matrix products, arithmetic and copies ran while one was open for 1% of the time, Pallas kernels for 10%

profile of v13, /device:TPU:8, one launch (start us, length us, event | category | flops | bytes accessed | tf_op | source)
XLA Modules:
  0.0 143.9 jit_solution(13307646299311831869)
XLA Ops:
  0.1 2.0 %pack.4 = f32[12,128,128]{2,1,0:T(8,128)S(1)} custom-call(s32[2]{0:T(128)S(1)} %pad_add_fusion.place_ref, s32[2,4,4]{2,1,0:T(4,128)} %pattern_ref.5, f32[2,4,128,128]{3,2,1,0:T(8,128)} %own_hbm.5, f32[4,2,4,128,128]{4,3,2,1,0:T(8,128)} %nb_hbm.5), custom_call_target="tpu_custom_call" | custom-call | tf_op jit(solution)/shard_map/pack/pallas_call | solution.py:499
  2.1 1.6 %collective-permute-start.2 = (f32[12,128,128]{2,1,0:T(8,128)S(1)}, f32[12,128,128]{2,1,0:T(8,128)S(1)}, u32[]{:S(2)}, u32[]{:S(2)}) collective-permute-start(f32[12,128,128]{2,1,0:T(8,128)S(1)} %pack.4), channel_id=1, source_target_pairs={{0,16},{16,0},{1,17},{17,1},{2,18},{18,2},{3,19},{19,3},{4,20},{20... | collective-permute-start | bytes 2359304 | tf_op jit(solution)/shard_map/ppermute | solution.py:512
  3.7 2.6 %pack.5 = f32[6,128,128]{2,1,0:T(8,128)} custom-call(s32[2]{0:T(128)S(1)} %pad_add_fusion.place_ref, s32[2,4,4]{2,1,0:T(4,128)} %pattern_ref.5, f32[2,4,128,128]{3,2,1,0:T(8,128)} %own_hbm.5, f32[4,2,4,128,128]{4,3,2,1,0:T(8,128)} %nb_hbm.5), custom_call_target="tpu_custom_call" | custom-call | tf_op jit(solution)/shard_map/pack/pallas_call | solution.py:499
  6.9 2.3 %pack.3 = (f32[20,128,128]{2,1,0:T(8,128)S(1)}, f32[2,128,128]{2,1,0:T(8,128)S(1)}) custom-call(s32[2]{0:T(128)S(1)} %pad_add_fusion.place_ref, s32[2,4,4]{2,1,0:T(4,128)} %pattern_ref.5, f32[2,4,128,128]{3,2,1,0:T(8,128)} %own_hbm.5, f32[4,2,4,128,128]{4,3,2,1,0:T(8,128)} %nb_hbm.5), custom_call_target="tpu_custom_call" | custom-call | tf_op jit(solution)/shard_map/pack/pallas_call | solution.py:499
  9.2 21.1 %conditional.1 = (f32[24,128]{1,0:T(8,128)}, f32[24,128]{1,0:T(8,128)}, f32[2,128,128]{2,1,0:T(8,128)S(1)}) conditional(s32[]{:T(128)} %convert_element_type.3, f32[2,128,128]{2,1,0:T(8,128)S(1)} %get-tuple-element.168, (f32[1,1,16,4,512]{4,3,2,1,0:T(4,128)S(1)}, s32[1,1,16,4]{2,3,1,0:T(4,128)S(1)}, s32[2]{0:T(128)S(1)}, f32[2,4,128]{2,1,0:T(4,128)}, ...), branch_computations={%region_0.1_spmd, %region_1.2_spmd} | conditional | bytes 1532612 | solution.py:539
  10.5 6.3 %all-to-all-start = ((f32[16,1,2176]{2,1,0:T(1,128)}), f32[16,1,2176]{2,1,0:T(1,128)S(1)}, u32[]{:S(2)}, u32[]{:S(2)}) async-start(f32[16,1,2176]{2,1,0:T(1,128)} %by_target.1), calls=%async_computation | async-start | bytes 278528 | tf_op jit(solution)/shard_map/cond/branch_1_fun/all_to_all | solution.py:526
  16.8 3.1 %collective-permute-start.1 = (f32[2,128,128]{2,1,0:T(8,128)S(1)}, f32[2,128,128]{2,1,0:T(8,128)}, u32[]{:S(2)}, u32[]{:S(2)}) collective-permute-start(f32[2,128,128]{2,1,0:T(8,128)S(1)} %get-tuple-element.25), channel_id=1, source_target_pairs={{16,17},{17,16},{1,2},{2,1},{18,19},{19,18},{3,4},{4,3},{20,21},{2... | collective-permute-start | bytes 393224 | tf_op jit(solution)/shard_map/cond/branch_1_fun/ppermute | solution.py:516
  19.9 2.4 %all-to-all-done = f32[16,1,2176]{2,1,0:T(1,128)S(1)} async-done(((f32[16,1,2176]{2,1,0:T(1,128)}), f32[16,1,2176]{2,1,0:T(1,128)S(1)}, u32[]{:S(2)}, u32[]{:S(2)}) %all-to-all-start) | async-done | bytes 139296 | tf_op jit(solution)/shard_map/cond/branch_1_fun/all_to_all | solution.py:526
  22.3 1.5 %small.1 = (f32[24,128]{1,0:T(8,128)}, f32[24,128]{1,0:T(8,128)S(1)}) custom-call(s32[2]{0:T(128)} %copy-done.1, f32[16,2176]{1,0:T(8,128)S(1)} %bitcast.11, f32[2,4,128]{2,1,0:T(4,128)} %get-tuple-element.314.capacity, f32[2,4,128]{2,1,0:T(4,128)} %get-tuple-element.315.initial), custom_call_target="tpu_custom_call" | custom-call | tf_op jit(solution)/shard_map/cond/branch_1_fun/small/pallas_call | solution.py:528
  23.8 1.5 %collective-permute-start = (f32[24,128]{1,0:T(8,128)S(1)}, f32[24,128]{1,0:T(8,128)}, u32[]{:S(2)}, u32[]{:S(2)}) collective-permute-start(f32[24,128]{1,0:T(8,128)S(1)} %get-tuple-element.24), channel_id=1, source_target_pairs={{0,16},{16,0},{1,17},{17,1},{2,18},{18,2},{3,19},{19,3},{4,20},{20... | collective-permute-start | bytes 36872 | tf_op jit(solution)/shard_map/cond/branch_1_fun/ppermute | solution.py:537
  26.3 4.0 %collective-permute-done = f32[24,128]{1,0:T(8,128)} collective-permute-done((f32[24,128]{1,0:T(8,128)S(1)}, f32[24,128]{1,0:T(8,128)}, u32[]{:S(2)}, u32[]{:S(2)}) %collective-permute-start) | collective-permute-done | bytes 12320 | tf_op jit(solution)/shard_map/cond/branch_1_fun/ppermute | solution.py:537
  31.3 1.9 %collective-permute-start.4 = (f32[264,128]{1,0:T(8,128)S(1)}, f32[264,128]{1,0:T(8,128)S(1)}, u32[]{:S(2)}, u32[]{:S(2)}) collective-permute-start(f32[264,128]{1,0:T(8,128)S(1)} %get-tuple-element.172), channel_id=1, source_target_pairs={{16,17},{17,16},{1,2},{2,1},{18,19},{19,18},{3,4},{4,3},{20,21},{2... | collective-permute-start | bytes 405512 | tf_op jit(solution)/shard_map/ppermute | solution.py:571
  33.2 1.6 %collective-permute-start.5 = (f32[264,128]{1,0:T(8,128)S(1)}, f32[264,128]{1,0:T(8,128)S(1)}, u32[]{:S(2)}, u32[]{:S(2)}) collective-permute-start(f32[264,128]{1,0:T(8,128)S(1)} %get-tuple-element.174), channel_id=1, source_target_pairs={{0,16},{16,0},{1,17},{17,1},{2,18},{18,2},{3,19},{19,3},{4,20},{20... | collective-permute-start | bytes 405512 | tf_op jit(solution)/shard_map/ppermute | solution.py:572
  34.8 3.8 %collective-permute-done.4.first_b.got_b = f32[264,128]{1,0:T(8,128)S(1)} collective-permute-done((f32[264,128]{1,0:T(8,128)S(1)}, f32[264,128]{1,0:T(8,128)S(1)}, u32[]{:S(2)}, u32[]{:S(2)}) %collective-permute-start.4) | collective-permute-done | bytes 135200 | tf_op jit(solution)/shard_map/ppermute | solution.py:571
  40.3 1.7 %collective-permute-start.7 = (f32[8,128]{1,0:T(8,128)S(1)}, f32[8,128]{1,0:T(8,128)S(1)}, u32[]{:S(2)}, u32[]{:S(2)}) collective-permute-start(f32[8,128]{1,0:T(8,128)S(1)} %get-tuple-element.180), channel_id=1, source_target_pairs={{0,16},{16,0},{1,17},{17,1},{2,18},{18,2},{3,19},{19,3},{4,20},{20... | collective-permute-start | bytes 12296 | tf_op jit(solution)/shard_map/ppermute | solution.py:572
  42.0 2.3 %collective-permute-start.6 = (f32[8,128]{1,0:T(8,128)S(1)}, f32[8,128]{1,0:T(8,128)S(1)}, u32[]{:S(2)}, u32[]{:S(2)}) collective-permute-start(f32[8,128]{1,0:T(8,128)S(1)} %get-tuple-element.179), channel_id=1, source_target_pairs={{16,17},{17,16},{1,2},{2,1},{18,19},{19,18},{3,4},{4,3},{20,21},{2... | collective-permute-start | bytes 12296 | tf_op jit(solution)/shard_map/ppermute | solution.py:571
  44.8 3.0 %collective-permute-done.6.got_b = f32[8,128]{1,0:T(8,128)S(1)} collective-permute-done((f32[8,128]{1,0:T(8,128)S(1)}, f32[8,128]{1,0:T(8,128)S(1)}, u32[]{:S(2)}, u32[]{:S(2)}) %collective-permute-start.6) | collective-permute-done | bytes 4128 | tf_op jit(solution)/shard_map/ppermute | solution.py:571
  48.5 2.3 %collective-permute-start.8 = (f32[8,128]{1,0:T(8,128)S(1)}, f32[8,128]{1,0:T(8,128)S(1)}, u32[]{:S(2)}, u32[]{:S(2)}) collective-permute-start(f32[8,128]{1,0:T(8,128)S(1)} %get-tuple-element.188), channel_id=1, source_target_pairs={{16,17},{17,16},{1,2},{2,1},{18,19},{19,18},{3,4},{4,3},{20,21},{2... | collective-permute-start | bytes 12296 | tf_op jit(solution)/shard_map/ppermute | solution.py:571
  50.8 1.3 collective-permute-done.9.got_a
  52.6 1.7 %collective-permute-done.8.got_b = f32[8,128]{1,0:T(8,128)S(1)} collective-permute-done((f32[8,128]{1,0:T(8,128)S(1)}, f32[8,128]{1,0:T(8,128)S(1)}, u32[]{:S(2)}, u32[]{:S(2)}) %collective-permute-start.8) | collective-permute-done | bytes 4128 | tf_op jit(solution)/shard_map/ppermute | solution.py:571
  55.0 2.3 %collective-permute-start.10 = (f32[8,128]{1,0:T(8,128)S(1)}, f32[8,128]{1,0:T(8,128)S(1)}, u32[]{:S(2)}, u32[]{:S(2)}) collective-permute-start(f32[8,128]{1,0:T(8,128)S(1)} %get-tuple-element.197), channel_id=1, source_target_pairs={{16,17},{17,16},{1,2},{2,1},{18,19},{19,18},{3,4},{4,3},{20,21},{2... | collective-permute-start | bytes 12296 | tf_op jit(solution)/shard_map/ppermute | solution.py:571
  59.1 1.7 %collective-permute-done.10.got_b = f32[8,128]{1,0:T(8,128)S(1)} collective-permute-done((f32[8,128]{1,0:T(8,128)S(1)}, f32[8,128]{1,0:T(8,128)S(1)}, u32[]{:S(2)}, u32[]{:S(2)}) %collective-permute-start.10) | collective-permute-done | bytes 4128 | tf_op jit(solution)/shard_map/ppermute | solution.py:571
  61.5 2.3 %collective-permute-start.12 = (f32[8,128]{1,0:T(8,128)S(1)}, f32[8,128]{1,0:T(8,128)S(1)}, u32[]{:S(2)}, u32[]{:S(2)}) collective-permute-start(f32[8,128]{1,0:T(8,128)S(1)} %get-tuple-element.207), channel_id=1, source_target_pairs={{16,17},{17,16},{1,2},{2,1},{18,19},{19,18},{3,4},{4,3},{20,21},{2... | collective-permute-start | bytes 12296 | tf_op jit(solution)/shard_map/ppermute | solution.py:571
  65.6 1.7 %collective-permute-done.12.got_b = f32[8,128]{1,0:T(8,128)S(1)} collective-permute-done((f32[8,128]{1,0:T(8,128)S(1)}, f32[8,128]{1,0:T(8,128)S(1)}, u32[]{:S(2)}, u32[]{:S(2)}) %collective-permute-start.12) | collective-permute-done | bytes 4128 | tf_op jit(solution)/shard_map/ppermute | solution.py:571
  68.0 2.3 %collective-permute-start.14 = (f32[8,128]{1,0:T(8,128)S(1)}, f32[8,128]{1,0:T(8,128)S(1)}, u32[]{:S(2)}, u32[]{:S(2)}) collective-permute-start(f32[8,128]{1,0:T(8,128)S(1)} %get-tuple-element.213), channel_id=1, source_target_pairs={{16,17},{17,16},{1,2},{2,1},{18,19},{19,18},{3,4},{4,3},{20,21},{2... | collective-permute-start | bytes 12296 | tf_op jit(solution)/shard_map/ppermute | solution.py:571
  72.2 1.7 %collective-permute-done.14.got_b = f32[8,128]{1,0:T(8,128)S(1)} collective-permute-done((f32[8,128]{1,0:T(8,128)S(1)}, f32[8,128]{1,0:T(8,128)S(1)}, u32[]{:S(2)}, u32[]{:S(2)}) %collective-permute-start.14) | collective-permute-done | bytes 4128 | tf_op jit(solution)/shard_map/ppermute | solution.py:571
  74.6 2.3 %collective-permute-start.16 = (f32[8,128]{1,0:T(8,128)S(1)}, f32[8,128]{1,0:T(8,128)S(1)}, u32[]{:S(2)}, u32[]{:S(2)}) collective-permute-start(f32[8,128]{1,0:T(8,128)S(1)} %get-tuple-element.222), channel_id=1, source_target_pairs={{16,17},{17,16},{1,2},{2,1},{18,19},{19,18},{3,4},{4,3},{20,21},{2... | collective-permute-start | bytes 12296 | tf_op jit(solution)/shard_map/ppermute | solution.py:571
  78.7 1.7 %collective-permute-done.16.got_b = f32[8,128]{1,0:T(8,128)S(1)} collective-permute-done((f32[8,128]{1,0:T(8,128)S(1)}, f32[8,128]{1,0:T(8,128)S(1)}, u32[]{:S(2)}, u32[]{:S(2)}) %collective-permute-start.16) | collective-permute-done | bytes 4128 | tf_op jit(solution)/shard_map/ppermute | solution.py:571
  81.1 2.3 %collective-permute-start.18 = (f32[8,128]{1,0:T(8,128)S(1)}, f32[8,128]{1,0:T(8,128)S(1)}, u32[]{:S(2)}, u32[]{:S(2)}) collective-permute-start(f32[8,128]{1,0:T(8,128)S(1)} %get-tuple-element.231), channel_id=1, source_target_pairs={{16,17},{17,16},{1,2},{2,1},{18,19},{19,18},{3,4},{4,3},{20,21},{2... | collective-permute-start | bytes 12296 | tf_op jit(solution)/shard_map/ppermute | solution.py:571
  83.4 1.3 collective-permute-done.19.got_a
  85.2 1.7 %collective-permute-done.18.got_b = f32[8,128]{1,0:T(8,128)S(1)} collective-permute-done((f32[8,128]{1,0:T(8,128)S(1)}, f32[8,128]{1,0:T(8,128)S(1)}, u32[]{:S(2)}, u32[]{:S(2)}) %collective-permute-start.18) | collective-permute-done | bytes 4128 | tf_op jit(solution)/shard_map/ppermute | solution.py:571
  87.6 2.5 %collective-permute-start.20 = (f32[8,128]{1,0:T(8,128)S(1)}, f32[8,128]{1,0:T(8,128)S(1)}, u32[]{:S(2)}, u32[]{:S(2)}) collective-permute-start(f32[8,128]{1,0:T(8,128)S(1)} %get-tuple-element.241), channel_id=1, source_target_pairs={{16,17},{17,16},{1,2},{2,1},{18,19},{19,18},{3,4},{4,3},{20,21},{2... | collective-permute-start | bytes 12296 | tf_op jit(solution)/shard_map/ppermute | solution.py:571
  91.7 1.7 %collective-permute-done.20.got_b = f32[8,128]{1,0:T(8,128)S(1)} collective-permute-done((f32[8,128]{1,0:T(8,128)S(1)}, f32[8,128]{1,0:T(8,128)S(1)}, u32[]{:S(2)}, u32[]{:S(2)}) %collective-permute-start.20) | collective-permute-done | bytes 4128 | tf_op jit(solution)/shard_map/ppermute | solution.py:571
  94.1 2.3 %collective-permute-start.22 = (f32[8,128]{1,0:T(8,128)S(1)}, f32[8,128]{1,0:T(8,128)S(1)}, u32[]{:S(2)}, u32[]{:S(2)}) collective-permute-start(f32[8,128]{1,0:T(8,128)S(1)} %get-tuple-element.247), channel_id=1, source_target_pairs={{16,17},{17,16},{1,2},{2,1},{18,19},{19,18},{3,4},{4,3},{20,21},{2... | collective-permute-start | bytes 12296 | tf_op jit(solution)/shard_map/ppermute | solution.py:571
  98.2 1.7 %collective-permute-done.22.got_b = f32[8,128]{1,0:T(8,128)S(1)} collective-permute-done((f32[8,128]{1,0:T(8,128)S(1)}, f32[8,128]{1,0:T(8,128)S(1)}, u32[]{:S(2)}, u32[]{:S(2)}) %collective-permute-start.22) | collective-permute-done | bytes 4128 | tf_op jit(solution)/shard_map/ppermute | solution.py:571
  100.7 2.3 %collective-permute-start.24 = (f32[8,128]{1,0:T(8,128)S(1)}, f32[8,128]{1,0:T(8,128)S(1)}, u32[]{:S(2)}, u32[]{:S(2)}) collective-permute-start(f32[8,128]{1,0:T(8,128)S(1)} %get-tuple-element.256), channel_id=1, source_target_pairs={{16,17},{17,16},{1,2},{2,1},{18,19},{19,18},{3,4},{4,3},{20,21},{2... | collective-permute-start | bytes 12296 | tf_op jit(solution)/shard_map/ppermute | solution.py:571
  104.8 1.7 %collective-permute-done.24.got_b = f32[8,128]{1,0:T(8,128)S(1)} collective-permute-done((f32[8,128]{1,0:T(8,128)S(1)}, f32[8,128]{1,0:T(8,128)S(1)}, u32[]{:S(2)}, u32[]{:S(2)}) %collective-permute-start.24) | collective-permute-done | bytes 4128 | tf_op jit(solution)/shard_map/ppermute | solution.py:571
  107.2 2.3 %collective-permute-start.26 = (f32[8,128]{1,0:T(8,128)S(1)}, f32[8,128]{1,0:T(8,128)S(1)}, u32[]{:S(2)}, u32[]{:S(2)}) collective-permute-start(f32[8,128]{1,0:T(8,128)S(1)} %get-tuple-element.265), channel_id=1, source_target_pairs={{16,17},{17,16},{1,2},{2,1},{18,19},{19,18},{3,4},{4,3},{20,21},{2... | collective-permute-start | bytes 12296 | tf_op jit(solution)/shard_map/ppermute | solution.py:571
  111.3 1.7 %collective-permute-done.26.got_b = f32[8,128]{1,0:T(8,128)S(1)} collective-permute-done((f32[8,128]{1,0:T(8,128)S(1)}, f32[8,128]{1,0:T(8,128)S(1)}, u32[]{:S(2)}, u32[]{:S(2)}) %collective-permute-start.26) | collective-permute-done | bytes 4128 | tf_op jit(solution)/shard_map/ppermute | solution.py:571
  113.7 2.3 %collective-permute-start.28 = (f32[8,128]{1,0:T(8,128)S(1)}, f32[8,128]{1,0:T(8,128)S(1)}, u32[]{:S(2)}, u32[]{:S(2)}) collective-permute-start(f32[8,128]{1,0:T(8,128)S(1)} %get-tuple-element.275), channel_id=1, source_target_pairs={{16,17},{17,16},{1,2},{2,1},{18,19},{19,18},{3,4},{4,3},{20,21},{2... | collective-permute-start | bytes 12296 | tf_op jit(solution)/shard_map/ppermute | solution.py:571
  117.8 1.7 %collective-permute-done.28.got_b = f32[8,128]{1,0:T(8,128)S(1)} collective-permute-done((f32[8,128]{1,0:T(8,128)S(1)}, f32[8,128]{1,0:T(8,128)S(1)}, u32[]{:S(2)}, u32[]{:S(2)}) %collective-permute-start.28) | collective-permute-done | bytes 4128 | tf_op jit(solution)/shard_map/ppermute | solution.py:571
  120.2 2.3 %collective-permute-start.30 = (f32[8,128]{1,0:T(8,128)S(1)}, f32[8,128]{1,0:T(8,128)S(1)}, u32[]{:S(2)}, u32[]{:S(2)}) collective-permute-start(f32[8,128]{1,0:T(8,128)S(1)} %get-tuple-element.281), channel_id=1, source_target_pairs={{16,17},{17,16},{1,2},{2,1},{18,19},{19,18},{3,4},{4,3},{20,21},{2... | collective-permute-start | bytes 12296 | tf_op jit(solution)/shard_map/ppermute | solution.py:571
  124.3 1.7 %collective-permute-done.30.got_b = f32[8,128]{1,0:T(8,128)S(1)} collective-permute-done((f32[8,128]{1,0:T(8,128)S(1)}, f32[8,128]{1,0:T(8,128)S(1)}, u32[]{:S(2)}, u32[]{:S(2)}) %collective-permute-start.30) | collective-permute-done | bytes 4128 | tf_op jit(solution)/shard_map/ppermute | solution.py:571
  126.8 2.3 %collective-permute-start.32 = (f32[8,128]{1,0:T(8,128)S(1)}, f32[8,128]{1,0:T(8,128)S(1)}, u32[]{:S(2)}, u32[]{:S(2)}) collective-permute-start(f32[8,128]{1,0:T(8,128)S(1)} %get-tuple-element.290), channel_id=1, source_target_pairs={{16,17},{17,16},{1,2},{2,1},{18,19},{19,18},{3,4},{4,3},{20,21},{2... | collective-permute-start | bytes 12296 | tf_op jit(solution)/shard_map/ppermute | solution.py:571
  130.9 1.7 %collective-permute-done.32.got_b = f32[8,128]{1,0:T(8,128)S(1)} collective-permute-done((f32[8,128]{1,0:T(8,128)S(1)}, f32[8,128]{1,0:T(8,128)S(1)}, u32[]{:S(2)}, u32[]{:S(2)}) %collective-permute-start.32) | collective-permute-done | bytes 4128 | tf_op jit(solution)/shard_map/ppermute | solution.py:571
  133.3 2.3 %collective-permute-start.34 = (f32[8,128]{1,0:T(8,128)S(1)}, f32[8,128]{1,0:T(8,128)S(1)}, u32[]{:S(2)}, u32[]{:S(2)}) collective-permute-start(f32[8,128]{1,0:T(8,128)S(1)} %get-tuple-element.299), channel_id=1, source_target_pairs={{16,17},{17,16},{1,2},{2,1},{18,19},{19,18},{3,4},{4,3},{20,21},{2... | collective-permute-start | bytes 12296 | tf_op jit(solution)/shard_map/ppermute | solution.py:571
  137.4 1.7 %collective-permute-done.34.got_b = f32[8,128]{1,0:T(8,128)S(1)} collective-permute-done((f32[8,128]{1,0:T(8,128)S(1)}, f32[8,128]{1,0:T(8,128)S(1)}, u32[]{:S(2)}, u32[]{:S(2)}) %collective-permute-start.34) | collective-permute-done | bytes 4128 | tf_op jit(solution)/shard_map/ppermute | solution.py:571
  139.6 3.6 %collective-permute-done.36 = f32[4,2,2,128]{3,2,1,0:T(2,128)S(1)} collective-permute-done((f32[4,2,2,128]{3,2,1,0:T(2,128)S(1)}, f32[4,2,2,128]{3,2,1,0:T(2,128)S(1)}, u32[]{:S(2)}, u32[]{:S(2)}) %collective-permute-start.36) | collective-permute-done | bytes 8224 | tf_op jit(solution)/shard_map/ppermute | solution.py:585
  (84 shorter events, 39.0 us)
Async XLA Ops:
  2.1 7.0 %copy-start = (f32[1,1,16,4,512]{4,3,2,1,0:T(4,128)S(1)}, f32[1,1,16,4,512]{4,3,2,1,0:T(4,128)}, u32[]{:S(2)}) copy-start(f32[1,1,16,4,512]{4,3,2,1,0:T(4,128)} %param.14) | copy-start | bytes 393220
  2.1 7.0 %copy-start.2 = (s32[1,1,16,4]{2,3,1,0:T(4,128)S(1)}, s32[1,1,16,4]{2,3,1,0:T(4,128)}, u32[]{:S(2)}) copy-start(s32[1,1,16,4]{2,3,1,0:T(4,128)} %param.15) | copy-start | bytes 772
  2.1 28.1 %collective-permute-start.2 = (f32[12,128,128]{2,1,0:T(8,128)S(1)}, f32[12,128,128]{2,1,0:T(8,128)S(1)}, u32[]{:S(2)}, u32[]{:S(2)}) collective-permute-start(f32[12,128,128]{2,1,0:T(8,128)S(1)} %pack.4), channel_id=1, source_target_pairs={{0,16},{16,0},{1,17},{17,1},{2,18},{18,2},{3,19},{19,3},{4,20},{20... | collective-permute-start | bytes 2359304 | tf_op jit(solution)/shard_map/ppermute | solution.py:512
  6.3 24.0 %collective-permute-start.3 = (f32[6,128,128]{2,1,0:T(8,128)}, f32[6,128,128]{2,1,0:T(8,128)S(1)}, u32[]{:S(2)}, u32[]{:S(2)}) collective-permute-start(f32[6,128,128]{2,1,0:T(8,128)} %pack.5), channel_id=1, source_target_pairs={{0,16},{16,0},{1,17},{17,1},{2,18},{18,2},{3,19},{19,3},{4,20},{20... | collective-permute-start | bytes 1179656 | tf_op jit(solution)/shard_map/ppermute | solution.py:512
  9.2 0.6 copy-start.1
  10.5 11.8 %all-to-all-start = ((f32[16,1,2176]{2,1,0:T(1,128)}), f32[16,1,2176]{2,1,0:T(1,128)S(1)}, u32[]{:S(2)}, u32[]{:S(2)}) async-start(f32[16,1,2176]{2,1,0:T(1,128)} %by_target.1), calls=%async_computation | async-start | bytes 278528 | tf_op jit(solution)/shard_map/cond/branch_1_fun/all_to_all | solution.py:526
  16.8 8.6 %collective-permute-start.1 = (f32[2,128,128]{2,1,0:T(8,128)S(1)}, f32[2,128,128]{2,1,0:T(8,128)}, u32[]{:S(2)}, u32[]{:S(2)}) collective-permute-start(f32[2,128,128]{2,1,0:T(8,128)S(1)} %get-tuple-element.25), channel_id=1, source_target_pairs={{16,17},{17,16},{1,2},{2,1},{18,19},{19,18},{3,4},{4,3},{20,21},{2... | collective-permute-start | bytes 393224 | tf_op jit(solution)/shard_map/cond/branch_1_fun/ppermute | solution.py:516
  23.8 6.4 %collective-permute-start = (f32[24,128]{1,0:T(8,128)S(1)}, f32[24,128]{1,0:T(8,128)}, u32[]{:S(2)}, u32[]{:S(2)}) collective-permute-start(f32[24,128]{1,0:T(8,128)S(1)} %get-tuple-element.24), channel_id=1, source_target_pairs={{0,16},{16,0},{1,17},{17,1},{2,18},{18,2},{3,19},{19,3},{4,20},{20... | collective-permute-start | bytes 36872 | tf_op jit(solution)/shard_map/cond/branch_1_fun/ppermute | solution.py:537
  31.3 7.3 %collective-permute-start.4 = (f32[264,128]{1,0:T(8,128)S(1)}, f32[264,128]{1,0:T(8,128)S(1)}, u32[]{:S(2)}, u32[]{:S(2)}) collective-permute-start(f32[264,128]{1,0:T(8,128)S(1)} %get-tuple-element.172), channel_id=1, source_target_pairs={{16,17},{17,16},{1,2},{2,1},{18,19},{19,18},{3,4},{4,3},{20,21},{2... | collective-permute-start | bytes 405512 | tf_op jit(solution)/shard_map/ppermute | solution.py:571
  33.2 6.0 %collective-permute-start.5 = (f32[264,128]{1,0:T(8,128)S(1)}, f32[264,128]{1,0:T(8,128)S(1)}, u32[]{:S(2)}, u32[]{:S(2)}) collective-permute-start(f32[264,128]{1,0:T(8,128)S(1)} %get-tuple-element.174), channel_id=1, source_target_pairs={{0,16},{16,0},{1,17},{17,1},{2,18},{18,2},{3,19},{19,3},{4,20},{20... | collective-permute-start | bytes 405512 | tf_op jit(solution)/shard_map/ppermute | solution.py:572
  40.3 4.0 %collective-permute-start.7 = (f32[8,128]{1,0:T(8,128)S(1)}, f32[8,128]{1,0:T(8,128)S(1)}, u32[]{:S(2)}, u32[]{:S(2)}) collective-permute-start(f32[8,128]{1,0:T(8,128)S(1)} %get-tuple-element.180), channel_id=1, source_target_pairs={{0,16},{16,0},{1,17},{17,1},{2,18},{18,2},{3,19},{19,3},{4,20},{20... | collective-permute-start | bytes 12296 | tf_op jit(solution)/shard_map/ppermute | solution.py:572
  42.0 5.8 %collective-permute-start.6 = (f32[8,128]{1,0:T(8,128)S(1)}, f32[8,128]{1,0:T(8,128)S(1)}, u32[]{:S(2)}, u32[]{:S(2)}) collective-permute-start(f32[8,128]{1,0:T(8,128)S(1)} %get-tuple-element.179), channel_id=1, source_target_pairs={{16,17},{17,16},{1,2},{2,1},{18,19},{19,18},{3,4},{4,3},{20,21},{2... | collective-permute-start | bytes 12296 | tf_op jit(solution)/shard_map/ppermute | solution.py:571
  48.4 3.7 %collective-permute-start.9 = (f32[8,128]{1,0:T(8,128)S(1)}, f32[8,128]{1,0:T(8,128)S(1)}, u32[]{:S(2)}, u32[]{:S(2)}) collective-permute-start(f32[8,128]{1,0:T(8,128)S(1)} %get-tuple-element.189), channel_id=1, source_target_pairs={{0,16},{16,0},{1,17},{17,1},{2,18},{18,2},{3,19},{19,3},{4,20},{20... | collective-permute-start | bytes 12296 | tf_op jit(solution)/shard_map/ppermute | solution.py:572
  48.5 5.8 %collective-permute-start.8 = (f32[8,128]{1,0:T(8,128)S(1)}, f32[8,128]{1,0:T(8,128)S(1)}, u32[]{:S(2)}, u32[]{:S(2)}) collective-permute-start(f32[8,128]{1,0:T(8,128)S(1)} %get-tuple-element.188), channel_id=1, source_target_pairs={{16,17},{17,16},{1,2},{2,1},{18,19},{19,18},{3,4},{4,3},{20,21},{2... | collective-permute-start | bytes 12296 | tf_op jit(solution)/shard_map/ppermute | solution.py:571
  54.9 3.7 %collective-permute-start.11 = (f32[8,128]{1,0:T(8,128)S(1)}, f32[8,128]{1,0:T(8,128)S(1)}, u32[]{:S(2)}, u32[]{:S(2)}) collective-permute-start(f32[8,128]{1,0:T(8,128)S(1)} %get-tuple-element.198), channel_id=1, source_target_pairs={{0,16},{16,0},{1,17},{17,1},{2,18},{18,2},{3,19},{19,3},{4,20},{20... | collective-permute-start | bytes 12296 | tf_op jit(solution)/shard_map/ppermute | solution.py:572
  55.0 5.8 %collective-permute-start.10 = (f32[8,128]{1,0:T(8,128)S(1)}, f32[8,128]{1,0:T(8,128)S(1)}, u32[]{:S(2)}, u32[]{:S(2)}) collective-permute-start(f32[8,128]{1,0:T(8,128)S(1)} %get-tuple-element.197), channel_id=1, source_target_pairs={{16,17},{17,16},{1,2},{2,1},{18,19},{19,18},{3,4},{4,3},{20,21},{2... | collective-permute-start | bytes 12296 | tf_op jit(solution)/shard_map/ppermute | solution.py:571
  61.4 3.7 %collective-permute-start.13 = (f32[8,128]{1,0:T(8,128)S(1)}, f32[8,128]{1,0:T(8,128)S(1)}, u32[]{:S(2)}, u32[]{:S(2)}) collective-permute-start(f32[8,128]{1,0:T(8,128)S(1)} %get-tuple-element.208), channel_id=1, source_target_pairs={{0,16},{16,0},{1,17},{17,1},{2,18},{18,2},{3,19},{19,3},{4,20},{20... | collective-permute-start | bytes 12296 | tf_op jit(solution)/shard_map/ppermute | solution.py:572
  61.5 5.8 %collective-permute-start.12 = (f32[8,128]{1,0:T(8,128)S(1)}, f32[8,128]{1,0:T(8,128)S(1)}, u32[]{:S(2)}, u32[]{:S(2)}) collective-permute-start(f32[8,128]{1,0:T(8,128)S(1)} %get-tuple-element.207), channel_id=1, source_target_pairs={{16,17},{17,16},{1,2},{2,1},{18,19},{19,18},{3,4},{4,3},{20,21},{2... | collective-permute-start | bytes 12296 | tf_op jit(solution)/shard_map/ppermute | solution.py:571
  68.0 3.7 %collective-permute-start.15 = (f32[8,128]{1,0:T(8,128)S(1)}, f32[8,128]{1,0:T(8,128)S(1)}, u32[]{:S(2)}, u32[]{:S(2)}) collective-permute-start(f32[8,128]{1,0:T(8,128)S(1)} %get-tuple-element.214), channel_id=1, source_target_pairs={{0,16},{16,0},{1,17},{17,1},{2,18},{18,2},{3,19},{19,3},{4,20},{20... | collective-permute-start | bytes 12296 | tf_op jit(solution)/shard_map/ppermute | solution.py:572
  68.0 5.8 %collective-permute-start.14 = (f32[8,128]{1,0:T(8,128)S(1)}, f32[8,128]{1,0:T(8,128)S(1)}, u32[]{:S(2)}, u32[]{:S(2)}) collective-permute-start(f32[8,128]{1,0:T(8,128)S(1)} %get-tuple-element.213), channel_id=1, source_target_pairs={{16,17},{17,16},{1,2},{2,1},{18,19},{19,18},{3,4},{4,3},{20,21},{2... | collective-permute-start | bytes 12296 | tf_op jit(solution)/shard_map/ppermute | solution.py:571
  74.5 3.7 %collective-permute-start.17 = (f32[8,128]{1,0:T(8,128)S(1)}, f32[8,128]{1,0:T(8,128)S(1)}, u32[]{:S(2)}, u32[]{:S(2)}) collective-permute-start(f32[8,128]{1,0:T(8,128)S(1)} %get-tuple-element.223), channel_id=1, source_target_pairs={{0,16},{16,0},{1,17},{17,1},{2,18},{18,2},{3,19},{19,3},{4,20},{20... | collective-permute-start | bytes 12296 | tf_op jit(solution)/shard_map/ppermute | solution.py:572
  74.6 5.8 %collective-permute-start.16 = (f32[8,128]{1,0:T(8,128)S(1)}, f32[8,128]{1,0:T(8,128)S(1)}, u32[]{:S(2)}, u32[]{:S(2)}) collective-permute-start(f32[8,128]{1,0:T(8,128)S(1)} %get-tuple-element.222), channel_id=1, source_target_pairs={{16,17},{17,16},{1,2},{2,1},{18,19},{19,18},{3,4},{4,3},{20,21},{2... | collective-permute-start | bytes 12296 | tf_op jit(solution)/shard_map/ppermute | solution.py:571
  81.0 3.7 %collective-permute-start.19 = (f32[8,128]{1,0:T(8,128)S(1)}, f32[8,128]{1,0:T(8,128)S(1)}, u32[]{:S(2)}, u32[]{:S(2)}) collective-permute-start(f32[8,128]{1,0:T(8,128)S(1)} %get-tuple-element.232), channel_id=1, source_target_pairs={{0,16},{16,0},{1,17},{17,1},{2,18},{18,2},{3,19},{19,3},{4,20},{20... | collective-permute-start | bytes 12296 | tf_op jit(solution)/shard_map/ppermute | solution.py:572
  81.1 5.8 %collective-permute-start.18 = (f32[8,128]{1,0:T(8,128)S(1)}, f32[8,128]{1,0:T(8,128)S(1)}, u32[]{:S(2)}, u32[]{:S(2)}) collective-permute-start(f32[8,128]{1,0:T(8,128)S(1)} %get-tuple-element.231), channel_id=1, source_target_pairs={{16,17},{17,16},{1,2},{2,1},{18,19},{19,18},{3,4},{4,3},{20,21},{2... | collective-permute-start | bytes 12296 | tf_op jit(solution)/shard_map/ppermute | solution.py:571
  87.5 3.7 %collective-permute-start.21 = (f32[8,128]{1,0:T(8,128)S(1)}, f32[8,128]{1,0:T(8,128)S(1)}, u32[]{:S(2)}, u32[]{:S(2)}) collective-permute-start(f32[8,128]{1,0:T(8,128)S(1)} %get-tuple-element.242), channel_id=1, source_target_pairs={{0,16},{16,0},{1,17},{17,1},{2,18},{18,2},{3,19},{19,3},{4,20},{20... | collective-permute-start | bytes 12296 | tf_op jit(solution)/shard_map/ppermute | solution.py:572
  87.6 5.8 %collective-permute-start.20 = (f32[8,128]{1,0:T(8,128)S(1)}, f32[8,128]{1,0:T(8,128)S(1)}, u32[]{:S(2)}, u32[]{:S(2)}) collective-permute-start(f32[8,128]{1,0:T(8,128)S(1)} %get-tuple-element.241), channel_id=1, source_target_pairs={{16,17},{17,16},{1,2},{2,1},{18,19},{19,18},{3,4},{4,3},{20,21},{2... | collective-permute-start | bytes 12296 | tf_op jit(solution)/shard_map/ppermute | solution.py:571
  94.1 3.7 %collective-permute-start.23 = (f32[8,128]{1,0:T(8,128)S(1)}, f32[8,128]{1,0:T(8,128)S(1)}, u32[]{:S(2)}, u32[]{:S(2)}) collective-permute-start(f32[8,128]{1,0:T(8,128)S(1)} %get-tuple-element.248), channel_id=1, source_target_pairs={{0,16},{16,0},{1,17},{17,1},{2,18},{18,2},{3,19},{19,3},{4,20},{20... | collective-permute-start | bytes 12296 | tf_op jit(solution)/shard_map/ppermute | solution.py:572
  94.1 5.8 %collective-permute-start.22 = (f32[8,128]{1,0:T(8,128)S(1)}, f32[8,128]{1,0:T(8,128)S(1)}, u32[]{:S(2)}, u32[]{:S(2)}) collective-permute-start(f32[8,128]{1,0:T(8,128)S(1)} %get-tuple-element.247), channel_id=1, source_target_pairs={{16,17},{17,16},{1,2},{2,1},{18,19},{19,18},{3,4},{4,3},{20,21},{2... | collective-permute-start | bytes 12296 | tf_op jit(solution)/shard_map/ppermute | solution.py:571
  100.6 3.7 %collective-permute-start.25 = (f32[8,128]{1,0:T(8,128)S(1)}, f32[8,128]{1,0:T(8,128)S(1)}, u32[]{:S(2)}, u32[]{:S(2)}) collective-permute-start(f32[8,128]{1,0:T(8,128)S(1)} %get-tuple-element.257), channel_id=1, source_target_pairs={{0,16},{16,0},{1,17},{17,1},{2,18},{18,2},{3,19},{19,3},{4,20},{20... | collective-permute-start | bytes 12296 | tf_op jit(solution)/shard_map/ppermute | solution.py:572
  100.7 5.8 %collective-permute-start.24 = (f32[8,128]{1,0:T(8,128)S(1)}, f32[8,128]{1,0:T(8,128)S(1)}, u32[]{:S(2)}, u32[]{:S(2)}) collective-permute-start(f32[8,128]{1,0:T(8,128)S(1)} %get-tuple-element.256), channel_id=1, source_target_pairs={{16,17},{17,16},{1,2},{2,1},{18,19},{19,18},{3,4},{4,3},{20,21},{2... | collective-permute-start | bytes 12296 | tf_op jit(solution)/shard_map/ppermute | solution.py:571
  107.1 3.7 %collective-permute-start.27 = (f32[8,128]{1,0:T(8,128)S(1)}, f32[8,128]{1,0:T(8,128)S(1)}, u32[]{:S(2)}, u32[]{:S(2)}) collective-permute-start(f32[8,128]{1,0:T(8,128)S(1)} %get-tuple-element.266), channel_id=1, source_target_pairs={{0,16},{16,0},{1,17},{17,1},{2,18},{18,2},{3,19},{19,3},{4,20},{20... | collective-permute-start | bytes 12296 | tf_op jit(solution)/shard_map/ppermute | solution.py:572
  107.2 5.8 %collective-permute-start.26 = (f32[8,128]{1,0:T(8,128)S(1)}, f32[8,128]{1,0:T(8,128)S(1)}, u32[]{:S(2)}, u32[]{:S(2)}) collective-permute-start(f32[8,128]{1,0:T(8,128)S(1)} %get-tuple-element.265), channel_id=1, source_target_pairs={{16,17},{17,16},{1,2},{2,1},{18,19},{19,18},{3,4},{4,3},{20,21},{2... | collective-permute-start | bytes 12296 | tf_op jit(solution)/shard_map/ppermute | solution.py:571
  113.6 3.7 %collective-permute-start.29 = (f32[8,128]{1,0:T(8,128)S(1)}, f32[8,128]{1,0:T(8,128)S(1)}, u32[]{:S(2)}, u32[]{:S(2)}) collective-permute-start(f32[8,128]{1,0:T(8,128)S(1)} %get-tuple-element.276), channel_id=1, source_target_pairs={{0,16},{16,0},{1,17},{17,1},{2,18},{18,2},{3,19},{19,3},{4,20},{20... | collective-permute-start | bytes 12296 | tf_op jit(solution)/shard_map/ppermute | solution.py:572
  113.7 5.8 %collective-permute-start.28 = (f32[8,128]{1,0:T(8,128)S(1)}, f32[8,128]{1,0:T(8,128)S(1)}, u32[]{:S(2)}, u32[]{:S(2)}) collective-permute-start(f32[8,128]{1,0:T(8,128)S(1)} %get-tuple-element.275), channel_id=1, source_target_pairs={{16,17},{17,16},{1,2},{2,1},{18,19},{19,18},{3,4},{4,3},{20,21},{2... | collective-permute-start | bytes 12296 | tf_op jit(solution)/shard_map/ppermute | solution.py:571
  120.1 3.7 %collective-permute-start.31 = (f32[8,128]{1,0:T(8,128)S(1)}, f32[8,128]{1,0:T(8,128)S(1)}, u32[]{:S(2)}, u32[]{:S(2)}) collective-permute-start(f32[8,128]{1,0:T(8,128)S(1)} %get-tuple-element.282), channel_id=1, source_target_pairs={{0,16},{16,0},{1,17},{17,1},{2,18},{18,2},{3,19},{19,3},{4,20},{20... | collective-permute-start | bytes 12296 | tf_op jit(solution)/shard_map/ppermute | solution.py:572
  120.2 5.8 %collective-permute-start.30 = (f32[8,128]{1,0:T(8,128)S(1)}, f32[8,128]{1,0:T(8,128)S(1)}, u32[]{:S(2)}, u32[]{:S(2)}) collective-permute-start(f32[8,128]{1,0:T(8,128)S(1)} %get-tuple-element.281), channel_id=1, source_target_pairs={{16,17},{17,16},{1,2},{2,1},{18,19},{19,18},{3,4},{4,3},{20,21},{2... | collective-permute-start | bytes 12296 | tf_op jit(solution)/shard_map/ppermute | solution.py:571
  126.7 3.7 %collective-permute-start.33 = (f32[8,128]{1,0:T(8,128)S(1)}, f32[8,128]{1,0:T(8,128)S(1)}, u32[]{:S(2)}, u32[]{:S(2)}) collective-permute-start(f32[8,128]{1,0:T(8,128)S(1)} %get-tuple-element.291), channel_id=1, source_target_pairs={{0,16},{16,0},{1,17},{17,1},{2,18},{18,2},{3,19},{19,3},{4,20},{20... | collective-permute-start | bytes 12296 | tf_op jit(solution)/shard_map/ppermute | solution.py:572
  126.8 5.8 %collective-permute-start.32 = (f32[8,128]{1,0:T(8,128)S(1)}, f32[8,128]{1,0:T(8,128)S(1)}, u32[]{:S(2)}, u32[]{:S(2)}) collective-permute-start(f32[8,128]{1,0:T(8,128)S(1)} %get-tuple-element.290), channel_id=1, source_target_pairs={{16,17},{17,16},{1,2},{2,1},{18,19},{19,18},{3,4},{4,3},{20,21},{2... | collective-permute-start | bytes 12296 | tf_op jit(solution)/shard_map/ppermute | solution.py:571
  133.2 3.7 %collective-permute-start.35 = (f32[8,128]{1,0:T(8,128)S(1)}, f32[8,128]{1,0:T(8,128)S(1)}, u32[]{:S(2)}, u32[]{:S(2)}) collective-permute-start(f32[8,128]{1,0:T(8,128)S(1)} %get-tuple-element.300), channel_id=1, source_target_pairs={{0,16},{16,0},{1,17},{17,1},{2,18},{18,2},{3,19},{19,3},{4,20},{20... | collective-permute-start | bytes 12296 | tf_op jit(solution)/shard_map/ppermute | solution.py:572
  133.3 5.8 %collective-permute-start.34 = (f32[8,128]{1,0:T(8,128)S(1)}, f32[8,128]{1,0:T(8,128)S(1)}, u32[]{:S(2)}, u32[]{:S(2)}) collective-permute-start(f32[8,128]{1,0:T(8,128)S(1)} %get-tuple-element.299), channel_id=1, source_target_pairs={{16,17},{17,16},{1,2},{2,1},{18,19},{19,18},{3,4},{4,3},{20,21},{2... | collective-permute-start | bytes 12296 | tf_op jit(solution)/shard_map/ppermute | solution.py:571
  139.5 3.7 %collective-permute-start.36 = (f32[4,2,2,128]{3,2,1,0:T(2,128)S(1)}, f32[4,2,2,128]{3,2,1,0:T(2,128)S(1)}, u32[]{:S(2)}, u32[]{:S(2)}) collective-permute-start(f32[4,2,2,128]{3,2,1,0:T(2,128)S(1)} %rev.12), channel_id=1, source_target_pairs={{0,16},{16,0},{1,17},{17,1},{2,18},{18,2},{3,19},{19,3},{4,20},{20... | collective-permute-start | bytes 24584 | tf_op jit(solution)/shard_map/ppermute | solution.py:585

commit v14 on v13

--- a/solution.py
+++ b/solution.py
@@ -294,31 +294,46 @@
     return jnp.sum(spread, axis=0, keepdims=True)
 
 
-def row_of(x, j, b):
-    i = j * HALF + b
-    return x[i:i + 1]
+def rows_of(ref, start=0, count=N * HALF):
+    return [ref[start + i:start + i + 1, :] for i in range(count)]
+
+
+def put(ref, rows, start=0):
+    for i, row in enumerate(rows):
+        ref[start + i:start + i + 1, :] = row
+
+
+def each(body, *fields):
+    return [body(*rows) for rows in zip(*fields)]
+
+
+def tile(j, b):
+    return j * HALF + b
+
+
+def products(terms, f):
+    return [(block, f[tile(*at)]) for block, at in terms]
 
 
 def inner_product(f, halves):
-    return jnp.concatenate(
-        [matvec([(block, row_of(f, *at)) for block, at in tile_terms(halves, j, b)]) for j, b in TILES], axis=0
-    )
+    return [matvec(products(tile_terms(halves, j, b), f)) for j, b in TILES]
 
 
 def message(f, g, b):
     order = range(N)[::-1] if b == 1 else range(N)
-    return jnp.concatenate([row_of(x, j, b) for x in (f, g) for j in order], axis=0)
-
-
-def ahead(first, sweep, f, residue, capacity, injected):
+    return [x[tile(j, b)] for x in (f, g) for j in order]
+
+
+def ahead(first, sweep, f, q, residue, capacity, injected):
     if first:
-        return injected, 1.0
-    return residue - STRIDES[sweep] * (capacity * f) + MOMENTA[sweep + 1] * f, STRIDES[sweep]
+        return each(lambda source, a: source - a, injected, q)
+    return each(
+        lambda v, a, r, c: r - STRIDES[sweep] * (a + c * v) + MOMENTA[sweep + 1] * v, f, q, residue, capacity
+    )
 
 
 def small_part(small, index):
-    n = N * HALF
-    return small[index * n:(index + 1) * n, :]
+    return rows_of(small, index * N * HALF)
 
 
 def start_kernel(keep, recv_0, recv_1, small_keep, small_recv, msg_a, msg_b, q_out, small):
@@ -330,10 +345,11 @@
     halves = ((keep,), (recv_0, recv_1))
     f = small_part(small, INITIAL)
     q = inner_product(f, halves)
-    q_out[...] = q
-    g = small_part(small, 0) - q
-    msg_a[:2 * N, :], msg_b[:2 * N, :] = message(f, g, 1), message(f, g, 0)
-    width = f.shape[1]
+    put(q_out, q)
+    g = ahead(True, 0, f, q, None, None, small_part(small, 0))
+    put(msg_a, message(f, g, 1))
+    put(msg_b, message(f, g, 0))
+    width = small.shape[1]
     for h in range(ROWS):
         start = 2 * N + h * width
         msg_a[start:start + width, :] = keep[SIDE_A + h * HALF + 1]
@@ -376,104 +392,91 @@
                     out[i:i + 1, :] = part
 
 
-def stacked(rows):
-    return jnp.concatenate(rows, axis=0)
-
-
-def responses(halves, beyond_0, first_a, first_b, f):
-    return stacked([
-        matvec([(facing_block(halves, beyond_0, first_a, first_b, j, b), row_of(f, j, b))]) for j, b in TILES
-    ])
-
-
 def advance(instant, pair, small, product, f, residue):
     if pair == 0:
-        residue = small_part(small, instant) - product
+        residue = each(lambda source, a: source - a, small_part(small, instant), product)
         return residue, residue, 1.0
     sweep = 2 * pair - 1
-    residue = residue - STRIDES[sweep] * (product + small_part(small, CAPACITY) * f)
-    return residue, residue + MOMENTA[sweep + 1] * f, STRIDES[sweep]
-
-
-def inner_and_side(halves, j, b, f):
-    terms = [(block, row_of(f, *at)) for block, at in tile_terms(halves, j, b)]
-    return terms[:-1], terms[-1:]
+    residue = each(lambda r, a, c, v: r - STRIDES[sweep] * (a + c * v), residue, product, small_part(small, CAPACITY), f)
+    return residue, each(lambda r, v: r + MOMENTA[sweep + 1] * v, residue, f), STRIDES[sweep]
 
 
 def beside_kernel(instant, pair, keep, recv_0, recv_1, beyond_0, first_a, first_b, small, got_a, q_ref, *refs):
     halves = ((keep,), (recv_0, recv_1))
     response_out, product_out, part_out = refs[-3:]
-    f = small_part(small, INITIAL) if instant == pair == 0 else refs[0][...]
-    residue = None if pair == 0 else refs[1][...]
-    q, response = q_ref[...], responses(halves, beyond_0, first_a, first_b, f)
-    response_out[...] = response
-    product = stacked([
-        row_of(q, j, b) + matvec([(halo_block(halves, j, b), got_a[j:j + 1, :])]) if b == 1 else row_of(q, j, b)
-        for j, b in TILES
-    ])
-    product_out[...] = product
+    f = small_part(small, INITIAL) if instant == pair == 0 else rows_of(refs[0])
+    residue = None if pair == 0 else rows_of(refs[1])
+    product = rows_of(q_ref)
+    for j in range(N):
+        product[tile(j, 1)] += matvec([(halo_block(halves, j, 1), got_a[j:j + 1, :])])
+    put(product_out, product)
+    response = [
+        matvec([(facing_block(halves, beyond_0, first_a, first_b, j, b), f[tile(j, b)])]) for j, b in TILES
+    ]
+    put(response_out, response)
     _, f2, scale = advance(instant, pair, small, product, f, residue)
     part = []
     for j, b in TILES:
-        inner, side = inner_and_side(halves, j, b, f2)
+        terms = products(tile_terms(halves, j, b), f2)
         if b == 1:
-            beside = got_a[N + j:N + j + 1, :] - scale * row_of(response, j, b)
-            part.append(matvec(inner + [(halo_block(halves, j, b), beside)]))
+            beside = got_a[N + j:N + j + 1, :] - scale * response[tile(j, b)]
+            part.append(matvec(terms[:-1] + [(halo_block(halves, j, b), beside)]))
         else:
-            part.append(matvec(side))
-    part_out[...] = stacked(part)
-
-
-def pair_kernel(instant, pair, last, keep, recv_0, recv_1, small, got_b, response_ref, product_ref, part_ref, *refs):
+            part.append(matvec(terms[-1:]))
+    put(part_out, part)
+
+
+def pair_kernel(instant, pair, last, keep, recv_0, recv_1, small, got_b, response, product_ref, part_ref, *refs):
     halves = ((keep,), (recv_0, recv_1))
     first = pair == 0
     capacity = small_part(small, CAPACITY)
     if first and instant == 0:
         f = small_part(small, INITIAL)
     else:
-        f, refs = refs[0][...], refs[1:]
+        f, refs = rows_of(refs[0]), refs[1:]
     residue = estimate = None
     if not first:
-        residue, estimate, refs = refs[0][...], refs[1][...], refs[2:]
-    response, product, part = response_ref[...], product_ref[...], part_ref[...]
-
-    product = stacked([
-        row_of(product, j, b) + matvec([(halo_block(halves, j, b), got_b[j:j + 1, :])]) if b == 0
-        else row_of(product, j, b) for j, b in TILES
-    ])
+        residue, estimate, refs = rows_of(refs[0]), rows_of(refs[1]), refs[2:]
+
+    product = rows_of(product_ref)
+    for j in range(N):
+        product[tile(j, 0)] += matvec([(halo_block(halves, j, 0), got_b[j:j + 1, :])])
     residue, f2, scale = advance(instant, pair, small, product, f, residue)
-    estimate = f + STRIDES[0] * f2 if first else estimate + STRIDES[2 * pair] * f2
-
-    outs = []
+    if first:
+        estimate = each(lambda v, p: v + STRIDES[0] * p, f, f2)
+    else:
+        estimate = each(lambda e, p: e + STRIDES[2 * pair] * p, estimate, f2)
+
+    total = rows_of(part_ref)
     for j, b in TILES:
-        inner, side = inner_and_side(halves, j, b, f2)
+        i = tile(j, b)
+        terms = products(tile_terms(halves, j, b), f2)
         if b == 0:
-            beside = got_b[N + j:N + j + 1, :] - scale * row_of(response, j, b)
-            rest = matvec(inner + [(halo_block(halves, j, b), beside)])
+            beside = got_b[N + j:N + j + 1, :] - scale * response[i:i + 1, :]
+            total[i] += matvec(terms[:-1] + [(halo_block(halves, j, b), beside)])
         else:
-            rest = matvec(side)
-        outs.append(row_of(part, j, b) + rest)
+            total[i] += matvec(terms[-1:])
     sweep = 2 * pair
-    residue = residue - STRIDES[sweep] * (stacked(outs) + capacity * f2)
-    f3 = residue + MOMENTA[sweep + 1] * f2
-    estimate = estimate + STRIDES[sweep + 1] * f3
+    residue = each(lambda r, a, c, v: r - STRIDES[sweep] * (a + c * v), residue, total, capacity, f2)
+    f3 = each(lambda r, v: r + MOMENTA[sweep + 1] * v, residue, f2)
+    estimate = each(lambda e, p: e + STRIDES[sweep + 1] * p, estimate, f3)
     closing = sweep + 2 == ITERS
     if closing:
         f3 = estimate
     f_out, refs = refs[0], refs[1:]
-    f_out[...] = f3
+    put(f_out, f3)
     if last:
         return
     q = inner_product(f3, halves)
     upcoming = small_part(small, instant + 1) if closing else None
-    base, factor = ahead(closing, sweep + 1, f3, residue, capacity, upcoming)
-    g = base - factor * q
+    g = ahead(closing, sweep + 1, f3, q, residue, capacity, upcoming)
     q_out, msg_a, msg_b = refs[:3]
-    q_out[...] = q
-    msg_a[...], msg_b[...] = message(f3, g, 1), message(f3, g, 0)
+    put(msg_a, message(f3, g, 1))
+    put(msg_b, message(f3, g, 0))
+    put(q_out, q)
     if not closing:
-        refs[3][...] = residue
-        refs[4][...] = estimate
+        put(refs[3], residue)
+        put(refs[4], estimate)
 
 
 def shards_chain(own_block, neighbor_block, pattern, capacity, initial, currents, slot_tile):

time: 145 us -> 143 us (0.986)
  Pallas kernels: 27.8 us -> 24.6 us
    pallas_call x33, Pallas kernels: 18.8 us -> 15.5 us  [call(): pl.pallas_call(body, out_shape=outs, in_specs=[vmem] * len(ins), out_spec...]
  transfers between devices with their start and end apart: 38 -> 38, of which waited for: 34 -> 34; matrix products, arithmetic and copies ran while one was open for 1% -> 1% of each run, Pallas kernels for 10% -> 9%
where the time goes in v14:
time: 143 us; the launch traced here: 142 us
  waiting for transfers between devices  60.1 us (42%)
  starting transfers between devices  54.3 us (38%)
  Pallas kernels  24.6 us (17%)
  local copies, waits for them, and re-layouts  1.62 us (1%)
    ppermute x16, starting transfers between devices, shards_chain(): got_b = lax.ppermute(msg_b, both, b_pairs)  37 us
    ppermute x16, waiting for transfers between devices, shards_chain(): got_b = lax.ppermute(msg_b, both, b_pairs)  32 us
    ppermute x16, waiting for transfers between devices, shards_chain(): got_a = lax.ppermute(msg_a, 'row', swap)  18 us
    pallas_call x33, Pallas kernels, call(): pl.pallas_call(body, out_shape=outs, in_specs=[vmem] * len(ins), out_spec...  15.5 us
    pallas_call x3, Pallas kernels, pack(): pl.pallas_call(functools.partial(pack_kernel, n_col, sent, first, count),...  6.85 us
    all_to_all x1, starting transfers between devices, beside(): lax.all_to_all(by_target, 'col', split_axis=0, concat_axis=0, tiled=True)  6.27 us
    ppermute x16, starting transfers between devices, shards_chain(): got_a = lax.ppermute(msg_a, 'row', swap)  4.26 us
    ppermute x1, waiting for transfers between devices, beside(): return (small, lax.ppermute(send, 'row', swap), beyond_0)  4.02 us
  transfers between devices with their start and end apart: 38, of which 34 were waited for; matrix products, arithmetic and copies ran while one was open for 1% of the time, Pallas kernels for 9%

profile of v14, /device:TPU:8, one launch (start us, length us, event | category | flops | bytes accessed | tf_op | source)
XLA Modules:
  0.0 141.9 jit_solution(766281361995159831)
XLA Ops:
  0.1 2.0 %pack.4 = f32[12,128,128]{2,1,0:T(8,128)S(1)} custom-call(s32[2]{0:T(128)S(1)} %pad_add_fusion.place_ref, s32[2,4,4]{2,1,0:T(4,128)} %pattern_ref.5, f32[2,4,128,128]{3,2,1,0:T(8,128)} %own_hbm.5, f32[4,2,4,128,128]{4,3,2,1,0:T(8,128)} %nb_hbm.5), custom_call_target="tpu_custom_call" | custom-call | tf_op jit(solution)/shard_map/pack/pallas_call | solution.py:502
  2.1 1.6 %collective-permute-start.2 = (f32[12,128,128]{2,1,0:T(8,128)S(1)}, f32[12,128,128]{2,1,0:T(8,128)S(1)}, u32[]{:S(2)}, u32[]{:S(2)}) collective-permute-start(f32[12,128,128]{2,1,0:T(8,128)S(1)} %pack.4), channel_id=1, source_target_pairs={{0,16},{16,0},{1,17},{17,1},{2,18},{18,2},{3,19},{19,3},{4,20},{20... | collective-permute-start | bytes 2359304 | tf_op jit(solution)/shard_map/ppermute | solution.py:515
  3.7 2.6 %pack.5 = f32[6,128,128]{2,1,0:T(8,128)} custom-call(s32[2]{0:T(128)S(1)} %pad_add_fusion.place_ref, s32[2,4,4]{2,1,0:T(4,128)} %pattern_ref.5, f32[2,4,128,128]{3,2,1,0:T(8,128)} %own_hbm.5, f32[4,2,4,128,128]{4,3,2,1,0:T(8,128)} %nb_hbm.5), custom_call_target="tpu_custom_call" | custom-call | tf_op jit(solution)/shard_map/pack/pallas_call | solution.py:502
  6.9 2.3 %pack.3 = (f32[20,128,128]{2,1,0:T(8,128)S(1)}, f32[2,128,128]{2,1,0:T(8,128)S(1)}) custom-call(s32[2]{0:T(128)S(1)} %pad_add_fusion.place_ref, s32[2,4,4]{2,1,0:T(4,128)} %pattern_ref.5, f32[2,4,128,128]{3,2,1,0:T(8,128)} %own_hbm.5, f32[4,2,4,128,128]{4,3,2,1,0:T(8,128)} %nb_hbm.5), custom_call_target="tpu_custom_call" | custom-call | tf_op jit(solution)/shard_map/pack/pallas_call | solution.py:502
  9.2 21.1 %conditional.1 = (f32[24,128]{1,0:T(8,128)}, f32[24,128]{1,0:T(8,128)}, f32[2,128,128]{2,1,0:T(8,128)S(1)}) conditional(s32[]{:T(128)} %convert_element_type.3, f32[2,128,128]{2,1,0:T(8,128)S(1)} %get-tuple-element.168, (f32[1,1,16,4,512]{4,3,2,1,0:T(4,128)S(1)}, s32[1,1,16,4]{2,3,1,0:T(4,128)S(1)}, s32[2]{0:T(128)S(1)}, f32[2,4,128]{2,1,0:T(4,128)}, ...), branch_computations={%region_0.1_spmd, %region_1.2_spmd} | conditional | bytes 1532612 | solution.py:542
  10.5 6.3 %all-to-all-start = ((f32[16,1,2176]{2,1,0:T(1,128)}), f32[16,1,2176]{2,1,0:T(1,128)S(1)}, u32[]{:S(2)}, u32[]{:S(2)}) async-start(f32[16,1,2176]{2,1,0:T(1,128)} %by_target.1), calls=%async_computation | async-start | bytes 278528 | tf_op jit(solution)/shard_map/cond/branch_1_fun/all_to_all | solution.py:529
  16.8 3.1 %collective-permute-start.1 = (f32[2,128,128]{2,1,0:T(8,128)S(1)}, f32[2,128,128]{2,1,0:T(8,128)}, u32[]{:S(2)}, u32[]{:S(2)}) collective-permute-start(f32[2,128,128]{2,1,0:T(8,128)S(1)} %get-tuple-element.25), channel_id=1, source_target_pairs={{16,17},{17,16},{1,2},{2,1},{18,19},{19,18},{3,4},{4,3},{20,21},{2... | collective-permute-start | bytes 393224 | tf_op jit(solution)/shard_map/cond/branch_1_fun/ppermute | solution.py:519
  19.9 2.4 %all-to-all-done = f32[16,1,2176]{2,1,0:T(1,128)S(1)} async-done(((f32[16,1,2176]{2,1,0:T(1,128)}), f32[16,1,2176]{2,1,0:T(1,128)S(1)}, u32[]{:S(2)}, u32[]{:S(2)}) %all-to-all-start) | async-done | bytes 139296 | tf_op jit(solution)/shard_map/cond/branch_1_fun/all_to_all | solution.py:529
  22.3 1.5 %small.1 = (f32[24,128]{1,0:T(8,128)}, f32[24,128]{1,0:T(8,128)S(1)}) custom-call(s32[2]{0:T(128)} %copy-done.1, f32[16,2176]{1,0:T(8,128)S(1)} %bitcast.11, f32[2,4,128]{2,1,0:T(4,128)} %get-tuple-element.314.capacity, f32[2,4,128]{2,1,0:T(4,128)} %get-tuple-element.315.initial), custom_call_target="tpu_custom_call" | custom-call | tf_op jit(solution)/shard_map/cond/branch_1_fun/small/pallas_call | solution.py:531
  23.8 1.5 %collective-permute-start = (f32[24,128]{1,0:T(8,128)S(1)}, f32[24,128]{1,0:T(8,128)}, u32[]{:S(2)}, u32[]{:S(2)}) collective-permute-start(f32[24,128]{1,0:T(8,128)S(1)} %get-tuple-element.24), channel_id=1, source_target_pairs={{0,16},{16,0},{1,17},{17,1},{2,18},{18,2},{3,19},{19,3},{4,20},{20... | collective-permute-start | bytes 36872 | tf_op jit(solution)/shard_map/cond/branch_1_fun/ppermute | solution.py:540
  26.3 4.0 %collective-permute-done = f32[24,128]{1,0:T(8,128)} collective-permute-done((f32[24,128]{1,0:T(8,128)S(1)}, f32[24,128]{1,0:T(8,128)}, u32[]{:S(2)}, u32[]{:S(2)}) %collective-permute-start) | collective-permute-done | bytes 12320 | tf_op jit(solution)/shard_map/cond/branch_1_fun/ppermute | solution.py:540
  31.3 1.9 %collective-permute-start.4 = (f32[264,128]{1,0:T(8,128)S(1)}, f32[264,128]{1,0:T(8,128)S(1)}, u32[]{:S(2)}, u32[]{:S(2)}) collective-permute-start(f32[264,128]{1,0:T(8,128)S(1)} %get-tuple-element.172), channel_id=1, source_target_pairs={{16,17},{17,16},{1,2},{2,1},{18,19},{19,18},{3,4},{4,3},{20,21},{2... | collective-permute-start | bytes 405512 | tf_op jit(solution)/shard_map/ppermute | solution.py:574
  33.2 1.6 %collective-permute-start.5 = (f32[264,128]{1,0:T(8,128)S(1)}, f32[264,128]{1,0:T(8,128)S(1)}, u32[]{:S(2)}, u32[]{:S(2)}) collective-permute-start(f32[264,128]{1,0:T(8,128)S(1)} %get-tuple-element.174), channel_id=1, source_target_pairs={{0,16},{16,0},{1,17},{17,1},{2,18},{18,2},{3,19},{19,3},{4,20},{20... | collective-permute-start | bytes 405512 | tf_op jit(solution)/shard_map/ppermute | solution.py:575
  34.8 3.8 %collective-permute-done.4.first_b.got_b = f32[264,128]{1,0:T(8,128)S(1)} collective-permute-done((f32[264,128]{1,0:T(8,128)S(1)}, f32[264,128]{1,0:T(8,128)S(1)}, u32[]{:S(2)}, u32[]{:S(2)}) %collective-permute-start.4) | collective-permute-done | bytes 135200 | tf_op jit(solution)/shard_map/ppermute | solution.py:574
  40.1 1.7 %collective-permute-start.7 = (f32[8,128]{1,0:T(8,128)S(1)}, f32[8,128]{1,0:T(8,128)S(1)}, u32[]{:S(2)}, u32[]{:S(2)}) collective-permute-start(f32[8,128]{1,0:T(8,128)S(1)} %get-tuple-element.180), channel_id=1, source_target_pairs={{0,16},{16,0},{1,17},{17,1},{2,18},{18,2},{3,19},{19,3},{4,20},{20... | collective-permute-start | bytes 12296 | tf_op jit(solution)/shard_map/ppermute | solution.py:575
  41.8 2.3 %collective-permute-start.6 = (f32[8,128]{1,0:T(8,128)S(1)}, f32[8,128]{1,0:T(8,128)S(1)}, u32[]{:S(2)}, u32[]{:S(2)}) collective-permute-start(f32[8,128]{1,0:T(8,128)S(1)} %get-tuple-element.179), channel_id=1, source_target_pairs={{16,17},{17,16},{1,2},{2,1},{18,19},{19,18},{3,4},{4,3},{20,21},{2... | collective-permute-start | bytes 12296 | tf_op jit(solution)/shard_map/ppermute | solution.py:574
  44.5 3.0 %collective-permute-done.6.got_b = f32[8,128]{1,0:T(8,128)S(1)} collective-permute-done((f32[8,128]{1,0:T(8,128)S(1)}, f32[8,128]{1,0:T(8,128)S(1)}, u32[]{:S(2)}, u32[]{:S(2)}) %collective-permute-start.6) | collective-permute-done | bytes 4128 | tf_op jit(solution)/shard_map/ppermute | solution.py:574
  48.1 2.3 %collective-permute-start.8 = (f32[8,128]{1,0:T(8,128)S(1)}, f32[8,128]{1,0:T(8,128)S(1)}, u32[]{:S(2)}, u32[]{:S(2)}) collective-permute-start(f32[8,128]{1,0:T(8,128)S(1)} %get-tuple-element.188), channel_id=1, source_target_pairs={{16,17},{17,16},{1,2},{2,1},{18,19},{19,18},{3,4},{4,3},{20,21},{2... | collective-permute-start | bytes 12296 | tf_op jit(solution)/shard_map/ppermute | solution.py:574
  50.5 1.3 collective-permute-done.9.got_a
  52.2 1.8 %collective-permute-done.8.got_b = f32[8,128]{1,0:T(8,128)S(1)} collective-permute-done((f32[8,128]{1,0:T(8,128)S(1)}, f32[8,128]{1,0:T(8,128)S(1)}, u32[]{:S(2)}, u32[]{:S(2)}) %collective-permute-start.8) | collective-permute-done | bytes 4128 | tf_op jit(solution)/shard_map/ppermute | solution.py:574
  54.5 2.3 %collective-permute-start.10 = (f32[8,128]{1,0:T(8,128)S(1)}, f32[8,128]{1,0:T(8,128)S(1)}, u32[]{:S(2)}, u32[]{:S(2)}) collective-permute-start(f32[8,128]{1,0:T(8,128)S(1)} %get-tuple-element.197), channel_id=1, source_target_pairs={{16,17},{17,16},{1,2},{2,1},{18,19},{19,18},{3,4},{4,3},{20,21},{2... | collective-permute-start | bytes 12296 | tf_op jit(solution)/shard_map/ppermute | solution.py:574
  56.9 1.3 collective-permute-done.11.got_a
  58.6 1.8 %collective-permute-done.10.got_b = f32[8,128]{1,0:T(8,128)S(1)} collective-permute-done((f32[8,128]{1,0:T(8,128)S(1)}, f32[8,128]{1,0:T(8,128)S(1)}, u32[]{:S(2)}, u32[]{:S(2)}) %collective-permute-start.10) | collective-permute-done | bytes 4128 | tf_op jit(solution)/shard_map/ppermute | solution.py:574
  60.9 2.3 %collective-permute-start.12 = (f32[8,128]{1,0:T(8,128)S(1)}, f32[8,128]{1,0:T(8,128)S(1)}, u32[]{:S(2)}, u32[]{:S(2)}) collective-permute-start(f32[8,128]{1,0:T(8,128)S(1)} %get-tuple-element.207), channel_id=1, source_target_pairs={{16,17},{17,16},{1,2},{2,1},{18,19},{19,18},{3,4},{4,3},{20,21},{2... | collective-permute-start | bytes 12296 | tf_op jit(solution)/shard_map/ppermute | solution.py:574
  65.0 1.8 %collective-permute-done.12.got_b = f32[8,128]{1,0:T(8,128)S(1)} collective-permute-done((f32[8,128]{1,0:T(8,128)S(1)}, f32[8,128]{1,0:T(8,128)S(1)}, u32[]{:S(2)}, u32[]{:S(2)}) %collective-permute-start.12) | collective-permute-done | bytes 4128 | tf_op jit(solution)/shard_map/ppermute | solution.py:574
  67.3 2.3 %collective-permute-start.14 = (f32[8,128]{1,0:T(8,128)S(1)}, f32[8,128]{1,0:T(8,128)S(1)}, u32[]{:S(2)}, u32[]{:S(2)}) collective-permute-start(f32[8,128]{1,0:T(8,128)S(1)} %get-tuple-element.213), channel_id=1, source_target_pairs={{16,17},{17,16},{1,2},{2,1},{18,19},{19,18},{3,4},{4,3},{20,21},{2... | collective-permute-start | bytes 12296 | tf_op jit(solution)/shard_map/ppermute | solution.py:574
  71.4 1.8 %collective-permute-done.14.got_b = f32[8,128]{1,0:T(8,128)S(1)} collective-permute-done((f32[8,128]{1,0:T(8,128)S(1)}, f32[8,128]{1,0:T(8,128)S(1)}, u32[]{:S(2)}, u32[]{:S(2)}) %collective-permute-start.14) | collective-permute-done | bytes 4128 | tf_op jit(solution)/shard_map/ppermute | solution.py:574
  73.7 2.3 %collective-permute-start.16 = (f32[8,128]{1,0:T(8,128)S(1)}, f32[8,128]{1,0:T(8,128)S(1)}, u32[]{:S(2)}, u32[]{:S(2)}) collective-permute-start(f32[8,128]{1,0:T(8,128)S(1)} %get-tuple-element.222), channel_id=1, source_target_pairs={{16,17},{17,16},{1,2},{2,1},{18,19},{19,18},{3,4},{4,3},{20,21},{2... | collective-permute-start | bytes 12296 | tf_op jit(solution)/shard_map/ppermute | solution.py:574
  77.8 1.8 %collective-permute-done.16.got_b = f32[8,128]{1,0:T(8,128)S(1)} collective-permute-done((f32[8,128]{1,0:T(8,128)S(1)}, f32[8,128]{1,0:T(8,128)S(1)}, u32[]{:S(2)}, u32[]{:S(2)}) %collective-permute-start.16) | collective-permute-done | bytes 4128 | tf_op jit(solution)/shard_map/ppermute | solution.py:574
  80.1 2.3 %collective-permute-start.18 = (f32[8,128]{1,0:T(8,128)S(1)}, f32[8,128]{1,0:T(8,128)S(1)}, u32[]{:S(2)}, u32[]{:S(2)}) collective-permute-start(f32[8,128]{1,0:T(8,128)S(1)} %get-tuple-element.231), channel_id=1, source_target_pairs={{16,17},{17,16},{1,2},{2,1},{18,19},{19,18},{3,4},{4,3},{20,21},{2... | collective-permute-start | bytes 12296 | tf_op jit(solution)/shard_map/ppermute | solution.py:574
  84.2 1.8 %collective-permute-done.18.got_b = f32[8,128]{1,0:T(8,128)S(1)} collective-permute-done((f32[8,128]{1,0:T(8,128)S(1)}, f32[8,128]{1,0:T(8,128)S(1)}, u32[]{:S(2)}, u32[]{:S(2)}) %collective-permute-start.18) | collective-permute-done | bytes 4128 | tf_op jit(solution)/shard_map/ppermute | solution.py:574
  86.5 2.3 %collective-permute-start.20 = (f32[8,128]{1,0:T(8,128)S(1)}, f32[8,128]{1,0:T(8,128)S(1)}, u32[]{:S(2)}, u32[]{:S(2)}) collective-permute-start(f32[8,128]{1,0:T(8,128)S(1)} %get-tuple-element.241), channel_id=1, source_target_pairs={{16,17},{17,16},{1,2},{2,1},{18,19},{19,18},{3,4},{4,3},{20,21},{2... | collective-permute-start | bytes 12296 | tf_op jit(solution)/shard_map/ppermute | solution.py:574
  90.5 1.8 %collective-permute-done.20.got_b = f32[8,128]{1,0:T(8,128)S(1)} collective-permute-done((f32[8,128]{1,0:T(8,128)S(1)}, f32[8,128]{1,0:T(8,128)S(1)}, u32[]{:S(2)}, u32[]{:S(2)}) %collective-permute-start.20) | collective-permute-done | bytes 4128 | tf_op jit(solution)/shard_map/ppermute | solution.py:574
  92.9 2.3 %collective-permute-start.22 = (f32[8,128]{1,0:T(8,128)S(1)}, f32[8,128]{1,0:T(8,128)S(1)}, u32[]{:S(2)}, u32[]{:S(2)}) collective-permute-start(f32[8,128]{1,0:T(8,128)S(1)} %get-tuple-element.247), channel_id=1, source_target_pairs={{16,17},{17,16},{1,2},{2,1},{18,19},{19,18},{3,4},{4,3},{20,21},{2... | collective-permute-start | bytes 12296 | tf_op jit(solution)/shard_map/ppermute | solution.py:574
  96.9 1.8 %collective-permute-done.22.got_b = f32[8,128]{1,0:T(8,128)S(1)} collective-permute-done((f32[8,128]{1,0:T(8,128)S(1)}, f32[8,128]{1,0:T(8,128)S(1)}, u32[]{:S(2)}, u32[]{:S(2)}) %collective-permute-start.22) | collective-permute-done | bytes 4128 | tf_op jit(solution)/shard_map/ppermute | solution.py:574
  99.3 2.5 %collective-permute-start.24 = (f32[8,128]{1,0:T(8,128)S(1)}, f32[8,128]{1,0:T(8,128)S(1)}, u32[]{:S(2)}, u32[]{:S(2)}) collective-permute-start(f32[8,128]{1,0:T(8,128)S(1)} %get-tuple-element.256), channel_id=1, source_target_pairs={{16,17},{17,16},{1,2},{2,1},{18,19},{19,18},{3,4},{4,3},{20,21},{2... | collective-permute-start | bytes 12296 | tf_op jit(solution)/shard_map/ppermute | solution.py:574
  103.3 1.8 %collective-permute-done.24.got_b = f32[8,128]{1,0:T(8,128)S(1)} collective-permute-done((f32[8,128]{1,0:T(8,128)S(1)}, f32[8,128]{1,0:T(8,128)S(1)}, u32[]{:S(2)}, u32[]{:S(2)}) %collective-permute-start.24) | collective-permute-done | bytes 4128 | tf_op jit(solution)/shard_map/ppermute | solution.py:574
  105.7 2.3 %collective-permute-start.26 = (f32[8,128]{1,0:T(8,128)S(1)}, f32[8,128]{1,0:T(8,128)S(1)}, u32[]{:S(2)}, u32[]{:S(2)}) collective-permute-start(f32[8,128]{1,0:T(8,128)S(1)} %get-tuple-element.265), channel_id=1, source_target_pairs={{16,17},{17,16},{1,2},{2,1},{18,19},{19,18},{3,4},{4,3},{20,21},{2... | collective-permute-start | bytes 12296 | tf_op jit(solution)/shard_map/ppermute | solution.py:574
  109.7 1.8 %collective-permute-done.26.got_b = f32[8,128]{1,0:T(8,128)S(1)} collective-permute-done((f32[8,128]{1,0:T(8,128)S(1)}, f32[8,128]{1,0:T(8,128)S(1)}, u32[]{:S(2)}, u32[]{:S(2)}) %collective-permute-start.26) | collective-permute-done | bytes 4128 | tf_op jit(solution)/shard_map/ppermute | solution.py:574
  112.1 2.3 %collective-permute-start.28 = (f32[8,128]{1,0:T(8,128)S(1)}, f32[8,128]{1,0:T(8,128)S(1)}, u32[]{:S(2)}, u32[]{:S(2)}) collective-permute-start(f32[8,128]{1,0:T(8,128)S(1)} %get-tuple-element.275), channel_id=1, source_target_pairs={{16,17},{17,16},{1,2},{2,1},{18,19},{19,18},{3,4},{4,3},{20,21},{2... | collective-permute-start | bytes 12296 | tf_op jit(solution)/shard_map/ppermute | solution.py:574
  116.1 1.8 %collective-permute-done.28.got_b = f32[8,128]{1,0:T(8,128)S(1)} collective-permute-done((f32[8,128]{1,0:T(8,128)S(1)}, f32[8,128]{1,0:T(8,128)S(1)}, u32[]{:S(2)}, u32[]{:S(2)}) %collective-permute-start.28) | collective-permute-done | bytes 4128 | tf_op jit(solution)/shard_map/ppermute | solution.py:574
  118.5 2.3 %collective-permute-start.30 = (f32[8,128]{1,0:T(8,128)S(1)}, f32[8,128]{1,0:T(8,128)S(1)}, u32[]{:S(2)}, u32[]{:S(2)}) collective-permute-start(f32[8,128]{1,0:T(8,128)S(1)} %get-tuple-element.281), channel_id=1, source_target_pairs={{16,17},{17,16},{1,2},{2,1},{18,19},{19,18},{3,4},{4,3},{20,21},{2... | collective-permute-start | bytes 12296 | tf_op jit(solution)/shard_map/ppermute | solution.py:574
  122.5 1.8 %collective-permute-done.30.got_b = f32[8,128]{1,0:T(8,128)S(1)} collective-permute-done((f32[8,128]{1,0:T(8,128)S(1)}, f32[8,128]{1,0:T(8,128)S(1)}, u32[]{:S(2)}, u32[]{:S(2)}) %collective-permute-start.30) | collective-permute-done | bytes 4128 | tf_op jit(solution)/shard_map/ppermute | solution.py:574
  124.9 2.3 %collective-permute-start.32 = (f32[8,128]{1,0:T(8,128)S(1)}, f32[8,128]{1,0:T(8,128)S(1)}, u32[]{:S(2)}, u32[]{:S(2)}) collective-permute-start(f32[8,128]{1,0:T(8,128)S(1)} %get-tuple-element.290), channel_id=1, source_target_pairs={{16,17},{17,16},{1,2},{2,1},{18,19},{19,18},{3,4},{4,3},{20,21},{2... | collective-permute-start | bytes 12296 | tf_op jit(solution)/shard_map/ppermute | solution.py:574
  128.9 1.8 %collective-permute-done.32.got_b = f32[8,128]{1,0:T(8,128)S(1)} collective-permute-done((f32[8,128]{1,0:T(8,128)S(1)}, f32[8,128]{1,0:T(8,128)S(1)}, u32[]{:S(2)}, u32[]{:S(2)}) %collective-permute-start.32) | collective-permute-done | bytes 4128 | tf_op jit(solution)/shard_map/ppermute | solution.py:574
  131.3 2.3 %collective-permute-start.34 = (f32[8,128]{1,0:T(8,128)S(1)}, f32[8,128]{1,0:T(8,128)S(1)}, u32[]{:S(2)}, u32[]{:S(2)}) collective-permute-start(f32[8,128]{1,0:T(8,128)S(1)} %get-tuple-element.299), channel_id=1, source_target_pairs={{16,17},{17,16},{1,2},{2,1},{18,19},{19,18},{3,4},{4,3},{20,21},{2... | collective-permute-start | bytes 12296 | tf_op jit(solution)/shard_map/ppermute | solution.py:574
  135.3 1.8 %collective-permute-done.34.got_b = f32[8,128]{1,0:T(8,128)S(1)} collective-permute-done((f32[8,128]{1,0:T(8,128)S(1)}, f32[8,128]{1,0:T(8,128)S(1)}, u32[]{:S(2)}, u32[]{:S(2)}) %collective-permute-start.34) | collective-permute-done | bytes 4128 | tf_op jit(solution)/shard_map/ppermute | solution.py:574
  137.6 3.6 %collective-permute-done.36 = f32[4,2,2,128]{3,2,1,0:T(2,128)S(1)} collective-permute-done((f32[4,2,2,128]{3,2,1,0:T(2,128)S(1)}, f32[4,2,2,128]{3,2,1,0:T(2,128)S(1)}, u32[]{:S(2)}, u32[]{:S(2)}) %collective-permute-start.36) | collective-permute-done | bytes 8224 | tf_op jit(solution)/shard_map/ppermute | solution.py:588
  (84 shorter events, 35.7 us)
Async XLA Ops:
  2.1 7.0 %copy-start = (f32[1,1,16,4,512]{4,3,2,1,0:T(4,128)S(1)}, f32[1,1,16,4,512]{4,3,2,1,0:T(4,128)}, u32[]{:S(2)}) copy-start(f32[1,1,16,4,512]{4,3,2,1,0:T(4,128)} %param.14) | copy-start | bytes 393220
  2.1 7.0 %copy-start.2 = (s32[1,1,16,4]{2,3,1,0:T(4,128)S(1)}, s32[1,1,16,4]{2,3,1,0:T(4,128)}, u32[]{:S(2)}) copy-start(s32[1,1,16,4]{2,3,1,0:T(4,128)} %param.15) | copy-start | bytes 772
  2.1 28.1 %collective-permute-start.2 = (f32[12,128,128]{2,1,0:T(8,128)S(1)}, f32[12,128,128]{2,1,0:T(8,128)S(1)}, u32[]{:S(2)}, u32[]{:S(2)}) collective-permute-start(f32[12,128,128]{2,1,0:T(8,128)S(1)} %pack.4), channel_id=1, source_target_pairs={{0,16},{16,0},{1,17},{17,1},{2,18},{18,2},{3,19},{19,3},{4,20},{20... | collective-permute-start | bytes 2359304 | tf_op jit(solution)/shard_map/ppermute | solution.py:515
  6.3 24.0 %collective-permute-start.3 = (f32[6,128,128]{2,1,0:T(8,128)}, f32[6,128,128]{2,1,0:T(8,128)S(1)}, u32[]{:S(2)}, u32[]{:S(2)}) collective-permute-start(f32[6,128,128]{2,1,0:T(8,128)} %pack.5), channel_id=1, source_target_pairs={{0,16},{16,0},{1,17},{17,1},{2,18},{18,2},{3,19},{19,3},{4,20},{20... | collective-permute-start | bytes 1179656 | tf_op jit(solution)/shard_map/ppermute | solution.py:515
  9.2 0.6 copy-start.1
  10.5 11.8 %all-to-all-start = ((f32[16,1,2176]{2,1,0:T(1,128)}), f32[16,1,2176]{2,1,0:T(1,128)S(1)}, u32[]{:S(2)}, u32[]{:S(2)}) async-start(f32[16,1,2176]{2,1,0:T(1,128)} %by_target.1), calls=%async_computation | async-start | bytes 278528 | tf_op jit(solution)/shard_map/cond/branch_1_fun/all_to_all | solution.py:529
  16.8 8.6 %collective-permute-start.1 = (f32[2,128,128]{2,1,0:T(8,128)S(1)}, f32[2,128,128]{2,1,0:T(8,128)}, u32[]{:S(2)}, u32[]{:S(2)}) collective-permute-start(f32[2,128,128]{2,1,0:T(8,128)S(1)} %get-tuple-element.25), channel_id=1, source_target_pairs={{16,17},{17,16},{1,2},{2,1},{18,19},{19,18},{3,4},{4,3},{20,21},{2... | collective-permute-start | bytes 393224 | tf_op jit(solution)/shard_map/cond/branch_1_fun/ppermute | solution.py:519
  23.8 6.4 %collective-permute-start = (f32[24,128]{1,0:T(8,128)S(1)}, f32[24,128]{1,0:T(8,128)}, u32[]{:S(2)}, u32[]{:S(2)}) collective-permute-start(f32[24,128]{1,0:T(8,128)S(1)} %get-tuple-element.24), channel_id=1, source_target_pairs={{0,16},{16,0},{1,17},{17,1},{2,18},{18,2},{3,19},{19,3},{4,20},{20... | collective-permute-start | bytes 36872 | tf_op jit(solution)/shard_map/cond/branch_1_fun/ppermute | solution.py:540
  31.3 7.3 %collective-permute-start.4 = (f32[264,128]{1,0:T(8,128)S(1)}, f32[264,128]{1,0:T(8,128)S(1)}, u32[]{:S(2)}, u32[]{:S(2)}) collective-permute-start(f32[264,128]{1,0:T(8,128)S(1)} %get-tuple-element.172), channel_id=1, source_target_pairs={{16,17},{17,16},{1,2},{2,1},{18,19},{19,18},{3,4},{4,3},{20,21},{2... | collective-permute-start | bytes 405512 | tf_op jit(solution)/shard_map/ppermute | solution.py:574
  33.2 6.0 %collective-permute-start.5 = (f32[264,128]{1,0:T(8,128)S(1)}, f32[264,128]{1,0:T(8,128)S(1)}, u32[]{:S(2)}, u32[]{:S(2)}) collective-permute-start(f32[264,128]{1,0:T(8,128)S(1)} %get-tuple-element.174), channel_id=1, source_target_pairs={{0,16},{16,0},{1,17},{17,1},{2,18},{18,2},{3,19},{19,3},{4,20},{20... | collective-permute-start | bytes 405512 | tf_op jit(solution)/shard_map/ppermute | solution.py:575
  40.1 4.0 %collective-permute-start.7 = (f32[8,128]{1,0:T(8,128)S(1)}, f32[8,128]{1,0:T(8,128)S(1)}, u32[]{:S(2)}, u32[]{:S(2)}) collective-permute-start(f32[8,128]{1,0:T(8,128)S(1)} %get-tuple-element.180), channel_id=1, source_target_pairs={{0,16},{16,0},{1,17},{17,1},{2,18},{18,2},{3,19},{19,3},{4,20},{20... | collective-permute-start | bytes 12296 | tf_op jit(solution)/shard_map/ppermute | solution.py:575
  41.8 5.8 %collective-permute-start.6 = (f32[8,128]{1,0:T(8,128)S(1)}, f32[8,128]{1,0:T(8,128)S(1)}, u32[]{:S(2)}, u32[]{:S(2)}) collective-permute-start(f32[8,128]{1,0:T(8,128)S(1)} %get-tuple-element.179), channel_id=1, source_target_pairs={{16,17},{17,16},{1,2},{2,1},{18,19},{19,18},{3,4},{4,3},{20,21},{2... | collective-permute-start | bytes 12296 | tf_op jit(solution)/shard_map/ppermute | solution.py:574
  48.1 3.7 %collective-permute-start.9 = (f32[8,128]{1,0:T(8,128)S(1)}, f32[8,128]{1,0:T(8,128)S(1)}, u32[]{:S(2)}, u32[]{:S(2)}) collective-permute-start(f32[8,128]{1,0:T(8,128)S(1)} %get-tuple-element.189), channel_id=1, source_target_pairs={{0,16},{16,0},{1,17},{17,1},{2,18},{18,2},{3,19},{19,3},{4,20},{20... | collective-permute-start | bytes 12296 | tf_op jit(solution)/shard_map/ppermute | solution.py:575
  48.1 5.8 %collective-permute-start.8 = (f32[8,128]{1,0:T(8,128)S(1)}, f32[8,128]{1,0:T(8,128)S(1)}, u32[]{:S(2)}, u32[]{:S(2)}) collective-permute-start(f32[8,128]{1,0:T(8,128)S(1)} %get-tuple-element.188), channel_id=1, source_target_pairs={{16,17},{17,16},{1,2},{2,1},{18,19},{19,18},{3,4},{4,3},{20,21},{2... | collective-permute-start | bytes 12296 | tf_op jit(solution)/shard_map/ppermute | solution.py:574
  54.5 3.7 %collective-permute-start.11 = (f32[8,128]{1,0:T(8,128)S(1)}, f32[8,128]{1,0:T(8,128)S(1)}, u32[]{:S(2)}, u32[]{:S(2)}) collective-permute-start(f32[8,128]{1,0:T(8,128)S(1)} %get-tuple-element.198), channel_id=1, source_target_pairs={{0,16},{16,0},{1,17},{17,1},{2,18},{18,2},{3,19},{19,3},{4,20},{20... | collective-permute-start | bytes 12296 | tf_op jit(solution)/shard_map/ppermute | solution.py:575
  54.5 5.8 %collective-permute-start.10 = (f32[8,128]{1,0:T(8,128)S(1)}, f32[8,128]{1,0:T(8,128)S(1)}, u32[]{:S(2)}, u32[]{:S(2)}) collective-permute-start(f32[8,128]{1,0:T(8,128)S(1)} %get-tuple-element.197), channel_id=1, source_target_pairs={{16,17},{17,16},{1,2},{2,1},{18,19},{19,18},{3,4},{4,3},{20,21},{2... | collective-permute-start | bytes 12296 | tf_op jit(solution)/shard_map/ppermute | solution.py:574
  60.9 3.7 %collective-permute-start.13 = (f32[8,128]{1,0:T(8,128)S(1)}, f32[8,128]{1,0:T(8,128)S(1)}, u32[]{:S(2)}, u32[]{:S(2)}) collective-permute-start(f32[8,128]{1,0:T(8,128)S(1)} %get-tuple-element.208), channel_id=1, source_target_pairs={{0,16},{16,0},{1,17},{17,1},{2,18},{18,2},{3,19},{19,3},{4,20},{20... | collective-permute-start | bytes 12296 | tf_op jit(solution)/shard_map/ppermute | solution.py:575
  60.9 5.8 %collective-permute-start.12 = (f32[8,128]{1,0:T(8,128)S(1)}, f32[8,128]{1,0:T(8,128)S(1)}, u32[]{:S(2)}, u32[]{:S(2)}) collective-permute-start(f32[8,128]{1,0:T(8,128)S(1)} %get-tuple-element.207), channel_id=1, source_target_pairs={{16,17},{17,16},{1,2},{2,1},{18,19},{19,18},{3,4},{4,3},{20,21},{2... | collective-permute-start | bytes 12296 | tf_op jit(solution)/shard_map/ppermute | solution.py:574
  67.2 3.7 %collective-permute-start.15 = (f32[8,128]{1,0:T(8,128)S(1)}, f32[8,128]{1,0:T(8,128)S(1)}, u32[]{:S(2)}, u32[]{:S(2)}) collective-permute-start(f32[8,128]{1,0:T(8,128)S(1)} %get-tuple-element.214), channel_id=1, source_target_pairs={{0,16},{16,0},{1,17},{17,1},{2,18},{18,2},{3,19},{19,3},{4,20},{20... | collective-permute-start | bytes 12296 | tf_op jit(solution)/shard_map/ppermute | solution.py:575
  67.3 5.8 %collective-permute-start.14 = (f32[8,128]{1,0:T(8,128)S(1)}, f32[8,128]{1,0:T(8,128)S(1)}, u32[]{:S(2)}, u32[]{:S(2)}) collective-permute-start(f32[8,128]{1,0:T(8,128)S(1)} %get-tuple-element.213), channel_id=1, source_target_pairs={{16,17},{17,16},{1,2},{2,1},{18,19},{19,18},{3,4},{4,3},{20,21},{2... | collective-permute-start | bytes 12296 | tf_op jit(solution)/shard_map/ppermute | solution.py:574
  73.6 3.7 %collective-permute-start.17 = (f32[8,128]{1,0:T(8,128)S(1)}, f32[8,128]{1,0:T(8,128)S(1)}, u32[]{:S(2)}, u32[]{:S(2)}) collective-permute-start(f32[8,128]{1,0:T(8,128)S(1)} %get-tuple-element.223), channel_id=1, source_target_pairs={{0,16},{16,0},{1,17},{17,1},{2,18},{18,2},{3,19},{19,3},{4,20},{20... | collective-permute-start | bytes 12296 | tf_op jit(solution)/shard_map/ppermute | solution.py:575
  73.7 5.8 %collective-permute-start.16 = (f32[8,128]{1,0:T(8,128)S(1)}, f32[8,128]{1,0:T(8,128)S(1)}, u32[]{:S(2)}, u32[]{:S(2)}) collective-permute-start(f32[8,128]{1,0:T(8,128)S(1)} %get-tuple-element.222), channel_id=1, source_target_pairs={{16,17},{17,16},{1,2},{2,1},{18,19},{19,18},{3,4},{4,3},{20,21},{2... | collective-permute-start | bytes 12296 | tf_op jit(solution)/shard_map/ppermute | solution.py:574
  80.0 3.7 %collective-permute-start.19 = (f32[8,128]{1,0:T(8,128)S(1)}, f32[8,128]{1,0:T(8,128)S(1)}, u32[]{:S(2)}, u32[]{:S(2)}) collective-permute-start(f32[8,128]{1,0:T(8,128)S(1)} %get-tuple-element.232), channel_id=1, source_target_pairs={{0,16},{16,0},{1,17},{17,1},{2,18},{18,2},{3,19},{19,3},{4,20},{20... | collective-permute-start | bytes 12296 | tf_op jit(solution)/shard_map/ppermute | solution.py:575
  80.1 5.8 %collective-permute-start.18 = (f32[8,128]{1,0:T(8,128)S(1)}, f32[8,128]{1,0:T(8,128)S(1)}, u32[]{:S(2)}, u32[]{:S(2)}) collective-permute-start(f32[8,128]{1,0:T(8,128)S(1)} %get-tuple-element.231), channel_id=1, source_target_pairs={{16,17},{17,16},{1,2},{2,1},{18,19},{19,18},{3,4},{4,3},{20,21},{2... | collective-permute-start | bytes 12296 | tf_op jit(solution)/shard_map/ppermute | solution.py:574
  86.4 3.7 %collective-permute-start.21 = (f32[8,128]{1,0:T(8,128)S(1)}, f32[8,128]{1,0:T(8,128)S(1)}, u32[]{:S(2)}, u32[]{:S(2)}) collective-permute-start(f32[8,128]{1,0:T(8,128)S(1)} %get-tuple-element.242), channel_id=1, source_target_pairs={{0,16},{16,0},{1,17},{17,1},{2,18},{18,2},{3,19},{19,3},{4,20},{20... | collective-permute-start | bytes 12296 | tf_op jit(solution)/shard_map/ppermute | solution.py:575
  86.5 5.8 %collective-permute-start.20 = (f32[8,128]{1,0:T(8,128)S(1)}, f32[8,128]{1,0:T(8,128)S(1)}, u32[]{:S(2)}, u32[]{:S(2)}) collective-permute-start(f32[8,128]{1,0:T(8,128)S(1)} %get-tuple-element.241), channel_id=1, source_target_pairs={{16,17},{17,16},{1,2},{2,1},{18,19},{19,18},{3,4},{4,3},{20,21},{2... | collective-permute-start | bytes 12296 | tf_op jit(solution)/shard_map/ppermute | solution.py:574
  92.8 3.7 %collective-permute-start.23 = (f32[8,128]{1,0:T(8,128)S(1)}, f32[8,128]{1,0:T(8,128)S(1)}, u32[]{:S(2)}, u32[]{:S(2)}) collective-permute-start(f32[8,128]{1,0:T(8,128)S(1)} %get-tuple-element.248), channel_id=1, source_target_pairs={{0,16},{16,0},{1,17},{17,1},{2,18},{18,2},{3,19},{19,3},{4,20},{20... | collective-permute-start | bytes 12296 | tf_op jit(solution)/shard_map/ppermute | solution.py:575
  92.9 5.8 %collective-permute-start.22 = (f32[8,128]{1,0:T(8,128)S(1)}, f32[8,128]{1,0:T(8,128)S(1)}, u32[]{:S(2)}, u32[]{:S(2)}) collective-permute-start(f32[8,128]{1,0:T(8,128)S(1)} %get-tuple-element.247), channel_id=1, source_target_pairs={{16,17},{17,16},{1,2},{2,1},{18,19},{19,18},{3,4},{4,3},{20,21},{2... | collective-permute-start | bytes 12296 | tf_op jit(solution)/shard_map/ppermute | solution.py:574
  99.2 3.7 %collective-permute-start.25 = (f32[8,128]{1,0:T(8,128)S(1)}, f32[8,128]{1,0:T(8,128)S(1)}, u32[]{:S(2)}, u32[]{:S(2)}) collective-permute-start(f32[8,128]{1,0:T(8,128)S(1)} %get-tuple-element.257), channel_id=1, source_target_pairs={{0,16},{16,0},{1,17},{17,1},{2,18},{18,2},{3,19},{19,3},{4,20},{20... | collective-permute-start | bytes 12296 | tf_op jit(solution)/shard_map/ppermute | solution.py:575
  99.3 5.8 %collective-permute-start.24 = (f32[8,128]{1,0:T(8,128)S(1)}, f32[8,128]{1,0:T(8,128)S(1)}, u32[]{:S(2)}, u32[]{:S(2)}) collective-permute-start(f32[8,128]{1,0:T(8,128)S(1)} %get-tuple-element.256), channel_id=1, source_target_pairs={{16,17},{17,16},{1,2},{2,1},{18,19},{19,18},{3,4},{4,3},{20,21},{2... | collective-permute-start | bytes 12296 | tf_op jit(solution)/shard_map/ppermute | solution.py:574
  105.6 3.7 %collective-permute-start.27 = (f32[8,128]{1,0:T(8,128)S(1)}, f32[8,128]{1,0:T(8,128)S(1)}, u32[]{:S(2)}, u32[]{:S(2)}) collective-permute-start(f32[8,128]{1,0:T(8,128)S(1)} %get-tuple-element.266), channel_id=1, source_target_pairs={{0,16},{16,0},{1,17},{17,1},{2,18},{18,2},{3,19},{19,3},{4,20},{20... | collective-permute-start | bytes 12296 | tf_op jit(solution)/shard_map/ppermute | solution.py:575
  105.7 5.8 %collective-permute-start.26 = (f32[8,128]{1,0:T(8,128)S(1)}, f32[8,128]{1,0:T(8,128)S(1)}, u32[]{:S(2)}, u32[]{:S(2)}) collective-permute-start(f32[8,128]{1,0:T(8,128)S(1)} %get-tuple-element.265), channel_id=1, source_target_pairs={{16,17},{17,16},{1,2},{2,1},{18,19},{19,18},{3,4},{4,3},{20,21},{2... | collective-permute-start | bytes 12296 | tf_op jit(solution)/shard_map/ppermute | solution.py:574
  112.0 3.7 %collective-permute-start.29 = (f32[8,128]{1,0:T(8,128)S(1)}, f32[8,128]{1,0:T(8,128)S(1)}, u32[]{:S(2)}, u32[]{:S(2)}) collective-permute-start(f32[8,128]{1,0:T(8,128)S(1)} %get-tuple-element.276), channel_id=1, source_target_pairs={{0,16},{16,0},{1,17},{17,1},{2,18},{18,2},{3,19},{19,3},{4,20},{20... | collective-permute-start | bytes 12296 | tf_op jit(solution)/shard_map/ppermute | solution.py:575
  112.1 5.8 %collective-permute-start.28 = (f32[8,128]{1,0:T(8,128)S(1)}, f32[8,128]{1,0:T(8,128)S(1)}, u32[]{:S(2)}, u32[]{:S(2)}) collective-permute-start(f32[8,128]{1,0:T(8,128)S(1)} %get-tuple-element.275), channel_id=1, source_target_pairs={{16,17},{17,16},{1,2},{2,1},{18,19},{19,18},{3,4},{4,3},{20,21},{2... | collective-permute-start | bytes 12296 | tf_op jit(solution)/shard_map/ppermute | solution.py:574
  118.4 3.7 %collective-permute-start.31 = (f32[8,128]{1,0:T(8,128)S(1)}, f32[8,128]{1,0:T(8,128)S(1)}, u32[]{:S(2)}, u32[]{:S(2)}) collective-permute-start(f32[8,128]{1,0:T(8,128)S(1)} %get-tuple-element.282), channel_id=1, source_target_pairs={{0,16},{16,0},{1,17},{17,1},{2,18},{18,2},{3,19},{19,3},{4,20},{20... | collective-permute-start | bytes 12296 | tf_op jit(solution)/shard_map/ppermute | solution.py:575
  118.5 5.8 %collective-permute-start.30 = (f32[8,128]{1,0:T(8,128)S(1)}, f32[8,128]{1,0:T(8,128)S(1)}, u32[]{:S(2)}, u32[]{:S(2)}) collective-permute-start(f32[8,128]{1,0:T(8,128)S(1)} %get-tuple-element.281), channel_id=1, source_target_pairs={{16,17},{17,16},{1,2},{2,1},{18,19},{19,18},{3,4},{4,3},{20,21},{2... | collective-permute-start | bytes 12296 | tf_op jit(solution)/shard_map/ppermute | solution.py:574
  124.8 3.7 %collective-permute-start.33 = (f32[8,128]{1,0:T(8,128)S(1)}, f32[8,128]{1,0:T(8,128)S(1)}, u32[]{:S(2)}, u32[]{:S(2)}) collective-permute-start(f32[8,128]{1,0:T(8,128)S(1)} %get-tuple-element.291), channel_id=1, source_target_pairs={{0,16},{16,0},{1,17},{17,1},{2,18},{18,2},{3,19},{19,3},{4,20},{20... | collective-permute-start | bytes 12296 | tf_op jit(solution)/shard_map/ppermute | solution.py:575
  124.9 5.8 %collective-permute-start.32 = (f32[8,128]{1,0:T(8,128)S(1)}, f32[8,128]{1,0:T(8,128)S(1)}, u32[]{:S(2)}, u32[]{:S(2)}) collective-permute-start(f32[8,128]{1,0:T(8,128)S(1)} %get-tuple-element.290), channel_id=1, source_target_pairs={{16,17},{17,16},{1,2},{2,1},{18,19},{19,18},{3,4},{4,3},{20,21},{2... | collective-permute-start | bytes 12296 | tf_op jit(solution)/shard_map/ppermute | solution.py:574
  131.2 3.7 %collective-permute-start.35 = (f32[8,128]{1,0:T(8,128)S(1)}, f32[8,128]{1,0:T(8,128)S(1)}, u32[]{:S(2)}, u32[]{:S(2)}) collective-permute-start(f32[8,128]{1,0:T(8,128)S(1)} %get-tuple-element.300), channel_id=1, source_target_pairs={{0,16},{16,0},{1,17},{17,1},{2,18},{18,2},{3,19},{19,3},{4,20},{20... | collective-permute-start | bytes 12296 | tf_op jit(solution)/shard_map/ppermute | solution.py:575
  131.3 5.8 %collective-permute-start.34 = (f32[8,128]{1,0:T(8,128)S(1)}, f32[8,128]{1,0:T(8,128)S(1)}, u32[]{:S(2)}, u32[]{:S(2)}) collective-permute-start(f32[8,128]{1,0:T(8,128)S(1)} %get-tuple-element.299), channel_id=1, source_target_pairs={{16,17},{17,16},{1,2},{2,1},{18,19},{19,18},{3,4},{4,3},{20,21},{2... | collective-permute-start | bytes 12296 | tf_op jit(solution)/shard_map/ppermute | solution.py:574
  137.5 3.7 %collective-permute-start.36 = (f32[4,2,2,128]{3,2,1,0:T(2,128)S(1)}, f32[4,2,2,128]{3,2,1,0:T(2,128)S(1)}, u32[]{:S(2)}, u32[]{:S(2)}) collective-permute-start(f32[4,2,2,128]{3,2,1,0:T(2,128)S(1)} %rev.12), channel_id=1, source_target_pairs={{0,16},{16,0},{1,17},{17,1},{2,18},{18,2},{3,19},{19,3},{4,20},{20... | collective-permute-start | bytes 24584 | tf_op jit(solution)/shard_map/ppermute | solution.py:588

commit v15 on v14

--- a/solution.py
+++ b/solution.py
@@ -221,9 +221,11 @@
     return tiles
 
 
-def pack_kernel(n_col, sent, first, count, place_ref, pattern_ref, own_hbm, nb_hbm, out, *rest):
-    sems = rest[-1]
-    tiles = half_tiles(place_ref[0], place_ref[1], n_col, own_hbm.shape[1], sent)
+def pack_kernel(n_col, sent, first, count, pattern_hbm, own_hbm, nb_hbm, out, *rest):
+    pattern_ref, sems = rest[-2:]
+    tiles = half_tiles(lax.axis_index("row"), lax.axis_index("col"), n_col, own_hbm.shape[1], sent)
+    pattern_copy = pltpu.make_async_copy(pattern_hbm, pattern_ref, sems.at[count])
+    pattern_copy.start()
     copies = []
     for i in range(count):
         direction, row, at, _ = tiles[first + i]
@@ -231,6 +233,7 @@
         copies.append(pltpu.make_async_copy(source, out.at[i], sems.at[i]))
     for copy in copies:
         copy.start()
+    pattern_copy.wait()
     for i in range(count):
         direction, row, at, weight = tiles[first + i]
         copies[i].wait()
@@ -336,12 +339,15 @@
     return rows_of(small, index * N * HALF)
 
 
-def start_kernel(keep, recv_0, recv_1, small_keep, small_recv, msg_a, msg_b, q_out, small):
+def join_kernel(keep, recv, small):
     n = ROWS * HALF
-    for i in range(0, small_keep.shape[0], n):
-        small[2 * i:2 * i + n, :] = small_keep[i:i + n, :]
-        small[2 * i + n:2 * i + n + HALF, :] = small_recv[i + HALF:i + n, :]
-        small[2 * i + n + HALF:2 * i + 2 * n, :] = small_recv[i:i + HALF, :]
+    for i in range(0, keep.shape[0], n):
+        small[2 * i:2 * i + n, :] = keep[i:i + n, :]
+        small[2 * i + n:2 * i + n + HALF, :] = recv[i + HALF:i + n, :]
+        small[2 * i + n + HALF:2 * i + 2 * n, :] = recv[i:i + HALF, :]
+
+
+def start_kernel(keep, recv_0, recv_1, small, msg_a, msg_b, q_out):
     halves = ((keep,), (recv_0, recv_1))
     f = small_part(small, INITIAL)
     q = inner_product(f, halves)
@@ -502,18 +508,20 @@
         return pl.pallas_call(
             functools.partial(pack_kernel, n_col, sent, first, count),
             out_shape=[jax.ShapeDtypeStruct((n, width, width), jnp.float32) for n in (count, *extra)],
-            in_specs=[smem, smem, hbm, hbm],
+            in_specs=[hbm, hbm, hbm],
             out_specs=[vmem] * (1 + len(extra)),
-            scratch_shapes=[pltpu.SemaphoreType.DMA((count,))],
+            scratch_shapes=[pltpu.SMEM(pattern.shape, jnp.int32), pltpu.SemaphoreType.DMA((count + 1,))],
             compiler_params=limit,
             name="pack",
-        )(place, *blocks)
+        )(*blocks)
 
     recv = []
     for first, count in ((0, SPLIT[1][0]), SPLIT[1]):
         (send,) = pack(1, first, count)
         recv.append(lax.ppermute(send, "row", swap))
     keep, facing_0 = pack(0, 0, PACKED, (ROWS,))
+
+    unit_small = jax.ShapeDtypeStruct(((STEPS + 2) * N * HALF, width), jnp.float32)
 
     def beside(currents, slot_tile, capacity, initial, facing_0):
         beyond_0 = lax.ppermute(facing_0, both, b_pairs)
@@ -537,13 +545,21 @@
             compiler_params=limit,
             name="small",
         )(place, arrived.reshape(n_col, slots * frames + width), capacity, initial)
-        return small, lax.ppermute(send, "row", swap), beyond_0
-
-    *small, beyond_0 = lax.cond(
+        small = pl.pallas_call(
+            join_kernel,
+            out_shape=unit_small,
+            in_specs=[vmem, vmem],
+            out_specs=vmem,
+            compiler_params=limit,
+            name="join",
+        )(small, lax.ppermute(send, "row", swap))
+        return small, beyond_0
+
+    small, beyond_0 = lax.cond(
         row < lax.axis_size("row"),
         beside,
         lambda currents, slot_tile, capacity, initial, facing_0: (
-            *jnp.zeros((2, (STEPS + 2) * ROWS * HALF, width), jnp.float32), facing_0
+            jnp.zeros(unit_small.shape, jnp.float32), facing_0
         ),
         currents, slot_tile, capacity, initial, facing_0,
     )
@@ -564,8 +580,7 @@
         )(*ins)
 
     first_shape = jax.ShapeDtypeStruct((2 * N + ROWS * width, width), jnp.float32)
-    unit_small = jax.ShapeDtypeStruct(((STEPS + 2) * N * HALF, width), jnp.float32)
-    msg_a, msg_b, q, small = call(start_kernel, (first_shape, first_shape, shape, unit_small), 28, *halves, *small)
+    msg_a, msg_b, q = call(start_kernel, (first_shape, first_shape, shape), 28, *halves, small)
     field, state, frames, first = (), (), [], None
     for instant in range(STEPS):
         for pair in range(ITERS // 2):

time: 143 us -> 141 us (0.986)
  Pallas kernels: 24.6 us -> 21.9 us
    pallas_call x3, Pallas kernels: 6.85 us -> 4.61 us  [pack(): pl.pallas_call(functools.partial(pack_kernel, n_col, sent, first, count),...]
where the time goes in v15:
time: 141 us; the launch traced here: 140 us
  waiting for transfers between devices  61.1 us (43%)
  starting transfers between devices  54.4 us (39%)
  Pallas kernels  21.9 us (16%)
    ppermute x16, starting transfers between devices, shards_chain(): got_b = lax.ppermute(msg_b, both, b_pairs)  37 us
    ppermute x16, waiting for transfers between devices, shards_chain(): got_b = lax.ppermute(msg_b, both, b_pairs)  32 us
    ppermute x16, waiting for transfers between devices, shards_chain(): got_a = lax.ppermute(msg_a, 'row', swap)  18 us
    pallas_call x33, Pallas kernels, call(): pl.pallas_call(body, out_shape=outs, in_specs=[vmem] * len(ins), out_spec...  14.8 us
    all_to_all x1, starting transfers between devices, beside(): lax.all_to_all(by_target, 'col', split_axis=0, concat_axis=0, tiled=True)  6.27 us
    ppermute x1, waiting for transfers between devices, beside(): lax.ppermute(send, 'row', swap)  5.02 us
    pallas_call x3, Pallas kernels, pack(): pl.pallas_call(functools.partial(pack_kernel, n_col, sent, first, count),...  4.61 us
    ppermute x16, starting transfers between devices, shards_chain(): got_a = lax.ppermute(msg_a, 'row', swap)  4.26 us
  transfers between devices with their start and end apart: 38, of which 34 were waited for; matrix products, arithmetic and copies ran while one was open for 1% of the time, Pallas kernels for 9%

profile of v15, /device:TPU:8, one launch (start us, length us, event | category | flops | bytes accessed | tf_op | source)
XLA Modules:
  0.0 140.2 jit_solution(3417430936292061930)
XLA Ops:
  0.0 1.3 pack.4
  1.3 1.6 %collective-permute-start.2 = (f32[12,128,128]{2,1,0:T(8,128)S(1)}, f32[12,128,128]{2,1,0:T(8,128)S(1)}, u32[]{:S(2)}, u32[]{:S(2)}) collective-permute-start(f32[12,128,128]{2,1,0:T(8,128)S(1)} %pack.4), channel_id=1, source_target_pairs={{0,16},{16,0},{1,17},{17,1},{2,18},{18,2},{3,19},{19,3},{4,20},{20... | collective-permute-start | bytes 2359304 | tf_op jit(solution)/shard_map/ppermute | solution.py:521
  2.9 1.8 %pack.5 = f32[6,128,128]{2,1,0:T(8,128)} custom-call(s32[2,4,4]{2,1,0:T(4,128)} %pattern_hbm.5, f32[2,4,128,128]{3,2,1,0:T(8,128)} %own_hbm.5, f32[4,2,4,128,128]{4,3,2,1,0:T(8,128)} %nb_hbm.5), custom_call_target="tpu_custom_call" | custom-call | tf_op jit(solution)/shard_map/pack/pallas_call | solution.py:508
  5.3 1.5 %pack.3 = (f32[20,128,128]{2,1,0:T(8,128)S(1)}, f32[2,128,128]{2,1,0:T(8,128)S(1)}) custom-call(s32[2,4,4]{2,1,0:T(4,128)} %pattern_hbm.5, f32[2,4,128,128]{3,2,1,0:T(8,128)} %own_hbm.5, f32[4,2,4,128,128]{4,3,2,1,0:T(8,128)} %nb_hbm.5), custom_call_target="tpu_custom_call" | custom-call | tf_op jit(solution)/shard_map/pack/pallas_call | solution.py:508
  7.4 21.9 %conditional.1 = (f32[48,128]{1,0:T(8,128)S(1)}, f32[2,128,128]{2,1,0:T(8,128)S(1)}) conditional(s32[]{:T(128)} %convert_element_type.3, f32[2,128,128]{2,1,0:T(8,128)S(1)} %get-tuple-element.166, (f32[1,1,16,4,512]{4,3,2,1,0:T(4,128)}, s32[1,1,16,4]{2,3,1,0:T(4,128)S(1)}, s32[2]{0:T(128)}, f32[2,4,128]{2,1,0:T(4,128)}, f32[2,4,128]{2,1,0:T(4,128)}, ...), branch_computations={%region_0.1_spmd, %region_1.2_spmd} | conditional | bytes 1532544 | solution.py:558
  7.5 1.6 %by_target.1 = f32[16,1,2176]{2,1,0:T(1,128)} custom-call(f32[16,4,512]{2,1,0:T(4,128)} %bitcast.16, s32[16,4]{1,0:T(8,128)S(1)} %copy.14.slot_tile), custom_call_target="tpu_custom_call" | custom-call | tf_op jit(solution)/shard_map/cond/branch_1_fun/by_target/pallas_call | solution.py:529
  9.1 6.3 %all-to-all-start = ((f32[16,1,2176]{2,1,0:T(1,128)}), f32[16,1,2176]{2,1,0:T(1,128)S(1)}, u32[]{:S(2)}, u32[]{:S(2)}) async-start(f32[16,1,2176]{2,1,0:T(1,128)} %by_target.1), calls=%async_computation | async-start | bytes 278528 | tf_op jit(solution)/shard_map/cond/branch_1_fun/all_to_all | solution.py:537
  15.4 3.1 %collective-permute-start.1 = (f32[2,128,128]{2,1,0:T(8,128)S(1)}, f32[2,128,128]{2,1,0:T(8,128)}, u32[]{:S(2)}, u32[]{:S(2)}) collective-permute-start(f32[2,128,128]{2,1,0:T(8,128)S(1)} %get-tuple-element.25), channel_id=1, source_target_pairs={{16,17},{17,16},{1,2},{2,1},{18,19},{19,18},{3,4},{4,3},{20,21},{2... | collective-permute-start | bytes 393224 | tf_op jit(solution)/shard_map/cond/branch_1_fun/ppermute | solution.py:527
  18.5 2.4 %all-to-all-done = f32[16,1,2176]{2,1,0:T(1,128)S(1)} async-done(((f32[16,1,2176]{2,1,0:T(1,128)}), f32[16,1,2176]{2,1,0:T(1,128)S(1)}, u32[]{:S(2)}, u32[]{:S(2)}) %all-to-all-start) | async-done | bytes 139296 | tf_op jit(solution)/shard_map/cond/branch_1_fun/all_to_all | solution.py:537
  21.8 1.6 %collective-permute-start = (f32[24,128]{1,0:T(8,128)S(1)}, f32[24,128]{1,0:T(8,128)S(1)}, u32[]{:S(2)}, u32[]{:S(2)}) collective-permute-start(f32[24,128]{1,0:T(8,128)S(1)} %get-tuple-element.24), channel_id=1, source_target_pairs={{0,16},{16,0},{1,17},{17,1},{2,18},{18,2},{3,19},{19,3},{4,20},{20... | collective-permute-start | bytes 36872 | tf_op jit(solution)/shard_map/cond/branch_1_fun/ppermute | solution.py:555
  24.3 5.0 %collective-permute-done.recv = f32[24,128]{1,0:T(8,128)S(1)} collective-permute-done((f32[24,128]{1,0:T(8,128)S(1)}, f32[24,128]{1,0:T(8,128)S(1)}, u32[]{:S(2)}, u32[]{:S(2)}) %collective-permute-start) | collective-permute-done | bytes 12320 | tf_op jit(solution)/shard_map/cond/branch_1_fun/ppermute | solution.py:555
  29.6 1.9 %collective-permute-start.4 = (f32[264,128]{1,0:T(8,128)S(1)}, f32[264,128]{1,0:T(8,128)S(1)}, u32[]{:S(2)}, u32[]{:S(2)}) collective-permute-start(f32[264,128]{1,0:T(8,128)S(1)} %get-tuple-element.168), channel_id=1, source_target_pairs={{16,17},{17,16},{1,2},{2,1},{18,19},{19,18},{3,4},{4,3},{20,21},{2... | collective-permute-start | bytes 405512 | tf_op jit(solution)/shard_map/ppermute | solution.py:589
  31.5 1.6 %collective-permute-start.5 = (f32[264,128]{1,0:T(8,128)S(1)}, f32[264,128]{1,0:T(8,128)S(1)}, u32[]{:S(2)}, u32[]{:S(2)}) collective-permute-start(f32[264,128]{1,0:T(8,128)S(1)} %get-tuple-element.170), channel_id=1, source_target_pairs={{0,16},{16,0},{1,17},{17,1},{2,18},{18,2},{3,19},{19,3},{4,20},{20... | collective-permute-start | bytes 405512 | tf_op jit(solution)/shard_map/ppermute | solution.py:590
  33.1 3.8 %collective-permute-done.4.first_b.got_b = f32[264,128]{1,0:T(8,128)S(1)} collective-permute-done((f32[264,128]{1,0:T(8,128)S(1)}, f32[264,128]{1,0:T(8,128)S(1)}, u32[]{:S(2)}, u32[]{:S(2)}) %collective-permute-start.4) | collective-permute-done | bytes 135200 | tf_op jit(solution)/shard_map/ppermute | solution.py:589
  38.4 1.7 %collective-permute-start.7 = (f32[8,128]{1,0:T(8,128)S(1)}, f32[8,128]{1,0:T(8,128)S(1)}, u32[]{:S(2)}, u32[]{:S(2)}) collective-permute-start(f32[8,128]{1,0:T(8,128)S(1)} %get-tuple-element.176), channel_id=1, source_target_pairs={{0,16},{16,0},{1,17},{17,1},{2,18},{18,2},{3,19},{19,3},{4,20},{20... | collective-permute-start | bytes 12296 | tf_op jit(solution)/shard_map/ppermute | solution.py:590
  40.1 2.3 %collective-permute-start.6 = (f32[8,128]{1,0:T(8,128)S(1)}, f32[8,128]{1,0:T(8,128)S(1)}, u32[]{:S(2)}, u32[]{:S(2)}) collective-permute-start(f32[8,128]{1,0:T(8,128)S(1)} %get-tuple-element.175), channel_id=1, source_target_pairs={{16,17},{17,16},{1,2},{2,1},{18,19},{19,18},{3,4},{4,3},{20,21},{2... | collective-permute-start | bytes 12296 | tf_op jit(solution)/shard_map/ppermute | solution.py:589
  42.9 3.0 %collective-permute-done.6.got_b = f32[8,128]{1,0:T(8,128)S(1)} collective-permute-done((f32[8,128]{1,0:T(8,128)S(1)}, f32[8,128]{1,0:T(8,128)S(1)}, u32[]{:S(2)}, u32[]{:S(2)}) %collective-permute-start.6) | collective-permute-done | bytes 4128 | tf_op jit(solution)/shard_map/ppermute | solution.py:589
  46.5 2.3 %collective-permute-start.8 = (f32[8,128]{1,0:T(8,128)S(1)}, f32[8,128]{1,0:T(8,128)S(1)}, u32[]{:S(2)}, u32[]{:S(2)}) collective-permute-start(f32[8,128]{1,0:T(8,128)S(1)} %get-tuple-element.184), channel_id=1, source_target_pairs={{16,17},{17,16},{1,2},{2,1},{18,19},{19,18},{3,4},{4,3},{20,21},{2... | collective-permute-start | bytes 12296 | tf_op jit(solution)/shard_map/ppermute | solution.py:589
  48.8 1.3 collective-permute-done.9.got_a
  50.5 1.8 %collective-permute-done.8.got_b = f32[8,128]{1,0:T(8,128)S(1)} collective-permute-done((f32[8,128]{1,0:T(8,128)S(1)}, f32[8,128]{1,0:T(8,128)S(1)}, u32[]{:S(2)}, u32[]{:S(2)}) %collective-permute-start.8) | collective-permute-done | bytes 4128 | tf_op jit(solution)/shard_map/ppermute | solution.py:589
  52.9 2.3 %collective-permute-start.10 = (f32[8,128]{1,0:T(8,128)S(1)}, f32[8,128]{1,0:T(8,128)S(1)}, u32[]{:S(2)}, u32[]{:S(2)}) collective-permute-start(f32[8,128]{1,0:T(8,128)S(1)} %get-tuple-element.193), channel_id=1, source_target_pairs={{16,17},{17,16},{1,2},{2,1},{18,19},{19,18},{3,4},{4,3},{20,21},{2... | collective-permute-start | bytes 12296 | tf_op jit(solution)/shard_map/ppermute | solution.py:589
  56.9 1.8 %collective-permute-done.10.got_b = f32[8,128]{1,0:T(8,128)S(1)} collective-permute-done((f32[8,128]{1,0:T(8,128)S(1)}, f32[8,128]{1,0:T(8,128)S(1)}, u32[]{:S(2)}, u32[]{:S(2)}) %collective-permute-start.10) | collective-permute-done | bytes 4128 | tf_op jit(solution)/shard_map/ppermute | solution.py:589
  59.3 2.3 %collective-permute-start.12 = (f32[8,128]{1,0:T(8,128)S(1)}, f32[8,128]{1,0:T(8,128)S(1)}, u32[]{:S(2)}, u32[]{:S(2)}) collective-permute-start(f32[8,128]{1,0:T(8,128)S(1)} %get-tuple-element.203), channel_id=1, source_target_pairs={{16,17},{17,16},{1,2},{2,1},{18,19},{19,18},{3,4},{4,3},{20,21},{2... | collective-permute-start | bytes 12296 | tf_op jit(solution)/shard_map/ppermute | solution.py:589
  63.3 1.8 %collective-permute-done.12.got_b = f32[8,128]{1,0:T(8,128)S(1)} collective-permute-done((f32[8,128]{1,0:T(8,128)S(1)}, f32[8,128]{1,0:T(8,128)S(1)}, u32[]{:S(2)}, u32[]{:S(2)}) %collective-permute-start.12) | collective-permute-done | bytes 4128 | tf_op jit(solution)/shard_map/ppermute | solution.py:589
  65.7 2.3 %collective-permute-start.14 = (f32[8,128]{1,0:T(8,128)S(1)}, f32[8,128]{1,0:T(8,128)S(1)}, u32[]{:S(2)}, u32[]{:S(2)}) collective-permute-start(f32[8,128]{1,0:T(8,128)S(1)} %get-tuple-element.209), channel_id=1, source_target_pairs={{16,17},{17,16},{1,2},{2,1},{18,19},{19,18},{3,4},{4,3},{20,21},{2... | collective-permute-start | bytes 12296 | tf_op jit(solution)/shard_map/ppermute | solution.py:589
  68.0 1.3 collective-permute-done.15.got_a
  69.7 1.8 %collective-permute-done.14.got_b = f32[8,128]{1,0:T(8,128)S(1)} collective-permute-done((f32[8,128]{1,0:T(8,128)S(1)}, f32[8,128]{1,0:T(8,128)S(1)}, u32[]{:S(2)}, u32[]{:S(2)}) %collective-permute-start.14) | collective-permute-done | bytes 4128 | tf_op jit(solution)/shard_map/ppermute | solution.py:589
  72.1 2.3 %collective-permute-start.16 = (f32[8,128]{1,0:T(8,128)S(1)}, f32[8,128]{1,0:T(8,128)S(1)}, u32[]{:S(2)}, u32[]{:S(2)}) collective-permute-start(f32[8,128]{1,0:T(8,128)S(1)} %get-tuple-element.218), channel_id=1, source_target_pairs={{16,17},{17,16},{1,2},{2,1},{18,19},{19,18},{3,4},{4,3},{20,21},{2... | collective-permute-start | bytes 12296 | tf_op jit(solution)/shard_map/ppermute | solution.py:589
  76.1 1.8 %collective-permute-done.16.got_b = f32[8,128]{1,0:T(8,128)S(1)} collective-permute-done((f32[8,128]{1,0:T(8,128)S(1)}, f32[8,128]{1,0:T(8,128)S(1)}, u32[]{:S(2)}, u32[]{:S(2)}) %collective-permute-start.16) | collective-permute-done | bytes 4128 | tf_op jit(solution)/shard_map/ppermute | solution.py:589
  78.5 2.3 %collective-permute-start.18 = (f32[8,128]{1,0:T(8,128)S(1)}, f32[8,128]{1,0:T(8,128)S(1)}, u32[]{:S(2)}, u32[]{:S(2)}) collective-permute-start(f32[8,128]{1,0:T(8,128)S(1)} %get-tuple-element.227), channel_id=1, source_target_pairs={{16,17},{17,16},{1,2},{2,1},{18,19},{19,18},{3,4},{4,3},{20,21},{2... | collective-permute-start | bytes 12296 | tf_op jit(solution)/shard_map/ppermute | solution.py:589
  82.5 1.8 %collective-permute-done.18.got_b = f32[8,128]{1,0:T(8,128)S(1)} collective-permute-done((f32[8,128]{1,0:T(8,128)S(1)}, f32[8,128]{1,0:T(8,128)S(1)}, u32[]{:S(2)}, u32[]{:S(2)}) %collective-permute-start.18) | collective-permute-done | bytes 4128 | tf_op jit(solution)/shard_map/ppermute | solution.py:589
  84.8 2.3 %collective-permute-start.20 = (f32[8,128]{1,0:T(8,128)S(1)}, f32[8,128]{1,0:T(8,128)S(1)}, u32[]{:S(2)}, u32[]{:S(2)}) collective-permute-start(f32[8,128]{1,0:T(8,128)S(1)} %get-tuple-element.237), channel_id=1, source_target_pairs={{16,17},{17,16},{1,2},{2,1},{18,19},{19,18},{3,4},{4,3},{20,21},{2... | collective-permute-start | bytes 12296 | tf_op jit(solution)/shard_map/ppermute | solution.py:589
  88.9 1.8 %collective-permute-done.20.got_b = f32[8,128]{1,0:T(8,128)S(1)} collective-permute-done((f32[8,128]{1,0:T(8,128)S(1)}, f32[8,128]{1,0:T(8,128)S(1)}, u32[]{:S(2)}, u32[]{:S(2)}) %collective-permute-start.20) | collective-permute-done | bytes 4128 | tf_op jit(solution)/shard_map/ppermute | solution.py:589
  91.2 2.3 %collective-permute-start.22 = (f32[8,128]{1,0:T(8,128)S(1)}, f32[8,128]{1,0:T(8,128)S(1)}, u32[]{:S(2)}, u32[]{:S(2)}) collective-permute-start(f32[8,128]{1,0:T(8,128)S(1)} %get-tuple-element.243), channel_id=1, source_target_pairs={{16,17},{17,16},{1,2},{2,1},{18,19},{19,18},{3,4},{4,3},{20,21},{2... | collective-permute-start | bytes 12296 | tf_op jit(solution)/shard_map/ppermute | solution.py:589
  95.3 1.8 %collective-permute-done.22.got_b = f32[8,128]{1,0:T(8,128)S(1)} collective-permute-done((f32[8,128]{1,0:T(8,128)S(1)}, f32[8,128]{1,0:T(8,128)S(1)}, u32[]{:S(2)}, u32[]{:S(2)}) %collective-permute-start.22) | collective-permute-done | bytes 4128 | tf_op jit(solution)/shard_map/ppermute | solution.py:589
  97.6 2.5 %collective-permute-start.24 = (f32[8,128]{1,0:T(8,128)S(1)}, f32[8,128]{1,0:T(8,128)S(1)}, u32[]{:S(2)}, u32[]{:S(2)}) collective-permute-start(f32[8,128]{1,0:T(8,128)S(1)} %get-tuple-element.252), channel_id=1, source_target_pairs={{16,17},{17,16},{1,2},{2,1},{18,19},{19,18},{3,4},{4,3},{20,21},{2... | collective-permute-start | bytes 12296 | tf_op jit(solution)/shard_map/ppermute | solution.py:589
  101.7 1.8 %collective-permute-done.24.got_b = f32[8,128]{1,0:T(8,128)S(1)} collective-permute-done((f32[8,128]{1,0:T(8,128)S(1)}, f32[8,128]{1,0:T(8,128)S(1)}, u32[]{:S(2)}, u32[]{:S(2)}) %collective-permute-start.24) | collective-permute-done | bytes 4128 | tf_op jit(solution)/shard_map/ppermute | solution.py:589
  104.0 2.3 %collective-permute-start.26 = (f32[8,128]{1,0:T(8,128)S(1)}, f32[8,128]{1,0:T(8,128)S(1)}, u32[]{:S(2)}, u32[]{:S(2)}) collective-permute-start(f32[8,128]{1,0:T(8,128)S(1)} %get-tuple-element.261), channel_id=1, source_target_pairs={{16,17},{17,16},{1,2},{2,1},{18,19},{19,18},{3,4},{4,3},{20,21},{2... | collective-permute-start | bytes 12296 | tf_op jit(solution)/shard_map/ppermute | solution.py:589
  108.1 1.8 %collective-permute-done.26.got_b = f32[8,128]{1,0:T(8,128)S(1)} collective-permute-done((f32[8,128]{1,0:T(8,128)S(1)}, f32[8,128]{1,0:T(8,128)S(1)}, u32[]{:S(2)}, u32[]{:S(2)}) %collective-permute-start.26) | collective-permute-done | bytes 4128 | tf_op jit(solution)/shard_map/ppermute | solution.py:589
  110.4 2.3 %collective-permute-start.28 = (f32[8,128]{1,0:T(8,128)S(1)}, f32[8,128]{1,0:T(8,128)S(1)}, u32[]{:S(2)}, u32[]{:S(2)}) collective-permute-start(f32[8,128]{1,0:T(8,128)S(1)} %get-tuple-element.271), channel_id=1, source_target_pairs={{16,17},{17,16},{1,2},{2,1},{18,19},{19,18},{3,4},{4,3},{20,21},{2... | collective-permute-start | bytes 12296 | tf_op jit(solution)/shard_map/ppermute | solution.py:589
  114.4 1.8 %collective-permute-done.28.got_b = f32[8,128]{1,0:T(8,128)S(1)} collective-permute-done((f32[8,128]{1,0:T(8,128)S(1)}, f32[8,128]{1,0:T(8,128)S(1)}, u32[]{:S(2)}, u32[]{:S(2)}) %collective-permute-start.28) | collective-permute-done | bytes 4128 | tf_op jit(solution)/shard_map/ppermute | solution.py:589
  116.8 2.3 %collective-permute-start.30 = (f32[8,128]{1,0:T(8,128)S(1)}, f32[8,128]{1,0:T(8,128)S(1)}, u32[]{:S(2)}, u32[]{:S(2)}) collective-permute-start(f32[8,128]{1,0:T(8,128)S(1)} %get-tuple-element.277), channel_id=1, source_target_pairs={{16,17},{17,16},{1,2},{2,1},{18,19},{19,18},{3,4},{4,3},{20,21},{2... | collective-permute-start | bytes 12296 | tf_op jit(solution)/shard_map/ppermute | solution.py:589
  120.8 1.8 %collective-permute-done.30.got_b = f32[8,128]{1,0:T(8,128)S(1)} collective-permute-done((f32[8,128]{1,0:T(8,128)S(1)}, f32[8,128]{1,0:T(8,128)S(1)}, u32[]{:S(2)}, u32[]{:S(2)}) %collective-permute-start.30) | collective-permute-done | bytes 4128 | tf_op jit(solution)/shard_map/ppermute | solution.py:589
  123.2 2.3 %collective-permute-start.32 = (f32[8,128]{1,0:T(8,128)S(1)}, f32[8,128]{1,0:T(8,128)S(1)}, u32[]{:S(2)}, u32[]{:S(2)}) collective-permute-start(f32[8,128]{1,0:T(8,128)S(1)} %get-tuple-element.286), channel_id=1, source_target_pairs={{16,17},{17,16},{1,2},{2,1},{18,19},{19,18},{3,4},{4,3},{20,21},{2... | collective-permute-start | bytes 12296 | tf_op jit(solution)/shard_map/ppermute | solution.py:589
  127.2 1.8 %collective-permute-done.32.got_b = f32[8,128]{1,0:T(8,128)S(1)} collective-permute-done((f32[8,128]{1,0:T(8,128)S(1)}, f32[8,128]{1,0:T(8,128)S(1)}, u32[]{:S(2)}, u32[]{:S(2)}) %collective-permute-start.32) | collective-permute-done | bytes 4128 | tf_op jit(solution)/shard_map/ppermute | solution.py:589
  129.6 2.3 %collective-permute-start.34 = (f32[8,128]{1,0:T(8,128)S(1)}, f32[8,128]{1,0:T(8,128)S(1)}, u32[]{:S(2)}, u32[]{:S(2)}) collective-permute-start(f32[8,128]{1,0:T(8,128)S(1)} %get-tuple-element.295), channel_id=1, source_target_pairs={{16,17},{17,16},{1,2},{2,1},{18,19},{19,18},{3,4},{4,3},{20,21},{2... | collective-permute-start | bytes 12296 | tf_op jit(solution)/shard_map/ppermute | solution.py:589
  133.6 1.8 %collective-permute-done.34.got_b = f32[8,128]{1,0:T(8,128)S(1)} collective-permute-done((f32[8,128]{1,0:T(8,128)S(1)}, f32[8,128]{1,0:T(8,128)S(1)}, u32[]{:S(2)}, u32[]{:S(2)}) %collective-permute-start.34) | collective-permute-done | bytes 4128 | tf_op jit(solution)/shard_map/ppermute | solution.py:589
  135.9 3.6 %collective-permute-done.36 = f32[4,2,2,128]{3,2,1,0:T(2,128)S(1)} collective-permute-done((f32[4,2,2,128]{3,2,1,0:T(2,128)S(1)}, f32[4,2,2,128]{3,2,1,0:T(2,128)S(1)}, u32[]{:S(2)}, u32[]{:S(2)}) %collective-permute-start.36) | collective-permute-done | bytes 8224 | tf_op jit(solution)/shard_map/ppermute | solution.py:603
  (81 shorter events, 35.1 us)
Async XLA Ops:
  1.3 6.1 %copy-start = (s32[1,1,16,4]{2,3,1,0:T(4,128)S(1)}, s32[1,1,16,4]{2,3,1,0:T(4,128)}, u32[]{:S(2)}) copy-start(s32[1,1,16,4]{2,3,1,0:T(4,128)} %param.15) | copy-start | bytes 772
  1.3 28.1 %collective-permute-start.2 = (f32[12,128,128]{2,1,0:T(8,128)S(1)}, f32[12,128,128]{2,1,0:T(8,128)S(1)}, u32[]{:S(2)}, u32[]{:S(2)}) collective-permute-start(f32[12,128,128]{2,1,0:T(8,128)S(1)} %pack.4), channel_id=1, source_target_pairs={{0,16},{16,0},{1,17},{17,1},{2,18},{18,2},{3,19},{19,3},{4,20},{20... | collective-permute-start | bytes 2359304 | tf_op jit(solution)/shard_map/ppermute | solution.py:521
  4.7 24.6 %collective-permute-start.3 = (f32[6,128,128]{2,1,0:T(8,128)}, f32[6,128,128]{2,1,0:T(8,128)S(1)}, u32[]{:S(2)}, u32[]{:S(2)}) collective-permute-start(f32[6,128,128]{2,1,0:T(8,128)} %pack.5), channel_id=1, source_target_pairs={{0,16},{16,0},{1,17},{17,1},{2,18},{18,2},{3,19},{19,3},{4,20},{20... | collective-permute-start | bytes 1179656 | tf_op jit(solution)/shard_map/ppermute | solution.py:521
  9.1 11.8 %all-to-all-start = ((f32[16,1,2176]{2,1,0:T(1,128)}), f32[16,1,2176]{2,1,0:T(1,128)S(1)}, u32[]{:S(2)}, u32[]{:S(2)}) async-start(f32[16,1,2176]{2,1,0:T(1,128)} %by_target.1), calls=%async_computation | async-start | bytes 278528 | tf_op jit(solution)/shard_map/cond/branch_1_fun/all_to_all | solution.py:537
  15.4 8.0 %collective-permute-start.1 = (f32[2,128,128]{2,1,0:T(8,128)S(1)}, f32[2,128,128]{2,1,0:T(8,128)}, u32[]{:S(2)}, u32[]{:S(2)}) collective-permute-start(f32[2,128,128]{2,1,0:T(8,128)S(1)} %get-tuple-element.25), channel_id=1, source_target_pairs={{16,17},{17,16},{1,2},{2,1},{18,19},{19,18},{3,4},{4,3},{20,21},{2... | collective-permute-start | bytes 393224 | tf_op jit(solution)/shard_map/cond/branch_1_fun/ppermute | solution.py:527
  21.8 7.5 %collective-permute-start = (f32[24,128]{1,0:T(8,128)S(1)}, f32[24,128]{1,0:T(8,128)S(1)}, u32[]{:S(2)}, u32[]{:S(2)}) collective-permute-start(f32[24,128]{1,0:T(8,128)S(1)} %get-tuple-element.24), channel_id=1, source_target_pairs={{0,16},{16,0},{1,17},{17,1},{2,18},{18,2},{3,19},{19,3},{4,20},{20... | collective-permute-start | bytes 36872 | tf_op jit(solution)/shard_map/cond/branch_1_fun/ppermute | solution.py:555
  29.6 7.3 %collective-permute-start.4 = (f32[264,128]{1,0:T(8,128)S(1)}, f32[264,128]{1,0:T(8,128)S(1)}, u32[]{:S(2)}, u32[]{:S(2)}) collective-permute-start(f32[264,128]{1,0:T(8,128)S(1)} %get-tuple-element.168), channel_id=1, source_target_pairs={{16,17},{17,16},{1,2},{2,1},{18,19},{19,18},{3,4},{4,3},{20,21},{2... | collective-permute-start | bytes 405512 | tf_op jit(solution)/shard_map/ppermute | solution.py:589
  31.5 6.0 %collective-permute-start.5 = (f32[264,128]{1,0:T(8,128)S(1)}, f32[264,128]{1,0:T(8,128)S(1)}, u32[]{:S(2)}, u32[]{:S(2)}) collective-permute-start(f32[264,128]{1,0:T(8,128)S(1)} %get-tuple-element.170), channel_id=1, source_target_pairs={{0,16},{16,0},{1,17},{17,1},{2,18},{18,2},{3,19},{19,3},{4,20},{20... | collective-permute-start | bytes 405512 | tf_op jit(solution)/shard_map/ppermute | solution.py:590
  38.4 4.0 %collective-permute-start.7 = (f32[8,128]{1,0:T(8,128)S(1)}, f32[8,128]{1,0:T(8,128)S(1)}, u32[]{:S(2)}, u32[]{:S(2)}) collective-permute-start(f32[8,128]{1,0:T(8,128)S(1)} %get-tuple-element.176), channel_id=1, source_target_pairs={{0,16},{16,0},{1,17},{17,1},{2,18},{18,2},{3,19},{19,3},{4,20},{20... | collective-permute-start | bytes 12296 | tf_op jit(solution)/shard_map/ppermute | solution.py:590
  40.1 5.8 %collective-permute-start.6 = (f32[8,128]{1,0:T(8,128)S(1)}, f32[8,128]{1,0:T(8,128)S(1)}, u32[]{:S(2)}, u32[]{:S(2)}) collective-permute-start(f32[8,128]{1,0:T(8,128)S(1)} %get-tuple-element.175), channel_id=1, source_target_pairs={{16,17},{17,16},{1,2},{2,1},{18,19},{19,18},{3,4},{4,3},{20,21},{2... | collective-permute-start | bytes 12296 | tf_op jit(solution)/shard_map/ppermute | solution.py:589
  46.4 3.7 %collective-permute-start.9 = (f32[8,128]{1,0:T(8,128)S(1)}, f32[8,128]{1,0:T(8,128)S(1)}, u32[]{:S(2)}, u32[]{:S(2)}) collective-permute-start(f32[8,128]{1,0:T(8,128)S(1)} %get-tuple-element.185), channel_id=1, source_target_pairs={{0,16},{16,0},{1,17},{17,1},{2,18},{18,2},{3,19},{19,3},{4,20},{20... | collective-permute-start | bytes 12296 | tf_op jit(solution)/shard_map/ppermute | solution.py:590
  46.5 5.8 %collective-permute-start.8 = (f32[8,128]{1,0:T(8,128)S(1)}, f32[8,128]{1,0:T(8,128)S(1)}, u32[]{:S(2)}, u32[]{:S(2)}) collective-permute-start(f32[8,128]{1,0:T(8,128)S(1)} %get-tuple-element.184), channel_id=1, source_target_pairs={{16,17},{17,16},{1,2},{2,1},{18,19},{19,18},{3,4},{4,3},{20,21},{2... | collective-permute-start | bytes 12296 | tf_op jit(solution)/shard_map/ppermute | solution.py:589
  52.8 3.7 %collective-permute-start.11 = (f32[8,128]{1,0:T(8,128)S(1)}, f32[8,128]{1,0:T(8,128)S(1)}, u32[]{:S(2)}, u32[]{:S(2)}) collective-permute-start(f32[8,128]{1,0:T(8,128)S(1)} %get-tuple-element.194), channel_id=1, source_target_pairs={{0,16},{16,0},{1,17},{17,1},{2,18},{18,2},{3,19},{19,3},{4,20},{20... | collective-permute-start | bytes 12296 | tf_op jit(solution)/shard_map/ppermute | solution.py:590
  52.9 5.8 %collective-permute-start.10 = (f32[8,128]{1,0:T(8,128)S(1)}, f32[8,128]{1,0:T(8,128)S(1)}, u32[]{:S(2)}, u32[]{:S(2)}) collective-permute-start(f32[8,128]{1,0:T(8,128)S(1)} %get-tuple-element.193), channel_id=1, source_target_pairs={{16,17},{17,16},{1,2},{2,1},{18,19},{19,18},{3,4},{4,3},{20,21},{2... | collective-permute-start | bytes 12296 | tf_op jit(solution)/shard_map/ppermute | solution.py:589
  59.2 3.7 %collective-permute-start.13 = (f32[8,128]{1,0:T(8,128)S(1)}, f32[8,128]{1,0:T(8,128)S(1)}, u32[]{:S(2)}, u32[]{:S(2)}) collective-permute-start(f32[8,128]{1,0:T(8,128)S(1)} %get-tuple-element.204), channel_id=1, source_target_pairs={{0,16},{16,0},{1,17},{17,1},{2,18},{18,2},{3,19},{19,3},{4,20},{20... | collective-permute-start | bytes 12296 | tf_op jit(solution)/shard_map/ppermute | solution.py:590
  59.3 5.8 %collective-permute-start.12 = (f32[8,128]{1,0:T(8,128)S(1)}, f32[8,128]{1,0:T(8,128)S(1)}, u32[]{:S(2)}, u32[]{:S(2)}) collective-permute-start(f32[8,128]{1,0:T(8,128)S(1)} %get-tuple-element.203), channel_id=1, source_target_pairs={{16,17},{17,16},{1,2},{2,1},{18,19},{19,18},{3,4},{4,3},{20,21},{2... | collective-permute-start | bytes 12296 | tf_op jit(solution)/shard_map/ppermute | solution.py:589
  65.6 3.7 %collective-permute-start.15 = (f32[8,128]{1,0:T(8,128)S(1)}, f32[8,128]{1,0:T(8,128)S(1)}, u32[]{:S(2)}, u32[]{:S(2)}) collective-permute-start(f32[8,128]{1,0:T(8,128)S(1)} %get-tuple-element.210), channel_id=1, source_target_pairs={{0,16},{16,0},{1,17},{17,1},{2,18},{18,2},{3,19},{19,3},{4,20},{20... | collective-permute-start | bytes 12296 | tf_op jit(solution)/shard_map/ppermute | solution.py:590
  65.7 5.8 %collective-permute-start.14 = (f32[8,128]{1,0:T(8,128)S(1)}, f32[8,128]{1,0:T(8,128)S(1)}, u32[]{:S(2)}, u32[]{:S(2)}) collective-permute-start(f32[8,128]{1,0:T(8,128)S(1)} %get-tuple-element.209), channel_id=1, source_target_pairs={{16,17},{17,16},{1,2},{2,1},{18,19},{19,18},{3,4},{4,3},{20,21},{2... | collective-permute-start | bytes 12296 | tf_op jit(solution)/shard_map/ppermute | solution.py:589
  72.0 3.7 %collective-permute-start.17 = (f32[8,128]{1,0:T(8,128)S(1)}, f32[8,128]{1,0:T(8,128)S(1)}, u32[]{:S(2)}, u32[]{:S(2)}) collective-permute-start(f32[8,128]{1,0:T(8,128)S(1)} %get-tuple-element.219), channel_id=1, source_target_pairs={{0,16},{16,0},{1,17},{17,1},{2,18},{18,2},{3,19},{19,3},{4,20},{20... | collective-permute-start | bytes 12296 | tf_op jit(solution)/shard_map/ppermute | solution.py:590
  72.1 5.8 %collective-permute-start.16 = (f32[8,128]{1,0:T(8,128)S(1)}, f32[8,128]{1,0:T(8,128)S(1)}, u32[]{:S(2)}, u32[]{:S(2)}) collective-permute-start(f32[8,128]{1,0:T(8,128)S(1)} %get-tuple-element.218), channel_id=1, source_target_pairs={{16,17},{17,16},{1,2},{2,1},{18,19},{19,18},{3,4},{4,3},{20,21},{2... | collective-permute-start | bytes 12296 | tf_op jit(solution)/shard_map/ppermute | solution.py:589
  78.4 3.7 %collective-permute-start.19 = (f32[8,128]{1,0:T(8,128)S(1)}, f32[8,128]{1,0:T(8,128)S(1)}, u32[]{:S(2)}, u32[]{:S(2)}) collective-permute-start(f32[8,128]{1,0:T(8,128)S(1)} %get-tuple-element.228), channel_id=1, source_target_pairs={{0,16},{16,0},{1,17},{17,1},{2,18},{18,2},{3,19},{19,3},{4,20},{20... | collective-permute-start | bytes 12296 | tf_op jit(solution)/shard_map/ppermute | solution.py:590
  78.5 5.8 %collective-permute-start.18 = (f32[8,128]{1,0:T(8,128)S(1)}, f32[8,128]{1,0:T(8,128)S(1)}, u32[]{:S(2)}, u32[]{:S(2)}) collective-permute-start(f32[8,128]{1,0:T(8,128)S(1)} %get-tuple-element.227), channel_id=1, source_target_pairs={{16,17},{17,16},{1,2},{2,1},{18,19},{19,18},{3,4},{4,3},{20,21},{2... | collective-permute-start | bytes 12296 | tf_op jit(solution)/shard_map/ppermute | solution.py:589
  84.8 3.7 %collective-permute-start.21 = (f32[8,128]{1,0:T(8,128)S(1)}, f32[8,128]{1,0:T(8,128)S(1)}, u32[]{:S(2)}, u32[]{:S(2)}) collective-permute-start(f32[8,128]{1,0:T(8,128)S(1)} %get-tuple-element.238), channel_id=1, source_target_pairs={{0,16},{16,0},{1,17},{17,1},{2,18},{18,2},{3,19},{19,3},{4,20},{20... | collective-permute-start | bytes 12296 | tf_op jit(solution)/shard_map/ppermute | solution.py:590
  84.8 5.8 %collective-permute-start.20 = (f32[8,128]{1,0:T(8,128)S(1)}, f32[8,128]{1,0:T(8,128)S(1)}, u32[]{:S(2)}, u32[]{:S(2)}) collective-permute-start(f32[8,128]{1,0:T(8,128)S(1)} %get-tuple-element.237), channel_id=1, source_target_pairs={{16,17},{17,16},{1,2},{2,1},{18,19},{19,18},{3,4},{4,3},{20,21},{2... | collective-permute-start | bytes 12296 | tf_op jit(solution)/shard_map/ppermute | solution.py:589
  91.2 3.7 %collective-permute-start.23 = (f32[8,128]{1,0:T(8,128)S(1)}, f32[8,128]{1,0:T(8,128)S(1)}, u32[]{:S(2)}, u32[]{:S(2)}) collective-permute-start(f32[8,128]{1,0:T(8,128)S(1)} %get-tuple-element.244), channel_id=1, source_target_pairs={{0,16},{16,0},{1,17},{17,1},{2,18},{18,2},{3,19},{19,3},{4,20},{20... | collective-permute-start | bytes 12296 | tf_op jit(solution)/shard_map/ppermute | solution.py:590
  91.2 5.8 %collective-permute-start.22 = (f32[8,128]{1,0:T(8,128)S(1)}, f32[8,128]{1,0:T(8,128)S(1)}, u32[]{:S(2)}, u32[]{:S(2)}) collective-permute-start(f32[8,128]{1,0:T(8,128)S(1)} %get-tuple-element.243), channel_id=1, source_target_pairs={{16,17},{17,16},{1,2},{2,1},{18,19},{19,18},{3,4},{4,3},{20,21},{2... | collective-permute-start | bytes 12296 | tf_op jit(solution)/shard_map/ppermute | solution.py:589
  97.6 3.7 %collective-permute-start.25 = (f32[8,128]{1,0:T(8,128)S(1)}, f32[8,128]{1,0:T(8,128)S(1)}, u32[]{:S(2)}, u32[]{:S(2)}) collective-permute-start(f32[8,128]{1,0:T(8,128)S(1)} %get-tuple-element.253), channel_id=1, source_target_pairs={{0,16},{16,0},{1,17},{17,1},{2,18},{18,2},{3,19},{19,3},{4,20},{20... | collective-permute-start | bytes 12296 | tf_op jit(solution)/shard_map/ppermute | solution.py:590
  97.6 5.8 %collective-permute-start.24 = (f32[8,128]{1,0:T(8,128)S(1)}, f32[8,128]{1,0:T(8,128)S(1)}, u32[]{:S(2)}, u32[]{:S(2)}) collective-permute-start(f32[8,128]{1,0:T(8,128)S(1)} %get-tuple-element.252), channel_id=1, source_target_pairs={{16,17},{17,16},{1,2},{2,1},{18,19},{19,18},{3,4},{4,3},{20,21},{2... | collective-permute-start | bytes 12296 | tf_op jit(solution)/shard_map/ppermute | solution.py:589
  103.9 3.7 %collective-permute-start.27 = (f32[8,128]{1,0:T(8,128)S(1)}, f32[8,128]{1,0:T(8,128)S(1)}, u32[]{:S(2)}, u32[]{:S(2)}) collective-permute-start(f32[8,128]{1,0:T(8,128)S(1)} %get-tuple-element.262), channel_id=1, source_target_pairs={{0,16},{16,0},{1,17},{17,1},{2,18},{18,2},{3,19},{19,3},{4,20},{20... | collective-permute-start | bytes 12296 | tf_op jit(solution)/shard_map/ppermute | solution.py:590
  104.0 5.8 %collective-permute-start.26 = (f32[8,128]{1,0:T(8,128)S(1)}, f32[8,128]{1,0:T(8,128)S(1)}, u32[]{:S(2)}, u32[]{:S(2)}) collective-permute-start(f32[8,128]{1,0:T(8,128)S(1)} %get-tuple-element.261), channel_id=1, source_target_pairs={{16,17},{17,16},{1,2},{2,1},{18,19},{19,18},{3,4},{4,3},{20,21},{2... | collective-permute-start | bytes 12296 | tf_op jit(solution)/shard_map/ppermute | solution.py:589
  110.3 3.7 %collective-permute-start.29 = (f32[8,128]{1,0:T(8,128)S(1)}, f32[8,128]{1,0:T(8,128)S(1)}, u32[]{:S(2)}, u32[]{:S(2)}) collective-permute-start(f32[8,128]{1,0:T(8,128)S(1)} %get-tuple-element.272), channel_id=1, source_target_pairs={{0,16},{16,0},{1,17},{17,1},{2,18},{18,2},{3,19},{19,3},{4,20},{20... | collective-permute-start | bytes 12296 | tf_op jit(solution)/shard_map/ppermute | solution.py:590
  110.4 5.8 %collective-permute-start.28 = (f32[8,128]{1,0:T(8,128)S(1)}, f32[8,128]{1,0:T(8,128)S(1)}, u32[]{:S(2)}, u32[]{:S(2)}) collective-permute-start(f32[8,128]{1,0:T(8,128)S(1)} %get-tuple-element.271), channel_id=1, source_target_pairs={{16,17},{17,16},{1,2},{2,1},{18,19},{19,18},{3,4},{4,3},{20,21},{2... | collective-permute-start | bytes 12296 | tf_op jit(solution)/shard_map/ppermute | solution.py:589
  116.7 3.7 %collective-permute-start.31 = (f32[8,128]{1,0:T(8,128)S(1)}, f32[8,128]{1,0:T(8,128)S(1)}, u32[]{:S(2)}, u32[]{:S(2)}) collective-permute-start(f32[8,128]{1,0:T(8,128)S(1)} %get-tuple-element.278), channel_id=1, source_target_pairs={{0,16},{16,0},{1,17},{17,1},{2,18},{18,2},{3,19},{19,3},{4,20},{20... | collective-permute-start | bytes 12296 | tf_op jit(solution)/shard_map/ppermute | solution.py:590
  116.8 5.8 %collective-permute-start.30 = (f32[8,128]{1,0:T(8,128)S(1)}, f32[8,128]{1,0:T(8,128)S(1)}, u32[]{:S(2)}, u32[]{:S(2)}) collective-permute-start(f32[8,128]{1,0:T(8,128)S(1)} %get-tuple-element.277), channel_id=1, source_target_pairs={{16,17},{17,16},{1,2},{2,1},{18,19},{19,18},{3,4},{4,3},{20,21},{2... | collective-permute-start | bytes 12296 | tf_op jit(solution)/shard_map/ppermute | solution.py:589
  123.1 3.7 %collective-permute-start.33 = (f32[8,128]{1,0:T(8,128)S(1)}, f32[8,128]{1,0:T(8,128)S(1)}, u32[]{:S(2)}, u32[]{:S(2)}) collective-permute-start(f32[8,128]{1,0:T(8,128)S(1)} %get-tuple-element.287), channel_id=1, source_target_pairs={{0,16},{16,0},{1,17},{17,1},{2,18},{18,2},{3,19},{19,3},{4,20},{20... | collective-permute-start | bytes 12296 | tf_op jit(solution)/shard_map/ppermute | solution.py:590
  123.2 5.8 %collective-permute-start.32 = (f32[8,128]{1,0:T(8,128)S(1)}, f32[8,128]{1,0:T(8,128)S(1)}, u32[]{:S(2)}, u32[]{:S(2)}) collective-permute-start(f32[8,128]{1,0:T(8,128)S(1)} %get-tuple-element.286), channel_id=1, source_target_pairs={{16,17},{17,16},{1,2},{2,1},{18,19},{19,18},{3,4},{4,3},{20,21},{2... | collective-permute-start | bytes 12296 | tf_op jit(solution)/shard_map/ppermute | solution.py:589
  129.5 3.7 %collective-permute-start.35 = (f32[8,128]{1,0:T(8,128)S(1)}, f32[8,128]{1,0:T(8,128)S(1)}, u32[]{:S(2)}, u32[]{:S(2)}) collective-permute-start(f32[8,128]{1,0:T(8,128)S(1)} %get-tuple-element.296), channel_id=1, source_target_pairs={{0,16},{16,0},{1,17},{17,1},{2,18},{18,2},{3,19},{19,3},{4,20},{20... | collective-permute-start | bytes 12296 | tf_op jit(solution)/shard_map/ppermute | solution.py:590
  129.6 5.8 %collective-permute-start.34 = (f32[8,128]{1,0:T(8,128)S(1)}, f32[8,128]{1,0:T(8,128)S(1)}, u32[]{:S(2)}, u32[]{:S(2)}) collective-permute-start(f32[8,128]{1,0:T(8,128)S(1)} %get-tuple-element.295), channel_id=1, source_target_pairs={{16,17},{17,16},{1,2},{2,1},{18,19},{19,18},{3,4},{4,3},{20,21},{2... | collective-permute-start | bytes 12296 | tf_op jit(solution)/shard_map/ppermute | solution.py:589
  135.8 3.7 %collective-permute-start.36 = (f32[4,2,2,128]{3,2,1,0:T(2,128)S(1)}, f32[4,2,2,128]{3,2,1,0:T(2,128)S(1)}, u32[]{:S(2)}, u32[]{:S(2)}) collective-permute-start(f32[4,2,2,128]{3,2,1,0:T(2,128)S(1)} %rev.12), channel_id=1, source_target_pairs={{0,16},{16,0},{1,17},{17,1},{2,18},{18,2},{3,19},{19,3},{4,20},{20... | collective-permute-start | bytes 24584 | tf_op jit(solution)/shard_map/ppermute | solution.py:603

commit v16 on v15

--- a/solution.py
+++ b/solution.py
@@ -282,7 +282,7 @@
     return lambda g, n: first[start + g:start + g + n, :]
 
 
-def matvec(terms, chunk=32):
+def matvec(terms, chunk=64):
     width = terms[0][1].shape[1]
     lane = lax.broadcasted_iota(jnp.int32, (chunk, width), 1)
     sub = lax.broadcasted_iota(jnp.int32, (chunk, width), 0)

time: 141 us -> 141 us (level)
  no operation moved by 1% of the time
where the time goes in v16:
time: 141 us; the launch traced here: 140 us
  waiting for transfers between devices  61.2 us (43%)
  starting transfers between devices  54.4 us (39%)
  Pallas kernels  21.9 us (16%)
    ppermute x16, starting transfers between devices, shards_chain(): got_b = lax.ppermute(msg_b, both, b_pairs)  37 us
    ppermute x16, waiting for transfers between devices, shards_chain(): got_b = lax.ppermute(msg_b, both, b_pairs)  32.1 us
    ppermute x16, waiting for transfers between devices, shards_chain(): got_a = lax.ppermute(msg_a, 'row', swap)  18 us
    pallas_call x33, Pallas kernels, call(): pl.pallas_call(body, out_shape=outs, in_specs=[vmem] * len(ins), out_spec...  14.7 us
    all_to_all x1, starting transfers between devices, beside(): lax.all_to_all(by_target, 'col', split_axis=0, concat_axis=0, tiled=True)  6.27 us
    ppermute x1, waiting for transfers between devices, beside(): lax.ppermute(send, 'row', swap)  5.02 us
    pallas_call x3, Pallas kernels, pack(): pl.pallas_call(functools.partial(pack_kernel, n_col, sent, first, count),...  4.61 us
    ppermute x16, starting transfers between devices, shards_chain(): got_a = lax.ppermute(msg_a, 'row', swap)  4.26 us
  transfers between devices with their start and end apart: 38, of which 34 were waited for; matrix products, arithmetic and copies ran while one was open for 1% of the time, Pallas kernels for 9%

profile of v16, /device:TPU:8, one launch (start us, length us, event | category | flops | bytes accessed | tf_op | source)
XLA Modules:
  0.0 140.3 jit_solution(4906966036004859350)
XLA Ops:
  0.0 1.3 pack.4
  1.3 1.6 %collective-permute-start.2 = (f32[12,128,128]{2,1,0:T(8,128)S(1)}, f32[12,128,128]{2,1,0:T(8,128)S(1)}, u32[]{:S(2)}, u32[]{:S(2)}) collective-permute-start(f32[12,128,128]{2,1,0:T(8,128)S(1)} %pack.4), channel_id=1, source_target_pairs={{0,16},{16,0},{1,17},{17,1},{2,18},{18,2},{3,19},{19,3},{4,20},{20... | collective-permute-start | bytes 2359304 | tf_op jit(solution)/shard_map/ppermute | solution.py:521
  2.9 1.8 %pack.5 = f32[6,128,128]{2,1,0:T(8,128)} custom-call(s32[2,4,4]{2,1,0:T(4,128)} %pattern_hbm.5, f32[2,4,128,128]{3,2,1,0:T(8,128)} %own_hbm.5, f32[4,2,4,128,128]{4,3,2,1,0:T(8,128)} %nb_hbm.5), custom_call_target="tpu_custom_call" | custom-call | tf_op jit(solution)/shard_map/pack/pallas_call | solution.py:508
  5.3 1.5 %pack.3 = (f32[20,128,128]{2,1,0:T(8,128)S(1)}, f32[2,128,128]{2,1,0:T(8,128)S(1)}) custom-call(s32[2,4,4]{2,1,0:T(4,128)} %pattern_hbm.5, f32[2,4,128,128]{3,2,1,0:T(8,128)} %own_hbm.5, f32[4,2,4,128,128]{4,3,2,1,0:T(8,128)} %nb_hbm.5), custom_call_target="tpu_custom_call" | custom-call | tf_op jit(solution)/shard_map/pack/pallas_call | solution.py:508
  7.4 21.9 %conditional.1 = (f32[48,128]{1,0:T(8,128)S(1)}, f32[2,128,128]{2,1,0:T(8,128)S(1)}) conditional(s32[]{:T(128)} %convert_element_type.3, f32[2,128,128]{2,1,0:T(8,128)S(1)} %get-tuple-element.166, (f32[1,1,16,4,512]{4,3,2,1,0:T(4,128)}, s32[1,1,16,4]{2,3,1,0:T(4,128)S(1)}, s32[2]{0:T(128)}, f32[2,4,128]{2,1,0:T(4,128)}, f32[2,4,128]{2,1,0:T(4,128)}, ...), branch_computations={%region_0.1_spmd, %region_1.2_spmd} | conditional | bytes 1532544 | solution.py:558
  7.5 1.6 %by_target.1 = f32[16,1,2176]{2,1,0:T(1,128)} custom-call(f32[16,4,512]{2,1,0:T(4,128)} %bitcast.16, s32[16,4]{1,0:T(8,128)S(1)} %copy.14.slot_tile), custom_call_target="tpu_custom_call" | custom-call | tf_op jit(solution)/shard_map/cond/branch_1_fun/by_target/pallas_call | solution.py:529
  9.1 6.3 %all-to-all-start = ((f32[16,1,2176]{2,1,0:T(1,128)}), f32[16,1,2176]{2,1,0:T(1,128)S(1)}, u32[]{:S(2)}, u32[]{:S(2)}) async-start(f32[16,1,2176]{2,1,0:T(1,128)} %by_target.1), calls=%async_computation | async-start | bytes 278528 | tf_op jit(solution)/shard_map/cond/branch_1_fun/all_to_all | solution.py:537
  15.4 3.1 %collective-permute-start.1 = (f32[2,128,128]{2,1,0:T(8,128)S(1)}, f32[2,128,128]{2,1,0:T(8,128)}, u32[]{:S(2)}, u32[]{:S(2)}) collective-permute-start(f32[2,128,128]{2,1,0:T(8,128)S(1)} %get-tuple-element.25), channel_id=1, source_target_pairs={{16,17},{17,16},{1,2},{2,1},{18,19},{19,18},{3,4},{4,3},{20,21},{2... | collective-permute-start | bytes 393224 | tf_op jit(solution)/shard_map/cond/branch_1_fun/ppermute | solution.py:527
  18.5 2.4 %all-to-all-done = f32[16,1,2176]{2,1,0:T(1,128)S(1)} async-done(((f32[16,1,2176]{2,1,0:T(1,128)}), f32[16,1,2176]{2,1,0:T(1,128)S(1)}, u32[]{:S(2)}, u32[]{:S(2)}) %all-to-all-start) | async-done | bytes 139296 | tf_op jit(solution)/shard_map/cond/branch_1_fun/all_to_all | solution.py:537
  21.8 1.6 %collective-permute-start = (f32[24,128]{1,0:T(8,128)S(1)}, f32[24,128]{1,0:T(8,128)S(1)}, u32[]{:S(2)}, u32[]{:S(2)}) collective-permute-start(f32[24,128]{1,0:T(8,128)S(1)} %get-tuple-element.24), channel_id=1, source_target_pairs={{0,16},{16,0},{1,17},{17,1},{2,18},{18,2},{3,19},{19,3},{4,20},{20... | collective-permute-start | bytes 36872 | tf_op jit(solution)/shard_map/cond/branch_1_fun/ppermute | solution.py:555
  24.3 5.0 %collective-permute-done.recv = f32[24,128]{1,0:T(8,128)S(1)} collective-permute-done((f32[24,128]{1,0:T(8,128)S(1)}, f32[24,128]{1,0:T(8,128)S(1)}, u32[]{:S(2)}, u32[]{:S(2)}) %collective-permute-start) | collective-permute-done | bytes 12320 | tf_op jit(solution)/shard_map/cond/branch_1_fun/ppermute | solution.py:555
  29.6 1.9 %collective-permute-start.4 = (f32[264,128]{1,0:T(8,128)S(1)}, f32[264,128]{1,0:T(8,128)S(1)}, u32[]{:S(2)}, u32[]{:S(2)}) collective-permute-start(f32[264,128]{1,0:T(8,128)S(1)} %get-tuple-element.168), channel_id=1, source_target_pairs={{16,17},{17,16},{1,2},{2,1},{18,19},{19,18},{3,4},{4,3},{20,21},{2... | collective-permute-start | bytes 405512 | tf_op jit(solution)/shard_map/ppermute | solution.py:589
  31.5 1.6 %collective-permute-start.5 = (f32[264,128]{1,0:T(8,128)S(1)}, f32[264,128]{1,0:T(8,128)S(1)}, u32[]{:S(2)}, u32[]{:S(2)}) collective-permute-start(f32[264,128]{1,0:T(8,128)S(1)} %get-tuple-element.170), channel_id=1, source_target_pairs={{0,16},{16,0},{1,17},{17,1},{2,18},{18,2},{3,19},{19,3},{4,20},{20... | collective-permute-start | bytes 405512 | tf_op jit(solution)/shard_map/ppermute | solution.py:590
  33.1 3.8 %collective-permute-done.4.first_b.got_b = f32[264,128]{1,0:T(8,128)S(1)} collective-permute-done((f32[264,128]{1,0:T(8,128)S(1)}, f32[264,128]{1,0:T(8,128)S(1)}, u32[]{:S(2)}, u32[]{:S(2)}) %collective-permute-start.4) | collective-permute-done | bytes 135200 | tf_op jit(solution)/shard_map/ppermute | solution.py:589
  38.4 1.7 %collective-permute-start.7 = (f32[8,128]{1,0:T(8,128)S(1)}, f32[8,128]{1,0:T(8,128)S(1)}, u32[]{:S(2)}, u32[]{:S(2)}) collective-permute-start(f32[8,128]{1,0:T(8,128)S(1)} %get-tuple-element.176), channel_id=1, source_target_pairs={{0,16},{16,0},{1,17},{17,1},{2,18},{18,2},{3,19},{19,3},{4,20},{20... | collective-permute-start | bytes 12296 | tf_op jit(solution)/shard_map/ppermute | solution.py:590
  40.1 2.3 %collective-permute-start.6 = (f32[8,128]{1,0:T(8,128)S(1)}, f32[8,128]{1,0:T(8,128)S(1)}, u32[]{:S(2)}, u32[]{:S(2)}) collective-permute-start(f32[8,128]{1,0:T(8,128)S(1)} %get-tuple-element.175), channel_id=1, source_target_pairs={{16,17},{17,16},{1,2},{2,1},{18,19},{19,18},{3,4},{4,3},{20,21},{2... | collective-permute-start | bytes 12296 | tf_op jit(solution)/shard_map/ppermute | solution.py:589
  42.8 3.0 %collective-permute-done.6.got_b = f32[8,128]{1,0:T(8,128)S(1)} collective-permute-done((f32[8,128]{1,0:T(8,128)S(1)}, f32[8,128]{1,0:T(8,128)S(1)}, u32[]{:S(2)}, u32[]{:S(2)}) %collective-permute-start.6) | collective-permute-done | bytes 4128 | tf_op jit(solution)/shard_map/ppermute | solution.py:589
  46.5 2.3 %collective-permute-start.8 = (f32[8,128]{1,0:T(8,128)S(1)}, f32[8,128]{1,0:T(8,128)S(1)}, u32[]{:S(2)}, u32[]{:S(2)}) collective-permute-start(f32[8,128]{1,0:T(8,128)S(1)} %get-tuple-element.184), channel_id=1, source_target_pairs={{16,17},{17,16},{1,2},{2,1},{18,19},{19,18},{3,4},{4,3},{20,21},{2... | collective-permute-start | bytes 12296 | tf_op jit(solution)/shard_map/ppermute | solution.py:589
  50.5 1.8 %collective-permute-done.8.got_b = f32[8,128]{1,0:T(8,128)S(1)} collective-permute-done((f32[8,128]{1,0:T(8,128)S(1)}, f32[8,128]{1,0:T(8,128)S(1)}, u32[]{:S(2)}, u32[]{:S(2)}) %collective-permute-start.8) | collective-permute-done | bytes 4128 | tf_op jit(solution)/shard_map/ppermute | solution.py:589
  52.9 2.3 %collective-permute-start.10 = (f32[8,128]{1,0:T(8,128)S(1)}, f32[8,128]{1,0:T(8,128)S(1)}, u32[]{:S(2)}, u32[]{:S(2)}) collective-permute-start(f32[8,128]{1,0:T(8,128)S(1)} %get-tuple-element.193), channel_id=1, source_target_pairs={{16,17},{17,16},{1,2},{2,1},{18,19},{19,18},{3,4},{4,3},{20,21},{2... | collective-permute-start | bytes 12296 | tf_op jit(solution)/shard_map/ppermute | solution.py:589
  56.9 1.8 %collective-permute-done.10.got_b = f32[8,128]{1,0:T(8,128)S(1)} collective-permute-done((f32[8,128]{1,0:T(8,128)S(1)}, f32[8,128]{1,0:T(8,128)S(1)}, u32[]{:S(2)}, u32[]{:S(2)}) %collective-permute-start.10) | collective-permute-done | bytes 4128 | tf_op jit(solution)/shard_map/ppermute | solution.py:589
  59.3 2.3 %collective-permute-start.12 = (f32[8,128]{1,0:T(8,128)S(1)}, f32[8,128]{1,0:T(8,128)S(1)}, u32[]{:S(2)}, u32[]{:S(2)}) collective-permute-start(f32[8,128]{1,0:T(8,128)S(1)} %get-tuple-element.203), channel_id=1, source_target_pairs={{16,17},{17,16},{1,2},{2,1},{18,19},{19,18},{3,4},{4,3},{20,21},{2... | collective-permute-start | bytes 12296 | tf_op jit(solution)/shard_map/ppermute | solution.py:589
  63.3 1.8 %collective-permute-done.12.got_b = f32[8,128]{1,0:T(8,128)S(1)} collective-permute-done((f32[8,128]{1,0:T(8,128)S(1)}, f32[8,128]{1,0:T(8,128)S(1)}, u32[]{:S(2)}, u32[]{:S(2)}) %collective-permute-start.12) | collective-permute-done | bytes 4128 | tf_op jit(solution)/shard_map/ppermute | solution.py:589
  65.7 2.3 %collective-permute-start.14 = (f32[8,128]{1,0:T(8,128)S(1)}, f32[8,128]{1,0:T(8,128)S(1)}, u32[]{:S(2)}, u32[]{:S(2)}) collective-permute-start(f32[8,128]{1,0:T(8,128)S(1)} %get-tuple-element.209), channel_id=1, source_target_pairs={{16,17},{17,16},{1,2},{2,1},{18,19},{19,18},{3,4},{4,3},{20,21},{2... | collective-permute-start | bytes 12296 | tf_op jit(solution)/shard_map/ppermute | solution.py:589
  68.0 1.3 collective-permute-done.15.got_a
  69.7 1.8 %collective-permute-done.14.got_b = f32[8,128]{1,0:T(8,128)S(1)} collective-permute-done((f32[8,128]{1,0:T(8,128)S(1)}, f32[8,128]{1,0:T(8,128)S(1)}, u32[]{:S(2)}, u32[]{:S(2)}) %collective-permute-start.14) | collective-permute-done | bytes 4128 | tf_op jit(solution)/shard_map/ppermute | solution.py:589
  72.1 2.3 %collective-permute-start.16 = (f32[8,128]{1,0:T(8,128)S(1)}, f32[8,128]{1,0:T(8,128)S(1)}, u32[]{:S(2)}, u32[]{:S(2)}) collective-permute-start(f32[8,128]{1,0:T(8,128)S(1)} %get-tuple-element.218), channel_id=1, source_target_pairs={{16,17},{17,16},{1,2},{2,1},{18,19},{19,18},{3,4},{4,3},{20,21},{2... | collective-permute-start | bytes 12296 | tf_op jit(solution)/shard_map/ppermute | solution.py:589
  74.4 1.3 collective-permute-done.17.got_a
  76.1 1.8 %collective-permute-done.16.got_b = f32[8,128]{1,0:T(8,128)S(1)} collective-permute-done((f32[8,128]{1,0:T(8,128)S(1)}, f32[8,128]{1,0:T(8,128)S(1)}, u32[]{:S(2)}, u32[]{:S(2)}) %collective-permute-start.16) | collective-permute-done | bytes 4128 | tf_op jit(solution)/shard_map/ppermute | solution.py:589
  78.5 2.3 %collective-permute-start.18 = (f32[8,128]{1,0:T(8,128)S(1)}, f32[8,128]{1,0:T(8,128)S(1)}, u32[]{:S(2)}, u32[]{:S(2)}) collective-permute-start(f32[8,128]{1,0:T(8,128)S(1)} %get-tuple-element.227), channel_id=1, source_target_pairs={{16,17},{17,16},{1,2},{2,1},{18,19},{19,18},{3,4},{4,3},{20,21},{2... | collective-permute-start | bytes 12296 | tf_op jit(solution)/shard_map/ppermute | solution.py:589
  82.5 1.8 %collective-permute-done.18.got_b = f32[8,128]{1,0:T(8,128)S(1)} collective-permute-done((f32[8,128]{1,0:T(8,128)S(1)}, f32[8,128]{1,0:T(8,128)S(1)}, u32[]{:S(2)}, u32[]{:S(2)}) %collective-permute-start.18) | collective-permute-done | bytes 4128 | tf_op jit(solution)/shard_map/ppermute | solution.py:589
  84.9 2.3 %collective-permute-start.20 = (f32[8,128]{1,0:T(8,128)S(1)}, f32[8,128]{1,0:T(8,128)S(1)}, u32[]{:S(2)}, u32[]{:S(2)}) collective-permute-start(f32[8,128]{1,0:T(8,128)S(1)} %get-tuple-element.237), channel_id=1, source_target_pairs={{16,17},{17,16},{1,2},{2,1},{18,19},{19,18},{3,4},{4,3},{20,21},{2... | collective-permute-start | bytes 12296 | tf_op jit(solution)/shard_map/ppermute | solution.py:589
  88.9 1.8 %collective-permute-done.20.got_b = f32[8,128]{1,0:T(8,128)S(1)} collective-permute-done((f32[8,128]{1,0:T(8,128)S(1)}, f32[8,128]{1,0:T(8,128)S(1)}, u32[]{:S(2)}, u32[]{:S(2)}) %collective-permute-start.20) | collective-permute-done | bytes 4128 | tf_op jit(solution)/shard_map/ppermute | solution.py:589
  91.3 2.3 %collective-permute-start.22 = (f32[8,128]{1,0:T(8,128)S(1)}, f32[8,128]{1,0:T(8,128)S(1)}, u32[]{:S(2)}, u32[]{:S(2)}) collective-permute-start(f32[8,128]{1,0:T(8,128)S(1)} %get-tuple-element.243), channel_id=1, source_target_pairs={{16,17},{17,16},{1,2},{2,1},{18,19},{19,18},{3,4},{4,3},{20,21},{2... | collective-permute-start | bytes 12296 | tf_op jit(solution)/shard_map/ppermute | solution.py:589
  95.3 1.8 %collective-permute-done.22.got_b = f32[8,128]{1,0:T(8,128)S(1)} collective-permute-done((f32[8,128]{1,0:T(8,128)S(1)}, f32[8,128]{1,0:T(8,128)S(1)}, u32[]{:S(2)}, u32[]{:S(2)}) %collective-permute-start.22) | collective-permute-done | bytes 4128 | tf_op jit(solution)/shard_map/ppermute | solution.py:589
  97.7 2.5 %collective-permute-start.24 = (f32[8,128]{1,0:T(8,128)S(1)}, f32[8,128]{1,0:T(8,128)S(1)}, u32[]{:S(2)}, u32[]{:S(2)}) collective-permute-start(f32[8,128]{1,0:T(8,128)S(1)} %get-tuple-element.252), channel_id=1, source_target_pairs={{16,17},{17,16},{1,2},{2,1},{18,19},{19,18},{3,4},{4,3},{20,21},{2... | collective-permute-start | bytes 12296 | tf_op jit(solution)/shard_map/ppermute | solution.py:589
  101.7 1.8 %collective-permute-done.24.got_b = f32[8,128]{1,0:T(8,128)S(1)} collective-permute-done((f32[8,128]{1,0:T(8,128)S(1)}, f32[8,128]{1,0:T(8,128)S(1)}, u32[]{:S(2)}, u32[]{:S(2)}) %collective-permute-start.24) | collective-permute-done | bytes 4128 | tf_op jit(solution)/shard_map/ppermute | solution.py:589
  104.1 2.3 %collective-permute-start.26 = (f32[8,128]{1,0:T(8,128)S(1)}, f32[8,128]{1,0:T(8,128)S(1)}, u32[]{:S(2)}, u32[]{:S(2)}) collective-permute-start(f32[8,128]{1,0:T(8,128)S(1)} %get-tuple-element.261), channel_id=1, source_target_pairs={{16,17},{17,16},{1,2},{2,1},{18,19},{19,18},{3,4},{4,3},{20,21},{2... | collective-permute-start | bytes 12296 | tf_op jit(solution)/shard_map/ppermute | solution.py:589
  108.1 1.8 %collective-permute-done.26.got_b = f32[8,128]{1,0:T(8,128)S(1)} collective-permute-done((f32[8,128]{1,0:T(8,128)S(1)}, f32[8,128]{1,0:T(8,128)S(1)}, u32[]{:S(2)}, u32[]{:S(2)}) %collective-permute-start.26) | collective-permute-done | bytes 4128 | tf_op jit(solution)/shard_map/ppermute | solution.py:589
  110.5 2.3 %collective-permute-start.28 = (f32[8,128]{1,0:T(8,128)S(1)}, f32[8,128]{1,0:T(8,128)S(1)}, u32[]{:S(2)}, u32[]{:S(2)}) collective-permute-start(f32[8,128]{1,0:T(8,128)S(1)} %get-tuple-element.271), channel_id=1, source_target_pairs={{16,17},{17,16},{1,2},{2,1},{18,19},{19,18},{3,4},{4,3},{20,21},{2... | collective-permute-start | bytes 12296 | tf_op jit(solution)/shard_map/ppermute | solution.py:589
  114.5 1.8 %collective-permute-done.28.got_b = f32[8,128]{1,0:T(8,128)S(1)} collective-permute-done((f32[8,128]{1,0:T(8,128)S(1)}, f32[8,128]{1,0:T(8,128)S(1)}, u32[]{:S(2)}, u32[]{:S(2)}) %collective-permute-start.28) | collective-permute-done | bytes 4128 | tf_op jit(solution)/shard_map/ppermute | solution.py:589
  116.9 2.3 %collective-permute-start.30 = (f32[8,128]{1,0:T(8,128)S(1)}, f32[8,128]{1,0:T(8,128)S(1)}, u32[]{:S(2)}, u32[]{:S(2)}) collective-permute-start(f32[8,128]{1,0:T(8,128)S(1)} %get-tuple-element.277), channel_id=1, source_target_pairs={{16,17},{17,16},{1,2},{2,1},{18,19},{19,18},{3,4},{4,3},{20,21},{2... | collective-permute-start | bytes 12296 | tf_op jit(solution)/shard_map/ppermute | solution.py:589
  120.9 1.8 %collective-permute-done.30.got_b = f32[8,128]{1,0:T(8,128)S(1)} collective-permute-done((f32[8,128]{1,0:T(8,128)S(1)}, f32[8,128]{1,0:T(8,128)S(1)}, u32[]{:S(2)}, u32[]{:S(2)}) %collective-permute-start.30) | collective-permute-done | bytes 4128 | tf_op jit(solution)/shard_map/ppermute | solution.py:589
  123.3 2.3 %collective-permute-start.32 = (f32[8,128]{1,0:T(8,128)S(1)}, f32[8,128]{1,0:T(8,128)S(1)}, u32[]{:S(2)}, u32[]{:S(2)}) collective-permute-start(f32[8,128]{1,0:T(8,128)S(1)} %get-tuple-element.286), channel_id=1, source_target_pairs={{16,17},{17,16},{1,2},{2,1},{18,19},{19,18},{3,4},{4,3},{20,21},{2... | collective-permute-start | bytes 12296 | tf_op jit(solution)/shard_map/ppermute | solution.py:589
  127.3 1.8 %collective-permute-done.32.got_b = f32[8,128]{1,0:T(8,128)S(1)} collective-permute-done((f32[8,128]{1,0:T(8,128)S(1)}, f32[8,128]{1,0:T(8,128)S(1)}, u32[]{:S(2)}, u32[]{:S(2)}) %collective-permute-start.32) | collective-permute-done | bytes 4128 | tf_op jit(solution)/shard_map/ppermute | solution.py:589
  129.7 2.3 %collective-permute-start.34 = (f32[8,128]{1,0:T(8,128)S(1)}, f32[8,128]{1,0:T(8,128)S(1)}, u32[]{:S(2)}, u32[]{:S(2)}) collective-permute-start(f32[8,128]{1,0:T(8,128)S(1)} %get-tuple-element.295), channel_id=1, source_target_pairs={{16,17},{17,16},{1,2},{2,1},{18,19},{19,18},{3,4},{4,3},{20,21},{2... | collective-permute-start | bytes 12296 | tf_op jit(solution)/shard_map/ppermute | solution.py:589
  133.7 1.8 %collective-permute-done.34.got_b = f32[8,128]{1,0:T(8,128)S(1)} collective-permute-done((f32[8,128]{1,0:T(8,128)S(1)}, f32[8,128]{1,0:T(8,128)S(1)}, u32[]{:S(2)}, u32[]{:S(2)}) %collective-permute-start.34) | collective-permute-done | bytes 4128 | tf_op jit(solution)/shard_map/ppermute | solution.py:589
  136.0 3.6 %collective-permute-done.36 = f32[4,2,2,128]{3,2,1,0:T(2,128)S(1)} collective-permute-done((f32[4,2,2,128]{3,2,1,0:T(2,128)S(1)}, f32[4,2,2,128]{3,2,1,0:T(2,128)S(1)}, u32[]{:S(2)}, u32[]{:S(2)}) %collective-permute-start.36) | collective-permute-done | bytes 8224 | tf_op jit(solution)/shard_map/ppermute | solution.py:603
  (81 shorter events, 35.1 us)
Async XLA Ops:
  1.3 6.1 %copy-start = (s32[1,1,16,4]{2,3,1,0:T(4,128)S(1)}, s32[1,1,16,4]{2,3,1,0:T(4,128)}, u32[]{:S(2)}) copy-start(s32[1,1,16,4]{2,3,1,0:T(4,128)} %param.15) | copy-start | bytes 772
  1.3 28.1 %collective-permute-start.2 = (f32[12,128,128]{2,1,0:T(8,128)S(1)}, f32[12,128,128]{2,1,0:T(8,128)S(1)}, u32[]{:S(2)}, u32[]{:S(2)}) collective-permute-start(f32[12,128,128]{2,1,0:T(8,128)S(1)} %pack.4), channel_id=1, source_target_pairs={{0,16},{16,0},{1,17},{17,1},{2,18},{18,2},{3,19},{19,3},{4,20},{20... | collective-permute-start | bytes 2359304 | tf_op jit(solution)/shard_map/ppermute | solution.py:521
  4.7 24.6 %collective-permute-start.3 = (f32[6,128,128]{2,1,0:T(8,128)}, f32[6,128,128]{2,1,0:T(8,128)S(1)}, u32[]{:S(2)}, u32[]{:S(2)}) collective-permute-start(f32[6,128,128]{2,1,0:T(8,128)} %pack.5), channel_id=1, source_target_pairs={{0,16},{16,0},{1,17},{17,1},{2,18},{18,2},{3,19},{19,3},{4,20},{20... | collective-permute-start | bytes 1179656 | tf_op jit(solution)/shard_map/ppermute | solution.py:521
  9.1 11.8 %all-to-all-start = ((f32[16,1,2176]{2,1,0:T(1,128)}), f32[16,1,2176]{2,1,0:T(1,128)S(1)}, u32[]{:S(2)}, u32[]{:S(2)}) async-start(f32[16,1,2176]{2,1,0:T(1,128)} %by_target.1), calls=%async_computation | async-start | bytes 278528 | tf_op jit(solution)/shard_map/cond/branch_1_fun/all_to_all | solution.py:537
  15.4 8.0 %collective-permute-start.1 = (f32[2,128,128]{2,1,0:T(8,128)S(1)}, f32[2,128,128]{2,1,0:T(8,128)}, u32[]{:S(2)}, u32[]{:S(2)}) collective-permute-start(f32[2,128,128]{2,1,0:T(8,128)S(1)} %get-tuple-element.25), channel_id=1, source_target_pairs={{16,17},{17,16},{1,2},{2,1},{18,19},{19,18},{3,4},{4,3},{20,21},{2... | collective-permute-start | bytes 393224 | tf_op jit(solution)/shard_map/cond/branch_1_fun/ppermute | solution.py:527
  21.8 7.5 %collective-permute-start = (f32[24,128]{1,0:T(8,128)S(1)}, f32[24,128]{1,0:T(8,128)S(1)}, u32[]{:S(2)}, u32[]{:S(2)}) collective-permute-start(f32[24,128]{1,0:T(8,128)S(1)} %get-tuple-element.24), channel_id=1, source_target_pairs={{0,16},{16,0},{1,17},{17,1},{2,18},{18,2},{3,19},{19,3},{4,20},{20... | collective-permute-start | bytes 36872 | tf_op jit(solution)/shard_map/cond/branch_1_fun/ppermute | solution.py:555
  29.6 7.3 %collective-permute-start.4 = (f32[264,128]{1,0:T(8,128)S(1)}, f32[264,128]{1,0:T(8,128)S(1)}, u32[]{:S(2)}, u32[]{:S(2)}) collective-permute-start(f32[264,128]{1,0:T(8,128)S(1)} %get-tuple-element.168), channel_id=1, source_target_pairs={{16,17},{17,16},{1,2},{2,1},{18,19},{19,18},{3,4},{4,3},{20,21},{2... | collective-permute-start | bytes 405512 | tf_op jit(solution)/shard_map/ppermute | solution.py:589
  31.5 6.0 %collective-permute-start.5 = (f32[264,128]{1,0:T(8,128)S(1)}, f32[264,128]{1,0:T(8,128)S(1)}, u32[]{:S(2)}, u32[]{:S(2)}) collective-permute-start(f32[264,128]{1,0:T(8,128)S(1)} %get-tuple-element.170), channel_id=1, source_target_pairs={{0,16},{16,0},{1,17},{17,1},{2,18},{18,2},{3,19},{19,3},{4,20},{20... | collective-permute-start | bytes 405512 | tf_op jit(solution)/shard_map/ppermute | solution.py:590
  38.4 4.0 %collective-permute-start.7 = (f32[8,128]{1,0:T(8,128)S(1)}, f32[8,128]{1,0:T(8,128)S(1)}, u32[]{:S(2)}, u32[]{:S(2)}) collective-permute-start(f32[8,128]{1,0:T(8,128)S(1)} %get-tuple-element.176), channel_id=1, source_target_pairs={{0,16},{16,0},{1,17},{17,1},{2,18},{18,2},{3,19},{19,3},{4,20},{20... | collective-permute-start | bytes 12296 | tf_op jit(solution)/shard_map/ppermute | solution.py:590
  40.1 5.8 %collective-permute-start.6 = (f32[8,128]{1,0:T(8,128)S(1)}, f32[8,128]{1,0:T(8,128)S(1)}, u32[]{:S(2)}, u32[]{:S(2)}) collective-permute-start(f32[8,128]{1,0:T(8,128)S(1)} %get-tuple-element.175), channel_id=1, source_target_pairs={{16,17},{17,16},{1,2},{2,1},{18,19},{19,18},{3,4},{4,3},{20,21},{2... | collective-permute-start | bytes 12296 | tf_op jit(solution)/shard_map/ppermute | solution.py:589
  46.4 3.7 %collective-permute-start.9 = (f32[8,128]{1,0:T(8,128)S(1)}, f32[8,128]{1,0:T(8,128)S(1)}, u32[]{:S(2)}, u32[]{:S(2)}) collective-permute-start(f32[8,128]{1,0:T(8,128)S(1)} %get-tuple-element.185), channel_id=1, source_target_pairs={{0,16},{16,0},{1,17},{17,1},{2,18},{18,2},{3,19},{19,3},{4,20},{20... | collective-permute-start | bytes 12296 | tf_op jit(solution)/shard_map/ppermute | solution.py:590
  46.5 5.8 %collective-permute-start.8 = (f32[8,128]{1,0:T(8,128)S(1)}, f32[8,128]{1,0:T(8,128)S(1)}, u32[]{:S(2)}, u32[]{:S(2)}) collective-permute-start(f32[8,128]{1,0:T(8,128)S(1)} %get-tuple-element.184), channel_id=1, source_target_pairs={{16,17},{17,16},{1,2},{2,1},{18,19},{19,18},{3,4},{4,3},{20,21},{2... | collective-permute-start | bytes 12296 | tf_op jit(solution)/shard_map/ppermute | solution.py:589
  52.8 3.7 %collective-permute-start.11 = (f32[8,128]{1,0:T(8,128)S(1)}, f32[8,128]{1,0:T(8,128)S(1)}, u32[]{:S(2)}, u32[]{:S(2)}) collective-permute-start(f32[8,128]{1,0:T(8,128)S(1)} %get-tuple-element.194), channel_id=1, source_target_pairs={{0,16},{16,0},{1,17},{17,1},{2,18},{18,2},{3,19},{19,3},{4,20},{20... | collective-permute-start | bytes 12296 | tf_op jit(solution)/shard_map/ppermute | solution.py:590
  52.9 5.8 %collective-permute-start.10 = (f32[8,128]{1,0:T(8,128)S(1)}, f32[8,128]{1,0:T(8,128)S(1)}, u32[]{:S(2)}, u32[]{:S(2)}) collective-permute-start(f32[8,128]{1,0:T(8,128)S(1)} %get-tuple-element.193), channel_id=1, source_target_pairs={{16,17},{17,16},{1,2},{2,1},{18,19},{19,18},{3,4},{4,3},{20,21},{2... | collective-permute-start | bytes 12296 | tf_op jit(solution)/shard_map/ppermute | solution.py:589
  59.2 3.7 %collective-permute-start.13 = (f32[8,128]{1,0:T(8,128)S(1)}, f32[8,128]{1,0:T(8,128)S(1)}, u32[]{:S(2)}, u32[]{:S(2)}) collective-permute-start(f32[8,128]{1,0:T(8,128)S(1)} %get-tuple-element.204), channel_id=1, source_target_pairs={{0,16},{16,0},{1,17},{17,1},{2,18},{18,2},{3,19},{19,3},{4,20},{20... | collective-permute-start | bytes 12296 | tf_op jit(solution)/shard_map/ppermute | solution.py:590
  59.3 5.8 %collective-permute-start.12 = (f32[8,128]{1,0:T(8,128)S(1)}, f32[8,128]{1,0:T(8,128)S(1)}, u32[]{:S(2)}, u32[]{:S(2)}) collective-permute-start(f32[8,128]{1,0:T(8,128)S(1)} %get-tuple-element.203), channel_id=1, source_target_pairs={{16,17},{17,16},{1,2},{2,1},{18,19},{19,18},{3,4},{4,3},{20,21},{2... | collective-permute-start | bytes 12296 | tf_op jit(solution)/shard_map/ppermute | solution.py:589
  65.6 3.7 %collective-permute-start.15 = (f32[8,128]{1,0:T(8,128)S(1)}, f32[8,128]{1,0:T(8,128)S(1)}, u32[]{:S(2)}, u32[]{:S(2)}) collective-permute-start(f32[8,128]{1,0:T(8,128)S(1)} %get-tuple-element.210), channel_id=1, source_target_pairs={{0,16},{16,0},{1,17},{17,1},{2,18},{18,2},{3,19},{19,3},{4,20},{20... | collective-permute-start | bytes 12296 | tf_op jit(solution)/shard_map/ppermute | solution.py:590
  65.7 5.8 %collective-permute-start.14 = (f32[8,128]{1,0:T(8,128)S(1)}, f32[8,128]{1,0:T(8,128)S(1)}, u32[]{:S(2)}, u32[]{:S(2)}) collective-permute-start(f32[8,128]{1,0:T(8,128)S(1)} %get-tuple-element.209), channel_id=1, source_target_pairs={{16,17},{17,16},{1,2},{2,1},{18,19},{19,18},{3,4},{4,3},{20,21},{2... | collective-permute-start | bytes 12296 | tf_op jit(solution)/shard_map/ppermute | solution.py:589
  72.0 3.7 %collective-permute-start.17 = (f32[8,128]{1,0:T(8,128)S(1)}, f32[8,128]{1,0:T(8,128)S(1)}, u32[]{:S(2)}, u32[]{:S(2)}) collective-permute-start(f32[8,128]{1,0:T(8,128)S(1)} %get-tuple-element.219), channel_id=1, source_target_pairs={{0,16},{16,0},{1,17},{17,1},{2,18},{18,2},{3,19},{19,3},{4,20},{20... | collective-permute-start | bytes 12296 | tf_op jit(solution)/shard_map/ppermute | solution.py:590
  72.1 5.8 %collective-permute-start.16 = (f32[8,128]{1,0:T(8,128)S(1)}, f32[8,128]{1,0:T(8,128)S(1)}, u32[]{:S(2)}, u32[]{:S(2)}) collective-permute-start(f32[8,128]{1,0:T(8,128)S(1)} %get-tuple-element.218), channel_id=1, source_target_pairs={{16,17},{17,16},{1,2},{2,1},{18,19},{19,18},{3,4},{4,3},{20,21},{2... | collective-permute-start | bytes 12296 | tf_op jit(solution)/shard_map/ppermute | solution.py:589
  78.4 3.7 %collective-permute-start.19 = (f32[8,128]{1,0:T(8,128)S(1)}, f32[8,128]{1,0:T(8,128)S(1)}, u32[]{:S(2)}, u32[]{:S(2)}) collective-permute-start(f32[8,128]{1,0:T(8,128)S(1)} %get-tuple-element.228), channel_id=1, source_target_pairs={{0,16},{16,0},{1,17},{17,1},{2,18},{18,2},{3,19},{19,3},{4,20},{20... | collective-permute-start | bytes 12296 | tf_op jit(solution)/shard_map/ppermute | solution.py:590
  78.5 5.8 %collective-permute-start.18 = (f32[8,128]{1,0:T(8,128)S(1)}, f32[8,128]{1,0:T(8,128)S(1)}, u32[]{:S(2)}, u32[]{:S(2)}) collective-permute-start(f32[8,128]{1,0:T(8,128)S(1)} %get-tuple-element.227), channel_id=1, source_target_pairs={{16,17},{17,16},{1,2},{2,1},{18,19},{19,18},{3,4},{4,3},{20,21},{2... | collective-permute-start | bytes 12296 | tf_op jit(solution)/shard_map/ppermute | solution.py:589
  84.8 3.7 %collective-permute-start.21 = (f32[8,128]{1,0:T(8,128)S(1)}, f32[8,128]{1,0:T(8,128)S(1)}, u32[]{:S(2)}, u32[]{:S(2)}) collective-permute-start(f32[8,128]{1,0:T(8,128)S(1)} %get-tuple-element.238), channel_id=1, source_target_pairs={{0,16},{16,0},{1,17},{17,1},{2,18},{18,2},{3,19},{19,3},{4,20},{20... | collective-permute-start | bytes 12296 | tf_op jit(solution)/shard_map/ppermute | solution.py:590
  84.9 5.8 %collective-permute-start.20 = (f32[8,128]{1,0:T(8,128)S(1)}, f32[8,128]{1,0:T(8,128)S(1)}, u32[]{:S(2)}, u32[]{:S(2)}) collective-permute-start(f32[8,128]{1,0:T(8,128)S(1)} %get-tuple-element.237), channel_id=1, source_target_pairs={{16,17},{17,16},{1,2},{2,1},{18,19},{19,18},{3,4},{4,3},{20,21},{2... | collective-permute-start | bytes 12296 | tf_op jit(solution)/shard_map/ppermute | solution.py:589
  91.2 3.7 %collective-permute-start.23 = (f32[8,128]{1,0:T(8,128)S(1)}, f32[8,128]{1,0:T(8,128)S(1)}, u32[]{:S(2)}, u32[]{:S(2)}) collective-permute-start(f32[8,128]{1,0:T(8,128)S(1)} %get-tuple-element.244), channel_id=1, source_target_pairs={{0,16},{16,0},{1,17},{17,1},{2,18},{18,2},{3,19},{19,3},{4,20},{20... | collective-permute-start | bytes 12296 | tf_op jit(solution)/shard_map/ppermute | solution.py:590
  91.3 5.8 %collective-permute-start.22 = (f32[8,128]{1,0:T(8,128)S(1)}, f32[8,128]{1,0:T(8,128)S(1)}, u32[]{:S(2)}, u32[]{:S(2)}) collective-permute-start(f32[8,128]{1,0:T(8,128)S(1)} %get-tuple-element.243), channel_id=1, source_target_pairs={{16,17},{17,16},{1,2},{2,1},{18,19},{19,18},{3,4},{4,3},{20,21},{2... | collective-permute-start | bytes 12296 | tf_op jit(solution)/shard_map/ppermute | solution.py:589
  97.6 3.7 %collective-permute-start.25 = (f32[8,128]{1,0:T(8,128)S(1)}, f32[8,128]{1,0:T(8,128)S(1)}, u32[]{:S(2)}, u32[]{:S(2)}) collective-permute-start(f32[8,128]{1,0:T(8,128)S(1)} %get-tuple-element.253), channel_id=1, source_target_pairs={{0,16},{16,0},{1,17},{17,1},{2,18},{18,2},{3,19},{19,3},{4,20},{20... | collective-permute-start | bytes 12296 | tf_op jit(solution)/shard_map/ppermute | solution.py:590
  97.7 5.8 %collective-permute-start.24 = (f32[8,128]{1,0:T(8,128)S(1)}, f32[8,128]{1,0:T(8,128)S(1)}, u32[]{:S(2)}, u32[]{:S(2)}) collective-permute-start(f32[8,128]{1,0:T(8,128)S(1)} %get-tuple-element.252), channel_id=1, source_target_pairs={{16,17},{17,16},{1,2},{2,1},{18,19},{19,18},{3,4},{4,3},{20,21},{2... | collective-permute-start | bytes 12296 | tf_op jit(solution)/shard_map/ppermute | solution.py:589
  104.0 3.7 %collective-permute-start.27 = (f32[8,128]{1,0:T(8,128)S(1)}, f32[8,128]{1,0:T(8,128)S(1)}, u32[]{:S(2)}, u32[]{:S(2)}) collective-permute-start(f32[8,128]{1,0:T(8,128)S(1)} %get-tuple-element.262), channel_id=1, source_target_pairs={{0,16},{16,0},{1,17},{17,1},{2,18},{18,2},{3,19},{19,3},{4,20},{20... | collective-permute-start | bytes 12296 | tf_op jit(solution)/shard_map/ppermute | solution.py:590
  104.1 5.8 %collective-permute-start.26 = (f32[8,128]{1,0:T(8,128)S(1)}, f32[8,128]{1,0:T(8,128)S(1)}, u32[]{:S(2)}, u32[]{:S(2)}) collective-permute-start(f32[8,128]{1,0:T(8,128)S(1)} %get-tuple-element.261), channel_id=1, source_target_pairs={{16,17},{17,16},{1,2},{2,1},{18,19},{19,18},{3,4},{4,3},{20,21},{2... | collective-permute-start | bytes 12296 | tf_op jit(solution)/shard_map/ppermute | solution.py:589
  110.4 3.7 %collective-permute-start.29 = (f32[8,128]{1,0:T(8,128)S(1)}, f32[8,128]{1,0:T(8,128)S(1)}, u32[]{:S(2)}, u32[]{:S(2)}) collective-permute-start(f32[8,128]{1,0:T(8,128)S(1)} %get-tuple-element.272), channel_id=1, source_target_pairs={{0,16},{16,0},{1,17},{17,1},{2,18},{18,2},{3,19},{19,3},{4,20},{20... | collective-permute-start | bytes 12296 | tf_op jit(solution)/shard_map/ppermute | solution.py:590
  110.5 5.8 %collective-permute-start.28 = (f32[8,128]{1,0:T(8,128)S(1)}, f32[8,128]{1,0:T(8,128)S(1)}, u32[]{:S(2)}, u32[]{:S(2)}) collective-permute-start(f32[8,128]{1,0:T(8,128)S(1)} %get-tuple-element.271), channel_id=1, source_target_pairs={{16,17},{17,16},{1,2},{2,1},{18,19},{19,18},{3,4},{4,3},{20,21},{2... | collective-permute-start | bytes 12296 | tf_op jit(solution)/shard_map/ppermute | solution.py:589
  116.8 3.7 %collective-permute-start.31 = (f32[8,128]{1,0:T(8,128)S(1)}, f32[8,128]{1,0:T(8,128)S(1)}, u32[]{:S(2)}, u32[]{:S(2)}) collective-permute-start(f32[8,128]{1,0:T(8,128)S(1)} %get-tuple-element.278), channel_id=1, source_target_pairs={{0,16},{16,0},{1,17},{17,1},{2,18},{18,2},{3,19},{19,3},{4,20},{20... | collective-permute-start | bytes 12296 | tf_op jit(solution)/shard_map/ppermute | solution.py:590
  116.9 5.8 %collective-permute-start.30 = (f32[8,128]{1,0:T(8,128)S(1)}, f32[8,128]{1,0:T(8,128)S(1)}, u32[]{:S(2)}, u32[]{:S(2)}) collective-permute-start(f32[8,128]{1,0:T(8,128)S(1)} %get-tuple-element.277), channel_id=1, source_target_pairs={{16,17},{17,16},{1,2},{2,1},{18,19},{19,18},{3,4},{4,3},{20,21},{2... | collective-permute-start | bytes 12296 | tf_op jit(solution)/shard_map/ppermute | solution.py:589
  123.2 3.7 %collective-permute-start.33 = (f32[8,128]{1,0:T(8,128)S(1)}, f32[8,128]{1,0:T(8,128)S(1)}, u32[]{:S(2)}, u32[]{:S(2)}) collective-permute-start(f32[8,128]{1,0:T(8,128)S(1)} %get-tuple-element.287), channel_id=1, source_target_pairs={{0,16},{16,0},{1,17},{17,1},{2,18},{18,2},{3,19},{19,3},{4,20},{20... | collective-permute-start | bytes 12296 | tf_op jit(solution)/shard_map/ppermute | solution.py:590
  123.3 5.8 %collective-permute-start.32 = (f32[8,128]{1,0:T(8,128)S(1)}, f32[8,128]{1,0:T(8,128)S(1)}, u32[]{:S(2)}, u32[]{:S(2)}) collective-permute-start(f32[8,128]{1,0:T(8,128)S(1)} %get-tuple-element.286), channel_id=1, source_target_pairs={{16,17},{17,16},{1,2},{2,1},{18,19},{19,18},{3,4},{4,3},{20,21},{2... | collective-permute-start | bytes 12296 | tf_op jit(solution)/shard_map/ppermute | solution.py:589
  129.6 3.7 %collective-permute-start.35 = (f32[8,128]{1,0:T(8,128)S(1)}, f32[8,128]{1,0:T(8,128)S(1)}, u32[]{:S(2)}, u32[]{:S(2)}) collective-permute-start(f32[8,128]{1,0:T(8,128)S(1)} %get-tuple-element.296), channel_id=1, source_target_pairs={{0,16},{16,0},{1,17},{17,1},{2,18},{18,2},{3,19},{19,3},{4,20},{20... | collective-permute-start | bytes 12296 | tf_op jit(solution)/shard_map/ppermute | solution.py:590
  129.7 5.8 %collective-permute-start.34 = (f32[8,128]{1,0:T(8,128)S(1)}, f32[8,128]{1,0:T(8,128)S(1)}, u32[]{:S(2)}, u32[]{:S(2)}) collective-permute-start(f32[8,128]{1,0:T(8,128)S(1)} %get-tuple-element.295), channel_id=1, source_target_pairs={{16,17},{17,16},{1,2},{2,1},{18,19},{19,18},{3,4},{4,3},{20,21},{2... | collective-permute-start | bytes 12296 | tf_op jit(solution)/shard_map/ppermute | solution.py:589
  135.9 3.7 %collective-permute-start.36 = (f32[4,2,2,128]{3,2,1,0:T(2,128)S(1)}, f32[4,2,2,128]{3,2,1,0:T(2,128)S(1)}, u32[]{:S(2)}, u32[]{:S(2)}) collective-permute-start(f32[4,2,2,128]{3,2,1,0:T(2,128)S(1)} %rev.12), channel_id=1, source_target_pairs={{0,16},{16,0},{1,17},{17,1},{2,18},{18,2},{3,19},{19,3},{4,20},{20... | collective-permute-start | bytes 24584 | tf_op jit(solution)/shard_map/ppermute | solution.py:603

commit v17 on v16

--- a/solution.py
+++ b/solution.py
@@ -189,11 +189,11 @@
 
 ROWS, HALF = 2, 2
 N = 2 * ROWS
-OWN, SIDE_A, SIDE_B, OUT_IN, IN_OUT, IN_IN, FACING, PACKED = 0, 4, 8, 12, 14, 16, 18, 20
+OWN, SIDE_B, ACROSS, OUT_IN, IN_OUT, IN_IN, EDGE_A, FACING, PACKED = 0, 4, 8, 10, 12, 14, 16, 18, 20
 TILES = [(j, b) for j in range(N) for b in range(HALF)]
 ORIGIN = [(0, 0), (0, 1), (1, 1), (1, 0)]
 CAPACITY, INITIAL = STEPS, STEPS + 1
-SPLIT = ((PACKED,), (OUT_IN, FACING - OUT_IN))
+SPLIT = ((PACKED,), (OUT_IN, EDGE_A - OUT_IN))
 
 
 def unit_device(unit, n_col):
@@ -211,7 +211,7 @@
     for h in range(ROWS):
         for b in range(HALF):
             tiles[OWN + h * HALF + b] = (None, rows[h], at[b], None)
-            tiles[SIDE_A + h * HALF + b] = (3 - k, rows[h], at[b], None)
+            tiles[(EDGE_A if b == 1 else ACROSS) + h] = (3 - k, rows[h], at[b], None)
             tiles[SIDE_B + h * HALF + b] = (2 + k, rows[h], at[b], inside if b == 0 else None)
         tiles[FACING + h] = (2 + k, rows[h], HALF - k, None)
     for b in range(HALF):
@@ -264,13 +264,18 @@
     else:
         terms.append((IN_OUT + b, ((0, 3)[i], b)))
         terms.append((IN_IN + b, ((2, 1)[i], b)))
-    terms.append(((SIDE_A if b == 0 else SIDE_B) + h * HALF + b, (j, 1 - b)))
+    terms.append((ACROSS + h if b == 0 else SIDE_B + h * HALF + b, (j, 1 - b)))
     return [(half_block(halves, i, slot), at) for slot, at in terms]
 
 
-def halo_block(halves, j, b):
+def halo_block(halves, first_a, j, b):
     i, h = ORIGIN[j]
-    return half_block(halves, i, (SIDE_B if b == 0 else SIDE_A) + h * HALF + b)
+    if b == 0:
+        return half_block(halves, i, SIDE_B + h * HALF)
+    if i == 0:
+        return half_block(halves, i, EDGE_A + h)
+    start = 2 * N + (ROWS + h) * first_a.shape[1]
+    return lambda g, n: first_a[start + g:start + g + n, :]
 
 
 def facing_block(halves, beyond_0, first_a, first_b, j, b):
@@ -347,7 +352,7 @@
         small[2 * i + n + HALF:2 * i + 2 * n, :] = recv[i:i + HALF, :]
 
 
-def start_kernel(keep, recv_0, recv_1, small, msg_a, msg_b, q_out):
+def start_kernel(keep, recv_0, recv_1, small, edge, msg_a, msg_b, q_out):
     halves = ((keep,), (recv_0, recv_1))
     f = small_part(small, INITIAL)
     q = inner_product(f, halves)
@@ -358,7 +363,8 @@
     width = small.shape[1]
     for h in range(ROWS):
         start = 2 * N + h * width
-        msg_a[start:start + width, :] = keep[SIDE_A + h * HALF + 1]
+        msg_a[start:start + width, :] = keep[EDGE_A + h]
+        msg_a[start + ROWS * width:start + (ROWS + 1) * width, :] = edge[h]
         msg_b[start:start + width, :] = recv_0[SIDE_B + h * HALF]
 
 
@@ -373,8 +379,8 @@
         out[d, :, slots * frames:] = names[d:d + 1, :]
 
 
-def small_kernel(place_ref, arrived, capacity, initial, keep, send, injected):
-    y, col = place_ref[0], place_ref[1]
+def small_kernel(arrived, capacity, initial, keep, send, injected):
+    y, col = lax.axis_index("row"), lax.axis_index("col")
     tiles, frames = injected.shape
     _, cols, width = capacity.shape
     slots = (arrived.shape[1] - width) // frames
@@ -414,7 +420,7 @@
     residue = None if pair == 0 else rows_of(refs[1])
     product = rows_of(q_ref)
     for j in range(N):
-        product[tile(j, 1)] += matvec([(halo_block(halves, j, 1), got_a[j:j + 1, :])])
+        product[tile(j, 1)] += matvec([(halo_block(halves, first_a, j, 1), got_a[j:j + 1, :])])
     put(product_out, product)
     response = [
         matvec([(facing_block(halves, beyond_0, first_a, first_b, j, b), f[tile(j, b)])]) for j, b in TILES
@@ -426,7 +432,7 @@
         terms = products(tile_terms(halves, j, b), f2)
         if b == 1:
             beside = got_a[N + j:N + j + 1, :] - scale * response[tile(j, b)]
-            part.append(matvec(terms[:-1] + [(halo_block(halves, j, b), beside)]))
+            part.append(matvec(terms[:-1] + [(halo_block(halves, first_a, j, b), beside)]))
         else:
             part.append(matvec(terms[-1:]))
     put(part_out, part)
@@ -446,7 +452,7 @@
 
     product = rows_of(product_ref)
     for j in range(N):
-        product[tile(j, 0)] += matvec([(halo_block(halves, j, 0), got_b[j:j + 1, :])])
+        product[tile(j, 0)] += matvec([(halo_block(halves, None, j, 0), got_b[j:j + 1, :])])
     residue, f2, scale = advance(instant, pair, small, product, f, residue)
     if first:
         estimate = each(lambda v, p: v + STRIDES[0] * p, f, f2)
@@ -459,7 +465,7 @@
         terms = products(tile_terms(halves, j, b), f2)
         if b == 0:
             beside = got_b[N + j:N + j + 1, :] - scale * response[i:i + 1, :]
-            total[i] += matvec(terms[:-1] + [(halo_block(halves, j, b), beside)])
+            total[i] += matvec(terms[:-1] + [(halo_block(halves, None, j, b), beside)])
         else:
             total[i] += matvec(terms[-1:])
     sweep = 2 * pair
@@ -498,10 +504,8 @@
     parity = (row + col) % 2
 
     vmem = pl.BlockSpec(memory_space=pltpu.VMEM)
-    smem = pl.BlockSpec(memory_space=pltpu.SMEM)
     hbm = pl.BlockSpec(memory_space=pltpu.HBM)
     limit = pltpu.CompilerParams(vmem_limit_bytes=16 * 2**20)
-    place = jnp.stack([row, col]).astype(jnp.int32)
     blocks = [pltpu.with_memory_space_constraint(x, pltpu.HBM) for x in (pattern, own_block, neighbor_block)]
 
     def pack(sent, first, count, extra=()):
@@ -520,6 +524,7 @@
         (send,) = pack(1, first, count)
         recv.append(lax.ppermute(send, "row", swap))
     keep, facing_0 = pack(0, 0, PACKED, (ROWS,))
+    (edge,) = pack(1, EDGE_A, ROWS)
 
     unit_small = jax.ShapeDtypeStruct(((STEPS + 2) * N * HALF, width), jnp.float32)
 
@@ -539,12 +544,12 @@
         small, send = pl.pallas_call(
             small_kernel,
             out_shape=(half, half),
-            in_specs=[smem, vmem, vmem, vmem],
+            in_specs=[vmem] * 3,
             out_specs=(vmem, vmem),
             scratch_shapes=[pltpu.VMEM((tile_rows * tile_cols, frames), jnp.float32)],
             compiler_params=limit,
             name="small",
-        )(place, arrived.reshape(n_col, slots * frames + width), capacity, initial)
+        )(arrived.reshape(n_col, slots * frames + width), capacity, initial)
         small = pl.pallas_call(
             join_kernel,
             out_shape=unit_small,
@@ -580,7 +585,8 @@
         )(*ins)
 
     first_shape = jax.ShapeDtypeStruct((2 * N + ROWS * width, width), jnp.float32)
-    msg_a, msg_b, q = call(start_kernel, (first_shape, first_shape, shape), 28, *halves, small)
+    first_a_shape = jax.ShapeDtypeStruct((2 * N + 2 * ROWS * width, width), jnp.float32)
+    msg_a, msg_b, q = call(start_kernel, (first_a_shape, first_shape, shape), 28, *halves, small, edge)
     field, state, frames, first = (), (), [], None
     for instant in range(STEPS):
         for pair in range(ITERS // 2):

time: 141 us -> 154 us (1.092); the launches traced: 140 us -> 152 us
  Pallas kernels: 21.9 us -> 46.8 us
  waiting for transfers between devices: 61.2 us -> 46 us
  local copies, waits for them, and re-layouts: 1.04 us -> 3.29 us
    pallas_call x33, Pallas kernels: 14.7 us -> 39 us  [call(): pl.pallas_call(body, out_shape=outs, in_specs=[vmem] * len(ins), out_spec...]
    ppermute x16, waiting for transfers between devices: 32.1 us -> 21.7 us  [shards_chain(): got_b = lax.ppermute(msg_b, both, b_pairs)]
    ppermute x1, waiting for transfers between devices: 5.02 us -> 0.6 us  [beside(): lax.ppermute(send, 'row', swap)]
    cond x2, local copies, waits for them, and re-layouts: 0.92 us -> 2.48 us
    pallas_call x3 -> x4, Pallas kernels: 4.61 us -> 5.4 us  [pack(): pl.pallas_call(functools.partial(pack_kernel, n_col, sent, first, count),...]
  transfers between devices with their start and end apart: 38 -> 38, of which waited for: 34 -> 34; matrix products, arithmetic and copies ran while one was open for 1% -> 2% of each run, Pallas kernels for 9% -> 16%
where the time goes in v17:
time: 154 us; the launch traced here: 152 us
  starting transfers between devices  54.2 us (35%)
  Pallas kernels  46.8 us (30%)
  waiting for transfers between devices  46 us (30%)
  local copies, waits for them, and re-layouts  3.29 us (2%)
    pallas_call x33, Pallas kernels, call(): pl.pallas_call(body, out_shape=outs, in_specs=[vmem] * len(ins), out_spec...  39 us
    ppermute x16, starting transfers between devices, shards_chain(): got_b = lax.ppermute(msg_b, both, b_pairs)  37.9 us
    ppermute x16, waiting for transfers between devices, shards_chain(): got_b = lax.ppermute(msg_b, both, b_pairs)  21.7 us
    ppermute x16, waiting for transfers between devices, shards_chain(): got_a = lax.ppermute(msg_a, 'row', swap)  17.6 us
    all_to_all x1, starting transfers between devices, beside(): lax.all_to_all(by_target, 'col', split_axis=0, concat_axis=0, tiled=True)  6.27 us
    pallas_call x4, Pallas kernels, pack(): pl.pallas_call(functools.partial(pack_kernel, n_col, sent, first, count),...  5.4 us
    ppermute x1, waiting for transfers between devices, shards_chain(): got = lax.ppermute(jnp.flip(done[:, ROWS:], 1), 'row', swap)  3.62 us
    ppermute x16, starting transfers between devices, shards_chain(): got_a = lax.ppermute(msg_a, 'row', swap)  3.15 us
  transfers between devices with their start and end apart: 38, of which 34 were waited for; matrix products, arithmetic and copies ran while one was open for 2% of the time, Pallas kernels for 16%

profile of v17, /device:TPU:8, one launch (start us, length us, event | category | flops | bytes accessed | tf_op | source)
XLA Modules:
  0.0 151.5 jit_solution(16243622232111331864)
XLA Ops:
  0.0 1.2 pack.5
  1.2 1.6 %collective-permute-start.2 = (f32[10,128,128]{2,1,0:T(8,128)S(1)}, f32[10,128,128]{2,1,0:T(8,128)S(1)}, u32[]{:S(2)}, u32[]{:S(2)}) collective-permute-start(f32[10,128,128]{2,1,0:T(8,128)S(1)} %pack.5), channel_id=1, source_target_pairs={{0,16},{16,0},{1,17},{17,1},{2,18},{18,2},{3,19},{19,3},{4,20},{20... | collective-permute-start | bytes 1966088 | tf_op jit(solution)/shard_map/ppermute | solution.py:525
  5.4 2.2 %pack.4 = (f32[20,128,128]{2,1,0:T(8,128)S(1)}, f32[2,128,128]{2,1,0:T(8,128)}) custom-call(s32[2,4,4]{2,1,0:T(4,128)} %pattern_hbm.7, f32[2,4,128,128]{3,2,1,0:T(8,128)} %own_hbm.7, f32[4,2,4,128,128]{4,3,2,1,0:T(8,128)} %nb_hbm.7), custom_call_target="tpu_custom_call" | custom-call | tf_op jit(solution)/shard_map/pack/pallas_call | solution.py:512
  7.6 19.8 %conditional.1 = (f32[48,128]{1,0:T(8,128)}, f32[2,128,128]{2,1,0:T(8,128)}) conditional(s32[]{:T(128)} %convert_element_type.3, f32[2,128,128]{2,1,0:T(8,128)} %get-tuple-element.163, (f32[1,1,16,4,512]{4,3,2,1,0:T(4,128)}, s32[1,1,16,4]{2,3,1,0:T(4,128)}, f32[2,4,128]{2,1,0:T(4,128)S(1)}, f32[2,4,128]{2,1,0:T(4,128)S(1)}, ...), branch_computations={%region_0.1_spmd, %region_1.2_spmd} | conditional | bytes 1532544 | solution.py:563
  8.4 1.6 %by_target.1 = f32[16,1,2176]{2,1,0:T(1,128)} custom-call(f32[16,4,512]{2,1,0:T(4,128)} %bitcast.14, s32[16,4]{1,0:T(8,128)S(1)} %copy.14.slot_tile), custom_call_target="tpu_custom_call" | custom-call | tf_op jit(solution)/shard_map/cond/branch_1_fun/by_target/pallas_call | solution.py:534
  10.0 6.3 %all-to-all-start = ((f32[16,1,2176]{2,1,0:T(1,128)}), f32[16,1,2176]{2,1,0:T(1,128)}, u32[]{:S(2)}, u32[]{:S(2)}) async-start(f32[16,1,2176]{2,1,0:T(1,128)} %by_target.1), calls=%async_computation | async-start | bytes 278528 | tf_op jit(solution)/shard_map/cond/branch_1_fun/all_to_all | solution.py:542
  16.3 3.1 %collective-permute-start.1 = (f32[2,128,128]{2,1,0:T(8,128)}, f32[2,128,128]{2,1,0:T(8,128)}, u32[]{:S(2)}, u32[]{:S(2)}) collective-permute-start(f32[2,128,128]{2,1,0:T(8,128)} %get-tuple-element.22), channel_id=1, source_target_pairs={{16,17},{17,16},{1,2},{2,1},{18,19},{19,18},{3,4},{4,3},{20,21},{2... | collective-permute-start | bytes 393224 | tf_op jit(solution)/shard_map/cond/branch_1_fun/ppermute | solution.py:532
  19.4 2.5 %all-to-all-done = f32[16,1,2176]{2,1,0:T(1,128)} async-done(((f32[16,1,2176]{2,1,0:T(1,128)}), f32[16,1,2176]{2,1,0:T(1,128)}, u32[]{:S(2)}, u32[]{:S(2)}) %all-to-all-start) | async-done | bytes 139296 | tf_op jit(solution)/shard_map/cond/branch_1_fun/all_to_all | solution.py:542
  23.0 1.6 %collective-permute-start = (f32[24,128]{1,0:T(8,128)S(1)}, f32[24,128]{1,0:T(8,128)S(1)}, u32[]{:S(2)}, u32[]{:S(2)}) collective-permute-start(f32[24,128]{1,0:T(8,128)S(1)} %get-tuple-element.21), channel_id=1, source_target_pairs={{0,16},{16,0},{1,17},{17,1},{2,18},{18,2},{3,19},{19,3},{4,20},{20... | collective-permute-start | bytes 36872 | tf_op jit(solution)/shard_map/cond/branch_1_fun/ppermute | solution.py:560
  24.6 1.6 %copy.21 = f32[2,128,128]{2,1,0:T(8,128)} copy(f32[2,128,128]{2,1,0:T(8,128)} %collective-permute-done.1) | data formatting | bytes 262144 | tf_op jit(solution)/shard_map/cond
  28.4 1.6 %collective-permute-start.5 = (f32[520,128]{1,0:T(8,128)S(1)}, f32[520,128]{1,0:T(8,128)S(1)}, u32[]{:S(2)}, u32[]{:S(2)}) collective-permute-start(f32[520,128]{1,0:T(8,128)S(1)} %get-tuple-element.167), channel_id=1, source_target_pairs={{0,16},{16,0},{1,17},{17,1},{2,18},{18,2},{3,19},{19,3},{4,20},{20... | collective-permute-start | bytes 798728 | tf_op jit(solution)/shard_map/ppermute | solution.py:596
  30.0 2.2 %collective-permute-start.4 = (f32[264,128]{1,0:T(8,128)S(1)}, f32[264,128]{1,0:T(8,128)S(1)}, u32[]{:S(2)}, u32[]{:S(2)}) collective-permute-start(f32[264,128]{1,0:T(8,128)S(1)} %get-tuple-element.165), channel_id=1, source_target_pairs={{16,17},{17,16},{1,2},{2,1},{18,19},{19,18},{3,4},{4,3},{20,21},{2... | collective-permute-start | bytes 405512 | tf_op jit(solution)/shard_map/ppermute | solution.py:595
  32.2 5.1 %collective-permute-done.4.first_b.got_b = f32[264,128]{1,0:T(8,128)S(1)} collective-permute-done((f32[264,128]{1,0:T(8,128)S(1)}, f32[264,128]{1,0:T(8,128)S(1)}, u32[]{:S(2)}, u32[]{:S(2)}) %collective-permute-start.4) | collective-permute-done | bytes 135200 | tf_op jit(solution)/shard_map/ppermute | solution.py:595
  38.5 1.2 pair.35
  40.3 1.9 %collective-permute-start.6 = (f32[8,128]{1,0:T(8,128)S(1)}, f32[8,128]{1,0:T(8,128)S(1)}, u32[]{:S(2)}, u32[]{:S(2)}) collective-permute-start(f32[8,128]{1,0:T(8,128)S(1)} %get-tuple-element.172), channel_id=1, source_target_pairs={{16,17},{17,16},{1,2},{2,1},{18,19},{19,18},{3,4},{4,3},{20,21},{2... | collective-permute-start | bytes 12296 | tf_op jit(solution)/shard_map/ppermute | solution.py:595
  42.2 1.2 collective-permute-done.7.got_a
  44.6 1.5 %collective-permute-done.6.got_b = f32[8,128]{1,0:T(8,128)S(1)} collective-permute-done((f32[8,128]{1,0:T(8,128)S(1)}, f32[8,128]{1,0:T(8,128)S(1)}, u32[]{:S(2)}, u32[]{:S(2)}) %collective-permute-start.6) | collective-permute-done | bytes 4128 | tf_op jit(solution)/shard_map/ppermute | solution.py:595
  46.1 1.2 pair.37
  47.4 2.4 %collective-permute-start.8 = (f32[8,128]{1,0:T(8,128)S(1)}, f32[8,128]{1,0:T(8,128)S(1)}, u32[]{:S(2)}, u32[]{:S(2)}) collective-permute-start(f32[8,128]{1,0:T(8,128)S(1)} %get-tuple-element.181), channel_id=1, source_target_pairs={{16,17},{17,16},{1,2},{2,1},{18,19},{19,18},{3,4},{4,3},{20,21},{2... | collective-permute-start | bytes 12296 | tf_op jit(solution)/shard_map/ppermute | solution.py:595
  49.8 1.2 collective-permute-done.9.got_a
  53.2 1.2 pair.39
  54.6 2.4 %collective-permute-start.10 = (f32[8,128]{1,0:T(8,128)S(1)}, f32[8,128]{1,0:T(8,128)S(1)}, u32[]{:S(2)}, u32[]{:S(2)}) collective-permute-start(f32[8,128]{1,0:T(8,128)S(1)} %get-tuple-element.190), channel_id=1, source_target_pairs={{16,17},{17,16},{1,2},{2,1},{18,19},{19,18},{3,4},{4,3},{20,21},{2... | collective-permute-start | bytes 12296 | tf_op jit(solution)/shard_map/ppermute | solution.py:595
  57.0 1.2 collective-permute-done.11.got_a
  60.4 1.2 pair.41
  61.7 2.4 %collective-permute-start.12 = (f32[8,128]{1,0:T(8,128)S(1)}, f32[8,128]{1,0:T(8,128)S(1)}, u32[]{:S(2)}, u32[]{:S(2)}) collective-permute-start(f32[8,128]{1,0:T(8,128)S(1)} %get-tuple-element.200), channel_id=1, source_target_pairs={{16,17},{17,16},{1,2},{2,1},{18,19},{19,18},{3,4},{4,3},{20,21},{2... | collective-permute-start | bytes 12296 | tf_op jit(solution)/shard_map/ppermute | solution.py:595
  67.5 1.2 pair.43
  68.8 2.4 %collective-permute-start.14 = (f32[8,128]{1,0:T(8,128)S(1)}, f32[8,128]{1,0:T(8,128)S(1)}, u32[]{:S(2)}, u32[]{:S(2)}) collective-permute-start(f32[8,128]{1,0:T(8,128)S(1)} %get-tuple-element.206), channel_id=1, source_target_pairs={{16,17},{17,16},{1,2},{2,1},{18,19},{19,18},{3,4},{4,3},{20,21},{2... | collective-permute-start | bytes 12296 | tf_op jit(solution)/shard_map/ppermute | solution.py:595
  74.6 1.2 pair.45
  76.0 2.4 %collective-permute-start.16 = (f32[8,128]{1,0:T(8,128)S(1)}, f32[8,128]{1,0:T(8,128)S(1)}, u32[]{:S(2)}, u32[]{:S(2)}) collective-permute-start(f32[8,128]{1,0:T(8,128)S(1)} %get-tuple-element.215), channel_id=1, source_target_pairs={{16,17},{17,16},{1,2},{2,1},{18,19},{19,18},{3,4},{4,3},{20,21},{2... | collective-permute-start | bytes 12296 | tf_op jit(solution)/shard_map/ppermute | solution.py:595
  81.8 1.2 pair.47
  83.1 2.4 %collective-permute-start.18 = (f32[8,128]{1,0:T(8,128)S(1)}, f32[8,128]{1,0:T(8,128)S(1)}, u32[]{:S(2)}, u32[]{:S(2)}) collective-permute-start(f32[8,128]{1,0:T(8,128)S(1)} %get-tuple-element.224), channel_id=1, source_target_pairs={{16,17},{17,16},{1,2},{2,1},{18,19},{19,18},{3,4},{4,3},{20,21},{2... | collective-permute-start | bytes 12296 | tf_op jit(solution)/shard_map/ppermute | solution.py:595
  88.9 1.2 pair.49
  90.2 2.4 %collective-permute-start.20 = (f32[8,128]{1,0:T(8,128)S(1)}, f32[8,128]{1,0:T(8,128)S(1)}, u32[]{:S(2)}, u32[]{:S(2)}) collective-permute-start(f32[8,128]{1,0:T(8,128)S(1)} %get-tuple-element.234), channel_id=1, source_target_pairs={{16,17},{17,16},{1,2},{2,1},{18,19},{19,18},{3,4},{4,3},{20,21},{2... | collective-permute-start | bytes 12296 | tf_op jit(solution)/shard_map/ppermute | solution.py:595
  96.0 1.2 pair.51
  97.4 2.4 %collective-permute-start.22 = (f32[8,128]{1,0:T(8,128)S(1)}, f32[8,128]{1,0:T(8,128)S(1)}, u32[]{:S(2)}, u32[]{:S(2)}) collective-permute-start(f32[8,128]{1,0:T(8,128)S(1)} %get-tuple-element.240), channel_id=1, source_target_pairs={{16,17},{17,16},{1,2},{2,1},{18,19},{19,18},{3,4},{4,3},{20,21},{2... | collective-permute-start | bytes 12296 | tf_op jit(solution)/shard_map/ppermute | solution.py:595
  103.2 1.2 pair.53
  104.5 2.6 %collective-permute-start.24 = (f32[8,128]{1,0:T(8,128)S(1)}, f32[8,128]{1,0:T(8,128)S(1)}, u32[]{:S(2)}, u32[]{:S(2)}) collective-permute-start(f32[8,128]{1,0:T(8,128)S(1)} %get-tuple-element.249), channel_id=1, source_target_pairs={{16,17},{17,16},{1,2},{2,1},{18,19},{19,18},{3,4},{4,3},{20,21},{2... | collective-permute-start | bytes 12296 | tf_op jit(solution)/shard_map/ppermute | solution.py:595
  110.3 1.2 pair.55
  111.6 2.4 %collective-permute-start.26 = (f32[8,128]{1,0:T(8,128)S(1)}, f32[8,128]{1,0:T(8,128)S(1)}, u32[]{:S(2)}, u32[]{:S(2)}) collective-permute-start(f32[8,128]{1,0:T(8,128)S(1)} %get-tuple-element.258), channel_id=1, source_target_pairs={{16,17},{17,16},{1,2},{2,1},{18,19},{19,18},{3,4},{4,3},{20,21},{2... | collective-permute-start | bytes 12296 | tf_op jit(solution)/shard_map/ppermute | solution.py:595
  117.5 1.2 pair.57
  118.8 2.4 %collective-permute-start.28 = (f32[8,128]{1,0:T(8,128)S(1)}, f32[8,128]{1,0:T(8,128)S(1)}, u32[]{:S(2)}, u32[]{:S(2)}) collective-permute-start(f32[8,128]{1,0:T(8,128)S(1)} %get-tuple-element.268), channel_id=1, source_target_pairs={{16,17},{17,16},{1,2},{2,1},{18,19},{19,18},{3,4},{4,3},{20,21},{2... | collective-permute-start | bytes 12296 | tf_op jit(solution)/shard_map/ppermute | solution.py:595
  124.6 1.2 pair.59
  125.9 2.4 %collective-permute-start.30 = (f32[8,128]{1,0:T(8,128)S(1)}, f32[8,128]{1,0:T(8,128)S(1)}, u32[]{:S(2)}, u32[]{:S(2)}) collective-permute-start(f32[8,128]{1,0:T(8,128)S(1)} %get-tuple-element.274), channel_id=1, source_target_pairs={{16,17},{17,16},{1,2},{2,1},{18,19},{19,18},{3,4},{4,3},{20,21},{2... | collective-permute-start | bytes 12296 | tf_op jit(solution)/shard_map/ppermute | solution.py:595
  131.7 1.2 pair.61
  133.0 2.4 %collective-permute-start.32 = (f32[8,128]{1,0:T(8,128)S(1)}, f32[8,128]{1,0:T(8,128)S(1)}, u32[]{:S(2)}, u32[]{:S(2)}) collective-permute-start(f32[8,128]{1,0:T(8,128)S(1)} %get-tuple-element.283), channel_id=1, source_target_pairs={{16,17},{17,16},{1,2},{2,1},{18,19},{19,18},{3,4},{4,3},{20,21},{2... | collective-permute-start | bytes 12296 | tf_op jit(solution)/shard_map/ppermute | solution.py:595
  138.9 1.2 pair.63
  140.2 2.4 %collective-permute-start.34 = (f32[8,128]{1,0:T(8,128)S(1)}, f32[8,128]{1,0:T(8,128)S(1)}, u32[]{:S(2)}, u32[]{:S(2)}) collective-permute-start(f32[8,128]{1,0:T(8,128)S(1)} %get-tuple-element.292), channel_id=1, source_target_pairs={{16,17},{17,16},{1,2},{2,1},{18,19},{19,18},{3,4},{4,3},{20,21},{2... | collective-permute-start | bytes 12296 | tf_op jit(solution)/shard_map/ppermute | solution.py:595
  147.2 3.6 %collective-permute-done.36 = f32[4,2,2,128]{3,2,1,0:T(2,128)S(1)} collective-permute-done((f32[4,2,2,128]{3,2,1,0:T(2,128)S(1)}, f32[4,2,2,128]{3,2,1,0:T(2,128)S(1)}, u32[]{:S(2)}, u32[]{:S(2)}) %collective-permute-start.36) | collective-permute-done | bytes 8224 | tf_op jit(solution)/shard_map/ppermute | solution.py:609
  (85 shorter events, 57.6 us)
Async XLA Ops:
  1.2 26.2 %collective-permute-start.2 = (f32[10,128,128]{2,1,0:T(8,128)S(1)}, f32[10,128,128]{2,1,0:T(8,128)S(1)}, u32[]{:S(2)}, u32[]{:S(2)}) collective-permute-start(f32[10,128,128]{2,1,0:T(8,128)S(1)} %pack.5), channel_id=1, source_target_pairs={{0,16},{16,0},{1,17},{17,1},{2,18},{18,2},{3,19},{19,3},{4,20},{20... | collective-permute-start | bytes 1966088 | tf_op jit(solution)/shard_map/ppermute | solution.py:525
  3.9 23.5 %collective-permute-start.3 = (f32[6,128,128]{2,1,0:T(8,128)S(1)}, f32[6,128,128]{2,1,0:T(8,128)S(1)}, u32[]{:S(2)}, u32[]{:S(2)}) collective-permute-start(f32[6,128,128]{2,1,0:T(8,128)S(1)} %pack.6), channel_id=1, source_target_pairs={{0,16},{16,0},{1,17},{17,1},{2,18},{18,2},{3,19},{19,3},{4,20},{20... | collective-permute-start | bytes 1179656 | tf_op jit(solution)/shard_map/ppermute | solution.py:525
  4.5 3.1 %copy-start.1 = (f32[2,4,128]{2,1,0:T(4,128)S(1)}, f32[2,4,128]{2,1,0:T(4,128)}, u32[]{:S(2)}) copy-start(f32[2,4,128]{2,1,0:T(4,128)} %param.12) | copy-start | bytes 12292
  4.5 3.2 %copy-start.2 = (f32[2,4,128]{2,1,0:T(4,128)S(1)}, f32[2,4,128]{2,1,0:T(4,128)}, u32[]{:S(2)}) copy-start(f32[2,4,128]{2,1,0:T(4,128)} %param.13) | copy-start | bytes 12292
  10.0 11.9 %all-to-all-start = ((f32[16,1,2176]{2,1,0:T(1,128)}), f32[16,1,2176]{2,1,0:T(1,128)}, u32[]{:S(2)}, u32[]{:S(2)}) async-start(f32[16,1,2176]{2,1,0:T(1,128)} %by_target.1), calls=%async_computation | async-start | bytes 278528 | tf_op jit(solution)/shard_map/cond/branch_1_fun/all_to_all | solution.py:542
  16.3 8.3 %collective-permute-start.1 = (f32[2,128,128]{2,1,0:T(8,128)}, f32[2,128,128]{2,1,0:T(8,128)}, u32[]{:S(2)}, u32[]{:S(2)}) collective-permute-start(f32[2,128,128]{2,1,0:T(8,128)} %get-tuple-element.22), channel_id=1, source_target_pairs={{16,17},{17,16},{1,2},{2,1},{18,19},{19,18},{3,4},{4,3},{20,21},{2... | collective-permute-start | bytes 393224 | tf_op jit(solution)/shard_map/cond/branch_1_fun/ppermute | solution.py:532
  23.0 3.8 %collective-permute-start = (f32[24,128]{1,0:T(8,128)S(1)}, f32[24,128]{1,0:T(8,128)S(1)}, u32[]{:S(2)}, u32[]{:S(2)}) collective-permute-start(f32[24,128]{1,0:T(8,128)S(1)} %get-tuple-element.21), channel_id=1, source_target_pairs={{0,16},{16,0},{1,17},{17,1},{2,18},{18,2},{3,19},{19,3},{4,20},{20... | collective-permute-start | bytes 36872 | tf_op jit(solution)/shard_map/cond/branch_1_fun/ppermute | solution.py:560
  27.4 9.9 %copy-start = (f32[2,128,128]{2,1,0:T(8,128)S(1)}, f32[2,128,128]{2,1,0:T(8,128)}, u32[]{:S(2)}) copy-start(f32[2,128,128]{2,1,0:T(8,128)} %get-tuple-element.166.beyond_0) | copy-start | bytes 393220
  28.4 8.9 %collective-permute-start.5 = (f32[520,128]{1,0:T(8,128)S(1)}, f32[520,128]{1,0:T(8,128)S(1)}, u32[]{:S(2)}, u32[]{:S(2)}) collective-permute-start(f32[520,128]{1,0:T(8,128)S(1)} %get-tuple-element.167), channel_id=1, source_target_pairs={{0,16},{16,0},{1,17},{17,1},{2,18},{18,2},{3,19},{19,3},{4,20},{20... | collective-permute-start | bytes 798728 | tf_op jit(solution)/shard_map/ppermute | solution.py:596
  30.0 7.3 %collective-permute-start.4 = (f32[264,128]{1,0:T(8,128)S(1)}, f32[264,128]{1,0:T(8,128)S(1)}, u32[]{:S(2)}, u32[]{:S(2)}) collective-permute-start(f32[264,128]{1,0:T(8,128)S(1)} %get-tuple-element.165), channel_id=1, source_target_pairs={{16,17},{17,16},{1,2},{2,1},{18,19},{19,18},{3,4},{4,3},{20,21},{2... | collective-permute-start | bytes 405512 | tf_op jit(solution)/shard_map/ppermute | solution.py:595
  39.7 3.7 %collective-permute-start.7 = (f32[8,128]{1,0:T(8,128)S(1)}, f32[8,128]{1,0:T(8,128)S(1)}, u32[]{:S(2)}, u32[]{:S(2)}) collective-permute-start(f32[8,128]{1,0:T(8,128)S(1)} %get-tuple-element.173), channel_id=1, source_target_pairs={{0,16},{16,0},{1,17},{17,1},{2,18},{18,2},{3,19},{19,3},{4,20},{20... | collective-permute-start | bytes 12296 | tf_op jit(solution)/shard_map/ppermute | solution.py:596
  40.3 5.8 %collective-permute-start.6 = (f32[8,128]{1,0:T(8,128)S(1)}, f32[8,128]{1,0:T(8,128)S(1)}, u32[]{:S(2)}, u32[]{:S(2)}) collective-permute-start(f32[8,128]{1,0:T(8,128)S(1)} %get-tuple-element.172), channel_id=1, source_target_pairs={{16,17},{17,16},{1,2},{2,1},{18,19},{19,18},{3,4},{4,3},{20,21},{2... | collective-permute-start | bytes 12296 | tf_op jit(solution)/shard_map/ppermute | solution.py:595
  47.3 3.7 %collective-permute-start.9 = (f32[8,128]{1,0:T(8,128)S(1)}, f32[8,128]{1,0:T(8,128)S(1)}, u32[]{:S(2)}, u32[]{:S(2)}) collective-permute-start(f32[8,128]{1,0:T(8,128)S(1)} %get-tuple-element.182), channel_id=1, source_target_pairs={{0,16},{16,0},{1,17},{17,1},{2,18},{18,2},{3,19},{19,3},{4,20},{20... | collective-permute-start | bytes 12296 | tf_op jit(solution)/shard_map/ppermute | solution.py:596
  47.4 5.8 %collective-permute-start.8 = (f32[8,128]{1,0:T(8,128)S(1)}, f32[8,128]{1,0:T(8,128)S(1)}, u32[]{:S(2)}, u32[]{:S(2)}) collective-permute-start(f32[8,128]{1,0:T(8,128)S(1)} %get-tuple-element.181), channel_id=1, source_target_pairs={{16,17},{17,16},{1,2},{2,1},{18,19},{19,18},{3,4},{4,3},{20,21},{2... | collective-permute-start | bytes 12296 | tf_op jit(solution)/shard_map/ppermute | solution.py:595
  54.5 3.7 %collective-permute-start.11 = (f32[8,128]{1,0:T(8,128)S(1)}, f32[8,128]{1,0:T(8,128)S(1)}, u32[]{:S(2)}, u32[]{:S(2)}) collective-permute-start(f32[8,128]{1,0:T(8,128)S(1)} %get-tuple-element.191), channel_id=1, source_target_pairs={{0,16},{16,0},{1,17},{17,1},{2,18},{18,2},{3,19},{19,3},{4,20},{20... | collective-permute-start | bytes 12296 | tf_op jit(solution)/shard_map/ppermute | solution.py:596
  54.6 5.8 %collective-permute-start.10 = (f32[8,128]{1,0:T(8,128)S(1)}, f32[8,128]{1,0:T(8,128)S(1)}, u32[]{:S(2)}, u32[]{:S(2)}) collective-permute-start(f32[8,128]{1,0:T(8,128)S(1)} %get-tuple-element.190), channel_id=1, source_target_pairs={{16,17},{17,16},{1,2},{2,1},{18,19},{19,18},{3,4},{4,3},{20,21},{2... | collective-permute-start | bytes 12296 | tf_op jit(solution)/shard_map/ppermute | solution.py:595
  61.6 3.7 %collective-permute-start.13 = (f32[8,128]{1,0:T(8,128)S(1)}, f32[8,128]{1,0:T(8,128)S(1)}, u32[]{:S(2)}, u32[]{:S(2)}) collective-permute-start(f32[8,128]{1,0:T(8,128)S(1)} %get-tuple-element.201), channel_id=1, source_target_pairs={{0,16},{16,0},{1,17},{17,1},{2,18},{18,2},{3,19},{19,3},{4,20},{20... | collective-permute-start | bytes 12296 | tf_op jit(solution)/shard_map/ppermute | solution.py:596
  61.7 5.8 %collective-permute-start.12 = (f32[8,128]{1,0:T(8,128)S(1)}, f32[8,128]{1,0:T(8,128)S(1)}, u32[]{:S(2)}, u32[]{:S(2)}) collective-permute-start(f32[8,128]{1,0:T(8,128)S(1)} %get-tuple-element.200), channel_id=1, source_target_pairs={{16,17},{17,16},{1,2},{2,1},{18,19},{19,18},{3,4},{4,3},{20,21},{2... | collective-permute-start | bytes 12296 | tf_op jit(solution)/shard_map/ppermute | solution.py:595
  68.7 3.7 %collective-permute-start.15 = (f32[8,128]{1,0:T(8,128)S(1)}, f32[8,128]{1,0:T(8,128)S(1)}, u32[]{:S(2)}, u32[]{:S(2)}) collective-permute-start(f32[8,128]{1,0:T(8,128)S(1)} %get-tuple-element.207), channel_id=1, source_target_pairs={{0,16},{16,0},{1,17},{17,1},{2,18},{18,2},{3,19},{19,3},{4,20},{20... | collective-permute-start | bytes 12296 | tf_op jit(solution)/shard_map/ppermute | solution.py:596
  68.8 5.8 %collective-permute-start.14 = (f32[8,128]{1,0:T(8,128)S(1)}, f32[8,128]{1,0:T(8,128)S(1)}, u32[]{:S(2)}, u32[]{:S(2)}) collective-permute-start(f32[8,128]{1,0:T(8,128)S(1)} %get-tuple-element.206), channel_id=1, source_target_pairs={{16,17},{17,16},{1,2},{2,1},{18,19},{19,18},{3,4},{4,3},{20,21},{2... | collective-permute-start | bytes 12296 | tf_op jit(solution)/shard_map/ppermute | solution.py:595
  75.9 3.7 %collective-permute-start.17 = (f32[8,128]{1,0:T(8,128)S(1)}, f32[8,128]{1,0:T(8,128)S(1)}, u32[]{:S(2)}, u32[]{:S(2)}) collective-permute-start(f32[8,128]{1,0:T(8,128)S(1)} %get-tuple-element.216), channel_id=1, source_target_pairs={{0,16},{16,0},{1,17},{17,1},{2,18},{18,2},{3,19},{19,3},{4,20},{20... | collective-permute-start | bytes 12296 | tf_op jit(solution)/shard_map/ppermute | solution.py:596
  76.0 5.8 %collective-permute-start.16 = (f32[8,128]{1,0:T(8,128)S(1)}, f32[8,128]{1,0:T(8,128)S(1)}, u32[]{:S(2)}, u32[]{:S(2)}) collective-permute-start(f32[8,128]{1,0:T(8,128)S(1)} %get-tuple-element.215), channel_id=1, source_target_pairs={{16,17},{17,16},{1,2},{2,1},{18,19},{19,18},{3,4},{4,3},{20,21},{2... | collective-permute-start | bytes 12296 | tf_op jit(solution)/shard_map/ppermute | solution.py:595
  83.0 3.7 %collective-permute-start.19 = (f32[8,128]{1,0:T(8,128)S(1)}, f32[8,128]{1,0:T(8,128)S(1)}, u32[]{:S(2)}, u32[]{:S(2)}) collective-permute-start(f32[8,128]{1,0:T(8,128)S(1)} %get-tuple-element.225), channel_id=1, source_target_pairs={{0,16},{16,0},{1,17},{17,1},{2,18},{18,2},{3,19},{19,3},{4,20},{20... | collective-permute-start | bytes 12296 | tf_op jit(solution)/shard_map/ppermute | solution.py:596
  83.1 5.8 %collective-permute-start.18 = (f32[8,128]{1,0:T(8,128)S(1)}, f32[8,128]{1,0:T(8,128)S(1)}, u32[]{:S(2)}, u32[]{:S(2)}) collective-permute-start(f32[8,128]{1,0:T(8,128)S(1)} %get-tuple-element.224), channel_id=1, source_target_pairs={{16,17},{17,16},{1,2},{2,1},{18,19},{19,18},{3,4},{4,3},{20,21},{2... | collective-permute-start | bytes 12296 | tf_op jit(solution)/shard_map/ppermute | solution.py:595
  90.1 3.7 %collective-permute-start.21 = (f32[8,128]{1,0:T(8,128)S(1)}, f32[8,128]{1,0:T(8,128)S(1)}, u32[]{:S(2)}, u32[]{:S(2)}) collective-permute-start(f32[8,128]{1,0:T(8,128)S(1)} %get-tuple-element.235), channel_id=1, source_target_pairs={{0,16},{16,0},{1,17},{17,1},{2,18},{18,2},{3,19},{19,3},{4,20},{20... | collective-permute-start | bytes 12296 | tf_op jit(solution)/shard_map/ppermute | solution.py:596
  90.2 5.8 %collective-permute-start.20 = (f32[8,128]{1,0:T(8,128)S(1)}, f32[8,128]{1,0:T(8,128)S(1)}, u32[]{:S(2)}, u32[]{:S(2)}) collective-permute-start(f32[8,128]{1,0:T(8,128)S(1)} %get-tuple-element.234), channel_id=1, source_target_pairs={{16,17},{17,16},{1,2},{2,1},{18,19},{19,18},{3,4},{4,3},{20,21},{2... | collective-permute-start | bytes 12296 | tf_op jit(solution)/shard_map/ppermute | solution.py:595
  97.3 3.7 %collective-permute-start.23 = (f32[8,128]{1,0:T(8,128)S(1)}, f32[8,128]{1,0:T(8,128)S(1)}, u32[]{:S(2)}, u32[]{:S(2)}) collective-permute-start(f32[8,128]{1,0:T(8,128)S(1)} %get-tuple-element.241), channel_id=1, source_target_pairs={{0,16},{16,0},{1,17},{17,1},{2,18},{18,2},{3,19},{19,3},{4,20},{20... | collective-permute-start | bytes 12296 | tf_op jit(solution)/shard_map/ppermute | solution.py:596
  97.4 5.8 %collective-permute-start.22 = (f32[8,128]{1,0:T(8,128)S(1)}, f32[8,128]{1,0:T(8,128)S(1)}, u32[]{:S(2)}, u32[]{:S(2)}) collective-permute-start(f32[8,128]{1,0:T(8,128)S(1)} %get-tuple-element.240), channel_id=1, source_target_pairs={{16,17},{17,16},{1,2},{2,1},{18,19},{19,18},{3,4},{4,3},{20,21},{2... | collective-permute-start | bytes 12296 | tf_op jit(solution)/shard_map/ppermute | solution.py:595
  104.4 3.7 %collective-permute-start.25 = (f32[8,128]{1,0:T(8,128)S(1)}, f32[8,128]{1,0:T(8,128)S(1)}, u32[]{:S(2)}, u32[]{:S(2)}) collective-permute-start(f32[8,128]{1,0:T(8,128)S(1)} %get-tuple-element.250), channel_id=1, source_target_pairs={{0,16},{16,0},{1,17},{17,1},{2,18},{18,2},{3,19},{19,3},{4,20},{20... | collective-permute-start | bytes 12296 | tf_op jit(solution)/shard_map/ppermute | solution.py:596
  104.5 5.8 %collective-permute-start.24 = (f32[8,128]{1,0:T(8,128)S(1)}, f32[8,128]{1,0:T(8,128)S(1)}, u32[]{:S(2)}, u32[]{:S(2)}) collective-permute-start(f32[8,128]{1,0:T(8,128)S(1)} %get-tuple-element.249), channel_id=1, source_target_pairs={{16,17},{17,16},{1,2},{2,1},{18,19},{19,18},{3,4},{4,3},{20,21},{2... | collective-permute-start | bytes 12296 | tf_op jit(solution)/shard_map/ppermute | solution.py:595
  111.6 3.7 %collective-permute-start.27 = (f32[8,128]{1,0:T(8,128)S(1)}, f32[8,128]{1,0:T(8,128)S(1)}, u32[]{:S(2)}, u32[]{:S(2)}) collective-permute-start(f32[8,128]{1,0:T(8,128)S(1)} %get-tuple-element.259), channel_id=1, source_target_pairs={{0,16},{16,0},{1,17},{17,1},{2,18},{18,2},{3,19},{19,3},{4,20},{20... | collective-permute-start | bytes 12296 | tf_op jit(solution)/shard_map/ppermute | solution.py:596
  111.6 5.8 %collective-permute-start.26 = (f32[8,128]{1,0:T(8,128)S(1)}, f32[8,128]{1,0:T(8,128)S(1)}, u32[]{:S(2)}, u32[]{:S(2)}) collective-permute-start(f32[8,128]{1,0:T(8,128)S(1)} %get-tuple-element.258), channel_id=1, source_target_pairs={{16,17},{17,16},{1,2},{2,1},{18,19},{19,18},{3,4},{4,3},{20,21},{2... | collective-permute-start | bytes 12296 | tf_op jit(solution)/shard_map/ppermute | solution.py:595
  118.7 3.7 %collective-permute-start.29 = (f32[8,128]{1,0:T(8,128)S(1)}, f32[8,128]{1,0:T(8,128)S(1)}, u32[]{:S(2)}, u32[]{:S(2)}) collective-permute-start(f32[8,128]{1,0:T(8,128)S(1)} %get-tuple-element.269), channel_id=1, source_target_pairs={{0,16},{16,0},{1,17},{17,1},{2,18},{18,2},{3,19},{19,3},{4,20},{20... | collective-permute-start | bytes 12296 | tf_op jit(solution)/shard_map/ppermute | solution.py:596
  118.8 5.8 %collective-permute-start.28 = (f32[8,128]{1,0:T(8,128)S(1)}, f32[8,128]{1,0:T(8,128)S(1)}, u32[]{:S(2)}, u32[]{:S(2)}) collective-permute-start(f32[8,128]{1,0:T(8,128)S(1)} %get-tuple-element.268), channel_id=1, source_target_pairs={{16,17},{17,16},{1,2},{2,1},{18,19},{19,18},{3,4},{4,3},{20,21},{2... | collective-permute-start | bytes 12296 | tf_op jit(solution)/shard_map/ppermute | solution.py:595
  125.8 3.7 %collective-permute-start.31 = (f32[8,128]{1,0:T(8,128)S(1)}, f32[8,128]{1,0:T(8,128)S(1)}, u32[]{:S(2)}, u32[]{:S(2)}) collective-permute-start(f32[8,128]{1,0:T(8,128)S(1)} %get-tuple-element.275), channel_id=1, source_target_pairs={{0,16},{16,0},{1,17},{17,1},{2,18},{18,2},{3,19},{19,3},{4,20},{20... | collective-permute-start | bytes 12296 | tf_op jit(solution)/shard_map/ppermute | solution.py:596
  125.9 5.8 %collective-permute-start.30 = (f32[8,128]{1,0:T(8,128)S(1)}, f32[8,128]{1,0:T(8,128)S(1)}, u32[]{:S(2)}, u32[]{:S(2)}) collective-permute-start(f32[8,128]{1,0:T(8,128)S(1)} %get-tuple-element.274), channel_id=1, source_target_pairs={{16,17},{17,16},{1,2},{2,1},{18,19},{19,18},{3,4},{4,3},{20,21},{2... | collective-permute-start | bytes 12296 | tf_op jit(solution)/shard_map/ppermute | solution.py:595
  133.0 3.7 %collective-permute-start.33 = (f32[8,128]{1,0:T(8,128)S(1)}, f32[8,128]{1,0:T(8,128)S(1)}, u32[]{:S(2)}, u32[]{:S(2)}) collective-permute-start(f32[8,128]{1,0:T(8,128)S(1)} %get-tuple-element.284), channel_id=1, source_target_pairs={{0,16},{16,0},{1,17},{17,1},{2,18},{18,2},{3,19},{19,3},{4,20},{20... | collective-permute-start | bytes 12296 | tf_op jit(solution)/shard_map/ppermute | solution.py:596
  133.0 5.8 %collective-permute-start.32 = (f32[8,128]{1,0:T(8,128)S(1)}, f32[8,128]{1,0:T(8,128)S(1)}, u32[]{:S(2)}, u32[]{:S(2)}) collective-permute-start(f32[8,128]{1,0:T(8,128)S(1)} %get-tuple-element.283), channel_id=1, source_target_pairs={{16,17},{17,16},{1,2},{2,1},{18,19},{19,18},{3,4},{4,3},{20,21},{2... | collective-permute-start | bytes 12296 | tf_op jit(solution)/shard_map/ppermute | solution.py:595
  140.1 3.7 %collective-permute-start.35 = (f32[8,128]{1,0:T(8,128)S(1)}, f32[8,128]{1,0:T(8,128)S(1)}, u32[]{:S(2)}, u32[]{:S(2)}) collective-permute-start(f32[8,128]{1,0:T(8,128)S(1)} %get-tuple-element.293), channel_id=1, source_target_pairs={{0,16},{16,0},{1,17},{17,1},{2,18},{18,2},{3,19},{19,3},{4,20},{20... | collective-permute-start | bytes 12296 | tf_op jit(solution)/shard_map/ppermute | solution.py:596
  140.2 5.8 %collective-permute-start.34 = (f32[8,128]{1,0:T(8,128)S(1)}, f32[8,128]{1,0:T(8,128)S(1)}, u32[]{:S(2)}, u32[]{:S(2)}) collective-permute-start(f32[8,128]{1,0:T(8,128)S(1)} %get-tuple-element.292), channel_id=1, source_target_pairs={{16,17},{17,16},{1,2},{2,1},{18,19},{19,18},{3,4},{4,3},{20,21},{2... | collective-permute-start | bytes 12296 | tf_op jit(solution)/shard_map/ppermute | solution.py:595
  147.1 3.7 %collective-permute-start.36 = (f32[4,2,2,128]{3,2,1,0:T(2,128)S(1)}, f32[4,2,2,128]{3,2,1,0:T(2,128)S(1)}, u32[]{:S(2)}, u32[]{:S(2)}) collective-permute-start(f32[4,2,2,128]{3,2,1,0:T(2,128)S(1)} %rev.12), channel_id=1, source_target_pairs={{0,16},{16,0},{1,17},{17,1},{2,18},{18,2},{3,19},{19,3},{4,20},{20... | collective-permute-start | bytes 24584 | tf_op jit(solution)/shard_map/ppermute | solution.py:609

commit v18 on v17

--- a/solution.py
+++ b/solution.py
@@ -344,15 +344,12 @@
     return rows_of(small, index * N * HALF)
 
 
-def join_kernel(keep, recv, small):
+def start_kernel(keep, recv_0, recv_1, small_keep, small_recv, edge, msg_a, msg_b, q_out, small):
     n = ROWS * HALF
-    for i in range(0, keep.shape[0], n):
-        small[2 * i:2 * i + n, :] = keep[i:i + n, :]
-        small[2 * i + n:2 * i + n + HALF, :] = recv[i + HALF:i + n, :]
-        small[2 * i + n + HALF:2 * i + 2 * n, :] = recv[i:i + HALF, :]
-
-
-def start_kernel(keep, recv_0, recv_1, small, edge, msg_a, msg_b, q_out):
+    for i in range(0, small_keep.shape[0], n):
+        small[2 * i:2 * i + n, :] = small_keep[i:i + n, :]
+        small[2 * i + n:2 * i + n + HALF, :] = small_recv[i + HALF:i + n, :]
+        small[2 * i + n + HALF:2 * i + 2 * n, :] = small_recv[i:i + HALF, :]
     halves = ((keep,), (recv_0, recv_1))
     f = small_part(small, INITIAL)
     q = inner_product(f, halves)
@@ -550,21 +547,13 @@
             compiler_params=limit,
             name="small",
         )(arrived.reshape(n_col, slots * frames + width), capacity, initial)
-        small = pl.pallas_call(
-            join_kernel,
-            out_shape=unit_small,
-            in_specs=[vmem, vmem],
-            out_specs=vmem,
-            compiler_params=limit,
-            name="join",
-        )(small, lax.ppermute(send, "row", swap))
-        return small, beyond_0
-
-    small, beyond_0 = lax.cond(
+        return small, lax.ppermute(send, "row", swap), beyond_0
+
+    *small, beyond_0 = lax.cond(
         row < lax.axis_size("row"),
         beside,
         lambda currents, slot_tile, capacity, initial, facing_0: (
-            jnp.zeros(unit_small.shape, jnp.float32), facing_0
+            *jnp.zeros((2, (STEPS + 2) * ROWS * HALF, width), jnp.float32), facing_0
         ),
         currents, slot_tile, capacity, initial, facing_0,
     )
@@ -586,7 +575,7 @@
 
     first_shape = jax.ShapeDtypeStruct((2 * N + ROWS * width, width), jnp.float32)
     first_a_shape = jax.ShapeDtypeStruct((2 * N + 2 * ROWS * width, width), jnp.float32)
-    msg_a, msg_b, q = call(start_kernel, (first_a_shape, first_shape, shape), 28, *halves, small, edge)
+    msg_a, msg_b, q, small = call(start_kernel, (first_a_shape, first_shape, shape, unit_small), 28, *halves, *small, edge)
     field, state, frames, first = (), (), [], None
     for instant in range(STEPS):
         for pair in range(ITERS // 2):

time: 154 us -> 140 us (0.909)
  Pallas kernels: 46.8 us -> 23.3 us
  waiting for transfers between devices: 46 us -> 61.9 us
  starting transfers between devices: 54.2 us -> 49.2 us
    pallas_call x33, Pallas kernels: 39 us -> 15.5 us  [call(): pl.pallas_call(body, out_shape=outs, in_specs=[vmem] * len(ins), out_spec...]
    ppermute x16, waiting for transfers between devices: 21.7 us -> 32.6 us  [shards_chain(): got_b = lax.ppermute(msg_b, both, b_pairs)]
    ppermute x16, starting transfers between devices: 37.9 us -> 32.9 us  [shards_chain(): got_b = lax.ppermute(msg_b, both, b_pairs)]
    ppermute x16, waiting for transfers between devices: 17.6 us -> 22.5 us  [shards_chain(): got_a = lax.ppermute(msg_a, 'row', swap)]
  transfers between devices with their start and end apart: 38 -> 38, of which waited for: 34 -> 34; matrix products, arithmetic and copies ran while one was open for 2% -> 2% of each run, Pallas kernels for 16% -> 9%
where the time goes in v18:
time: 140 us; the launch traced here: 139 us
  waiting for transfers between devices  61.9 us (44%)
  starting transfers between devices  49.2 us (35%)
  Pallas kernels  23.3 us (17%)
  local copies, waits for them, and re-layouts  3.29 us (2%)
    ppermute x16, starting transfers between devices, shards_chain(): got_b = lax.ppermute(msg_b, both, b_pairs)  32.9 us
    ppermute x16, waiting for transfers between devices, shards_chain(): got_b = lax.ppermute(msg_b, both, b_pairs)  32.6 us
    ppermute x16, waiting for transfers between devices, shards_chain(): got_a = lax.ppermute(msg_a, 'row', swap)  22.5 us
    pallas_call x33, Pallas kernels, call(): pl.pallas_call(body, out_shape=outs, in_specs=[vmem] * len(ins), out_spec...  15.5 us
    all_to_all x1, starting transfers between devices, beside(): lax.all_to_all(by_target, 'col', split_axis=0, concat_axis=0, tiled=True)  6.27 us
    pallas_call x4, Pallas kernels, pack(): pl.pallas_call(functools.partial(pack_kernel, n_col, sent, first, count),...  5.4 us
    ppermute x1, waiting for transfers between devices, shards_chain(): got = lax.ppermute(jnp.flip(done[:, ROWS:], 1), 'row', swap)  3.62 us
    ppermute x16, starting transfers between devices, shards_chain(): got_a = lax.ppermute(msg_a, 'row', swap)  3.22 us
  transfers between devices with their start and end apart: 38, of which 34 were waited for; matrix products, arithmetic and copies ran while one was open for 2% of the time, Pallas kernels for 9%

profile of v18, /device:TPU:8, one launch (start us, length us, event | category | flops | bytes accessed | tf_op | source)
XLA Modules:
  0.0 139.0 jit_solution(3327633210597687718)
XLA Ops:
  1.2 1.6 %collective-permute-start.2 = (f32[10,128,128]{2,1,0:T(8,128)S(1)}, f32[10,128,128]{2,1,0:T(8,128)S(1)}, u32[]{:S(2)}, u32[]{:S(2)}) collective-permute-start(f32[10,128,128]{2,1,0:T(8,128)S(1)} %pack.5), channel_id=1, source_target_pairs={{0,16},{16,0},{1,17},{17,1},{2,18},{18,2},{3,19},{19,3},{4,20},{20... | collective-permute-start | bytes 1966088 | tf_op jit(solution)/shard_map/ppermute | solution.py:522
  5.4 2.2 %pack.4 = (f32[20,128,128]{2,1,0:T(8,128)S(1)}, f32[2,128,128]{2,1,0:T(8,128)}) custom-call(s32[2,4,4]{2,1,0:T(4,128)} %pattern_hbm.7, f32[2,4,128,128]{3,2,1,0:T(8,128)} %own_hbm.7, f32[4,2,4,128,128]{4,3,2,1,0:T(8,128)} %nb_hbm.7), custom_call_target="tpu_custom_call" | custom-call | tf_op jit(solution)/shard_map/pack/pallas_call | solution.py:509
  7.6 19.8 %conditional.1 = (f32[24,128]{1,0:T(8,128)}, f32[24,128]{1,0:T(8,128)}, f32[2,128,128]{2,1,0:T(8,128)}) conditional(s32[]{:T(128)} %convert_element_type.3, f32[2,128,128]{2,1,0:T(8,128)} %get-tuple-element.165, (f32[1,1,16,4,512]{4,3,2,1,0:T(4,128)}, s32[1,1,16,4]{2,3,1,0:T(4,128)}, f32[2,4,128]{2,1,0:T(4,128)S(1)}, f32[2,4,128]{2,1,0:T(4,128)S(1)}, ...), branch_computations={%region_0.1_spmd, %region_1.2_spmd} | conditional | bytes 1532552 | solution.py:552
  8.4 1.6 %by_target.1 = f32[16,1,2176]{2,1,0:T(1,128)} custom-call(f32[16,4,512]{2,1,0:T(4,128)} %bitcast.14, s32[16,4]{1,0:T(8,128)S(1)} %copy.14.slot_tile), custom_call_target="tpu_custom_call" | custom-call | tf_op jit(solution)/shard_map/cond/branch_1_fun/by_target/pallas_call | solution.py:531
  10.0 6.3 %all-to-all-start = ((f32[16,1,2176]{2,1,0:T(1,128)}), f32[16,1,2176]{2,1,0:T(1,128)}, u32[]{:S(2)}, u32[]{:S(2)}) async-start(f32[16,1,2176]{2,1,0:T(1,128)} %by_target.1), calls=%async_computation | async-start | bytes 278528 | tf_op jit(solution)/shard_map/cond/branch_1_fun/all_to_all | solution.py:539
  16.3 3.1 %collective-permute-start.1 = (f32[2,128,128]{2,1,0:T(8,128)}, f32[2,128,128]{2,1,0:T(8,128)}, u32[]{:S(2)}, u32[]{:S(2)}) collective-permute-start(f32[2,128,128]{2,1,0:T(8,128)} %get-tuple-element.22), channel_id=1, source_target_pairs={{16,17},{17,16},{1,2},{2,1},{18,19},{19,18},{3,4},{4,3},{20,21},{2... | collective-permute-start | bytes 393224 | tf_op jit(solution)/shard_map/cond/branch_1_fun/ppermute | solution.py:529
  19.4 2.5 %all-to-all-done = f32[16,1,2176]{2,1,0:T(1,128)} async-done(((f32[16,1,2176]{2,1,0:T(1,128)}), f32[16,1,2176]{2,1,0:T(1,128)}, u32[]{:S(2)}, u32[]{:S(2)}) %all-to-all-start) | async-done | bytes 139296 | tf_op jit(solution)/shard_map/cond/branch_1_fun/all_to_all | solution.py:539
  25.1 1.6 %copy.23 = f32[2,128,128]{2,1,0:T(8,128)} copy(f32[2,128,128]{2,1,0:T(8,128)} %collective-permute-done.1) | data formatting | bytes 262144 | tf_op jit(solution)/shard_map/cond
  28.4 1.6 %collective-permute-start.5 = (f32[520,128]{1,0:T(8,128)S(1)}, f32[520,128]{1,0:T(8,128)S(1)}, u32[]{:S(2)}, u32[]{:S(2)}) collective-permute-start(f32[520,128]{1,0:T(8,128)S(1)} %get-tuple-element.171), channel_id=1, source_target_pairs={{0,16},{16,0},{1,17},{17,1},{2,18},{18,2},{3,19},{19,3},{4,20},{20... | collective-permute-start | bytes 798728 | tf_op jit(solution)/shard_map/ppermute | solution.py:585
  30.0 2.2 %collective-permute-start.4 = (f32[264,128]{1,0:T(8,128)S(1)}, f32[264,128]{1,0:T(8,128)S(1)}, u32[]{:S(2)}, u32[]{:S(2)}) collective-permute-start(f32[264,128]{1,0:T(8,128)S(1)} %get-tuple-element.169), channel_id=1, source_target_pairs={{16,17},{17,16},{1,2},{2,1},{18,19},{19,18},{3,4},{4,3},{20,21},{2... | collective-permute-start | bytes 405512 | tf_op jit(solution)/shard_map/ppermute | solution.py:584
  32.2 5.1 %collective-permute-done.4.first_b.got_b = f32[264,128]{1,0:T(8,128)S(1)} collective-permute-done((f32[264,128]{1,0:T(8,128)S(1)}, f32[264,128]{1,0:T(8,128)S(1)}, u32[]{:S(2)}, u32[]{:S(2)}) %collective-permute-start.4) | collective-permute-done | bytes 135200 | tf_op jit(solution)/shard_map/ppermute | solution.py:584
  38.8 1.9 %collective-permute-start.6 = (f32[8,128]{1,0:T(8,128)S(1)}, f32[8,128]{1,0:T(8,128)S(1)}, u32[]{:S(2)}, u32[]{:S(2)}) collective-permute-start(f32[8,128]{1,0:T(8,128)S(1)} %get-tuple-element.176), channel_id=1, source_target_pairs={{16,17},{17,16},{1,2},{2,1},{18,19},{19,18},{3,4},{4,3},{20,21},{2... | collective-permute-start | bytes 12296 | tf_op jit(solution)/shard_map/ppermute | solution.py:584
  42.3 2.4 %collective-permute-done.6.got_b = f32[8,128]{1,0:T(8,128)S(1)} collective-permute-done((f32[8,128]{1,0:T(8,128)S(1)}, f32[8,128]{1,0:T(8,128)S(1)}, u32[]{:S(2)}, u32[]{:S(2)}) %collective-permute-start.6) | collective-permute-done | bytes 4128 | tf_op jit(solution)/shard_map/ppermute | solution.py:584
  45.2 2.0 %collective-permute-start.8 = (f32[8,128]{1,0:T(8,128)S(1)}, f32[8,128]{1,0:T(8,128)S(1)}, u32[]{:S(2)}, u32[]{:S(2)}) collective-permute-start(f32[8,128]{1,0:T(8,128)S(1)} %get-tuple-element.185), channel_id=1, source_target_pairs={{16,17},{17,16},{1,2},{2,1},{18,19},{19,18},{3,4},{4,3},{20,21},{2... | collective-permute-start | bytes 12296 | tf_op jit(solution)/shard_map/ppermute | solution.py:584
  47.3 1.6 %collective-permute-done.9.got_a = f32[8,128]{1,0:T(8,128)S(1)} collective-permute-done((f32[8,128]{1,0:T(8,128)S(1)}, f32[8,128]{1,0:T(8,128)S(1)}, u32[]{:S(2)}, u32[]{:S(2)}) %collective-permute-start.9) | collective-permute-done | bytes 4128 | tf_op jit(solution)/shard_map/ppermute | solution.py:585
  49.2 1.8 %collective-permute-done.8.got_b = f32[8,128]{1,0:T(8,128)S(1)} collective-permute-done((f32[8,128]{1,0:T(8,128)S(1)}, f32[8,128]{1,0:T(8,128)S(1)}, u32[]{:S(2)}, u32[]{:S(2)}) %collective-permute-start.8) | collective-permute-done | bytes 4128 | tf_op jit(solution)/shard_map/ppermute | solution.py:584
  51.6 2.0 %collective-permute-start.10 = (f32[8,128]{1,0:T(8,128)S(1)}, f32[8,128]{1,0:T(8,128)S(1)}, u32[]{:S(2)}, u32[]{:S(2)}) collective-permute-start(f32[8,128]{1,0:T(8,128)S(1)} %get-tuple-element.194), channel_id=1, source_target_pairs={{16,17},{17,16},{1,2},{2,1},{18,19},{19,18},{3,4},{4,3},{20,21},{2... | collective-permute-start | bytes 12296 | tf_op jit(solution)/shard_map/ppermute | solution.py:584
  53.7 1.6 %collective-permute-done.11.got_a = f32[8,128]{1,0:T(8,128)S(1)} collective-permute-done((f32[8,128]{1,0:T(8,128)S(1)}, f32[8,128]{1,0:T(8,128)S(1)}, u32[]{:S(2)}, u32[]{:S(2)}) %collective-permute-start.11) | collective-permute-done | bytes 4128 | tf_op jit(solution)/shard_map/ppermute | solution.py:585
  55.6 1.8 %collective-permute-done.10.got_b = f32[8,128]{1,0:T(8,128)S(1)} collective-permute-done((f32[8,128]{1,0:T(8,128)S(1)}, f32[8,128]{1,0:T(8,128)S(1)}, u32[]{:S(2)}, u32[]{:S(2)}) %collective-permute-start.10) | collective-permute-done | bytes 4128 | tf_op jit(solution)/shard_map/ppermute | solution.py:584
  58.0 2.0 %collective-permute-start.12 = (f32[8,128]{1,0:T(8,128)S(1)}, f32[8,128]{1,0:T(8,128)S(1)}, u32[]{:S(2)}, u32[]{:S(2)}) collective-permute-start(f32[8,128]{1,0:T(8,128)S(1)} %get-tuple-element.204), channel_id=1, source_target_pairs={{16,17},{17,16},{1,2},{2,1},{18,19},{19,18},{3,4},{4,3},{20,21},{2... | collective-permute-start | bytes 12296 | tf_op jit(solution)/shard_map/ppermute | solution.py:584
  62.0 1.8 %collective-permute-done.12.got_b = f32[8,128]{1,0:T(8,128)S(1)} collective-permute-done((f32[8,128]{1,0:T(8,128)S(1)}, f32[8,128]{1,0:T(8,128)S(1)}, u32[]{:S(2)}, u32[]{:S(2)}) %collective-permute-start.12) | collective-permute-done | bytes 4128 | tf_op jit(solution)/shard_map/ppermute | solution.py:584
  64.4 2.0 %collective-permute-start.14 = (f32[8,128]{1,0:T(8,128)S(1)}, f32[8,128]{1,0:T(8,128)S(1)}, u32[]{:S(2)}, u32[]{:S(2)}) collective-permute-start(f32[8,128]{1,0:T(8,128)S(1)} %get-tuple-element.210), channel_id=1, source_target_pairs={{16,17},{17,16},{1,2},{2,1},{18,19},{19,18},{3,4},{4,3},{20,21},{2... | collective-permute-start | bytes 12296 | tf_op jit(solution)/shard_map/ppermute | solution.py:584
  66.4 1.6 %collective-permute-done.15.got_a = f32[8,128]{1,0:T(8,128)S(1)} collective-permute-done((f32[8,128]{1,0:T(8,128)S(1)}, f32[8,128]{1,0:T(8,128)S(1)}, u32[]{:S(2)}, u32[]{:S(2)}) %collective-permute-start.15) | collective-permute-done | bytes 4128 | tf_op jit(solution)/shard_map/ppermute | solution.py:585
  68.4 1.8 %collective-permute-done.14.got_b = f32[8,128]{1,0:T(8,128)S(1)} collective-permute-done((f32[8,128]{1,0:T(8,128)S(1)}, f32[8,128]{1,0:T(8,128)S(1)}, u32[]{:S(2)}, u32[]{:S(2)}) %collective-permute-start.14) | collective-permute-done | bytes 4128 | tf_op jit(solution)/shard_map/ppermute | solution.py:584
  70.8 2.0 %collective-permute-start.16 = (f32[8,128]{1,0:T(8,128)S(1)}, f32[8,128]{1,0:T(8,128)S(1)}, u32[]{:S(2)}, u32[]{:S(2)}) collective-permute-start(f32[8,128]{1,0:T(8,128)S(1)} %get-tuple-element.219), channel_id=1, source_target_pairs={{16,17},{17,16},{1,2},{2,1},{18,19},{19,18},{3,4},{4,3},{20,21},{2... | collective-permute-start | bytes 12296 | tf_op jit(solution)/shard_map/ppermute | solution.py:584
  72.8 1.6 %collective-permute-done.17.got_a = f32[8,128]{1,0:T(8,128)S(1)} collective-permute-done((f32[8,128]{1,0:T(8,128)S(1)}, f32[8,128]{1,0:T(8,128)S(1)}, u32[]{:S(2)}, u32[]{:S(2)}) %collective-permute-start.17) | collective-permute-done | bytes 4128 | tf_op jit(solution)/shard_map/ppermute | solution.py:585
  74.8 1.8 %collective-permute-done.16.got_b = f32[8,128]{1,0:T(8,128)S(1)} collective-permute-done((f32[8,128]{1,0:T(8,128)S(1)}, f32[8,128]{1,0:T(8,128)S(1)}, u32[]{:S(2)}, u32[]{:S(2)}) %collective-permute-start.16) | collective-permute-done | bytes 4128 | tf_op jit(solution)/shard_map/ppermute | solution.py:584
  77.2 2.0 %collective-permute-start.18 = (f32[8,128]{1,0:T(8,128)S(1)}, f32[8,128]{1,0:T(8,128)S(1)}, u32[]{:S(2)}, u32[]{:S(2)}) collective-permute-start(f32[8,128]{1,0:T(8,128)S(1)} %get-tuple-element.228), channel_id=1, source_target_pairs={{16,17},{17,16},{1,2},{2,1},{18,19},{19,18},{3,4},{4,3},{20,21},{2... | collective-permute-start | bytes 12296 | tf_op jit(solution)/shard_map/ppermute | solution.py:584
  79.2 1.6 %collective-permute-done.19.got_a = f32[8,128]{1,0:T(8,128)S(1)} collective-permute-done((f32[8,128]{1,0:T(8,128)S(1)}, f32[8,128]{1,0:T(8,128)S(1)}, u32[]{:S(2)}, u32[]{:S(2)}) %collective-permute-start.19) | collective-permute-done | bytes 4128 | tf_op jit(solution)/shard_map/ppermute | solution.py:585
  81.2 1.8 %collective-permute-done.18.got_b = f32[8,128]{1,0:T(8,128)S(1)} collective-permute-done((f32[8,128]{1,0:T(8,128)S(1)}, f32[8,128]{1,0:T(8,128)S(1)}, u32[]{:S(2)}, u32[]{:S(2)}) %collective-permute-start.18) | collective-permute-done | bytes 4128 | tf_op jit(solution)/shard_map/ppermute | solution.py:584
  83.6 2.0 %collective-permute-start.20 = (f32[8,128]{1,0:T(8,128)S(1)}, f32[8,128]{1,0:T(8,128)S(1)}, u32[]{:S(2)}, u32[]{:S(2)}) collective-permute-start(f32[8,128]{1,0:T(8,128)S(1)} %get-tuple-element.238), channel_id=1, source_target_pairs={{16,17},{17,16},{1,2},{2,1},{18,19},{19,18},{3,4},{4,3},{20,21},{2... | collective-permute-start | bytes 12296 | tf_op jit(solution)/shard_map/ppermute | solution.py:584
  87.6 1.8 %collective-permute-done.20.got_b = f32[8,128]{1,0:T(8,128)S(1)} collective-permute-done((f32[8,128]{1,0:T(8,128)S(1)}, f32[8,128]{1,0:T(8,128)S(1)}, u32[]{:S(2)}, u32[]{:S(2)}) %collective-permute-start.20) | collective-permute-done | bytes 4128 | tf_op jit(solution)/shard_map/ppermute | solution.py:584
  90.0 2.0 %collective-permute-start.22 = (f32[8,128]{1,0:T(8,128)S(1)}, f32[8,128]{1,0:T(8,128)S(1)}, u32[]{:S(2)}, u32[]{:S(2)}) collective-permute-start(f32[8,128]{1,0:T(8,128)S(1)} %get-tuple-element.244), channel_id=1, source_target_pairs={{16,17},{17,16},{1,2},{2,1},{18,19},{19,18},{3,4},{4,3},{20,21},{2... | collective-permute-start | bytes 12296 | tf_op jit(solution)/shard_map/ppermute | solution.py:584
  92.0 1.6 %collective-permute-done.23.got_a = f32[8,128]{1,0:T(8,128)S(1)} collective-permute-done((f32[8,128]{1,0:T(8,128)S(1)}, f32[8,128]{1,0:T(8,128)S(1)}, u32[]{:S(2)}, u32[]{:S(2)}) %collective-permute-start.23) | collective-permute-done | bytes 4128 | tf_op jit(solution)/shard_map/ppermute | solution.py:585
  94.0 1.8 %collective-permute-done.22.got_b = f32[8,128]{1,0:T(8,128)S(1)} collective-permute-done((f32[8,128]{1,0:T(8,128)S(1)}, f32[8,128]{1,0:T(8,128)S(1)}, u32[]{:S(2)}, u32[]{:S(2)}) %collective-permute-start.22) | collective-permute-done | bytes 4128 | tf_op jit(solution)/shard_map/ppermute | solution.py:584
  96.4 2.1 %collective-permute-start.24 = (f32[8,128]{1,0:T(8,128)S(1)}, f32[8,128]{1,0:T(8,128)S(1)}, u32[]{:S(2)}, u32[]{:S(2)}) collective-permute-start(f32[8,128]{1,0:T(8,128)S(1)} %get-tuple-element.253), channel_id=1, source_target_pairs={{16,17},{17,16},{1,2},{2,1},{18,19},{19,18},{3,4},{4,3},{20,21},{2... | collective-permute-start | bytes 12296 | tf_op jit(solution)/shard_map/ppermute | solution.py:584
  100.4 1.8 %collective-permute-done.24.got_b = f32[8,128]{1,0:T(8,128)S(1)} collective-permute-done((f32[8,128]{1,0:T(8,128)S(1)}, f32[8,128]{1,0:T(8,128)S(1)}, u32[]{:S(2)}, u32[]{:S(2)}) %collective-permute-start.24) | collective-permute-done | bytes 4128 | tf_op jit(solution)/shard_map/ppermute | solution.py:584
  102.8 2.1 %collective-permute-start.26 = (f32[8,128]{1,0:T(8,128)S(1)}, f32[8,128]{1,0:T(8,128)S(1)}, u32[]{:S(2)}, u32[]{:S(2)}) collective-permute-start(f32[8,128]{1,0:T(8,128)S(1)} %get-tuple-element.262), channel_id=1, source_target_pairs={{16,17},{17,16},{1,2},{2,1},{18,19},{19,18},{3,4},{4,3},{20,21},{2... | collective-permute-start | bytes 12296 | tf_op jit(solution)/shard_map/ppermute | solution.py:584
  106.8 1.8 %collective-permute-done.26.got_b = f32[8,128]{1,0:T(8,128)S(1)} collective-permute-done((f32[8,128]{1,0:T(8,128)S(1)}, f32[8,128]{1,0:T(8,128)S(1)}, u32[]{:S(2)}, u32[]{:S(2)}) %collective-permute-start.26) | collective-permute-done | bytes 4128 | tf_op jit(solution)/shard_map/ppermute | solution.py:584
  109.2 2.1 %collective-permute-start.28 = (f32[8,128]{1,0:T(8,128)S(1)}, f32[8,128]{1,0:T(8,128)S(1)}, u32[]{:S(2)}, u32[]{:S(2)}) collective-permute-start(f32[8,128]{1,0:T(8,128)S(1)} %get-tuple-element.272), channel_id=1, source_target_pairs={{16,17},{17,16},{1,2},{2,1},{18,19},{19,18},{3,4},{4,3},{20,21},{2... | collective-permute-start | bytes 12296 | tf_op jit(solution)/shard_map/ppermute | solution.py:584
  113.2 1.8 %collective-permute-done.28.got_b = f32[8,128]{1,0:T(8,128)S(1)} collective-permute-done((f32[8,128]{1,0:T(8,128)S(1)}, f32[8,128]{1,0:T(8,128)S(1)}, u32[]{:S(2)}, u32[]{:S(2)}) %collective-permute-start.28) | collective-permute-done | bytes 4128 | tf_op jit(solution)/shard_map/ppermute | solution.py:584
  115.6 2.1 %collective-permute-start.30 = (f32[8,128]{1,0:T(8,128)S(1)}, f32[8,128]{1,0:T(8,128)S(1)}, u32[]{:S(2)}, u32[]{:S(2)}) collective-permute-start(f32[8,128]{1,0:T(8,128)S(1)} %get-tuple-element.278), channel_id=1, source_target_pairs={{16,17},{17,16},{1,2},{2,1},{18,19},{19,18},{3,4},{4,3},{20,21},{2... | collective-permute-start | bytes 12296 | tf_op jit(solution)/shard_map/ppermute | solution.py:584
  119.6 1.8 %collective-permute-done.30.got_b = f32[8,128]{1,0:T(8,128)S(1)} collective-permute-done((f32[8,128]{1,0:T(8,128)S(1)}, f32[8,128]{1,0:T(8,128)S(1)}, u32[]{:S(2)}, u32[]{:S(2)}) %collective-permute-start.30) | collective-permute-done | bytes 4128 | tf_op jit(solution)/shard_map/ppermute | solution.py:584
  122.0 2.1 %collective-permute-start.32 = (f32[8,128]{1,0:T(8,128)S(1)}, f32[8,128]{1,0:T(8,128)S(1)}, u32[]{:S(2)}, u32[]{:S(2)}) collective-permute-start(f32[8,128]{1,0:T(8,128)S(1)} %get-tuple-element.287), channel_id=1, source_target_pairs={{16,17},{17,16},{1,2},{2,1},{18,19},{19,18},{3,4},{4,3},{20,21},{2... | collective-permute-start | bytes 12296 | tf_op jit(solution)/shard_map/ppermute | solution.py:584
  126.0 1.8 %collective-permute-done.32.got_b = f32[8,128]{1,0:T(8,128)S(1)} collective-permute-done((f32[8,128]{1,0:T(8,128)S(1)}, f32[8,128]{1,0:T(8,128)S(1)}, u32[]{:S(2)}, u32[]{:S(2)}) %collective-permute-start.32) | collective-permute-done | bytes 4128 | tf_op jit(solution)/shard_map/ppermute | solution.py:584
  128.4 2.1 %collective-permute-start.34 = (f32[8,128]{1,0:T(8,128)S(1)}, f32[8,128]{1,0:T(8,128)S(1)}, u32[]{:S(2)}, u32[]{:S(2)}) collective-permute-start(f32[8,128]{1,0:T(8,128)S(1)} %get-tuple-element.296), channel_id=1, source_target_pairs={{16,17},{17,16},{1,2},{2,1},{18,19},{19,18},{3,4},{4,3},{20,21},{2... | collective-permute-start | bytes 12296 | tf_op jit(solution)/shard_map/ppermute | solution.py:584
  132.4 1.8 %collective-permute-done.34.got_b = f32[8,128]{1,0:T(8,128)S(1)} collective-permute-done((f32[8,128]{1,0:T(8,128)S(1)}, f32[8,128]{1,0:T(8,128)S(1)}, u32[]{:S(2)}, u32[]{:S(2)}) %collective-permute-start.34) | collective-permute-done | bytes 4128 | tf_op jit(solution)/shard_map/ppermute | solution.py:584
  134.7 3.6 %collective-permute-done.36 = f32[4,2,2,128]{3,2,1,0:T(2,128)S(1)} collective-permute-done((f32[4,2,2,128]{3,2,1,0:T(2,128)S(1)}, f32[4,2,2,128]{3,2,1,0:T(2,128)S(1)}, u32[]{:S(2)}, u32[]{:S(2)}) %collective-permute-start.36) | collective-permute-done | bytes 8224 | tf_op jit(solution)/shard_map/ppermute | solution.py:598
  (84 shorter events, 39.6 us)
Async XLA Ops:
  1.2 26.2 %collective-permute-start.2 = (f32[10,128,128]{2,1,0:T(8,128)S(1)}, f32[10,128,128]{2,1,0:T(8,128)S(1)}, u32[]{:S(2)}, u32[]{:S(2)}) collective-permute-start(f32[10,128,128]{2,1,0:T(8,128)S(1)} %pack.5), channel_id=1, source_target_pairs={{0,16},{16,0},{1,17},{17,1},{2,18},{18,2},{3,19},{19,3},{4,20},{20... | collective-permute-start | bytes 1966088 | tf_op jit(solution)/shard_map/ppermute | solution.py:522
  3.9 23.5 %collective-permute-start.3 = (f32[6,128,128]{2,1,0:T(8,128)S(1)}, f32[6,128,128]{2,1,0:T(8,128)S(1)}, u32[]{:S(2)}, u32[]{:S(2)}) collective-permute-start(f32[6,128,128]{2,1,0:T(8,128)S(1)} %pack.6), channel_id=1, source_target_pairs={{0,16},{16,0},{1,17},{17,1},{2,18},{18,2},{3,19},{19,3},{4,20},{20... | collective-permute-start | bytes 1179656 | tf_op jit(solution)/shard_map/ppermute | solution.py:522
  4.5 3.1 %copy-start.1 = (f32[2,4,128]{2,1,0:T(4,128)S(1)}, f32[2,4,128]{2,1,0:T(4,128)}, u32[]{:S(2)}) copy-start(f32[2,4,128]{2,1,0:T(4,128)} %param.12) | copy-start | bytes 12292
  4.5 3.2 %copy-start.2 = (f32[2,4,128]{2,1,0:T(4,128)S(1)}, f32[2,4,128]{2,1,0:T(4,128)}, u32[]{:S(2)}) copy-start(f32[2,4,128]{2,1,0:T(4,128)} %param.13) | copy-start | bytes 12292
  10.0 11.9 %all-to-all-start = ((f32[16,1,2176]{2,1,0:T(1,128)}), f32[16,1,2176]{2,1,0:T(1,128)}, u32[]{:S(2)}, u32[]{:S(2)}) async-start(f32[16,1,2176]{2,1,0:T(1,128)} %by_target.1), calls=%async_computation | async-start | bytes 278528 | tf_op jit(solution)/shard_map/cond/branch_1_fun/all_to_all | solution.py:539
  16.3 8.9 %collective-permute-start.1 = (f32[2,128,128]{2,1,0:T(8,128)}, f32[2,128,128]{2,1,0:T(8,128)}, u32[]{:S(2)}, u32[]{:S(2)}) collective-permute-start(f32[2,128,128]{2,1,0:T(8,128)} %get-tuple-element.22), channel_id=1, source_target_pairs={{16,17},{17,16},{1,2},{2,1},{18,19},{19,18},{3,4},{4,3},{20,21},{2... | collective-permute-start | bytes 393224 | tf_op jit(solution)/shard_map/cond/branch_1_fun/ppermute | solution.py:529
  23.6 3.8 %collective-permute-start = (f32[24,128]{1,0:T(8,128)S(1)}, f32[24,128]{1,0:T(8,128)}, u32[]{:S(2)}, u32[]{:S(2)}) collective-permute-start(f32[24,128]{1,0:T(8,128)S(1)} %get-tuple-element.21), channel_id=1, source_target_pairs={{0,16},{16,0},{1,17},{17,1},{2,18},{18,2},{3,19},{19,3},{4,20},{20... | collective-permute-start | bytes 36872 | tf_op jit(solution)/shard_map/cond/branch_1_fun/ppermute | solution.py:550
  27.4 9.9 %copy-start = (f32[2,128,128]{2,1,0:T(8,128)S(1)}, f32[2,128,128]{2,1,0:T(8,128)}, u32[]{:S(2)}) copy-start(f32[2,128,128]{2,1,0:T(8,128)} %get-tuple-element.170.beyond_0) | copy-start | bytes 393220
  28.4 8.8 %collective-permute-start.5 = (f32[520,128]{1,0:T(8,128)S(1)}, f32[520,128]{1,0:T(8,128)S(1)}, u32[]{:S(2)}, u32[]{:S(2)}) collective-permute-start(f32[520,128]{1,0:T(8,128)S(1)} %get-tuple-element.171), channel_id=1, source_target_pairs={{0,16},{16,0},{1,17},{17,1},{2,18},{18,2},{3,19},{19,3},{4,20},{20... | collective-permute-start | bytes 798728 | tf_op jit(solution)/shard_map/ppermute | solution.py:585
  30.0 7.2 %collective-permute-start.4 = (f32[264,128]{1,0:T(8,128)S(1)}, f32[264,128]{1,0:T(8,128)S(1)}, u32[]{:S(2)}, u32[]{:S(2)}) collective-permute-start(f32[264,128]{1,0:T(8,128)S(1)} %get-tuple-element.169), channel_id=1, source_target_pairs={{16,17},{17,16},{1,2},{2,1},{18,19},{19,18},{3,4},{4,3},{20,21},{2... | collective-permute-start | bytes 405512 | tf_op jit(solution)/shard_map/ppermute | solution.py:584
  38.2 3.7 %collective-permute-start.7 = (f32[8,128]{1,0:T(8,128)S(1)}, f32[8,128]{1,0:T(8,128)S(1)}, u32[]{:S(2)}, u32[]{:S(2)}) collective-permute-start(f32[8,128]{1,0:T(8,128)S(1)} %get-tuple-element.177), channel_id=1, source_target_pairs={{0,16},{16,0},{1,17},{17,1},{2,18},{18,2},{3,19},{19,3},{4,20},{20... | collective-permute-start | bytes 12296 | tf_op jit(solution)/shard_map/ppermute | solution.py:585
  38.8 5.8 %collective-permute-start.6 = (f32[8,128]{1,0:T(8,128)S(1)}, f32[8,128]{1,0:T(8,128)S(1)}, u32[]{:S(2)}, u32[]{:S(2)}) collective-permute-start(f32[8,128]{1,0:T(8,128)S(1)} %get-tuple-element.176), channel_id=1, source_target_pairs={{16,17},{17,16},{1,2},{2,1},{18,19},{19,18},{3,4},{4,3},{20,21},{2... | collective-permute-start | bytes 12296 | tf_op jit(solution)/shard_map/ppermute | solution.py:584
  45.1 3.7 %collective-permute-start.9 = (f32[8,128]{1,0:T(8,128)S(1)}, f32[8,128]{1,0:T(8,128)S(1)}, u32[]{:S(2)}, u32[]{:S(2)}) collective-permute-start(f32[8,128]{1,0:T(8,128)S(1)} %get-tuple-element.186), channel_id=1, source_target_pairs={{0,16},{16,0},{1,17},{17,1},{2,18},{18,2},{3,19},{19,3},{4,20},{20... | collective-permute-start | bytes 12296 | tf_op jit(solution)/shard_map/ppermute | solution.py:585
  45.2 5.8 %collective-permute-start.8 = (f32[8,128]{1,0:T(8,128)S(1)}, f32[8,128]{1,0:T(8,128)S(1)}, u32[]{:S(2)}, u32[]{:S(2)}) collective-permute-start(f32[8,128]{1,0:T(8,128)S(1)} %get-tuple-element.185), channel_id=1, source_target_pairs={{16,17},{17,16},{1,2},{2,1},{18,19},{19,18},{3,4},{4,3},{20,21},{2... | collective-permute-start | bytes 12296 | tf_op jit(solution)/shard_map/ppermute | solution.py:584
  51.5 3.7 %collective-permute-start.11 = (f32[8,128]{1,0:T(8,128)S(1)}, f32[8,128]{1,0:T(8,128)S(1)}, u32[]{:S(2)}, u32[]{:S(2)}) collective-permute-start(f32[8,128]{1,0:T(8,128)S(1)} %get-tuple-element.195), channel_id=1, source_target_pairs={{0,16},{16,0},{1,17},{17,1},{2,18},{18,2},{3,19},{19,3},{4,20},{20... | collective-permute-start | bytes 12296 | tf_op jit(solution)/shard_map/ppermute | solution.py:585
  51.6 5.8 %collective-permute-start.10 = (f32[8,128]{1,0:T(8,128)S(1)}, f32[8,128]{1,0:T(8,128)S(1)}, u32[]{:S(2)}, u32[]{:S(2)}) collective-permute-start(f32[8,128]{1,0:T(8,128)S(1)} %get-tuple-element.194), channel_id=1, source_target_pairs={{16,17},{17,16},{1,2},{2,1},{18,19},{19,18},{3,4},{4,3},{20,21},{2... | collective-permute-start | bytes 12296 | tf_op jit(solution)/shard_map/ppermute | solution.py:584
  57.9 3.7 %collective-permute-start.13 = (f32[8,128]{1,0:T(8,128)S(1)}, f32[8,128]{1,0:T(8,128)S(1)}, u32[]{:S(2)}, u32[]{:S(2)}) collective-permute-start(f32[8,128]{1,0:T(8,128)S(1)} %get-tuple-element.205), channel_id=1, source_target_pairs={{0,16},{16,0},{1,17},{17,1},{2,18},{18,2},{3,19},{19,3},{4,20},{20... | collective-permute-start | bytes 12296 | tf_op jit(solution)/shard_map/ppermute | solution.py:585
  58.0 5.8 %collective-permute-start.12 = (f32[8,128]{1,0:T(8,128)S(1)}, f32[8,128]{1,0:T(8,128)S(1)}, u32[]{:S(2)}, u32[]{:S(2)}) collective-permute-start(f32[8,128]{1,0:T(8,128)S(1)} %get-tuple-element.204), channel_id=1, source_target_pairs={{16,17},{17,16},{1,2},{2,1},{18,19},{19,18},{3,4},{4,3},{20,21},{2... | collective-permute-start | bytes 12296 | tf_op jit(solution)/shard_map/ppermute | solution.py:584
  64.3 3.7 %collective-permute-start.15 = (f32[8,128]{1,0:T(8,128)S(1)}, f32[8,128]{1,0:T(8,128)S(1)}, u32[]{:S(2)}, u32[]{:S(2)}) collective-permute-start(f32[8,128]{1,0:T(8,128)S(1)} %get-tuple-element.211), channel_id=1, source_target_pairs={{0,16},{16,0},{1,17},{17,1},{2,18},{18,2},{3,19},{19,3},{4,20},{20... | collective-permute-start | bytes 12296 | tf_op jit(solution)/shard_map/ppermute | solution.py:585
  64.4 5.8 %collective-permute-start.14 = (f32[8,128]{1,0:T(8,128)S(1)}, f32[8,128]{1,0:T(8,128)S(1)}, u32[]{:S(2)}, u32[]{:S(2)}) collective-permute-start(f32[8,128]{1,0:T(8,128)S(1)} %get-tuple-element.210), channel_id=1, source_target_pairs={{16,17},{17,16},{1,2},{2,1},{18,19},{19,18},{3,4},{4,3},{20,21},{2... | collective-permute-start | bytes 12296 | tf_op jit(solution)/shard_map/ppermute | solution.py:584
  70.7 3.7 %collective-permute-start.17 = (f32[8,128]{1,0:T(8,128)S(1)}, f32[8,128]{1,0:T(8,128)S(1)}, u32[]{:S(2)}, u32[]{:S(2)}) collective-permute-start(f32[8,128]{1,0:T(8,128)S(1)} %get-tuple-element.220), channel_id=1, source_target_pairs={{0,16},{16,0},{1,17},{17,1},{2,18},{18,2},{3,19},{19,3},{4,20},{20... | collective-permute-start | bytes 12296 | tf_op jit(solution)/shard_map/ppermute | solution.py:585
  70.8 5.8 %collective-permute-start.16 = (f32[8,128]{1,0:T(8,128)S(1)}, f32[8,128]{1,0:T(8,128)S(1)}, u32[]{:S(2)}, u32[]{:S(2)}) collective-permute-start(f32[8,128]{1,0:T(8,128)S(1)} %get-tuple-element.219), channel_id=1, source_target_pairs={{16,17},{17,16},{1,2},{2,1},{18,19},{19,18},{3,4},{4,3},{20,21},{2... | collective-permute-start | bytes 12296 | tf_op jit(solution)/shard_map/ppermute | solution.py:584
  77.1 3.7 %collective-permute-start.19 = (f32[8,128]{1,0:T(8,128)S(1)}, f32[8,128]{1,0:T(8,128)S(1)}, u32[]{:S(2)}, u32[]{:S(2)}) collective-permute-start(f32[8,128]{1,0:T(8,128)S(1)} %get-tuple-element.229), channel_id=1, source_target_pairs={{0,16},{16,0},{1,17},{17,1},{2,18},{18,2},{3,19},{19,3},{4,20},{20... | collective-permute-start | bytes 12296 | tf_op jit(solution)/shard_map/ppermute | solution.py:585
  77.2 5.8 %collective-permute-start.18 = (f32[8,128]{1,0:T(8,128)S(1)}, f32[8,128]{1,0:T(8,128)S(1)}, u32[]{:S(2)}, u32[]{:S(2)}) collective-permute-start(f32[8,128]{1,0:T(8,128)S(1)} %get-tuple-element.228), channel_id=1, source_target_pairs={{16,17},{17,16},{1,2},{2,1},{18,19},{19,18},{3,4},{4,3},{20,21},{2... | collective-permute-start | bytes 12296 | tf_op jit(solution)/shard_map/ppermute | solution.py:584
  83.5 3.7 %collective-permute-start.21 = (f32[8,128]{1,0:T(8,128)S(1)}, f32[8,128]{1,0:T(8,128)S(1)}, u32[]{:S(2)}, u32[]{:S(2)}) collective-permute-start(f32[8,128]{1,0:T(8,128)S(1)} %get-tuple-element.239), channel_id=1, source_target_pairs={{0,16},{16,0},{1,17},{17,1},{2,18},{18,2},{3,19},{19,3},{4,20},{20... | collective-permute-start | bytes 12296 | tf_op jit(solution)/shard_map/ppermute | solution.py:585
  83.6 5.8 %collective-permute-start.20 = (f32[8,128]{1,0:T(8,128)S(1)}, f32[8,128]{1,0:T(8,128)S(1)}, u32[]{:S(2)}, u32[]{:S(2)}) collective-permute-start(f32[8,128]{1,0:T(8,128)S(1)} %get-tuple-element.238), channel_id=1, source_target_pairs={{16,17},{17,16},{1,2},{2,1},{18,19},{19,18},{3,4},{4,3},{20,21},{2... | collective-permute-start | bytes 12296 | tf_op jit(solution)/shard_map/ppermute | solution.py:584
  89.9 3.7 %collective-permute-start.23 = (f32[8,128]{1,0:T(8,128)S(1)}, f32[8,128]{1,0:T(8,128)S(1)}, u32[]{:S(2)}, u32[]{:S(2)}) collective-permute-start(f32[8,128]{1,0:T(8,128)S(1)} %get-tuple-element.245), channel_id=1, source_target_pairs={{0,16},{16,0},{1,17},{17,1},{2,18},{18,2},{3,19},{19,3},{4,20},{20... | collective-permute-start | bytes 12296 | tf_op jit(solution)/shard_map/ppermute | solution.py:585
  90.0 5.8 %collective-permute-start.22 = (f32[8,128]{1,0:T(8,128)S(1)}, f32[8,128]{1,0:T(8,128)S(1)}, u32[]{:S(2)}, u32[]{:S(2)}) collective-permute-start(f32[8,128]{1,0:T(8,128)S(1)} %get-tuple-element.244), channel_id=1, source_target_pairs={{16,17},{17,16},{1,2},{2,1},{18,19},{19,18},{3,4},{4,3},{20,21},{2... | collective-permute-start | bytes 12296 | tf_op jit(solution)/shard_map/ppermute | solution.py:584
  96.3 3.7 %collective-permute-start.25 = (f32[8,128]{1,0:T(8,128)S(1)}, f32[8,128]{1,0:T(8,128)S(1)}, u32[]{:S(2)}, u32[]{:S(2)}) collective-permute-start(f32[8,128]{1,0:T(8,128)S(1)} %get-tuple-element.254), channel_id=1, source_target_pairs={{0,16},{16,0},{1,17},{17,1},{2,18},{18,2},{3,19},{19,3},{4,20},{20... | collective-permute-start | bytes 12296 | tf_op jit(solution)/shard_map/ppermute | solution.py:585
  96.4 5.8 %collective-permute-start.24 = (f32[8,128]{1,0:T(8,128)S(1)}, f32[8,128]{1,0:T(8,128)S(1)}, u32[]{:S(2)}, u32[]{:S(2)}) collective-permute-start(f32[8,128]{1,0:T(8,128)S(1)} %get-tuple-element.253), channel_id=1, source_target_pairs={{16,17},{17,16},{1,2},{2,1},{18,19},{19,18},{3,4},{4,3},{20,21},{2... | collective-permute-start | bytes 12296 | tf_op jit(solution)/shard_map/ppermute | solution.py:584
  102.7 3.7 %collective-permute-start.27 = (f32[8,128]{1,0:T(8,128)S(1)}, f32[8,128]{1,0:T(8,128)S(1)}, u32[]{:S(2)}, u32[]{:S(2)}) collective-permute-start(f32[8,128]{1,0:T(8,128)S(1)} %get-tuple-element.263), channel_id=1, source_target_pairs={{0,16},{16,0},{1,17},{17,1},{2,18},{18,2},{3,19},{19,3},{4,20},{20... | collective-permute-start | bytes 12296 | tf_op jit(solution)/shard_map/ppermute | solution.py:585
  102.8 5.8 %collective-permute-start.26 = (f32[8,128]{1,0:T(8,128)S(1)}, f32[8,128]{1,0:T(8,128)S(1)}, u32[]{:S(2)}, u32[]{:S(2)}) collective-permute-start(f32[8,128]{1,0:T(8,128)S(1)} %get-tuple-element.262), channel_id=1, source_target_pairs={{16,17},{17,16},{1,2},{2,1},{18,19},{19,18},{3,4},{4,3},{20,21},{2... | collective-permute-start | bytes 12296 | tf_op jit(solution)/shard_map/ppermute | solution.py:584
  109.1 3.7 %collective-permute-start.29 = (f32[8,128]{1,0:T(8,128)S(1)}, f32[8,128]{1,0:T(8,128)S(1)}, u32[]{:S(2)}, u32[]{:S(2)}) collective-permute-start(f32[8,128]{1,0:T(8,128)S(1)} %get-tuple-element.273), channel_id=1, source_target_pairs={{0,16},{16,0},{1,17},{17,1},{2,18},{18,2},{3,19},{19,3},{4,20},{20... | collective-permute-start | bytes 12296 | tf_op jit(solution)/shard_map/ppermute | solution.py:585
  109.2 5.8 %collective-permute-start.28 = (f32[8,128]{1,0:T(8,128)S(1)}, f32[8,128]{1,0:T(8,128)S(1)}, u32[]{:S(2)}, u32[]{:S(2)}) collective-permute-start(f32[8,128]{1,0:T(8,128)S(1)} %get-tuple-element.272), channel_id=1, source_target_pairs={{16,17},{17,16},{1,2},{2,1},{18,19},{19,18},{3,4},{4,3},{20,21},{2... | collective-permute-start | bytes 12296 | tf_op jit(solution)/shard_map/ppermute | solution.py:584
  115.5 3.7 %collective-permute-start.31 = (f32[8,128]{1,0:T(8,128)S(1)}, f32[8,128]{1,0:T(8,128)S(1)}, u32[]{:S(2)}, u32[]{:S(2)}) collective-permute-start(f32[8,128]{1,0:T(8,128)S(1)} %get-tuple-element.279), channel_id=1, source_target_pairs={{0,16},{16,0},{1,17},{17,1},{2,18},{18,2},{3,19},{19,3},{4,20},{20... | collective-permute-start | bytes 12296 | tf_op jit(solution)/shard_map/ppermute | solution.py:585
  115.6 5.8 %collective-permute-start.30 = (f32[8,128]{1,0:T(8,128)S(1)}, f32[8,128]{1,0:T(8,128)S(1)}, u32[]{:S(2)}, u32[]{:S(2)}) collective-permute-start(f32[8,128]{1,0:T(8,128)S(1)} %get-tuple-element.278), channel_id=1, source_target_pairs={{16,17},{17,16},{1,2},{2,1},{18,19},{19,18},{3,4},{4,3},{20,21},{2... | collective-permute-start | bytes 12296 | tf_op jit(solution)/shard_map/ppermute | solution.py:584
  121.9 3.7 %collective-permute-start.33 = (f32[8,128]{1,0:T(8,128)S(1)}, f32[8,128]{1,0:T(8,128)S(1)}, u32[]{:S(2)}, u32[]{:S(2)}) collective-permute-start(f32[8,128]{1,0:T(8,128)S(1)} %get-tuple-element.288), channel_id=1, source_target_pairs={{0,16},{16,0},{1,17},{17,1},{2,18},{18,2},{3,19},{19,3},{4,20},{20... | collective-permute-start | bytes 12296 | tf_op jit(solution)/shard_map/ppermute | solution.py:585
  122.0 5.8 %collective-permute-start.32 = (f32[8,128]{1,0:T(8,128)S(1)}, f32[8,128]{1,0:T(8,128)S(1)}, u32[]{:S(2)}, u32[]{:S(2)}) collective-permute-start(f32[8,128]{1,0:T(8,128)S(1)} %get-tuple-element.287), channel_id=1, source_target_pairs={{16,17},{17,16},{1,2},{2,1},{18,19},{19,18},{3,4},{4,3},{20,21},{2... | collective-permute-start | bytes 12296 | tf_op jit(solution)/shard_map/ppermute | solution.py:584
  128.3 3.7 %collective-permute-start.35 = (f32[8,128]{1,0:T(8,128)S(1)}, f32[8,128]{1,0:T(8,128)S(1)}, u32[]{:S(2)}, u32[]{:S(2)}) collective-permute-start(f32[8,128]{1,0:T(8,128)S(1)} %get-tuple-element.297), channel_id=1, source_target_pairs={{0,16},{16,0},{1,17},{17,1},{2,18},{18,2},{3,19},{19,3},{4,20},{20... | collective-permute-start | bytes 12296 | tf_op jit(solution)/shard_map/ppermute | solution.py:585
  128.4 5.8 %collective-permute-start.34 = (f32[8,128]{1,0:T(8,128)S(1)}, f32[8,128]{1,0:T(8,128)S(1)}, u32[]{:S(2)}, u32[]{:S(2)}) collective-permute-start(f32[8,128]{1,0:T(8,128)S(1)} %get-tuple-element.296), channel_id=1, source_target_pairs={{16,17},{17,16},{1,2},{2,1},{18,19},{19,18},{3,4},{4,3},{20,21},{2... | collective-permute-start | bytes 12296 | tf_op jit(solution)/shard_map/ppermute | solution.py:584
  134.6 3.7 %collective-permute-start.36 = (f32[4,2,2,128]{3,2,1,0:T(2,128)S(1)}, f32[4,2,2,128]{3,2,1,0:T(2,128)S(1)}, u32[]{:S(2)}, u32[]{:S(2)}) collective-permute-start(f32[4,2,2,128]{3,2,1,0:T(2,128)S(1)} %rev.12), channel_id=1, source_target_pairs={{0,16},{16,0},{1,17},{17,1},{2,18},{18,2},{3,19},{19,3},{4,20},{20... | collective-permute-start | bytes 24584 | tf_op jit(solution)/shard_map/ppermute | solution.py:598

commit v19 on v18

--- a/solution.py
+++ b/solution.py
@@ -221,28 +221,29 @@
     return tiles
 
 
-def pack_kernel(n_col, sent, first, count, pattern_hbm, own_hbm, nb_hbm, out, *rest):
-    pattern_ref, sems = rest[-2:]
-    tiles = half_tiles(lax.axis_index("row"), lax.axis_index("col"), n_col, own_hbm.shape[1], sent)
-    pattern_copy = pltpu.make_async_copy(pattern_hbm, pattern_ref, sems.at[count])
+def pack_kernel(n_col, segments, pattern_hbm, own_hbm, nb_hbm, *refs):
+    *outs, pattern_ref, sems = refs
+    work = []
+    for out, (sent, first, count) in zip(outs, segments):
+        tiles = half_tiles(lax.axis_index("row"), lax.axis_index("col"), n_col, own_hbm.shape[1], sent)
+        work += [(out, i, *tiles[first + i]) for i in range(count)]
+    pattern_copy = pltpu.make_async_copy(pattern_hbm, pattern_ref, sems.at[len(work)])
     pattern_copy.start()
     copies = []
-    for i in range(count):
-        direction, row, at, _ = tiles[first + i]
+    for out, i, direction, row, at, _ in work:
         source = own_hbm.at[row, at] if direction is None else nb_hbm.at[direction, row, at]
-        copies.append(pltpu.make_async_copy(source, out.at[i], sems.at[i]))
+        copies.append(pltpu.make_async_copy(source, out.at[i], sems.at[len(copies)]))
     for copy in copies:
         copy.start()
     pattern_copy.wait()
-    for i in range(count):
-        direction, row, at, weight = tiles[first + i]
-        copies[i].wait()
+    for copy, (out, i, direction, row, at, weight) in zip(copies, work):
+        copy.wait()
         if direction is not None:
             scale = pattern_ref[row, at, direction].astype(jnp.float32)
             out[i] = out[i] * (scale if weight is None else scale * weight)
-    if not sent:
+    if len(outs) > len(segments):
         for h in range(ROWS):
-            rest[0][h] = out[SIDE_B + h * HALF]
+            outs[-1][h] = outs[0][SIDE_B + h * HALF]
 
 
 def block_of(refs, sizes, slot):
@@ -505,23 +506,23 @@
     limit = pltpu.CompilerParams(vmem_limit_bytes=16 * 2**20)
     blocks = [pltpu.with_memory_space_constraint(x, pltpu.HBM) for x in (pattern, own_block, neighbor_block)]
 
-    def pack(sent, first, count, extra=()):
+    def pack(segments, extra=()):
+        counts = [count for _, _, count in segments]
         return pl.pallas_call(
-            functools.partial(pack_kernel, n_col, sent, first, count),
-            out_shape=[jax.ShapeDtypeStruct((n, width, width), jnp.float32) for n in (count, *extra)],
+            functools.partial(pack_kernel, n_col, segments),
+            out_shape=[jax.ShapeDtypeStruct((n, width, width), jnp.float32) for n in (*counts, *extra)],
             in_specs=[hbm, hbm, hbm],
-            out_specs=[vmem] * (1 + len(extra)),
-            scratch_shapes=[pltpu.SMEM(pattern.shape, jnp.int32), pltpu.SemaphoreType.DMA((count + 1,))],
+            out_specs=[vmem] * (len(counts) + len(extra)),
+            scratch_shapes=[pltpu.SMEM(pattern.shape, jnp.int32), pltpu.SemaphoreType.DMA((sum(counts) + 1,))],
             compiler_params=limit,
             name="pack",
         )(*blocks)
 
     recv = []
     for first, count in ((0, SPLIT[1][0]), SPLIT[1]):
-        (send,) = pack(1, first, count)
+        (send,) = pack(((1, first, count),))
         recv.append(lax.ppermute(send, "row", swap))
-    keep, facing_0 = pack(0, 0, PACKED, (ROWS,))
-    (edge,) = pack(1, EDGE_A, ROWS)
+    keep, edge, facing_0 = pack(((0, 0, PACKED), (1, EDGE_A, ROWS)), (ROWS,))
 
     unit_small = jax.ShapeDtypeStruct(((STEPS + 2) * N * HALF, width), jnp.float32)
 

time: 140 us -> 140 us (level)
  waiting for transfers between devices: 61.9 us -> 63.6 us
    ppermute x16, waiting for transfers between devices: 22.5 us -> 24 us  [shards_chain(): got_a = lax.ppermute(msg_a, 'row', swap)]
    ppermute x16, starting transfers between devices: 32.9 us -> 31.4 us  [shards_chain(): got_b = lax.ppermute(msg_b, both, b_pairs)]
    pallas_call x4 -> x3, Pallas kernels: 5.4 us -> 4.5 us  [pack(): pl.pallas_call(functools.partial(pack_kernel, n_col, segments), out_shape...]
where the time goes in v19:
time: 140 us; the launch traced here: 138 us
  waiting for transfers between devices  63.6 us (45%)
  starting transfers between devices  48 us (34%)
  Pallas kernels  22.4 us (16%)
  local copies, waits for them, and re-layouts  3.3 us (2%)
    ppermute x16, waiting for transfers between devices, shards_chain(): got_b = lax.ppermute(msg_b, both, b_pairs)  32.6 us
    ppermute x16, starting transfers between devices, shards_chain(): got_b = lax.ppermute(msg_b, both, b_pairs)  31.4 us
    ppermute x16, waiting for transfers between devices, shards_chain(): got_a = lax.ppermute(msg_a, 'row', swap)  24 us
    pallas_call x33, Pallas kernels, call(): pl.pallas_call(body, out_shape=outs, in_specs=[vmem] * len(ins), out_spec...  15.5 us
    all_to_all x1, starting transfers between devices, beside(): lax.all_to_all(by_target, 'col', split_axis=0, concat_axis=0, tiled=True)  6.27 us
    pallas_call x3, Pallas kernels, pack(): pl.pallas_call(functools.partial(pack_kernel, n_col, segments), out_shape...  4.5 us
    ppermute x1, waiting for transfers between devices, shards_chain(): got = lax.ppermute(jnp.flip(done[:, ROWS:], 1), 'row', swap)  3.62 us
    ppermute x16, starting transfers between devices, shards_chain(): got_a = lax.ppermute(msg_a, 'row', swap)  3.44 us
  transfers between devices with their start and end apart: 38, of which 34 were waited for; matrix products, arithmetic and copies ran while one was open for 2% of the time, Pallas kernels for 9%

profile of v19, /device:TPU:8, one launch (start us, length us, event | category | flops | bytes accessed | tf_op | source)
XLA Modules:
  0.0 138.5 jit_solution(65842659711509466)
XLA Ops:
  4.5 2.2 %pack.3 = (f32[20,128,128]{2,1,0:T(8,128)S(1)}, f32[2,128,128]{2,1,0:T(8,128)S(1)}, f32[2,128,128]{2,1,0:T(8,128)}) custom-call(s32[2,4,4]{2,1,0:T(4,128)} %pattern_hbm.5, f32[2,4,128,128]{3,2,1,0:T(8,128)} %own_hbm.5, f32[4,2,4,128,128]{4,3,2,1,0:T(8,128)} %nb_hbm.5), custom_call_target="tpu_custom_call" | custom-call | tf_op jit(solution)/shard_map/pack/pallas_call | solution.py:511
  6.7 19.9 %conditional.1 = (f32[24,128]{1,0:T(8,128)}, f32[24,128]{1,0:T(8,128)}, f32[2,128,128]{2,1,0:T(8,128)}) conditional(s32[]{:T(128)} %convert_element_type.3, f32[2,128,128]{2,1,0:T(8,128)} %get-tuple-element.166, (f32[1,1,16,4,512]{4,3,2,1,0:T(4,128)}, s32[1,1,16,4]{2,3,1,0:T(4,128)}, f32[2,4,128]{2,1,0:T(4,128)S(1)}, f32[2,4,128]{2,1,0:T(4,128)S(1)}, ...), branch_computations={%region_0.1_spmd, %region_1.2_spmd} | conditional | bytes 1532552 | solution.py:553
  9.1 6.3 %all-to-all-start = ((f32[16,1,2176]{2,1,0:T(1,128)}), f32[16,1,2176]{2,1,0:T(1,128)}, u32[]{:S(2)}, u32[]{:S(2)}) async-start(f32[16,1,2176]{2,1,0:T(1,128)} %by_target.1), calls=%async_computation | async-start | bytes 278528 | tf_op jit(solution)/shard_map/cond/branch_1_fun/all_to_all | solution.py:540
  15.4 3.1 %collective-permute-start.1 = (f32[2,128,128]{2,1,0:T(8,128)}, f32[2,128,128]{2,1,0:T(8,128)}, u32[]{:S(2)}, u32[]{:S(2)}) collective-permute-start(f32[2,128,128]{2,1,0:T(8,128)} %get-tuple-element.22), channel_id=1, source_target_pairs={{16,17},{17,16},{1,2},{2,1},{18,19},{19,18},{3,4},{4,3},{20,21},{2... | collective-permute-start | bytes 393224 | tf_op jit(solution)/shard_map/cond/branch_1_fun/ppermute | solution.py:530
  18.5 2.5 %all-to-all-done = f32[16,1,2176]{2,1,0:T(1,128)} async-done(((f32[16,1,2176]{2,1,0:T(1,128)}), f32[16,1,2176]{2,1,0:T(1,128)}, u32[]{:S(2)}, u32[]{:S(2)}) %all-to-all-start) | async-done | bytes 139296 | tf_op jit(solution)/shard_map/cond/branch_1_fun/all_to_all | solution.py:540
  29.2 2.5 %collective-permute-start.4 = (f32[264,128]{1,0:T(8,128)S(1)}, f32[264,128]{1,0:T(8,128)S(1)}, u32[]{:S(2)}, u32[]{:S(2)}) collective-permute-start(f32[264,128]{1,0:T(8,128)S(1)} %get-tuple-element.171), channel_id=1, source_target_pairs={{16,17},{17,16},{1,2},{2,1},{18,19},{19,18},{3,4},{4,3},{20,21},{2... | collective-permute-start | bytes 405512 | tf_op jit(solution)/shard_map/ppermute | solution.py:585
  31.7 4.8 %collective-permute-done.4.first_b.got_b = f32[264,128]{1,0:T(8,128)S(1)} collective-permute-done((f32[264,128]{1,0:T(8,128)S(1)}, f32[264,128]{1,0:T(8,128)S(1)}, u32[]{:S(2)}, u32[]{:S(2)}) %collective-permute-start.4) | collective-permute-done | bytes 135200 | tf_op jit(solution)/shard_map/ppermute | solution.py:585
  38.3 1.9 %collective-permute-start.6 = (f32[8,128]{1,0:T(8,128)S(1)}, f32[8,128]{1,0:T(8,128)S(1)}, u32[]{:S(2)}, u32[]{:S(2)}) collective-permute-start(f32[8,128]{1,0:T(8,128)S(1)} %get-tuple-element.178), channel_id=1, source_target_pairs={{16,17},{17,16},{1,2},{2,1},{18,19},{19,18},{3,4},{4,3},{20,21},{2... | collective-permute-start | bytes 12296 | tf_op jit(solution)/shard_map/ppermute | solution.py:585
  41.6 2.6 %collective-permute-done.6.got_b = f32[8,128]{1,0:T(8,128)S(1)} collective-permute-done((f32[8,128]{1,0:T(8,128)S(1)}, f32[8,128]{1,0:T(8,128)S(1)}, u32[]{:S(2)}, u32[]{:S(2)}) %collective-permute-start.6) | collective-permute-done | bytes 4128 | tf_op jit(solution)/shard_map/ppermute | solution.py:585
  44.7 1.9 %collective-permute-start.8 = (f32[8,128]{1,0:T(8,128)S(1)}, f32[8,128]{1,0:T(8,128)S(1)}, u32[]{:S(2)}, u32[]{:S(2)}) collective-permute-start(f32[8,128]{1,0:T(8,128)S(1)} %get-tuple-element.187), channel_id=1, source_target_pairs={{16,17},{17,16},{1,2},{2,1},{18,19},{19,18},{3,4},{4,3},{20,21},{2... | collective-permute-start | bytes 12296 | tf_op jit(solution)/shard_map/ppermute | solution.py:585
  46.6 1.7 %collective-permute-done.9.got_a = f32[8,128]{1,0:T(8,128)S(1)} collective-permute-done((f32[8,128]{1,0:T(8,128)S(1)}, f32[8,128]{1,0:T(8,128)S(1)}, u32[]{:S(2)}, u32[]{:S(2)}) %collective-permute-start.9) | collective-permute-done | bytes 4128 | tf_op jit(solution)/shard_map/ppermute | solution.py:586
  48.7 1.8 %collective-permute-done.8.got_b = f32[8,128]{1,0:T(8,128)S(1)} collective-permute-done((f32[8,128]{1,0:T(8,128)S(1)}, f32[8,128]{1,0:T(8,128)S(1)}, u32[]{:S(2)}, u32[]{:S(2)}) %collective-permute-start.8) | collective-permute-done | bytes 4128 | tf_op jit(solution)/shard_map/ppermute | solution.py:585
  51.1 1.9 %collective-permute-start.10 = (f32[8,128]{1,0:T(8,128)S(1)}, f32[8,128]{1,0:T(8,128)S(1)}, u32[]{:S(2)}, u32[]{:S(2)}) collective-permute-start(f32[8,128]{1,0:T(8,128)S(1)} %get-tuple-element.196), channel_id=1, source_target_pairs={{16,17},{17,16},{1,2},{2,1},{18,19},{19,18},{3,4},{4,3},{20,21},{2... | collective-permute-start | bytes 12296 | tf_op jit(solution)/shard_map/ppermute | solution.py:585
  53.0 1.7 %collective-permute-done.11.got_a = f32[8,128]{1,0:T(8,128)S(1)} collective-permute-done((f32[8,128]{1,0:T(8,128)S(1)}, f32[8,128]{1,0:T(8,128)S(1)}, u32[]{:S(2)}, u32[]{:S(2)}) %collective-permute-start.11) | collective-permute-done | bytes 4128 | tf_op jit(solution)/shard_map/ppermute | solution.py:586
  55.1 1.8 %collective-permute-done.10.got_b = f32[8,128]{1,0:T(8,128)S(1)} collective-permute-done((f32[8,128]{1,0:T(8,128)S(1)}, f32[8,128]{1,0:T(8,128)S(1)}, u32[]{:S(2)}, u32[]{:S(2)}) %collective-permute-start.10) | collective-permute-done | bytes 4128 | tf_op jit(solution)/shard_map/ppermute | solution.py:585
  57.5 1.9 %collective-permute-start.12 = (f32[8,128]{1,0:T(8,128)S(1)}, f32[8,128]{1,0:T(8,128)S(1)}, u32[]{:S(2)}, u32[]{:S(2)}) collective-permute-start(f32[8,128]{1,0:T(8,128)S(1)} %get-tuple-element.206), channel_id=1, source_target_pairs={{16,17},{17,16},{1,2},{2,1},{18,19},{19,18},{3,4},{4,3},{20,21},{2... | collective-permute-start | bytes 12296 | tf_op jit(solution)/shard_map/ppermute | solution.py:585
  59.4 1.7 %collective-permute-done.13.got_a = f32[8,128]{1,0:T(8,128)S(1)} collective-permute-done((f32[8,128]{1,0:T(8,128)S(1)}, f32[8,128]{1,0:T(8,128)S(1)}, u32[]{:S(2)}, u32[]{:S(2)}) %collective-permute-start.13) | collective-permute-done | bytes 4128 | tf_op jit(solution)/shard_map/ppermute | solution.py:586
  61.5 1.8 %collective-permute-done.12.got_b = f32[8,128]{1,0:T(8,128)S(1)} collective-permute-done((f32[8,128]{1,0:T(8,128)S(1)}, f32[8,128]{1,0:T(8,128)S(1)}, u32[]{:S(2)}, u32[]{:S(2)}) %collective-permute-start.12) | collective-permute-done | bytes 4128 | tf_op jit(solution)/shard_map/ppermute | solution.py:585
  63.9 1.9 %collective-permute-start.14 = (f32[8,128]{1,0:T(8,128)S(1)}, f32[8,128]{1,0:T(8,128)S(1)}, u32[]{:S(2)}, u32[]{:S(2)}) collective-permute-start(f32[8,128]{1,0:T(8,128)S(1)} %get-tuple-element.212), channel_id=1, source_target_pairs={{16,17},{17,16},{1,2},{2,1},{18,19},{19,18},{3,4},{4,3},{20,21},{2... | collective-permute-start | bytes 12296 | tf_op jit(solution)/shard_map/ppermute | solution.py:585
  65.8 1.7 %collective-permute-done.15.got_a = f32[8,128]{1,0:T(8,128)S(1)} collective-permute-done((f32[8,128]{1,0:T(8,128)S(1)}, f32[8,128]{1,0:T(8,128)S(1)}, u32[]{:S(2)}, u32[]{:S(2)}) %collective-permute-start.15) | collective-permute-done | bytes 4128 | tf_op jit(solution)/shard_map/ppermute | solution.py:586
  67.9 1.8 %collective-permute-done.14.got_b = f32[8,128]{1,0:T(8,128)S(1)} collective-permute-done((f32[8,128]{1,0:T(8,128)S(1)}, f32[8,128]{1,0:T(8,128)S(1)}, u32[]{:S(2)}, u32[]{:S(2)}) %collective-permute-start.14) | collective-permute-done | bytes 4128 | tf_op jit(solution)/shard_map/ppermute | solution.py:585
  70.3 1.9 %collective-permute-start.16 = (f32[8,128]{1,0:T(8,128)S(1)}, f32[8,128]{1,0:T(8,128)S(1)}, u32[]{:S(2)}, u32[]{:S(2)}) collective-permute-start(f32[8,128]{1,0:T(8,128)S(1)} %get-tuple-element.221), channel_id=1, source_target_pairs={{16,17},{17,16},{1,2},{2,1},{18,19},{19,18},{3,4},{4,3},{20,21},{2... | collective-permute-start | bytes 12296 | tf_op jit(solution)/shard_map/ppermute | solution.py:585
  72.2 1.7 %collective-permute-done.17.got_a = f32[8,128]{1,0:T(8,128)S(1)} collective-permute-done((f32[8,128]{1,0:T(8,128)S(1)}, f32[8,128]{1,0:T(8,128)S(1)}, u32[]{:S(2)}, u32[]{:S(2)}) %collective-permute-start.17) | collective-permute-done | bytes 4128 | tf_op jit(solution)/shard_map/ppermute | solution.py:586
  74.3 1.8 %collective-permute-done.16.got_b = f32[8,128]{1,0:T(8,128)S(1)} collective-permute-done((f32[8,128]{1,0:T(8,128)S(1)}, f32[8,128]{1,0:T(8,128)S(1)}, u32[]{:S(2)}, u32[]{:S(2)}) %collective-permute-start.16) | collective-permute-done | bytes 4128 | tf_op jit(solution)/shard_map/ppermute | solution.py:585
  76.7 1.9 %collective-permute-start.18 = (f32[8,128]{1,0:T(8,128)S(1)}, f32[8,128]{1,0:T(8,128)S(1)}, u32[]{:S(2)}, u32[]{:S(2)}) collective-permute-start(f32[8,128]{1,0:T(8,128)S(1)} %get-tuple-element.230), channel_id=1, source_target_pairs={{16,17},{17,16},{1,2},{2,1},{18,19},{19,18},{3,4},{4,3},{20,21},{2... | collective-permute-start | bytes 12296 | tf_op jit(solution)/shard_map/ppermute | solution.py:585
  78.6 1.7 %collective-permute-done.19.got_a = f32[8,128]{1,0:T(8,128)S(1)} collective-permute-done((f32[8,128]{1,0:T(8,128)S(1)}, f32[8,128]{1,0:T(8,128)S(1)}, u32[]{:S(2)}, u32[]{:S(2)}) %collective-permute-start.19) | collective-permute-done | bytes 4128 | tf_op jit(solution)/shard_map/ppermute | solution.py:586
  80.7 1.8 %collective-permute-done.18.got_b = f32[8,128]{1,0:T(8,128)S(1)} collective-permute-done((f32[8,128]{1,0:T(8,128)S(1)}, f32[8,128]{1,0:T(8,128)S(1)}, u32[]{:S(2)}, u32[]{:S(2)}) %collective-permute-start.18) | collective-permute-done | bytes 4128 | tf_op jit(solution)/shard_map/ppermute | solution.py:585
  83.1 1.9 %collective-permute-start.20 = (f32[8,128]{1,0:T(8,128)S(1)}, f32[8,128]{1,0:T(8,128)S(1)}, u32[]{:S(2)}, u32[]{:S(2)}) collective-permute-start(f32[8,128]{1,0:T(8,128)S(1)} %get-tuple-element.240), channel_id=1, source_target_pairs={{16,17},{17,16},{1,2},{2,1},{18,19},{19,18},{3,4},{4,3},{20,21},{2... | collective-permute-start | bytes 12296 | tf_op jit(solution)/shard_map/ppermute | solution.py:585
  85.0 1.7 %collective-permute-done.21.got_a = f32[8,128]{1,0:T(8,128)S(1)} collective-permute-done((f32[8,128]{1,0:T(8,128)S(1)}, f32[8,128]{1,0:T(8,128)S(1)}, u32[]{:S(2)}, u32[]{:S(2)}) %collective-permute-start.21) | collective-permute-done | bytes 4128 | tf_op jit(solution)/shard_map/ppermute | solution.py:586
  87.1 1.8 %collective-permute-done.20.got_b = f32[8,128]{1,0:T(8,128)S(1)} collective-permute-done((f32[8,128]{1,0:T(8,128)S(1)}, f32[8,128]{1,0:T(8,128)S(1)}, u32[]{:S(2)}, u32[]{:S(2)}) %collective-permute-start.20) | collective-permute-done | bytes 4128 | tf_op jit(solution)/shard_map/ppermute | solution.py:585
  89.5 1.9 %collective-permute-start.22 = (f32[8,128]{1,0:T(8,128)S(1)}, f32[8,128]{1,0:T(8,128)S(1)}, u32[]{:S(2)}, u32[]{:S(2)}) collective-permute-start(f32[8,128]{1,0:T(8,128)S(1)} %get-tuple-element.246), channel_id=1, source_target_pairs={{16,17},{17,16},{1,2},{2,1},{18,19},{19,18},{3,4},{4,3},{20,21},{2... | collective-permute-start | bytes 12296 | tf_op jit(solution)/shard_map/ppermute | solution.py:585
  91.4 1.7 %collective-permute-done.23.got_a = f32[8,128]{1,0:T(8,128)S(1)} collective-permute-done((f32[8,128]{1,0:T(8,128)S(1)}, f32[8,128]{1,0:T(8,128)S(1)}, u32[]{:S(2)}, u32[]{:S(2)}) %collective-permute-start.23) | collective-permute-done | bytes 4128 | tf_op jit(solution)/shard_map/ppermute | solution.py:586
  93.5 1.8 %collective-permute-done.22.got_b = f32[8,128]{1,0:T(8,128)S(1)} collective-permute-done((f32[8,128]{1,0:T(8,128)S(1)}, f32[8,128]{1,0:T(8,128)S(1)}, u32[]{:S(2)}, u32[]{:S(2)}) %collective-permute-start.22) | collective-permute-done | bytes 4128 | tf_op jit(solution)/shard_map/ppermute | solution.py:585
  95.9 2.1 %collective-permute-start.24 = (f32[8,128]{1,0:T(8,128)S(1)}, f32[8,128]{1,0:T(8,128)S(1)}, u32[]{:S(2)}, u32[]{:S(2)}) collective-permute-start(f32[8,128]{1,0:T(8,128)S(1)} %get-tuple-element.255), channel_id=1, source_target_pairs={{16,17},{17,16},{1,2},{2,1},{18,19},{19,18},{3,4},{4,3},{20,21},{2... | collective-permute-start | bytes 12296 | tf_op jit(solution)/shard_map/ppermute | solution.py:585
  99.9 1.8 %collective-permute-done.24.got_b = f32[8,128]{1,0:T(8,128)S(1)} collective-permute-done((f32[8,128]{1,0:T(8,128)S(1)}, f32[8,128]{1,0:T(8,128)S(1)}, u32[]{:S(2)}, u32[]{:S(2)}) %collective-permute-start.24) | collective-permute-done | bytes 4128 | tf_op jit(solution)/shard_map/ppermute | solution.py:585
  102.3 1.9 %collective-permute-start.26 = (f32[8,128]{1,0:T(8,128)S(1)}, f32[8,128]{1,0:T(8,128)S(1)}, u32[]{:S(2)}, u32[]{:S(2)}) collective-permute-start(f32[8,128]{1,0:T(8,128)S(1)} %get-tuple-element.264), channel_id=1, source_target_pairs={{16,17},{17,16},{1,2},{2,1},{18,19},{19,18},{3,4},{4,3},{20,21},{2... | collective-permute-start | bytes 12296 | tf_op jit(solution)/shard_map/ppermute | solution.py:585
  104.2 1.7 %collective-permute-done.27.got_a = f32[8,128]{1,0:T(8,128)S(1)} collective-permute-done((f32[8,128]{1,0:T(8,128)S(1)}, f32[8,128]{1,0:T(8,128)S(1)}, u32[]{:S(2)}, u32[]{:S(2)}) %collective-permute-start.27) | collective-permute-done | bytes 4128 | tf_op jit(solution)/shard_map/ppermute | solution.py:586
  106.3 1.8 %collective-permute-done.26.got_b = f32[8,128]{1,0:T(8,128)S(1)} collective-permute-done((f32[8,128]{1,0:T(8,128)S(1)}, f32[8,128]{1,0:T(8,128)S(1)}, u32[]{:S(2)}, u32[]{:S(2)}) %collective-permute-start.26) | collective-permute-done | bytes 4128 | tf_op jit(solution)/shard_map/ppermute | solution.py:585
  108.7 1.9 %collective-permute-start.28 = (f32[8,128]{1,0:T(8,128)S(1)}, f32[8,128]{1,0:T(8,128)S(1)}, u32[]{:S(2)}, u32[]{:S(2)}) collective-permute-start(f32[8,128]{1,0:T(8,128)S(1)} %get-tuple-element.274), channel_id=1, source_target_pairs={{16,17},{17,16},{1,2},{2,1},{18,19},{19,18},{3,4},{4,3},{20,21},{2... | collective-permute-start | bytes 12296 | tf_op jit(solution)/shard_map/ppermute | solution.py:585
  112.7 1.8 %collective-permute-done.28.got_b = f32[8,128]{1,0:T(8,128)S(1)} collective-permute-done((f32[8,128]{1,0:T(8,128)S(1)}, f32[8,128]{1,0:T(8,128)S(1)}, u32[]{:S(2)}, u32[]{:S(2)}) %collective-permute-start.28) | collective-permute-done | bytes 4128 | tf_op jit(solution)/shard_map/ppermute | solution.py:585
  115.1 1.9 %collective-permute-start.30 = (f32[8,128]{1,0:T(8,128)S(1)}, f32[8,128]{1,0:T(8,128)S(1)}, u32[]{:S(2)}, u32[]{:S(2)}) collective-permute-start(f32[8,128]{1,0:T(8,128)S(1)} %get-tuple-element.280), channel_id=1, source_target_pairs={{16,17},{17,16},{1,2},{2,1},{18,19},{19,18},{3,4},{4,3},{20,21},{2... | collective-permute-start | bytes 12296 | tf_op jit(solution)/shard_map/ppermute | solution.py:585
  119.1 1.8 %collective-permute-done.30.got_b = f32[8,128]{1,0:T(8,128)S(1)} collective-permute-done((f32[8,128]{1,0:T(8,128)S(1)}, f32[8,128]{1,0:T(8,128)S(1)}, u32[]{:S(2)}, u32[]{:S(2)}) %collective-permute-start.30) | collective-permute-done | bytes 4128 | tf_op jit(solution)/shard_map/ppermute | solution.py:585
  121.5 1.9 %collective-permute-start.32 = (f32[8,128]{1,0:T(8,128)S(1)}, f32[8,128]{1,0:T(8,128)S(1)}, u32[]{:S(2)}, u32[]{:S(2)}) collective-permute-start(f32[8,128]{1,0:T(8,128)S(1)} %get-tuple-element.289), channel_id=1, source_target_pairs={{16,17},{17,16},{1,2},{2,1},{18,19},{19,18},{3,4},{4,3},{20,21},{2... | collective-permute-start | bytes 12296 | tf_op jit(solution)/shard_map/ppermute | solution.py:585
  125.5 1.8 %collective-permute-done.32.got_b = f32[8,128]{1,0:T(8,128)S(1)} collective-permute-done((f32[8,128]{1,0:T(8,128)S(1)}, f32[8,128]{1,0:T(8,128)S(1)}, u32[]{:S(2)}, u32[]{:S(2)}) %collective-permute-start.32) | collective-permute-done | bytes 4128 | tf_op jit(solution)/shard_map/ppermute | solution.py:585
  127.9 1.9 %collective-permute-start.34 = (f32[8,128]{1,0:T(8,128)S(1)}, f32[8,128]{1,0:T(8,128)S(1)}, u32[]{:S(2)}, u32[]{:S(2)}) collective-permute-start(f32[8,128]{1,0:T(8,128)S(1)} %get-tuple-element.298), channel_id=1, source_target_pairs={{16,17},{17,16},{1,2},{2,1},{18,19},{19,18},{3,4},{4,3},{20,21},{2... | collective-permute-start | bytes 12296 | tf_op jit(solution)/shard_map/ppermute | solution.py:585
  129.8 1.7 %collective-permute-done.35.got_a = f32[8,128]{1,0:T(8,128)S(1)} collective-permute-done((f32[8,128]{1,0:T(8,128)S(1)}, f32[8,128]{1,0:T(8,128)S(1)}, u32[]{:S(2)}, u32[]{:S(2)}) %collective-permute-start.35) | collective-permute-done | bytes 4128 | tf_op jit(solution)/shard_map/ppermute | solution.py:586
  131.9 1.8 %collective-permute-done.34.got_b = f32[8,128]{1,0:T(8,128)S(1)} collective-permute-done((f32[8,128]{1,0:T(8,128)S(1)}, f32[8,128]{1,0:T(8,128)S(1)}, u32[]{:S(2)}, u32[]{:S(2)}) %collective-permute-start.34) | collective-permute-done | bytes 4128 | tf_op jit(solution)/shard_map/ppermute | solution.py:585
  134.2 3.6 %collective-permute-done.36 = f32[4,2,2,128]{3,2,1,0:T(2,128)S(1)} collective-permute-done((f32[4,2,2,128]{3,2,1,0:T(2,128)S(1)}, f32[4,2,2,128]{3,2,1,0:T(2,128)S(1)}, u32[]{:S(2)}, u32[]{:S(2)}) %collective-permute-start.36) | collective-permute-done | bytes 8224 | tf_op jit(solution)/shard_map/ppermute | solution.py:599
  (83 shorter events, 39.5 us)
Async XLA Ops:
  1.2 5.5 %copy-start.1 = (f32[2,4,128]{2,1,0:T(4,128)S(1)}, f32[2,4,128]{2,1,0:T(4,128)}, u32[]{:S(2)}) copy-start(f32[2,4,128]{2,1,0:T(4,128)} %param.12) | copy-start | bytes 12292
  1.2 5.5 %copy-start.2 = (f32[2,4,128]{2,1,0:T(4,128)S(1)}, f32[2,4,128]{2,1,0:T(4,128)}, u32[]{:S(2)}) copy-start(f32[2,4,128]{2,1,0:T(4,128)} %param.13) | copy-start | bytes 12292
  1.2 25.3 %collective-permute-start.2 = (f32[10,128,128]{2,1,0:T(8,128)S(1)}, f32[10,128,128]{2,1,0:T(8,128)S(1)}, u32[]{:S(2)}, u32[]{:S(2)}) collective-permute-start(f32[10,128,128]{2,1,0:T(8,128)S(1)} %pack.4), channel_id=1, source_target_pairs={{0,16},{16,0},{1,17},{17,1},{2,18},{18,2},{3,19},{19,3},{4,20},{20... | collective-permute-start | bytes 1966088 | tf_op jit(solution)/shard_map/ppermute | solution.py:524
  3.9 22.7 %collective-permute-start.3 = (f32[6,128,128]{2,1,0:T(8,128)S(1)}, f32[6,128,128]{2,1,0:T(8,128)S(1)}, u32[]{:S(2)}, u32[]{:S(2)}) collective-permute-start(f32[6,128,128]{2,1,0:T(8,128)S(1)} %pack.5), channel_id=1, source_target_pairs={{0,16},{16,0},{1,17},{17,1},{2,18},{18,2},{3,19},{19,3},{4,20},{20... | collective-permute-start | bytes 1179656 | tf_op jit(solution)/shard_map/ppermute | solution.py:524
  9.1 11.9 %all-to-all-start = ((f32[16,1,2176]{2,1,0:T(1,128)}), f32[16,1,2176]{2,1,0:T(1,128)}, u32[]{:S(2)}, u32[]{:S(2)}) async-start(f32[16,1,2176]{2,1,0:T(1,128)} %by_target.1), calls=%async_computation | async-start | bytes 278528 | tf_op jit(solution)/shard_map/cond/branch_1_fun/all_to_all | solution.py:540
  15.4 8.9 %collective-permute-start.1 = (f32[2,128,128]{2,1,0:T(8,128)}, f32[2,128,128]{2,1,0:T(8,128)}, u32[]{:S(2)}, u32[]{:S(2)}) collective-permute-start(f32[2,128,128]{2,1,0:T(8,128)} %get-tuple-element.22), channel_id=1, source_target_pairs={{16,17},{17,16},{1,2},{2,1},{18,19},{19,18},{3,4},{4,3},{20,21},{2... | collective-permute-start | bytes 393224 | tf_op jit(solution)/shard_map/cond/branch_1_fun/ppermute | solution.py:530
  22.7 3.9 %collective-permute-start = (f32[24,128]{1,0:T(8,128)S(1)}, f32[24,128]{1,0:T(8,128)}, u32[]{:S(2)}, u32[]{:S(2)}) collective-permute-start(f32[24,128]{1,0:T(8,128)S(1)} %get-tuple-element.21), channel_id=1, source_target_pairs={{0,16},{16,0},{1,17},{17,1},{2,18},{18,2},{3,19},{19,3},{4,20},{20... | collective-permute-start | bytes 36872 | tf_op jit(solution)/shard_map/cond/branch_1_fun/ppermute | solution.py:551
  26.6 10.0 %copy-start = (f32[2,128,128]{2,1,0:T(8,128)S(1)}, f32[2,128,128]{2,1,0:T(8,128)}, u32[]{:S(2)}) copy-start(f32[2,128,128]{2,1,0:T(8,128)} %get-tuple-element.172.beyond_0) | copy-start | bytes 393220
  27.6 8.9 %collective-permute-start.5 = (f32[520,128]{1,0:T(8,128)S(1)}, f32[520,128]{1,0:T(8,128)S(1)}, u32[]{:S(2)}, u32[]{:S(2)}) collective-permute-start(f32[520,128]{1,0:T(8,128)S(1)} %get-tuple-element.173), channel_id=1, source_target_pairs={{0,16},{16,0},{1,17},{17,1},{2,18},{18,2},{3,19},{19,3},{4,20},{20... | collective-permute-start | bytes 798728 | tf_op jit(solution)/shard_map/ppermute | solution.py:586
  29.2 7.3 %collective-permute-start.4 = (f32[264,128]{1,0:T(8,128)S(1)}, f32[264,128]{1,0:T(8,128)S(1)}, u32[]{:S(2)}, u32[]{:S(2)}) collective-permute-start(f32[264,128]{1,0:T(8,128)S(1)} %get-tuple-element.171), channel_id=1, source_target_pairs={{16,17},{17,16},{1,2},{2,1},{18,19},{19,18},{3,4},{4,3},{20,21},{2... | collective-permute-start | bytes 405512 | tf_op jit(solution)/shard_map/ppermute | solution.py:585
  37.5 3.7 %collective-permute-start.7 = (f32[8,128]{1,0:T(8,128)S(1)}, f32[8,128]{1,0:T(8,128)S(1)}, u32[]{:S(2)}, u32[]{:S(2)}) collective-permute-start(f32[8,128]{1,0:T(8,128)S(1)} %get-tuple-element.179), channel_id=1, source_target_pairs={{0,16},{16,0},{1,17},{17,1},{2,18},{18,2},{3,19},{19,3},{4,20},{20... | collective-permute-start | bytes 12296 | tf_op jit(solution)/shard_map/ppermute | solution.py:586
  38.3 5.8 %collective-permute-start.6 = (f32[8,128]{1,0:T(8,128)S(1)}, f32[8,128]{1,0:T(8,128)S(1)}, u32[]{:S(2)}, u32[]{:S(2)}) collective-permute-start(f32[8,128]{1,0:T(8,128)S(1)} %get-tuple-element.178), channel_id=1, source_target_pairs={{16,17},{17,16},{1,2},{2,1},{18,19},{19,18},{3,4},{4,3},{20,21},{2... | collective-permute-start | bytes 12296 | tf_op jit(solution)/shard_map/ppermute | solution.py:585
  44.6 3.7 %collective-permute-start.9 = (f32[8,128]{1,0:T(8,128)S(1)}, f32[8,128]{1,0:T(8,128)S(1)}, u32[]{:S(2)}, u32[]{:S(2)}) collective-permute-start(f32[8,128]{1,0:T(8,128)S(1)} %get-tuple-element.188), channel_id=1, source_target_pairs={{0,16},{16,0},{1,17},{17,1},{2,18},{18,2},{3,19},{19,3},{4,20},{20... | collective-permute-start | bytes 12296 | tf_op jit(solution)/shard_map/ppermute | solution.py:586
  44.7 5.8 %collective-permute-start.8 = (f32[8,128]{1,0:T(8,128)S(1)}, f32[8,128]{1,0:T(8,128)S(1)}, u32[]{:S(2)}, u32[]{:S(2)}) collective-permute-start(f32[8,128]{1,0:T(8,128)S(1)} %get-tuple-element.187), channel_id=1, source_target_pairs={{16,17},{17,16},{1,2},{2,1},{18,19},{19,18},{3,4},{4,3},{20,21},{2... | collective-permute-start | bytes 12296 | tf_op jit(solution)/shard_map/ppermute | solution.py:585
  51.0 3.7 %collective-permute-start.11 = (f32[8,128]{1,0:T(8,128)S(1)}, f32[8,128]{1,0:T(8,128)S(1)}, u32[]{:S(2)}, u32[]{:S(2)}) collective-permute-start(f32[8,128]{1,0:T(8,128)S(1)} %get-tuple-element.197), channel_id=1, source_target_pairs={{0,16},{16,0},{1,17},{17,1},{2,18},{18,2},{3,19},{19,3},{4,20},{20... | collective-permute-start | bytes 12296 | tf_op jit(solution)/shard_map/ppermute | solution.py:586
  51.1 5.8 %collective-permute-start.10 = (f32[8,128]{1,0:T(8,128)S(1)}, f32[8,128]{1,0:T(8,128)S(1)}, u32[]{:S(2)}, u32[]{:S(2)}) collective-permute-start(f32[8,128]{1,0:T(8,128)S(1)} %get-tuple-element.196), channel_id=1, source_target_pairs={{16,17},{17,16},{1,2},{2,1},{18,19},{19,18},{3,4},{4,3},{20,21},{2... | collective-permute-start | bytes 12296 | tf_op jit(solution)/shard_map/ppermute | solution.py:585
  57.4 3.7 %collective-permute-start.13 = (f32[8,128]{1,0:T(8,128)S(1)}, f32[8,128]{1,0:T(8,128)S(1)}, u32[]{:S(2)}, u32[]{:S(2)}) collective-permute-start(f32[8,128]{1,0:T(8,128)S(1)} %get-tuple-element.207), channel_id=1, source_target_pairs={{0,16},{16,0},{1,17},{17,1},{2,18},{18,2},{3,19},{19,3},{4,20},{20... | collective-permute-start | bytes 12296 | tf_op jit(solution)/shard_map/ppermute | solution.py:586
  57.5 5.8 %collective-permute-start.12 = (f32[8,128]{1,0:T(8,128)S(1)}, f32[8,128]{1,0:T(8,128)S(1)}, u32[]{:S(2)}, u32[]{:S(2)}) collective-permute-start(f32[8,128]{1,0:T(8,128)S(1)} %get-tuple-element.206), channel_id=1, source_target_pairs={{16,17},{17,16},{1,2},{2,1},{18,19},{19,18},{3,4},{4,3},{20,21},{2... | collective-permute-start | bytes 12296 | tf_op jit(solution)/shard_map/ppermute | solution.py:585
  63.8 3.7 %collective-permute-start.15 = (f32[8,128]{1,0:T(8,128)S(1)}, f32[8,128]{1,0:T(8,128)S(1)}, u32[]{:S(2)}, u32[]{:S(2)}) collective-permute-start(f32[8,128]{1,0:T(8,128)S(1)} %get-tuple-element.213), channel_id=1, source_target_pairs={{0,16},{16,0},{1,17},{17,1},{2,18},{18,2},{3,19},{19,3},{4,20},{20... | collective-permute-start | bytes 12296 | tf_op jit(solution)/shard_map/ppermute | solution.py:586
  63.9 5.8 %collective-permute-start.14 = (f32[8,128]{1,0:T(8,128)S(1)}, f32[8,128]{1,0:T(8,128)S(1)}, u32[]{:S(2)}, u32[]{:S(2)}) collective-permute-start(f32[8,128]{1,0:T(8,128)S(1)} %get-tuple-element.212), channel_id=1, source_target_pairs={{16,17},{17,16},{1,2},{2,1},{18,19},{19,18},{3,4},{4,3},{20,21},{2... | collective-permute-start | bytes 12296 | tf_op jit(solution)/shard_map/ppermute | solution.py:585
  70.2 3.7 %collective-permute-start.17 = (f32[8,128]{1,0:T(8,128)S(1)}, f32[8,128]{1,0:T(8,128)S(1)}, u32[]{:S(2)}, u32[]{:S(2)}) collective-permute-start(f32[8,128]{1,0:T(8,128)S(1)} %get-tuple-element.222), channel_id=1, source_target_pairs={{0,16},{16,0},{1,17},{17,1},{2,18},{18,2},{3,19},{19,3},{4,20},{20... | collective-permute-start | bytes 12296 | tf_op jit(solution)/shard_map/ppermute | solution.py:586
  70.3 5.8 %collective-permute-start.16 = (f32[8,128]{1,0:T(8,128)S(1)}, f32[8,128]{1,0:T(8,128)S(1)}, u32[]{:S(2)}, u32[]{:S(2)}) collective-permute-start(f32[8,128]{1,0:T(8,128)S(1)} %get-tuple-element.221), channel_id=1, source_target_pairs={{16,17},{17,16},{1,2},{2,1},{18,19},{19,18},{3,4},{4,3},{20,21},{2... | collective-permute-start | bytes 12296 | tf_op jit(solution)/shard_map/ppermute | solution.py:585
  76.6 3.7 %collective-permute-start.19 = (f32[8,128]{1,0:T(8,128)S(1)}, f32[8,128]{1,0:T(8,128)S(1)}, u32[]{:S(2)}, u32[]{:S(2)}) collective-permute-start(f32[8,128]{1,0:T(8,128)S(1)} %get-tuple-element.231), channel_id=1, source_target_pairs={{0,16},{16,0},{1,17},{17,1},{2,18},{18,2},{3,19},{19,3},{4,20},{20... | collective-permute-start | bytes 12296 | tf_op jit(solution)/shard_map/ppermute | solution.py:586
  76.7 5.8 %collective-permute-start.18 = (f32[8,128]{1,0:T(8,128)S(1)}, f32[8,128]{1,0:T(8,128)S(1)}, u32[]{:S(2)}, u32[]{:S(2)}) collective-permute-start(f32[8,128]{1,0:T(8,128)S(1)} %get-tuple-element.230), channel_id=1, source_target_pairs={{16,17},{17,16},{1,2},{2,1},{18,19},{19,18},{3,4},{4,3},{20,21},{2... | collective-permute-start | bytes 12296 | tf_op jit(solution)/shard_map/ppermute | solution.py:585
  83.0 3.7 %collective-permute-start.21 = (f32[8,128]{1,0:T(8,128)S(1)}, f32[8,128]{1,0:T(8,128)S(1)}, u32[]{:S(2)}, u32[]{:S(2)}) collective-permute-start(f32[8,128]{1,0:T(8,128)S(1)} %get-tuple-element.241), channel_id=1, source_target_pairs={{0,16},{16,0},{1,17},{17,1},{2,18},{18,2},{3,19},{19,3},{4,20},{20... | collective-permute-start | bytes 12296 | tf_op jit(solution)/shard_map/ppermute | solution.py:586
  83.1 5.8 %collective-permute-start.20 = (f32[8,128]{1,0:T(8,128)S(1)}, f32[8,128]{1,0:T(8,128)S(1)}, u32[]{:S(2)}, u32[]{:S(2)}) collective-permute-start(f32[8,128]{1,0:T(8,128)S(1)} %get-tuple-element.240), channel_id=1, source_target_pairs={{16,17},{17,16},{1,2},{2,1},{18,19},{19,18},{3,4},{4,3},{20,21},{2... | collective-permute-start | bytes 12296 | tf_op jit(solution)/shard_map/ppermute | solution.py:585
  89.4 3.7 %collective-permute-start.23 = (f32[8,128]{1,0:T(8,128)S(1)}, f32[8,128]{1,0:T(8,128)S(1)}, u32[]{:S(2)}, u32[]{:S(2)}) collective-permute-start(f32[8,128]{1,0:T(8,128)S(1)} %get-tuple-element.247), channel_id=1, source_target_pairs={{0,16},{16,0},{1,17},{17,1},{2,18},{18,2},{3,19},{19,3},{4,20},{20... | collective-permute-start | bytes 12296 | tf_op jit(solution)/shard_map/ppermute | solution.py:586
  89.5 5.8 %collective-permute-start.22 = (f32[8,128]{1,0:T(8,128)S(1)}, f32[8,128]{1,0:T(8,128)S(1)}, u32[]{:S(2)}, u32[]{:S(2)}) collective-permute-start(f32[8,128]{1,0:T(8,128)S(1)} %get-tuple-element.246), channel_id=1, source_target_pairs={{16,17},{17,16},{1,2},{2,1},{18,19},{19,18},{3,4},{4,3},{20,21},{2... | collective-permute-start | bytes 12296 | tf_op jit(solution)/shard_map/ppermute | solution.py:585
  95.8 3.7 %collective-permute-start.25 = (f32[8,128]{1,0:T(8,128)S(1)}, f32[8,128]{1,0:T(8,128)S(1)}, u32[]{:S(2)}, u32[]{:S(2)}) collective-permute-start(f32[8,128]{1,0:T(8,128)S(1)} %get-tuple-element.256), channel_id=1, source_target_pairs={{0,16},{16,0},{1,17},{17,1},{2,18},{18,2},{3,19},{19,3},{4,20},{20... | collective-permute-start | bytes 12296 | tf_op jit(solution)/shard_map/ppermute | solution.py:586
  95.9 5.8 %collective-permute-start.24 = (f32[8,128]{1,0:T(8,128)S(1)}, f32[8,128]{1,0:T(8,128)S(1)}, u32[]{:S(2)}, u32[]{:S(2)}) collective-permute-start(f32[8,128]{1,0:T(8,128)S(1)} %get-tuple-element.255), channel_id=1, source_target_pairs={{16,17},{17,16},{1,2},{2,1},{18,19},{19,18},{3,4},{4,3},{20,21},{2... | collective-permute-start | bytes 12296 | tf_op jit(solution)/shard_map/ppermute | solution.py:585
  102.2 3.7 %collective-permute-start.27 = (f32[8,128]{1,0:T(8,128)S(1)}, f32[8,128]{1,0:T(8,128)S(1)}, u32[]{:S(2)}, u32[]{:S(2)}) collective-permute-start(f32[8,128]{1,0:T(8,128)S(1)} %get-tuple-element.265), channel_id=1, source_target_pairs={{0,16},{16,0},{1,17},{17,1},{2,18},{18,2},{3,19},{19,3},{4,20},{20... | collective-permute-start | bytes 12296 | tf_op jit(solution)/shard_map/ppermute | solution.py:586
  102.3 5.8 %collective-permute-start.26 = (f32[8,128]{1,0:T(8,128)S(1)}, f32[8,128]{1,0:T(8,128)S(1)}, u32[]{:S(2)}, u32[]{:S(2)}) collective-permute-start(f32[8,128]{1,0:T(8,128)S(1)} %get-tuple-element.264), channel_id=1, source_target_pairs={{16,17},{17,16},{1,2},{2,1},{18,19},{19,18},{3,4},{4,3},{20,21},{2... | collective-permute-start | bytes 12296 | tf_op jit(solution)/shard_map/ppermute | solution.py:585
  108.6 3.7 %collective-permute-start.29 = (f32[8,128]{1,0:T(8,128)S(1)}, f32[8,128]{1,0:T(8,128)S(1)}, u32[]{:S(2)}, u32[]{:S(2)}) collective-permute-start(f32[8,128]{1,0:T(8,128)S(1)} %get-tuple-element.275), channel_id=1, source_target_pairs={{0,16},{16,0},{1,17},{17,1},{2,18},{18,2},{3,19},{19,3},{4,20},{20... | collective-permute-start | bytes 12296 | tf_op jit(solution)/shard_map/ppermute | solution.py:586
  108.7 5.8 %collective-permute-start.28 = (f32[8,128]{1,0:T(8,128)S(1)}, f32[8,128]{1,0:T(8,128)S(1)}, u32[]{:S(2)}, u32[]{:S(2)}) collective-permute-start(f32[8,128]{1,0:T(8,128)S(1)} %get-tuple-element.274), channel_id=1, source_target_pairs={{16,17},{17,16},{1,2},{2,1},{18,19},{19,18},{3,4},{4,3},{20,21},{2... | collective-permute-start | bytes 12296 | tf_op jit(solution)/shard_map/ppermute | solution.py:585
  115.0 3.7 %collective-permute-start.31 = (f32[8,128]{1,0:T(8,128)S(1)}, f32[8,128]{1,0:T(8,128)S(1)}, u32[]{:S(2)}, u32[]{:S(2)}) collective-permute-start(f32[8,128]{1,0:T(8,128)S(1)} %get-tuple-element.281), channel_id=1, source_target_pairs={{0,16},{16,0},{1,17},{17,1},{2,18},{18,2},{3,19},{19,3},{4,20},{20... | collective-permute-start | bytes 12296 | tf_op jit(solution)/shard_map/ppermute | solution.py:586
  115.1 5.8 %collective-permute-start.30 = (f32[8,128]{1,0:T(8,128)S(1)}, f32[8,128]{1,0:T(8,128)S(1)}, u32[]{:S(2)}, u32[]{:S(2)}) collective-permute-start(f32[8,128]{1,0:T(8,128)S(1)} %get-tuple-element.280), channel_id=1, source_target_pairs={{16,17},{17,16},{1,2},{2,1},{18,19},{19,18},{3,4},{4,3},{20,21},{2... | collective-permute-start | bytes 12296 | tf_op jit(solution)/shard_map/ppermute | solution.py:585
  121.4 3.7 %collective-permute-start.33 = (f32[8,128]{1,0:T(8,128)S(1)}, f32[8,128]{1,0:T(8,128)S(1)}, u32[]{:S(2)}, u32[]{:S(2)}) collective-permute-start(f32[8,128]{1,0:T(8,128)S(1)} %get-tuple-element.290), channel_id=1, source_target_pairs={{0,16},{16,0},{1,17},{17,1},{2,18},{18,2},{3,19},{19,3},{4,20},{20... | collective-permute-start | bytes 12296 | tf_op jit(solution)/shard_map/ppermute | solution.py:586
  121.5 5.8 %collective-permute-start.32 = (f32[8,128]{1,0:T(8,128)S(1)}, f32[8,128]{1,0:T(8,128)S(1)}, u32[]{:S(2)}, u32[]{:S(2)}) collective-permute-start(f32[8,128]{1,0:T(8,128)S(1)} %get-tuple-element.289), channel_id=1, source_target_pairs={{16,17},{17,16},{1,2},{2,1},{18,19},{19,18},{3,4},{4,3},{20,21},{2... | collective-permute-start | bytes 12296 | tf_op jit(solution)/shard_map/ppermute | solution.py:585
  127.8 3.7 %collective-permute-start.35 = (f32[8,128]{1,0:T(8,128)S(1)}, f32[8,128]{1,0:T(8,128)S(1)}, u32[]{:S(2)}, u32[]{:S(2)}) collective-permute-start(f32[8,128]{1,0:T(8,128)S(1)} %get-tuple-element.299), channel_id=1, source_target_pairs={{0,16},{16,0},{1,17},{17,1},{2,18},{18,2},{3,19},{19,3},{4,20},{20... | collective-permute-start | bytes 12296 | tf_op jit(solution)/shard_map/ppermute | solution.py:586
  127.9 5.8 %collective-permute-start.34 = (f32[8,128]{1,0:T(8,128)S(1)}, f32[8,128]{1,0:T(8,128)S(1)}, u32[]{:S(2)}, u32[]{:S(2)}) collective-permute-start(f32[8,128]{1,0:T(8,128)S(1)} %get-tuple-element.298), channel_id=1, source_target_pairs={{16,17},{17,16},{1,2},{2,1},{18,19},{19,18},{3,4},{4,3},{20,21},{2... | collective-permute-start | bytes 12296 | tf_op jit(solution)/shard_map/ppermute | solution.py:585
  134.1 3.7 %collective-permute-start.36 = (f32[4,2,2,128]{3,2,1,0:T(2,128)S(1)}, f32[4,2,2,128]{3,2,1,0:T(2,128)S(1)}, u32[]{:S(2)}, u32[]{:S(2)}) collective-permute-start(f32[4,2,2,128]{3,2,1,0:T(2,128)S(1)} %rev.12), channel_id=1, source_target_pairs={{0,16},{16,0},{1,17},{17,1},{2,18},{18,2},{3,19},{19,3},{4,20},{20... | collective-permute-start | bytes 24584 | tf_op jit(solution)/shard_map/ppermute | solution.py:599

commit v20 on v19

--- a/solution.py
+++ b/solution.py
@@ -288,7 +288,7 @@
     return lambda g, n: first[start + g:start + g + n, :]
 
 
-def matvec(terms, chunk=64):
+def matvec(terms, chunk=128):
     width = terms[0][1].shape[1]
     lane = lax.broadcasted_iota(jnp.int32, (chunk, width), 1)
     sub = lax.broadcasted_iota(jnp.int32, (chunk, width), 0)

time: 140 us -> 140 us (level)
  no operation moved by 1% of the time
where the time goes in v20:
time: 140 us; the launch traced here: 139 us
  waiting for transfers between devices  63.6 us (45%)
  starting transfers between devices  48 us (34%)
  Pallas kernels  22.5 us (16%)
  local copies, waits for them, and re-layouts  3.3 us (2%)
    ppermute x16, waiting for transfers between devices, shards_chain(): got_b = lax.ppermute(msg_b, both, b_pairs)  32.6 us
    ppermute x16, starting transfers between devices, shards_chain(): got_b = lax.ppermute(msg_b, both, b_pairs)  31.4 us
    ppermute x16, waiting for transfers between devices, shards_chain(): got_a = lax.ppermute(msg_a, 'row', swap)  24 us
    pallas_call x33, Pallas kernels, call(): pl.pallas_call(body, out_shape=outs, in_specs=[vmem] * len(ins), out_spec...  15.6 us
    all_to_all x1, starting transfers between devices, beside(): lax.all_to_all(by_target, 'col', split_axis=0, concat_axis=0, tiled=True)  6.27 us
    pallas_call x3, Pallas kernels, pack(): pl.pallas_call(functools.partial(pack_kernel, n_col, segments), out_shape...  4.5 us
    ppermute x1, waiting for transfers between devices, shards_chain(): got = lax.ppermute(jnp.flip(done[:, ROWS:], 1), 'row', swap)  3.62 us
    ppermute x16, starting transfers between devices, shards_chain(): got_a = lax.ppermute(msg_a, 'row', swap)  3.44 us
  transfers between devices with their start and end apart: 38, of which 34 were waited for; matrix products, arithmetic and copies ran while one was open for 2% of the time, Pallas kernels for 9%

profile of v20, /device:TPU:8, one launch (start us, length us, event | category | flops | bytes accessed | tf_op | source)
XLA Modules:
  0.0 138.5 jit_solution(15498538637767365255)
XLA Ops:
  4.5 2.2 %pack.3 = (f32[20,128,128]{2,1,0:T(8,128)S(1)}, f32[2,128,128]{2,1,0:T(8,128)S(1)}, f32[2,128,128]{2,1,0:T(8,128)}) custom-call(s32[2,4,4]{2,1,0:T(4,128)} %pattern_hbm.5, f32[2,4,128,128]{3,2,1,0:T(8,128)} %own_hbm.5, f32[4,2,4,128,128]{4,3,2,1,0:T(8,128)} %nb_hbm.5), custom_call_target="tpu_custom_call" | custom-call | tf_op jit(solution)/shard_map/pack/pallas_call | solution.py:511
  6.7 19.9 %conditional.1 = (f32[24,128]{1,0:T(8,128)}, f32[24,128]{1,0:T(8,128)}, f32[2,128,128]{2,1,0:T(8,128)}) conditional(s32[]{:T(128)} %convert_element_type.3, f32[2,128,128]{2,1,0:T(8,128)} %get-tuple-element.166, (f32[1,1,16,4,512]{4,3,2,1,0:T(4,128)}, s32[1,1,16,4]{2,3,1,0:T(4,128)}, f32[2,4,128]{2,1,0:T(4,128)S(1)}, f32[2,4,128]{2,1,0:T(4,128)S(1)}, ...), branch_computations={%region_0.1_spmd, %region_1.2_spmd} | conditional | bytes 1532552 | solution.py:553
  9.1 6.3 %all-to-all-start = ((f32[16,1,2176]{2,1,0:T(1,128)}), f32[16,1,2176]{2,1,0:T(1,128)}, u32[]{:S(2)}, u32[]{:S(2)}) async-start(f32[16,1,2176]{2,1,0:T(1,128)} %by_target.1), calls=%async_computation | async-start | bytes 278528 | tf_op jit(solution)/shard_map/cond/branch_1_fun/all_to_all | solution.py:540
  15.4 3.1 %collective-permute-start.1 = (f32[2,128,128]{2,1,0:T(8,128)}, f32[2,128,128]{2,1,0:T(8,128)}, u32[]{:S(2)}, u32[]{:S(2)}) collective-permute-start(f32[2,128,128]{2,1,0:T(8,128)} %get-tuple-element.22), channel_id=1, source_target_pairs={{16,17},{17,16},{1,2},{2,1},{18,19},{19,18},{3,4},{4,3},{20,21},{2... | collective-permute-start | bytes 393224 | tf_op jit(solution)/shard_map/cond/branch_1_fun/ppermute | solution.py:530
  18.5 2.5 %all-to-all-done = f32[16,1,2176]{2,1,0:T(1,128)} async-done(((f32[16,1,2176]{2,1,0:T(1,128)}), f32[16,1,2176]{2,1,0:T(1,128)}, u32[]{:S(2)}, u32[]{:S(2)}) %all-to-all-start) | async-done | bytes 139296 | tf_op jit(solution)/shard_map/cond/branch_1_fun/all_to_all | solution.py:540
  29.2 2.5 %collective-permute-start.4 = (f32[264,128]{1,0:T(8,128)S(1)}, f32[264,128]{1,0:T(8,128)S(1)}, u32[]{:S(2)}, u32[]{:S(2)}) collective-permute-start(f32[264,128]{1,0:T(8,128)S(1)} %get-tuple-element.171), channel_id=1, source_target_pairs={{16,17},{17,16},{1,2},{2,1},{18,19},{19,18},{3,4},{4,3},{20,21},{2... | collective-permute-start | bytes 405512 | tf_op jit(solution)/shard_map/ppermute | solution.py:585
  31.7 4.8 %collective-permute-done.4.first_b.got_b = f32[264,128]{1,0:T(8,128)S(1)} collective-permute-done((f32[264,128]{1,0:T(8,128)S(1)}, f32[264,128]{1,0:T(8,128)S(1)}, u32[]{:S(2)}, u32[]{:S(2)}) %collective-permute-start.4) | collective-permute-done | bytes 135200 | tf_op jit(solution)/shard_map/ppermute | solution.py:585
  38.3 1.9 %collective-permute-start.6 = (f32[8,128]{1,0:T(8,128)S(1)}, f32[8,128]{1,0:T(8,128)S(1)}, u32[]{:S(2)}, u32[]{:S(2)}) collective-permute-start(f32[8,128]{1,0:T(8,128)S(1)} %get-tuple-element.178), channel_id=1, source_target_pairs={{16,17},{17,16},{1,2},{2,1},{18,19},{19,18},{3,4},{4,3},{20,21},{2... | collective-permute-start | bytes 12296 | tf_op jit(solution)/shard_map/ppermute | solution.py:585
  41.6 2.6 %collective-permute-done.6.got_b = f32[8,128]{1,0:T(8,128)S(1)} collective-permute-done((f32[8,128]{1,0:T(8,128)S(1)}, f32[8,128]{1,0:T(8,128)S(1)}, u32[]{:S(2)}, u32[]{:S(2)}) %collective-permute-start.6) | collective-permute-done | bytes 4128 | tf_op jit(solution)/shard_map/ppermute | solution.py:585
  44.7 1.9 %collective-permute-start.8 = (f32[8,128]{1,0:T(8,128)S(1)}, f32[8,128]{1,0:T(8,128)S(1)}, u32[]{:S(2)}, u32[]{:S(2)}) collective-permute-start(f32[8,128]{1,0:T(8,128)S(1)} %get-tuple-element.187), channel_id=1, source_target_pairs={{16,17},{17,16},{1,2},{2,1},{18,19},{19,18},{3,4},{4,3},{20,21},{2... | collective-permute-start | bytes 12296 | tf_op jit(solution)/shard_map/ppermute | solution.py:585
  46.6 1.7 %collective-permute-done.9.got_a = f32[8,128]{1,0:T(8,128)S(1)} collective-permute-done((f32[8,128]{1,0:T(8,128)S(1)}, f32[8,128]{1,0:T(8,128)S(1)}, u32[]{:S(2)}, u32[]{:S(2)}) %collective-permute-start.9) | collective-permute-done | bytes 4128 | tf_op jit(solution)/shard_map/ppermute | solution.py:586
  48.7 1.8 %collective-permute-done.8.got_b = f32[8,128]{1,0:T(8,128)S(1)} collective-permute-done((f32[8,128]{1,0:T(8,128)S(1)}, f32[8,128]{1,0:T(8,128)S(1)}, u32[]{:S(2)}, u32[]{:S(2)}) %collective-permute-start.8) | collective-permute-done | bytes 4128 | tf_op jit(solution)/shard_map/ppermute | solution.py:585
  51.1 1.9 %collective-permute-start.10 = (f32[8,128]{1,0:T(8,128)S(1)}, f32[8,128]{1,0:T(8,128)S(1)}, u32[]{:S(2)}, u32[]{:S(2)}) collective-permute-start(f32[8,128]{1,0:T(8,128)S(1)} %get-tuple-element.196), channel_id=1, source_target_pairs={{16,17},{17,16},{1,2},{2,1},{18,19},{19,18},{3,4},{4,3},{20,21},{2... | collective-permute-start | bytes 12296 | tf_op jit(solution)/shard_map/ppermute | solution.py:585
  53.0 1.7 %collective-permute-done.11.got_a = f32[8,128]{1,0:T(8,128)S(1)} collective-permute-done((f32[8,128]{1,0:T(8,128)S(1)}, f32[8,128]{1,0:T(8,128)S(1)}, u32[]{:S(2)}, u32[]{:S(2)}) %collective-permute-start.11) | collective-permute-done | bytes 4128 | tf_op jit(solution)/shard_map/ppermute | solution.py:586
  55.1 1.8 %collective-permute-done.10.got_b = f32[8,128]{1,0:T(8,128)S(1)} collective-permute-done((f32[8,128]{1,0:T(8,128)S(1)}, f32[8,128]{1,0:T(8,128)S(1)}, u32[]{:S(2)}, u32[]{:S(2)}) %collective-permute-start.10) | collective-permute-done | bytes 4128 | tf_op jit(solution)/shard_map/ppermute | solution.py:585
  57.5 1.9 %collective-permute-start.12 = (f32[8,128]{1,0:T(8,128)S(1)}, f32[8,128]{1,0:T(8,128)S(1)}, u32[]{:S(2)}, u32[]{:S(2)}) collective-permute-start(f32[8,128]{1,0:T(8,128)S(1)} %get-tuple-element.206), channel_id=1, source_target_pairs={{16,17},{17,16},{1,2},{2,1},{18,19},{19,18},{3,4},{4,3},{20,21},{2... | collective-permute-start | bytes 12296 | tf_op jit(solution)/shard_map/ppermute | solution.py:585
  59.4 1.7 %collective-permute-done.13.got_a = f32[8,128]{1,0:T(8,128)S(1)} collective-permute-done((f32[8,128]{1,0:T(8,128)S(1)}, f32[8,128]{1,0:T(8,128)S(1)}, u32[]{:S(2)}, u32[]{:S(2)}) %collective-permute-start.13) | collective-permute-done | bytes 4128 | tf_op jit(solution)/shard_map/ppermute | solution.py:586
  61.5 1.8 %collective-permute-done.12.got_b = f32[8,128]{1,0:T(8,128)S(1)} collective-permute-done((f32[8,128]{1,0:T(8,128)S(1)}, f32[8,128]{1,0:T(8,128)S(1)}, u32[]{:S(2)}, u32[]{:S(2)}) %collective-permute-start.12) | collective-permute-done | bytes 4128 | tf_op jit(solution)/shard_map/ppermute | solution.py:585
  63.9 1.9 %collective-permute-start.14 = (f32[8,128]{1,0:T(8,128)S(1)}, f32[8,128]{1,0:T(8,128)S(1)}, u32[]{:S(2)}, u32[]{:S(2)}) collective-permute-start(f32[8,128]{1,0:T(8,128)S(1)} %get-tuple-element.212), channel_id=1, source_target_pairs={{16,17},{17,16},{1,2},{2,1},{18,19},{19,18},{3,4},{4,3},{20,21},{2... | collective-permute-start | bytes 12296 | tf_op jit(solution)/shard_map/ppermute | solution.py:585
  65.8 1.7 %collective-permute-done.15.got_a = f32[8,128]{1,0:T(8,128)S(1)} collective-permute-done((f32[8,128]{1,0:T(8,128)S(1)}, f32[8,128]{1,0:T(8,128)S(1)}, u32[]{:S(2)}, u32[]{:S(2)}) %collective-permute-start.15) | collective-permute-done | bytes 4128 | tf_op jit(solution)/shard_map/ppermute | solution.py:586
  67.9 1.8 %collective-permute-done.14.got_b = f32[8,128]{1,0:T(8,128)S(1)} collective-permute-done((f32[8,128]{1,0:T(8,128)S(1)}, f32[8,128]{1,0:T(8,128)S(1)}, u32[]{:S(2)}, u32[]{:S(2)}) %collective-permute-start.14) | collective-permute-done | bytes 4128 | tf_op jit(solution)/shard_map/ppermute | solution.py:585
  70.3 1.9 %collective-permute-start.16 = (f32[8,128]{1,0:T(8,128)S(1)}, f32[8,128]{1,0:T(8,128)S(1)}, u32[]{:S(2)}, u32[]{:S(2)}) collective-permute-start(f32[8,128]{1,0:T(8,128)S(1)} %get-tuple-element.221), channel_id=1, source_target_pairs={{16,17},{17,16},{1,2},{2,1},{18,19},{19,18},{3,4},{4,3},{20,21},{2... | collective-permute-start | bytes 12296 | tf_op jit(solution)/shard_map/ppermute | solution.py:585
  72.2 1.7 %collective-permute-done.17.got_a = f32[8,128]{1,0:T(8,128)S(1)} collective-permute-done((f32[8,128]{1,0:T(8,128)S(1)}, f32[8,128]{1,0:T(8,128)S(1)}, u32[]{:S(2)}, u32[]{:S(2)}) %collective-permute-start.17) | collective-permute-done | bytes 4128 | tf_op jit(solution)/shard_map/ppermute | solution.py:586
  74.3 1.8 %collective-permute-done.16.got_b = f32[8,128]{1,0:T(8,128)S(1)} collective-permute-done((f32[8,128]{1,0:T(8,128)S(1)}, f32[8,128]{1,0:T(8,128)S(1)}, u32[]{:S(2)}, u32[]{:S(2)}) %collective-permute-start.16) | collective-permute-done | bytes 4128 | tf_op jit(solution)/shard_map/ppermute | solution.py:585
  76.7 1.9 %collective-permute-start.18 = (f32[8,128]{1,0:T(8,128)S(1)}, f32[8,128]{1,0:T(8,128)S(1)}, u32[]{:S(2)}, u32[]{:S(2)}) collective-permute-start(f32[8,128]{1,0:T(8,128)S(1)} %get-tuple-element.230), channel_id=1, source_target_pairs={{16,17},{17,16},{1,2},{2,1},{18,19},{19,18},{3,4},{4,3},{20,21},{2... | collective-permute-start | bytes 12296 | tf_op jit(solution)/shard_map/ppermute | solution.py:585
  78.6 1.7 %collective-permute-done.19.got_a = f32[8,128]{1,0:T(8,128)S(1)} collective-permute-done((f32[8,128]{1,0:T(8,128)S(1)}, f32[8,128]{1,0:T(8,128)S(1)}, u32[]{:S(2)}, u32[]{:S(2)}) %collective-permute-start.19) | collective-permute-done | bytes 4128 | tf_op jit(solution)/shard_map/ppermute | solution.py:586
  80.7 1.8 %collective-permute-done.18.got_b = f32[8,128]{1,0:T(8,128)S(1)} collective-permute-done((f32[8,128]{1,0:T(8,128)S(1)}, f32[8,128]{1,0:T(8,128)S(1)}, u32[]{:S(2)}, u32[]{:S(2)}) %collective-permute-start.18) | collective-permute-done | bytes 4128 | tf_op jit(solution)/shard_map/ppermute | solution.py:585
  83.1 1.9 %collective-permute-start.20 = (f32[8,128]{1,0:T(8,128)S(1)}, f32[8,128]{1,0:T(8,128)S(1)}, u32[]{:S(2)}, u32[]{:S(2)}) collective-permute-start(f32[8,128]{1,0:T(8,128)S(1)} %get-tuple-element.240), channel_id=1, source_target_pairs={{16,17},{17,16},{1,2},{2,1},{18,19},{19,18},{3,4},{4,3},{20,21},{2... | collective-permute-start | bytes 12296 | tf_op jit(solution)/shard_map/ppermute | solution.py:585
  85.0 1.7 %collective-permute-done.21.got_a = f32[8,128]{1,0:T(8,128)S(1)} collective-permute-done((f32[8,128]{1,0:T(8,128)S(1)}, f32[8,128]{1,0:T(8,128)S(1)}, u32[]{:S(2)}, u32[]{:S(2)}) %collective-permute-start.21) | collective-permute-done | bytes 4128 | tf_op jit(solution)/shard_map/ppermute | solution.py:586
  87.1 1.8 %collective-permute-done.20.got_b = f32[8,128]{1,0:T(8,128)S(1)} collective-permute-done((f32[8,128]{1,0:T(8,128)S(1)}, f32[8,128]{1,0:T(8,128)S(1)}, u32[]{:S(2)}, u32[]{:S(2)}) %collective-permute-start.20) | collective-permute-done | bytes 4128 | tf_op jit(solution)/shard_map/ppermute | solution.py:585
  89.5 2.1 %collective-permute-start.22 = (f32[8,128]{1,0:T(8,128)S(1)}, f32[8,128]{1,0:T(8,128)S(1)}, u32[]{:S(2)}, u32[]{:S(2)}) collective-permute-start(f32[8,128]{1,0:T(8,128)S(1)} %get-tuple-element.246), channel_id=1, source_target_pairs={{16,17},{17,16},{1,2},{2,1},{18,19},{19,18},{3,4},{4,3},{20,21},{2... | collective-permute-start | bytes 12296 | tf_op jit(solution)/shard_map/ppermute | solution.py:585
  93.5 1.8 %collective-permute-done.22.got_b = f32[8,128]{1,0:T(8,128)S(1)} collective-permute-done((f32[8,128]{1,0:T(8,128)S(1)}, f32[8,128]{1,0:T(8,128)S(1)}, u32[]{:S(2)}, u32[]{:S(2)}) %collective-permute-start.22) | collective-permute-done | bytes 4128 | tf_op jit(solution)/shard_map/ppermute | solution.py:585
  95.9 1.9 %collective-permute-start.24 = (f32[8,128]{1,0:T(8,128)S(1)}, f32[8,128]{1,0:T(8,128)S(1)}, u32[]{:S(2)}, u32[]{:S(2)}) collective-permute-start(f32[8,128]{1,0:T(8,128)S(1)} %get-tuple-element.255), channel_id=1, source_target_pairs={{16,17},{17,16},{1,2},{2,1},{18,19},{19,18},{3,4},{4,3},{20,21},{2... | collective-permute-start | bytes 12296 | tf_op jit(solution)/shard_map/ppermute | solution.py:585
  97.8 1.7 %collective-permute-done.25.got_a = f32[8,128]{1,0:T(8,128)S(1)} collective-permute-done((f32[8,128]{1,0:T(8,128)S(1)}, f32[8,128]{1,0:T(8,128)S(1)}, u32[]{:S(2)}, u32[]{:S(2)}) %collective-permute-start.25) | collective-permute-done | bytes 4128 | tf_op jit(solution)/shard_map/ppermute | solution.py:586
  99.9 1.8 %collective-permute-done.24.got_b = f32[8,128]{1,0:T(8,128)S(1)} collective-permute-done((f32[8,128]{1,0:T(8,128)S(1)}, f32[8,128]{1,0:T(8,128)S(1)}, u32[]{:S(2)}, u32[]{:S(2)}) %collective-permute-start.24) | collective-permute-done | bytes 4128 | tf_op jit(solution)/shard_map/ppermute | solution.py:585
  102.3 1.9 %collective-permute-start.26 = (f32[8,128]{1,0:T(8,128)S(1)}, f32[8,128]{1,0:T(8,128)S(1)}, u32[]{:S(2)}, u32[]{:S(2)}) collective-permute-start(f32[8,128]{1,0:T(8,128)S(1)} %get-tuple-element.264), channel_id=1, source_target_pairs={{16,17},{17,16},{1,2},{2,1},{18,19},{19,18},{3,4},{4,3},{20,21},{2... | collective-permute-start | bytes 12296 | tf_op jit(solution)/shard_map/ppermute | solution.py:585
  104.2 1.7 %collective-permute-done.27.got_a = f32[8,128]{1,0:T(8,128)S(1)} collective-permute-done((f32[8,128]{1,0:T(8,128)S(1)}, f32[8,128]{1,0:T(8,128)S(1)}, u32[]{:S(2)}, u32[]{:S(2)}) %collective-permute-start.27) | collective-permute-done | bytes 4128 | tf_op jit(solution)/shard_map/ppermute | solution.py:586
  106.3 1.8 %collective-permute-done.26.got_b = f32[8,128]{1,0:T(8,128)S(1)} collective-permute-done((f32[8,128]{1,0:T(8,128)S(1)}, f32[8,128]{1,0:T(8,128)S(1)}, u32[]{:S(2)}, u32[]{:S(2)}) %collective-permute-start.26) | collective-permute-done | bytes 4128 | tf_op jit(solution)/shard_map/ppermute | solution.py:585
  108.7 1.9 %collective-permute-start.28 = (f32[8,128]{1,0:T(8,128)S(1)}, f32[8,128]{1,0:T(8,128)S(1)}, u32[]{:S(2)}, u32[]{:S(2)}) collective-permute-start(f32[8,128]{1,0:T(8,128)S(1)} %get-tuple-element.274), channel_id=1, source_target_pairs={{16,17},{17,16},{1,2},{2,1},{18,19},{19,18},{3,4},{4,3},{20,21},{2... | collective-permute-start | bytes 12296 | tf_op jit(solution)/shard_map/ppermute | solution.py:585
  110.7 1.7 %collective-permute-done.29.got_a = f32[8,128]{1,0:T(8,128)S(1)} collective-permute-done((f32[8,128]{1,0:T(8,128)S(1)}, f32[8,128]{1,0:T(8,128)S(1)}, u32[]{:S(2)}, u32[]{:S(2)}) %collective-permute-start.29) | collective-permute-done | bytes 4128 | tf_op jit(solution)/shard_map/ppermute | solution.py:586
  112.7 1.8 %collective-permute-done.28.got_b = f32[8,128]{1,0:T(8,128)S(1)} collective-permute-done((f32[8,128]{1,0:T(8,128)S(1)}, f32[8,128]{1,0:T(8,128)S(1)}, u32[]{:S(2)}, u32[]{:S(2)}) %collective-permute-start.28) | collective-permute-done | bytes 4128 | tf_op jit(solution)/shard_map/ppermute | solution.py:585
  115.1 1.9 %collective-permute-start.30 = (f32[8,128]{1,0:T(8,128)S(1)}, f32[8,128]{1,0:T(8,128)S(1)}, u32[]{:S(2)}, u32[]{:S(2)}) collective-permute-start(f32[8,128]{1,0:T(8,128)S(1)} %get-tuple-element.280), channel_id=1, source_target_pairs={{16,17},{17,16},{1,2},{2,1},{18,19},{19,18},{3,4},{4,3},{20,21},{2... | collective-permute-start | bytes 12296 | tf_op jit(solution)/shard_map/ppermute | solution.py:585
  119.1 1.8 %collective-permute-done.30.got_b = f32[8,128]{1,0:T(8,128)S(1)} collective-permute-done((f32[8,128]{1,0:T(8,128)S(1)}, f32[8,128]{1,0:T(8,128)S(1)}, u32[]{:S(2)}, u32[]{:S(2)}) %collective-permute-start.30) | collective-permute-done | bytes 4128 | tf_op jit(solution)/shard_map/ppermute | solution.py:585
  121.5 1.9 %collective-permute-start.32 = (f32[8,128]{1,0:T(8,128)S(1)}, f32[8,128]{1,0:T(8,128)S(1)}, u32[]{:S(2)}, u32[]{:S(2)}) collective-permute-start(f32[8,128]{1,0:T(8,128)S(1)} %get-tuple-element.289), channel_id=1, source_target_pairs={{16,17},{17,16},{1,2},{2,1},{18,19},{19,18},{3,4},{4,3},{20,21},{2... | collective-permute-start | bytes 12296 | tf_op jit(solution)/shard_map/ppermute | solution.py:585
  125.5 1.8 %collective-permute-done.32.got_b = f32[8,128]{1,0:T(8,128)S(1)} collective-permute-done((f32[8,128]{1,0:T(8,128)S(1)}, f32[8,128]{1,0:T(8,128)S(1)}, u32[]{:S(2)}, u32[]{:S(2)}) %collective-permute-start.32) | collective-permute-done | bytes 4128 | tf_op jit(solution)/shard_map/ppermute | solution.py:585
  127.9 1.9 %collective-permute-start.34 = (f32[8,128]{1,0:T(8,128)S(1)}, f32[8,128]{1,0:T(8,128)S(1)}, u32[]{:S(2)}, u32[]{:S(2)}) collective-permute-start(f32[8,128]{1,0:T(8,128)S(1)} %get-tuple-element.298), channel_id=1, source_target_pairs={{16,17},{17,16},{1,2},{2,1},{18,19},{19,18},{3,4},{4,3},{20,21},{2... | collective-permute-start | bytes 12296 | tf_op jit(solution)/shard_map/ppermute | solution.py:585
  131.9 1.8 %collective-permute-done.34.got_b = f32[8,128]{1,0:T(8,128)S(1)} collective-permute-done((f32[8,128]{1,0:T(8,128)S(1)}, f32[8,128]{1,0:T(8,128)S(1)}, u32[]{:S(2)}, u32[]{:S(2)}) %collective-permute-start.34) | collective-permute-done | bytes 4128 | tf_op jit(solution)/shard_map/ppermute | solution.py:585
  134.2 3.6 %collective-permute-done.36 = f32[4,2,2,128]{3,2,1,0:T(2,128)S(1)} collective-permute-done((f32[4,2,2,128]{3,2,1,0:T(2,128)S(1)}, f32[4,2,2,128]{3,2,1,0:T(2,128)S(1)}, u32[]{:S(2)}, u32[]{:S(2)}) %collective-permute-start.36) | collective-permute-done | bytes 8224 | tf_op jit(solution)/shard_map/ppermute | solution.py:599
  (83 shorter events, 39.6 us)
Async XLA Ops:
  1.2 5.5 %copy-start.1 = (f32[2,4,128]{2,1,0:T(4,128)S(1)}, f32[2,4,128]{2,1,0:T(4,128)}, u32[]{:S(2)}) copy-start(f32[2,4,128]{2,1,0:T(4,128)} %param.12) | copy-start | bytes 12292
  1.2 5.5 %copy-start.2 = (f32[2,4,128]{2,1,0:T(4,128)S(1)}, f32[2,4,128]{2,1,0:T(4,128)}, u32[]{:S(2)}) copy-start(f32[2,4,128]{2,1,0:T(4,128)} %param.13) | copy-start | bytes 12292
  1.2 25.3 %collective-permute-start.2 = (f32[10,128,128]{2,1,0:T(8,128)S(1)}, f32[10,128,128]{2,1,0:T(8,128)S(1)}, u32[]{:S(2)}, u32[]{:S(2)}) collective-permute-start(f32[10,128,128]{2,1,0:T(8,128)S(1)} %pack.4), channel_id=1, source_target_pairs={{0,16},{16,0},{1,17},{17,1},{2,18},{18,2},{3,19},{19,3},{4,20},{20... | collective-permute-start | bytes 1966088 | tf_op jit(solution)/shard_map/ppermute | solution.py:524
  3.9 22.7 %collective-permute-start.3 = (f32[6,128,128]{2,1,0:T(8,128)S(1)}, f32[6,128,128]{2,1,0:T(8,128)S(1)}, u32[]{:S(2)}, u32[]{:S(2)}) collective-permute-start(f32[6,128,128]{2,1,0:T(8,128)S(1)} %pack.5), channel_id=1, source_target_pairs={{0,16},{16,0},{1,17},{17,1},{2,18},{18,2},{3,19},{19,3},{4,20},{20... | collective-permute-start | bytes 1179656 | tf_op jit(solution)/shard_map/ppermute | solution.py:524
  9.1 11.9 %all-to-all-start = ((f32[16,1,2176]{2,1,0:T(1,128)}), f32[16,1,2176]{2,1,0:T(1,128)}, u32[]{:S(2)}, u32[]{:S(2)}) async-start(f32[16,1,2176]{2,1,0:T(1,128)} %by_target.1), calls=%async_computation | async-start | bytes 278528 | tf_op jit(solution)/shard_map/cond/branch_1_fun/all_to_all | solution.py:540
  15.4 8.9 %collective-permute-start.1 = (f32[2,128,128]{2,1,0:T(8,128)}, f32[2,128,128]{2,1,0:T(8,128)}, u32[]{:S(2)}, u32[]{:S(2)}) collective-permute-start(f32[2,128,128]{2,1,0:T(8,128)} %get-tuple-element.22), channel_id=1, source_target_pairs={{16,17},{17,16},{1,2},{2,1},{18,19},{19,18},{3,4},{4,3},{20,21},{2... | collective-permute-start | bytes 393224 | tf_op jit(solution)/shard_map/cond/branch_1_fun/ppermute | solution.py:530
  22.7 3.9 %collective-permute-start = (f32[24,128]{1,0:T(8,128)S(1)}, f32[24,128]{1,0:T(8,128)}, u32[]{:S(2)}, u32[]{:S(2)}) collective-permute-start(f32[24,128]{1,0:T(8,128)S(1)} %get-tuple-element.21), channel_id=1, source_target_pairs={{0,16},{16,0},{1,17},{17,1},{2,18},{18,2},{3,19},{19,3},{4,20},{20... | collective-permute-start | bytes 36872 | tf_op jit(solution)/shard_map/cond/branch_1_fun/ppermute | solution.py:551
  26.6 10.0 %copy-start = (f32[2,128,128]{2,1,0:T(8,128)S(1)}, f32[2,128,128]{2,1,0:T(8,128)}, u32[]{:S(2)}) copy-start(f32[2,128,128]{2,1,0:T(8,128)} %get-tuple-element.172.beyond_0) | copy-start | bytes 393220
  27.6 8.9 %collective-permute-start.5 = (f32[520,128]{1,0:T(8,128)S(1)}, f32[520,128]{1,0:T(8,128)S(1)}, u32[]{:S(2)}, u32[]{:S(2)}) collective-permute-start(f32[520,128]{1,0:T(8,128)S(1)} %get-tuple-element.173), channel_id=1, source_target_pairs={{0,16},{16,0},{1,17},{17,1},{2,18},{18,2},{3,19},{19,3},{4,20},{20... | collective-permute-start | bytes 798728 | tf_op jit(solution)/shard_map/ppermute | solution.py:586
  29.2 7.3 %collective-permute-start.4 = (f32[264,128]{1,0:T(8,128)S(1)}, f32[264,128]{1,0:T(8,128)S(1)}, u32[]{:S(2)}, u32[]{:S(2)}) collective-permute-start(f32[264,128]{1,0:T(8,128)S(1)} %get-tuple-element.171), channel_id=1, source_target_pairs={{16,17},{17,16},{1,2},{2,1},{18,19},{19,18},{3,4},{4,3},{20,21},{2... | collective-permute-start | bytes 405512 | tf_op jit(solution)/shard_map/ppermute | solution.py:585
  37.5 3.7 %collective-permute-start.7 = (f32[8,128]{1,0:T(8,128)S(1)}, f32[8,128]{1,0:T(8,128)S(1)}, u32[]{:S(2)}, u32[]{:S(2)}) collective-permute-start(f32[8,128]{1,0:T(8,128)S(1)} %get-tuple-element.179), channel_id=1, source_target_pairs={{0,16},{16,0},{1,17},{17,1},{2,18},{18,2},{3,19},{19,3},{4,20},{20... | collective-permute-start | bytes 12296 | tf_op jit(solution)/shard_map/ppermute | solution.py:586
  38.3 5.8 %collective-permute-start.6 = (f32[8,128]{1,0:T(8,128)S(1)}, f32[8,128]{1,0:T(8,128)S(1)}, u32[]{:S(2)}, u32[]{:S(2)}) collective-permute-start(f32[8,128]{1,0:T(8,128)S(1)} %get-tuple-element.178), channel_id=1, source_target_pairs={{16,17},{17,16},{1,2},{2,1},{18,19},{19,18},{3,4},{4,3},{20,21},{2... | collective-permute-start | bytes 12296 | tf_op jit(solution)/shard_map/ppermute | solution.py:585
  44.6 3.7 %collective-permute-start.9 = (f32[8,128]{1,0:T(8,128)S(1)}, f32[8,128]{1,0:T(8,128)S(1)}, u32[]{:S(2)}, u32[]{:S(2)}) collective-permute-start(f32[8,128]{1,0:T(8,128)S(1)} %get-tuple-element.188), channel_id=1, source_target_pairs={{0,16},{16,0},{1,17},{17,1},{2,18},{18,2},{3,19},{19,3},{4,20},{20... | collective-permute-start | bytes 12296 | tf_op jit(solution)/shard_map/ppermute | solution.py:586
  44.7 5.8 %collective-permute-start.8 = (f32[8,128]{1,0:T(8,128)S(1)}, f32[8,128]{1,0:T(8,128)S(1)}, u32[]{:S(2)}, u32[]{:S(2)}) collective-permute-start(f32[8,128]{1,0:T(8,128)S(1)} %get-tuple-element.187), channel_id=1, source_target_pairs={{16,17},{17,16},{1,2},{2,1},{18,19},{19,18},{3,4},{4,3},{20,21},{2... | collective-permute-start | bytes 12296 | tf_op jit(solution)/shard_map/ppermute | solution.py:585
  51.0 3.7 %collective-permute-start.11 = (f32[8,128]{1,0:T(8,128)S(1)}, f32[8,128]{1,0:T(8,128)S(1)}, u32[]{:S(2)}, u32[]{:S(2)}) collective-permute-start(f32[8,128]{1,0:T(8,128)S(1)} %get-tuple-element.197), channel_id=1, source_target_pairs={{0,16},{16,0},{1,17},{17,1},{2,18},{18,2},{3,19},{19,3},{4,20},{20... | collective-permute-start | bytes 12296 | tf_op jit(solution)/shard_map/ppermute | solution.py:586
  51.1 5.8 %collective-permute-start.10 = (f32[8,128]{1,0:T(8,128)S(1)}, f32[8,128]{1,0:T(8,128)S(1)}, u32[]{:S(2)}, u32[]{:S(2)}) collective-permute-start(f32[8,128]{1,0:T(8,128)S(1)} %get-tuple-element.196), channel_id=1, source_target_pairs={{16,17},{17,16},{1,2},{2,1},{18,19},{19,18},{3,4},{4,3},{20,21},{2... | collective-permute-start | bytes 12296 | tf_op jit(solution)/shard_map/ppermute | solution.py:585
  57.4 3.7 %collective-permute-start.13 = (f32[8,128]{1,0:T(8,128)S(1)}, f32[8,128]{1,0:T(8,128)S(1)}, u32[]{:S(2)}, u32[]{:S(2)}) collective-permute-start(f32[8,128]{1,0:T(8,128)S(1)} %get-tuple-element.207), channel_id=1, source_target_pairs={{0,16},{16,0},{1,17},{17,1},{2,18},{18,2},{3,19},{19,3},{4,20},{20... | collective-permute-start | bytes 12296 | tf_op jit(solution)/shard_map/ppermute | solution.py:586
  57.5 5.8 %collective-permute-start.12 = (f32[8,128]{1,0:T(8,128)S(1)}, f32[8,128]{1,0:T(8,128)S(1)}, u32[]{:S(2)}, u32[]{:S(2)}) collective-permute-start(f32[8,128]{1,0:T(8,128)S(1)} %get-tuple-element.206), channel_id=1, source_target_pairs={{16,17},{17,16},{1,2},{2,1},{18,19},{19,18},{3,4},{4,3},{20,21},{2... | collective-permute-start | bytes 12296 | tf_op jit(solution)/shard_map/ppermute | solution.py:585
  63.8 3.7 %collective-permute-start.15 = (f32[8,128]{1,0:T(8,128)S(1)}, f32[8,128]{1,0:T(8,128)S(1)}, u32[]{:S(2)}, u32[]{:S(2)}) collective-permute-start(f32[8,128]{1,0:T(8,128)S(1)} %get-tuple-element.213), channel_id=1, source_target_pairs={{0,16},{16,0},{1,17},{17,1},{2,18},{18,2},{3,19},{19,3},{4,20},{20... | collective-permute-start | bytes 12296 | tf_op jit(solution)/shard_map/ppermute | solution.py:586
  63.9 5.8 %collective-permute-start.14 = (f32[8,128]{1,0:T(8,128)S(1)}, f32[8,128]{1,0:T(8,128)S(1)}, u32[]{:S(2)}, u32[]{:S(2)}) collective-permute-start(f32[8,128]{1,0:T(8,128)S(1)} %get-tuple-element.212), channel_id=1, source_target_pairs={{16,17},{17,16},{1,2},{2,1},{18,19},{19,18},{3,4},{4,3},{20,21},{2... | collective-permute-start | bytes 12296 | tf_op jit(solution)/shard_map/ppermute | solution.py:585
  70.2 3.7 %collective-permute-start.17 = (f32[8,128]{1,0:T(8,128)S(1)}, f32[8,128]{1,0:T(8,128)S(1)}, u32[]{:S(2)}, u32[]{:S(2)}) collective-permute-start(f32[8,128]{1,0:T(8,128)S(1)} %get-tuple-element.222), channel_id=1, source_target_pairs={{0,16},{16,0},{1,17},{17,1},{2,18},{18,2},{3,19},{19,3},{4,20},{20... | collective-permute-start | bytes 12296 | tf_op jit(solution)/shard_map/ppermute | solution.py:586
  70.3 5.8 %collective-permute-start.16 = (f32[8,128]{1,0:T(8,128)S(1)}, f32[8,128]{1,0:T(8,128)S(1)}, u32[]{:S(2)}, u32[]{:S(2)}) collective-permute-start(f32[8,128]{1,0:T(8,128)S(1)} %get-tuple-element.221), channel_id=1, source_target_pairs={{16,17},{17,16},{1,2},{2,1},{18,19},{19,18},{3,4},{4,3},{20,21},{2... | collective-permute-start | bytes 12296 | tf_op jit(solution)/shard_map/ppermute | solution.py:585
  76.6 3.7 %collective-permute-start.19 = (f32[8,128]{1,0:T(8,128)S(1)}, f32[8,128]{1,0:T(8,128)S(1)}, u32[]{:S(2)}, u32[]{:S(2)}) collective-permute-start(f32[8,128]{1,0:T(8,128)S(1)} %get-tuple-element.231), channel_id=1, source_target_pairs={{0,16},{16,0},{1,17},{17,1},{2,18},{18,2},{3,19},{19,3},{4,20},{20... | collective-permute-start | bytes 12296 | tf_op jit(solution)/shard_map/ppermute | solution.py:586
  76.7 5.8 %collective-permute-start.18 = (f32[8,128]{1,0:T(8,128)S(1)}, f32[8,128]{1,0:T(8,128)S(1)}, u32[]{:S(2)}, u32[]{:S(2)}) collective-permute-start(f32[8,128]{1,0:T(8,128)S(1)} %get-tuple-element.230), channel_id=1, source_target_pairs={{16,17},{17,16},{1,2},{2,1},{18,19},{19,18},{3,4},{4,3},{20,21},{2... | collective-permute-start | bytes 12296 | tf_op jit(solution)/shard_map/ppermute | solution.py:585
  83.0 3.7 %collective-permute-start.21 = (f32[8,128]{1,0:T(8,128)S(1)}, f32[8,128]{1,0:T(8,128)S(1)}, u32[]{:S(2)}, u32[]{:S(2)}) collective-permute-start(f32[8,128]{1,0:T(8,128)S(1)} %get-tuple-element.241), channel_id=1, source_target_pairs={{0,16},{16,0},{1,17},{17,1},{2,18},{18,2},{3,19},{19,3},{4,20},{20... | collective-permute-start | bytes 12296 | tf_op jit(solution)/shard_map/ppermute | solution.py:586
  83.1 5.8 %collective-permute-start.20 = (f32[8,128]{1,0:T(8,128)S(1)}, f32[8,128]{1,0:T(8,128)S(1)}, u32[]{:S(2)}, u32[]{:S(2)}) collective-permute-start(f32[8,128]{1,0:T(8,128)S(1)} %get-tuple-element.240), channel_id=1, source_target_pairs={{16,17},{17,16},{1,2},{2,1},{18,19},{19,18},{3,4},{4,3},{20,21},{2... | collective-permute-start | bytes 12296 | tf_op jit(solution)/shard_map/ppermute | solution.py:585
  89.4 3.7 %collective-permute-start.23 = (f32[8,128]{1,0:T(8,128)S(1)}, f32[8,128]{1,0:T(8,128)S(1)}, u32[]{:S(2)}, u32[]{:S(2)}) collective-permute-start(f32[8,128]{1,0:T(8,128)S(1)} %get-tuple-element.247), channel_id=1, source_target_pairs={{0,16},{16,0},{1,17},{17,1},{2,18},{18,2},{3,19},{19,3},{4,20},{20... | collective-permute-start | bytes 12296 | tf_op jit(solution)/shard_map/ppermute | solution.py:586
  89.5 5.8 %collective-permute-start.22 = (f32[8,128]{1,0:T(8,128)S(1)}, f32[8,128]{1,0:T(8,128)S(1)}, u32[]{:S(2)}, u32[]{:S(2)}) collective-permute-start(f32[8,128]{1,0:T(8,128)S(1)} %get-tuple-element.246), channel_id=1, source_target_pairs={{16,17},{17,16},{1,2},{2,1},{18,19},{19,18},{3,4},{4,3},{20,21},{2... | collective-permute-start | bytes 12296 | tf_op jit(solution)/shard_map/ppermute | solution.py:585
  95.8 3.7 %collective-permute-start.25 = (f32[8,128]{1,0:T(8,128)S(1)}, f32[8,128]{1,0:T(8,128)S(1)}, u32[]{:S(2)}, u32[]{:S(2)}) collective-permute-start(f32[8,128]{1,0:T(8,128)S(1)} %get-tuple-element.256), channel_id=1, source_target_pairs={{0,16},{16,0},{1,17},{17,1},{2,18},{18,2},{3,19},{19,3},{4,20},{20... | collective-permute-start | bytes 12296 | tf_op jit(solution)/shard_map/ppermute | solution.py:586
  95.9 5.8 %collective-permute-start.24 = (f32[8,128]{1,0:T(8,128)S(1)}, f32[8,128]{1,0:T(8,128)S(1)}, u32[]{:S(2)}, u32[]{:S(2)}) collective-permute-start(f32[8,128]{1,0:T(8,128)S(1)} %get-tuple-element.255), channel_id=1, source_target_pairs={{16,17},{17,16},{1,2},{2,1},{18,19},{19,18},{3,4},{4,3},{20,21},{2... | collective-permute-start | bytes 12296 | tf_op jit(solution)/shard_map/ppermute | solution.py:585
  102.2 3.7 %collective-permute-start.27 = (f32[8,128]{1,0:T(8,128)S(1)}, f32[8,128]{1,0:T(8,128)S(1)}, u32[]{:S(2)}, u32[]{:S(2)}) collective-permute-start(f32[8,128]{1,0:T(8,128)S(1)} %get-tuple-element.265), channel_id=1, source_target_pairs={{0,16},{16,0},{1,17},{17,1},{2,18},{18,2},{3,19},{19,3},{4,20},{20... | collective-permute-start | bytes 12296 | tf_op jit(solution)/shard_map/ppermute | solution.py:586
  102.3 5.8 %collective-permute-start.26 = (f32[8,128]{1,0:T(8,128)S(1)}, f32[8,128]{1,0:T(8,128)S(1)}, u32[]{:S(2)}, u32[]{:S(2)}) collective-permute-start(f32[8,128]{1,0:T(8,128)S(1)} %get-tuple-element.264), channel_id=1, source_target_pairs={{16,17},{17,16},{1,2},{2,1},{18,19},{19,18},{3,4},{4,3},{20,21},{2... | collective-permute-start | bytes 12296 | tf_op jit(solution)/shard_map/ppermute | solution.py:585
  108.6 3.7 %collective-permute-start.29 = (f32[8,128]{1,0:T(8,128)S(1)}, f32[8,128]{1,0:T(8,128)S(1)}, u32[]{:S(2)}, u32[]{:S(2)}) collective-permute-start(f32[8,128]{1,0:T(8,128)S(1)} %get-tuple-element.275), channel_id=1, source_target_pairs={{0,16},{16,0},{1,17},{17,1},{2,18},{18,2},{3,19},{19,3},{4,20},{20... | collective-permute-start | bytes 12296 | tf_op jit(solution)/shard_map/ppermute | solution.py:586
  108.7 5.8 %collective-permute-start.28 = (f32[8,128]{1,0:T(8,128)S(1)}, f32[8,128]{1,0:T(8,128)S(1)}, u32[]{:S(2)}, u32[]{:S(2)}) collective-permute-start(f32[8,128]{1,0:T(8,128)S(1)} %get-tuple-element.274), channel_id=1, source_target_pairs={{16,17},{17,16},{1,2},{2,1},{18,19},{19,18},{3,4},{4,3},{20,21},{2... | collective-permute-start | bytes 12296 | tf_op jit(solution)/shard_map/ppermute | solution.py:585
  115.0 3.7 %collective-permute-start.31 = (f32[8,128]{1,0:T(8,128)S(1)}, f32[8,128]{1,0:T(8,128)S(1)}, u32[]{:S(2)}, u32[]{:S(2)}) collective-permute-start(f32[8,128]{1,0:T(8,128)S(1)} %get-tuple-element.281), channel_id=1, source_target_pairs={{0,16},{16,0},{1,17},{17,1},{2,18},{18,2},{3,19},{19,3},{4,20},{20... | collective-permute-start | bytes 12296 | tf_op jit(solution)/shard_map/ppermute | solution.py:586
  115.1 5.8 %collective-permute-start.30 = (f32[8,128]{1,0:T(8,128)S(1)}, f32[8,128]{1,0:T(8,128)S(1)}, u32[]{:S(2)}, u32[]{:S(2)}) collective-permute-start(f32[8,128]{1,0:T(8,128)S(1)} %get-tuple-element.280), channel_id=1, source_target_pairs={{16,17},{17,16},{1,2},{2,1},{18,19},{19,18},{3,4},{4,3},{20,21},{2... | collective-permute-start | bytes 12296 | tf_op jit(solution)/shard_map/ppermute | solution.py:585
  121.4 3.7 %collective-permute-start.33 = (f32[8,128]{1,0:T(8,128)S(1)}, f32[8,128]{1,0:T(8,128)S(1)}, u32[]{:S(2)}, u32[]{:S(2)}) collective-permute-start(f32[8,128]{1,0:T(8,128)S(1)} %get-tuple-element.290), channel_id=1, source_target_pairs={{0,16},{16,0},{1,17},{17,1},{2,18},{18,2},{3,19},{19,3},{4,20},{20... | collective-permute-start | bytes 12296 | tf_op jit(solution)/shard_map/ppermute | solution.py:586
  121.5 5.8 %collective-permute-start.32 = (f32[8,128]{1,0:T(8,128)S(1)}, f32[8,128]{1,0:T(8,128)S(1)}, u32[]{:S(2)}, u32[]{:S(2)}) collective-permute-start(f32[8,128]{1,0:T(8,128)S(1)} %get-tuple-element.289), channel_id=1, source_target_pairs={{16,17},{17,16},{1,2},{2,1},{18,19},{19,18},{3,4},{4,3},{20,21},{2... | collective-permute-start | bytes 12296 | tf_op jit(solution)/shard_map/ppermute | solution.py:585
  127.8 3.7 %collective-permute-start.35 = (f32[8,128]{1,0:T(8,128)S(1)}, f32[8,128]{1,0:T(8,128)S(1)}, u32[]{:S(2)}, u32[]{:S(2)}) collective-permute-start(f32[8,128]{1,0:T(8,128)S(1)} %get-tuple-element.299), channel_id=1, source_target_pairs={{0,16},{16,0},{1,17},{17,1},{2,18},{18,2},{3,19},{19,3},{4,20},{20... | collective-permute-start | bytes 12296 | tf_op jit(solution)/shard_map/ppermute | solution.py:586
  127.9 5.8 %collective-permute-start.34 = (f32[8,128]{1,0:T(8,128)S(1)}, f32[8,128]{1,0:T(8,128)S(1)}, u32[]{:S(2)}, u32[]{:S(2)}) collective-permute-start(f32[8,128]{1,0:T(8,128)S(1)} %get-tuple-element.298), channel_id=1, source_target_pairs={{16,17},{17,16},{1,2},{2,1},{18,19},{19,18},{3,4},{4,3},{20,21},{2... | collective-permute-start | bytes 12296 | tf_op jit(solution)/shard_map/ppermute | solution.py:585
  134.1 3.7 %collective-permute-start.36 = (f32[4,2,2,128]{3,2,1,0:T(2,128)S(1)}, f32[4,2,2,128]{3,2,1,0:T(2,128)S(1)}, u32[]{:S(2)}, u32[]{:S(2)}) collective-permute-start(f32[4,2,2,128]{3,2,1,0:T(2,128)S(1)} %rev.12), channel_id=1, source_target_pairs={{0,16},{16,0},{1,17},{17,1},{2,18},{18,2},{3,19},{19,3},{4,20},{20... | collective-permute-start | bytes 24584 | tf_op jit(solution)/shard_map/ppermute | solution.py:599
